TPU v7x, 128 devices: a whole 4x4x4 slice. The times are simulated.
128 devices in a mesh: learner: 32 (over z_hi, y, x), tensor: 4 (over z_lo, core).
Axes of the slice: x: 4, y: 4, z: 4 (z_hi: 2, z_lo: 2; z = z_hi * 2 + z_lo), core: 2. Of those that a mesh axis runs over, the one named last changes fastest.
Arguments:
- inputs: bfloat16 [2, 256, 8192], P(None, 'learner', 'tensor'), may hold values from -6 to 6
- frozen_gate_weight: bfloat16 [28672, 8192], P(('learner', 'tensor')), may hold values from -0.0625 to 0.0625
- frozen_up_weight: bfloat16 [28672, 8192], P(('learner', 'tensor')), may hold values from -0.0625 to 0.0625
- frozen_down_weight: bfloat16 [28672, 8192], P(('learner', 'tensor')), may hold values from -0.125 to 0.125
- adapter_first_gate: bfloat16 [64, 8192], P(None, 'learner'), may hold values from -0.0625 to 0.0625
- adapter_second_gate: bfloat16 [28672, 64], P(('learner', 'tensor')), may hold values from -0.75 to 0.75
- adapter_first_up: bfloat16 [64, 8192], P(None, 'learner'), may hold values from -0.0625 to 0.0625
- adapter_second_up: bfloat16 [28672, 64], P(('learner', 'tensor')), may hold values from -0.75 to 0.75
- adapter_first_down: bfloat16 [28672, 64], P(('learner', 'tensor')), may hold values from -0.03125 to 0.03125
- adapter_second_down: bfloat16 [64, 8192], P(None, 'learner'), may hold values from -0.75 to 0.75
Outputs:
- outputs: bfloat16 [2, 256, 8192], P(None, 'learner', 'tensor')
All inputs are finite; a program needn't handle non-finite values.
Results may differ from a plain program's by a relative error of at most 0.0071.
Values may be sent and summed in bfloat16 or wider, within the bound.
No kernel may reach another device: no remote copies, remote signals or barrier semaphores. Data moves between devices by JAX's collectives and lax.ppermute only.
A program may use at most 128 MiB of HBM per device.

v0:
```python
import jax
import jax.numpy as jnp
from jax import lax
from jax.sharding import PartitionSpec as P

adapter_scale = 0.5


def merge_adapter_weight(frozen_matrix, left, right):
    low_rank_update = jnp.dot(left, right, preferred_element_type=jnp.float32)
    return (frozen_matrix.astype(jnp.float32) + adapter_scale * low_rank_update).astype(
        jnp.bfloat16
    )


def project_rows(rows, weight):
    return lax.dot_general(
        rows, weight, (((1,), (1,)), ((), ())), preferred_element_type=jnp.float32
    )


def shards(
    inputs,
    frozen_gate_weight,
    frozen_up_weight,
    frozen_down_weight,
    adapter_first_gate,
    adapter_second_gate,
    adapter_first_up,
    adapter_second_up,
    adapter_first_down,
    adapter_second_down,
):
    complete_gate_first, complete_up_first, complete_down_second = (
        lax.all_gather(adapter_first_gate, "learner", axis=1, tiled=True),
        lax.all_gather(adapter_first_up, "learner", axis=1, tiled=True),
        lax.all_gather(adapter_second_down, "learner", axis=1, tiled=True),
    )
    combined_gate_weight = merge_adapter_weight(
        frozen_gate_weight, adapter_second_gate, complete_gate_first
    )
    combined_up_weight = merge_adapter_weight(
        frozen_up_weight, adapter_second_up, complete_up_first
    )
    combined_down_weight = merge_adapter_weight(
        frozen_down_weight, adapter_first_down, complete_down_second
    )
    results = []
    for step in range(inputs.shape[0]):
        features = lax.all_gather(inputs[step], "tensor", axis=1, tiled=True)
        all_rows = lax.all_gather(features, "learner", axis=0, tiled=True)
        gate = project_rows(all_rows, combined_gate_weight)
        upper = project_rows(all_rows, combined_up_weight)
        hidden = (jax.nn.silu(gate) * upper).astype(jnp.bfloat16)
        replica_sum = lax.psum_scatter(
            jnp.dot(hidden, combined_down_weight, preferred_element_type=jnp.float32),
            "learner",
            scatter_dimension=0,
            tiled=True,
        )
        summed = lax.psum_scatter(replica_sum, "tensor", scatter_dimension=1, tiled=True)
        results.append(summed.astype(jnp.bfloat16))
    return jnp.stack(results)


def solution(mesh):
    in_specs = (
        P(None, "learner", "tensor"),
        P(("learner", "tensor"), None),
        P(("learner", "tensor"), None),
        P(("learner", "tensor"), None),
        P(None, "learner"),
        P(("learner", "tensor"), None),
        P(None, "learner"),
        P(("learner", "tensor"), None),
        P(("learner", "tensor"), None),
        P(None, "learner"),
    )
    out_specs = P(None, "learner", "tensor")
    return jax.shard_map(shards, mesh=mesh, in_specs=in_specs, out_specs=out_specs, check_vma=False)
```

profile of v0, /device:TPU:1, one launch (start us, length us, event | category | flops | bytes accessed | tf_op | source)
XLA Modules:
  0.0 829.5 jit_solution(18329327257791384727)
XLA Ops:
  6.5 0.0 copy-start
  6.5 0.0 all-gather.10.cloned.1.call-start
  6.5 0.7 all-gather.10.cloned.1.call-update
  7.3 0.0 all-gather.12.cloned.1.call-start
  7.3 0.7 all-gather.12.cloned.1.call-update
  8.0 0.0 all-gather.14.cloned.1.call-start
  8.1 0.7 all-gather.14.cloned.1.call-update
  8.7 0.0 all-gather.16.cloned.1.call-start
  8.8 0.8 fusion.38
  9.6 7.2 all-gather
  16.8 0.0 all-gather.16.cloned.1.call-update
  16.8 0.0 all-gather.18.cloned.1.call-start
  16.9 6.0 all-gather.2
  22.9 0.0 all-gather.18.cloned.1.call-update
  22.9 0.0 copy-start.1
  23.0 0.0 reduce-scatter.5.cloned.1.call-start
  23.0 57.6 %all-gather.10.cloned.1.call-done = bf16[64,8192]{1,0:T(8,128)(2,1)} async-done(((bf16[64,256]{1,0:T(8,128)(2,1)}), bf16[64,8192]{1,0:T(8,128)(2,1)}) %all-gather.10.cloned.1.call-update) | async-done | bytes 1048592 | tf_op jit(solution)/shard_map/all_gather | solution.py:35
  80.6 0.0 copy-done
  80.6 5.3 fusion.3
  85.9 0.0 copy-start.2
  85.9 63.1 %all-gather.12.cloned.1.call-done = bf16[64,8192]{1,0:T(8,128)(2,1)} async-done(((bf16[64,256]{1,0:T(8,128)(2,1)}), bf16[64,8192]{1,0:T(8,128)(2,1)}) %all-gather.12.cloned.1.call-update) | async-done | bytes 1048592 | tf_op jit(solution)/shard_map/all_gather | solution.py:36
  149.0 0.0 copy-done.1
  149.0 5.3 fusion.4
  154.3 63.2 %all-gather.14.cloned.1.call-done = bf16[64,8192]{1,0:T(8,128)(2,1)} async-done(((bf16[64,256]{1,0:T(8,128)(2,1)}), bf16[64,8192]{1,0:T(8,128)(2,1)}) %all-gather.14.cloned.1.call-update) | async-done | bytes 1048592 | tf_op jit(solution)/shard_map/all_gather | solution.py:37
  217.5 0.0 copy-done.2
  217.5 5.4 fusion.5
  222.9 76.8 %all-gather.16.cloned.1.call-done = bf16[1,256,8192]{2,1,0:T(8,128)(2,1)} async-done(((bf16[1,8,8192]{2,1,0:T(8,128)(2,1)}), bf16[1,256,8192]{2,1,0:T(8,128)(2,1)}) %all-gather.16.cloned.1.call-update) | async-done | bytes 4194320 | tf_op jit(solution)/shard_map/all_gather | solution.py:51
  299.7 4.7 fusion.14
  304.4 12.3 %fusion.39 = f32[256,8192]{1,0:T(8,128)} fusion(bf16[224,8192]{1,0:T(8,128)(2,1)} %fusion.5, bf16[224,8192]{1,0:T(8,128)(2,1)} %fusion.4, bf16[1,256,8192]{2,1,0:T(8,128)(2,1)} %all-gather.16.cloned.1.call-done, f32[256,224]{0,1:T(8,128)S(1)} %fusion.14), kind=kOutput, calls=%fused_computation.29 | convolution fusion | flops 1879392256 | bytes 20152320 | tf_op jit(solution)/shard_map/dot_general | solution.py:56
  316.7 0.0 reduce-scatter.5.cloned.1.call-update
  316.7 0.2 reduce-scatter.9.cloned.1.call-start
  316.9 64.9 %all-gather.18.cloned.1.call-done = bf16[1,256,8192]{2,1,0:T(8,128)(2,1)} async-done(((bf16[1,8,8192]{2,1,0:T(8,128)(2,1)}), bf16[1,256,8192]{2,1,0:T(8,128)(2,1)}) %all-gather.18.cloned.1.call-update) | async-done | bytes 4194320 | tf_op jit(solution)/shard_map/all_gather | solution.py:51
  381.9 4.7 fusion.23
  386.6 12.3 %fusion.40 = f32[256,8192]{1,0:T(8,128)} fusion(bf16[224,8192]{1,0:T(8,128)(2,1)} %fusion.5, bf16[224,8192]{1,0:T(8,128)(2,1)} %fusion.4, bf16[1,256,8192]{2,1,0:T(8,128)(2,1)} %all-gather.18.cloned.1.call-done, f32[256,224]{0,1:T(8,128)S(1)} %fusion.23), kind=kOutput, calls=%fused_computation.30 | convolution fusion | flops 1879392256 | bytes 20152320 | tf_op jit(solution)/shard_map/dot_general | solution.py:56
  398.9 0.0 reduce-scatter.9.cloned.1.call-update
  398.9 0.0 reduce-scatter.7.cloned.1.call-start
  399.0 162.4 %reduce-scatter.5.cloned.1.call-done = f32[8,8192]{1,0:T(8,128)} async-done(((f32[256,8192]{1,0:T(8,128)}), f32[8,8192]{1,0:T(8,128)}) %reduce-scatter.5.cloned.1.call-update) | async-done | bytes 262160 | tf_op jit(solution)/shard_map/reduce_scatter | solution.py:55
  561.3 0.0 reduce-scatter.7.cloned.1.call-update
  561.3 0.0 reduce-scatter.11.cloned.1.call-start
  561.4 200.6 %reduce-scatter.9.cloned.1.call-done = f32[8,8192]{1,0:T(8,128)} async-done(((f32[256,8192]{1,0:T(8,128)}), f32[8,8192]{1,0:T(8,128)}) %reduce-scatter.9.cloned.1.call-update) | async-done | bytes 262160 | tf_op jit(solution)/shard_map/reduce_scatter | solution.py:55
  762.0 0.0 reduce-scatter.11.cloned.1.call-update
  762.0 38.7 %reduce-scatter.7.cloned.1.call-done = f32[8,2048]{1,0:T(8,128)} async-done(((f32[8,8192]{1,0:T(8,128)}), f32[8,2048]{1,0:T(8,128)}) %reduce-scatter.7.cloned.1.call-update) | async-done | bytes 65552 | tf_op jit(solution)/shard_map/reduce_scatter | solution.py:61
  800.7 0.8 convert_bitcast_fusion.1
  801.5 19.9 %reduce-scatter.11.cloned.1.call-done = f32[8,2048]{1,0:T(8,128)} async-done(((f32[8,8192]{1,0:T(8,128)}), f32[8,2048]{1,0:T(8,128)}) %reduce-scatter.11.cloned.1.call-update) | async-done | bytes 65552 | tf_op jit(solution)/shard_map/reduce_scatter | solution.py:61
  821.5 0.8 convert_bitcast_fusion
  822.3 0.6 pad_maximum_fusion
Async XLA Ops:
  6.5 74.1 %copy-start = (bf16[224,64]{0,1:T(8,128)(2,1)S(1)}, bf16[224,64]{0,1:T(8,128)(2,1)}, u32[]{:S(2)}) copy-start(bf16[224,64]{0,1:T(8,128)(2,1)} %param.15) | copy-start | bytes 86020
  6.5 74.0 %all-gather.10.cloned.1.call-start = ((), (), s32[]{:S(2)}) async-start(), calls=%async_computation.4 | async-start | bytes 1081344 | tf_op jit(solution)/shard_map/all_gather | solution.py:35
  7.3 141.8 %all-gather.12.cloned.1.call-start = ((), (), s32[]{:S(2)}) async-start(), calls=%async_computation.5 | async-start | bytes 1081344 | tf_op jit(solution)/shard_map/all_gather | solution.py:36
  8.0 209.5 %all-gather.14.cloned.1.call-start = ((), (), s32[]{:S(2)}) async-start(), calls=%async_computation.6 | async-start | bytes 1081344 | tf_op jit(solution)/shard_map/all_gather | solution.py:37
  8.7 291.0 %all-gather.16.cloned.1.call-start = ((), (), s32[]{:S(2)}) async-start(), calls=%async_computation.11 | async-start | bytes 4325376 | tf_op jit(solution)/shard_map/all_gather | solution.py:51
  16.8 365.1 %all-gather.18.cloned.1.call-start = ((), (), s32[]{:S(2)}) async-start(), calls=%async_computation.12 | async-start | bytes 4325376 | tf_op jit(solution)/shard_map/all_gather | solution.py:51
  22.9 126.1 %copy-start.1 = (bf16[224,64]{0,1:T(8,128)(2,1)S(1)}, bf16[224,64]{0,1:T(8,128)(2,1)}, u32[]{:S(2)}) copy-start(bf16[224,64]{0,1:T(8,128)(2,1)} %param.17) | copy-start | bytes 86020
  23.0 538.4 %reduce-scatter.5.cloned.1.call-start = ((), (), s32[]{:S(2)}) async-start(), calls=%async_computation.7 | async-start | bytes 8650752 | tf_op jit(solution)/shard_map/reduce_scatter | solution.py:55
  85.9 131.6 %copy-start.2 = (bf16[224,64]{0,1:T(8,128)(2,1)S(1)}, bf16[224,64]{0,1:T(8,128)(2,1)}, u32[]{:S(2)}) copy-start(bf16[224,64]{0,1:T(8,128)(2,1)} %param.18) | copy-start | bytes 86020
  316.7 445.3 %reduce-scatter.9.cloned.1.call-start = ((), (), s32[]{:S(2)}) async-start(), calls=%async_computation.9 | async-start | bytes 8650752 | tf_op jit(solution)/shard_map/reduce_scatter | solution.py:55
  398.9 401.8 %reduce-scatter.7.cloned.1.call-start = ((), (), s32[]{:S(2)}) async-start(), calls=%async_computation.8 | async-start | bytes 327680 | tf_op jit(solution)/shard_map/reduce_scatter | solution.py:61
  561.3 260.1 %reduce-scatter.11.cloned.1.call-start = ((), (), s32[]{:S(2)}) async-start(), calls=%async_computation.10 | async-start | bytes 327680 | tf_op jit(solution)/shard_map/reduce_scatter | solution.py:61
Sparse Core Ops, SparseCore 0:
  10.1 70.3 all-gather.9
  83.4 65.6 all-gather.11
  151.8 65.6 all-gather.13
  220.3 79.3 all-gather.15
  302.5 79.3 all-gather.17
  384.2 177.1 reduce-scatter.4
  563.7 198.2 reduce-scatter.8
  764.4 36.2 reduce-scatter.6
  803.2 18.2 reduce-scatter.10
where the time goes:
time: 830 us; the launch traced here: 829 us
  waiting for transfers between devices  749 us (90%)
  matrix products  49.9 us (6%)
  blocking collectives  13.3 us (2%)
  between operations  13.2 us (2%)
    reduce_scatter x2, waiting for transfers between devices, shards(): lax.psum_scatter(jnp.dot(hidden, combined_down_weight, preferred_element_...  363 us
    all_gather x2, waiting for transfers between devices, shards(): all_rows = lax.all_gather(features, 'learner', axis=0, tiled=True)  142 us
    all_gather x1, waiting for transfers between devices, shards(): lax.all_gather(adapter_second_down, 'learner', axis=1, tiled=True)  63.2 us
    all_gather x1, waiting for transfers between devices, shards(): lax.all_gather(adapter_first_up, 'learner', axis=1, tiled=True)  63.1 us
    reduce_scatter x2, waiting for transfers between devices, shards(): lax.psum_scatter(replica_sum, 'tensor', scatter_dimension=1, tiled=True)  58.6 us
    all_gather x1, waiting for transfers between devices, shards(): lax.all_gather(adapter_first_gate, 'learner', axis=1, tiled=True)  57.6 us
    dot_general x2, matrix products, shards(): jnp.dot(hidden, combined_down_weight, preferred_element_type=jnp.float32)  24.5 us
  transfers between devices with their start and end apart: 9, of which 9 were waited for; matrix products, arithmetic and copies ran while one was open for 6% of the time, Pallas kernels for 0%

commit v1 on v0

v1 whole, which is shorter than its diff:
```python
import itertools

import jax
import jax.numpy as jnp
from jax import lax
from jax.experimental import pallas as pl
from jax.experimental.pallas import tpu as pltpu
from jax.sharding import Mesh, PartitionSpec as P

AXES = ("zh", "y", "x", "zl", "c")
SIZES = (2, 4, 4, 2, 2)
adapter_scale = 0.5
WIDTH = 8192
UNITS = 224
TILE = 1024
STEPS = WIDTH // TILE
PARTS = TILE // 256
f32, bf16 = jnp.float32, jnp.bfloat16


def index(zh, y, x, zl, c):
    return (((zh * 4 + y) * 4 + x) * 2 + zl) * 2 + c


def pairs(partner):
    out = []
    for zh, y, x, zl, c in itertools.product(*map(range, SIZES)):
        z, y2, x2, c2 = partner(zh * 2 + zl, y, x, c)
        out.append((index(zh, y, x, zl, c), index(z >> 1, y2, x2, z & 1, c2)))
    return out


CORE = pairs(lambda z, y, x, c: (z, y, x, 1 - c))
ALONG_Z = {k: pairs(lambda z, y, x, c: (z ^ k, y, x, c)) for k in (1, 2, 3)}
FIRST = {
    k: pairs(lambda z, y, x, c: (z, y ^ k, x, c) if c else (z, y, x ^ k, c))
    for k in (1, 2, 3)
}
SECOND = {
    k: pairs(lambda z, y, x, c: (z, y, x ^ k, c) if c else (z, y ^ k, x, c))
    for k in (1, 2, 3)
}


def send(value, route):
    return lax.ppermute(value, AXES, route)


def nt(a, b):
    return lax.dot_general(a, b, (((1,), (1,)), ((), ())), preferred_element_type=f32)


def nn(a, b):
    return jnp.dot(a, b, preferred_element_type=f32)


def ffn_kernel(n, sends, place, *refs):
    rows = refs[:n]
    gate_w, gate_w2, up_w, up_w2, down_w, down_w2 = refs[n : n + 6]
    factors = refs[n + 6 : n + 6 + 2 * PARTS]
    second_gate, second_up, first_down = refs[n + 6 + 2 * PARTS : n + 9 + 2 * PARTS]
    outs = refs[n + 9 + 2 * PARTS : 2 * n + 9 + 2 * PARTS]
    gate, up, low, hidden, low_down, first, second = refs[2 * n + 9 + 2 * PARTS :]
    step = pl.program_id(0)
    mine, theirs = slice(0, UNITS), slice(UNITS, 2 * UNITS)

    @pl.when(step == 0)
    def _():
        gate[...] = jnp.zeros_like(gate)
        up[...] = jnp.zeros_like(up)
        low[...] = jnp.zeros_like(low)

    @pl.when(step < STEPS)
    def _():
        for j in range(PARTS):
            cols = slice(j * 256, (j + 1) * 256)
            first[0:64, cols] = factors[j][0:64, :]
            first[64:128, cols] = factors[PARTS + j][0:64, :]
        x = jnp.concatenate([r[...] for r in rows], axis=0)
        gate[0] += nt(x, gate_w[...])
        gate[1] += nt(x, gate_w2[...])
        up[0] += nt(x, up_w[...])
        up[1] += nt(x, up_w2[...])
        low[...] += nt(x, first[...])

    @pl.when(step == STEPS - 1)
    def _():
        u = (adapter_scale * low[...]).astype(bf16)
        total = None
        for half, part in ((0, mine), (1, theirs)):
            g = gate[half] + nt(u, second_gate[part, :])
            v = up[half] + nt(u, second_up[part, :])
            h = (g / (1.0 + jnp.exp(-g)) * v).astype(bf16)
            hidden[half] = h
            term = nn(h, first_down[part, :])
            total = term if total is None else total + term
        low_down[...] = (adapter_scale * total).astype(bf16)

    @pl.when(step >= STEPS)
    def _():
        for j in range(PARTS):
            cols = slice(j * 256, (j + 1) * 256)
            second[0:32, cols] = factors[j][64:96, :]
            second[32:64, cols] = factors[PARTS + j][64:96, :]
        result = nn(hidden[0], down_w[...])
        result += nn(hidden[1], down_w2[...])
        result += nn(low_down[...], second[...])
        for i, out in enumerate(outs):
            out[...] = result[i * 64 : (i + 1) * 64].astype(out.dtype)


def ffn(place, rows, weights, factor, factor2, seconds, kinds):
    n = len(rows)
    m = 64 * n

    def early(i, place):
        return (0, jnp.minimum(i, STEPS - 1))

    def late(i, place):
        return (0, jnp.maximum(i - STEPS, 0))

    def shard(other, j):
        def block(i, place):
            learner = lax.rem(i, STEPS) * PARTS + j
            zh, y, x = learner // 16, (learner // 4) % 4, learner % 4
            dz, dy, dx = zh ^ place[0], y ^ place[1], x ^ place[2]
            along_x = (place[3] ^ other) == 0
            near = jnp.where(along_x, dx, dy)
            far = jnp.where(along_x, dy, dx)
            return (far * 4 + near, dz)

        return pl.BlockSpec((96, 256), block)

    whole = lambda a: pl.BlockSpec(a.shape, lambda i, place: (0, 0))
    in_specs = (
        [pl.BlockSpec((64, TILE), early)] * n
        + [pl.BlockSpec((UNITS, TILE), early)] * 4
        + [pl.BlockSpec((UNITS, TILE), late)] * 2
        + [shard(0, j) for j in range(PARTS)]
        + [shard(1, j) for j in range(PARTS)]
        + [whole(a) for a in seconds]
    )
    flops = 2 * m * WIDTH * (6 * UNITS + 192)
    traffic = 2 * WIDTH * (6 * UNITS + 192 + 2 * m)
    return pl.pallas_call(
        lambda *refs: ffn_kernel(n, kinds, *refs),
        grid_spec=pltpu.PrefetchScalarGridSpec(
            num_scalar_prefetch=1,
            grid=(2 * STEPS,),
            in_specs=in_specs,
            out_specs=[pl.BlockSpec((64, TILE), late)] * n,
            scratch_shapes=[
                pltpu.VMEM((2, m, UNITS), f32),
                pltpu.VMEM((2, m, UNITS), f32),
                pltpu.VMEM((m, 128), f32),
                pltpu.VMEM((2, m, UNITS), bf16),
                pltpu.VMEM((m, 64), bf16),
                pltpu.VMEM((128, TILE), bf16),
                pltpu.VMEM((64, TILE), bf16),
            ],
        ),
        out_shape=[jax.ShapeDtypeStruct((64, WIDTH), kind) for kind in kinds],
        compiler_params=pltpu.CompilerParams(vmem_limit_bytes=40 * 1024 * 1024),
        cost_estimate=pl.CostEstimate(
            flops=flops, bytes_accessed=traffic, transcendentals=m * 2 * UNITS
        ),
    )(place, *rows, *weights, *([factor] * PARTS), *([factor2] * PARTS), *seconds)


def shards(
    inputs,
    frozen_gate_weight,
    frozen_up_weight,
    frozen_down_weight,
    adapter_first_gate,
    adapter_second_gate,
    adapter_first_up,
    adapter_second_up,
    adapter_first_down,
    adapter_second_down,
):
    zh, y, x, zl, c = (lax.axis_index(a) for a in AXES)
    place = jnp.stack([zh, y, x, c]).astype(jnp.int32)

    def ordered(flag, a, b, axis):
        return jnp.where(
            flag == 0, jnp.concatenate([a, b], axis), jnp.concatenate([b, a], axis)
        )

    own = jnp.where(c == 0, inputs[0], inputs[1])
    other = jnp.where(c == 0, inputs[1], inputs[0])
    wide = ordered(c, own, send(other, CORE), 1)
    from_z = {k: send(wide, ALONG_Z[k]) for k in (1, 2, 3)}
    block = jnp.concatenate(
        [ordered(zl, wide, from_z[1], 1), ordered(zl, from_z[2], from_z[3], 1)], 0
    )
    block = jnp.concatenate([block] + [send(block, FIRST[k]) for k in (1, 2, 3)], 0)
    rows = [block] + [send(block, SECOND[k]) for k in (1, 2, 3)]

    ranks = jnp.stack([adapter_first_gate, adapter_first_up, adapter_second_down])
    half = jnp.where(c == 0, ranks[:, :32], ranks[:, 32:]).reshape(96, 256)
    factor = jnp.concatenate([half, send(half, ALONG_Z[3])], 1)
    factor = jnp.concatenate([factor] + [send(factor, FIRST[k]) for k in (1, 2, 3)], 0)
    factor = jnp.concatenate([factor] + [send(factor, SECOND[k]) for k in (1, 2, 3)], 0)
    factor2 = send(factor, CORE)

    weights = []
    for w in (frozen_gate_weight, frozen_up_weight, frozen_down_weight):
        weights += [w, send(w, CORE)]
    seconds = jnp.concatenate(
        [adapter_second_gate, adapter_second_up, adapter_first_down], 1
    )
    seconds = jnp.concatenate([seconds, send(seconds, CORE)], 0)
    gate_b, up_b, down_b = (
        ordered(c, s[:, :32], s[:, 32:], 1)
        for s in (seconds[:, :64], seconds[:, 64:128], seconds[:, 128:])
    )
    blank = jnp.zeros((2 * UNITS, 32), bf16)
    gate_b = jnp.concatenate([gate_b[:, :32], blank, gate_b[:, 32:], blank], 1)
    up_b = jnp.concatenate([blank, up_b[:, :32], blank, up_b[:, 32:]], 1)

    parts = ffn(
        place, rows, weights, factor, factor2, (gate_b, up_b, down_b),
        (f32, bf16, bf16, bf16),
    )

    def widen(a):
        return a.astype(f32)

    total = parts[0]
    for k in (1, 2, 3):
        total = total + widen(send(parts[k], SECOND[k]))
    mine = total[:16]
    for k in (1, 2, 3):
        back = send(total[16 * k : 16 * (k + 1)].astype(bf16), FIRST[k])
        mine = mine + widen(back)
    lower, upper = mine[:, : WIDTH // 2], mine[:, WIDTH // 2 :]
    near = jnp.where(zl == 0, lower, upper)
    away = jnp.where(zl == 0, upper, lower)
    done = near[:8]
    for k, piece in ((1, away[:8]), (2, near[8:]), (3, away[8:])):
        done = done + widen(send(piece.astype(bf16), ALONG_Z[k]))
    done = done.astype(bf16)
    keep = jnp.where(c == 0, done[:, :2048], done[:, 2048:])
    give = jnp.where(c == 0, done[:, 2048:], done[:, :2048])
    got = send(give, CORE)
    return ordered(c, keep[None], got[None], 0)


def solution(mesh):
    fine = Mesh(mesh.devices.reshape(SIZES), AXES)
    learner, tensor = ("zh", "y", "x"), ("zl", "c")
    in_specs = (
        P(None, learner, tensor),
        P(AXES, None),
        P(AXES, None),
        P(AXES, None),
        P(None, learner),
        P(AXES, None),
        P(None, learner),
        P(AXES, None),
        P(AXES, None),
        P(None, learner),
    )
    return jax.shard_map(
        shards,
        mesh=fine,
        in_specs=in_specs,
        out_specs=P(None, learner, tensor),
        check_vma=False,
    )
```

time: 830 us -> 181 us (0.22)
  waiting for transfers between devices: 749 us -> 95.1 us
  starting transfers between devices: 0.5 us -> 51.5 us
  matrix products: 49.9 us -> 0 us
  Pallas kernels: 0 us -> 22 us
  blocking collectives: 13.3 us -> 0 us
  between operations: 13.2 us -> 0.25 us
    reduce_scatter x4 -> x0, waiting for transfers between devices: 422 us -> none  [the longest x2 363 us: shards(): lax.psum_scatter(jnp.dot(hidden, combined_down_weight, preferred_element_...]
    all_gather x5 -> x0, waiting for transfers between devices: 326 us -> none  [the longest x2 142 us: shards(): all_rows = lax.all_gather(features, 'learner', axis=0, tiled=True)]
    ppermute x0 -> x32, waiting for transfers between devices: none -> 95.1 us  [send(): return lax.ppermute(value, AXES, route)]
    ppermute x0 -> x32, starting transfers between devices: none -> 51.5 us  [send(): return lax.ppermute(value, AXES, route)]
    dot_general x7 -> x0, matrix products: 49.9 us -> none  [the longest x2 24.5 us: shards(): jnp.dot(hidden, combined_down_weight, preferred_element_type=jnp.float32)]
    pallas_call x0 -> x1, Pallas kernels: none -> 22 us  [ffn(): pl.pallas_call(lambda *refs: ffn_kernel(n, kinds, *refs), grid_spec=pltpu...]
    all_gather x2 -> x0, blocking collectives: 13.3 us -> none  [shards(): features = lax.all_gather(inputs[step], 'tensor', axis=1, tiled=True)]
  transfers between devices with their start and end apart: 9 -> 32, of which waited for: 9 -> 19; matrix products, arithmetic and copies ran while one was open for 6% -> 5% of each run, Pallas kernels for 0% -> 0%
where the time goes in v1:
time: 181 us
  waiting for transfers between devices  95.1 us (53%)
  starting transfers between devices  51.5 us (28%)
  Pallas kernels  22 us (12%)
  local copies, waits for them, and re-layouts  6.35 us (4%)
  other arithmetic  5.24 us (3%)
    ppermute x32, waiting for transfers between devices, send(): return lax.ppermute(value, AXES, route)  95.1 us
    ppermute x32, starting transfers between devices, send(): return lax.ppermute(value, AXES, route)  51.5 us
    pallas_call x1, Pallas kernels, ffn(): pl.pallas_call(lambda *refs: ffn_kernel(n, kinds, *refs), grid_spec=pltpu...  22 us
    unnamed x14, local copies, waits for them, and re-layouts  5.18 us
  transfers between devices with their start and end apart: 32, of which 19 were waited for; matrix products, arithmetic and copies ran while one was open for 5% of the time, Pallas kernels for 0%

profile of v1, /device:TPU:1, one launch (start us, length us, event | category | flops | bytes accessed | tf_op | source)
XLA Modules:
  0.0 180.5 jit_solution(3335874227844915553)
XLA Ops:
  0.0 0.8 select_bitcast_fusion.2
  0.8 1.5 collective-permute-start
  2.3 0.8 pad_maximum_fusion.6
  3.2 1.8 collective-permute-start.1
  5.0 2.3 %collective-permute-start.13 = (bf16[96,256]{1,0:T(8,128)(2,1)S(1)}, bf16[96,256]{1,0:T(8,128)(2,1)S(1)}, u32[]{:S(2)}, u32[]{:S(2)}) collective-permute-start(bf16[96,256]{1,0:T(8,128)(2,1)S(1)} %bitcast.15), channel_id=1, source_target_pairs={{0,66},{1,67},{2,64},{3,65},{4,70},{5,71},{6,68},{7,69},{8,74},{9,... | collective-permute-start | bytes 147464 | tf_op jit(solution)/shard_map/ppermute | solution.py:46
  7.3 0.9 copy.11
  8.2 0.9 copy.12
  9.0 0.9 copy.13
  9.9 1.2 collective-permute-start.2
  11.1 2.0 %collective-permute-start.3 = (bf16[8,4096]{1,0:T(8,128)(2,1)S(1)}, bf16[8,4096]{1,0:T(8,128)(2,1)S(1)}, u32[]{:S(2)}, u32[]{:S(2)}) collective-permute-start(bf16[8,4096]{1,0:T(8,128)(2,1)S(1)} %maximum_select_fusion.2), channel_id=1, source_target_pairs={{0,66},{1,67},{2,64},{3,65},{4,70},{5,71},{6,68},{7,69},{8,74},{9,... | collective-permute-start | bytes 196616 | tf_op jit(solution)/shard_map/ppermute | solution.py:46
  13.8 0.8 collective-permute-done.2
  14.6 1.7 collective-permute-done.3
  17.0 1.4 collective-permute-start.4
  18.4 2.7 %collective-permute-start.15 = (bf16[96,512]{1,0:T(8,128)(2,1)S(1)}, bf16[96,512]{1,0:T(8,128)(2,1)S(1)}, u32[]{:S(2)}, u32[]{:S(2)}) collective-permute-start(bf16[96,512]{1,0:T(8,128)(2,1)S(1)} %get-tuple-element.39), channel_id=1, source_target_pairs={{0,8},{1,33},{2,10},{3,35},{4,12},{5,37},{6,14},{7,39},{8,0},{9,41... | collective-permute-start | bytes 294920 | tf_op jit(solution)/shard_map/ppermute | solution.py:46
  21.8 2.3 %collective-permute-start.21 = (bf16[224,192]{1,0:T(8,128)(2,1)S(1)}, bf16[224,192]{1,0:T(8,128)(2,1)S(1)}, u32[]{:S(2)}, u32[]{:S(2)}) collective-permute-start(bf16[224,192]{1,0:T(8,128)(2,1)S(1)} %pad_maximum_fusion.3), channel_id=1, source_target_pairs={{0,1},{1,0},{2,3},{3,2},{4,5},{5,4},{6,7},{7,6},{8,9},{9,8},{10,11... | collective-permute-start | bytes 258056 | tf_op jit(solution)/shard_map/ppermute | solution.py:46
  24.2 1.7 collective-permute-done.15
  25.9 2.0 %collective-permute-start.10 = (bf16[224,8192]{1,0:T(8,128)(2,1)}, bf16[224,8192]{1,0:T(8,128)(2,1)}, u32[]{:S(2)}, u32[]{:S(2)}) collective-permute-start(bf16[224,8192]{1,0:T(8,128)(2,1)} %refs_5_.1), channel_id=1, source_target_pairs={{0,1},{1,0},{2,3},{3,2},{4,5},{5,4},{6,7},{7,6},{8,9},{9,8},{10,11... | collective-permute-start | bytes 11010056 | tf_op jit(solution)/shard_map/ppermute | solution.py:46
  27.9 1.0 collective-permute-start.12
  29.0 3.0 %collective-permute-start.5 = (bf16[16,8192]{1,0:T(8,128)(2,1)S(1)}, bf16[16,8192]{1,0:T(8,128)(2,1)S(1)}, u32[]{:S(2)}, u32[]{:S(2)}) collective-permute-start(bf16[16,8192]{1,0:T(8,128)(2,1)S(1)} %pad_maximum_fusion.1), channel_id=1, source_target_pairs={{0,8},{1,33},{2,10},{3,35},{4,12},{5,37},{6,14},{7,39},{8,0},{9,41... | collective-permute-start | bytes 786440 | tf_op jit(solution)/shard_map/ppermute | solution.py:46
  32.7 3.4 %collective-permute-done.5 = bf16[16,8192]{1,0:T(8,128)(2,1)S(1)} collective-permute-done((bf16[16,8192]{1,0:T(8,128)(2,1)S(1)}, bf16[16,8192]{1,0:T(8,128)(2,1)S(1)}, u32[]{:S(2)}, u32[]{:S(2)}) %collective-permute-start.5) | collective-permute-done | bytes 262176 | tf_op jit(solution)/shard_map/ppermute | solution.py:46
  36.1 2.7 %collective-permute-start.6 = (bf16[16,8192]{1,0:T(8,128)(2,1)S(1)}, bf16[16,8192]{1,0:T(8,128)(2,1)S(1)}, u32[]{:S(2)}, u32[]{:S(2)}) collective-permute-start(bf16[16,8192]{1,0:T(8,128)(2,1)S(1)} %pad_maximum_fusion.1), channel_id=1, source_target_pairs={{0,12},{1,49},{2,14},{3,51},{4,8},{5,53},{6,10},{7,55},{8,4},{9,57... | collective-permute-start | bytes 786440 | tf_op jit(solution)/shard_map/ppermute | solution.py:46
  40.1 2.8 %collective-permute-done.6 = bf16[16,8192]{1,0:T(8,128)(2,1)S(1)} collective-permute-done((bf16[16,8192]{1,0:T(8,128)(2,1)S(1)}, bf16[16,8192]{1,0:T(8,128)(2,1)S(1)}, u32[]{:S(2)}, u32[]{:S(2)}) %collective-permute-start.6) | collective-permute-done | bytes 262176 | tf_op jit(solution)/shard_map/ppermute | solution.py:46
  42.9 0.7 constant_dynamic-update-slice_fusion.refs_1_
  43.6 8.7 %collective-permute-done.19 = bf16[384,512]{1,0:T(8,128)(2,1)S(1)} collective-permute-done((bf16[384,512]{1,0:T(8,128)(2,1)S(1)}, bf16[384,512]{1,0:T(8,128)(2,1)S(1)}, u32[]{:S(2)}, u32[]{:S(2)}) %collective-permute-start.19) | collective-permute-done | bytes 393248 | tf_op jit(solution)/shard_map/ppermute | solution.py:46
  52.3 0.8 collective-permute-start.9
  53.1 6.9 %collective-permute-done.17 = bf16[384,512]{1,0:T(8,128)(2,1)S(1)} collective-permute-done((bf16[384,512]{1,0:T(8,128)(2,1)S(1)}, bf16[384,512]{1,0:T(8,128)(2,1)S(1)}, u32[]{:S(2)}, u32[]{:S(2)}) %collective-permute-start.17) | collective-permute-done | bytes 393248 | tf_op jit(solution)/shard_map/ppermute | solution.py:46
  60.0 1.6 collective-permute-start.8
  61.7 17.3 %collective-permute-done.9.refs_4_ = bf16[64,8192]{1,0:T(8,128)(2,1)S(1)} collective-permute-done((bf16[64,8192]{1,0:T(8,128)(2,1)}, bf16[64,8192]{1,0:T(8,128)(2,1)S(1)}, u32[]{:S(2)}, u32[]{:S(2)}) %collective-permute-start.9) | collective-permute-done | bytes 1048608 | tf_op jit(solution)/shard_map/ppermute | solution.py:46
  79.0 1.0 copy-done
  81.2 13.0 %collective-permute-done.7.refs_2_ = bf16[64,8192]{1,0:T(8,128)(2,1)S(1)} collective-permute-done((bf16[64,8192]{1,0:T(8,128)(2,1)}, bf16[64,8192]{1,0:T(8,128)(2,1)S(1)}, u32[]{:S(2)}, u32[]{:S(2)}) %collective-permute-start.7) | collective-permute-done | bytes 1048608 | tf_op jit(solution)/shard_map/ppermute | solution.py:46
  94.2 22.0 %shard_map.100 = (f32[64,8192]{1,0:T(8,128)S(1)}, bf16[64,8192]{1,0:T(8,128)(2,1)S(1)}, bf16[64,8192]{1,0:T(8,128)(2,1)S(1)}, bf16[64,8192]{1,0:T(8,128)(2,1)S(1)}) custom-call(s32[4]{0:T(128)S(1)} %pad_add_fusion.refs_0_, bf16[64,8192]{1,0:T(8,128)(2,1)} %constant_dynamic-update-slice_fusion.refs_1_, bf16[64,8192]{1,0:T(8,128)(2,1)S(1)} %collective-permute-done.7.refs_2_, ...), custom_call_target="tpu_custom_call" | custom-call | flops 6442450944 | bytes 33554432 | tf_op jit(solution)/shard_map/pallas_call | solution.py:145
  116.3 2.0 %collective-permute-start.23 = (bf16[64,8192]{1,0:T(8,128)(2,1)S(1)}, bf16[64,8192]{1,0:T(8,128)(2,1)S(1)}, u32[]{:S(2)}, u32[]{:S(2)}) collective-permute-start(bf16[64,8192]{1,0:T(8,128)(2,1)S(1)} %get-tuple-element.11), channel_id=1, source_target_pairs={{0,32},{1,9},{2,34},{3,11},{4,36},{5,13},{6,38},{7,15},{8,40},{9,1... | collective-permute-start | bytes 3145736 | tf_op jit(solution)/shard_map/ppermute | solution.py:46
  118.3 1.8 %collective-permute-start.24 = (bf16[64,8192]{1,0:T(8,128)(2,1)S(1)}, bf16[64,8192]{1,0:T(8,128)(2,1)S(1)}, u32[]{:S(2)}, u32[]{:S(2)}) collective-permute-start(bf16[64,8192]{1,0:T(8,128)(2,1)S(1)} %get-tuple-element.12), channel_id=1, source_target_pairs={{0,48},{1,13},{2,50},{3,15},{4,52},{5,9},{6,54},{7,11},{8,56},{9,5... | collective-permute-start | bytes 3145736 | tf_op jit(solution)/shard_map/ppermute | solution.py:46
  120.2 10.1 %collective-permute-done.22 = bf16[64,8192]{1,0:T(8,128)(2,1)S(1)} collective-permute-done((bf16[64,8192]{1,0:T(8,128)(2,1)S(1)}, bf16[64,8192]{1,0:T(8,128)(2,1)S(1)}, u32[]{:S(2)}, u32[]{:S(2)}) %collective-permute-start.22) | collective-permute-done | bytes 1048608 | tf_op jit(solution)/shard_map/ppermute | solution.py:46
  130.3 11.8 %collective-permute-done.23 = bf16[64,8192]{1,0:T(8,128)(2,1)S(1)} collective-permute-done((bf16[64,8192]{1,0:T(8,128)(2,1)S(1)}, bf16[64,8192]{1,0:T(8,128)(2,1)S(1)}, u32[]{:S(2)}, u32[]{:S(2)}) %collective-permute-start.23) | collective-permute-done | bytes 1048608 | tf_op jit(solution)/shard_map/ppermute | solution.py:46
  142.1 2.6 %collective-permute-done.24 = bf16[64,8192]{1,0:T(8,128)(2,1)S(1)} collective-permute-done((bf16[64,8192]{1,0:T(8,128)(2,1)S(1)}, bf16[64,8192]{1,0:T(8,128)(2,1)S(1)}, u32[]{:S(2)}, u32[]{:S(2)}) %collective-permute-start.24) | collective-permute-done | bytes 1048608 | tf_op jit(solution)/shard_map/ppermute | solution.py:46
  145.3 1.0 collective-permute-start.25
  146.3 1.2 collective-permute-start.27
  147.6 1.1 collective-permute-start.26
  148.7 2.3 %collective-permute-done.25 = bf16[16,8192]{1,0:T(8,128)(2,1)S(1)} collective-permute-done((bf16[16,8192]{1,0:T(8,128)(2,1)S(1)}, bf16[16,8192]{1,0:T(8,128)(2,1)S(1)}, u32[]{:S(2)}, u32[]{:S(2)}) %collective-permute-start.25) | collective-permute-done | bytes 262176 | tf_op jit(solution)/shard_map/ppermute | solution.py:46
  150.9 6.9 %collective-permute-done.27 = bf16[16,8192]{1,0:T(8,128)(2,1)S(1)} collective-permute-done((bf16[16,8192]{1,0:T(8,128)(2,1)S(1)}, bf16[16,8192]{1,0:T(8,128)(2,1)S(1)}, u32[]{:S(2)}, u32[]{:S(2)}) %collective-permute-start.27) | collective-permute-done | bytes 262176 | tf_op jit(solution)/shard_map/ppermute | solution.py:46
  158.1 1.1 collective-permute-start.29
  159.1 1.9 %collective-permute-start.28 = (bf16[8,4096]{1,0:T(8,128)(2,1)S(1)}, bf16[8,4096]{1,0:T(8,128)(2,1)S(1)}, u32[]{:S(2)}, u32[]{:S(2)}) collective-permute-start(bf16[8,4096]{1,0:T(8,128)(2,1)S(1)} %get-tuple-element.31), channel_id=1, source_target_pairs={{0,2},{1,3},{2,0},{3,1},{4,6},{5,7},{6,4},{7,5},{8,10},{9,11},{10,... | collective-permute-start | bytes 196616 | tf_op jit(solution)/shard_map/ppermute | solution.py:46
  161.4 1.4 collective-permute-done.29
  162.8 0.9 collective-permute-done.28
  163.7 2.0 %collective-permute-done.30 = bf16[8,4096]{1,0:T(8,128)(2,1)S(1)} collective-permute-done((bf16[8,4096]{1,0:T(8,128)(2,1)S(1)}, bf16[8,4096]{1,0:T(8,128)(2,1)S(1)}, u32[]{:S(2)}, u32[]{:S(2)}) %collective-permute-start.30) | collective-permute-done | bytes 65568 | tf_op jit(solution)/shard_map/ppermute | solution.py:46
  165.7 13.3 %collective-permute-start.31 = (bf16[8,2048]{1,0:T(8,128)(2,1)S(1)}, bf16[8,2048]{1,0:T(8,128)(2,1)S(1)}, u32[]{:S(2)}, u32[]{:S(2)}) collective-permute-start(bf16[8,2048]{1,0:T(8,128)(2,1)S(1)} %get-tuple-element.42), channel_id=1, source_target_pairs={{0,1},{1,0},{2,3},{3,2},{4,5},{5,4},{6,7},{7,6},{8,9},{9,8},{10,11... | collective-permute-start | bytes 98312 | tf_op jit(solution)/shard_map/ppermute | solution.py:46
  179.0 0.9 collective-permute-done.31
  (60 shorter events, 7.4 us)
Async XLA Ops:
  0.8 2.4 %collective-permute-start = (bf16[8,2048]{1,0:T(8,128)(2,1)S(1)}, bf16[8,2048]{1,0:T(8,128)(2,1)S(1)}, u32[]{:S(2)}, u32[]{:S(2)}) collective-permute-start(bf16[8,2048]{1,0:T(8,128)(2,1)S(1)} %get-tuple-element.44), channel_id=1, source_target_pairs={{0,1},{1,0},{2,3},{3,2},{4,5},{5,4},{6,7},{7,6},{8,9},{9,8},{10,11... | collective-permute-start | bytes 98312 | tf_op jit(solution)/shard_map/ppermute | solution.py:46
  3.2 10.0 %collective-permute-start.1 = (bf16[8,4096]{1,0:T(8,128)(2,1)S(1)}, bf16[8,4096]{1,0:T(8,128)(2,1)S(1)}, u32[]{:S(2)}, u32[]{:S(2)}) collective-permute-start(bf16[8,4096]{1,0:T(8,128)(2,1)S(1)} %maximum_select_fusion.2), channel_id=1, source_target_pairs={{0,2},{1,3},{2,0},{3,1},{4,6},{5,7},{6,4},{7,5},{8,10},{9,11},{10,... | collective-permute-start | bytes 196616 | tf_op jit(solution)/shard_map/ppermute | solution.py:46
  5.0 13.4 %collective-permute-start.13 = (bf16[96,256]{1,0:T(8,128)(2,1)S(1)}, bf16[96,256]{1,0:T(8,128)(2,1)S(1)}, u32[]{:S(2)}, u32[]{:S(2)}) collective-permute-start(bf16[96,256]{1,0:T(8,128)(2,1)S(1)} %bitcast.15), channel_id=1, source_target_pairs={{0,66},{1,67},{2,64},{3,65},{4,70},{5,71},{6,68},{7,69},{8,74},{9,... | collective-permute-start | bytes 147464 | tf_op jit(solution)/shard_map/ppermute | solution.py:46
  9.9 4.7 %collective-permute-start.2 = (bf16[8,4096]{1,0:T(8,128)(2,1)S(1)}, bf16[8,4096]{1,0:T(8,128)(2,1)S(1)}, u32[]{:S(2)}, u32[]{:S(2)}) collective-permute-start(bf16[8,4096]{1,0:T(8,128)(2,1)S(1)} %maximum_select_fusion.2), channel_id=1, source_target_pairs={{0,64},{1,65},{2,66},{3,67},{4,68},{5,69},{6,70},{7,71},{8,72},{9,... | collective-permute-start | bytes 196616 | tf_op jit(solution)/shard_map/ppermute | solution.py:46
  11.1 5.2 %collective-permute-start.3 = (bf16[8,4096]{1,0:T(8,128)(2,1)S(1)}, bf16[8,4096]{1,0:T(8,128)(2,1)S(1)}, u32[]{:S(2)}, u32[]{:S(2)}) collective-permute-start(bf16[8,4096]{1,0:T(8,128)(2,1)S(1)} %maximum_select_fusion.2), channel_id=1, source_target_pairs={{0,66},{1,67},{2,64},{3,65},{4,70},{5,71},{6,68},{7,69},{8,74},{9,... | collective-permute-start | bytes 196616 | tf_op jit(solution)/shard_map/ppermute | solution.py:46
  17.0 12.0 %collective-permute-start.4 = (bf16[16,8192]{1,0:T(8,128)(2,1)S(1)}, bf16[16,8192]{1,0:T(8,128)(2,1)S(1)}, u32[]{:S(2)}, u32[]{:S(2)}) collective-permute-start(bf16[16,8192]{1,0:T(8,128)(2,1)S(1)} %pad_maximum_fusion.1), channel_id=1, source_target_pairs={{0,4},{1,17},{2,6},{3,19},{4,0},{5,21},{6,2},{7,23},{8,12},{9,25},... | collective-permute-start | bytes 786440 | tf_op jit(solution)/shard_map/ppermute | solution.py:46
  18.4 7.5 %collective-permute-start.15 = (bf16[96,512]{1,0:T(8,128)(2,1)S(1)}, bf16[96,512]{1,0:T(8,128)(2,1)S(1)}, u32[]{:S(2)}, u32[]{:S(2)}) collective-permute-start(bf16[96,512]{1,0:T(8,128)(2,1)S(1)} %get-tuple-element.39), channel_id=1, source_target_pairs={{0,8},{1,33},{2,10},{3,35},{4,12},{5,37},{6,14},{7,39},{8,0},{9,41... | collective-permute-start | bytes 294920 | tf_op jit(solution)/shard_map/ppermute | solution.py:46
  21.1 6.9 %collective-permute-start.14 = (bf16[96,512]{1,0:T(8,128)(2,1)S(1)}, bf16[96,512]{1,0:T(8,128)(2,1)S(1)}, u32[]{:S(2)}, u32[]{:S(2)}) collective-permute-start(bf16[96,512]{1,0:T(8,128)(2,1)S(1)} %get-tuple-element.39), channel_id=1, source_target_pairs={{0,4},{1,17},{2,6},{3,19},{4,0},{5,21},{6,2},{7,23},{8,12},{9,25},... | collective-permute-start | bytes 294920 | tf_op jit(solution)/shard_map/ppermute | solution.py:46
  21.1 6.9 %collective-permute-start.16 = (bf16[96,512]{1,0:T(8,128)(2,1)S(1)}, bf16[96,512]{1,0:T(8,128)(2,1)S(1)}, u32[]{:S(2)}, u32[]{:S(2)}) collective-permute-start(bf16[96,512]{1,0:T(8,128)(2,1)S(1)} %get-tuple-element.39), channel_id=1, source_target_pairs={{0,12},{1,49},{2,14},{3,51},{4,8},{5,53},{6,10},{7,55},{8,4},{9,57... | collective-permute-start | bytes 294920 | tf_op jit(solution)/shard_map/ppermute | solution.py:46
  21.8 17.7 %collective-permute-start.21 = (bf16[224,192]{1,0:T(8,128)(2,1)S(1)}, bf16[224,192]{1,0:T(8,128)(2,1)S(1)}, u32[]{:S(2)}, u32[]{:S(2)}) collective-permute-start(bf16[224,192]{1,0:T(8,128)(2,1)S(1)} %pad_maximum_fusion.3), channel_id=1, source_target_pairs={{0,1},{1,0},{2,3},{3,2},{4,5},{5,4},{6,7},{7,6},{8,9},{9,8},{10,11... | collective-permute-start | bytes 258056 | tf_op jit(solution)/shard_map/ppermute | solution.py:46
  25.9 68.3 %collective-permute-start.10 = (bf16[224,8192]{1,0:T(8,128)(2,1)}, bf16[224,8192]{1,0:T(8,128)(2,1)}, u32[]{:S(2)}, u32[]{:S(2)}) collective-permute-start(bf16[224,8192]{1,0:T(8,128)(2,1)} %refs_5_.1), channel_id=1, source_target_pairs={{0,1},{1,0},{2,3},{3,2},{4,5},{5,4},{6,7},{7,6},{8,9},{9,8},{10,11... | collective-permute-start | bytes 11010056 | tf_op jit(solution)/shard_map/ppermute | solution.py:46
  27.9 66.3 %collective-permute-start.11 = (bf16[224,8192]{1,0:T(8,128)(2,1)}, bf16[224,8192]{1,0:T(8,128)(2,1)}, u32[]{:S(2)}, u32[]{:S(2)}) collective-permute-start(bf16[224,8192]{1,0:T(8,128)(2,1)} %refs_7_.1), channel_id=1, source_target_pairs={{0,1},{1,0},{2,3},{3,2},{4,5},{5,4},{6,7},{7,6},{8,9},{9,8},{10,11... | collective-permute-start | bytes 11010056 | tf_op jit(solution)/shard_map/ppermute | solution.py:46
  27.9 66.3 %collective-permute-start.12 = (bf16[224,8192]{1,0:T(8,128)(2,1)}, bf16[224,8192]{1,0:T(8,128)(2,1)}, u32[]{:S(2)}, u32[]{:S(2)}) collective-permute-start(bf16[224,8192]{1,0:T(8,128)(2,1)} %refs_9_.1), channel_id=1, source_target_pairs={{0,1},{1,0},{2,3},{3,2},{4,5},{5,4},{6,7},{7,6},{8,9},{9,8},{10,11... | collective-permute-start | bytes 11010056 | tf_op jit(solution)/shard_map/ppermute | solution.py:46
  29.0 7.1 %collective-permute-start.5 = (bf16[16,8192]{1,0:T(8,128)(2,1)S(1)}, bf16[16,8192]{1,0:T(8,128)(2,1)S(1)}, u32[]{:S(2)}, u32[]{:S(2)}) collective-permute-start(bf16[16,8192]{1,0:T(8,128)(2,1)S(1)} %pad_maximum_fusion.1), channel_id=1, source_target_pairs={{0,8},{1,33},{2,10},{3,35},{4,12},{5,37},{6,14},{7,39},{8,0},{9,41... | collective-permute-start | bytes 786440 | tf_op jit(solution)/shard_map/ppermute | solution.py:46
  36.1 6.8 %collective-permute-start.6 = (bf16[16,8192]{1,0:T(8,128)(2,1)S(1)}, bf16[16,8192]{1,0:T(8,128)(2,1)S(1)}, u32[]{:S(2)}, u32[]{:S(2)}) collective-permute-start(bf16[16,8192]{1,0:T(8,128)(2,1)S(1)} %pad_maximum_fusion.1), channel_id=1, source_target_pairs={{0,12},{1,49},{2,14},{3,51},{4,8},{5,53},{6,10},{7,55},{8,4},{9,57... | collective-permute-start | bytes 786440 | tf_op jit(solution)/shard_map/ppermute | solution.py:46
  39.6 12.7 %collective-permute-start.19 = (bf16[384,512]{1,0:T(8,128)(2,1)S(1)}, bf16[384,512]{1,0:T(8,128)(2,1)S(1)}, u32[]{:S(2)}, u32[]{:S(2)}) collective-permute-start(bf16[384,512]{1,0:T(8,128)(2,1)S(1)} %pad_maximum_fusion), channel_id=1, source_target_pairs={{0,48},{1,13},{2,50},{3,15},{4,52},{5,9},{6,54},{7,11},{8,56},{9,5... | collective-permute-start | bytes 1179656 | tf_op jit(solution)/shard_map/ppermute | solution.py:46
  42.9 10.2 %collective-permute-start.18 = (bf16[384,512]{1,0:T(8,128)(2,1)S(1)}, bf16[384,512]{1,0:T(8,128)(2,1)S(1)}, u32[]{:S(2)}, u32[]{:S(2)}) collective-permute-start(bf16[384,512]{1,0:T(8,128)(2,1)S(1)} %pad_maximum_fusion), channel_id=1, source_target_pairs={{0,32},{1,9},{2,34},{3,11},{4,36},{5,13},{6,38},{7,15},{8,40},{9,1... | collective-permute-start | bytes 1179656 | tf_op jit(solution)/shard_map/ppermute | solution.py:46
  52.3 26.7 %collective-permute-start.9 = (bf16[64,8192]{1,0:T(8,128)(2,1)}, bf16[64,8192]{1,0:T(8,128)(2,1)S(1)}, u32[]{:S(2)}, u32[]{:S(2)}) collective-permute-start(bf16[64,8192]{1,0:T(8,128)(2,1)} %constant_dynamic-update-slice_fusion.refs_1_), channel_id=1, source_target_pairs={{0,48},{1,13},{2,50},{3,15},{4,52},{5,9},{6,54},{7,11},{8,56},{9,5... | collective-permute-start | bytes 3145736 | tf_op jit(solution)/shard_map/ppermute | solution.py:46
  53.1 6.9 %collective-permute-start.17 = (bf16[384,512]{1,0:T(8,128)(2,1)S(1)}, bf16[384,512]{1,0:T(8,128)(2,1)S(1)}, u32[]{:S(2)}, u32[]{:S(2)}) collective-permute-start(bf16[384,512]{1,0:T(8,128)(2,1)S(1)} %pad_maximum_fusion), channel_id=1, source_target_pairs={{0,16},{1,5},{2,18},{3,7},{4,20},{5,1},{6,22},{7,3},{8,24},{9,13},... | collective-permute-start | bytes 1179656 | tf_op jit(solution)/shard_map/ppermute | solution.py:46
  60.0 20.0 %collective-permute-start.8 = (bf16[64,8192]{1,0:T(8,128)(2,1)}, bf16[64,8192]{1,0:T(8,128)(2,1)}, u32[]{:S(2)}, u32[]{:S(2)}) collective-permute-start(bf16[64,8192]{1,0:T(8,128)(2,1)} %constant_dynamic-update-slice_fusion.refs_1_), channel_id=1, source_target_pairs={{0,32},{1,9},{2,34},{3,11},{4,36},{5,13},{6,38},{7,15},{8,40},{9,1... | collective-permute-start | bytes 3145736 | tf_op jit(solution)/shard_map/ppermute | solution.py:46
  79.0 1.1 copy-start
  80.0 14.2 %collective-permute-start.20 = (bf16[1536,512]{1,0:T(8,128)(2,1)S(1)}, bf16[1536,512]{1,0:T(8,128)(2,1)S(1)}, u32[]{:S(2)}, u32[]{:S(2)}) collective-permute-start(bf16[1536,512]{1,0:T(8,128)(2,1)S(1)} %constant_dynamic-update-slice_fusion.5.refs_11_.refs_12_.refs_13_.refs_14_), channel_id=1, source_target_pairs={{0,1},{1,0},{2,3},{3,2},{4,5},{5,4},{6,7},{7,6},{8,9},{9,8},{10,11... | collective-permute-start | bytes 4718600 | tf_op jit(solution)/shard_map/ppermute | solution.py:46
  80.0 14.2 %collective-permute-start.7 = (bf16[64,8192]{1,0:T(8,128)(2,1)}, bf16[64,8192]{1,0:T(8,128)(2,1)S(1)}, u32[]{:S(2)}, u32[]{:S(2)}) collective-permute-start(bf16[64,8192]{1,0:T(8,128)(2,1)} %constant_dynamic-update-slice_fusion.refs_1_), channel_id=1, source_target_pairs={{0,16},{1,5},{2,18},{3,7},{4,20},{5,1},{6,22},{7,3},{8,24},{9,13},... | collective-permute-start | bytes 3145736 | tf_op jit(solution)/shard_map/ppermute | solution.py:46
  80.4 13.8 %copy-start.1 = (bf16[64,8192]{1,0:T(8,128)(2,1)S(1)}, bf16[64,8192]{1,0:T(8,128)(2,1)}, u32[]{:S(2)}) copy-start(bf16[64,8192]{1,0:T(8,128)(2,1)} %copy-done) | copy-start | bytes 3145732
  116.2 14.0 %collective-permute-start.22 = (bf16[64,8192]{1,0:T(8,128)(2,1)S(1)}, bf16[64,8192]{1,0:T(8,128)(2,1)S(1)}, u32[]{:S(2)}, u32[]{:S(2)}) collective-permute-start(bf16[64,8192]{1,0:T(8,128)(2,1)S(1)} %get-tuple-element.10), channel_id=1, source_target_pairs={{0,16},{1,5},{2,18},{3,7},{4,20},{5,1},{6,22},{7,3},{8,24},{9,13},... | collective-permute-start | bytes 3145736 | tf_op jit(solution)/shard_map/ppermute | solution.py:46
  116.3 25.8 %collective-permute-start.23 = (bf16[64,8192]{1,0:T(8,128)(2,1)S(1)}, bf16[64,8192]{1,0:T(8,128)(2,1)S(1)}, u32[]{:S(2)}, u32[]{:S(2)}) collective-permute-start(bf16[64,8192]{1,0:T(8,128)(2,1)S(1)} %get-tuple-element.11), channel_id=1, source_target_pairs={{0,32},{1,9},{2,34},{3,11},{4,36},{5,13},{6,38},{7,15},{8,40},{9,1... | collective-permute-start | bytes 3145736 | tf_op jit(solution)/shard_map/ppermute | solution.py:46
  118.3 26.4 %collective-permute-start.24 = (bf16[64,8192]{1,0:T(8,128)(2,1)S(1)}, bf16[64,8192]{1,0:T(8,128)(2,1)S(1)}, u32[]{:S(2)}, u32[]{:S(2)}) collective-permute-start(bf16[64,8192]{1,0:T(8,128)(2,1)S(1)} %get-tuple-element.12), channel_id=1, source_target_pairs={{0,48},{1,13},{2,50},{3,15},{4,52},{5,9},{6,54},{7,11},{8,56},{9,5... | collective-permute-start | bytes 3145736 | tf_op jit(solution)/shard_map/ppermute | solution.py:46
  145.3 5.6 %collective-permute-start.25 = (bf16[16,8192]{1,0:T(8,128)(2,1)S(1)}, bf16[16,8192]{1,0:T(8,128)(2,1)S(1)}, u32[]{:S(2)}, u32[]{:S(2)}) collective-permute-start(bf16[16,8192]{1,0:T(8,128)(2,1)S(1)} %get-tuple-element.19), channel_id=1, source_target_pairs={{0,4},{1,17},{2,6},{3,19},{4,0},{5,21},{6,2},{7,23},{8,12},{9,25},... | collective-permute-start | bytes 786440 | tf_op jit(solution)/shard_map/ppermute | solution.py:46
  146.3 11.5 %collective-permute-start.27 = (bf16[16,8192]{1,0:T(8,128)(2,1)S(1)}, bf16[16,8192]{1,0:T(8,128)(2,1)S(1)}, u32[]{:S(2)}, u32[]{:S(2)}) collective-permute-start(bf16[16,8192]{1,0:T(8,128)(2,1)S(1)} %get-tuple-element.20), channel_id=1, source_target_pairs={{0,12},{1,49},{2,14},{3,51},{4,8},{5,53},{6,10},{7,55},{8,4},{9,57... | collective-permute-start | bytes 786440 | tf_op jit(solution)/shard_map/ppermute | solution.py:46
  147.6 10.3 %collective-permute-start.26 = (bf16[16,8192]{1,0:T(8,128)(2,1)S(1)}, bf16[16,8192]{1,0:T(8,128)(2,1)S(1)}, u32[]{:S(2)}, u32[]{:S(2)}) collective-permute-start(bf16[16,8192]{1,0:T(8,128)(2,1)S(1)} %get-tuple-element.21), channel_id=1, source_target_pairs={{0,8},{1,33},{2,10},{3,35},{4,12},{5,37},{6,14},{7,39},{8,0},{9,41... | collective-permute-start | bytes 786440 | tf_op jit(solution)/shard_map/ppermute | solution.py:46
  158.1 4.7 %collective-permute-start.29 = (bf16[8,4096]{1,0:T(8,128)(2,1)S(1)}, bf16[8,4096]{1,0:T(8,128)(2,1)S(1)}, u32[]{:S(2)}, u32[]{:S(2)}) collective-permute-start(bf16[8,4096]{1,0:T(8,128)(2,1)S(1)} %slice.177), channel_id=1, source_target_pairs={{0,64},{1,65},{2,66},{3,67},{4,68},{5,69},{6,70},{7,71},{8,72},{9,... | collective-permute-start | bytes 196616 | tf_op jit(solution)/shard_map/ppermute | solution.py:46
  159.1 4.5 %collective-permute-start.28 = (bf16[8,4096]{1,0:T(8,128)(2,1)S(1)}, bf16[8,4096]{1,0:T(8,128)(2,1)S(1)}, u32[]{:S(2)}, u32[]{:S(2)}) collective-permute-start(bf16[8,4096]{1,0:T(8,128)(2,1)S(1)} %get-tuple-element.31), channel_id=1, source_target_pairs={{0,2},{1,3},{2,0},{3,1},{4,6},{5,7},{6,4},{7,5},{8,10},{9,11},{10,... | collective-permute-start | bytes 196616 | tf_op jit(solution)/shard_map/ppermute | solution.py:46
  161.0 4.6 %collective-permute-start.30 = (bf16[8,4096]{1,0:T(8,128)(2,1)S(1)}, bf16[8,4096]{1,0:T(8,128)(2,1)S(1)}, u32[]{:S(2)}, u32[]{:S(2)}) collective-permute-start(bf16[8,4096]{1,0:T(8,128)(2,1)S(1)} %get-tuple-element.32), channel_id=1, source_target_pairs={{0,66},{1,67},{2,64},{3,65},{4,70},{5,71},{6,68},{7,69},{8,74},{9,... | collective-permute-start | bytes 196616 | tf_op jit(solution)/shard_map/ppermute | solution.py:46
  165.7 14.2 %collective-permute-start.31 = (bf16[8,2048]{1,0:T(8,128)(2,1)S(1)}, bf16[8,2048]{1,0:T(8,128)(2,1)S(1)}, u32[]{:S(2)}, u32[]{:S(2)}) collective-permute-start(bf16[8,2048]{1,0:T(8,128)(2,1)S(1)} %get-tuple-element.42), channel_id=1, source_target_pairs={{0,1},{1,0},{2,3},{3,2},{4,5},{5,4},{6,7},{7,6},{8,9},{9,8},{10,11... | collective-permute-start | bytes 98312 | tf_op jit(solution)/shard_map/ppermute | solution.py:46

commit v2 on v1

v2 whole, which is shorter than its diff:
```python
import itertools

import jax
import jax.numpy as jnp
from jax import lax
from jax.experimental import pallas as pl
from jax.experimental.pallas import tpu as pltpu
from jax.sharding import Mesh, PartitionSpec as P

AXES = ("zh", "y", "x", "zl", "c")
SIZES = (2, 4, 4, 2, 2)
adapter_scale = 0.5
WIDTH = 8192
HALF = WIDTH // 2
UNITS = 224
TILE = 2048
STEPS = WIDTH // TILE
PARTS = TILE // 256
f32, bf16 = jnp.float32, jnp.bfloat16


def index(zh, y, x, zl, c):
    return (((zh * 4 + y) * 4 + x) * 2 + zl) * 2 + c


def pairs(partner):
    out = []
    for zh, y, x, zl, c in itertools.product(*map(range, SIZES)):
        z, y2, x2, c2 = partner(zh * 2 + zl, y, x, c)
        out.append((index(zh, y, x, zl, c), index(z >> 1, y2, x2, z & 1, c2)))
    return out


CORE = pairs(lambda z, y, x, c: (z, y, x, 1 - c))
ALONG_Z = {k: pairs(lambda z, y, x, c: (z ^ k, y, x, c)) for k in (1, 2, 3)}
FIRST = {
    k: pairs(lambda z, y, x, c: (z, y ^ k, x, c) if c else (z, y, x ^ k, c))
    for k in (1, 2, 3)
}
SECOND = {
    k: pairs(lambda z, y, x, c: (z, y, x ^ k, c) if c else (z, y ^ k, x, c))
    for k in (1, 2, 3)
}


def send(value, route):
    return lax.ppermute(value, AXES, route)


def nt(a, b):
    return lax.dot_general(a, b, (((1,), (1,)), ((), ())), preferred_element_type=f32)


def nn(a, b):
    return jnp.dot(a, b, preferred_element_type=f32)


def widen(a):
    return a.astype(f32)


def after(value, others):
    return lax.optimization_barrier((value, others))[0]


def ffn_kernel(n, place, *refs):
    rows = refs[:n]
    gate_w, gate_w2, up_w, up_w2, down_w, down_w2 = refs[n : n + 6]
    factor, factor2, second_gate, second_up, first_down = refs[n + 6 : n + 11]
    outs = refs[n + 11 : 2 * n + 11]
    gate, up, low, first, second = refs[2 * n + 11 :]
    mine, theirs = slice(0, UNITS), slice(UNITS, 2 * UNITS)
    gate[...] = jnp.zeros_like(gate)
    up[...] = jnp.zeros_like(up)
    low[...] = jnp.zeros_like(low)

    def block(i, j, other):
        learner = i * PARTS + j
        zh, y, x = learner // 16, (learner // 4) % 4, learner % 4
        dz, dy, dx = zh ^ place[0], y ^ place[1], x ^ place[2]
        along_x = (place[3] ^ other) == 0
        near = jnp.where(along_x, dx, dy)
        far = jnp.where(along_x, dy, dx)
        return pl.ds(pl.multiple_of((far * 4 + near) * 16, 16), 16), dz * 256

    @pl.loop(0, STEPS)
    def _(i):
        tile = pl.ds(pl.multiple_of(i * TILE, TILE), TILE)
        for j in range(PARTS):
            cols = slice(j * 256, (j + 1) * 256)
            for o, src in ((0, factor), (1, factor2)):
                r, q = block(i, j, o)
                for k in range(4):
                    piece = src[r, pl.ds(pl.multiple_of(k * 512 + q, 256), 256)]
                    first[o * 64 + k * 16 : o * 64 + k * 16 + 16, cols] = piece
        x = jnp.concatenate([r[:, tile] for r in rows], axis=0)
        gate[0] += nt(gate_w[:, tile], x)
        gate[1] += nt(gate_w2[:, tile], x)
        up[0] += nt(up_w[:, tile], x)
        up[1] += nt(up_w2[:, tile], x)
        low[...] += nt(first[...], x)

    u = (adapter_scale * low[...]).astype(bf16)
    hidden, total = [], None
    for half, part in ((0, mine), (1, theirs)):
        g = gate[half] + nn(second_gate[part, :], u)
        v = up[half] + nn(second_up[part, :], u)
        hidden.append((g / (1.0 + jnp.exp(-g)) * v).T.astype(bf16))
        term = nn(hidden[half], first_down[part, :])
        total = term if total is None else total + term
    low_down = (adapter_scale * total).astype(bf16)

    @pl.loop(0, STEPS)
    def _(i):
        tile = pl.ds(pl.multiple_of(i * TILE, TILE), TILE)
        for j in range(PARTS):
            cols = slice(j * 256, (j + 1) * 256)
            for o, src in ((0, factor), (1, factor2)):
                r, q = block(i, j, o)
                for k in range(2):
                    piece = src[r, pl.ds(pl.multiple_of(2048 + k * 512 + q, 256), 256)]
                    second[o * 32 + k * 16 : o * 32 + k * 16 + 16, cols] = piece
        result = nn(hidden[0], down_w[:, tile])
        result += nn(hidden[1], down_w2[:, tile])
        result += nn(low_down, second[...])
        for k, out in enumerate(outs):
            out[:, tile] = result[k * 64 : (k + 1) * 64].astype(out.dtype)


def ffn(place, rows, weights, factor, factor2, seconds, kinds):
    n = len(rows)
    m = 64 * n
    flops = 2 * m * WIDTH * (6 * UNITS + 192)
    traffic = 2 * WIDTH * (6 * UNITS + 192 + 2 * m)
    operands = [*rows, *weights, factor, factor2, *seconds]
    operands = [pltpu.with_memory_space_constraint(a, pltpu.VMEM) for a in operands]
    vmem = pl.BlockSpec(memory_space=pltpu.VMEM)
    return pl.pallas_call(
        lambda *refs: ffn_kernel(n, *refs),
        in_specs=[pl.BlockSpec(memory_space=pltpu.SMEM)] + [vmem] * len(operands),
        out_specs=[vmem] * n,
        out_shape=[jax.ShapeDtypeStruct((64, WIDTH), kind) for kind in kinds],
        scratch_shapes=[
            pltpu.VMEM((2, UNITS, m), f32),
            pltpu.VMEM((2, UNITS, m), f32),
            pltpu.VMEM((128, m), f32),
            pltpu.VMEM((128, TILE), bf16),
            pltpu.VMEM((64, TILE), bf16),
        ],
        compiler_params=pltpu.CompilerParams(vmem_limit_bytes=14 * 1024 * 1024),
        cost_estimate=pl.CostEstimate(
            flops=flops, bytes_accessed=traffic, transcendentals=m * 2 * UNITS
        ),
    )(place, *operands)


def local(body, shapes, operands, place=None):
    vmem = pl.BlockSpec(memory_space=pltpu.VMEM)
    lead = [] if place is None else [place]
    return pl.pallas_call(
        body,
        in_specs=[pl.BlockSpec(memory_space=pltpu.SMEM)] * len(lead)
        + [vmem] * len(operands),
        out_specs=[vmem] * len(shapes),
        out_shape=[jax.ShapeDtypeStruct(s, kind) for s, kind in shapes],
        compiler_params=pltpu.CompilerParams(vmem_limit_bytes=14 * 1024 * 1024),
    )(*lead, *operands)


def pack_kernel(place, wide, z1, z2, z3, half, far_half, out):
    zl = place[4]
    here = pl.ds(pl.multiple_of(zl * HALF, HALF), HALF)
    there = pl.ds(pl.multiple_of((1 - zl) * HALF, HALF), HALF)
    pair = lambda a, b: jnp.concatenate([widen(a[...]), widen(b[...])], 0).astype(bf16)
    out[:, here] = pair(wide, z2)
    out[:, there] = pair(z1, z3)
    for i in range(6):
        at = WIDTH + 512 * i
        out[:, at : at + 256] = half[16 * i : 16 * i + 16, :]
        out[:, at + 256 : at + 512] = far_half[16 * i : 16 * i + 16, :]


def unpack_kernel(*refs):
    got, (block, factor) = refs[:4], refs[4:]
    for k, g in enumerate(got):
        block[16 * k : 16 * k + 16, :] = g[:, :WIDTH]
        factor[16 * k : 16 * k + 16, :] = g[:, WIDTH:]


def stack_kernel(*refs):
    out = refs[-1]
    for k, r in enumerate(refs[:-1]):
        out[64 * k : 64 * k + 64, :] = r[...]


def sum_kernel(own, b1, b2, b3, keep, s1, s2, s3):
    for k, out in enumerate((keep, s1, s2, s3)):
        part = slice(16 * k, 16 * k + 16)
        total = own[part, :]
        for b in (b1, b3, b2):
            total += widen(b[part, :])
        out[...] = total.astype(out.dtype)


def split_kernel(place, own, b1, b2, b3, keep, s1, s2, s3):
    zl = place[4]
    here = pl.ds(pl.multiple_of(zl * HALF, HALF), HALF)
    there = pl.ds(pl.multiple_of((1 - zl) * HALF, HALF), HALF)
    for cols, near, far in ((here, keep, s2), (there, s1, s3)):
        total = own[:, cols]
        for b in (b1, b2, b3):
            total += widen(b[:, cols])
        near[...] = total[:8].astype(near.dtype)
        far[...] = total[8:].astype(far.dtype)


def shards(
    inputs,
    frozen_gate_weight,
    frozen_up_weight,
    frozen_down_weight,
    adapter_first_gate,
    adapter_second_gate,
    adapter_first_up,
    adapter_second_up,
    adapter_first_down,
    adapter_second_down,
):
    zh, y, x, zl, c = (lax.axis_index(a) for a in AXES)
    place = jnp.stack([zh, y, x, c, zl]).astype(jnp.int32)

    def ordered(flag, a, b, axis):
        return jnp.where(
            flag == 0, jnp.concatenate([a, b], axis), jnp.concatenate([b, a], axis)
        )

    own = jnp.where(c == 0, inputs[0], inputs[1])
    other = jnp.where(c == 0, inputs[1], inputs[0])
    wide = ordered(c, own, send(other, CORE), 1)
    ranks = jnp.stack([adapter_first_gate, adapter_first_up, adapter_second_down])
    half = jnp.where(c == 0, ranks[:, :32], ranks[:, 32:]).reshape(96, 256)
    far_half = send(half, ALONG_Z[3])
    gate2 = send(frozen_gate_weight, CORE)

    from_z = {k: send(wide, ALONG_Z[k]) for k in (1, 2, 3)}
    (packed,) = local(
        pack_kernel,
        [((16, WIDTH + 3072), bf16)],
        (wide, from_z[1], from_z[2], from_z[3], half, far_half),
        place,
    )
    packed = after(packed, gate2)

    got = [packed] + [send(packed, FIRST[k]) for k in (1, 2, 3)]
    up2 = send(after(frozen_up_weight, packed), CORE)
    own_b = after((adapter_second_gate, adapter_second_up, adapter_first_down), packed)
    own_b = jnp.concatenate(own_b, 1)
    far_b = send(own_b, CORE)
    block, factor = local(
        unpack_kernel, [((64, WIDTH), bf16), ((64, 3072), bf16)], got
    )
    block, factor = after((block, factor), (up2, far_b))

    (factor,) = local(
        stack_kernel,
        [((256, 3072), bf16)],
        [factor] + [send(factor, SECOND[k]) for k in (1, 2, 3)],
    )
    rows = [block] + [send(block, SECOND[k]) for k in (1, 3)]
    factor2 = send(factor, CORE)
    rows.append(send(after(block, factor), SECOND[2]))
    down2 = send(after(frozen_down_weight, factor), CORE)

    seconds = jnp.concatenate([own_b, far_b], 0)
    gate_b, up_b, down_b = (
        ordered(c, s[:, :32], s[:, 32:], 1)
        for s in (seconds[:, :64], seconds[:, 64:128], seconds[:, 128:])
    )
    blank = jnp.zeros((2 * UNITS, 32), bf16)
    gate_b = jnp.concatenate([gate_b[:, :32], blank, gate_b[:, 32:], blank], 1)
    up_b = jnp.concatenate([blank, up_b[:, :32], blank, up_b[:, 32:]], 1)

    weights = (
        frozen_gate_weight, gate2, frozen_up_weight, up2, frozen_down_weight, down2,
    )
    seconds = (gate_b, up_b, down_b)

    total, part1, part3 = ffn(
        place, rows[:3], weights, factor, factor2, seconds, (f32, bf16, bf16)
    )
    back = {1: send(part1, SECOND[1]), 3: send(part3, SECOND[3])}
    (part2,) = ffn(
        place, [after(rows[3], part1)], weights, factor, factor2, seconds, (bf16,)
    )
    back[2] = send(part2, SECOND[2])
    small = [((16, WIDTH), f32)] + [((16, WIDTH), bf16)] * 3
    mine, *parts = local(sum_kernel, small, (total, back[1], back[2], back[3]))
    backs = [send(p, FIRST[k]) for k, p in zip((1, 2, 3), parts, strict=True)]
    small = [((8, HALF), f32)] + [((8, HALF), bf16)] * 3
    done, *parts = local(split_kernel, small, (mine, *backs), place)
    for k, p in zip((1, 2, 3), parts, strict=True):
        done = done + widen(send(p, ALONG_Z[k]))
    done = done.astype(bf16)
    keep = jnp.where(c == 0, done[:, :2048], done[:, 2048:])
    give = jnp.where(c == 0, done[:, 2048:], done[:, :2048])
    got = send(give, CORE)
    return ordered(c, keep[None], got[None], 0)


def solution(mesh):
    fine = Mesh(mesh.devices.reshape(SIZES), AXES)
    learner, tensor = ("zh", "y", "x"), ("zl", "c")
    in_specs = (
        P(None, learner, tensor),
        P(AXES, None),
        P(AXES, None),
        P(AXES, None),
        P(None, learner),
        P(AXES, None),
        P(None, learner),
        P(AXES, None),
        P(AXES, None),
        P(None, learner),
    )
    return jax.shard_map(
        shards,
        mesh=fine,
        in_specs=in_specs,
        out_specs=P(None, learner, tensor),
        check_vma=False,
    )
```

time: 181 us -> 160 us (0.88)
  waiting for transfers between devices: 95.1 us -> 82.8 us
  starting transfers between devices: 51.5 us -> 43.6 us
  Pallas kernels: 22 us -> 25.1 us
  other arithmetic: 5.24 us -> 3.06 us
    ppermute x32 -> x29, waiting for transfers between devices: 95.1 us -> 82.8 us  [send(): return lax.ppermute(value, AXES, route)]
    ppermute x32 -> x29, starting transfers between devices: 51.5 us -> 43.6 us  [send(): return lax.ppermute(value, AXES, route)]
    unnamed x14 -> x6, local copies, waits for them, and re-layouts: 5.18 us -> 2.05 us
    pallas_call x1 -> x7, Pallas kernels: 22 us -> 25.1 us  [the longest x2 23.2 us: ffn(): pl.pallas_call(lambda *refs: ffn_kernel(n, *refs), in_specs=[pl.BlockSpec...]
    optimization_barrier x0 -> x3, local copies, waits for them, and re-layouts: none -> 2.62 us  [after(): return lax.optimization_barrier((value, others))[0]]
  transfers between devices with their start and end apart: 32 -> 29, of which waited for: 19 -> 17; matrix products, arithmetic and copies ran while one was open for 5% -> 3% of each run, Pallas kernels for 0% -> 15%
where the time goes in v2:
time: 160 us
  waiting for transfers between devices  82.8 us (52%)
  starting transfers between devices  43.6 us (27%)
  Pallas kernels  25.1 us (16%)
  local copies, waits for them, and re-layouts  5.09 us (3%)
  other arithmetic  3.06 us (2%)
    ppermute x29, waiting for transfers between devices, send(): return lax.ppermute(value, AXES, route)  82.8 us
    ppermute x29, starting transfers between devices, send(): return lax.ppermute(value, AXES, route)  43.6 us
    pallas_call x2, Pallas kernels, ffn(): pl.pallas_call(lambda *refs: ffn_kernel(n, *refs), in_specs=[pl.BlockSpec...  23.2 us
  transfers between devices with their start and end apart: 29, of which 17 were waited for; matrix products, arithmetic and copies ran while one was open for 3% of the time, Pallas kernels for 15%

profile of v2, /device:TPU:1, one launch (start us, length us, event | category | flops | bytes accessed | tf_op | source)
XLA Modules:
  0.0 160.0 jit_solution(13104369463508566875)
XLA Ops:
  0.0 1.4 collective-permute-start.5
  1.4 0.8 select_bitcast_fusion.2
  2.3 0.8 pad_maximum_fusion.4
  3.1 4.4 %collective-permute-done = bf16[8,2048]{1,0:T(8,128)(2,1)S(1)} collective-permute-done((bf16[8,2048]{1,0:T(8,128)(2,1)S(1)}, bf16[8,2048]{1,0:T(8,128)(2,1)S(1)}, u32[]{:S(2)}, u32[]{:S(2)}) %collective-permute-start) | collective-permute-done | bytes 32800 | tf_op jit(solution)/shard_map/ppermute | solution.py:47
  7.5 1.8 %collective-permute-start.1 = (bf16[8,4096]{1,0:T(8,128)(2,1)S(1)}, bf16[8,4096]{1,0:T(8,128)(2,1)S(1)}, u32[]{:S(2)}, u32[]{:S(2)}) collective-permute-start(bf16[8,4096]{1,0:T(8,128)(2,1)S(1)} %maximum_select_fusion.wide), channel_id=1, source_target_pairs={{0,2},{1,3},{2,0},{3,1},{4,6},{5,7},{6,4},{7,5},{8,10},{9,11},{10,... | collective-permute-start | bytes 196616 | tf_op jit(solution)/shard_map/ppermute | solution.py:47
  9.3 3.3 %collective-permute-start.2 = (bf16[8,4096]{1,0:T(8,128)(2,1)S(1)}, bf16[8,4096]{1,0:T(8,128)(2,1)S(1)}, u32[]{:S(2)}, u32[]{:S(2)}) collective-permute-start(bf16[8,4096]{1,0:T(8,128)(2,1)S(1)} %maximum_select_fusion.wide), channel_id=1, source_target_pairs={{0,64},{1,65},{2,66},{3,67},{4,68},{5,69},{6,70},{7,71},{8,72},{9,... | collective-permute-start | bytes 196616 | tf_op jit(solution)/shard_map/ppermute | solution.py:47
  12.6 2.8 %collective-permute-start.4 = (bf16[96,256]{1,0:T(8,128)(2,1)S(1)}, bf16[96,256]{1,0:T(8,128)(2,1)S(1)}, u32[]{:S(2)}, u32[]{:S(2)}) collective-permute-start(bf16[96,256]{1,0:T(8,128)(2,1)S(1)} %bitcast.16), channel_id=1, source_target_pairs={{0,66},{1,67},{2,64},{3,65},{4,70},{5,71},{6,68},{7,69},{8,74},{9,... | collective-permute-start | bytes 147464 | tf_op jit(solution)/shard_map/ppermute | solution.py:47
  15.5 2.1 %collective-permute-done.4.far_half = bf16[96,256]{1,0:T(8,128)(2,1)S(1)} collective-permute-done((bf16[96,256]{1,0:T(8,128)(2,1)S(1)}, bf16[96,256]{1,0:T(8,128)(2,1)S(1)}, u32[]{:S(2)}, u32[]{:S(2)}) %collective-permute-start.4) | collective-permute-done | bytes 49184 | tf_op jit(solution)/shard_map/ppermute | solution.py:47
  17.6 0.6 shard_map.100.refs_0_
  18.2 2.0 %collective-permute-start.9 = (bf16[224,8192]{1,0:T(8,128)(2,1)}, bf16[224,8192]{1,0:T(8,128)(2,1)}, u32[]{:S(2)}, u32[]{:S(2)}) collective-permute-start(bf16[224,8192]{1,0:T(8,128)(2,1)} %refs_4_.3), channel_id=1, source_target_pairs={{0,1},{1,0},{2,3},{3,2},{4,5},{5,4},{6,7},{7,6},{8,9},{9,8},{10,11... | collective-permute-start | bytes 11010056 | tf_op jit(solution)/shard_map/ppermute | solution.py:47
  20.2 1.3 collective-permute-start.6
  21.5 2.6 %collective-permute-start.7 = (bf16[16,11264]{1,0:T(8,128)(2,1)S(1)}, bf16[16,11264]{1,0:T(8,128)(2,1)S(1)}, u32[]{:S(2)}, u32[]{:S(2)}) collective-permute-start(bf16[16,11264]{1,0:T(8,128)(2,1)S(1)} %shard_map.100.refs_0_), channel_id=1, source_target_pairs={{0,8},{1,33},{2,10},{3,35},{4,12},{5,37},{6,14},{7,39},{8,0},{9,41... | collective-permute-start | bytes 1081352 | tf_op jit(solution)/shard_map/ppermute | solution.py:47
  24.2 0.9 copy.13
  25.0 0.9 copy.12
  25.9 0.9 copy.11
  26.9 1.0 collective-permute-start.10
  27.9 5.3 %collective-permute-done.7.refs_2_ = bf16[16,11264]{1,0:T(8,128)(2,1)S(1)} collective-permute-done((bf16[16,11264]{1,0:T(8,128)(2,1)S(1)}, bf16[16,11264]{1,0:T(8,128)(2,1)S(1)}, u32[]{:S(2)}, u32[]{:S(2)}) %collective-permute-start.7) | collective-permute-done | bytes 360480 | tf_op jit(solution)/shard_map/ppermute | solution.py:47
  33.2 2.6 %collective-permute-done.8.refs_3_ = bf16[16,11264]{1,0:T(8,128)(2,1)S(1)} collective-permute-done((bf16[16,11264]{1,0:T(8,128)(2,1)S(1)}, bf16[16,11264]{1,0:T(8,128)(2,1)S(1)}, u32[]{:S(2)}, u32[]{:S(2)}) %collective-permute-start.8) | collective-permute-done | bytes 360480 | tf_op jit(solution)/shard_map/ppermute | solution.py:47
  36.0 1.0 collective-permute-start.13
  36.9 2.5 %collective-permute-start.14 = (bf16[64,3072]{1,0:T(8,128)(2,1)S(1)}, bf16[64,3072]{1,0:T(8,128)(2,1)S(1)}, u32[]{:S(2)}, u32[]{:S(2)}) collective-permute-start(bf16[64,3072]{1,0:T(8,128)(2,1)S(1)} %get-tuple-element.36.refs_0_), channel_id=1, source_target_pairs={{0,32},{1,9},{2,34},{3,11},{4,36},{5,13},{6,38},{7,15},{8,40},{9,1... | collective-permute-start | bytes 1179656 | tf_op jit(solution)/shard_map/ppermute | solution.py:47
  39.4 0.5 collective-permute-start.15
  39.9 3.1 %collective-permute-done.13.refs_1_ = bf16[64,3072]{1,0:T(8,128)(2,1)S(1)} collective-permute-done((bf16[64,3072]{1,0:T(8,128)(2,1)S(1)}, bf16[64,3072]{1,0:T(8,128)(2,1)S(1)}, u32[]{:S(2)}, u32[]{:S(2)}) %collective-permute-start.13) | collective-permute-done | bytes 393248 | tf_op jit(solution)/shard_map/ppermute | solution.py:47
  43.0 6.2 %collective-permute-done.14.refs_2_ = bf16[64,3072]{1,0:T(8,128)(2,1)S(1)} collective-permute-done((bf16[64,3072]{1,0:T(8,128)(2,1)S(1)}, bf16[64,3072]{1,0:T(8,128)(2,1)S(1)}, u32[]{:S(2)}, u32[]{:S(2)}) %collective-permute-start.14) | collective-permute-done | bytes 393248 | tf_op jit(solution)/shard_map/ppermute | solution.py:47
  49.1 2.6 %collective-permute-done.15.refs_3_ = bf16[64,3072]{1,0:T(8,128)(2,1)S(1)} collective-permute-done((bf16[64,3072]{1,0:T(8,128)(2,1)S(1)}, bf16[64,3072]{1,0:T(8,128)(2,1)S(1)}, u32[]{:S(2)}, u32[]{:S(2)}) %collective-permute-start.15) | collective-permute-done | bytes 393248 | tf_op jit(solution)/shard_map/ppermute | solution.py:47
  51.8 3.3 %collective-permute-start.16 = (bf16[224,8192]{1,0:T(8,128)(2,1)}, bf16[224,8192]{1,0:T(8,128)(2,1)S(1)}, u32[]{:S(2)}, u32[]{:S(2)}) collective-permute-start(bf16[224,8192]{1,0:T(8,128)(2,1)} %refs_6_.3), channel_id=1, source_target_pairs={{0,1},{1,0},{2,3},{3,2},{4,5},{5,4},{6,7},{7,6},{8,9},{9,8},{10,11... | collective-permute-start | bytes 11010056 | tf_op jit(solution)/shard_map/ppermute | solution.py:47
  55.8 3.1 %collective-permute-start.19 = (bf16[64,8192]{1,0:T(8,128)(2,1)S(1)}, bf16[64,8192]{1,0:T(8,128)(2,1)S(1)}, u32[]{:S(2)}, u32[]{:S(2)}) collective-permute-start(bf16[64,8192]{1,0:T(8,128)(2,1)S(1)} %get-tuple-element.40.refs_1_), channel_id=1, source_target_pairs={{0,32},{1,9},{2,34},{3,11},{4,36},{5,13},{6,38},{7,15},{8,40},{9,1... | collective-permute-start | bytes 3145736 | tf_op jit(solution)/shard_map/ppermute | solution.py:47
  59.6 9.6 %collective-permute-done.11.refs_2_ = bf16[64,8192]{1,0:T(8,128)(2,1)S(1)} collective-permute-done((bf16[64,8192]{1,0:T(8,128)(2,1)S(1)}, bf16[64,8192]{1,0:T(8,128)(2,1)S(1)}, u32[]{:S(2)}, u32[]{:S(2)}) %collective-permute-start.11) | collective-permute-done | bytes 1048608 | tf_op jit(solution)/shard_map/ppermute | solution.py:47
  69.2 12.4 %collective-permute-done.12.refs_3_ = bf16[64,8192]{1,0:T(8,128)(2,1)S(1)} collective-permute-done((bf16[64,8192]{1,0:T(8,128)(2,1)S(1)}, bf16[64,8192]{1,0:T(8,128)(2,1)S(1)}, u32[]{:S(2)}, u32[]{:S(2)}) %collective-permute-start.12) | collective-permute-done | bytes 1048608 | tf_op jit(solution)/shard_map/ppermute | solution.py:47
  81.7 2.0 %copy-done.2 = bf16[224,8192]{1,0:T(8,128)(2,1)S(1)} copy-done((bf16[224,8192]{1,0:T(8,128)(2,1)S(1)}, bf16[224,8192]{1,0:T(8,128)(2,1)}, u32[]{:S(2)}) %copy-start.2) | copy-done | bytes 3670040
  83.7 12.3 %shard_map.103 = (f32[64,8192]{1,0:T(8,128)S(1)}, bf16[64,8192]{1,0:T(8,128)(2,1)S(1)}, bf16[64,8192]{1,0:T(8,128)(2,1)S(1)}) custom-call(s32[5]{0:T(128)S(1)} %stack.35.place.refs_0_, bf16[64,8192]{1,0:T(8,128)(2,1)S(1)} %get-tuple-element.40.refs_1_, bf16[64,8192]{1,0:T(8,128)(2,1)S(1)} %collective-permute-done.11.refs_2_, ...), custom_call_target="tpu_custom_call" | custom-call | flops 4831838208 | bytes 31457280 | tf_op jit(solution)/shard_map/pallas_call | solution.py:138
  96.1 10.9 %shard_map.104 = bf16[64,8192]{1,0:T(8,128)(2,1)S(1)} custom-call(s32[5]{0:T(128)S(1)} %stack.35.place.refs_0_, bf16[64,8192]{1,0:T(8,128)(2,1)S(1)} %collective-permute-done.19.refs_1_, bf16[224,8192]{1,0:T(8,128)(2,1)S(1)} %copy-done, bf16[224,8192]{1,0:T(8,128)(2,1)} %collective-permute-done.5.refs_5_.refs_3_, bf16[224,8192]{1,0:T(8,128)(2,1)S(1)} %copy-done.1, ...), custom_call_target="tpu_custom_call" | custom-call | flops 1610612736 | bytes 27262976 | tf_op jit(solution)/shard_map/pallas_call | solution.py:138
  107.0 0.5 collective-permute-start.20
  107.5 3.4 %collective-permute-start.21 = (bf16[64,8192]{1,0:T(8,128)(2,1)S(1)}, bf16[64,8192]{1,0:T(8,128)(2,1)S(1)}, u32[]{:S(2)}, u32[]{:S(2)}) collective-permute-start(bf16[64,8192]{1,0:T(8,128)(2,1)S(1)} %get-tuple-element.42), channel_id=1, source_target_pairs={{0,48},{1,13},{2,50},{3,15},{4,52},{5,9},{6,54},{7,11},{8,56},{9,5... | collective-permute-start | bytes 3145736 | tf_op jit(solution)/shard_map/ppermute | solution.py:47
  111.0 11.6 %collective-permute-done.20.b2 = bf16[64,8192]{1,0:T(8,128)(2,1)S(1)} collective-permute-done((bf16[64,8192]{1,0:T(8,128)(2,1)S(1)}, bf16[64,8192]{1,0:T(8,128)(2,1)S(1)}, u32[]{:S(2)}, u32[]{:S(2)}) %collective-permute-start.20) | collective-permute-done | bytes 1048608 | tf_op jit(solution)/shard_map/ppermute | solution.py:47
  122.6 11.2 %collective-permute-done.21.b3 = bf16[64,8192]{1,0:T(8,128)(2,1)S(1)} collective-permute-done((bf16[64,8192]{1,0:T(8,128)(2,1)S(1)}, bf16[64,8192]{1,0:T(8,128)(2,1)S(1)}, u32[]{:S(2)}, u32[]{:S(2)}) %collective-permute-start.21) | collective-permute-done | bytes 1048608 | tf_op jit(solution)/shard_map/ppermute | solution.py:47
  134.4 1.3 collective-permute-start.23
  135.7 2.5 %collective-permute-start.24 = (bf16[16,8192]{1,0:T(8,128)(2,1)S(1)}, bf16[16,8192]{1,0:T(8,128)(2,1)S(1)}, u32[]{:S(2)}, u32[]{:S(2)}) collective-permute-start(bf16[16,8192]{1,0:T(8,128)(2,1)S(1)} %get-tuple-element.46), channel_id=1, source_target_pairs={{0,12},{1,49},{2,14},{3,51},{4,8},{5,53},{6,10},{7,55},{8,4},{9,57... | collective-permute-start | bytes 786440 | tf_op jit(solution)/shard_map/ppermute | solution.py:47
  138.2 1.4 collective-permute-done.22.b1
  139.6 2.8 %collective-permute-done.23.b2 = bf16[16,8192]{1,0:T(8,128)(2,1)S(1)} collective-permute-done((bf16[16,8192]{1,0:T(8,128)(2,1)S(1)}, bf16[16,8192]{1,0:T(8,128)(2,1)S(1)}, u32[]{:S(2)}, u32[]{:S(2)}) %collective-permute-start.23) | collective-permute-done | bytes 262176 | tf_op jit(solution)/shard_map/ppermute | solution.py:47
  142.4 2.9 %collective-permute-done.24.b3 = bf16[16,8192]{1,0:T(8,128)(2,1)S(1)} collective-permute-done((bf16[16,8192]{1,0:T(8,128)(2,1)S(1)}, bf16[16,8192]{1,0:T(8,128)(2,1)S(1)}, u32[]{:S(2)}, u32[]{:S(2)}) %collective-permute-start.24) | collective-permute-done | bytes 262176 | tf_op jit(solution)/shard_map/ppermute | solution.py:47
  145.2 0.7 shard_map.106
  145.9 2.4 %collective-permute-start.27 = (bf16[8,4096]{1,0:T(8,128)(2,1)S(1)}, bf16[8,4096]{1,0:T(8,128)(2,1)S(1)}, u32[]{:S(2)}, u32[]{:S(2)}) collective-permute-start(bf16[8,4096]{1,0:T(8,128)(2,1)S(1)} %get-tuple-element.50), channel_id=1, source_target_pairs={{0,66},{1,67},{2,64},{3,65},{4,70},{5,71},{6,68},{7,69},{8,74},{9,... | collective-permute-start | bytes 196616 | tf_op jit(solution)/shard_map/ppermute | solution.py:47
  148.4 0.9 collective-permute-start.25
  149.2 1.1 collective-permute-done.27
  150.3 2.7 %collective-permute-done.26 = bf16[8,4096]{1,0:T(8,128)(2,1)S(1)} collective-permute-done((bf16[8,4096]{1,0:T(8,128)(2,1)S(1)}, bf16[8,4096]{1,0:T(8,128)(2,1)S(1)}, u32[]{:S(2)}, u32[]{:S(2)}) %collective-permute-start.26) | collective-permute-done | bytes 65568 | tf_op jit(solution)/shard_map/ppermute | solution.py:47
  153.0 5.4 %collective-permute-start.28 = (bf16[8,2048]{1,0:T(8,128)(2,1)S(1)}, bf16[8,2048]{1,0:T(8,128)(2,1)S(1)}, u32[]{:S(2)}, u32[]{:S(2)}) collective-permute-start(bf16[8,2048]{1,0:T(8,128)(2,1)S(1)} %get-tuple-element.67), channel_id=1, source_target_pairs={{0,1},{1,0},{2,3},{3,2},{4,5},{5,4},{6,7},{7,6},{8,9},{9,8},{10,11... | collective-permute-start | bytes 98312 | tf_op jit(solution)/shard_map/ppermute | solution.py:47
  158.5 0.9 collective-permute-done.28
  159.3 0.6 maximum_select_fusion.1
  (41 shorter events, 2.5 us)
Async XLA Ops:
  0.0 18.2 %collective-permute-start.5 = (bf16[224,8192]{1,0:T(8,128)(2,1)}, bf16[224,8192]{1,0:T(8,128)(2,1)}, u32[]{:S(2)}, u32[]{:S(2)}) collective-permute-start(bf16[224,8192]{1,0:T(8,128)(2,1)} %refs_2_.1), channel_id=1, source_target_pairs={{0,1},{1,0},{2,3},{3,2},{4,5},{5,4},{6,7},{7,6},{8,9},{9,8},{10,11... | collective-permute-start | bytes 11010056 | tf_op jit(solution)/shard_map/ppermute | solution.py:47
  2.2 5.3 %collective-permute-start = (bf16[8,2048]{1,0:T(8,128)(2,1)S(1)}, bf16[8,2048]{1,0:T(8,128)(2,1)S(1)}, u32[]{:S(2)}, u32[]{:S(2)}) collective-permute-start(bf16[8,2048]{1,0:T(8,128)(2,1)S(1)} %get-tuple-element.69), channel_id=1, source_target_pairs={{0,1},{1,0},{2,3},{3,2},{4,5},{5,4},{6,7},{7,6},{8,9},{9,8},{10,11... | collective-permute-start | bytes 98312 | tf_op jit(solution)/shard_map/ppermute | solution.py:47
  7.5 10.1 %collective-permute-start.1 = (bf16[8,4096]{1,0:T(8,128)(2,1)S(1)}, bf16[8,4096]{1,0:T(8,128)(2,1)S(1)}, u32[]{:S(2)}, u32[]{:S(2)}) collective-permute-start(bf16[8,4096]{1,0:T(8,128)(2,1)S(1)} %maximum_select_fusion.wide), channel_id=1, source_target_pairs={{0,2},{1,3},{2,0},{3,1},{4,6},{5,7},{6,4},{7,5},{8,10},{9,11},{10,... | collective-permute-start | bytes 196616 | tf_op jit(solution)/shard_map/ppermute | solution.py:47
  9.3 8.3 %collective-permute-start.2 = (bf16[8,4096]{1,0:T(8,128)(2,1)S(1)}, bf16[8,4096]{1,0:T(8,128)(2,1)S(1)}, u32[]{:S(2)}, u32[]{:S(2)}) collective-permute-start(bf16[8,4096]{1,0:T(8,128)(2,1)S(1)} %maximum_select_fusion.wide), channel_id=1, source_target_pairs={{0,64},{1,65},{2,66},{3,67},{4,68},{5,69},{6,70},{7,71},{8,72},{9,... | collective-permute-start | bytes 196616 | tf_op jit(solution)/shard_map/ppermute | solution.py:47
  12.6 5.0 %collective-permute-start.3 = (bf16[8,4096]{1,0:T(8,128)(2,1)S(1)}, bf16[8,4096]{1,0:T(8,128)(2,1)S(1)}, u32[]{:S(2)}, u32[]{:S(2)}) collective-permute-start(bf16[8,4096]{1,0:T(8,128)(2,1)S(1)} %maximum_select_fusion.wide), channel_id=1, source_target_pairs={{0,66},{1,67},{2,64},{3,65},{4,70},{5,71},{6,68},{7,69},{8,74},{9,... | collective-permute-start | bytes 196616 | tf_op jit(solution)/shard_map/ppermute | solution.py:47
  12.6 5.0 %collective-permute-start.4 = (bf16[96,256]{1,0:T(8,128)(2,1)S(1)}, bf16[96,256]{1,0:T(8,128)(2,1)S(1)}, u32[]{:S(2)}, u32[]{:S(2)}) collective-permute-start(bf16[96,256]{1,0:T(8,128)(2,1)S(1)} %bitcast.16), channel_id=1, source_target_pairs={{0,66},{1,67},{2,64},{3,65},{4,70},{5,71},{6,68},{7,69},{8,74},{9,... | collective-permute-start | bytes 147464 | tf_op jit(solution)/shard_map/ppermute | solution.py:47
  18.2 17.7 %collective-permute-start.9 = (bf16[224,8192]{1,0:T(8,128)(2,1)}, bf16[224,8192]{1,0:T(8,128)(2,1)}, u32[]{:S(2)}, u32[]{:S(2)}) collective-permute-start(bf16[224,8192]{1,0:T(8,128)(2,1)} %refs_4_.3), channel_id=1, source_target_pairs={{0,1},{1,0},{2,3},{3,2},{4,5},{5,4},{6,7},{7,6},{8,9},{9,8},{10,11... | collective-permute-start | bytes 11010056 | tf_op jit(solution)/shard_map/ppermute | solution.py:47
  20.2 7.6 %collective-permute-start.6 = (bf16[16,11264]{1,0:T(8,128)(2,1)S(1)}, bf16[16,11264]{1,0:T(8,128)(2,1)S(1)}, u32[]{:S(2)}, u32[]{:S(2)}) collective-permute-start(bf16[16,11264]{1,0:T(8,128)(2,1)S(1)} %shard_map.100.refs_0_), channel_id=1, source_target_pairs={{0,4},{1,17},{2,6},{3,19},{4,0},{5,21},{6,2},{7,23},{8,12},{9,25},... | collective-permute-start | bytes 1081352 | tf_op jit(solution)/shard_map/ppermute | solution.py:47
  21.5 11.6 %collective-permute-start.7 = (bf16[16,11264]{1,0:T(8,128)(2,1)S(1)}, bf16[16,11264]{1,0:T(8,128)(2,1)S(1)}, u32[]{:S(2)}, u32[]{:S(2)}) collective-permute-start(bf16[16,11264]{1,0:T(8,128)(2,1)S(1)} %shard_map.100.refs_0_), channel_id=1, source_target_pairs={{0,8},{1,33},{2,10},{3,35},{4,12},{5,37},{6,14},{7,39},{8,0},{9,41... | collective-permute-start | bytes 1081352 | tf_op jit(solution)/shard_map/ppermute | solution.py:47
  24.2 11.6 %collective-permute-start.8 = (bf16[16,11264]{1,0:T(8,128)(2,1)S(1)}, bf16[16,11264]{1,0:T(8,128)(2,1)S(1)}, u32[]{:S(2)}, u32[]{:S(2)}) collective-permute-start(bf16[16,11264]{1,0:T(8,128)(2,1)S(1)} %shard_map.100.refs_0_), channel_id=1, source_target_pairs={{0,12},{1,49},{2,14},{3,51},{4,8},{5,53},{6,10},{7,55},{8,4},{9,57... | collective-permute-start | bytes 1081352 | tf_op jit(solution)/shard_map/ppermute | solution.py:47
  26.9 9.0 %collective-permute-start.10 = (bf16[224,192]{1,0:T(8,128)(2,1)S(1)}, bf16[224,192]{1,0:T(8,128)(2,1)S(1)}, u32[]{:S(2)}, u32[]{:S(2)}) collective-permute-start(bf16[224,192]{1,0:T(8,128)(2,1)S(1)} %pad_maximum_fusion.1), channel_id=1, source_target_pairs={{0,1},{1,0},{2,3},{3,2},{4,5},{5,4},{6,7},{7,6},{8,9},{9,8},{10,11... | collective-permute-start | bytes 258056 | tf_op jit(solution)/shard_map/ppermute | solution.py:47
  35.9 45.7 %copy-start = (bf16[224,8192]{1,0:T(8,128)(2,1)S(1)}, bf16[224,8192]{1,0:T(8,128)(2,1)}, u32[]{:S(2)}) copy-start(bf16[224,8192]{1,0:T(8,128)(2,1)} %refs_2_.1) | copy-start | bytes 11010052
  35.9 45.7 %copy-start.1 = (bf16[224,8192]{1,0:T(8,128)(2,1)S(1)}, bf16[224,8192]{1,0:T(8,128)(2,1)}, u32[]{:S(2)}) copy-start(bf16[224,8192]{1,0:T(8,128)(2,1)} %refs_4_.3) | copy-start | bytes 11010052
  36.0 7.0 %collective-permute-start.13 = (bf16[64,3072]{1,0:T(8,128)(2,1)S(1)}, bf16[64,3072]{1,0:T(8,128)(2,1)S(1)}, u32[]{:S(2)}, u32[]{:S(2)}) collective-permute-start(bf16[64,3072]{1,0:T(8,128)(2,1)S(1)} %get-tuple-element.36.refs_0_), channel_id=1, source_target_pairs={{0,16},{1,5},{2,18},{3,7},{4,20},{5,1},{6,22},{7,3},{8,24},{9,13},... | collective-permute-start | bytes 1179656 | tf_op jit(solution)/shard_map/ppermute | solution.py:47
  36.9 12.2 %collective-permute-start.14 = (bf16[64,3072]{1,0:T(8,128)(2,1)S(1)}, bf16[64,3072]{1,0:T(8,128)(2,1)S(1)}, u32[]{:S(2)}, u32[]{:S(2)}) collective-permute-start(bf16[64,3072]{1,0:T(8,128)(2,1)S(1)} %get-tuple-element.36.refs_0_), channel_id=1, source_target_pairs={{0,32},{1,9},{2,34},{3,11},{4,36},{5,13},{6,38},{7,15},{8,40},{9,1... | collective-permute-start | bytes 1179656 | tf_op jit(solution)/shard_map/ppermute | solution.py:47
  39.4 12.3 %collective-permute-start.15 = (bf16[64,3072]{1,0:T(8,128)(2,1)S(1)}, bf16[64,3072]{1,0:T(8,128)(2,1)S(1)}, u32[]{:S(2)}, u32[]{:S(2)}) collective-permute-start(bf16[64,3072]{1,0:T(8,128)(2,1)S(1)} %get-tuple-element.36.refs_0_), channel_id=1, source_target_pairs={{0,48},{1,13},{2,50},{3,15},{4,52},{5,9},{6,54},{7,11},{8,56},{9,5... | collective-permute-start | bytes 1179656 | tf_op jit(solution)/shard_map/ppermute | solution.py:47
  51.8 29.8 %collective-permute-start.16 = (bf16[224,8192]{1,0:T(8,128)(2,1)}, bf16[224,8192]{1,0:T(8,128)(2,1)S(1)}, u32[]{:S(2)}, u32[]{:S(2)}) collective-permute-start(bf16[224,8192]{1,0:T(8,128)(2,1)} %refs_6_.3), channel_id=1, source_target_pairs={{0,1},{1,0},{2,3},{3,2},{4,5},{5,4},{6,7},{7,6},{8,9},{9,8},{10,11... | collective-permute-start | bytes 11010056 | tf_op jit(solution)/shard_map/ppermute | solution.py:47
  55.1 26.5 %collective-permute-start.17 = (bf16[256,3072]{1,0:T(8,128)(2,1)S(1)}, bf16[256,3072]{1,0:T(8,128)(2,1)S(1)}, u32[]{:S(2)}, u32[]{:S(2)}) collective-permute-start(bf16[256,3072]{1,0:T(8,128)(2,1)S(1)} %shard_map.102.refs_10_.refs_8_), channel_id=1, source_target_pairs={{0,1},{1,0},{2,3},{3,2},{4,5},{5,4},{6,7},{7,6},{8,9},{9,8},{10,11... | collective-permute-start | bytes 4718600 | tf_op jit(solution)/shard_map/ppermute | solution.py:47
  55.2 13.9 %collective-permute-start.11 = (bf16[64,8192]{1,0:T(8,128)(2,1)S(1)}, bf16[64,8192]{1,0:T(8,128)(2,1)S(1)}, u32[]{:S(2)}, u32[]{:S(2)}) collective-permute-start(bf16[64,8192]{1,0:T(8,128)(2,1)S(1)} %get-tuple-element.40.refs_1_), channel_id=1, source_target_pairs={{0,16},{1,5},{2,18},{3,7},{4,20},{5,1},{6,22},{7,3},{8,24},{9,13},... | collective-permute-start | bytes 3145736 | tf_op jit(solution)/shard_map/ppermute | solution.py:47
  55.2 26.4 %collective-permute-start.12 = (bf16[64,8192]{1,0:T(8,128)(2,1)S(1)}, bf16[64,8192]{1,0:T(8,128)(2,1)S(1)}, u32[]{:S(2)}, u32[]{:S(2)}) collective-permute-start(bf16[64,8192]{1,0:T(8,128)(2,1)S(1)} %get-tuple-element.40.refs_1_), channel_id=1, source_target_pairs={{0,48},{1,13},{2,50},{3,15},{4,52},{5,9},{6,54},{7,11},{8,56},{9,5... | collective-permute-start | bytes 3145736 | tf_op jit(solution)/shard_map/ppermute | solution.py:47
  55.8 40.3 %collective-permute-start.19 = (bf16[64,8192]{1,0:T(8,128)(2,1)S(1)}, bf16[64,8192]{1,0:T(8,128)(2,1)S(1)}, u32[]{:S(2)}, u32[]{:S(2)}) collective-permute-start(bf16[64,8192]{1,0:T(8,128)(2,1)S(1)} %get-tuple-element.40.refs_1_), channel_id=1, source_target_pairs={{0,32},{1,9},{2,34},{3,11},{4,36},{5,13},{6,38},{7,15},{8,40},{9,1... | collective-permute-start | bytes 3145736 | tf_op jit(solution)/shard_map/ppermute | solution.py:47
  81.7 2.0 %copy-start.2 = (bf16[224,8192]{1,0:T(8,128)(2,1)S(1)}, bf16[224,8192]{1,0:T(8,128)(2,1)}, u32[]{:S(2)}) copy-start(bf16[224,8192]{1,0:T(8,128)(2,1)} %refs_6_.3) | copy-start | bytes 11010052
  96.0 15.0 %collective-permute-start.18 = (bf16[64,8192]{1,0:T(8,128)(2,1)S(1)}, bf16[64,8192]{1,0:T(8,128)(2,1)S(1)}, u32[]{:S(2)}, u32[]{:S(2)}) collective-permute-start(bf16[64,8192]{1,0:T(8,128)(2,1)S(1)} %get-tuple-element.39), channel_id=1, source_target_pairs={{0,16},{1,5},{2,18},{3,7},{4,20},{5,1},{6,22},{7,3},{8,24},{9,13},... | collective-permute-start | bytes 3145736 | tf_op jit(solution)/shard_map/ppermute | solution.py:47
  107.0 15.6 %collective-permute-start.20 = (bf16[64,8192]{1,0:T(8,128)(2,1)S(1)}, bf16[64,8192]{1,0:T(8,128)(2,1)S(1)}, u32[]{:S(2)}, u32[]{:S(2)}) collective-permute-start(bf16[64,8192]{1,0:T(8,128)(2,1)S(1)} %shard_map.104), channel_id=1, source_target_pairs={{0,32},{1,9},{2,34},{3,11},{4,36},{5,13},{6,38},{7,15},{8,40},{9,1... | collective-permute-start | bytes 3145736 | tf_op jit(solution)/shard_map/ppermute | solution.py:47
  107.5 26.3 %collective-permute-start.21 = (bf16[64,8192]{1,0:T(8,128)(2,1)S(1)}, bf16[64,8192]{1,0:T(8,128)(2,1)S(1)}, u32[]{:S(2)}, u32[]{:S(2)}) collective-permute-start(bf16[64,8192]{1,0:T(8,128)(2,1)S(1)} %get-tuple-element.42), channel_id=1, source_target_pairs={{0,48},{1,13},{2,50},{3,15},{4,52},{5,9},{6,54},{7,11},{8,56},{9,5... | collective-permute-start | bytes 3145736 | tf_op jit(solution)/shard_map/ppermute | solution.py:47
  134.3 5.3 %collective-permute-start.22 = (bf16[16,8192]{1,0:T(8,128)(2,1)S(1)}, bf16[16,8192]{1,0:T(8,128)(2,1)S(1)}, u32[]{:S(2)}, u32[]{:S(2)}) collective-permute-start(bf16[16,8192]{1,0:T(8,128)(2,1)S(1)} %get-tuple-element.44), channel_id=1, source_target_pairs={{0,4},{1,17},{2,6},{3,19},{4,0},{5,21},{6,2},{7,23},{8,12},{9,25},... | collective-permute-start | bytes 786440 | tf_op jit(solution)/shard_map/ppermute | solution.py:47
  134.4 8.0 %collective-permute-start.23 = (bf16[16,8192]{1,0:T(8,128)(2,1)S(1)}, bf16[16,8192]{1,0:T(8,128)(2,1)S(1)}, u32[]{:S(2)}, u32[]{:S(2)}) collective-permute-start(bf16[16,8192]{1,0:T(8,128)(2,1)S(1)} %get-tuple-element.45), channel_id=1, source_target_pairs={{0,8},{1,33},{2,10},{3,35},{4,12},{5,37},{6,14},{7,39},{8,0},{9,41... | collective-permute-start | bytes 786440 | tf_op jit(solution)/shard_map/ppermute | solution.py:47
  135.7 9.5 %collective-permute-start.24 = (bf16[16,8192]{1,0:T(8,128)(2,1)S(1)}, bf16[16,8192]{1,0:T(8,128)(2,1)S(1)}, u32[]{:S(2)}, u32[]{:S(2)}) collective-permute-start(bf16[16,8192]{1,0:T(8,128)(2,1)S(1)} %get-tuple-element.46), channel_id=1, source_target_pairs={{0,12},{1,49},{2,14},{3,51},{4,8},{5,53},{6,10},{7,55},{8,4},{9,57... | collective-permute-start | bytes 786440 | tf_op jit(solution)/shard_map/ppermute | solution.py:47
  145.9 4.4 %collective-permute-start.27 = (bf16[8,4096]{1,0:T(8,128)(2,1)S(1)}, bf16[8,4096]{1,0:T(8,128)(2,1)S(1)}, u32[]{:S(2)}, u32[]{:S(2)}) collective-permute-start(bf16[8,4096]{1,0:T(8,128)(2,1)S(1)} %get-tuple-element.50), channel_id=1, source_target_pairs={{0,66},{1,67},{2,64},{3,65},{4,70},{5,71},{6,68},{7,69},{8,74},{9,... | collective-permute-start | bytes 196616 | tf_op jit(solution)/shard_map/ppermute | solution.py:47
  148.3 4.6 %collective-permute-start.26 = (bf16[8,4096]{1,0:T(8,128)(2,1)S(1)}, bf16[8,4096]{1,0:T(8,128)(2,1)S(1)}, u32[]{:S(2)}, u32[]{:S(2)}) collective-permute-start(bf16[8,4096]{1,0:T(8,128)(2,1)S(1)} %get-tuple-element.49), channel_id=1, source_target_pairs={{0,64},{1,65},{2,66},{3,67},{4,68},{5,69},{6,70},{7,71},{8,72},{9,... | collective-permute-start | bytes 196616 | tf_op jit(solution)/shard_map/ppermute | solution.py:47
  148.4 4.6 %collective-permute-start.25 = (bf16[8,4096]{1,0:T(8,128)(2,1)S(1)}, bf16[8,4096]{1,0:T(8,128)(2,1)S(1)}, u32[]{:S(2)}, u32[]{:S(2)}) collective-permute-start(bf16[8,4096]{1,0:T(8,128)(2,1)S(1)} %get-tuple-element.48), channel_id=1, source_target_pairs={{0,2},{1,3},{2,0},{3,1},{4,6},{5,7},{6,4},{7,5},{8,10},{9,11},{10,... | collective-permute-start | bytes 196616 | tf_op jit(solution)/shard_map/ppermute | solution.py:47
  153.0 6.3 %collective-permute-start.28 = (bf16[8,2048]{1,0:T(8,128)(2,1)S(1)}, bf16[8,2048]{1,0:T(8,128)(2,1)S(1)}, u32[]{:S(2)}, u32[]{:S(2)}) collective-permute-start(bf16[8,2048]{1,0:T(8,128)(2,1)S(1)} %get-tuple-element.67), channel_id=1, source_target_pairs={{0,1},{1,0},{2,3},{3,2},{4,5},{5,4},{6,7},{7,6},{8,9},{9,8},{10,11... | collective-permute-start | bytes 98312 | tf_op jit(solution)/shard_map/ppermute | solution.py:47

commit v3 on v2

v3 whole, which is shorter than its diff:
```python
import itertools

import jax
import jax.numpy as jnp
from jax import lax
from jax.experimental import pallas as pl
from jax.experimental.pallas import tpu as pltpu
from jax.sharding import Mesh, PartitionSpec as P

AXES = ("zh", "y", "x", "zl", "c")
SIZES = (2, 4, 4, 2, 2)
adapter_scale = 0.5
WIDTH = 8192
HALF = WIDTH // 2
UNITS = 224
TILE = 2048
STEPS = WIDTH // TILE
PARTS = TILE // 256
f32, bf16 = jnp.float32, jnp.bfloat16
SMALL = pl.CostEstimate(flops=1, bytes_accessed=1, transcendentals=0)


def index(zh, y, x, zl, c):
    return (((zh * 4 + y) * 4 + x) * 2 + zl) * 2 + c


def pairs(partner):
    out = []
    for zh, y, x, zl, c in itertools.product(*map(range, SIZES)):
        z, y2, x2, c2 = partner(zh * 2 + zl, y, x, c)
        out.append((index(zh, y, x, zl, c), index(z >> 1, y2, x2, z & 1, c2)))
    return out


CORE = pairs(lambda z, y, x, c: (z, y, x, 1 - c))
ALONG_Z = {k: pairs(lambda z, y, x, c: (z ^ k, y, x, c)) for k in (1, 2, 3)}
FIRST = {
    k: pairs(lambda z, y, x, c: (z, y ^ k, x, c) if c else (z, y, x ^ k, c))
    for k in (1, 2, 3)
}
SECOND = {
    k: pairs(lambda z, y, x, c: (z, y, x ^ k, c) if c else (z, y ^ k, x, c))
    for k in (1, 2, 3)
}


def send(value, route):
    return lax.ppermute(value, AXES, route)


def nt(a, b):
    return lax.dot_general(a, b, (((1,), (1,)), ((), ())), preferred_element_type=f32)


def tn(a, b):
    return lax.dot_general(a, b, (((0,), (0,)), ((), ())), preferred_element_type=f32)


def nn(a, b):
    return jnp.dot(a, b, preferred_element_type=f32)


def widen(a):
    return a.astype(f32)


def after(value, others):
    return lax.optimization_barrier((value, others))[0]


def project_kernel(n, *refs):
    rows, weights, out = refs[:n], refs[n : n + 4], refs[n + 4]
    for i in range(WIDTH // TILE):
        tile = slice(i * TILE, (i + 1) * TILE)
        x = jnp.concatenate([r[:, tile] for r in rows], axis=0)
        w = jnp.concatenate([r[:, tile] for r in weights], axis=0)
        if i == 0:
            out[...] = nt(w, x)
        else:
            out[...] += nt(w, x)


def down_kernel(n, place, *refs):
    rows = refs[:n]
    acc, down_w, down_w2, factor, factor2 = refs[n : n + 5]
    seconds = refs[n + 5]
    outs = refs[n + 6 : 2 * n + 6]
    low, first, second, hidden = refs[2 * n + 6 :]

    def shards_of(i, to, groups, base):
        for j in range(PARTS):
            learner = i * PARTS + j
            zh, y, x = learner // 16, (learner // 4) % 4, learner % 4
            dz, dy, dx = zh ^ place[0], y ^ place[1], x ^ place[2]
            for other, src in ((0, factor), (1, factor2)):
                along_x = (place[3] ^ other) == 0
                near = jnp.where(along_x, dx, dy)
                far = jnp.where(along_x, dy, dx)
                r = pl.ds(pl.multiple_of((far * 4 + near) * 16, 16), 16)
                for k in range(groups):
                    at = pl.multiple_of((base + k) * 512 + dz * 256, 256)
                    row = (place[3] ^ other) * 32 + (k // 2) * 64 + (k % 2) * 16
                    row = pl.ds(pl.multiple_of(row, 16), 16)
                    to[row, j * 256 : j * 256 + 256] = src[r, pl.ds(at, 256)]

    low[...] = jnp.zeros_like(low)

    @pl.loop(0, STEPS)
    def _(i):
        tile = pl.ds(pl.multiple_of(i * TILE, TILE), TILE)
        shards_of(i, first, 4, 0)
        x = jnp.concatenate([r[:, tile] for r in rows], axis=0)
        low[...] += nt(first[...], x)

    u = (adapter_scale * low[...]).astype(bf16)
    hs, back = [], 0.0
    for half, (ref, c) in enumerate(((seconds, 0), (factor2, 3072))):
        b = [ref[64 * k : 64 * k + 64, c : c + UNITS] for k in range(3)]
        at = half * UNITS
        g = acc[at : at + UNITS] + tn(b[0], u[:64])
        at += 2 * UNITS
        v = acc[at : at + UNITS] + tn(b[1], u[64:])
        h = g / (1.0 + jnp.exp(-g)) * v
        back += nn(b[2], h.astype(bf16))
        hs.append(h)
    h, back = jnp.concatenate(hs, axis=0), adapter_scale * back
    hidden[...] = jnp.concatenate([h, back], axis=0).T.astype(bf16)

    @pl.loop(0, STEPS)
    def _(i):
        tile = pl.ds(pl.multiple_of(i * TILE, TILE), TILE)
        shards_of(i, second, 2, 4)
        w = jnp.concatenate([down_w[:, tile], down_w2[:, tile], second[...]], axis=0)
        result = nn(hidden[...], w)
        for k, out in enumerate(outs):
            out[:, tile] = result[k * 64 : (k + 1) * 64].astype(out.dtype)


VMEM = pl.BlockSpec(memory_space=pltpu.VMEM)
SMEM = pl.BlockSpec(memory_space=pltpu.SMEM)


def in_vmem(operands):
    return [pltpu.with_memory_space_constraint(a, pltpu.VMEM) for a in operands]


def cost(macs):
    return pl.CostEstimate(flops=2 * macs, bytes_accessed=2 * macs // 64, transcendentals=0)


def project(rows, weights):
    n = len(rows)
    return pl.pallas_call(
        lambda *refs: project_kernel(n, *refs),
        in_specs=[VMEM] * (n + 4),
        out_specs=VMEM,
        out_shape=jax.ShapeDtypeStruct((4 * UNITS, 64 * n), f32),
        compiler_params=pltpu.CompilerParams(vmem_limit_bytes=10 * 1024 * 1024),
        cost_estimate=cost(64 * n * WIDTH * 4 * UNITS),
    )(*in_vmem([*rows, *weights]))


def down(place, rows, acc, weights, factors, seconds, kinds):
    n = len(rows)
    m = 64 * n
    operands = in_vmem([*rows, acc, *weights, *factors, seconds])
    return pl.pallas_call(
        lambda *refs: down_kernel(n, *refs),
        in_specs=[SMEM] + [VMEM] * len(operands),
        out_specs=[VMEM] * n,
        out_shape=[jax.ShapeDtypeStruct((64, WIDTH), kind) for kind in kinds],
        scratch_shapes=[
            pltpu.VMEM((128, m), f32),
            pltpu.VMEM((128, TILE), bf16),
            pltpu.VMEM((64, TILE), bf16),
            pltpu.VMEM((m, 512), bf16),
        ],
        compiler_params=pltpu.CompilerParams(vmem_limit_bytes=10 * 1024 * 1024),
        cost_estimate=cost(m * WIDTH * (2 * UNITS + 192)),
    )(place, *operands)


def local(body, shapes, operands, place=None, price=SMALL):
    lead = [] if place is None else [place]
    return pl.pallas_call(
        body,
        in_specs=[SMEM] * len(lead) + [VMEM] * len(operands),
        out_specs=[VMEM] * len(shapes),
        out_shape=[jax.ShapeDtypeStruct(s, kind) for s, kind in shapes],
        compiler_params=pltpu.CompilerParams(vmem_limit_bytes=6 * 1024 * 1024),
        cost_estimate=price,
    )(*lead, *operands)


def pack_kernel(place, wide, z1, z2, z3, half, far_half, out):
    zl = place[4]
    here = pl.ds(pl.multiple_of(zl * HALF, HALF), HALF)
    there = pl.ds(pl.multiple_of((1 - zl) * HALF, HALF), HALF)
    pair = lambda a, b: jnp.concatenate([widen(a[...]), widen(b[...])], 0).astype(bf16)
    out[:, here] = pair(wide, z2)
    out[:, there] = pair(z1, z3)
    for i in range(6):
        at = WIDTH + 512 * i
        out[:, at : at + 256] = half[16 * i : 16 * i + 16, :]
        out[:, at + 256 : at + 512] = far_half[16 * i : 16 * i + 16, :]


def unpack_kernel(*refs):
    got, (block, factor, packed) = refs[:4], refs[4:]
    for k, g in enumerate(got):
        at = slice(16 * k, 16 * k + 16)
        block[at, :] = g[:, :WIDTH]
        factor[at, :] = g[:, WIDTH:]
        packed[at, :] = g[...]


def seconds_kernel(*refs):
    out = refs[-1]
    out[...] = jnp.zeros_like(out)
    for k, r in enumerate(refs[:-1]):
        out[64 * k : 64 * k + 64, :UNITS] = r[...]


def stack_kernel(own, f1, f3, packed2, seconds, out, rows2):
    for k, r in enumerate((own, f1, packed2, f3)):
        out[64 * k : 64 * k + 64, :3072] = r[:, -3072:]
    out[:, 3072:] = seconds[...]
    rows2[...] = packed2[:, :WIDTH]


def add_kernel(own, b, out):
    out[...] = own[...] + widen(b[...])


def sum_kernel(own, b1, b3, keep, s1, s2, s3):
    for k, out in enumerate((keep, s1, s2, s3)):
        part = slice(16 * k, 16 * k + 16)
        total = own[part, :]
        for b in (b1, b3):
            total += widen(b[part, :])
        out[...] = total.astype(out.dtype)


def split_kernel(place, own, b1, b2, b3, keep, s1, s2, s3):
    zl = place[4]
    here = pl.ds(pl.multiple_of(zl * HALF, HALF), HALF)
    there = pl.ds(pl.multiple_of((1 - zl) * HALF, HALF), HALF)
    for cols, near, far in ((here, keep, s2), (there, s1, s3)):
        total = own[:, cols]
        for b in (b1, b2, b3):
            total += widen(b[:, cols])
        near[...] = total[:8].astype(near.dtype)
        far[...] = total[8:].astype(far.dtype)


def shards(
    inputs,
    frozen_gate_weight,
    frozen_up_weight,
    frozen_down_weight,
    adapter_first_gate,
    adapter_second_gate,
    adapter_first_up,
    adapter_second_up,
    adapter_first_down,
    adapter_second_down,
):
    zh, y, x, zl, c = (lax.axis_index(a) for a in AXES)
    place = jnp.stack([zh, y, x, c, zl]).astype(jnp.int32)

    def ordered(flag, a, b, axis):
        return jnp.where(
            flag == 0, jnp.concatenate([a, b], axis), jnp.concatenate([b, a], axis)
        )

    own = jnp.where(c == 0, inputs[0], inputs[1])
    other = jnp.where(c == 0, inputs[1], inputs[0])
    wide = ordered(c, own, send(other, CORE), 1)
    ranks = jnp.stack([adapter_first_gate, adapter_first_up, adapter_second_down])
    half = jnp.where(c == 0, ranks[:, :32], ranks[:, 32:]).reshape(96, 256)
    far_half = send(half, ALONG_Z[3])

    from_z = {k: send(wide, ALONG_Z[k]) for k in (1, 2, 3)}
    gate2 = send(after(frozen_gate_weight, wide), CORE)
    (packed,) = local(
        pack_kernel,
        [((16, WIDTH + 3072), bf16)],
        (wide, from_z[1], from_z[2], from_z[3], half, far_half),
        place,
    )
    packed = after(packed, gate2)

    got = [packed] + [send(packed, FIRST[k]) for k in (1, 2, 3)]
    up2 = send(after(frozen_up_weight, packed), CORE)
    seconds = (adapter_second_gate, adapter_second_up, adapter_first_down)
    (seconds,) = local(
        seconds_kernel,
        [((256, 256), bf16)],
        [a.T for a in after(seconds, packed)],
    )
    block, factor, packed = local(
        unpack_kernel,
        [((64, WIDTH), bf16), ((64, 3072), bf16), ((64, WIDTH + 3072), bf16)],
        got,
    )
    block, factor, packed = after((block, factor, packed), up2)

    got = [send(factor, SECOND[1]), send(factor, SECOND[3]), send(packed, SECOND[2])]
    down2 = send(after(frozen_down_weight, packed), CORE)
    factor, rows2 = local(
        stack_kernel,
        [((256, 3072 + 256), bf16), ((64, WIDTH), bf16)],
        (factor, *got, seconds),
    )
    factor2 = send(factor, CORE)
    rows1, rows3 = (send(after(block, factor), SECOND[k]) for k in (1, 3))

    weights = (frozen_gate_weight, gate2, frozen_up_weight, up2)
    down_weights = (frozen_down_weight, down2)

    rows = (block, rows2)
    acc = project(rows, weights)
    total, part2 = down(
        place, rows, acc, down_weights, (factor, factor2), seconds, (f32, bf16)
    )
    back2 = send(part2, SECOND[2])
    rows = after((rows1, rows3), part2)
    acc = project(rows, weights)
    part1, part3 = down(
        place, rows, acc, down_weights, (factor, factor2), seconds, (bf16, bf16)
    )
    back1, back3 = send(part1, SECOND[1]), send(part3, SECOND[3])
    (total,) = local(
        add_kernel, [((64, WIDTH), f32)], (total, back2), price=cost(64 * WIDTH * 64 * 16)
    )
    small = [((16, WIDTH), f32)] + [((16, WIDTH), bf16)] * 3
    mine, *parts = local(sum_kernel, small, (total, back1, back3))
    backs = [send(p, FIRST[k]) for k, p in zip((1, 2, 3), parts, strict=True)]
    small = [((8, HALF), f32)] + [((8, HALF), bf16)] * 3
    done, *parts = local(split_kernel, small, (mine, *backs), place)
    for k, p in zip((1, 2, 3), parts, strict=True):
        done = done + widen(send(p, ALONG_Z[k]))
    done = done.astype(bf16)
    keep = jnp.where(c == 0, done[:, :2048], done[:, 2048:])
    give = jnp.where(c == 0, done[:, 2048:], done[:, :2048])
    got = send(give, CORE)
    return ordered(c, keep[None], got[None], 0)


def solution(mesh):
    fine = Mesh(mesh.devices.reshape(SIZES), AXES)
    learner, tensor = ("zh", "y", "x"), ("zl", "c")
    in_specs = (
        P(None, learner, tensor),
        P(AXES, None),
        P(AXES, None),
        P(AXES, None),
        P(None, learner),
        P(AXES, None),
        P(None, learner),
        P(AXES, None),
        P(AXES, None),
        P(None, learner),
    )
    return jax.shard_map(
        shards,
        mesh=fine,
        in_specs=in_specs,
        out_specs=P(None, learner, tensor),
        check_vma=False,
    )
```

time: 160 us -> 130 us (0.81)
  waiting for transfers between devices: 82.8 us -> 60.7 us
  starting transfers between devices: 43.6 us -> 36.9 us
    ppermute x29 -> x27, waiting for transfers between devices: 82.8 us -> 60.7 us  [send(): return lax.ppermute(value, AXES, route)]
    ppermute x29 -> x27, starting transfers between devices: 43.6 us -> 36.9 us  [send(): return lax.ppermute(value, AXES, route)]
    optimization_barrier x3 -> x0, local copies, waits for them, and re-layouts: 2.62 us -> none  [after(): return lax.optimization_barrier((value, others))[0]]
    unnamed x6 -> x14, local copies, waits for them, and re-layouts: 2.05 us -> 4.32 us
    pallas_call x7 -> x11, Pallas kernels: 25.1 us -> 25.4 us  [the longest x2 12.1 us: project(): pl.pallas_call(lambda *refs: project_kernel(n, *refs), in_specs=[VMEM] *...]
  transfers between devices with their start and end apart: 29 -> 27, of which waited for: 17 -> 16; matrix products, arithmetic and copies ran while one was open for 3% -> 1% of each run, Pallas kernels for 15% -> 19%
where the time goes in v3:
time: 130 us
  waiting for transfers between devices  60.7 us (47%)
  starting transfers between devices  36.9 us (28%)
  Pallas kernels  25.4 us (20%)
  local copies, waits for them, and re-layouts  4.41 us (3%)
  other arithmetic  2.29 us (2%)
    ppermute x27, waiting for transfers between devices, send(): return lax.ppermute(value, AXES, route)  60.7 us
    ppermute x27, starting transfers between devices, send(): return lax.ppermute(value, AXES, route)  36.9 us
    pallas_call x2, Pallas kernels, project(): pl.pallas_call(lambda *refs: project_kernel(n, *refs), in_specs=[VMEM] *...  12.1 us
    pallas_call x2, Pallas kernels, down(): pl.pallas_call(lambda *refs: down_kernel(n, *refs), in_specs=[SMEM] + [VM...  11.2 us
    unnamed x14, local copies, waits for them, and re-layouts  4.32 us
  transfers between devices with their start and end apart: 27, of which 16 were waited for; matrix products, arithmetic and copies ran while one was open for 1% of the time, Pallas kernels for 19%

profile of v3, /device:TPU:1, one launch (start us, length us, event | category | flops | bytes accessed | tf_op | source)
XLA Modules:
  0.0 129.9 jit_solution(8170485334486915691)
XLA Ops:
  0.0 0.8 select_bitcast_fusion.2
  0.8 1.5 %collective-permute-start = (bf16[8,2048]{1,0:T(8,128)(2,1)S(1)}, bf16[8,2048]{1,0:T(8,128)(2,1)S(1)}, u32[]{:S(2)}, u32[]{:S(2)}) collective-permute-start(bf16[8,2048]{1,0:T(8,128)(2,1)S(1)} %get-tuple-element.68), channel_id=1, source_target_pairs={{0,1},{1,0},{2,3},{3,2},{4,5},{5,4},{6,7},{7,6},{8,9},{9,8},{10,11... | collective-permute-start | bytes 98312 | tf_op jit(solution)/shard_map/ppermute | solution.py:48
  2.3 0.9 collective-permute-done
  3.6 0.8 pad_maximum_fusion
  4.4 1.8 %collective-permute-start.1 = (bf16[8,4096]{1,0:T(8,128)(2,1)S(1)}, bf16[8,4096]{1,0:T(8,128)(2,1)S(1)}, u32[]{:S(2)}, u32[]{:S(2)}) collective-permute-start(bf16[8,4096]{1,0:T(8,128)(2,1)S(1)} %maximum_select_fusion.wide), channel_id=1, source_target_pairs={{0,2},{1,3},{2,0},{3,1},{4,6},{5,7},{6,4},{7,5},{8,10},{9,11},{10,... | collective-permute-start | bytes 196616 | tf_op jit(solution)/shard_map/ppermute | solution.py:48
  6.2 3.3 %collective-permute-start.2 = (bf16[8,4096]{1,0:T(8,128)(2,1)S(1)}, bf16[8,4096]{1,0:T(8,128)(2,1)S(1)}, u32[]{:S(2)}, u32[]{:S(2)}) collective-permute-start(bf16[8,4096]{1,0:T(8,128)(2,1)S(1)} %maximum_select_fusion.wide), channel_id=1, source_target_pairs={{0,64},{1,65},{2,66},{3,67},{4,68},{5,69},{6,70},{7,71},{8,72},{9,... | collective-permute-start | bytes 196616 | tf_op jit(solution)/shard_map/ppermute | solution.py:48
  9.5 2.8 %collective-permute-start.4 = (bf16[96,256]{1,0:T(8,128)(2,1)S(1)}, bf16[96,256]{1,0:T(8,128)(2,1)S(1)}, u32[]{:S(2)}, u32[]{:S(2)}) collective-permute-start(bf16[96,256]{1,0:T(8,128)(2,1)S(1)} %bitcast.19), channel_id=1, source_target_pairs={{0,66},{1,67},{2,64},{3,65},{4,70},{5,71},{6,68},{7,69},{8,74},{9,... | collective-permute-start | bytes 147464 | tf_op jit(solution)/shard_map/ppermute | solution.py:48
  12.3 2.6 %collective-permute-done.4.far_half = bf16[96,256]{1,0:T(8,128)(2,1)S(1)} collective-permute-done((bf16[96,256]{1,0:T(8,128)(2,1)S(1)}, bf16[96,256]{1,0:T(8,128)(2,1)S(1)}, u32[]{:S(2)}, u32[]{:S(2)}) %collective-permute-start.4) | collective-permute-done | bytes 49184 | tf_op jit(solution)/shard_map/ppermute | solution.py:48
  14.9 0.6 shard_map.100.refs_0_
  15.5 1.5 %collective-permute-start.9 = (bf16[224,8192]{1,0:T(8,128)(2,1)}, bf16[224,8192]{1,0:T(8,128)(2,1)S(1)}, u32[]{:S(2)}, u32[]{:S(2)}) collective-permute-start(bf16[224,8192]{1,0:T(8,128)(2,1)} %refs_4_.6), channel_id=1, source_target_pairs={{0,1},{1,0},{2,3},{3,2},{4,5},{5,4},{6,7},{7,6},{8,9},{9,8},{10,11... | collective-permute-start | bytes 11010056 | tf_op jit(solution)/shard_map/ppermute | solution.py:48
  17.1 1.3 collective-permute-start.6
  18.4 2.6 %collective-permute-start.7 = (bf16[16,11264]{1,0:T(8,128)(2,1)S(1)}, bf16[16,11264]{1,0:T(8,128)(2,1)S(1)}, u32[]{:S(2)}, u32[]{:S(2)}) collective-permute-start(bf16[16,11264]{1,0:T(8,128)(2,1)S(1)} %shard_map.100.refs_0_), channel_id=1, source_target_pairs={{0,8},{1,33},{2,10},{3,35},{4,12},{5,37},{6,14},{7,39},{8,0},{9,41... | collective-permute-start | bytes 1081352 | tf_op jit(solution)/shard_map/ppermute | solution.py:48
  21.0 2.6 %collective-permute-done.6.refs_1_ = bf16[16,11264]{1,0:T(8,128)(2,1)S(1)} collective-permute-done((bf16[16,11264]{1,0:T(8,128)(2,1)S(1)}, bf16[16,11264]{1,0:T(8,128)(2,1)S(1)}, u32[]{:S(2)}, u32[]{:S(2)}) %collective-permute-start.6) | collective-permute-done | bytes 360480 | tf_op jit(solution)/shard_map/ppermute | solution.py:48
  23.6 6.4 %collective-permute-done.7.refs_2_ = bf16[16,11264]{1,0:T(8,128)(2,1)S(1)} collective-permute-done((bf16[16,11264]{1,0:T(8,128)(2,1)S(1)}, bf16[16,11264]{1,0:T(8,128)(2,1)S(1)}, u32[]{:S(2)}, u32[]{:S(2)}) %collective-permute-start.7) | collective-permute-done | bytes 360480 | tf_op jit(solution)/shard_map/ppermute | solution.py:48
  30.0 2.6 %collective-permute-done.8.refs_3_ = bf16[16,11264]{1,0:T(8,128)(2,1)S(1)} collective-permute-done((bf16[16,11264]{1,0:T(8,128)(2,1)S(1)}, bf16[16,11264]{1,0:T(8,128)(2,1)S(1)}, u32[]{:S(2)}, u32[]{:S(2)}) %collective-permute-start.8) | collective-permute-done | bytes 360480 | tf_op jit(solution)/shard_map/ppermute | solution.py:48
  32.8 1.3 %collective-permute-start.13 = (bf16[224,8192]{1,0:T(8,128)(2,1)}, bf16[224,8192]{1,0:T(8,128)(2,1)S(1)}, u32[]{:S(2)}, u32[]{:S(2)}) collective-permute-start(bf16[224,8192]{1,0:T(8,128)(2,1)} %refs_4_.7), channel_id=1, source_target_pairs={{0,1},{1,0},{2,3},{3,2},{4,5},{5,4},{6,7},{7,6},{8,9},{9,8},{10,11... | collective-permute-start | bytes 11010056 | tf_op jit(solution)/shard_map/ppermute | solution.py:48
  34.2 1.3 collective-permute-start.12
  35.8 1.7 %collective-permute-start.11 = (bf16[64,3072]{1,0:T(8,128)(2,1)S(1)}, bf16[64,3072]{1,0:T(8,128)(2,1)S(1)}, u32[]{:S(2)}, u32[]{:S(2)}) collective-permute-start(bf16[64,3072]{1,0:T(8,128)(2,1)S(1)} %get-tuple-element.42.own), channel_id=1, source_target_pairs={{0,48},{1,13},{2,50},{3,15},{4,52},{5,9},{6,54},{7,11},{8,56},{9,5... | collective-permute-start | bytes 1179656 | tf_op jit(solution)/shard_map/ppermute | solution.py:48
  37.4 0.8 copy-done.4
  38.2 0.8 copy-done.5
  38.9 0.8 copy-done.6
  39.7 17.0 %collective-permute-done.10.f1 = bf16[64,3072]{1,0:T(8,128)(2,1)S(1)} collective-permute-done((bf16[64,3072]{1,0:T(8,128)(2,1)S(1)}, bf16[64,3072]{1,0:T(8,128)(2,1)S(1)}, u32[]{:S(2)}, u32[]{:S(2)}) %collective-permute-start.10) | collective-permute-done | bytes 393248 | tf_op jit(solution)/shard_map/ppermute | solution.py:48
  56.7 1.3 %collective-permute-done.11.f3 = bf16[64,3072]{1,0:T(8,128)(2,1)S(1)} collective-permute-done((bf16[64,3072]{1,0:T(8,128)(2,1)S(1)}, bf16[64,3072]{1,0:T(8,128)(2,1)S(1)}, u32[]{:S(2)}, u32[]{:S(2)}) %collective-permute-start.11) | collective-permute-done | bytes 393248 | tf_op jit(solution)/shard_map/ppermute | solution.py:48
  58.2 1.4 %collective-permute-start.14 = (bf16[256,3328]{1,0:T(8,128)(2,1)S(1)}, bf16[256,3328]{1,0:T(8,128)(2,1)S(1)}, u32[]{:S(2)}, u32[]{:S(2)}) collective-permute-start(bf16[256,3328]{1,0:T(8,128)(2,1)S(1)} %get-tuple-element.49.refs_6_), channel_id=1, source_target_pairs={{0,1},{1,0},{2,3},{3,2},{4,5},{5,4},{6,7},{7,6},{8,9},{9,8},{10,11... | collective-permute-start | bytes 5111816 | tf_op jit(solution)/shard_map/ppermute | solution.py:48
  59.7 1.5 %collective-permute-start.17 = (bf16[64,8192]{1,0:T(8,128)(2,1)S(1)}, bf16[64,8192]{1,0:T(8,128)(2,1)S(1)}, u32[]{:S(2)}, u32[]{:S(2)}) collective-permute-start(bf16[64,8192]{1,0:T(8,128)(2,1)S(1)} %get-tuple-element.52.refs_0_.refs_1_), channel_id=1, source_target_pairs={{0,48},{1,13},{2,50},{3,15},{4,52},{5,9},{6,54},{7,11},{8,56},{9,5... | collective-permute-start | bytes 3145736 | tf_op jit(solution)/shard_map/ppermute | solution.py:48
  61.2 2.0 %copy-done.1 = bf16[224,8192]{1,0:T(8,128)(2,1)S(1)} copy-done((bf16[224,8192]{1,0:T(8,128)(2,1)S(1)}, bf16[224,8192]{1,0:T(8,128)(2,1)}, u32[]{:S(2)}) %copy-start.1) | copy-done | bytes 3670040
  63.2 6.1 %shard_map.104.refs_3_ = f32[896,128]{1,0:T(8,128)S(1)} custom-call(bf16[64,8192]{1,0:T(8,128)(2,1)S(1)} %get-tuple-element.52.refs_0_.refs_1_, bf16[64,8192]{1,0:T(8,128)(2,1)S(1)} %get-tuple-element.47.refs_1_.refs_2_, bf16[224,8192]{1,0:T(8,128)(2,1)S(1)} %copy-done, bf16[224,8192]{1,0:T(8,128)(2,1)} %collective-permute-done.5.refs_3_, ...), custom_call_target="tpu_custom_call" | custom-call | flops 1879048192 | bytes 29360128 | tf_op jit(solution)/shard_map/pallas_call | solution.py:153
  69.4 5.6 %shard_map.105 = (f32[64,8192]{1,0:T(8,128)S(1)}, bf16[64,8192]{1,0:T(8,128)(2,1)S(1)}) custom-call(s32[5]{0:T(128)S(1)} %stack.35.place.refs_0_, bf16[64,8192]{1,0:T(8,128)(2,1)S(1)} %get-tuple-element.52.refs_0_.refs_1_, bf16[64,8192]{1,0:T(8,128)(2,1)S(1)} %get-tuple-element.47.refs_1_.refs_2_, f32[896,128]{1,0:T(8,128)S(1)} %shard_map.104.refs_3_, ...), custom_call_target="tpu_custom_call" | custom-call | flops 1342177280 | bytes 20971520 | tf_op jit(solution)/shard_map/pallas_call | solution.py:167
  75.0 2.0 %collective-permute-start.15 = (bf16[64,8192]{1,0:T(8,128)(2,1)S(1)}, bf16[64,8192]{1,0:T(8,128)(2,1)S(1)}, u32[]{:S(2)}, u32[]{:S(2)}) collective-permute-start(bf16[64,8192]{1,0:T(8,128)(2,1)S(1)} %get-tuple-element.51), channel_id=1, source_target_pairs={{0,32},{1,9},{2,34},{3,11},{4,36},{5,13},{6,38},{7,15},{8,40},{9,1... | collective-permute-start | bytes 3145736 | tf_op jit(solution)/shard_map/ppermute | solution.py:48
  77.0 6.0 %shard_map.107.refs_3_ = f32[896,128]{1,0:T(8,128)S(1)} custom-call(bf16[64,8192]{1,0:T(8,128)(2,1)S(1)} %collective-permute-done.16.refs_0_.refs_1_, bf16[64,8192]{1,0:T(8,128)(2,1)S(1)} %collective-permute-done.17.refs_1_.refs_2_, bf16[224,8192]{1,0:T(8,128)(2,1)S(1)} %copy-done, bf16[224,8192]{1,0:T(8,128)(2,1)} %collective-permute-done.5.refs_3_, ...), custom_call_target="tpu_custom_call" | custom-call | flops 1879048192 | bytes 29360128 | tf_op jit(solution)/shard_map/pallas_call | solution.py:153
  83.0 5.6 %shard_map.108 = (bf16[64,8192]{1,0:T(8,128)(2,1)S(1)}, bf16[64,8192]{1,0:T(8,128)(2,1)S(1)}) custom-call(s32[5]{0:T(128)S(1)} %stack.35.place.refs_0_, bf16[64,8192]{1,0:T(8,128)(2,1)S(1)} %collective-permute-done.16.refs_0_.refs_1_, bf16[64,8192]{1,0:T(8,128)(2,1)S(1)} %collective-permute-done.17.refs_1_.refs_2_, f32[896,128]{1,0:T(8,128)S(1)} %shard_map.107.refs_3_, ...), custom_call_target="tpu_custom_call" | custom-call | flops 1342177280 | bytes 20971520 | tf_op jit(solution)/shard_map/pallas_call | solution.py:167
  88.7 1.5 %collective-permute-start.19 = (bf16[64,8192]{1,0:T(8,128)(2,1)S(1)}, bf16[64,8192]{1,0:T(8,128)(2,1)S(1)}, u32[]{:S(2)}, u32[]{:S(2)}) collective-permute-start(bf16[64,8192]{1,0:T(8,128)(2,1)S(1)} %get-tuple-element.56), channel_id=1, source_target_pairs={{0,48},{1,13},{2,50},{3,15},{4,52},{5,9},{6,54},{7,11},{8,56},{9,5... | collective-permute-start | bytes 3145736 | tf_op jit(solution)/shard_map/ppermute | solution.py:48
  90.2 0.5 collective-permute-done.15.b
  90.9 11.8 %collective-permute-done.18.b1 = bf16[64,8192]{1,0:T(8,128)(2,1)S(1)} collective-permute-done((bf16[64,8192]{1,0:T(8,128)(2,1)S(1)}, bf16[64,8192]{1,0:T(8,128)(2,1)S(1)}, u32[]{:S(2)}, u32[]{:S(2)}) %collective-permute-start.18) | collective-permute-done | bytes 1048608 | tf_op jit(solution)/shard_map/ppermute | solution.py:48
  102.6 1.3 %collective-permute-done.19.b3 = bf16[64,8192]{1,0:T(8,128)(2,1)S(1)} collective-permute-done((bf16[64,8192]{1,0:T(8,128)(2,1)S(1)}, bf16[64,8192]{1,0:T(8,128)(2,1)S(1)}, u32[]{:S(2)}, u32[]{:S(2)}) %collective-permute-start.19) | collective-permute-done | bytes 1048608 | tf_op jit(solution)/shard_map/ppermute | solution.py:48
  104.2 0.9 collective-permute-start.20
  105.1 2.8 %collective-permute-start.21 = (bf16[16,8192]{1,0:T(8,128)(2,1)S(1)}, bf16[16,8192]{1,0:T(8,128)(2,1)S(1)}, u32[]{:S(2)}, u32[]{:S(2)}) collective-permute-start(bf16[16,8192]{1,0:T(8,128)(2,1)S(1)} %get-tuple-element.59), channel_id=1, source_target_pairs={{0,8},{1,33},{2,10},{3,35},{4,12},{5,37},{6,14},{7,39},{8,0},{9,41... | collective-permute-start | bytes 786440 | tf_op jit(solution)/shard_map/ppermute | solution.py:48
  108.2 1.4 %collective-permute-done.20.b1 = bf16[16,8192]{1,0:T(8,128)(2,1)S(1)} collective-permute-done((bf16[16,8192]{1,0:T(8,128)(2,1)S(1)}, bf16[16,8192]{1,0:T(8,128)(2,1)S(1)}, u32[]{:S(2)}, u32[]{:S(2)}) %collective-permute-start.20) | collective-permute-done | bytes 262176 | tf_op jit(solution)/shard_map/ppermute | solution.py:48
  109.5 5.2 %collective-permute-done.21.b2 = bf16[16,8192]{1,0:T(8,128)(2,1)S(1)} collective-permute-done((bf16[16,8192]{1,0:T(8,128)(2,1)S(1)}, bf16[16,8192]{1,0:T(8,128)(2,1)S(1)}, u32[]{:S(2)}, u32[]{:S(2)}) %collective-permute-start.21) | collective-permute-done | bytes 262176 | tf_op jit(solution)/shard_map/ppermute | solution.py:48
  114.8 2.6 %collective-permute-done.22.b3 = bf16[16,8192]{1,0:T(8,128)(2,1)S(1)} collective-permute-done((bf16[16,8192]{1,0:T(8,128)(2,1)S(1)}, bf16[16,8192]{1,0:T(8,128)(2,1)S(1)}, u32[]{:S(2)}, u32[]{:S(2)}) %collective-permute-start.22) | collective-permute-done | bytes 262176 | tf_op jit(solution)/shard_map/ppermute | solution.py:48
  117.4 0.7 shard_map.110
  118.1 2.2 %collective-permute-start.25 = (bf16[8,4096]{1,0:T(8,128)(2,1)S(1)}, bf16[8,4096]{1,0:T(8,128)(2,1)S(1)}, u32[]{:S(2)}, u32[]{:S(2)}) collective-permute-start(bf16[8,4096]{1,0:T(8,128)(2,1)S(1)} %get-tuple-element.64), channel_id=1, source_target_pairs={{0,66},{1,67},{2,64},{3,65},{4,70},{5,71},{6,68},{7,69},{8,74},{9,... | collective-permute-start | bytes 196616 | tf_op jit(solution)/shard_map/ppermute | solution.py:48
  120.3 1.1 collective-permute-start.23
  121.4 1.1 collective-permute-done.25
  122.5 2.6 %collective-permute-done.24 = bf16[8,4096]{1,0:T(8,128)(2,1)S(1)} collective-permute-done((bf16[8,4096]{1,0:T(8,128)(2,1)S(1)}, bf16[8,4096]{1,0:T(8,128)(2,1)S(1)}, u32[]{:S(2)}, u32[]{:S(2)}) %collective-permute-start.24) | collective-permute-done | bytes 65568 | tf_op jit(solution)/shard_map/ppermute | solution.py:48
  125.1 3.3 %collective-permute-start.26 = (bf16[8,2048]{1,0:T(8,128)(2,1)S(1)}, bf16[8,2048]{1,0:T(8,128)(2,1)S(1)}, u32[]{:S(2)}, u32[]{:S(2)}) collective-permute-start(bf16[8,2048]{1,0:T(8,128)(2,1)S(1)} %get-tuple-element.66), channel_id=1, source_target_pairs={{0,1},{1,0},{2,3},{3,2},{4,5},{5,4},{6,7},{7,6},{8,9},{9,8},{10,11... | collective-permute-start | bytes 98312 | tf_op jit(solution)/shard_map/ppermute | solution.py:48
  128.4 0.9 collective-permute-done.26
  129.2 0.6 maximum_select_fusion.1
  (39 shorter events, 2.2 us)
Async XLA Ops:
  0.8 2.4 %collective-permute-start = (bf16[8,2048]{1,0:T(8,128)(2,1)S(1)}, bf16[8,2048]{1,0:T(8,128)(2,1)S(1)}, u32[]{:S(2)}, u32[]{:S(2)}) collective-permute-start(bf16[8,2048]{1,0:T(8,128)(2,1)S(1)} %get-tuple-element.68), channel_id=1, source_target_pairs={{0,1},{1,0},{2,3},{3,2},{4,5},{5,4},{6,7},{7,6},{8,9},{9,8},{10,11... | collective-permute-start | bytes 98312 | tf_op jit(solution)/shard_map/ppermute | solution.py:48
  3.2 12.4 %collective-permute-start.5 = (bf16[224,8192]{1,0:T(8,128)(2,1)}, bf16[224,8192]{1,0:T(8,128)(2,1)}, u32[]{:S(2)}, u32[]{:S(2)}) collective-permute-start(bf16[224,8192]{1,0:T(8,128)(2,1)} %refs_2_.3), channel_id=1, source_target_pairs={{0,1},{1,0},{2,3},{3,2},{4,5},{5,4},{6,7},{7,6},{8,9},{9,8},{10,11... | collective-permute-start | bytes 11010056 | tf_op jit(solution)/shard_map/ppermute | solution.py:48
  4.4 10.5 %collective-permute-start.1 = (bf16[8,4096]{1,0:T(8,128)(2,1)S(1)}, bf16[8,4096]{1,0:T(8,128)(2,1)S(1)}, u32[]{:S(2)}, u32[]{:S(2)}) collective-permute-start(bf16[8,4096]{1,0:T(8,128)(2,1)S(1)} %maximum_select_fusion.wide), channel_id=1, source_target_pairs={{0,2},{1,3},{2,0},{3,1},{4,6},{5,7},{6,4},{7,5},{8,10},{9,11},{10,... | collective-permute-start | bytes 196616 | tf_op jit(solution)/shard_map/ppermute | solution.py:48
  6.2 8.7 %collective-permute-start.2 = (bf16[8,4096]{1,0:T(8,128)(2,1)S(1)}, bf16[8,4096]{1,0:T(8,128)(2,1)S(1)}, u32[]{:S(2)}, u32[]{:S(2)}) collective-permute-start(bf16[8,4096]{1,0:T(8,128)(2,1)S(1)} %maximum_select_fusion.wide), channel_id=1, source_target_pairs={{0,64},{1,65},{2,66},{3,67},{4,68},{5,69},{6,70},{7,71},{8,72},{9,... | collective-permute-start | bytes 196616 | tf_op jit(solution)/shard_map/ppermute | solution.py:48
  9.5 5.4 %collective-permute-start.3 = (bf16[8,4096]{1,0:T(8,128)(2,1)S(1)}, bf16[8,4096]{1,0:T(8,128)(2,1)S(1)}, u32[]{:S(2)}, u32[]{:S(2)}) collective-permute-start(bf16[8,4096]{1,0:T(8,128)(2,1)S(1)} %maximum_select_fusion.wide), channel_id=1, source_target_pairs={{0,66},{1,67},{2,64},{3,65},{4,70},{5,71},{6,68},{7,69},{8,74},{9,... | collective-permute-start | bytes 196616 | tf_op jit(solution)/shard_map/ppermute | solution.py:48
  9.5 5.4 %collective-permute-start.4 = (bf16[96,256]{1,0:T(8,128)(2,1)S(1)}, bf16[96,256]{1,0:T(8,128)(2,1)S(1)}, u32[]{:S(2)}, u32[]{:S(2)}) collective-permute-start(bf16[96,256]{1,0:T(8,128)(2,1)S(1)} %bitcast.19), channel_id=1, source_target_pairs={{0,66},{1,67},{2,64},{3,65},{4,70},{5,71},{6,68},{7,69},{8,74},{9,... | collective-permute-start | bytes 147464 | tf_op jit(solution)/shard_map/ppermute | solution.py:48
  12.3 48.8 %copy-start = (bf16[224,8192]{1,0:T(8,128)(2,1)S(1)}, bf16[224,8192]{1,0:T(8,128)(2,1)}, u32[]{:S(2)}) copy-start(bf16[224,8192]{1,0:T(8,128)(2,1)} %refs_2_.3) | copy-start | bytes 11010052
  15.5 17.3 %collective-permute-start.9 = (bf16[224,8192]{1,0:T(8,128)(2,1)}, bf16[224,8192]{1,0:T(8,128)(2,1)S(1)}, u32[]{:S(2)}, u32[]{:S(2)}) collective-permute-start(bf16[224,8192]{1,0:T(8,128)(2,1)} %refs_4_.6), channel_id=1, source_target_pairs={{0,1},{1,0},{2,3},{3,2},{4,5},{5,4},{6,7},{7,6},{8,9},{9,8},{10,11... | collective-permute-start | bytes 11010056 | tf_op jit(solution)/shard_map/ppermute | solution.py:48
  17.1 6.6 %collective-permute-start.6 = (bf16[16,11264]{1,0:T(8,128)(2,1)S(1)}, bf16[16,11264]{1,0:T(8,128)(2,1)S(1)}, u32[]{:S(2)}, u32[]{:S(2)}) collective-permute-start(bf16[16,11264]{1,0:T(8,128)(2,1)S(1)} %shard_map.100.refs_0_), channel_id=1, source_target_pairs={{0,4},{1,17},{2,6},{3,19},{4,0},{5,21},{6,2},{7,23},{8,12},{9,25},... | collective-permute-start | bytes 1081352 | tf_op jit(solution)/shard_map/ppermute | solution.py:48
  18.4 11.6 %collective-permute-start.7 = (bf16[16,11264]{1,0:T(8,128)(2,1)S(1)}, bf16[16,11264]{1,0:T(8,128)(2,1)S(1)}, u32[]{:S(2)}, u32[]{:S(2)}) collective-permute-start(bf16[16,11264]{1,0:T(8,128)(2,1)S(1)} %shard_map.100.refs_0_), channel_id=1, source_target_pairs={{0,8},{1,33},{2,10},{3,35},{4,12},{5,37},{6,14},{7,39},{8,0},{9,41... | collective-permute-start | bytes 1081352 | tf_op jit(solution)/shard_map/ppermute | solution.py:48
  21.0 11.6 %collective-permute-start.8 = (bf16[16,11264]{1,0:T(8,128)(2,1)S(1)}, bf16[16,11264]{1,0:T(8,128)(2,1)S(1)}, u32[]{:S(2)}, u32[]{:S(2)}) collective-permute-start(bf16[16,11264]{1,0:T(8,128)(2,1)S(1)} %shard_map.100.refs_0_), channel_id=1, source_target_pairs={{0,12},{1,49},{2,14},{3,51},{4,8},{5,53},{6,10},{7,55},{8,4},{9,57... | collective-permute-start | bytes 1081352 | tf_op jit(solution)/shard_map/ppermute | solution.py:48
  32.8 36.5 %collective-permute-start.13 = (bf16[224,8192]{1,0:T(8,128)(2,1)}, bf16[224,8192]{1,0:T(8,128)(2,1)S(1)}, u32[]{:S(2)}, u32[]{:S(2)}) collective-permute-start(bf16[224,8192]{1,0:T(8,128)(2,1)} %refs_4_.7), channel_id=1, source_target_pairs={{0,1},{1,0},{2,3},{3,2},{4,5},{5,4},{6,7},{7,6},{8,9},{9,8},{10,11... | collective-permute-start | bytes 11010056 | tf_op jit(solution)/shard_map/ppermute | solution.py:48
  34.2 23.9 %collective-permute-start.12 = (bf16[64,11264]{1,0:T(8,128)(2,1)S(1)}, bf16[64,11264]{1,0:T(8,128)(2,1)S(1)}, u32[]{:S(2)}, u32[]{:S(2)}) collective-permute-start(bf16[64,11264]{1,0:T(8,128)(2,1)S(1)} %get-tuple-element.43), channel_id=1, source_target_pairs={{0,32},{1,9},{2,34},{3,11},{4,36},{5,13},{6,38},{7,15},{8,40},{9,1... | collective-permute-start | bytes 4325384 | tf_op jit(solution)/shard_map/ppermute | solution.py:48
  35.5 21.3 %collective-permute-start.10 = (bf16[64,3072]{1,0:T(8,128)(2,1)S(1)}, bf16[64,3072]{1,0:T(8,128)(2,1)S(1)}, u32[]{:S(2)}, u32[]{:S(2)}) collective-permute-start(bf16[64,3072]{1,0:T(8,128)(2,1)S(1)} %get-tuple-element.42.own), channel_id=1, source_target_pairs={{0,16},{1,5},{2,18},{3,7},{4,20},{5,1},{6,22},{7,3},{8,24},{9,13},... | collective-permute-start | bytes 1179656 | tf_op jit(solution)/shard_map/ppermute | solution.py:48
  35.8 22.3 %collective-permute-start.11 = (bf16[64,3072]{1,0:T(8,128)(2,1)S(1)}, bf16[64,3072]{1,0:T(8,128)(2,1)S(1)}, u32[]{:S(2)}, u32[]{:S(2)}) collective-permute-start(bf16[64,3072]{1,0:T(8,128)(2,1)S(1)} %get-tuple-element.42.own), channel_id=1, source_target_pairs={{0,48},{1,13},{2,50},{3,15},{4,52},{5,9},{6,54},{7,11},{8,56},{9,5... | collective-permute-start | bytes 1179656 | tf_op jit(solution)/shard_map/ppermute | solution.py:48
  37.4 0.8 copy-start.4
  38.2 0.8 copy-start.5
  38.9 0.8 copy-start.6
  58.2 11.1 %collective-permute-start.14 = (bf16[256,3328]{1,0:T(8,128)(2,1)S(1)}, bf16[256,3328]{1,0:T(8,128)(2,1)S(1)}, u32[]{:S(2)}, u32[]{:S(2)}) collective-permute-start(bf16[256,3328]{1,0:T(8,128)(2,1)S(1)} %get-tuple-element.49.refs_6_), channel_id=1, source_target_pairs={{0,1},{1,0},{2,3},{3,2},{4,5},{5,4},{6,7},{7,6},{8,9},{9,8},{10,11... | collective-permute-start | bytes 5111816 | tf_op jit(solution)/shard_map/ppermute | solution.py:48
  59.7 17.3 %collective-permute-start.16 = (bf16[64,8192]{1,0:T(8,128)(2,1)S(1)}, bf16[64,8192]{1,0:T(8,128)(2,1)S(1)}, u32[]{:S(2)}, u32[]{:S(2)}) collective-permute-start(bf16[64,8192]{1,0:T(8,128)(2,1)S(1)} %get-tuple-element.52.refs_0_.refs_1_), channel_id=1, source_target_pairs={{0,16},{1,5},{2,18},{3,7},{4,20},{5,1},{6,22},{7,3},{8,24},{9,13},... | collective-permute-start | bytes 3145736 | tf_op jit(solution)/shard_map/ppermute | solution.py:48
  59.7 17.3 %collective-permute-start.17 = (bf16[64,8192]{1,0:T(8,128)(2,1)S(1)}, bf16[64,8192]{1,0:T(8,128)(2,1)S(1)}, u32[]{:S(2)}, u32[]{:S(2)}) collective-permute-start(bf16[64,8192]{1,0:T(8,128)(2,1)S(1)} %get-tuple-element.52.refs_0_.refs_1_), channel_id=1, source_target_pairs={{0,48},{1,13},{2,50},{3,15},{4,52},{5,9},{6,54},{7,11},{8,56},{9,5... | collective-permute-start | bytes 3145736 | tf_op jit(solution)/shard_map/ppermute | solution.py:48
  61.2 2.0 %copy-start.1 = (bf16[224,8192]{1,0:T(8,128)(2,1)S(1)}, bf16[224,8192]{1,0:T(8,128)(2,1)}, u32[]{:S(2)}) copy-start(bf16[224,8192]{1,0:T(8,128)(2,1)} %refs_4_.6) | copy-start | bytes 11010052
  63.2 6.2 %copy-start.3 = (bf16[224,8192]{1,0:T(8,128)(2,1)S(1)}, bf16[224,8192]{1,0:T(8,128)(2,1)}, u32[]{:S(2)}) copy-start(bf16[224,8192]{1,0:T(8,128)(2,1)} %refs_4_.7) | copy-start | bytes 11010052
  69.3 7.7 %copy-start.2 = (bf16[224,8192]{1,0:T(8,128)(2,1)S(1)}, bf16[224,8192]{1,0:T(8,128)(2,1)}, u32[]{:S(2)}) copy-start(bf16[224,8192]{1,0:T(8,128)(2,1)} %refs_4_.6) | copy-start | bytes 11010052
  75.0 15.7 %collective-permute-start.15 = (bf16[64,8192]{1,0:T(8,128)(2,1)S(1)}, bf16[64,8192]{1,0:T(8,128)(2,1)S(1)}, u32[]{:S(2)}, u32[]{:S(2)}) collective-permute-start(bf16[64,8192]{1,0:T(8,128)(2,1)S(1)} %get-tuple-element.51), channel_id=1, source_target_pairs={{0,32},{1,9},{2,34},{3,11},{4,36},{5,13},{6,38},{7,15},{8,40},{9,1... | collective-permute-start | bytes 3145736 | tf_op jit(solution)/shard_map/ppermute | solution.py:48
  88.6 14.0 %collective-permute-start.18 = (bf16[64,8192]{1,0:T(8,128)(2,1)S(1)}, bf16[64,8192]{1,0:T(8,128)(2,1)S(1)}, u32[]{:S(2)}, u32[]{:S(2)}) collective-permute-start(bf16[64,8192]{1,0:T(8,128)(2,1)S(1)} %get-tuple-element.55), channel_id=1, source_target_pairs={{0,16},{1,5},{2,18},{3,7},{4,20},{5,1},{6,22},{7,3},{8,24},{9,13},... | collective-permute-start | bytes 3145736 | tf_op jit(solution)/shard_map/ppermute | solution.py:48
  88.7 15.2 %collective-permute-start.19 = (bf16[64,8192]{1,0:T(8,128)(2,1)S(1)}, bf16[64,8192]{1,0:T(8,128)(2,1)S(1)}, u32[]{:S(2)}, u32[]{:S(2)}) collective-permute-start(bf16[64,8192]{1,0:T(8,128)(2,1)S(1)} %get-tuple-element.56), channel_id=1, source_target_pairs={{0,48},{1,13},{2,50},{3,15},{4,52},{5,9},{6,54},{7,11},{8,56},{9,5... | collective-permute-start | bytes 3145736 | tf_op jit(solution)/shard_map/ppermute | solution.py:48
  104.2 5.3 %collective-permute-start.20 = (bf16[16,8192]{1,0:T(8,128)(2,1)S(1)}, bf16[16,8192]{1,0:T(8,128)(2,1)S(1)}, u32[]{:S(2)}, u32[]{:S(2)}) collective-permute-start(bf16[16,8192]{1,0:T(8,128)(2,1)S(1)} %get-tuple-element.58), channel_id=1, source_target_pairs={{0,4},{1,17},{2,6},{3,19},{4,0},{5,21},{6,2},{7,23},{8,12},{9,25},... | collective-permute-start | bytes 786440 | tf_op jit(solution)/shard_map/ppermute | solution.py:48
  105.1 9.7 %collective-permute-start.21 = (bf16[16,8192]{1,0:T(8,128)(2,1)S(1)}, bf16[16,8192]{1,0:T(8,128)(2,1)S(1)}, u32[]{:S(2)}, u32[]{:S(2)}) collective-permute-start(bf16[16,8192]{1,0:T(8,128)(2,1)S(1)} %get-tuple-element.59), channel_id=1, source_target_pairs={{0,8},{1,33},{2,10},{3,35},{4,12},{5,37},{6,14},{7,39},{8,0},{9,41... | collective-permute-start | bytes 786440 | tf_op jit(solution)/shard_map/ppermute | solution.py:48
  107.9 9.5 %collective-permute-start.22 = (bf16[16,8192]{1,0:T(8,128)(2,1)S(1)}, bf16[16,8192]{1,0:T(8,128)(2,1)S(1)}, u32[]{:S(2)}, u32[]{:S(2)}) collective-permute-start(bf16[16,8192]{1,0:T(8,128)(2,1)S(1)} %get-tuple-element.60), channel_id=1, source_target_pairs={{0,12},{1,49},{2,14},{3,51},{4,8},{5,53},{6,10},{7,55},{8,4},{9,57... | collective-permute-start | bytes 786440 | tf_op jit(solution)/shard_map/ppermute | solution.py:48
  118.1 4.4 %collective-permute-start.25 = (bf16[8,4096]{1,0:T(8,128)(2,1)S(1)}, bf16[8,4096]{1,0:T(8,128)(2,1)S(1)}, u32[]{:S(2)}, u32[]{:S(2)}) collective-permute-start(bf16[8,4096]{1,0:T(8,128)(2,1)S(1)} %get-tuple-element.64), channel_id=1, source_target_pairs={{0,66},{1,67},{2,64},{3,65},{4,70},{5,71},{6,68},{7,69},{8,74},{9,... | collective-permute-start | bytes 196616 | tf_op jit(solution)/shard_map/ppermute | solution.py:48
  120.3 4.7 %collective-permute-start.24 = (bf16[8,4096]{1,0:T(8,128)(2,1)S(1)}, bf16[8,4096]{1,0:T(8,128)(2,1)S(1)}, u32[]{:S(2)}, u32[]{:S(2)}) collective-permute-start(bf16[8,4096]{1,0:T(8,128)(2,1)S(1)} %get-tuple-element.63), channel_id=1, source_target_pairs={{0,64},{1,65},{2,66},{3,67},{4,68},{5,69},{6,70},{7,71},{8,72},{9,... | collective-permute-start | bytes 196616 | tf_op jit(solution)/shard_map/ppermute | solution.py:48
  120.3 4.7 %collective-permute-start.23 = (bf16[8,4096]{1,0:T(8,128)(2,1)S(1)}, bf16[8,4096]{1,0:T(8,128)(2,1)S(1)}, u32[]{:S(2)}, u32[]{:S(2)}) collective-permute-start(bf16[8,4096]{1,0:T(8,128)(2,1)S(1)} %get-tuple-element.62), channel_id=1, source_target_pairs={{0,2},{1,3},{2,0},{3,1},{4,6},{5,7},{6,4},{7,5},{8,10},{9,11},{10,... | collective-permute-start | bytes 196616 | tf_op jit(solution)/shard_map/ppermute | solution.py:48
  125.1 4.1 %collective-permute-start.26 = (bf16[8,2048]{1,0:T(8,128)(2,1)S(1)}, bf16[8,2048]{1,0:T(8,128)(2,1)S(1)}, u32[]{:S(2)}, u32[]{:S(2)}) collective-permute-start(bf16[8,2048]{1,0:T(8,128)(2,1)S(1)} %get-tuple-element.66), channel_id=1, source_target_pairs={{0,1},{1,0},{2,3},{3,2},{4,5},{5,4},{6,7},{7,6},{8,9},{9,8},{10,11... | collective-permute-start | bytes 98312 | tf_op jit(solution)/shard_map/ppermute | solution.py:48

commit v4 on v3

v4 whole, which is shorter than its diff:
```python
import itertools

import jax
import jax.numpy as jnp
from jax import lax
from jax.experimental import pallas as pl
from jax.experimental.pallas import tpu as pltpu
from jax.sharding import Mesh, PartitionSpec as P

AXES = ("zh", "y", "x", "zl", "c")
SIZES = (2, 4, 4, 2, 2)
adapter_scale = 0.5
WIDTH = 8192
HALF = WIDTH // 2
QUARTER = WIDTH // 4
UNITS = 224
TILE = 4096
STEPS = WIDTH // TILE
PARTS = TILE // 256
f32, bf16 = jnp.float32, jnp.bfloat16
SMALL = pl.CostEstimate(flops=1, bytes_accessed=1, transcendentals=0)


def index(zh, y, x, zl, c):
    return (((zh * 4 + y) * 4 + x) * 2 + zl) * 2 + c


def pairs(partner):
    out = []
    for zh, y, x, zl, c in itertools.product(*map(range, SIZES)):
        z, y2, x2, c2 = partner(zh * 2 + zl, y, x, c)
        out.append((index(zh, y, x, zl, c), index(z >> 1, y2, x2, z & 1, c2)))
    return out


CORE = pairs(lambda z, y, x, c: (z, y, x, 1 - c))
ALONG_Z = {k: pairs(lambda z, y, x, c: (z ^ k, y, x, c)) for k in (1, 2, 3)}
FIRST = {
    k: pairs(lambda z, y, x, c: (z, y ^ k, x, c) if c else (z, y, x ^ k, c))
    for k in (1, 2, 3)
}
SECOND = {
    k: pairs(lambda z, y, x, c: (z, y, x ^ k, c) if c else (z, y ^ k, x, c))
    for k in (1, 2, 3)
}


def send(value, route):
    return lax.ppermute(value, AXES, route)


def nt(a, b):
    return lax.dot_general(a, b, (((1,), (1,)), ((), ())), preferred_element_type=f32)


def tn(a, b):
    return lax.dot_general(a, b, (((0,), (0,)), ((), ())), preferred_element_type=f32)


def nn(a, b):
    return jnp.dot(a, b, preferred_element_type=f32)


def widen(a):
    return a.astype(f32)


def after(value, others):
    return lax.optimization_barrier((value, others))[0]


def project_kernel(n, *refs):
    rows, weights, out = refs[:n], refs[n : n + 4], refs[n + 4]
    for i in range(WIDTH // TILE):
        tile = slice(i * TILE, (i + 1) * TILE)
        x = jnp.concatenate([r[:, tile] for r in rows], axis=0)
        w = jnp.concatenate([r[:, tile] for r in weights], axis=0)
        if i == 0:
            out[...] = nt(w, x)
        else:
            out[...] += nt(w, x)


def down_kernel(n, place, *refs):
    rows = refs[:n]
    acc, down_w, down_w2, seconds, theirs = refs[n : n + 5]
    if place is None:
        first, second = refs[n + 5 : n + 7]
    else:
        sources = refs[n + 5 : n + 7]
        first, second = refs[2 * n + 7 : 2 * n + 9]
    outs = refs[n + 7 : 2 * n + 7]
    hidden = refs[-1]

    def shards_of(learner, to, groups, base):
        if place is None:
            return
        zh, y, x = learner // 16, (learner // 4) % 4, learner % 4
        dz, dy, dx = zh ^ place[0], y ^ place[1], x ^ place[2]
        for other, src in enumerate(sources):
            along_x = (place[3] ^ other) == 0
            near = jnp.where(along_x, dx, dy)
            far = jnp.where(along_x, dy, dx)
            r = pl.ds(pl.multiple_of((far * 4 + near) * 16, 16), 16)
            for k in range(groups):
                at = pl.multiple_of((base + k) * 512 + dz * 256, 256)
                row = (place[3] ^ other) * 32 + (k // 2) * 64 + (k % 2) * 16
                row = pl.ds(pl.multiple_of(row, 16), 16)
                to[row, learner * 256 : learner * 256 + 256] = src[r, pl.ds(at, 256)]

    low = 0.0
    for i in range(STEPS):
        tile = slice(i * TILE, (i + 1) * TILE)
        for j in range(PARTS):
            shards_of(i * PARTS + j, first, 4, 0)
        x = jnp.concatenate([r[:, tile] for r in rows], axis=0)
        low += nt(first[:, tile], x)

    u = (adapter_scale * low).astype(bf16)
    hs, back = [], 0.0
    for half, (ref, c) in enumerate(((seconds, 0), (theirs, 3072))):
        b = [ref[64 * k : 64 * k + 64, c : c + UNITS] for k in range(3)]
        at = half * UNITS
        g = acc[at : at + UNITS] + tn(b[0], u[:64])
        at += 2 * UNITS
        v = acc[at : at + UNITS] + tn(b[1], u[64:])
        h = g / (1.0 + jnp.exp(-g)) * v
        back += nn(b[2], h.astype(bf16))
        hs.append(h)
    h = jnp.concatenate([*hs, adapter_scale * back], axis=0)
    hidden[...] = h.T.astype(bf16)

    for i in range(STEPS):
        tile = slice(i * TILE, (i + 1) * TILE)
        for j in range(PARTS):
            shards_of(i * PARTS + j, second, 2, 4)
        w = jnp.concatenate([r[:, tile] for r in (down_w, down_w2, second)], axis=0)
        result = nn(hidden[...], w)
        for k, out in enumerate(outs):
            out[:, tile] = result[k * 64 : (k + 1) * 64].astype(out.dtype)


VMEM = pl.BlockSpec(memory_space=pltpu.VMEM)
SMEM = pl.BlockSpec(memory_space=pltpu.SMEM)


def in_vmem(operands):
    return [pltpu.with_memory_space_constraint(a, pltpu.VMEM) for a in operands]


def cost(macs):
    return pl.CostEstimate(flops=2 * macs, bytes_accessed=2 * macs // 64, transcendentals=0)


def project(rows, weights):
    n = len(rows)
    return pl.pallas_call(
        lambda *refs: project_kernel(n, *refs),
        in_specs=[VMEM] * (n + 4),
        out_specs=VMEM,
        out_shape=jax.ShapeDtypeStruct((4 * UNITS, 64 * n), f32),
        compiler_params=pltpu.CompilerParams(vmem_limit_bytes=10 * 1024 * 1024),
        cost_estimate=SMALL,
    )(*in_vmem([*rows, *weights]))


def down(place, rows, acc, weights, seconds, factors, kinds):
    n = len(rows)
    theirs = factors[1] if place is not None else seconds[1]
    operands = in_vmem([*rows, acc, *weights, seconds[0], theirs, *factors])
    shapes = [((64, WIDTH), kind) for kind in kinds]
    lead = []
    body = lambda *refs: down_kernel(n, None, *refs)
    if place is not None:
        lead = [place]
        body = lambda *refs: down_kernel(n, *refs)
        shapes += [((128, WIDTH), bf16), ((64, WIDTH), bf16)]
    return pl.pallas_call(
        body,
        in_specs=[SMEM] * len(lead) + [VMEM] * len(operands),
        out_specs=[VMEM] * len(shapes),
        out_shape=[jax.ShapeDtypeStruct(s, kind) for s, kind in shapes],
        scratch_shapes=[pltpu.VMEM((64 * n, 512), bf16)],
        compiler_params=pltpu.CompilerParams(vmem_limit_bytes=10 * 1024 * 1024),
        cost_estimate=SMALL,
    )(*lead, *operands)


def local(body, shapes, operands, place=None, price=SMALL, far=(), scratch=()):
    lead = [] if place is None else [place]
    return pl.pallas_call(
        body,
        in_specs=[SMEM] * len(lead)
        + [VMEM] * len(operands)
        + [pl.BlockSpec(memory_space=pltpu.HBM)] * len(far),
        out_specs=[VMEM] * len(shapes),
        out_shape=[jax.ShapeDtypeStruct(s, kind) for s, kind in shapes],
        scratch_shapes=list(scratch),
        compiler_params=pltpu.CompilerParams(vmem_limit_bytes=6 * 1024 * 1024),
        cost_estimate=price,
    )(*lead, *operands, *far)


def shape_kernel(place, own, other, gate, up, down, wide, message, ranks, sems):
    c = place[3]
    half = pl.ds(pl.multiple_of(c * 32, 32), 32)
    copies = [
        pltpu.make_async_copy(r.at[half, :], ranks.at[k], sems.at[k])
        for k, r in enumerate((gate, up, down))
    ]
    for copy in copies:
        copy.start()
    wide[:, pl.ds(pl.multiple_of(c * QUARTER, QUARTER), QUARTER)] = own[...]
    wide[:, pl.ds(pl.multiple_of((1 - c) * QUARTER, QUARTER), QUARTER)] = other[...]
    rows = widen(wide[...])
    rows = jnp.concatenate([rows[:, :QUARTER], rows[:, QUARTER:]], axis=0)
    message[:, :QUARTER] = rows.astype(bf16)
    for copy in copies:
        copy.wait()
    for i in range(6):
        col = QUARTER + 256 * i
        message[:, col : col + 256] = ranks[i // 2, (i % 2) * 16 : (i % 2) * 16 + 16, :]


def pack_kernel(place, wide, z1, z2, message, far_message, out):
    zl = place[4]
    here = pl.ds(pl.multiple_of(zl * HALF, HALF), HALF)
    there = pl.ds(pl.multiple_of((1 - zl) * HALF, HALF), HALF)
    z3 = widen(far_message[:, :QUARTER])
    z3 = jnp.concatenate([z3[:8], z3[8:]], axis=1)
    pair = lambda a, b: jnp.concatenate([widen(a), widen(b)], 0).astype(bf16)
    out[:, here] = pair(wide[...], z2[...])
    out[:, there] = pair(z1[...], z3)
    for i in range(6):
        at, col = WIDTH + 512 * i, QUARTER + 256 * i
        out[:, at : at + 256] = message[:, col : col + 256]
        out[:, at + 256 : at + 512] = far_message[:, col : col + 256]


def unpack_kernel(*refs):
    got, (block, factor, packed) = refs[:4], refs[4:]
    for k, g in enumerate(got):
        at = slice(16 * k, 16 * k + 16)
        block[at, :] = g[:, :WIDTH]
        factor[at, :] = g[:, WIDTH:]
        packed[at, :] = g[...]


def seconds_kernel(gate_w, up_w, down_w, gate, up, down, out):
    out[...] = jnp.zeros_like(out)
    for k, r in enumerate((gate, up, down)):
        out[64 * k : 64 * k + 64, :UNITS] = r[...]


def stack_kernel(own, packed1, f2, packed3, seconds, out):
    for k, r in enumerate((own, packed1, f2, packed3)):
        out[64 * k : 64 * k + 64, :3072] = r[:, -3072:]
    out[:, 3072:] = seconds[...]


def add_kernel(own, b1, b3, out):
    out[...] = own[...] + widen(b1[...]) + widen(b3[...])


def sum_kernel(own, b, keep, s1, s2, s3):
    for k, out in enumerate((keep, s1, s2, s3)):
        part = slice(16 * k, 16 * k + 16)
        out[...] = (own[part, :] + widen(b[part, :])).astype(out.dtype)


def split_kernel(place, own, b1, b2, b3, keep, s1, s2, s3):
    zl = place[4]
    here = pl.ds(pl.multiple_of(zl * HALF, HALF), HALF)
    there = pl.ds(pl.multiple_of((1 - zl) * HALF, HALF), HALF)
    for cols, near, far in ((here, keep, s2), (there, s1, s3)):
        total = own[:, cols]
        for b in (b1, b2, b3):
            total += widen(b[:, cols])
        near[...] = total[:8].astype(near.dtype)
        far[...] = total[8:].astype(far.dtype)


def shards(
    inputs,
    frozen_gate_weight,
    frozen_up_weight,
    frozen_down_weight,
    adapter_first_gate,
    adapter_second_gate,
    adapter_first_up,
    adapter_second_up,
    adapter_first_down,
    adapter_second_down,
):
    zh, y, x, zl, c = (lax.axis_index(a) for a in AXES)
    place = jnp.stack([zh, y, x, c, zl]).astype(jnp.int32)

    def ordered(flag, a, b, axis):
        return jnp.where(
            flag == 0, jnp.concatenate([a, b], axis), jnp.concatenate([b, a], axis)
        )

    own = jnp.where(c == 0, inputs[0], inputs[1])
    other = jnp.where(c == 0, inputs[1], inputs[0])
    wide, message = local(
        shape_kernel,
        [((8, HALF), bf16), ((16, QUARTER + 1536), bf16)],
        (own, send(other, CORE)),
        place,
        far=(adapter_first_gate, adapter_first_up, adapter_second_down),
        scratch=[pltpu.VMEM((3, 32, 256), bf16), pltpu.SemaphoreType.DMA((3,))],
    )

    z1, z2, z3 = (
        send(v, ALONG_Z[k]) for k, v in ((1, wide), (2, wide), (3, message))
    )
    gate2 = send(after(frozen_gate_weight, wide), CORE)
    up2 = send(after(frozen_up_weight, wide), CORE)
    (packed,) = local(
        pack_kernel,
        [((16, WIDTH + 3072), bf16)],
        (wide, z1, z2, message, z3),
        place,
    )

    packed = after(packed, gate2)
    got = [packed] + [send(packed, FIRST[k]) for k in (1, 2, 3)]
    down2 = send(after(frozen_down_weight, packed), CORE)
    block, factor, packed = local(
        unpack_kernel,
        [((64, WIDTH), bf16), ((64, 3072), bf16), ((64, WIDTH + 3072), bf16)],
        got,
    )
    block, factor, packed = after((block, factor, packed), (up2, down2))

    packed1, packed3 = send(packed, SECOND[1]), send(packed, SECOND[3])
    factor_2 = send(factor, SECOND[2])
    seconds = (adapter_second_gate, adapter_second_up, adapter_first_down)
    owned, seconds = after(
        ((frozen_gate_weight, frozen_up_weight, frozen_down_weight), seconds), packed
    )
    (seconds,) = local(
        seconds_kernel, [((256, 256), bf16)], [*in_vmem(owned), *(a.T for a in seconds)]
    )
    (factor,) = local(
        stack_kernel,
        [((256, 3072 + 256), bf16)],
        (factor, packed1, factor_2, packed3, seconds),
    )
    factor2 = send(factor, CORE)
    rows2 = send(after(block, factor), SECOND[2])

    weights = (owned[0], gate2, owned[1], up2)
    down_weights = (owned[2], down2)

    rows = (block, packed1, packed3)
    acc = project(rows, weights)
    total, part1, part3, first, second = down(
        place, rows, acc, down_weights, (seconds, factor2), (factor, factor2),
        (f32, bf16, bf16),
    )
    back1, back3 = send(part1, SECOND[1]), send(part3, SECOND[3])
    rows = (after(rows2, part1),)
    acc = project(rows, weights)
    (part2,) = down(
        None, rows, acc, down_weights, (seconds, factor2), (first, second), (bf16,)
    )
    back2 = send(part2, SECOND[2])
    (total,) = local(
        add_kernel,
        [((64, WIDTH), f32)],
        (total, back1, back3),
        price=cost(64 * WIDTH * 64 * 16),
    )
    small = [((16, WIDTH), f32)] + [((16, WIDTH), bf16)] * 3
    mine, *parts = local(sum_kernel, small, (total, back2))
    backs = [send(p, FIRST[k]) for k, p in zip((1, 2, 3), parts, strict=True)]
    small = [((8, HALF), f32)] + [((8, HALF), bf16)] * 3
    done, *parts = local(split_kernel, small, (mine, *backs), place)
    for k, p in zip((1, 2, 3), parts, strict=True):
        done = done + widen(send(p, ALONG_Z[k]))
    done = done.astype(bf16)
    keep = jnp.where(c == 0, done[:, :2048], done[:, 2048:])
    give = jnp.where(c == 0, done[:, 2048:], done[:, :2048])
    got = send(give, CORE)
    return ordered(c, keep[None], got[None], 0)


def solution(mesh):
    fine = Mesh(mesh.devices.reshape(SIZES), AXES)
    learner, tensor = ("zh", "y", "x"), ("zl", "c")
    in_specs = (
        P(None, learner, tensor),
        P(AXES, None),
        P(AXES, None),
        P(AXES, None),
        P(None, learner),
        P(AXES, None),
        P(None, learner),
        P(AXES, None),
        P(AXES, None),
        P(None, learner),
    )
    return jax.shard_map(
        shards,
        mesh=fine,
        in_specs=in_specs,
        out_specs=P(None, learner, tensor),
        check_vma=False,
    )
```

time: 130 us -> 125 us (0.962)
  Pallas kernels: 25.4 us -> 20.5 us
  local copies, waits for them, and re-layouts: 4.41 us -> 8.49 us
  starting transfers between devices: 36.9 us -> 34 us
    unnamed x14 -> x24, local copies, waits for them, and re-layouts: 4.32 us -> 8.41 us
    pallas_call x2, Pallas kernels: 12.1 us -> 8.14 us  [project(): pl.pallas_call(lambda *refs: project_kernel(n, *refs), in_specs=[VMEM] *...]
    ppermute x27 -> x25, starting transfers between devices: 36.9 us -> 34 us  [send(): return lax.ppermute(value, AXES, route)]
    pallas_call x2, Pallas kernels: 11.2 us -> 9.61 us  [down(): pl.pallas_call(body, in_specs=[SMEM] * len(lead) + [VMEM] * len(operands)...]
    ppermute x27 -> x25, waiting for transfers between devices: 60.7 us -> 60 us  [send(): return lax.ppermute(value, AXES, route)]
    pallas_call x7 -> x8, Pallas kernels: 2.09 us -> 2.71 us  [local(): pl.pallas_call(body, in_specs=[SMEM] * len(lead) + [VMEM] * len(operands)...]
  transfers between devices with their start and end apart: 27 -> 25, of which waited for: 16 -> 19; matrix products, arithmetic and copies ran while one was open for 1% -> 0% of each run, Pallas kernels for 19% -> 15%
where the time goes in v4:
time: 125 us
  waiting for transfers between devices  60 us (48%)
  starting transfers between devices  34 us (27%)
  Pallas kernels  20.5 us (16%)
  local copies, waits for them, and re-layouts  8.49 us (7%)
  other arithmetic  1.5 us (1%)
    ppermute x25, waiting for transfers between devices, send(): return lax.ppermute(value, AXES, route)  60 us
    ppermute x25, starting transfers between devices, send(): return lax.ppermute(value, AXES, route)  34 us
    pallas_call x2, Pallas kernels, down(): pl.pallas_call(body, in_specs=[SMEM] * len(lead) + [VMEM] * len(operands)...  9.61 us
    unnamed x24, local copies, waits for them, and re-layouts  8.41 us
    pallas_call x2, Pallas kernels, project(): pl.pallas_call(lambda *refs: project_kernel(n, *refs), in_specs=[VMEM] *...  8.14 us
    pallas_call x8, Pallas kernels, local(): pl.pallas_call(body, in_specs=[SMEM] * len(lead) + [VMEM] * len(operands)...  2.71 us
  transfers between devices with their start and end apart: 25, of which 19 were waited for; matrix products, arithmetic and copies ran while one was open for 0% of the time, Pallas kernels for 15%

profile of v4, /device:TPU:1, one launch (start us, length us, event | category | flops | bytes accessed | tf_op | source)
XLA Modules:
  0.0 124.7 jit_solution(4657259000346369742)
XLA Ops:
  0.0 0.8 select_bitcast_fusion.1
  0.8 1.5 %collective-permute-start = (bf16[8,2048]{1,0:T(8,128)(2,1)S(1)}, bf16[8,2048]{1,0:T(8,128)(2,1)S(1)}, u32[]{:S(2)}, u32[]{:S(2)}) collective-permute-start(bf16[8,2048]{1,0:T(8,128)(2,1)S(1)} %get-tuple-element.73), channel_id=1, source_target_pairs={{0,1},{1,0},{2,3},{3,2},{4,5},{5,4},{6,7},{7,6},{8,9},{9,8},{10,11... | collective-permute-start | bytes 98312 | tf_op jit(solution)/shard_map/ppermute | solution.py:49
  2.4 0.8 collective-permute-done.other
  3.2 0.8 copy-done.9
  3.9 0.8 copy-done.10
  4.7 0.8 copy-done.11
  5.4 0.7 shard_map.100
  6.5 3.9 %collective-permute-start.3 = (bf16[16,3584]{1,0:T(8,128)(2,1)S(1)}, bf16[16,3584]{1,0:T(8,128)(2,1)S(1)}, u32[]{:S(2)}, u32[]{:S(2)}) collective-permute-start(bf16[16,3584]{1,0:T(8,128)(2,1)S(1)} %get-tuple-element.39.message), channel_id=1, source_target_pairs={{0,66},{1,67},{2,64},{3,65},{4,70},{5,71},{6,68},{7,69},{8,74},{9,... | collective-permute-start | bytes 344072 | tf_op jit(solution)/shard_map/ppermute | solution.py:49
  10.4 1.2 collective-permute-start.2
  11.6 0.7 collective-permute-start.8
  12.3 1.5 %collective-permute-done.1.z1 = bf16[8,4096]{1,0:T(8,128)(2,1)S(1)} collective-permute-done((bf16[8,4096]{1,0:T(8,128)(2,1)S(1)}, bf16[8,4096]{1,0:T(8,128)(2,1)S(1)}, u32[]{:S(2)}, u32[]{:S(2)}) %collective-permute-start.1) | collective-permute-done | bytes 65568 | tf_op jit(solution)/shard_map/ppermute | solution.py:49
  13.8 1.2 collective-permute-done.2.z2
  15.6 1.7 %collective-permute-start.9 = (bf16[224,8192]{1,0:T(8,128)(2,1)}, bf16[224,8192]{1,0:T(8,128)(2,1)S(1)}, u32[]{:S(2)}, u32[]{:S(2)}) collective-permute-start(bf16[224,8192]{1,0:T(8,128)(2,1)} %refs_2_), channel_id=1, source_target_pairs={{0,1},{1,0},{2,3},{3,2},{4,5},{5,4},{6,7},{7,6},{8,9},{9,8},{10,11... | collective-permute-start | bytes 11010056 | tf_op jit(solution)/shard_map/ppermute | solution.py:49
  17.3 1.3 %collective-permute-start.5 = (bf16[16,11264]{1,0:T(8,128)(2,1)S(1)}, bf16[16,11264]{1,0:T(8,128)(2,1)S(1)}, u32[]{:S(2)}, u32[]{:S(2)}) collective-permute-start(bf16[16,11264]{1,0:T(8,128)(2,1)S(1)} %shard_map.101.refs_0_), channel_id=1, source_target_pairs={{0,4},{1,17},{2,6},{3,19},{4,0},{5,21},{6,2},{7,23},{8,12},{9,25},... | collective-permute-start | bytes 1081352 | tf_op jit(solution)/shard_map/ppermute | solution.py:49
  18.6 2.6 %collective-permute-start.6 = (bf16[16,11264]{1,0:T(8,128)(2,1)S(1)}, bf16[16,11264]{1,0:T(8,128)(2,1)S(1)}, u32[]{:S(2)}, u32[]{:S(2)}) collective-permute-start(bf16[16,11264]{1,0:T(8,128)(2,1)S(1)} %shard_map.101.refs_0_), channel_id=1, source_target_pairs={{0,8},{1,33},{2,10},{3,35},{4,12},{5,37},{6,14},{7,39},{8,0},{9,41... | collective-permute-start | bytes 1081352 | tf_op jit(solution)/shard_map/ppermute | solution.py:49
  21.2 2.6 %collective-permute-done.5.refs_1_ = bf16[16,11264]{1,0:T(8,128)(2,1)S(1)} collective-permute-done((bf16[16,11264]{1,0:T(8,128)(2,1)S(1)}, bf16[16,11264]{1,0:T(8,128)(2,1)S(1)}, u32[]{:S(2)}, u32[]{:S(2)}) %collective-permute-start.5) | collective-permute-done | bytes 360480 | tf_op jit(solution)/shard_map/ppermute | solution.py:49
  23.9 6.4 %collective-permute-done.6.refs_2_ = bf16[16,11264]{1,0:T(8,128)(2,1)S(1)} collective-permute-done((bf16[16,11264]{1,0:T(8,128)(2,1)S(1)}, bf16[16,11264]{1,0:T(8,128)(2,1)S(1)}, u32[]{:S(2)}, u32[]{:S(2)}) %collective-permute-start.6) | collective-permute-done | bytes 360480 | tf_op jit(solution)/shard_map/ppermute | solution.py:49
  30.2 2.6 %collective-permute-done.7.refs_3_ = bf16[16,11264]{1,0:T(8,128)(2,1)S(1)} collective-permute-done((bf16[16,11264]{1,0:T(8,128)(2,1)S(1)}, bf16[16,11264]{1,0:T(8,128)(2,1)S(1)}, u32[]{:S(2)}, u32[]{:S(2)}) %collective-permute-start.7) | collective-permute-done | bytes 360480 | tf_op jit(solution)/shard_map/ppermute | solution.py:49
  33.1 1.0 collective-permute-start.10
  34.0 1.8 %collective-permute-start.11 = (bf16[64,11264]{1,0:T(8,128)(2,1)S(1)}, bf16[64,11264]{1,0:T(8,128)(2,1)S(1)}, u32[]{:S(2)}, u32[]{:S(2)}) collective-permute-start(bf16[64,11264]{1,0:T(8,128)(2,1)S(1)} %get-tuple-element.48), channel_id=1, source_target_pairs={{0,48},{1,13},{2,50},{3,15},{4,52},{5,9},{6,54},{7,11},{8,56},{9,5... | collective-permute-start | bytes 4325384 | tf_op jit(solution)/shard_map/ppermute | solution.py:49
  36.5 2.0 %copy-done = bf16[224,8192]{1,0:T(8,128)(2,1)S(1)} copy-done((bf16[224,8192]{1,0:T(8,128)(2,1)S(1)}, bf16[224,8192]{1,0:T(8,128)(2,1)}, u32[]{:S(2)}) %copy-start) | copy-done | bytes 3670040
  38.6 2.0 %copy-done.2 = bf16[224,8192]{1,0:T(8,128)(2,1)S(1)} copy-done((bf16[224,8192]{1,0:T(8,128)(2,1)S(1)}, bf16[224,8192]{1,0:T(8,128)(2,1)}, u32[]{:S(2)}) %copy-start.2) | copy-done | bytes 3670040
  40.6 2.0 %copy-done.4 = bf16[224,8192]{1,0:T(8,128)(2,1)S(1)} copy-done((bf16[224,8192]{1,0:T(8,128)(2,1)S(1)}, bf16[224,8192]{1,0:T(8,128)(2,1)}, u32[]{:S(2)}) %copy-start.4) | copy-done | bytes 3670040
  42.7 14.8 %collective-permute-done.12.f2 = bf16[64,3072]{1,0:T(8,128)(2,1)S(1)} collective-permute-done((bf16[64,3072]{1,0:T(8,128)(2,1)S(1)}, bf16[64,3072]{1,0:T(8,128)(2,1)S(1)}, u32[]{:S(2)}, u32[]{:S(2)}) %collective-permute-start.12) | collective-permute-done | bytes 393248 | tf_op jit(solution)/shard_map/ppermute | solution.py:49
  57.7 2.8 %collective-permute-start.13 = (bf16[256,3328]{1,0:T(8,128)(2,1)S(1)}, bf16[256,3328]{1,0:T(8,128)(2,1)S(1)}, u32[]{:S(2)}, u32[]{:S(2)}) collective-permute-start(bf16[256,3328]{1,0:T(8,128)(2,1)S(1)} %shard_map.105.refs_9_), channel_id=1, source_target_pairs={{0,1},{1,0},{2,3},{3,2},{4,5},{5,4},{6,7},{7,6},{8,9},{9,8},{10,11... | collective-permute-start | bytes 5111816 | tf_op jit(solution)/shard_map/ppermute | solution.py:49
  60.6 4.1 %shard_map.103.refs_4_ = f32[896,192]{1,0:T(8,128)S(1)} custom-call(bf16[64,8192]{1,0:T(8,128)(2,1)S(1)} %get-tuple-element.59.refs_0_.refs_1_, bf16[64,11264]{1,0:T(8,128)(2,1)S(1)} %collective-permute-done.10.refs_1_.packed1.refs_2_, bf16[64,11264]{1,0:T(8,128)(2,1)S(1)} %collective-permute-done.11.refs_2_.packed3.refs_3_, ...), custom_call_target="tpu_custom_call" | custom-call | flops 1 | bytes 1 | tf_op jit(solution)/shard_map/pallas_call | solution.py:157
  64.7 6.1 %shard_map.106 = (f32[64,8192]{1,0:T(8,128)S(1)}, bf16[64,8192]{1,0:T(8,128)(2,1)S(1)}, bf16[64,8192]{1,0:T(8,128)(2,1)S(1)}, bf16[128,8192]{1,0:T(8,128)(2,1)S(1)}, bf16[64,8192]{1,0:T(8,128)(2,1)S(1)}) custom-call(s32[5]{0:T(128)S(1)} %stack.23.place.refs_0_, bf16[64,8192]{1,0:T(8,128)(2,1)S(1)} %get-tuple-element.59.refs_0_.refs_1_, ...), custom_call_target="tpu_custom_call" | custom-call | flops 1 | bytes 1 | tf_op jit(solution)/shard_map/pallas_call | solution.py:178
  70.8 1.0 collective-permute-start.14
  71.8 2.5 %collective-permute-start.15 = (bf16[64,8192]{1,0:T(8,128)(2,1)S(1)}, bf16[64,8192]{1,0:T(8,128)(2,1)S(1)}, u32[]{:S(2)}, u32[]{:S(2)}) collective-permute-start(bf16[64,8192]{1,0:T(8,128)(2,1)S(1)} %get-tuple-element.58), channel_id=1, source_target_pairs={{0,48},{1,13},{2,50},{3,15},{4,52},{5,9},{6,54},{7,11},{8,56},{9,5... | collective-permute-start | bytes 3145736 | tf_op jit(solution)/shard_map/ppermute | solution.py:49
  74.3 1.8 %collective-permute-done.16.refs_0_ = bf16[64,8192]{1,0:T(8,128)(2,1)S(1)} collective-permute-done((bf16[64,8192]{1,0:T(8,128)(2,1)S(1)}, bf16[64,8192]{1,0:T(8,128)(2,1)S(1)}, u32[]{:S(2)}, u32[]{:S(2)}) %collective-permute-start.16) | collective-permute-done | bytes 1048608 | tf_op jit(solution)/shard_map/ppermute | solution.py:49
  76.0 4.1 %shard_map.108.refs_1_ = f32[896,64]{1,0:T(8,128)S(1)} custom-call(bf16[64,8192]{1,0:T(8,128)(2,1)S(1)} %collective-permute-done.16.refs_0_, bf16[224,8192]{1,0:T(8,128)(2,1)S(1)} %copy-done.3, bf16[224,8192]{1,0:T(8,128)(2,1)S(1)} %collective-permute-done.4.refs_4_.refs_2_, bf16[224,8192]{1,0:T(8,128)(2,1)S(1)} %copy-done.5, ...), custom_call_target="tpu_custom_call" | custom-call | flops 1 | bytes 1 | tf_op jit(solution)/shard_map/pallas_call | solution.py:157
  80.1 3.6 %shard_map.109 = bf16[64,8192]{1,0:T(8,128)(2,1)S(1)} custom-call(bf16[64,8192]{1,0:T(8,128)(2,1)S(1)} %collective-permute-done.16.refs_0_, f32[896,64]{1,0:T(8,128)S(1)} %shard_map.108.refs_1_, bf16[224,8192]{1,0:T(8,128)(2,1)S(1)} %copy-done.1, bf16[224,8192]{1,0:T(8,128)(2,1)S(1)} %collective-permute-done.9.refs_6_.refs_3_, ...), custom_call_target="tpu_custom_call" | custom-call | flops 1 | bytes 1 | tf_op jit(solution)/shard_map/pallas_call | solution.py:178
  83.8 1.3 %collective-permute-done.14.b1 = bf16[64,8192]{1,0:T(8,128)(2,1)S(1)} collective-permute-done((bf16[64,8192]{1,0:T(8,128)(2,1)S(1)}, bf16[64,8192]{1,0:T(8,128)(2,1)S(1)}, u32[]{:S(2)}, u32[]{:S(2)}) %collective-permute-start.14) | collective-permute-done | bytes 1048608 | tf_op jit(solution)/shard_map/ppermute | solution.py:49
  85.1 12.2 %collective-permute-done.15.b3 = bf16[64,8192]{1,0:T(8,128)(2,1)S(1)} collective-permute-done((bf16[64,8192]{1,0:T(8,128)(2,1)S(1)}, bf16[64,8192]{1,0:T(8,128)(2,1)S(1)}, u32[]{:S(2)}, u32[]{:S(2)}) %collective-permute-start.15) | collective-permute-done | bytes 1048608 | tf_op jit(solution)/shard_map/ppermute | solution.py:49
  97.6 1.6 %collective-permute-done.17.b = bf16[64,8192]{1,0:T(8,128)(2,1)S(1)} collective-permute-done((bf16[64,8192]{1,0:T(8,128)(2,1)S(1)}, bf16[64,8192]{1,0:T(8,128)(2,1)S(1)}, u32[]{:S(2)}, u32[]{:S(2)}) %collective-permute-start.17) | collective-permute-done | bytes 1048608 | tf_op jit(solution)/shard_map/ppermute | solution.py:49
  99.5 3.1 %collective-permute-start.19 = (bf16[16,8192]{1,0:T(8,128)(2,1)S(1)}, bf16[16,8192]{1,0:T(8,128)(2,1)S(1)}, u32[]{:S(2)}, u32[]{:S(2)}) collective-permute-start(bf16[16,8192]{1,0:T(8,128)(2,1)S(1)} %get-tuple-element.65), channel_id=1, source_target_pairs={{0,8},{1,33},{2,10},{3,35},{4,12},{5,37},{6,14},{7,39},{8,0},{9,41... | collective-permute-start | bytes 786440 | tf_op jit(solution)/shard_map/ppermute | solution.py:49
  102.5 0.8 collective-permute-start.20
  103.3 1.4 %collective-permute-done.18.b1 = bf16[16,8192]{1,0:T(8,128)(2,1)S(1)} collective-permute-done((bf16[16,8192]{1,0:T(8,128)(2,1)S(1)}, bf16[16,8192]{1,0:T(8,128)(2,1)S(1)}, u32[]{:S(2)}, u32[]{:S(2)}) %collective-permute-start.18) | collective-permute-done | bytes 262176 | tf_op jit(solution)/shard_map/ppermute | solution.py:49
  104.7 4.8 %collective-permute-done.19.b2 = bf16[16,8192]{1,0:T(8,128)(2,1)S(1)} collective-permute-done((bf16[16,8192]{1,0:T(8,128)(2,1)S(1)}, bf16[16,8192]{1,0:T(8,128)(2,1)S(1)}, u32[]{:S(2)}, u32[]{:S(2)}) %collective-permute-start.19) | collective-permute-done | bytes 262176 | tf_op jit(solution)/shard_map/ppermute | solution.py:49
  109.4 2.6 %collective-permute-done.20.b3 = bf16[16,8192]{1,0:T(8,128)(2,1)S(1)} collective-permute-done((bf16[16,8192]{1,0:T(8,128)(2,1)S(1)}, bf16[16,8192]{1,0:T(8,128)(2,1)S(1)}, u32[]{:S(2)}, u32[]{:S(2)}) %collective-permute-start.20) | collective-permute-done | bytes 262176 | tf_op jit(solution)/shard_map/ppermute | solution.py:49
  112.1 0.7 shard_map.111
  112.7 2.2 %collective-permute-start.23 = (bf16[8,4096]{1,0:T(8,128)(2,1)S(1)}, bf16[8,4096]{1,0:T(8,128)(2,1)S(1)}, u32[]{:S(2)}, u32[]{:S(2)}) collective-permute-start(bf16[8,4096]{1,0:T(8,128)(2,1)S(1)} %get-tuple-element.70), channel_id=1, source_target_pairs={{0,66},{1,67},{2,64},{3,65},{4,70},{5,71},{6,68},{7,69},{8,74},{9,... | collective-permute-start | bytes 196616 | tf_op jit(solution)/shard_map/ppermute | solution.py:49
  114.9 1.4 %collective-permute-start.22 = (bf16[8,4096]{1,0:T(8,128)(2,1)S(1)}, bf16[8,4096]{1,0:T(8,128)(2,1)S(1)}, u32[]{:S(2)}, u32[]{:S(2)}) collective-permute-start(bf16[8,4096]{1,0:T(8,128)(2,1)S(1)} %get-tuple-element.69), channel_id=1, source_target_pairs={{0,64},{1,65},{2,66},{3,67},{4,68},{5,69},{6,70},{7,71},{8,72},{9,... | collective-permute-start | bytes 196616 | tf_op jit(solution)/shard_map/ppermute | solution.py:49
  116.4 0.8 collective-permute-done.23
  117.1 2.5 %collective-permute-done.22 = bf16[8,4096]{1,0:T(8,128)(2,1)S(1)} collective-permute-done((bf16[8,4096]{1,0:T(8,128)(2,1)S(1)}, bf16[8,4096]{1,0:T(8,128)(2,1)S(1)}, u32[]{:S(2)}, u32[]{:S(2)}) %collective-permute-start.22) | collective-permute-done | bytes 65568 | tf_op jit(solution)/shard_map/ppermute | solution.py:49
  119.8 3.3 %collective-permute-start.24 = (bf16[8,2048]{1,0:T(8,128)(2,1)S(1)}, bf16[8,2048]{1,0:T(8,128)(2,1)S(1)}, u32[]{:S(2)}, u32[]{:S(2)}) collective-permute-start(bf16[8,2048]{1,0:T(8,128)(2,1)S(1)} %get-tuple-element.72), channel_id=1, source_target_pairs={{0,1},{1,0},{2,3},{3,2},{4,5},{5,4},{6,7},{7,6},{8,9},{9,8},{10,11... | collective-permute-start | bytes 98312 | tf_op jit(solution)/shard_map/ppermute | solution.py:49
  123.2 0.9 collective-permute-done.24
  124.0 0.6 maximum_select_fusion
  (43 shorter events, 3.1 us)
Async XLA Ops:
  0.0 36.5 %copy-start.6 = (bf16[224,64]{0,1:T(8,128)(2,1)S(1)}, bf16[224,64]{0,1:T(8,128)(2,1)}, u32[]{:S(2)}) copy-start(bf16[224,64]{0,1:T(8,128)(2,1)} %param.15) | copy-start | bytes 86020
  0.0 36.5 %copy-start.7 = (bf16[224,64]{0,1:T(8,128)(2,1)S(1)}, bf16[224,64]{0,1:T(8,128)(2,1)}, u32[]{:S(2)}) copy-start(bf16[224,64]{0,1:T(8,128)(2,1)} %param.17) | copy-start | bytes 86020
  0.0 36.5 %copy-start.8 = (bf16[224,64]{0,1:T(8,128)(2,1)S(1)}, bf16[224,64]{0,1:T(8,128)(2,1)}, u32[]{:S(2)}) copy-start(bf16[224,64]{0,1:T(8,128)(2,1)} %param.18) | copy-start | bytes 86020
  0.8 2.3 %collective-permute-start = (bf16[8,2048]{1,0:T(8,128)(2,1)S(1)}, bf16[8,2048]{1,0:T(8,128)(2,1)S(1)}, u32[]{:S(2)}, u32[]{:S(2)}) collective-permute-start(bf16[8,2048]{1,0:T(8,128)(2,1)S(1)} %get-tuple-element.73), channel_id=1, source_target_pairs={{0,1},{1,0},{2,3},{3,2},{4,5},{5,4},{6,7},{7,6},{8,9},{9,8},{10,11... | collective-permute-start | bytes 98312 | tf_op jit(solution)/shard_map/ppermute | solution.py:49
  3.2 0.8 copy-start.9
  3.9 0.8 copy-start.10
  4.7 0.8 copy-start.11
  6.1 9.5 %collective-permute-start.4 = (bf16[224,8192]{1,0:T(8,128)(2,1)}, bf16[224,8192]{1,0:T(8,128)(2,1)S(1)}, u32[]{:S(2)}, u32[]{:S(2)}) collective-permute-start(bf16[224,8192]{1,0:T(8,128)(2,1)} %refs_1_), channel_id=1, source_target_pairs={{0,1},{1,0},{2,3},{3,2},{4,5},{5,4},{6,7},{7,6},{8,9},{9,8},{10,11... | collective-permute-start | bytes 11010056 | tf_op jit(solution)/shard_map/ppermute | solution.py:49
  6.5 8.5 %collective-permute-start.3 = (bf16[16,3584]{1,0:T(8,128)(2,1)S(1)}, bf16[16,3584]{1,0:T(8,128)(2,1)S(1)}, u32[]{:S(2)}, u32[]{:S(2)}) collective-permute-start(bf16[16,3584]{1,0:T(8,128)(2,1)S(1)} %get-tuple-element.39.message), channel_id=1, source_target_pairs={{0,66},{1,67},{2,64},{3,65},{4,70},{5,71},{6,68},{7,69},{8,74},{9,... | collective-permute-start | bytes 344072 | tf_op jit(solution)/shard_map/ppermute | solution.py:49
  10.4 3.4 %collective-permute-start.1 = (bf16[8,4096]{1,0:T(8,128)(2,1)S(1)}, bf16[8,4096]{1,0:T(8,128)(2,1)S(1)}, u32[]{:S(2)}, u32[]{:S(2)}) collective-permute-start(bf16[8,4096]{1,0:T(8,128)(2,1)S(1)} %get-tuple-element.38.wide), channel_id=1, source_target_pairs={{0,2},{1,3},{2,0},{3,1},{4,6},{5,7},{6,4},{7,5},{8,10},{9,11},{10,... | collective-permute-start | bytes 196616 | tf_op jit(solution)/shard_map/ppermute | solution.py:49
  10.4 4.6 %collective-permute-start.2 = (bf16[8,4096]{1,0:T(8,128)(2,1)S(1)}, bf16[8,4096]{1,0:T(8,128)(2,1)S(1)}, u32[]{:S(2)}, u32[]{:S(2)}) collective-permute-start(bf16[8,4096]{1,0:T(8,128)(2,1)S(1)} %get-tuple-element.38.wide), channel_id=1, source_target_pairs={{0,64},{1,65},{2,66},{3,67},{4,68},{5,69},{6,70},{7,71},{8,72},{9,... | collective-permute-start | bytes 196616 | tf_op jit(solution)/shard_map/ppermute | solution.py:49
  11.6 21.5 %collective-permute-start.8 = (bf16[224,8192]{1,0:T(8,128)(2,1)}, bf16[224,8192]{1,0:T(8,128)(2,1)S(1)}, u32[]{:S(2)}, u32[]{:S(2)}) collective-permute-start(bf16[224,8192]{1,0:T(8,128)(2,1)} %refs_3_.1), channel_id=1, source_target_pairs={{0,1},{1,0},{2,3},{3,2},{4,5},{5,4},{6,7},{7,6},{8,9},{9,8},{10,11... | collective-permute-start | bytes 11010056 | tf_op jit(solution)/shard_map/ppermute | solution.py:49
  15.6 17.4 %collective-permute-start.9 = (bf16[224,8192]{1,0:T(8,128)(2,1)}, bf16[224,8192]{1,0:T(8,128)(2,1)S(1)}, u32[]{:S(2)}, u32[]{:S(2)}) collective-permute-start(bf16[224,8192]{1,0:T(8,128)(2,1)} %refs_2_), channel_id=1, source_target_pairs={{0,1},{1,0},{2,3},{3,2},{4,5},{5,4},{6,7},{7,6},{8,9},{9,8},{10,11... | collective-permute-start | bytes 11010056 | tf_op jit(solution)/shard_map/ppermute | solution.py:49
  17.3 6.6 %collective-permute-start.5 = (bf16[16,11264]{1,0:T(8,128)(2,1)S(1)}, bf16[16,11264]{1,0:T(8,128)(2,1)S(1)}, u32[]{:S(2)}, u32[]{:S(2)}) collective-permute-start(bf16[16,11264]{1,0:T(8,128)(2,1)S(1)} %shard_map.101.refs_0_), channel_id=1, source_target_pairs={{0,4},{1,17},{2,6},{3,19},{4,0},{5,21},{6,2},{7,23},{8,12},{9,25},... | collective-permute-start | bytes 1081352 | tf_op jit(solution)/shard_map/ppermute | solution.py:49
  18.6 11.6 %collective-permute-start.6 = (bf16[16,11264]{1,0:T(8,128)(2,1)S(1)}, bf16[16,11264]{1,0:T(8,128)(2,1)S(1)}, u32[]{:S(2)}, u32[]{:S(2)}) collective-permute-start(bf16[16,11264]{1,0:T(8,128)(2,1)S(1)} %shard_map.101.refs_0_), channel_id=1, source_target_pairs={{0,8},{1,33},{2,10},{3,35},{4,12},{5,37},{6,14},{7,39},{8,0},{9,41... | collective-permute-start | bytes 1081352 | tf_op jit(solution)/shard_map/ppermute | solution.py:49
  21.2 11.6 %collective-permute-start.7 = (bf16[16,11264]{1,0:T(8,128)(2,1)S(1)}, bf16[16,11264]{1,0:T(8,128)(2,1)S(1)}, u32[]{:S(2)}, u32[]{:S(2)}) collective-permute-start(bf16[16,11264]{1,0:T(8,128)(2,1)S(1)} %shard_map.101.refs_0_), channel_id=1, source_target_pairs={{0,12},{1,49},{2,14},{3,51},{4,8},{5,53},{6,10},{7,55},{8,4},{9,57... | collective-permute-start | bytes 1081352 | tf_op jit(solution)/shard_map/ppermute | solution.py:49
  33.1 24.4 %collective-permute-start.10 = (bf16[64,11264]{1,0:T(8,128)(2,1)S(1)}, bf16[64,11264]{1,0:T(8,128)(2,1)S(1)}, u32[]{:S(2)}, u32[]{:S(2)}) collective-permute-start(bf16[64,11264]{1,0:T(8,128)(2,1)S(1)} %get-tuple-element.48), channel_id=1, source_target_pairs={{0,16},{1,5},{2,18},{3,7},{4,20},{5,1},{6,22},{7,3},{8,24},{9,13},... | collective-permute-start | bytes 4325384 | tf_op jit(solution)/shard_map/ppermute | solution.py:49
  34.0 23.6 %collective-permute-start.11 = (bf16[64,11264]{1,0:T(8,128)(2,1)S(1)}, bf16[64,11264]{1,0:T(8,128)(2,1)S(1)}, u32[]{:S(2)}, u32[]{:S(2)}) collective-permute-start(bf16[64,11264]{1,0:T(8,128)(2,1)S(1)} %get-tuple-element.48), channel_id=1, source_target_pairs={{0,48},{1,13},{2,50},{3,15},{4,52},{5,9},{6,54},{7,11},{8,56},{9,5... | collective-permute-start | bytes 4325384 | tf_op jit(solution)/shard_map/ppermute | solution.py:49
  35.9 21.6 %collective-permute-start.12 = (bf16[64,3072]{1,0:T(8,128)(2,1)S(1)}, bf16[64,3072]{1,0:T(8,128)(2,1)S(1)}, u32[]{:S(2)}, u32[]{:S(2)}) collective-permute-start(bf16[64,3072]{1,0:T(8,128)(2,1)S(1)} %get-tuple-element.55.own), channel_id=1, source_target_pairs={{0,32},{1,9},{2,34},{3,11},{4,36},{5,13},{6,38},{7,15},{8,40},{9,1... | collective-permute-start | bytes 1179656 | tf_op jit(solution)/shard_map/ppermute | solution.py:49
  36.5 2.0 %copy-start = (bf16[224,8192]{1,0:T(8,128)(2,1)S(1)}, bf16[224,8192]{1,0:T(8,128)(2,1)}, u32[]{:S(2)}) copy-start(bf16[224,8192]{1,0:T(8,128)(2,1)} %refs_2_) | copy-start | bytes 11010052
  38.5 2.0 %copy-start.2 = (bf16[224,8192]{1,0:T(8,128)(2,1)S(1)}, bf16[224,8192]{1,0:T(8,128)(2,1)}, u32[]{:S(2)}) copy-start(bf16[224,8192]{1,0:T(8,128)(2,1)} %refs_1_) | copy-start | bytes 11010052
  40.6 2.0 %copy-start.4 = (bf16[224,8192]{1,0:T(8,128)(2,1)S(1)}, bf16[224,8192]{1,0:T(8,128)(2,1)}, u32[]{:S(2)}) copy-start(bf16[224,8192]{1,0:T(8,128)(2,1)} %refs_3_.1) | copy-start | bytes 11010052
  42.6 18.0 %copy-start.5 = (bf16[224,8192]{1,0:T(8,128)(2,1)S(1)}, bf16[224,8192]{1,0:T(8,128)(2,1)}, u32[]{:S(2)}) copy-start(bf16[224,8192]{1,0:T(8,128)(2,1)} %refs_3_.1) | copy-start | bytes 11010052
  42.6 18.0 %copy-start.3 = (bf16[224,8192]{1,0:T(8,128)(2,1)S(1)}, bf16[224,8192]{1,0:T(8,128)(2,1)}, u32[]{:S(2)}) copy-start(bf16[224,8192]{1,0:T(8,128)(2,1)} %refs_1_) | copy-start | bytes 11010052
  57.7 6.9 %collective-permute-start.13 = (bf16[256,3328]{1,0:T(8,128)(2,1)S(1)}, bf16[256,3328]{1,0:T(8,128)(2,1)S(1)}, u32[]{:S(2)}, u32[]{:S(2)}) collective-permute-start(bf16[256,3328]{1,0:T(8,128)(2,1)S(1)} %shard_map.105.refs_9_), channel_id=1, source_target_pairs={{0,1},{1,0},{2,3},{3,2},{4,5},{5,4},{6,7},{7,6},{8,9},{9,8},{10,11... | collective-permute-start | bytes 5111816 | tf_op jit(solution)/shard_map/ppermute | solution.py:49
  60.6 15.4 %collective-permute-start.16 = (bf16[64,8192]{1,0:T(8,128)(2,1)S(1)}, bf16[64,8192]{1,0:T(8,128)(2,1)S(1)}, u32[]{:S(2)}, u32[]{:S(2)}) collective-permute-start(bf16[64,8192]{1,0:T(8,128)(2,1)S(1)} %get-tuple-element.59.refs_0_.refs_1_), channel_id=1, source_target_pairs={{0,32},{1,9},{2,34},{3,11},{4,36},{5,13},{6,38},{7,15},{8,40},{9,1... | collective-permute-start | bytes 3145736 | tf_op jit(solution)/shard_map/ppermute | solution.py:49
  60.6 4.1 %copy-start.1 = (bf16[224,8192]{1,0:T(8,128)(2,1)S(1)}, bf16[224,8192]{1,0:T(8,128)(2,1)}, u32[]{:S(2)}) copy-start(bf16[224,8192]{1,0:T(8,128)(2,1)} %refs_2_) | copy-start | bytes 11010052
  70.8 14.3 %collective-permute-start.14 = (bf16[64,8192]{1,0:T(8,128)(2,1)S(1)}, bf16[64,8192]{1,0:T(8,128)(2,1)S(1)}, u32[]{:S(2)}, u32[]{:S(2)}) collective-permute-start(bf16[64,8192]{1,0:T(8,128)(2,1)S(1)} %get-tuple-element.57), channel_id=1, source_target_pairs={{0,16},{1,5},{2,18},{3,7},{4,20},{5,1},{6,22},{7,3},{8,24},{9,13},... | collective-permute-start | bytes 3145736 | tf_op jit(solution)/shard_map/ppermute | solution.py:49
  71.8 25.5 %collective-permute-start.15 = (bf16[64,8192]{1,0:T(8,128)(2,1)S(1)}, bf16[64,8192]{1,0:T(8,128)(2,1)S(1)}, u32[]{:S(2)}, u32[]{:S(2)}) collective-permute-start(bf16[64,8192]{1,0:T(8,128)(2,1)S(1)} %get-tuple-element.58), channel_id=1, source_target_pairs={{0,48},{1,13},{2,50},{3,15},{4,52},{5,9},{6,54},{7,11},{8,56},{9,5... | collective-permute-start | bytes 3145736 | tf_op jit(solution)/shard_map/ppermute | solution.py:49
  83.7 15.5 %collective-permute-start.17 = (bf16[64,8192]{1,0:T(8,128)(2,1)S(1)}, bf16[64,8192]{1,0:T(8,128)(2,1)S(1)}, u32[]{:S(2)}, u32[]{:S(2)}) collective-permute-start(bf16[64,8192]{1,0:T(8,128)(2,1)S(1)} %shard_map.109), channel_id=1, source_target_pairs={{0,32},{1,9},{2,34},{3,11},{4,36},{5,13},{6,38},{7,15},{8,40},{9,1... | collective-permute-start | bytes 3145736 | tf_op jit(solution)/shard_map/ppermute | solution.py:49
  99.4 5.3 %collective-permute-start.18 = (bf16[16,8192]{1,0:T(8,128)(2,1)S(1)}, bf16[16,8192]{1,0:T(8,128)(2,1)S(1)}, u32[]{:S(2)}, u32[]{:S(2)}) collective-permute-start(bf16[16,8192]{1,0:T(8,128)(2,1)S(1)} %get-tuple-element.64), channel_id=1, source_target_pairs={{0,4},{1,17},{2,6},{3,19},{4,0},{5,21},{6,2},{7,23},{8,12},{9,25},... | collective-permute-start | bytes 786440 | tf_op jit(solution)/shard_map/ppermute | solution.py:49
  99.5 10.0 %collective-permute-start.19 = (bf16[16,8192]{1,0:T(8,128)(2,1)S(1)}, bf16[16,8192]{1,0:T(8,128)(2,1)S(1)}, u32[]{:S(2)}, u32[]{:S(2)}) collective-permute-start(bf16[16,8192]{1,0:T(8,128)(2,1)S(1)} %get-tuple-element.65), channel_id=1, source_target_pairs={{0,8},{1,33},{2,10},{3,35},{4,12},{5,37},{6,14},{7,39},{8,0},{9,41... | collective-permute-start | bytes 786440 | tf_op jit(solution)/shard_map/ppermute | solution.py:49
  102.5 9.5 %collective-permute-start.20 = (bf16[16,8192]{1,0:T(8,128)(2,1)S(1)}, bf16[16,8192]{1,0:T(8,128)(2,1)S(1)}, u32[]{:S(2)}, u32[]{:S(2)}) collective-permute-start(bf16[16,8192]{1,0:T(8,128)(2,1)S(1)} %get-tuple-element.66), channel_id=1, source_target_pairs={{0,12},{1,49},{2,14},{3,51},{4,8},{5,53},{6,10},{7,55},{8,4},{9,57... | collective-permute-start | bytes 786440 | tf_op jit(solution)/shard_map/ppermute | solution.py:49
  112.7 4.4 %collective-permute-start.23 = (bf16[8,4096]{1,0:T(8,128)(2,1)S(1)}, bf16[8,4096]{1,0:T(8,128)(2,1)S(1)}, u32[]{:S(2)}, u32[]{:S(2)}) collective-permute-start(bf16[8,4096]{1,0:T(8,128)(2,1)S(1)} %get-tuple-element.70), channel_id=1, source_target_pairs={{0,66},{1,67},{2,64},{3,65},{4,70},{5,71},{6,68},{7,69},{8,74},{9,... | collective-permute-start | bytes 196616 | tf_op jit(solution)/shard_map/ppermute | solution.py:49
  114.9 4.7 %collective-permute-start.22 = (bf16[8,4096]{1,0:T(8,128)(2,1)S(1)}, bf16[8,4096]{1,0:T(8,128)(2,1)S(1)}, u32[]{:S(2)}, u32[]{:S(2)}) collective-permute-start(bf16[8,4096]{1,0:T(8,128)(2,1)S(1)} %get-tuple-element.69), channel_id=1, source_target_pairs={{0,64},{1,65},{2,66},{3,67},{4,68},{5,69},{6,70},{7,71},{8,72},{9,... | collective-permute-start | bytes 196616 | tf_op jit(solution)/shard_map/ppermute | solution.py:49
  116.3 3.4 %collective-permute-start.21 = (bf16[8,4096]{1,0:T(8,128)(2,1)S(1)}, bf16[8,4096]{1,0:T(8,128)(2,1)S(1)}, u32[]{:S(2)}, u32[]{:S(2)}) collective-permute-start(bf16[8,4096]{1,0:T(8,128)(2,1)S(1)} %get-tuple-element.68), channel_id=1, source_target_pairs={{0,2},{1,3},{2,0},{3,1},{4,6},{5,7},{6,4},{7,5},{8,10},{9,11},{10,... | collective-permute-start | bytes 196616 | tf_op jit(solution)/shard_map/ppermute | solution.py:49
  119.8 4.2 %collective-permute-start.24 = (bf16[8,2048]{1,0:T(8,128)(2,1)S(1)}, bf16[8,2048]{1,0:T(8,128)(2,1)S(1)}, u32[]{:S(2)}, u32[]{:S(2)}) collective-permute-start(bf16[8,2048]{1,0:T(8,128)(2,1)S(1)} %get-tuple-element.72), channel_id=1, source_target_pairs={{0,1},{1,0},{2,3},{3,2},{4,5},{5,4},{6,7},{7,6},{8,9},{9,8},{10,11... | collective-permute-start | bytes 98312 | tf_op jit(solution)/shard_map/ppermute | solution.py:49

commit v5 on v4

--- a/solution.py
+++ b/solution.py
@@ -18,6 +18,7 @@
 STEPS = WIDTH // TILE
 PARTS = TILE // 256
 f32, bf16 = jnp.float32, jnp.bfloat16
+C1, C2, CK = 3.6, 3.8, 8
 SMALL = pl.CostEstimate(flops=1, bytes_accessed=1, transcendentals=0)
 
 
@@ -148,20 +149,22 @@
     return [pltpu.with_memory_space_constraint(a, pltpu.VMEM) for a in operands]
 
 
-def cost(macs):
-    return pl.CostEstimate(flops=2 * macs, bytes_accessed=2 * macs // 64, transcendentals=0)
-
-
-def project(rows, weights):
-    n = len(rows)
+def price_of(us):
+    return pl.CostEstimate(
+        flops=int(us * 1.15e9), bytes_accessed=int(us * 3.6e6), transcendentals=0
+    )
+
+
+def project(rows, weights, *extra):
+    n, more = len(rows), len(extra)
     return pl.pallas_call(
-        lambda *refs: project_kernel(n, *refs),
-        in_specs=[VMEM] * (n + 4),
+        lambda *refs: project_kernel(n, *refs[more:]),
+        in_specs=[VMEM] * (more + n + 4),
         out_specs=VMEM,
         out_shape=jax.ShapeDtypeStruct((4 * UNITS, 64 * n), f32),
         compiler_params=pltpu.CompilerParams(vmem_limit_bytes=10 * 1024 * 1024),
-        cost_estimate=SMALL,
-    )(*in_vmem([*rows, *weights]))
+        cost_estimate=price_of(CK),
+    )(*extra, *in_vmem([*rows, *weights]))
 
 
 def down(place, rows, acc, weights, seconds, factors, kinds):
@@ -198,63 +201,71 @@
         scratch_shapes=list(scratch),
         compiler_params=pltpu.CompilerParams(vmem_limit_bytes=6 * 1024 * 1024),
         cost_estimate=price,
-    )(*lead, *operands, *far)
-
-
-def shape_kernel(place, own, other, gate, up, down, wide, message, ranks, sems):
+    )(*lead, *operands, *(pltpu.with_memory_space_constraint(a, pltpu.HBM) for a in far))
+
+
+def begin_kernel(place, inputs, gate, up, down, own, other, factor, ranks, sems):
     c = place[3]
     half = pl.ds(pl.multiple_of(c * 32, 32), 32)
-    copies = [
-        pltpu.make_async_copy(r.at[half, :], ranks.at[k], sems.at[k])
-        for k, r in enumerate((gate, up, down))
-    ]
+    copies = [pltpu.make_async_copy(inputs.at[c], own, sems.at[0])]
+    copies += [pltpu.make_async_copy(inputs.at[1 - c], other, sems.at[1])]
+    for k, r in enumerate((gate, up, down)):
+        copies += [pltpu.make_async_copy(r.at[half, :], ranks.at[k], sems.at[2 + k])]
     for copy in copies:
         copy.start()
-    wide[:, pl.ds(pl.multiple_of(c * QUARTER, QUARTER), QUARTER)] = own[...]
-    wide[:, pl.ds(pl.multiple_of((1 - c) * QUARTER, QUARTER), QUARTER)] = other[...]
-    rows = widen(wide[...])
-    rows = jnp.concatenate([rows[:, :QUARTER], rows[:, QUARTER:]], axis=0)
-    message[:, :QUARTER] = rows.astype(bf16)
     for copy in copies:
         copy.wait()
     for i in range(6):
-        col = QUARTER + 256 * i
-        message[:, col : col + 256] = ranks[i // 2, (i % 2) * 16 : (i % 2) * 16 + 16, :]
-
-
-def pack_kernel(place, wide, z1, z2, message, far_message, out):
+        col = slice(256 * i, 256 * i + 256)
+        factor[:, col] = ranks[i // 2, (i % 2) * 16 : (i % 2) * 16 + 16, :]
+
+
+def shape_kernel(place, own, other, wide):
+    c = place[3]
+    wide[:, pl.ds(pl.multiple_of(c * QUARTER, QUARTER), QUARTER)] = own[...]
+    wide[:, pl.ds(pl.multiple_of((1 - c) * QUARTER, QUARTER), QUARTER)] = other[...]
+
+
+def pack_kernel(place, wide, z1, z2, z3, out):
     zl = place[4]
     here = pl.ds(pl.multiple_of(zl * HALF, HALF), HALF)
     there = pl.ds(pl.multiple_of((1 - zl) * HALF, HALF), HALF)
-    z3 = widen(far_message[:, :QUARTER])
-    z3 = jnp.concatenate([z3[:8], z3[8:]], axis=1)
-    pair = lambda a, b: jnp.concatenate([widen(a), widen(b)], 0).astype(bf16)
-    out[:, here] = pair(wide[...], z2[...])
-    out[:, there] = pair(z1[...], z3)
+    pair = lambda a, b: jnp.concatenate([widen(a[...]), widen(b[...])], 0).astype(bf16)
+    out[:, here] = pair(wide, z2)
+    out[:, there] = pair(z1, z3)
+
+
+def pair_kernel(near, far, out):
     for i in range(6):
-        at, col = WIDTH + 512 * i, QUARTER + 256 * i
-        out[:, at : at + 256] = message[:, col : col + 256]
-        out[:, at + 256 : at + 512] = far_message[:, col : col + 256]
-
-
-def unpack_kernel(*refs):
-    got, (block, factor, packed) = refs[:4], refs[4:]
-    for k, g in enumerate(got):
-        at = slice(16 * k, 16 * k + 16)
-        block[at, :] = g[:, :WIDTH]
-        factor[at, :] = g[:, WIDTH:]
-        packed[at, :] = g[...]
-
-
-def seconds_kernel(gate_w, up_w, down_w, gate, up, down, out):
+        out[:, 512 * i : 512 * i + 256] = near[:, 256 * i : 256 * i + 256]
+        out[:, 512 * i + 256 : 512 * i + 512] = far[:, 256 * i : 256 * i + 256]
+
+
+def swap_kernel(a, b, out):
+    out[:32, :] = a[...]
+    out[32:48, :] = b[16:, :]
+    out[48:, :] = b[:16, :]
+
+
+def rows_kernel(*refs):
+    out, step = refs[-1], refs[0].shape[0]
+    for k, r in enumerate(refs[:-1]):
+        out[step * k : step * k + step, :] = r[...]
+
+
+def touch_kernel(gate_w, up_w, down_w, out):
+    out[...] = jnp.zeros_like(out)
+
+
+def seconds_kernel(gate, up, down, out):
     out[...] = jnp.zeros_like(out)
     for k, r in enumerate((gate, up, down)):
         out[64 * k : 64 * k + 64, :UNITS] = r[...]
 
 
-def stack_kernel(own, packed1, f2, packed3, seconds, out):
-    for k, r in enumerate((own, packed1, f2, packed3)):
-        out[64 * k : 64 * k + 64, :3072] = r[:, -3072:]
+def stack_kernel(f0, f1, f2, f3, seconds, out):
+    for k, r in enumerate((f0, f1, f2, f3)):
+        out[64 * k : 64 * k + 64, :3072] = r[...]
     out[:, 3072:] = seconds[...]
 
 
@@ -300,61 +311,60 @@
             flag == 0, jnp.concatenate([a, b], axis), jnp.concatenate([b, a], axis)
         )
 
-    own = jnp.where(c == 0, inputs[0], inputs[1])
-    other = jnp.where(c == 0, inputs[1], inputs[0])
-    wide, message = local(
-        shape_kernel,
-        [((8, HALF), bf16), ((16, QUARTER + 1536), bf16)],
-        (own, send(other, CORE)),
+    own, other, factor = local(
+        begin_kernel,
+        [((8, QUARTER), bf16), ((8, QUARTER), bf16), ((16, 1536), bf16)],
+        (),
         place,
-        far=(adapter_first_gate, adapter_first_up, adapter_second_down),
-        scratch=[pltpu.VMEM((3, 32, 256), bf16), pltpu.SemaphoreType.DMA((3,))],
-    )
-
-    z1, z2, z3 = (
-        send(v, ALONG_Z[k]) for k, v in ((1, wide), (2, wide), (3, message))
-    )
+        far=(inputs, adapter_first_gate, adapter_first_up, adapter_second_down),
+        scratch=[pltpu.VMEM((3, 32, 256), bf16), pltpu.SemaphoreType.DMA((5,))],
+    )
+    other = send(other, CORE)
+    (wide,) = local(shape_kernel, [((8, HALF), bf16)], (own, other), place)
+
+    far_factor = send(factor, ALONG_Z[3])
+    z1, z2, z3 = (send(wide, ALONG_Z[k]) for k in (1, 2, 3))
     gate2 = send(after(frozen_gate_weight, wide), CORE)
-    up2 = send(after(frozen_up_weight, wide), CORE)
-    (packed,) = local(
-        pack_kernel,
-        [((16, WIDTH + 3072), bf16)],
-        (wide, z1, z2, message, z3),
-        place,
-    )
-
-    packed = after(packed, gate2)
-    got = [packed] + [send(packed, FIRST[k]) for k in (1, 2, 3)]
-    down2 = send(after(frozen_down_weight, packed), CORE)
-    block, factor, packed = local(
-        unpack_kernel,
-        [((64, WIDTH), bf16), ((64, 3072), bf16), ((64, WIDTH + 3072), bf16)],
-        got,
-    )
-    block, factor, packed = after((block, factor, packed), (up2, down2))
-
-    packed1, packed3 = send(packed, SECOND[1]), send(packed, SECOND[3])
-    factor_2 = send(factor, SECOND[2])
+    (factor,) = local(pair_kernel, [((16, 3072), bf16)], (factor, far_factor))
+    near = send(factor, FIRST[1])
+    (rows,) = local(
+        pack_kernel, [((16, WIDTH), bf16)], (wide, z1, z2, z3), place, price=price_of(C2)
+    )
+
+    rows = after(rows, gate2)
+    (factor,) = local(rows_kernel, [((32, 3072), bf16)], (factor, near))
+    near = send(factor, FIRST[3])
+    rows = [rows] + [send(rows, FIRST[k]) for k in (1, 2, 3)]
+    (factor,) = local(swap_kernel, [((64, 3072), bf16)], (factor, near))
+    factors = {0: factor, 1: send(factor, SECOND[1]), 3: send(factor, SECOND[3])}
     seconds = (adapter_second_gate, adapter_second_up, adapter_first_down)
-    owned, seconds = after(
-        ((frozen_gate_weight, frozen_up_weight, frozen_down_weight), seconds), packed
-    )
     (seconds,) = local(
-        seconds_kernel, [((256, 256), bf16)], [*in_vmem(owned), *(a.T for a in seconds)]
-    )
+        seconds_kernel, [((256, 256), bf16)], [a.T for a in after(seconds, rows[0])]
+    )
+    (block,) = local(rows_kernel, [((64, WIDTH), bf16)], rows, price=price_of(C1))
+
+    block, factors = after((block, factors), (block, factors))
+    block = after(block, seconds)
+    factors[2] = send(factors[0], SECOND[2])
+    rows1, rows3 = send(block, SECOND[1]), send(block, SECOND[3])
+    frozen = (frozen_gate_weight, frozen_up_weight, frozen_down_weight)
+    frozen = after(frozen, block)
+    up2, down2 = send(frozen[1], CORE), send(frozen[2], CORE)
     (factor,) = local(
         stack_kernel,
         [((256, 3072 + 256), bf16)],
-        (factor, packed1, factor_2, packed3, seconds),
+        (*(factors[k] for k in range(4)), seconds),
     )
     factor2 = send(factor, CORE)
-    rows2 = send(after(block, factor), SECOND[2])
+    rows2 = send(after(block, up2), SECOND[2])
+    (touched,) = local(touch_kernel, [((8, 128), f32)], in_vmem(frozen))
+    owned = frozen
 
     weights = (owned[0], gate2, owned[1], up2)
     down_weights = (owned[2], down2)
 
-    rows = (block, packed1, packed3)
-    acc = project(rows, weights)
+    rows = (block, rows1, rows3)
+    acc = project(rows, weights, touched)
     total, part1, part3, first, second = down(
         place, rows, acc, down_weights, (seconds, factor2), (factor, factor2),
         (f32, bf16, bf16),
@@ -370,7 +380,7 @@
         add_kernel,
         [((64, WIDTH), f32)],
         (total, back1, back3),
-        price=cost(64 * WIDTH * 64 * 16),
+        price=price_of(4.5),
     )
     small = [((16, WIDTH), f32)] + [((16, WIDTH), bf16)] * 3
     mine, *parts = local(sum_kernel, small, (total, back2))

time: 125 us -> 129 us (1.032)
  starting transfers between devices: 34 us -> 42.4 us
  local copies, waits for them, and re-layouts: 8.49 us -> 0.12 us
  waiting for transfers between devices: 60 us -> 63.6 us
    ppermute x25 -> x30, starting transfers between devices: 34 us -> 42.4 us  [send(): return lax.ppermute(value, AXES, route)]
    unnamed x24 -> x12, local copies, waits for them, and re-layouts: 8.41 us -> 0.04 us
    ppermute x25 -> x30, waiting for transfers between devices: 60 us -> 63.6 us  [send(): return lax.ppermute(value, AXES, route)]
    pallas_call x8 -> x13, Pallas kernels: 2.71 us -> 3.91 us  [local(): pl.pallas_call(body, in_specs=[SMEM] * len(lead) + [VMEM] * len(operands)...]
  transfers between devices with their start and end apart: 25 -> 30, of which waited for: 19 -> 16; matrix products, arithmetic and copies ran while one was open for 0% -> 0% of each run, Pallas kernels for 15% -> 15%
where the time goes in v5:
time: 129 us
  waiting for transfers between devices  63.6 us (49%)
  starting transfers between devices  42.4 us (33%)
  Pallas kernels  21.6 us (17%)
    ppermute x30, waiting for transfers between devices, send(): return lax.ppermute(value, AXES, route)  63.6 us
    ppermute x30, starting transfers between devices, send(): return lax.ppermute(value, AXES, route)  42.4 us
    pallas_call x2, Pallas kernels, down(): pl.pallas_call(body, in_specs=[SMEM] * len(lead) + [VMEM] * len(operands)...  9.58 us
    pallas_call x2, Pallas kernels, project(): pl.pallas_call(lambda *refs: project_kernel(n, *refs[more:]), in_specs=[V...  8.14 us
    pallas_call x13, Pallas kernels, local(): pl.pallas_call(body, in_specs=[SMEM] * len(lead) + [VMEM] * len(operands)...  3.91 us
  transfers between devices with their start and end apart: 30, of which 16 were waited for; matrix products, arithmetic and copies ran while one was open for 0% of the time, Pallas kernels for 15%

profile of v5, /device:TPU:1, one launch (start us, length us, event | category | flops | bytes accessed | tf_op | source)
XLA Modules:
  0.0 128.7 jit_solution(1049036349237783490)
XLA Ops:
  0.1 1.4 %shard_map.100 = (bf16[8,2048]{1,0:T(8,128)(2,1)S(1)}, bf16[8,2048]{1,0:T(8,128)(2,1)S(1)}, bf16[16,1536]{1,0:T(8,128)(2,1)S(1)}) custom-call(s32[5]{0:T(128)S(1)} %stack.23.place.refs_0_, bf16[2,8,2048]{2,1,0:T(8,128)(2,1)} %inputs.1, bf16[64,256]{1,0:T(8,128)(2,1)} %gate.1, bf16[64,256]{1,0:T(8,128)(2,1)} %up.1, bf16[64,256]{1,0:T(8,128)(2,1)} %down.1), custom_call_target="tpu_custom_call" | custom-call | flops 1 | bytes 1 | tf_op jit(solution)/shard_map/pallas_call | solution.py:194
  1.5 1.5 %collective-permute-start = (bf16[8,2048]{1,0:T(8,128)(2,1)S(1)}, bf16[8,2048]{1,0:T(8,128)(2,1)S(1)}, u32[]{:S(2)}, u32[]{:S(2)}) collective-permute-start(bf16[8,2048]{1,0:T(8,128)(2,1)S(1)} %get-tuple-element.37), channel_id=1, source_target_pairs={{0,1},{1,0},{2,3},{3,2},{4,5},{5,4},{6,7},{7,6},{8,9},{9,8},{10,11... | collective-permute-start | bytes 98312 | tf_op jit(solution)/shard_map/ppermute | solution.py:50
  3.0 0.9 collective-permute-done.other
  3.8 0.5 shard_map.101.wide
  4.4 0.4 collective-permute-start.4
  4.8 1.7 %collective-permute-start.1 = (bf16[8,4096]{1,0:T(8,128)(2,1)S(1)}, bf16[8,4096]{1,0:T(8,128)(2,1)S(1)}, u32[]{:S(2)}, u32[]{:S(2)}) collective-permute-start(bf16[8,4096]{1,0:T(8,128)(2,1)S(1)} %shard_map.101.wide), channel_id=1, source_target_pairs={{0,2},{1,3},{2,0},{3,1},{4,6},{5,7},{6,4},{7,5},{8,10},{9,11},{10,... | collective-permute-start | bytes 196616 | tf_op jit(solution)/shard_map/ppermute | solution.py:50
  6.5 3.3 %collective-permute-start.2 = (bf16[8,4096]{1,0:T(8,128)(2,1)S(1)}, bf16[8,4096]{1,0:T(8,128)(2,1)S(1)}, u32[]{:S(2)}, u32[]{:S(2)}) collective-permute-start(bf16[8,4096]{1,0:T(8,128)(2,1)S(1)} %shard_map.101.wide), channel_id=1, source_target_pairs={{0,64},{1,65},{2,66},{3,67},{4,68},{5,69},{6,70},{7,71},{8,72},{9,... | collective-permute-start | bytes 196616 | tf_op jit(solution)/shard_map/ppermute | solution.py:50
  9.8 2.7 %collective-permute-start.8 = (bf16[16,1536]{1,0:T(8,128)(2,1)S(1)}, bf16[16,1536]{1,0:T(8,128)(2,1)S(1)}, u32[]{:S(2)}, u32[]{:S(2)}) collective-permute-start(bf16[16,1536]{1,0:T(8,128)(2,1)S(1)} %get-tuple-element.40.near), channel_id=1, source_target_pairs={{0,66},{1,67},{2,64},{3,65},{4,70},{5,71},{6,68},{7,69},{8,74},{9,... | collective-permute-start | bytes 147464 | tf_op jit(solution)/shard_map/ppermute | solution.py:50
  12.5 2.8 %collective-permute-done.8.far = bf16[16,1536]{1,0:T(8,128)(2,1)S(1)} collective-permute-done((bf16[16,1536]{1,0:T(8,128)(2,1)S(1)}, bf16[16,1536]{1,0:T(8,128)(2,1)S(1)}, u32[]{:S(2)}, u32[]{:S(2)}) %collective-permute-start.8) | collective-permute-done | bytes 49184 | tf_op jit(solution)/shard_map/ppermute | solution.py:50
  15.3 1.4 %collective-permute-start.9 = (bf16[16,3072]{1,0:T(8,128)(2,1)S(1)}, bf16[16,3072]{1,0:T(8,128)(2,1)S(1)}, u32[]{:S(2)}, u32[]{:S(2)}) collective-permute-start(bf16[16,3072]{1,0:T(8,128)(2,1)S(1)} %shard_map.104.refs_0_), channel_id=1, source_target_pairs={{0,4},{1,17},{2,6},{3,19},{4,0},{5,21},{6,2},{7,23},{8,12},{9,25},... | collective-permute-start | bytes 294920 | tf_op jit(solution)/shard_map/ppermute | solution.py:50
  16.7 0.6 shard_map.102.refs_0_
  17.3 0.2 collective-permute-start.5
  17.5 2.9 %collective-permute-start.6 = (bf16[16,8192]{1,0:T(8,128)(2,1)S(1)}, bf16[16,8192]{1,0:T(8,128)(2,1)S(1)}, u32[]{:S(2)}, u32[]{:S(2)}) collective-permute-start(bf16[16,8192]{1,0:T(8,128)(2,1)S(1)} %shard_map.102.refs_0_), channel_id=1, source_target_pairs={{0,8},{1,33},{2,10},{3,35},{4,12},{5,37},{6,14},{7,39},{8,0},{9,41... | collective-permute-start | bytes 786440 | tf_op jit(solution)/shard_map/ppermute | solution.py:50
  20.5 0.8 collective-permute-start.7
  21.2 2.0 %collective-permute-start.10 = (bf16[32,3072]{1,0:T(8,128)(2,1)S(1)}, bf16[32,3072]{1,0:T(8,128)(2,1)S(1)}, u32[]{:S(2)}, u32[]{:S(2)}) collective-permute-start(bf16[32,3072]{1,0:T(8,128)(2,1)S(1)} %shard_map.105.a), channel_id=1, source_target_pairs={{0,12},{1,49},{2,14},{3,51},{4,8},{5,53},{6,10},{7,55},{8,4},{9,57... | collective-permute-start | bytes 589832 | tf_op jit(solution)/shard_map/ppermute | solution.py:50
  23.2 8.9 %collective-permute-done.10.b = bf16[32,3072]{1,0:T(8,128)(2,1)S(1)} collective-permute-done((bf16[32,3072]{1,0:T(8,128)(2,1)S(1)}, bf16[32,3072]{1,0:T(8,128)(2,1)S(1)}, u32[]{:S(2)}, u32[]{:S(2)}) %collective-permute-start.10) | collective-permute-done | bytes 196640 | tf_op jit(solution)/shard_map/ppermute | solution.py:50
  32.1 1.0 collective-permute-start.11
  33.1 1.8 %collective-permute-start.12 = (bf16[64,3072]{1,0:T(8,128)(2,1)S(1)}, bf16[64,3072]{1,0:T(8,128)(2,1)S(1)}, u32[]{:S(2)}, u32[]{:S(2)}) collective-permute-start(bf16[64,3072]{1,0:T(8,128)(2,1)S(1)} %shard_map.106.f0), channel_id=1, source_target_pairs={{0,48},{1,13},{2,50},{3,15},{4,52},{5,9},{6,54},{7,11},{8,56},{9,5... | collective-permute-start | bytes 1179656 | tf_op jit(solution)/shard_map/ppermute | solution.py:50
  35.1 4.0 %collective-permute-done.11.f1 = bf16[64,3072]{1,0:T(8,128)(2,1)S(1)} collective-permute-done((bf16[64,3072]{1,0:T(8,128)(2,1)S(1)}, bf16[64,3072]{1,0:T(8,128)(2,1)S(1)}, u32[]{:S(2)}, u32[]{:S(2)}) %collective-permute-start.11) | collective-permute-done | bytes 393248 | tf_op jit(solution)/shard_map/ppermute | solution.py:50
  39.1 2.1 %collective-permute-done.12.f3 = bf16[64,3072]{1,0:T(8,128)(2,1)S(1)} collective-permute-done((bf16[64,3072]{1,0:T(8,128)(2,1)S(1)}, bf16[64,3072]{1,0:T(8,128)(2,1)S(1)}, u32[]{:S(2)}, u32[]{:S(2)}) %collective-permute-start.12) | collective-permute-done | bytes 393248 | tf_op jit(solution)/shard_map/ppermute | solution.py:50
  41.3 4.1 %collective-permute-start.15 = (bf16[224,8192]{1,0:T(8,128)(2,1)S(1)}, bf16[224,8192]{1,0:T(8,128)(2,1)S(1)}, u32[]{:S(2)}, u32[]{:S(2)}) collective-permute-start(bf16[224,8192]{1,0:T(8,128)(2,1)S(1)} %copy-done.2), channel_id=1, source_target_pairs={{0,1},{1,0},{2,3},{3,2},{4,5},{5,4},{6,7},{7,6},{8,9},{9,8},{10,11... | collective-permute-start | bytes 11010056 | tf_op jit(solution)/shard_map/ppermute | solution.py:50
  45.4 1.4 %collective-permute-start.13 = (bf16[64,8192]{1,0:T(8,128)(2,1)S(1)}, bf16[64,8192]{1,0:T(8,128)(2,1)S(1)}, u32[]{:S(2)}, u32[]{:S(2)}) collective-permute-start(bf16[64,8192]{1,0:T(8,128)(2,1)S(1)} %shard_map.103.refs_1_), channel_id=1, source_target_pairs={{0,16},{1,5},{2,18},{3,7},{4,20},{5,1},{6,22},{7,3},{8,24},{9,13},... | collective-permute-start | bytes 3145736 | tf_op jit(solution)/shard_map/ppermute | solution.py:50
  46.9 1.8 %collective-permute-start.14 = (bf16[64,8192]{1,0:T(8,128)(2,1)S(1)}, bf16[64,8192]{1,0:T(8,128)(2,1)S(1)}, u32[]{:S(2)}, u32[]{:S(2)}) collective-permute-start(bf16[64,8192]{1,0:T(8,128)(2,1)S(1)} %shard_map.103.refs_1_), channel_id=1, source_target_pairs={{0,48},{1,13},{2,50},{3,15},{4,52},{5,9},{6,54},{7,11},{8,56},{9,5... | collective-permute-start | bytes 3145736 | tf_op jit(solution)/shard_map/ppermute | solution.py:50
  48.7 5.2 %collective-permute-done.17.f2 = bf16[64,3072]{1,0:T(8,128)(2,1)S(1)} collective-permute-done((bf16[64,3072]{1,0:T(8,128)(2,1)S(1)}, bf16[64,3072]{1,0:T(8,128)(2,1)S(1)}, u32[]{:S(2)}, u32[]{:S(2)}) %collective-permute-start.17) | collective-permute-done | bytes 393248 | tf_op jit(solution)/shard_map/ppermute | solution.py:50
  54.0 1.4 %collective-permute-start.18 = (bf16[256,3328]{1,0:T(8,128)(2,1)S(1)}, bf16[256,3328]{1,0:T(8,128)(2,1)S(1)}, u32[]{:S(2)}, u32[]{:S(2)}) collective-permute-start(bf16[256,3328]{1,0:T(8,128)(2,1)S(1)} %shard_map.110.refs_9_), channel_id=1, source_target_pairs={{0,1},{1,0},{2,3},{3,2},{4,5},{5,4},{6,7},{7,6},{8,9},{9,8},{10,11... | collective-permute-start | bytes 5111816 | tf_op jit(solution)/shard_map/ppermute | solution.py:50
  55.5 8.1 %collective-permute-done.13.refs_2_ = bf16[64,8192]{1,0:T(8,128)(2,1)S(1)} collective-permute-done((bf16[64,8192]{1,0:T(8,128)(2,1)S(1)}, bf16[64,8192]{1,0:T(8,128)(2,1)S(1)}, u32[]{:S(2)}, u32[]{:S(2)}) %collective-permute-start.13) | collective-permute-done | bytes 1048608 | tf_op jit(solution)/shard_map/ppermute | solution.py:50
  63.6 1.5 %collective-permute-done.14.refs_3_ = bf16[64,8192]{1,0:T(8,128)(2,1)S(1)} collective-permute-done((bf16[64,8192]{1,0:T(8,128)(2,1)S(1)}, bf16[64,8192]{1,0:T(8,128)(2,1)S(1)}, u32[]{:S(2)}, u32[]{:S(2)}) %collective-permute-start.14) | collective-permute-done | bytes 1048608 | tf_op jit(solution)/shard_map/ppermute | solution.py:50
  65.1 4.1 %shard_map.109.refs_4_ = f32[896,192]{1,0:T(8,128)S(1)} custom-call(f32[8,128]{1,0:T(8,128)S(1)} %shard_map.108.refs_0_, bf16[64,8192]{1,0:T(8,128)(2,1)S(1)} %shard_map.103.refs_1_, bf16[64,8192]{1,0:T(8,128)(2,1)S(1)} %collective-permute-done.13.refs_2_, bf16[64,8192]{1,0:T(8,128)(2,1)S(1)} %collective-permute-done.14.refs_3_, ...), custom_call_target="tpu_custom_call" | custom-call | flops 9200000000 | bytes 28800000 | tf_op jit(solution)/shard_map/pallas_call | solution.py:160
  69.2 6.0 %shard_map.111 = (f32[64,8192]{1,0:T(8,128)S(1)}, bf16[64,8192]{1,0:T(8,128)(2,1)S(1)}, bf16[64,8192]{1,0:T(8,128)(2,1)S(1)}, bf16[128,8192]{1,0:T(8,128)(2,1)S(1)}, bf16[64,8192]{1,0:T(8,128)(2,1)S(1)}) custom-call(s32[5]{0:T(128)S(1)} %stack.23.place.refs_0_, bf16[64,8192]{1,0:T(8,128)(2,1)S(1)} %shard_map.103.refs_1_, ...), custom_call_target="tpu_custom_call" | custom-call | flops 1 | bytes 1 | tf_op jit(solution)/shard_map/pallas_call | solution.py:181
  75.3 1.2 collective-permute-start.20
  76.5 4.1 %shard_map.113.refs_1_ = f32[896,64]{1,0:T(8,128)S(1)} custom-call(bf16[64,8192]{1,0:T(8,128)(2,1)S(1)} %collective-permute-done.21.refs_0_, bf16[224,8192]{1,0:T(8,128)(2,1)S(1)} %copy-done.1, bf16[224,8192]{1,0:T(8,128)(2,1)S(1)} %collective-permute-done.4.refs_5_.refs_2_, bf16[224,8192]{1,0:T(8,128)(2,1)S(1)} %copy-done.2, ...), custom_call_target="tpu_custom_call" | custom-call | flops 9200000000 | bytes 28800000 | tf_op jit(solution)/shard_map/pallas_call | solution.py:160
  80.5 3.5 %shard_map.114 = bf16[64,8192]{1,0:T(8,128)(2,1)S(1)} custom-call(bf16[64,8192]{1,0:T(8,128)(2,1)S(1)} %collective-permute-done.21.refs_0_, f32[896,64]{1,0:T(8,128)S(1)} %shard_map.113.refs_1_, bf16[224,8192]{1,0:T(8,128)(2,1)S(1)} %copy-done, bf16[224,8192]{1,0:T(8,128)(2,1)S(1)} %collective-permute-done.16.refs_6_.refs_3_, ...), custom_call_target="tpu_custom_call" | custom-call | flops 1 | bytes 1 | tf_op jit(solution)/shard_map/pallas_call | solution.py:181
  84.1 2.1 %collective-permute-start.22 = (bf16[64,8192]{1,0:T(8,128)(2,1)S(1)}, bf16[64,8192]{1,0:T(8,128)(2,1)S(1)}, u32[]{:S(2)}, u32[]{:S(2)}) collective-permute-start(bf16[64,8192]{1,0:T(8,128)(2,1)S(1)} %shard_map.114), channel_id=1, source_target_pairs={{0,32},{1,9},{2,34},{3,11},{4,36},{5,13},{6,38},{7,15},{8,40},{9,1... | collective-permute-start | bytes 3145736 | tf_op jit(solution)/shard_map/ppermute | solution.py:50
  86.2 3.0 %collective-permute-done.19.b1 = bf16[64,8192]{1,0:T(8,128)(2,1)S(1)} collective-permute-done((bf16[64,8192]{1,0:T(8,128)(2,1)S(1)}, bf16[64,8192]{1,0:T(8,128)(2,1)S(1)}, u32[]{:S(2)}, u32[]{:S(2)}) %collective-permute-start.19) | collective-permute-done | bytes 1048608 | tf_op jit(solution)/shard_map/ppermute | solution.py:50
  89.2 12.8 %collective-permute-done.20.b3 = bf16[64,8192]{1,0:T(8,128)(2,1)S(1)} collective-permute-done((bf16[64,8192]{1,0:T(8,128)(2,1)S(1)}, bf16[64,8192]{1,0:T(8,128)(2,1)S(1)}, u32[]{:S(2)}, u32[]{:S(2)}) %collective-permute-start.20) | collective-permute-done | bytes 1048608 | tf_op jit(solution)/shard_map/ppermute | solution.py:50
  102.0 0.3 shard_map.112.own
  102.6 3.3 %collective-permute-start.24 = (bf16[16,8192]{1,0:T(8,128)(2,1)S(1)}, bf16[16,8192]{1,0:T(8,128)(2,1)S(1)}, u32[]{:S(2)}, u32[]{:S(2)}) collective-permute-start(bf16[16,8192]{1,0:T(8,128)(2,1)S(1)} %get-tuple-element.61), channel_id=1, source_target_pairs={{0,8},{1,33},{2,10},{3,35},{4,12},{5,37},{6,14},{7,39},{8,0},{9,41... | collective-permute-start | bytes 786440 | tf_op jit(solution)/shard_map/ppermute | solution.py:50
  106.0 0.5 collective-permute-start.25
  106.5 1.7 %collective-permute-done.23.b1 = bf16[16,8192]{1,0:T(8,128)(2,1)S(1)} collective-permute-done((bf16[16,8192]{1,0:T(8,128)(2,1)S(1)}, bf16[16,8192]{1,0:T(8,128)(2,1)S(1)}, u32[]{:S(2)}, u32[]{:S(2)}) %collective-permute-start.23) | collective-permute-done | bytes 262176 | tf_op jit(solution)/shard_map/ppermute | solution.py:50
  108.1 4.7 %collective-permute-done.24.b2 = bf16[16,8192]{1,0:T(8,128)(2,1)S(1)} collective-permute-done((bf16[16,8192]{1,0:T(8,128)(2,1)S(1)}, bf16[16,8192]{1,0:T(8,128)(2,1)S(1)}, u32[]{:S(2)}, u32[]{:S(2)}) %collective-permute-start.24) | collective-permute-done | bytes 262176 | tf_op jit(solution)/shard_map/ppermute | solution.py:50
  112.9 2.6 %collective-permute-done.25.b3 = bf16[16,8192]{1,0:T(8,128)(2,1)S(1)} collective-permute-done((bf16[16,8192]{1,0:T(8,128)(2,1)S(1)}, bf16[16,8192]{1,0:T(8,128)(2,1)S(1)}, u32[]{:S(2)}, u32[]{:S(2)}) %collective-permute-start.25) | collective-permute-done | bytes 262176 | tf_op jit(solution)/shard_map/ppermute | solution.py:50
  115.5 0.7 shard_map.116
  116.3 3.9 %collective-permute-start.27 = (bf16[8,4096]{1,0:T(8,128)(2,1)S(1)}, bf16[8,4096]{1,0:T(8,128)(2,1)S(1)}, u32[]{:S(2)}, u32[]{:S(2)}) collective-permute-start(bf16[8,4096]{1,0:T(8,128)(2,1)S(1)} %get-tuple-element.65), channel_id=1, source_target_pairs={{0,64},{1,65},{2,66},{3,67},{4,68},{5,69},{6,70},{7,71},{8,72},{9,... | collective-permute-start | bytes 196616 | tf_op jit(solution)/shard_map/ppermute | solution.py:50
  120.2 2.4 %collective-permute-done.27 = bf16[8,4096]{1,0:T(8,128)(2,1)S(1)} collective-permute-done((bf16[8,4096]{1,0:T(8,128)(2,1)S(1)}, bf16[8,4096]{1,0:T(8,128)(2,1)S(1)}, u32[]{:S(2)}, u32[]{:S(2)}) %collective-permute-start.27) | collective-permute-done | bytes 65568 | tf_op jit(solution)/shard_map/ppermute | solution.py:50
  122.6 2.1 %collective-permute-done.28 = bf16[8,4096]{1,0:T(8,128)(2,1)S(1)} collective-permute-done((bf16[8,4096]{1,0:T(8,128)(2,1)S(1)}, bf16[8,4096]{1,0:T(8,128)(2,1)S(1)}, u32[]{:S(2)}, u32[]{:S(2)}) %collective-permute-start.28) | collective-permute-done | bytes 65568 | tf_op jit(solution)/shard_map/ppermute | solution.py:50
  124.7 2.5 %collective-permute-start.29 = (bf16[8,2048]{1,0:T(8,128)(2,1)S(1)}, bf16[8,2048]{1,0:T(8,128)(2,1)S(1)}, u32[]{:S(2)}, u32[]{:S(2)}) collective-permute-start(bf16[8,2048]{1,0:T(8,128)(2,1)S(1)} %get-tuple-element.68), channel_id=1, source_target_pairs={{0,1},{1,0},{2,3},{3,2},{4,5},{5,4},{6,7},{7,6},{8,9},{9,8},{10,11... | collective-permute-start | bytes 98312 | tf_op jit(solution)/shard_map/ppermute | solution.py:50
  127.2 0.9 collective-permute-done.29
  128.1 0.6 maximum_select_fusion
  (45 shorter events, 1.0 us)
Async XLA Ops:
  1.5 2.4 %collective-permute-start = (bf16[8,2048]{1,0:T(8,128)(2,1)S(1)}, bf16[8,2048]{1,0:T(8,128)(2,1)S(1)}, u32[]{:S(2)}, u32[]{:S(2)}) collective-permute-start(bf16[8,2048]{1,0:T(8,128)(2,1)S(1)} %get-tuple-element.37), channel_id=1, source_target_pairs={{0,1},{1,0},{2,3},{3,2},{4,5},{5,4},{6,7},{7,6},{8,9},{9,8},{10,11... | collective-permute-start | bytes 98312 | tf_op jit(solution)/shard_map/ppermute | solution.py:50
  4.4 12.9 %collective-permute-start.4 = (bf16[224,8192]{1,0:T(8,128)(2,1)}, bf16[224,8192]{1,0:T(8,128)(2,1)S(1)}, u32[]{:S(2)}, u32[]{:S(2)}) collective-permute-start(bf16[224,8192]{1,0:T(8,128)(2,1)} %refs_1_), channel_id=1, source_target_pairs={{0,1},{1,0},{2,3},{3,2},{4,5},{5,4},{6,7},{7,6},{8,9},{9,8},{10,11... | collective-permute-start | bytes 11010056 | tf_op jit(solution)/shard_map/ppermute | solution.py:50
  4.8 11.9 %collective-permute-start.1 = (bf16[8,4096]{1,0:T(8,128)(2,1)S(1)}, bf16[8,4096]{1,0:T(8,128)(2,1)S(1)}, u32[]{:S(2)}, u32[]{:S(2)}) collective-permute-start(bf16[8,4096]{1,0:T(8,128)(2,1)S(1)} %shard_map.101.wide), channel_id=1, source_target_pairs={{0,2},{1,3},{2,0},{3,1},{4,6},{5,7},{6,4},{7,5},{8,10},{9,11},{10,... | collective-permute-start | bytes 196616 | tf_op jit(solution)/shard_map/ppermute | solution.py:50
  6.5 10.2 %collective-permute-start.2 = (bf16[8,4096]{1,0:T(8,128)(2,1)S(1)}, bf16[8,4096]{1,0:T(8,128)(2,1)S(1)}, u32[]{:S(2)}, u32[]{:S(2)}) collective-permute-start(bf16[8,4096]{1,0:T(8,128)(2,1)S(1)} %shard_map.101.wide), channel_id=1, source_target_pairs={{0,64},{1,65},{2,66},{3,67},{4,68},{5,69},{6,70},{7,71},{8,72},{9,... | collective-permute-start | bytes 196616 | tf_op jit(solution)/shard_map/ppermute | solution.py:50
  9.8 6.9 %collective-permute-start.3 = (bf16[8,4096]{1,0:T(8,128)(2,1)S(1)}, bf16[8,4096]{1,0:T(8,128)(2,1)S(1)}, u32[]{:S(2)}, u32[]{:S(2)}) collective-permute-start(bf16[8,4096]{1,0:T(8,128)(2,1)S(1)} %shard_map.101.wide), channel_id=1, source_target_pairs={{0,66},{1,67},{2,64},{3,65},{4,70},{5,71},{6,68},{7,69},{8,74},{9,... | collective-permute-start | bytes 196616 | tf_op jit(solution)/shard_map/ppermute | solution.py:50
  9.8 5.4 %collective-permute-start.8 = (bf16[16,1536]{1,0:T(8,128)(2,1)S(1)}, bf16[16,1536]{1,0:T(8,128)(2,1)S(1)}, u32[]{:S(2)}, u32[]{:S(2)}) collective-permute-start(bf16[16,1536]{1,0:T(8,128)(2,1)S(1)} %get-tuple-element.40.near), channel_id=1, source_target_pairs={{0,66},{1,67},{2,64},{3,65},{4,70},{5,71},{6,68},{7,69},{8,74},{9,... | collective-permute-start | bytes 147464 | tf_op jit(solution)/shard_map/ppermute | solution.py:50
  15.3 19.7 %copy-start.3 = (bf16[224,64]{0,1:T(8,128)(2,1)S(1)}, bf16[224,64]{0,1:T(8,128)(2,1)}, u32[]{:S(2)}) copy-start(bf16[224,64]{0,1:T(8,128)(2,1)} %param.15) | copy-start | bytes 86020
  15.3 19.7 %copy-start.4 = (bf16[224,64]{0,1:T(8,128)(2,1)S(1)}, bf16[224,64]{0,1:T(8,128)(2,1)}, u32[]{:S(2)}) copy-start(bf16[224,64]{0,1:T(8,128)(2,1)} %param.17) | copy-start | bytes 86020
  15.3 19.6 %copy-start.5 = (bf16[224,64]{0,1:T(8,128)(2,1)S(1)}, bf16[224,64]{0,1:T(8,128)(2,1)}, u32[]{:S(2)}) copy-start(bf16[224,64]{0,1:T(8,128)(2,1)} %param.18) | copy-start | bytes 86020
  15.3 5.9 %collective-permute-start.9 = (bf16[16,3072]{1,0:T(8,128)(2,1)S(1)}, bf16[16,3072]{1,0:T(8,128)(2,1)S(1)}, u32[]{:S(2)}, u32[]{:S(2)}) collective-permute-start(bf16[16,3072]{1,0:T(8,128)(2,1)S(1)} %shard_map.104.refs_0_), channel_id=1, source_target_pairs={{0,4},{1,17},{2,6},{3,19},{4,0},{5,21},{6,2},{7,23},{8,12},{9,25},... | collective-permute-start | bytes 294920 | tf_op jit(solution)/shard_map/ppermute | solution.py:50
  17.3 17.7 %collective-permute-start.5 = (bf16[16,8192]{1,0:T(8,128)(2,1)S(1)}, bf16[16,8192]{1,0:T(8,128)(2,1)S(1)}, u32[]{:S(2)}, u32[]{:S(2)}) collective-permute-start(bf16[16,8192]{1,0:T(8,128)(2,1)S(1)} %shard_map.102.refs_0_), channel_id=1, source_target_pairs={{0,4},{1,17},{2,6},{3,19},{4,0},{5,21},{6,2},{7,23},{8,12},{9,25},... | collective-permute-start | bytes 786440 | tf_op jit(solution)/shard_map/ppermute | solution.py:50
  17.5 17.5 %collective-permute-start.6 = (bf16[16,8192]{1,0:T(8,128)(2,1)S(1)}, bf16[16,8192]{1,0:T(8,128)(2,1)S(1)}, u32[]{:S(2)}, u32[]{:S(2)}) collective-permute-start(bf16[16,8192]{1,0:T(8,128)(2,1)S(1)} %shard_map.102.refs_0_), channel_id=1, source_target_pairs={{0,8},{1,33},{2,10},{3,35},{4,12},{5,37},{6,14},{7,39},{8,0},{9,41... | collective-permute-start | bytes 786440 | tf_op jit(solution)/shard_map/ppermute | solution.py:50
  20.5 14.6 %collective-permute-start.7 = (bf16[16,8192]{1,0:T(8,128)(2,1)S(1)}, bf16[16,8192]{1,0:T(8,128)(2,1)S(1)}, u32[]{:S(2)}, u32[]{:S(2)}) collective-permute-start(bf16[16,8192]{1,0:T(8,128)(2,1)S(1)} %shard_map.102.refs_0_), channel_id=1, source_target_pairs={{0,12},{1,49},{2,14},{3,51},{4,8},{5,53},{6,10},{7,55},{8,4},{9,57... | collective-permute-start | bytes 786440 | tf_op jit(solution)/shard_map/ppermute | solution.py:50
  21.2 10.8 %collective-permute-start.10 = (bf16[32,3072]{1,0:T(8,128)(2,1)S(1)}, bf16[32,3072]{1,0:T(8,128)(2,1)S(1)}, u32[]{:S(2)}, u32[]{:S(2)}) collective-permute-start(bf16[32,3072]{1,0:T(8,128)(2,1)S(1)} %shard_map.105.a), channel_id=1, source_target_pairs={{0,12},{1,49},{2,14},{3,51},{4,8},{5,53},{6,10},{7,55},{8,4},{9,57... | collective-permute-start | bytes 589832 | tf_op jit(solution)/shard_map/ppermute | solution.py:50
  32.1 7.0 %collective-permute-start.11 = (bf16[64,3072]{1,0:T(8,128)(2,1)S(1)}, bf16[64,3072]{1,0:T(8,128)(2,1)S(1)}, u32[]{:S(2)}, u32[]{:S(2)}) collective-permute-start(bf16[64,3072]{1,0:T(8,128)(2,1)S(1)} %shard_map.106.f0), channel_id=1, source_target_pairs={{0,16},{1,5},{2,18},{3,7},{4,20},{5,1},{6,22},{7,3},{8,24},{9,13},... | collective-permute-start | bytes 1179656 | tf_op jit(solution)/shard_map/ppermute | solution.py:50
  33.1 8.1 %collective-permute-start.12 = (bf16[64,3072]{1,0:T(8,128)(2,1)S(1)}, bf16[64,3072]{1,0:T(8,128)(2,1)S(1)}, u32[]{:S(2)}, u32[]{:S(2)}) collective-permute-start(bf16[64,3072]{1,0:T(8,128)(2,1)S(1)} %shard_map.106.f0), channel_id=1, source_target_pairs={{0,48},{1,13},{2,50},{3,15},{4,52},{5,9},{6,54},{7,11},{8,56},{9,5... | collective-permute-start | bytes 1179656 | tf_op jit(solution)/shard_map/ppermute | solution.py:50
  35.0 6.3 %copy-start.2 = (bf16[224,8192]{1,0:T(8,128)(2,1)S(1)}, bf16[224,8192]{1,0:T(8,128)(2,1)}, u32[]{:S(2)}) copy-start(bf16[224,8192]{1,0:T(8,128)(2,1)} %refs_3_) | copy-start | bytes 11010052
  35.0 10.4 %copy-start = (bf16[224,8192]{1,0:T(8,128)(2,1)S(1)}, bf16[224,8192]{1,0:T(8,128)(2,1)}, u32[]{:S(2)}) copy-start(bf16[224,8192]{1,0:T(8,128)(2,1)} %refs_2_) | copy-start | bytes 11010052
  35.0 20.4 %copy-start.1 = (bf16[224,8192]{1,0:T(8,128)(2,1)S(1)}, bf16[224,8192]{1,0:T(8,128)(2,1)}, u32[]{:S(2)}) copy-start(bf16[224,8192]{1,0:T(8,128)(2,1)} %refs_1_) | copy-start | bytes 11010052
  41.3 14.2 %collective-permute-start.15 = (bf16[224,8192]{1,0:T(8,128)(2,1)S(1)}, bf16[224,8192]{1,0:T(8,128)(2,1)S(1)}, u32[]{:S(2)}, u32[]{:S(2)}) collective-permute-start(bf16[224,8192]{1,0:T(8,128)(2,1)S(1)} %copy-done.2), channel_id=1, source_target_pairs={{0,1},{1,0},{2,3},{3,2},{4,5},{5,4},{6,7},{7,6},{8,9},{9,8},{10,11... | collective-permute-start | bytes 11010056 | tf_op jit(solution)/shard_map/ppermute | solution.py:50
  45.3 23.8 %collective-permute-start.16 = (bf16[224,8192]{1,0:T(8,128)(2,1)S(1)}, bf16[224,8192]{1,0:T(8,128)(2,1)S(1)}, u32[]{:S(2)}, u32[]{:S(2)}) collective-permute-start(bf16[224,8192]{1,0:T(8,128)(2,1)S(1)} %copy-done), channel_id=1, source_target_pairs={{0,1},{1,0},{2,3},{3,2},{4,5},{5,4},{6,7},{7,6},{8,9},{9,8},{10,11... | collective-permute-start | bytes 11010056 | tf_op jit(solution)/shard_map/ppermute | solution.py:50
  45.4 8.5 %collective-permute-start.17 = (bf16[64,3072]{1,0:T(8,128)(2,1)S(1)}, bf16[64,3072]{1,0:T(8,128)(2,1)S(1)}, u32[]{:S(2)}, u32[]{:S(2)}) collective-permute-start(bf16[64,3072]{1,0:T(8,128)(2,1)S(1)} %shard_map.106.f0), channel_id=1, source_target_pairs={{0,32},{1,9},{2,34},{3,11},{4,36},{5,13},{6,38},{7,15},{8,40},{9,1... | collective-permute-start | bytes 1179656 | tf_op jit(solution)/shard_map/ppermute | solution.py:50
  45.4 18.2 %collective-permute-start.13 = (bf16[64,8192]{1,0:T(8,128)(2,1)S(1)}, bf16[64,8192]{1,0:T(8,128)(2,1)S(1)}, u32[]{:S(2)}, u32[]{:S(2)}) collective-permute-start(bf16[64,8192]{1,0:T(8,128)(2,1)S(1)} %shard_map.103.refs_1_), channel_id=1, source_target_pairs={{0,16},{1,5},{2,18},{3,7},{4,20},{5,1},{6,22},{7,3},{8,24},{9,13},... | collective-permute-start | bytes 3145736 | tf_op jit(solution)/shard_map/ppermute | solution.py:50
  46.9 18.2 %collective-permute-start.14 = (bf16[64,8192]{1,0:T(8,128)(2,1)S(1)}, bf16[64,8192]{1,0:T(8,128)(2,1)S(1)}, u32[]{:S(2)}, u32[]{:S(2)}) collective-permute-start(bf16[64,8192]{1,0:T(8,128)(2,1)S(1)} %shard_map.103.refs_1_), channel_id=1, source_target_pairs={{0,48},{1,13},{2,50},{3,15},{4,52},{5,9},{6,54},{7,11},{8,56},{9,5... | collective-permute-start | bytes 3145736 | tf_op jit(solution)/shard_map/ppermute | solution.py:50
  54.0 15.2 %collective-permute-start.18 = (bf16[256,3328]{1,0:T(8,128)(2,1)S(1)}, bf16[256,3328]{1,0:T(8,128)(2,1)S(1)}, u32[]{:S(2)}, u32[]{:S(2)}) collective-permute-start(bf16[256,3328]{1,0:T(8,128)(2,1)S(1)} %shard_map.110.refs_9_), channel_id=1, source_target_pairs={{0,1},{1,0},{2,3},{3,2},{4,5},{5,4},{6,7},{7,6},{8,9},{9,8},{10,11... | collective-permute-start | bytes 5111816 | tf_op jit(solution)/shard_map/ppermute | solution.py:50
  55.4 21.0 %collective-permute-start.21 = (bf16[64,8192]{1,0:T(8,128)(2,1)S(1)}, bf16[64,8192]{1,0:T(8,128)(2,1)S(1)}, u32[]{:S(2)}, u32[]{:S(2)}) collective-permute-start(bf16[64,8192]{1,0:T(8,128)(2,1)S(1)} %shard_map.103.refs_1_), channel_id=1, source_target_pairs={{0,32},{1,9},{2,34},{3,11},{4,36},{5,13},{6,38},{7,15},{8,40},{9,1... | collective-permute-start | bytes 3145736 | tf_op jit(solution)/shard_map/ppermute | solution.py:50
  75.2 14.0 %collective-permute-start.19 = (bf16[64,8192]{1,0:T(8,128)(2,1)S(1)}, bf16[64,8192]{1,0:T(8,128)(2,1)S(1)}, u32[]{:S(2)}, u32[]{:S(2)}) collective-permute-start(bf16[64,8192]{1,0:T(8,128)(2,1)S(1)} %get-tuple-element.53), channel_id=1, source_target_pairs={{0,16},{1,5},{2,18},{3,7},{4,20},{5,1},{6,22},{7,3},{8,24},{9,13},... | collective-permute-start | bytes 3145736 | tf_op jit(solution)/shard_map/ppermute | solution.py:50
  75.3 26.7 %collective-permute-start.20 = (bf16[64,8192]{1,0:T(8,128)(2,1)S(1)}, bf16[64,8192]{1,0:T(8,128)(2,1)S(1)}, u32[]{:S(2)}, u32[]{:S(2)}) collective-permute-start(bf16[64,8192]{1,0:T(8,128)(2,1)S(1)} %get-tuple-element.54), channel_id=1, source_target_pairs={{0,48},{1,13},{2,50},{3,15},{4,52},{5,9},{6,54},{7,11},{8,56},{9,5... | collective-permute-start | bytes 3145736 | tf_op jit(solution)/shard_map/ppermute | solution.py:50
  84.1 18.2 %collective-permute-start.22 = (bf16[64,8192]{1,0:T(8,128)(2,1)S(1)}, bf16[64,8192]{1,0:T(8,128)(2,1)S(1)}, u32[]{:S(2)}, u32[]{:S(2)}) collective-permute-start(bf16[64,8192]{1,0:T(8,128)(2,1)S(1)} %shard_map.114), channel_id=1, source_target_pairs={{0,32},{1,9},{2,34},{3,11},{4,36},{5,13},{6,38},{7,15},{8,40},{9,1... | collective-permute-start | bytes 3145736 | tf_op jit(solution)/shard_map/ppermute | solution.py:50
  102.5 5.6 %collective-permute-start.23 = (bf16[16,8192]{1,0:T(8,128)(2,1)S(1)}, bf16[16,8192]{1,0:T(8,128)(2,1)S(1)}, u32[]{:S(2)}, u32[]{:S(2)}) collective-permute-start(bf16[16,8192]{1,0:T(8,128)(2,1)S(1)} %get-tuple-element.60), channel_id=1, source_target_pairs={{0,4},{1,17},{2,6},{3,19},{4,0},{5,21},{6,2},{7,23},{8,12},{9,25},... | collective-permute-start | bytes 786440 | tf_op jit(solution)/shard_map/ppermute | solution.py:50
  102.6 10.2 %collective-permute-start.24 = (bf16[16,8192]{1,0:T(8,128)(2,1)S(1)}, bf16[16,8192]{1,0:T(8,128)(2,1)S(1)}, u32[]{:S(2)}, u32[]{:S(2)}) collective-permute-start(bf16[16,8192]{1,0:T(8,128)(2,1)S(1)} %get-tuple-element.61), channel_id=1, source_target_pairs={{0,8},{1,33},{2,10},{3,35},{4,12},{5,37},{6,14},{7,39},{8,0},{9,41... | collective-permute-start | bytes 786440 | tf_op jit(solution)/shard_map/ppermute | solution.py:50
  106.0 9.5 %collective-permute-start.25 = (bf16[16,8192]{1,0:T(8,128)(2,1)S(1)}, bf16[16,8192]{1,0:T(8,128)(2,1)S(1)}, u32[]{:S(2)}, u32[]{:S(2)}) collective-permute-start(bf16[16,8192]{1,0:T(8,128)(2,1)S(1)} %get-tuple-element.62), channel_id=1, source_target_pairs={{0,12},{1,49},{2,14},{3,51},{4,8},{5,53},{6,10},{7,55},{8,4},{9,57... | collective-permute-start | bytes 786440 | tf_op jit(solution)/shard_map/ppermute | solution.py:50
  116.2 4.0 %collective-permute-start.26 = (bf16[8,4096]{1,0:T(8,128)(2,1)S(1)}, bf16[8,4096]{1,0:T(8,128)(2,1)S(1)}, u32[]{:S(2)}, u32[]{:S(2)}) collective-permute-start(bf16[8,4096]{1,0:T(8,128)(2,1)S(1)} %get-tuple-element.64), channel_id=1, source_target_pairs={{0,2},{1,3},{2,0},{3,1},{4,6},{5,7},{6,4},{7,5},{8,10},{9,11},{10,... | collective-permute-start | bytes 196616 | tf_op jit(solution)/shard_map/ppermute | solution.py:50
  116.3 6.3 %collective-permute-start.27 = (bf16[8,4096]{1,0:T(8,128)(2,1)S(1)}, bf16[8,4096]{1,0:T(8,128)(2,1)S(1)}, u32[]{:S(2)}, u32[]{:S(2)}) collective-permute-start(bf16[8,4096]{1,0:T(8,128)(2,1)S(1)} %get-tuple-element.65), channel_id=1, source_target_pairs={{0,64},{1,65},{2,66},{3,67},{4,68},{5,69},{6,70},{7,71},{8,72},{9,... | collective-permute-start | bytes 196616 | tf_op jit(solution)/shard_map/ppermute | solution.py:50
  120.2 4.5 %collective-permute-start.28 = (bf16[8,4096]{1,0:T(8,128)(2,1)S(1)}, bf16[8,4096]{1,0:T(8,128)(2,1)S(1)}, u32[]{:S(2)}, u32[]{:S(2)}) collective-permute-start(bf16[8,4096]{1,0:T(8,128)(2,1)S(1)} %get-tuple-element.66), channel_id=1, source_target_pairs={{0,66},{1,67},{2,64},{3,65},{4,70},{5,71},{6,68},{7,69},{8,74},{9,... | collective-permute-start | bytes 196616 | tf_op jit(solution)/shard_map/ppermute | solution.py:50
  124.7 3.4 %collective-permute-start.29 = (bf16[8,2048]{1,0:T(8,128)(2,1)S(1)}, bf16[8,2048]{1,0:T(8,128)(2,1)S(1)}, u32[]{:S(2)}, u32[]{:S(2)}) collective-permute-start(bf16[8,2048]{1,0:T(8,128)(2,1)S(1)} %get-tuple-element.68), channel_id=1, source_target_pairs={{0,1},{1,0},{2,3},{3,2},{4,5},{5,4},{6,7},{7,6},{8,9},{9,8},{10,11... | collective-permute-start | bytes 98312 | tf_op jit(solution)/shard_map/ppermute | solution.py:50

commit v6 on v5

--- a/solution.py
+++ b/solution.py
@@ -18,7 +18,7 @@
 STEPS = WIDTH // TILE
 PARTS = TILE // 256
 f32, bf16 = jnp.float32, jnp.bfloat16
-C1, C2, CK = 3.6, 3.8, 8
+CK = 8
 SMALL = pl.CostEstimate(flops=1, bytes_accessed=1, transcendentals=0)
 
 
@@ -220,37 +220,36 @@
         factor[:, col] = ranks[i // 2, (i % 2) * 16 : (i % 2) * 16 + 16, :]
 
 
-def shape_kernel(place, own, other, wide):
+def shape_kernel(place, own, other, factor, wide, message):
     c = place[3]
     wide[:, pl.ds(pl.multiple_of(c * QUARTER, QUARTER), QUARTER)] = own[...]
     wide[:, pl.ds(pl.multiple_of((1 - c) * QUARTER, QUARTER), QUARTER)] = other[...]
-
-
-def pack_kernel(place, wide, z1, z2, z3, out):
+    rows = widen(wide[...])
+    rows = jnp.concatenate([rows[:, :QUARTER], rows[:, QUARTER:]], axis=0)
+    message[:, :QUARTER] = rows.astype(bf16)
+    message[:, QUARTER:] = factor[...]
+
+
+def pack_kernel(place, wide, z1, z2, message, far_message, out):
     zl = place[4]
     here = pl.ds(pl.multiple_of(zl * HALF, HALF), HALF)
     there = pl.ds(pl.multiple_of((1 - zl) * HALF, HALF), HALF)
-    pair = lambda a, b: jnp.concatenate([widen(a[...]), widen(b[...])], 0).astype(bf16)
-    out[:, here] = pair(wide, z2)
-    out[:, there] = pair(z1, z3)
-
-
-def pair_kernel(near, far, out):
+    z3 = widen(far_message[:, :QUARTER])
+    z3 = jnp.concatenate([z3[:8], z3[8:]], axis=1)
+    pair = lambda a, b: jnp.concatenate([widen(a), widen(b)], 0).astype(bf16)
+    out[:, here] = pair(wide[...], z2[...])
+    out[:, there] = pair(z1[...], z3)
     for i in range(6):
-        out[:, 512 * i : 512 * i + 256] = near[:, 256 * i : 256 * i + 256]
-        out[:, 512 * i + 256 : 512 * i + 512] = far[:, 256 * i : 256 * i + 256]
-
-
-def swap_kernel(a, b, out):
-    out[:32, :] = a[...]
-    out[32:48, :] = b[16:, :]
-    out[48:, :] = b[:16, :]
-
-
-def rows_kernel(*refs):
-    out, step = refs[-1], refs[0].shape[0]
-    for k, r in enumerate(refs[:-1]):
-        out[step * k : step * k + step, :] = r[...]
+        at, col = WIDTH + 512 * i, QUARTER + 256 * i
+        out[:, at : at + 256] = message[:, col : col + 256]
+        out[:, at + 256 : at + 512] = far_message[:, col : col + 256]
+
+
+def unpack_kernel(*refs):
+    got, (block, factor) = refs[:4], refs[4:]
+    for k, g in enumerate(got):
+        block[16 * k : 16 * k + 16, :] = g[:, :WIDTH]
+        factor[16 * k : 16 * k + 16, :] = g[:, WIDTH:]
 
 
 def touch_kernel(gate_w, up_w, down_w, out):
@@ -320,45 +319,40 @@
         scratch=[pltpu.VMEM((3, 32, 256), bf16), pltpu.SemaphoreType.DMA((5,))],
     )
     other = send(other, CORE)
-    (wide,) = local(shape_kernel, [((8, HALF), bf16)], (own, other), place)
-
-    far_factor = send(factor, ALONG_Z[3])
-    z1, z2, z3 = (send(wide, ALONG_Z[k]) for k in (1, 2, 3))
+    wide, message = local(
+        shape_kernel,
+        [((8, HALF), bf16), ((16, QUARTER + 1536), bf16)],
+        (own, other, factor),
+        place,
+    )
+
+    z1, z2, z3 = (
+        send(v, ALONG_Z[k]) for k, v in ((1, wide), (2, wide), (3, message))
+    )
     gate2 = send(after(frozen_gate_weight, wide), CORE)
-    (factor,) = local(pair_kernel, [((16, 3072), bf16)], (factor, far_factor))
-    near = send(factor, FIRST[1])
-    (rows,) = local(
-        pack_kernel, [((16, WIDTH), bf16)], (wide, z1, z2, z3), place, price=price_of(C2)
-    )
-
-    rows = after(rows, gate2)
-    (factor,) = local(rows_kernel, [((32, 3072), bf16)], (factor, near))
-    near = send(factor, FIRST[3])
-    rows = [rows] + [send(rows, FIRST[k]) for k in (1, 2, 3)]
-    (factor,) = local(swap_kernel, [((64, 3072), bf16)], (factor, near))
-    factors = {0: factor, 1: send(factor, SECOND[1]), 3: send(factor, SECOND[3])}
+    up2 = send(after(frozen_up_weight, wide), CORE)
+    (packed,) = local(
+        pack_kernel, [((16, WIDTH + 3072), bf16)], (wide, z1, z2, message, z3), place
+    )
+
+    packed = after(packed, gate2)
+    got = [packed] + [send(packed, FIRST[k]) for k in (1, 2, 3)]
+    down2 = send(after(frozen_down_weight, packed), CORE)
     seconds = (adapter_second_gate, adapter_second_up, adapter_first_down)
     (seconds,) = local(
-        seconds_kernel, [((256, 256), bf16)], [a.T for a in after(seconds, rows[0])]
-    )
-    (block,) = local(rows_kernel, [((64, WIDTH), bf16)], rows, price=price_of(C1))
-
-    block, factors = after((block, factors), (block, factors))
-    block = after(block, seconds)
-    factors[2] = send(factors[0], SECOND[2])
+        seconds_kernel, [((256, 256), bf16)], [a.T for a in after(seconds, packed)]
+    )
+    block, factor = local(unpack_kernel, [((64, WIDTH), bf16), ((64, 3072), bf16)], got)
+
+    block, factor = after((block, factor), (up2, down2, seconds))
+    factors = [factor] + [send(factor, SECOND[k]) for k in (1, 2, 3)]
     rows1, rows3 = send(block, SECOND[1]), send(block, SECOND[3])
+    (factor,) = local(stack_kernel, [((256, 3072 + 256), bf16)], (*factors, seconds))
+    factor2 = send(factor, CORE)
+    rows2 = send(after(block, factor), SECOND[2])
     frozen = (frozen_gate_weight, frozen_up_weight, frozen_down_weight)
-    frozen = after(frozen, block)
-    up2, down2 = send(frozen[1], CORE), send(frozen[2], CORE)
-    (factor,) = local(
-        stack_kernel,
-        [((256, 3072 + 256), bf16)],
-        (*(factors[k] for k in range(4)), seconds),
-    )
-    factor2 = send(factor, CORE)
-    rows2 = send(after(block, up2), SECOND[2])
-    (touched,) = local(touch_kernel, [((8, 128), f32)], in_vmem(frozen))
-    owned = frozen
+    owned = after(frozen, block)
+    (touched,) = local(touch_kernel, [((8, 128), f32)], in_vmem(owned))
 
     weights = (owned[0], gate2, owned[1], up2)
     down_weights = (owned[2], down2)

time: 129 us -> 134 us (1.039)
  local copies, waits for them, and re-layouts: 0.12 us -> 6.44 us
  starting transfers between devices: 42.4 us -> 40.3 us
    unnamed x12 -> x16, local copies, waits for them, and re-layouts: 0.04 us -> 6.36 us
    ppermute x30 -> x27, starting transfers between devices: 42.4 us -> 40.3 us  [send(): return lax.ppermute(value, AXES, route)]
    ppermute x30 -> x27, waiting for transfers between devices: 63.6 us -> 64.5 us  [send(): return lax.ppermute(value, AXES, route)]
    pallas_call x13 -> x10, Pallas kernels: 3.91 us -> 4.1 us  [local(): pl.pallas_call(body, in_specs=[SMEM] * len(lead) + [VMEM] * len(operands)...]
  transfers between devices with their start and end apart: 30 -> 27, of which waited for: 16 -> 18; matrix products, arithmetic and copies ran while one was open for 0% -> 0% of each run, Pallas kernels for 15% -> 14%
where the time goes in v6:
time: 134 us
  waiting for transfers between devices  64.5 us (48%)
  starting transfers between devices  40.3 us (30%)
  Pallas kernels  21.8 us (16%)
  local copies, waits for them, and re-layouts  6.44 us (5%)
    ppermute x27, waiting for transfers between devices, send(): return lax.ppermute(value, AXES, route)  64.5 us
    ppermute x27, starting transfers between devices, send(): return lax.ppermute(value, AXES, route)  40.3 us
    pallas_call x2, Pallas kernels, down(): pl.pallas_call(body, in_specs=[SMEM] * len(lead) + [VMEM] * len(operands)...  9.6 us
    pallas_call x2, Pallas kernels, project(): pl.pallas_call(lambda *refs: project_kernel(n, *refs[more:]), in_specs=[V...  8.14 us
    unnamed x16, local copies, waits for them, and re-layouts  6.36 us
    pallas_call x10, Pallas kernels, local(): pl.pallas_call(body, in_specs=[SMEM] * len(lead) + [VMEM] * len(operands)...  4.1 us
  transfers between devices with their start and end apart: 27, of which 18 were waited for; matrix products, arithmetic and copies ran while one was open for 0% of the time, Pallas kernels for 14%

profile of v6, /device:TPU:1, one launch (start us, length us, event | category | flops | bytes accessed | tf_op | source)
XLA Modules:
  0.0 133.9 jit_solution(9625628089306387571)
XLA Ops:
  0.1 1.6 %shard_map.100 = (bf16[8,2048]{1,0:T(8,128)(2,1)S(1)}, bf16[8,2048]{1,0:T(8,128)(2,1)S(1)}, bf16[16,1536]{1,0:T(8,128)(2,1)S(1)}) custom-call(s32[5]{0:T(128)S(1)} %stack.23.place.refs_0_, bf16[2,8,2048]{2,1,0:T(8,128)(2,1)} %inputs.1, bf16[64,256]{1,0:T(8,128)(2,1)} %gate.1, bf16[64,256]{1,0:T(8,128)(2,1)} %up.1, bf16[64,256]{1,0:T(8,128)(2,1)} %down.1), custom_call_target="tpu_custom_call" | custom-call | flops 1 | bytes 1 | tf_op jit(solution)/shard_map/pallas_call | solution.py:194
  1.7 1.5 %collective-permute-start = (bf16[8,2048]{1,0:T(8,128)(2,1)S(1)}, bf16[8,2048]{1,0:T(8,128)(2,1)S(1)}, u32[]{:S(2)}, u32[]{:S(2)}) collective-permute-start(bf16[8,2048]{1,0:T(8,128)(2,1)S(1)} %get-tuple-element.40), channel_id=1, source_target_pairs={{0,1},{1,0},{2,3},{3,2},{4,5},{5,4},{6,7},{7,6},{8,9},{9,8},{10,11... | collective-permute-start | bytes 98312 | tf_op jit(solution)/shard_map/ppermute | solution.py:50
  3.2 0.9 collective-permute-done.other
  5.1 3.8 %collective-permute-start.3 = (bf16[16,3584]{1,0:T(8,128)(2,1)S(1)}, bf16[16,3584]{1,0:T(8,128)(2,1)S(1)}, u32[]{:S(2)}, u32[]{:S(2)}) collective-permute-start(bf16[16,3584]{1,0:T(8,128)(2,1)S(1)} %get-tuple-element.43.message), channel_id=1, source_target_pairs={{0,66},{1,67},{2,64},{3,65},{4,70},{5,71},{6,68},{7,69},{8,74},{9,... | collective-permute-start | bytes 344072 | tf_op jit(solution)/shard_map/ppermute | solution.py:50
  8.9 1.2 collective-permute-start.2
  10.1 0.7 collective-permute-start.8
  10.9 1.5 %collective-permute-done.1.z1 = bf16[8,4096]{1,0:T(8,128)(2,1)S(1)} collective-permute-done((bf16[8,4096]{1,0:T(8,128)(2,1)S(1)}, bf16[8,4096]{1,0:T(8,128)(2,1)S(1)}, u32[]{:S(2)}, u32[]{:S(2)}) %collective-permute-start.1) | collective-permute-done | bytes 65568 | tf_op jit(solution)/shard_map/ppermute | solution.py:50
  12.3 1.2 collective-permute-done.2.z2
  13.6 0.6 shard_map.102.refs_0_
  14.1 1.7 %collective-permute-start.9 = (bf16[224,8192]{1,0:T(8,128)(2,1)}, bf16[224,8192]{1,0:T(8,128)(2,1)S(1)}, u32[]{:S(2)}, u32[]{:S(2)}) collective-permute-start(bf16[224,8192]{1,0:T(8,128)(2,1)} %refs_2_), channel_id=1, source_target_pairs={{0,1},{1,0},{2,3},{3,2},{4,5},{5,4},{6,7},{7,6},{8,9},{9,8},{10,11... | collective-permute-start | bytes 11010056 | tf_op jit(solution)/shard_map/ppermute | solution.py:50
  15.8 1.3 collective-permute-start.5
  17.1 2.6 %collective-permute-start.6 = (bf16[16,11264]{1,0:T(8,128)(2,1)S(1)}, bf16[16,11264]{1,0:T(8,128)(2,1)S(1)}, u32[]{:S(2)}, u32[]{:S(2)}) collective-permute-start(bf16[16,11264]{1,0:T(8,128)(2,1)S(1)} %shard_map.102.refs_0_), channel_id=1, source_target_pairs={{0,8},{1,33},{2,10},{3,35},{4,12},{5,37},{6,14},{7,39},{8,0},{9,41... | collective-permute-start | bytes 1081352 | tf_op jit(solution)/shard_map/ppermute | solution.py:50
  19.7 0.8 copy-done.5
  20.5 0.8 copy-done.6
  21.3 0.8 copy-done.7
  22.4 6.4 %collective-permute-done.6.refs_2_ = bf16[16,11264]{1,0:T(8,128)(2,1)S(1)} collective-permute-done((bf16[16,11264]{1,0:T(8,128)(2,1)S(1)}, bf16[16,11264]{1,0:T(8,128)(2,1)S(1)}, u32[]{:S(2)}, u32[]{:S(2)}) %collective-permute-start.6) | collective-permute-done | bytes 360480 | tf_op jit(solution)/shard_map/ppermute | solution.py:50
  28.7 2.6 %collective-permute-done.7.refs_3_ = bf16[16,11264]{1,0:T(8,128)(2,1)S(1)} collective-permute-done((bf16[16,11264]{1,0:T(8,128)(2,1)S(1)}, bf16[16,11264]{1,0:T(8,128)(2,1)S(1)}, u32[]{:S(2)}, u32[]{:S(2)}) %collective-permute-start.7) | collective-permute-done | bytes 360480 | tf_op jit(solution)/shard_map/ppermute | solution.py:50
  31.5 1.0 collective-permute-start.12
  32.5 2.5 %collective-permute-start.13 = (bf16[64,3072]{1,0:T(8,128)(2,1)S(1)}, bf16[64,3072]{1,0:T(8,128)(2,1)S(1)}, u32[]{:S(2)}, u32[]{:S(2)}) collective-permute-start(bf16[64,3072]{1,0:T(8,128)(2,1)S(1)} %get-tuple-element.57.f0), channel_id=1, source_target_pairs={{0,32},{1,9},{2,34},{3,11},{4,36},{5,13},{6,38},{7,15},{8,40},{9,1... | collective-permute-start | bytes 1179656 | tf_op jit(solution)/shard_map/ppermute | solution.py:50
  35.4 2.2 %collective-permute-start.11 = (bf16[64,8192]{1,0:T(8,128)(2,1)S(1)}, bf16[64,8192]{1,0:T(8,128)(2,1)S(1)}, u32[]{:S(2)}, u32[]{:S(2)}) collective-permute-start(bf16[64,8192]{1,0:T(8,128)(2,1)S(1)} %get-tuple-element.61.refs_1_), channel_id=1, source_target_pairs={{0,48},{1,13},{2,50},{3,15},{4,52},{5,9},{6,54},{7,11},{8,56},{9,5... | collective-permute-start | bytes 3145736 | tf_op jit(solution)/shard_map/ppermute | solution.py:50
  37.6 0.9 collective-permute-done.12.f1
  38.5 6.2 %collective-permute-done.13.f2 = bf16[64,3072]{1,0:T(8,128)(2,1)S(1)} collective-permute-done((bf16[64,3072]{1,0:T(8,128)(2,1)S(1)}, bf16[64,3072]{1,0:T(8,128)(2,1)S(1)}, u32[]{:S(2)}, u32[]{:S(2)}) %collective-permute-start.13) | collective-permute-done | bytes 393248 | tf_op jit(solution)/shard_map/ppermute | solution.py:50
  44.7 2.6 %collective-permute-done.14.f3 = bf16[64,3072]{1,0:T(8,128)(2,1)S(1)} collective-permute-done((bf16[64,3072]{1,0:T(8,128)(2,1)S(1)}, bf16[64,3072]{1,0:T(8,128)(2,1)S(1)}, u32[]{:S(2)}, u32[]{:S(2)}) %collective-permute-start.14) | collective-permute-done | bytes 393248 | tf_op jit(solution)/shard_map/ppermute | solution.py:50
  47.4 3.3 %collective-permute-start.15 = (bf16[256,3328]{1,0:T(8,128)(2,1)S(1)}, bf16[256,3328]{1,0:T(8,128)(2,1)S(1)}, u32[]{:S(2)}, u32[]{:S(2)}) collective-permute-start(bf16[256,3328]{1,0:T(8,128)(2,1)S(1)} %shard_map.107.refs_9_), channel_id=1, source_target_pairs={{0,1},{1,0},{2,3},{3,2},{4,5},{5,4},{6,7},{7,6},{8,9},{9,8},{10,11... | collective-permute-start | bytes 5111816 | tf_op jit(solution)/shard_map/ppermute | solution.py:50
  50.7 2.0 %copy-done.1 = bf16[224,8192]{1,0:T(8,128)(2,1)S(1)} copy-done((bf16[224,8192]{1,0:T(8,128)(2,1)S(1)}, bf16[224,8192]{1,0:T(8,128)(2,1)}, u32[]{:S(2)}) %copy-start.1) | copy-done | bytes 3670040
  52.8 2.0 %copy-done.3 = bf16[224,8192]{1,0:T(8,128)(2,1)S(1)} copy-done((bf16[224,8192]{1,0:T(8,128)(2,1)S(1)}, bf16[224,8192]{1,0:T(8,128)(2,1)}, u32[]{:S(2)}) %copy-start.3) | copy-done | bytes 3670040
  54.8 15.0 %collective-permute-done.11.refs_3_ = bf16[64,8192]{1,0:T(8,128)(2,1)S(1)} collective-permute-done((bf16[64,8192]{1,0:T(8,128)(2,1)S(1)}, bf16[64,8192]{1,0:T(8,128)(2,1)S(1)}, u32[]{:S(2)}, u32[]{:S(2)}) %collective-permute-start.11) | collective-permute-done | bytes 1048608 | tf_op jit(solution)/shard_map/ppermute | solution.py:50
  69.8 4.1 %shard_map.106.refs_4_ = f32[896,192]{1,0:T(8,128)S(1)} custom-call(f32[8,128]{1,0:T(8,128)S(1)} %shard_map.105.refs_0_, bf16[64,8192]{1,0:T(8,128)(2,1)S(1)} %get-tuple-element.61.refs_1_, bf16[64,8192]{1,0:T(8,128)(2,1)S(1)} %collective-permute-done.10.refs_2_, bf16[64,8192]{1,0:T(8,128)(2,1)S(1)} %collective-permute-done.11.refs_3_, ...), custom_call_target="tpu_custom_call" | custom-call | flops 9200000000 | bytes 28800000 | tf_op jit(solution)/shard_map/pallas_call | solution.py:160
  73.9 6.0 %shard_map.108 = (f32[64,8192]{1,0:T(8,128)S(1)}, bf16[64,8192]{1,0:T(8,128)(2,1)S(1)}, bf16[64,8192]{1,0:T(8,128)(2,1)S(1)}, bf16[128,8192]{1,0:T(8,128)(2,1)S(1)}, bf16[64,8192]{1,0:T(8,128)(2,1)S(1)}) custom-call(s32[5]{0:T(128)S(1)} %stack.23.place.refs_0_, bf16[64,8192]{1,0:T(8,128)(2,1)S(1)} %get-tuple-element.61.refs_1_, ...), custom_call_target="tpu_custom_call" | custom-call | flops 1 | bytes 1 | tf_op jit(solution)/shard_map/pallas_call | solution.py:181
  80.0 0.8 collective-permute-start.17
  80.8 4.1 %shard_map.110.refs_1_ = f32[896,64]{1,0:T(8,128)S(1)} custom-call(bf16[64,8192]{1,0:T(8,128)(2,1)S(1)} %collective-permute-done.18.refs_0_, bf16[224,8192]{1,0:T(8,128)(2,1)S(1)} %copy-done.2, bf16[224,8192]{1,0:T(8,128)(2,1)S(1)} %collective-permute-done.4.refs_5_.refs_2_, bf16[224,8192]{1,0:T(8,128)(2,1)S(1)} %copy-done.4, ...), custom_call_target="tpu_custom_call" | custom-call | flops 9200000000 | bytes 28800000 | tf_op jit(solution)/shard_map/pallas_call | solution.py:160
  84.9 3.6 %shard_map.111 = bf16[64,8192]{1,0:T(8,128)(2,1)S(1)} custom-call(bf16[64,8192]{1,0:T(8,128)(2,1)S(1)} %collective-permute-done.18.refs_0_, f32[896,64]{1,0:T(8,128)S(1)} %shard_map.110.refs_1_, bf16[224,8192]{1,0:T(8,128)(2,1)S(1)} %copy-done, bf16[224,8192]{1,0:T(8,128)(2,1)S(1)} %collective-permute-done.9.refs_6_.refs_3_, ...), custom_call_target="tpu_custom_call" | custom-call | flops 1 | bytes 1 | tf_op jit(solution)/shard_map/pallas_call | solution.py:181
  88.4 2.5 %collective-permute-start.19 = (bf16[64,8192]{1,0:T(8,128)(2,1)S(1)}, bf16[64,8192]{1,0:T(8,128)(2,1)S(1)}, u32[]{:S(2)}, u32[]{:S(2)}) collective-permute-start(bf16[64,8192]{1,0:T(8,128)(2,1)S(1)} %shard_map.111), channel_id=1, source_target_pairs={{0,32},{1,9},{2,34},{3,11},{4,36},{5,13},{6,38},{7,15},{8,40},{9,1... | collective-permute-start | bytes 3145736 | tf_op jit(solution)/shard_map/ppermute | solution.py:50
  90.9 3.0 %collective-permute-done.16.b1 = bf16[64,8192]{1,0:T(8,128)(2,1)S(1)} collective-permute-done((bf16[64,8192]{1,0:T(8,128)(2,1)S(1)}, bf16[64,8192]{1,0:T(8,128)(2,1)S(1)}, u32[]{:S(2)}, u32[]{:S(2)}) %collective-permute-start.16) | collective-permute-done | bytes 1048608 | tf_op jit(solution)/shard_map/ppermute | solution.py:50
  93.9 12.8 %collective-permute-done.17.b3 = bf16[64,8192]{1,0:T(8,128)(2,1)S(1)} collective-permute-done((bf16[64,8192]{1,0:T(8,128)(2,1)S(1)}, bf16[64,8192]{1,0:T(8,128)(2,1)S(1)}, u32[]{:S(2)}, u32[]{:S(2)}) %collective-permute-start.17) | collective-permute-done | bytes 1048608 | tf_op jit(solution)/shard_map/ppermute | solution.py:50
  107.2 1.5 %collective-permute-start.21 = (bf16[16,8192]{1,0:T(8,128)(2,1)S(1)}, bf16[16,8192]{1,0:T(8,128)(2,1)S(1)}, u32[]{:S(2)}, u32[]{:S(2)}) collective-permute-start(bf16[16,8192]{1,0:T(8,128)(2,1)S(1)} %get-tuple-element.67), channel_id=1, source_target_pairs={{0,8},{1,33},{2,10},{3,35},{4,12},{5,37},{6,14},{7,39},{8,0},{9,41... | collective-permute-start | bytes 786440 | tf_op jit(solution)/shard_map/ppermute | solution.py:50
  108.7 2.4 %collective-permute-start.22 = (bf16[16,8192]{1,0:T(8,128)(2,1)S(1)}, bf16[16,8192]{1,0:T(8,128)(2,1)S(1)}, u32[]{:S(2)}, u32[]{:S(2)}) collective-permute-start(bf16[16,8192]{1,0:T(8,128)(2,1)S(1)} %get-tuple-element.68), channel_id=1, source_target_pairs={{0,12},{1,49},{2,14},{3,51},{4,8},{5,53},{6,10},{7,55},{8,4},{9,57... | collective-permute-start | bytes 786440 | tf_op jit(solution)/shard_map/ppermute | solution.py:50
  111.1 1.4 %collective-permute-done.20.b1 = bf16[16,8192]{1,0:T(8,128)(2,1)S(1)} collective-permute-done((bf16[16,8192]{1,0:T(8,128)(2,1)S(1)}, bf16[16,8192]{1,0:T(8,128)(2,1)S(1)}, u32[]{:S(2)}, u32[]{:S(2)}) %collective-permute-start.20) | collective-permute-done | bytes 262176 | tf_op jit(solution)/shard_map/ppermute | solution.py:50
  112.4 2.9 %collective-permute-done.21.b2 = bf16[16,8192]{1,0:T(8,128)(2,1)S(1)} collective-permute-done((bf16[16,8192]{1,0:T(8,128)(2,1)S(1)}, bf16[16,8192]{1,0:T(8,128)(2,1)S(1)}, u32[]{:S(2)}, u32[]{:S(2)}) %collective-permute-start.21) | collective-permute-done | bytes 262176 | tf_op jit(solution)/shard_map/ppermute | solution.py:50
  115.4 2.9 %collective-permute-done.22.b3 = bf16[16,8192]{1,0:T(8,128)(2,1)S(1)} collective-permute-done((bf16[16,8192]{1,0:T(8,128)(2,1)S(1)}, bf16[16,8192]{1,0:T(8,128)(2,1)S(1)}, u32[]{:S(2)}, u32[]{:S(2)}) %collective-permute-start.22) | collective-permute-done | bytes 262176 | tf_op jit(solution)/shard_map/ppermute | solution.py:50
  118.2 0.7 shard_map.113
  118.9 2.2 %collective-permute-start.25 = (bf16[8,4096]{1,0:T(8,128)(2,1)S(1)}, bf16[8,4096]{1,0:T(8,128)(2,1)S(1)}, u32[]{:S(2)}, u32[]{:S(2)}) collective-permute-start(bf16[8,4096]{1,0:T(8,128)(2,1)S(1)} %get-tuple-element.72), channel_id=1, source_target_pairs={{0,66},{1,67},{2,64},{3,65},{4,70},{5,71},{6,68},{7,69},{8,74},{9,... | collective-permute-start | bytes 196616 | tf_op jit(solution)/shard_map/ppermute | solution.py:50
  121.1 1.4 %collective-permute-start.24 = (bf16[8,4096]{1,0:T(8,128)(2,1)S(1)}, bf16[8,4096]{1,0:T(8,128)(2,1)S(1)}, u32[]{:S(2)}, u32[]{:S(2)}) collective-permute-start(bf16[8,4096]{1,0:T(8,128)(2,1)S(1)} %get-tuple-element.71), channel_id=1, source_target_pairs={{0,64},{1,65},{2,66},{3,67},{4,68},{5,69},{6,70},{7,71},{8,72},{9,... | collective-permute-start | bytes 196616 | tf_op jit(solution)/shard_map/ppermute | solution.py:50
  122.5 0.8 collective-permute-done.25
  123.3 2.4 %collective-permute-done.24 = bf16[8,4096]{1,0:T(8,128)(2,1)S(1)} collective-permute-done((bf16[8,4096]{1,0:T(8,128)(2,1)S(1)}, bf16[8,4096]{1,0:T(8,128)(2,1)S(1)}, u32[]{:S(2)}, u32[]{:S(2)}) %collective-permute-start.24) | collective-permute-done | bytes 65568 | tf_op jit(solution)/shard_map/ppermute | solution.py:50
  125.8 6.7 %collective-permute-start.26 = (bf16[8,2048]{1,0:T(8,128)(2,1)S(1)}, bf16[8,2048]{1,0:T(8,128)(2,1)S(1)}, u32[]{:S(2)}, u32[]{:S(2)}) collective-permute-start(bf16[8,2048]{1,0:T(8,128)(2,1)S(1)} %get-tuple-element.74), channel_id=1, source_target_pairs={{0,1},{1,0},{2,3},{3,2},{4,5},{5,4},{6,7},{7,6},{8,9},{9,8},{10,11... | collective-permute-start | bytes 98312 | tf_op jit(solution)/shard_map/ppermute | solution.py:50
  132.4 0.9 collective-permute-done.26
  133.3 0.6 maximum_select_fusion
  (40 shorter events, 2.9 us)
Async XLA Ops:
  0.1 50.6 %copy-start = (bf16[224,8192]{1,0:T(8,128)(2,1)S(1)}, bf16[224,8192]{1,0:T(8,128)(2,1)}, u32[]{:S(2)}) copy-start(bf16[224,8192]{1,0:T(8,128)(2,1)} %refs_2_) | copy-start | bytes 11010052
  1.7 2.4 %collective-permute-start = (bf16[8,2048]{1,0:T(8,128)(2,1)S(1)}, bf16[8,2048]{1,0:T(8,128)(2,1)S(1)}, u32[]{:S(2)}, u32[]{:S(2)}) collective-permute-start(bf16[8,2048]{1,0:T(8,128)(2,1)S(1)} %get-tuple-element.40), channel_id=1, source_target_pairs={{0,1},{1,0},{2,3},{3,2},{4,5},{5,4},{6,7},{7,6},{8,9},{9,8},{10,11... | collective-permute-start | bytes 98312 | tf_op jit(solution)/shard_map/ppermute | solution.py:50
  4.7 9.5 %collective-permute-start.4 = (bf16[224,8192]{1,0:T(8,128)(2,1)}, bf16[224,8192]{1,0:T(8,128)(2,1)S(1)}, u32[]{:S(2)}, u32[]{:S(2)}) collective-permute-start(bf16[224,8192]{1,0:T(8,128)(2,1)} %refs_1_), channel_id=1, source_target_pairs={{0,1},{1,0},{2,3},{3,2},{4,5},{5,4},{6,7},{7,6},{8,9},{9,8},{10,11... | collective-permute-start | bytes 11010056 | tf_op jit(solution)/shard_map/ppermute | solution.py:50
  5.1 8.5 %collective-permute-start.3 = (bf16[16,3584]{1,0:T(8,128)(2,1)S(1)}, bf16[16,3584]{1,0:T(8,128)(2,1)S(1)}, u32[]{:S(2)}, u32[]{:S(2)}) collective-permute-start(bf16[16,3584]{1,0:T(8,128)(2,1)S(1)} %get-tuple-element.43.message), channel_id=1, source_target_pairs={{0,66},{1,67},{2,64},{3,65},{4,70},{5,71},{6,68},{7,69},{8,74},{9,... | collective-permute-start | bytes 344072 | tf_op jit(solution)/shard_map/ppermute | solution.py:50
  8.9 3.4 %collective-permute-start.1 = (bf16[8,4096]{1,0:T(8,128)(2,1)S(1)}, bf16[8,4096]{1,0:T(8,128)(2,1)S(1)}, u32[]{:S(2)}, u32[]{:S(2)}) collective-permute-start(bf16[8,4096]{1,0:T(8,128)(2,1)S(1)} %get-tuple-element.42.wide), channel_id=1, source_target_pairs={{0,2},{1,3},{2,0},{3,1},{4,6},{5,7},{6,4},{7,5},{8,10},{9,11},{10,... | collective-permute-start | bytes 196616 | tf_op jit(solution)/shard_map/ppermute | solution.py:50
  8.9 4.6 %collective-permute-start.2 = (bf16[8,4096]{1,0:T(8,128)(2,1)S(1)}, bf16[8,4096]{1,0:T(8,128)(2,1)S(1)}, u32[]{:S(2)}, u32[]{:S(2)}) collective-permute-start(bf16[8,4096]{1,0:T(8,128)(2,1)S(1)} %get-tuple-element.42.wide), channel_id=1, source_target_pairs={{0,64},{1,65},{2,66},{3,67},{4,68},{5,69},{6,70},{7,71},{8,72},{9,... | collective-permute-start | bytes 196616 | tf_op jit(solution)/shard_map/ppermute | solution.py:50
  10.1 21.4 %collective-permute-start.8 = (bf16[224,8192]{1,0:T(8,128)(2,1)}, bf16[224,8192]{1,0:T(8,128)(2,1)S(1)}, u32[]{:S(2)}, u32[]{:S(2)}) collective-permute-start(bf16[224,8192]{1,0:T(8,128)(2,1)} %refs_3_), channel_id=1, source_target_pairs={{0,1},{1,0},{2,3},{3,2},{4,5},{5,4},{6,7},{7,6},{8,9},{9,8},{10,11... | collective-permute-start | bytes 11010056 | tf_op jit(solution)/shard_map/ppermute | solution.py:50
  14.1 17.3 %collective-permute-start.9 = (bf16[224,8192]{1,0:T(8,128)(2,1)}, bf16[224,8192]{1,0:T(8,128)(2,1)S(1)}, u32[]{:S(2)}, u32[]{:S(2)}) collective-permute-start(bf16[224,8192]{1,0:T(8,128)(2,1)} %refs_2_), channel_id=1, source_target_pairs={{0,1},{1,0},{2,3},{3,2},{4,5},{5,4},{6,7},{7,6},{8,9},{9,8},{10,11... | collective-permute-start | bytes 11010056 | tf_op jit(solution)/shard_map/ppermute | solution.py:50
  15.8 6.6 %collective-permute-start.5 = (bf16[16,11264]{1,0:T(8,128)(2,1)S(1)}, bf16[16,11264]{1,0:T(8,128)(2,1)S(1)}, u32[]{:S(2)}, u32[]{:S(2)}) collective-permute-start(bf16[16,11264]{1,0:T(8,128)(2,1)S(1)} %shard_map.102.refs_0_), channel_id=1, source_target_pairs={{0,4},{1,17},{2,6},{3,19},{4,0},{5,21},{6,2},{7,23},{8,12},{9,25},... | collective-permute-start | bytes 1081352 | tf_op jit(solution)/shard_map/ppermute | solution.py:50
  17.1 11.6 %collective-permute-start.6 = (bf16[16,11264]{1,0:T(8,128)(2,1)S(1)}, bf16[16,11264]{1,0:T(8,128)(2,1)S(1)}, u32[]{:S(2)}, u32[]{:S(2)}) collective-permute-start(bf16[16,11264]{1,0:T(8,128)(2,1)S(1)} %shard_map.102.refs_0_), channel_id=1, source_target_pairs={{0,8},{1,33},{2,10},{3,35},{4,12},{5,37},{6,14},{7,39},{8,0},{9,41... | collective-permute-start | bytes 1081352 | tf_op jit(solution)/shard_map/ppermute | solution.py:50
  19.7 11.6 %collective-permute-start.7 = (bf16[16,11264]{1,0:T(8,128)(2,1)S(1)}, bf16[16,11264]{1,0:T(8,128)(2,1)S(1)}, u32[]{:S(2)}, u32[]{:S(2)}) collective-permute-start(bf16[16,11264]{1,0:T(8,128)(2,1)S(1)} %shard_map.102.refs_0_), channel_id=1, source_target_pairs={{0,12},{1,49},{2,14},{3,51},{4,8},{5,53},{6,10},{7,55},{8,4},{9,57... | collective-permute-start | bytes 1081352 | tf_op jit(solution)/shard_map/ppermute | solution.py:50
  19.7 0.8 copy-start.5
  20.5 0.8 copy-start.6
  21.3 0.8 copy-start.7
  31.5 7.0 %collective-permute-start.12 = (bf16[64,3072]{1,0:T(8,128)(2,1)S(1)}, bf16[64,3072]{1,0:T(8,128)(2,1)S(1)}, u32[]{:S(2)}, u32[]{:S(2)}) collective-permute-start(bf16[64,3072]{1,0:T(8,128)(2,1)S(1)} %get-tuple-element.57.f0), channel_id=1, source_target_pairs={{0,16},{1,5},{2,18},{3,7},{4,20},{5,1},{6,22},{7,3},{8,24},{9,13},... | collective-permute-start | bytes 1179656 | tf_op jit(solution)/shard_map/ppermute | solution.py:50
  32.5 12.2 %collective-permute-start.13 = (bf16[64,3072]{1,0:T(8,128)(2,1)S(1)}, bf16[64,3072]{1,0:T(8,128)(2,1)S(1)}, u32[]{:S(2)}, u32[]{:S(2)}) collective-permute-start(bf16[64,3072]{1,0:T(8,128)(2,1)S(1)} %get-tuple-element.57.f0), channel_id=1, source_target_pairs={{0,32},{1,9},{2,34},{3,11},{4,36},{5,13},{6,38},{7,15},{8,40},{9,1... | collective-permute-start | bytes 1179656 | tf_op jit(solution)/shard_map/ppermute | solution.py:50
  34.9 12.3 %collective-permute-start.14 = (bf16[64,3072]{1,0:T(8,128)(2,1)S(1)}, bf16[64,3072]{1,0:T(8,128)(2,1)S(1)}, u32[]{:S(2)}, u32[]{:S(2)}) collective-permute-start(bf16[64,3072]{1,0:T(8,128)(2,1)S(1)} %get-tuple-element.57.f0), channel_id=1, source_target_pairs={{0,48},{1,13},{2,50},{3,15},{4,52},{5,9},{6,54},{7,11},{8,56},{9,5... | collective-permute-start | bytes 1179656 | tf_op jit(solution)/shard_map/ppermute | solution.py:50
  35.4 19.4 %collective-permute-start.10 = (bf16[64,8192]{1,0:T(8,128)(2,1)S(1)}, bf16[64,8192]{1,0:T(8,128)(2,1)S(1)}, u32[]{:S(2)}, u32[]{:S(2)}) collective-permute-start(bf16[64,8192]{1,0:T(8,128)(2,1)S(1)} %get-tuple-element.61.refs_1_), channel_id=1, source_target_pairs={{0,16},{1,5},{2,18},{3,7},{4,20},{5,1},{6,22},{7,3},{8,24},{9,13},... | collective-permute-start | bytes 3145736 | tf_op jit(solution)/shard_map/ppermute | solution.py:50
  35.4 34.3 %collective-permute-start.11 = (bf16[64,8192]{1,0:T(8,128)(2,1)S(1)}, bf16[64,8192]{1,0:T(8,128)(2,1)S(1)}, u32[]{:S(2)}, u32[]{:S(2)}) collective-permute-start(bf16[64,8192]{1,0:T(8,128)(2,1)S(1)} %get-tuple-element.61.refs_1_), channel_id=1, source_target_pairs={{0,48},{1,13},{2,50},{3,15},{4,52},{5,9},{6,54},{7,11},{8,56},{9,5... | collective-permute-start | bytes 3145736 | tf_op jit(solution)/shard_map/ppermute | solution.py:50
  47.4 26.4 %collective-permute-start.15 = (bf16[256,3328]{1,0:T(8,128)(2,1)S(1)}, bf16[256,3328]{1,0:T(8,128)(2,1)S(1)}, u32[]{:S(2)}, u32[]{:S(2)}) collective-permute-start(bf16[256,3328]{1,0:T(8,128)(2,1)S(1)} %shard_map.107.refs_9_), channel_id=1, source_target_pairs={{0,1},{1,0},{2,3},{3,2},{4,5},{5,4},{6,7},{7,6},{8,9},{9,8},{10,11... | collective-permute-start | bytes 5111816 | tf_op jit(solution)/shard_map/ppermute | solution.py:50
  50.7 30.1 %collective-permute-start.18 = (bf16[64,8192]{1,0:T(8,128)(2,1)S(1)}, bf16[64,8192]{1,0:T(8,128)(2,1)S(1)}, u32[]{:S(2)}, u32[]{:S(2)}) collective-permute-start(bf16[64,8192]{1,0:T(8,128)(2,1)S(1)} %get-tuple-element.61.refs_1_), channel_id=1, source_target_pairs={{0,32},{1,9},{2,34},{3,11},{4,36},{5,13},{6,38},{7,15},{8,40},{9,1... | collective-permute-start | bytes 3145736 | tf_op jit(solution)/shard_map/ppermute | solution.py:50
  50.7 2.0 %copy-start.1 = (bf16[224,8192]{1,0:T(8,128)(2,1)S(1)}, bf16[224,8192]{1,0:T(8,128)(2,1)}, u32[]{:S(2)}) copy-start(bf16[224,8192]{1,0:T(8,128)(2,1)} %refs_1_) | copy-start | bytes 11010052
  52.8 2.0 %copy-start.3 = (bf16[224,8192]{1,0:T(8,128)(2,1)S(1)}, bf16[224,8192]{1,0:T(8,128)(2,1)}, u32[]{:S(2)}) copy-start(bf16[224,8192]{1,0:T(8,128)(2,1)} %refs_3_) | copy-start | bytes 11010052
  54.8 15.0 %copy-start.2 = (bf16[224,8192]{1,0:T(8,128)(2,1)S(1)}, bf16[224,8192]{1,0:T(8,128)(2,1)}, u32[]{:S(2)}) copy-start(bf16[224,8192]{1,0:T(8,128)(2,1)} %refs_1_) | copy-start | bytes 11010052
  54.8 15.0 %copy-start.4 = (bf16[224,8192]{1,0:T(8,128)(2,1)S(1)}, bf16[224,8192]{1,0:T(8,128)(2,1)}, u32[]{:S(2)}) copy-start(bf16[224,8192]{1,0:T(8,128)(2,1)} %refs_3_) | copy-start | bytes 11010052
  79.9 14.0 %collective-permute-start.16 = (bf16[64,8192]{1,0:T(8,128)(2,1)S(1)}, bf16[64,8192]{1,0:T(8,128)(2,1)S(1)}, u32[]{:S(2)}, u32[]{:S(2)}) collective-permute-start(bf16[64,8192]{1,0:T(8,128)(2,1)S(1)} %get-tuple-element.59), channel_id=1, source_target_pairs={{0,16},{1,5},{2,18},{3,7},{4,20},{5,1},{6,22},{7,3},{8,24},{9,13},... | collective-permute-start | bytes 3145736 | tf_op jit(solution)/shard_map/ppermute | solution.py:50
  80.0 26.7 %collective-permute-start.17 = (bf16[64,8192]{1,0:T(8,128)(2,1)S(1)}, bf16[64,8192]{1,0:T(8,128)(2,1)S(1)}, u32[]{:S(2)}, u32[]{:S(2)}) collective-permute-start(bf16[64,8192]{1,0:T(8,128)(2,1)S(1)} %get-tuple-element.60), channel_id=1, source_target_pairs={{0,48},{1,13},{2,50},{3,15},{4,52},{5,9},{6,54},{7,11},{8,56},{9,5... | collective-permute-start | bytes 3145736 | tf_op jit(solution)/shard_map/ppermute | solution.py:50
  88.4 18.5 %collective-permute-start.19 = (bf16[64,8192]{1,0:T(8,128)(2,1)S(1)}, bf16[64,8192]{1,0:T(8,128)(2,1)S(1)}, u32[]{:S(2)}, u32[]{:S(2)}) collective-permute-start(bf16[64,8192]{1,0:T(8,128)(2,1)S(1)} %shard_map.111), channel_id=1, source_target_pairs={{0,32},{1,9},{2,34},{3,11},{4,36},{5,13},{6,38},{7,15},{8,40},{9,1... | collective-permute-start | bytes 3145736 | tf_op jit(solution)/shard_map/ppermute | solution.py:50
  107.1 5.3 %collective-permute-start.20 = (bf16[16,8192]{1,0:T(8,128)(2,1)S(1)}, bf16[16,8192]{1,0:T(8,128)(2,1)S(1)}, u32[]{:S(2)}, u32[]{:S(2)}) collective-permute-start(bf16[16,8192]{1,0:T(8,128)(2,1)S(1)} %get-tuple-element.66), channel_id=1, source_target_pairs={{0,4},{1,17},{2,6},{3,19},{4,0},{5,21},{6,2},{7,23},{8,12},{9,25},... | collective-permute-start | bytes 786440 | tf_op jit(solution)/shard_map/ppermute | solution.py:50
  107.2 8.1 %collective-permute-start.21 = (bf16[16,8192]{1,0:T(8,128)(2,1)S(1)}, bf16[16,8192]{1,0:T(8,128)(2,1)S(1)}, u32[]{:S(2)}, u32[]{:S(2)}) collective-permute-start(bf16[16,8192]{1,0:T(8,128)(2,1)S(1)} %get-tuple-element.67), channel_id=1, source_target_pairs={{0,8},{1,33},{2,10},{3,35},{4,12},{5,37},{6,14},{7,39},{8,0},{9,41... | collective-permute-start | bytes 786440 | tf_op jit(solution)/shard_map/ppermute | solution.py:50
  108.7 9.5 %collective-permute-start.22 = (bf16[16,8192]{1,0:T(8,128)(2,1)S(1)}, bf16[16,8192]{1,0:T(8,128)(2,1)S(1)}, u32[]{:S(2)}, u32[]{:S(2)}) collective-permute-start(bf16[16,8192]{1,0:T(8,128)(2,1)S(1)} %get-tuple-element.68), channel_id=1, source_target_pairs={{0,12},{1,49},{2,14},{3,51},{4,8},{5,53},{6,10},{7,55},{8,4},{9,57... | collective-permute-start | bytes 786440 | tf_op jit(solution)/shard_map/ppermute | solution.py:50
  118.9 4.4 %collective-permute-start.25 = (bf16[8,4096]{1,0:T(8,128)(2,1)S(1)}, bf16[8,4096]{1,0:T(8,128)(2,1)S(1)}, u32[]{:S(2)}, u32[]{:S(2)}) collective-permute-start(bf16[8,4096]{1,0:T(8,128)(2,1)S(1)} %get-tuple-element.72), channel_id=1, source_target_pairs={{0,66},{1,67},{2,64},{3,65},{4,70},{5,71},{6,68},{7,69},{8,74},{9,... | collective-permute-start | bytes 196616 | tf_op jit(solution)/shard_map/ppermute | solution.py:50
  121.1 4.6 %collective-permute-start.24 = (bf16[8,4096]{1,0:T(8,128)(2,1)S(1)}, bf16[8,4096]{1,0:T(8,128)(2,1)S(1)}, u32[]{:S(2)}, u32[]{:S(2)}) collective-permute-start(bf16[8,4096]{1,0:T(8,128)(2,1)S(1)} %get-tuple-element.71), channel_id=1, source_target_pairs={{0,64},{1,65},{2,66},{3,67},{4,68},{5,69},{6,70},{7,71},{8,72},{9,... | collective-permute-start | bytes 196616 | tf_op jit(solution)/shard_map/ppermute | solution.py:50
  122.5 3.2 %collective-permute-start.23 = (bf16[8,4096]{1,0:T(8,128)(2,1)S(1)}, bf16[8,4096]{1,0:T(8,128)(2,1)S(1)}, u32[]{:S(2)}, u32[]{:S(2)}) collective-permute-start(bf16[8,4096]{1,0:T(8,128)(2,1)S(1)} %get-tuple-element.70), channel_id=1, source_target_pairs={{0,2},{1,3},{2,0},{3,1},{4,6},{5,7},{6,4},{7,5},{8,10},{9,11},{10,... | collective-permute-start | bytes 196616 | tf_op jit(solution)/shard_map/ppermute | solution.py:50
  125.8 7.5 %collective-permute-start.26 = (bf16[8,2048]{1,0:T(8,128)(2,1)S(1)}, bf16[8,2048]{1,0:T(8,128)(2,1)S(1)}, u32[]{:S(2)}, u32[]{:S(2)}) collective-permute-start(bf16[8,2048]{1,0:T(8,128)(2,1)S(1)} %get-tuple-element.74), channel_id=1, source_target_pairs={{0,1},{1,0},{2,3},{3,2},{4,5},{5,4},{6,7},{7,6},{8,9},{9,8},{10,11... | collective-permute-start | bytes 98312 | tf_op jit(solution)/shard_map/ppermute | solution.py:50

commit v7 on v6

--- a/solution.py
+++ b/solution.py
@@ -50,6 +50,11 @@
     return lax.ppermute(value, AXES, route)
 
 
+def spread(value, routes):
+    got = {k: send(value, routes[k]) for k in (2, 1, 3)}
+    return [value, got[1], got[2], got[3]]
+
+
 def nt(a, b):
     return lax.dot_general(a, b, (((1,), (1,)), ((), ())), preferred_element_type=f32)
 
@@ -82,15 +87,15 @@
             out[...] += nt(w, x)
 
 
-def down_kernel(n, place, *refs):
+def down_kernel(n, n_out, place, *refs):
     rows = refs[:n]
     acc, down_w, down_w2, seconds, theirs = refs[n : n + 5]
     if place is None:
         first, second = refs[n + 5 : n + 7]
     else:
         sources = refs[n + 5 : n + 7]
-        first, second = refs[2 * n + 7 : 2 * n + 9]
-    outs = refs[n + 7 : 2 * n + 7]
+        first, second = refs[n + 7 + n_out : n + 9 + n_out]
+    outs = refs[n + 7 : n + 7 + n_out]
     hidden = refs[-1]
 
     def shards_of(learner, to, groups, base):
@@ -161,7 +166,7 @@
         lambda *refs: project_kernel(n, *refs[more:]),
         in_specs=[VMEM] * (more + n + 4),
         out_specs=VMEM,
-        out_shape=jax.ShapeDtypeStruct((4 * UNITS, 64 * n), f32),
+        out_shape=jax.ShapeDtypeStruct((4 * UNITS, sum(r.shape[0] for r in rows)), f32),
         compiler_params=pltpu.CompilerParams(vmem_limit_bytes=10 * 1024 * 1024),
         cost_estimate=price_of(CK),
     )(*extra, *in_vmem([*rows, *weights]))
@@ -173,17 +178,18 @@
     operands = in_vmem([*rows, acc, *weights, seconds[0], theirs, *factors])
     shapes = [((64, WIDTH), kind) for kind in kinds]
     lead = []
-    body = lambda *refs: down_kernel(n, None, *refs)
+    n_out = len(kinds)
+    body = lambda *refs: down_kernel(n, n_out, None, *refs)
     if place is not None:
         lead = [place]
-        body = lambda *refs: down_kernel(n, *refs)
+        body = lambda *refs: down_kernel(n, n_out, *refs)
         shapes += [((128, WIDTH), bf16), ((64, WIDTH), bf16)]
     return pl.pallas_call(
         body,
         in_specs=[SMEM] * len(lead) + [VMEM] * len(operands),
         out_specs=[VMEM] * len(shapes),
         out_shape=[jax.ShapeDtypeStruct(s, kind) for s, kind in shapes],
-        scratch_shapes=[pltpu.VMEM((64 * n, 512), bf16)],
+        scratch_shapes=[pltpu.VMEM((64 * n_out, 512), bf16)],
         compiler_params=pltpu.CompilerParams(vmem_limit_bytes=10 * 1024 * 1024),
         cost_estimate=SMALL,
     )(*lead, *operands)
@@ -252,6 +258,11 @@
         factor[16 * k : 16 * k + 16, :] = g[:, WIDTH:]
 
 
+def halves_kernel(rows3, rows1, to1, to3):
+    to1[...] = rows3[:32, :]
+    to3[...] = rows1[32:, :]
+
+
 def touch_kernel(gate_w, up_w, down_w, out):
     out[...] = jnp.zeros_like(out)
 
@@ -336,7 +347,7 @@
     )
 
     packed = after(packed, gate2)
-    got = [packed] + [send(packed, FIRST[k]) for k in (1, 2, 3)]
+    got = spread(packed, FIRST)
     down2 = send(after(frozen_down_weight, packed), CORE)
     seconds = (adapter_second_gate, adapter_second_up, adapter_first_down)
     (seconds,) = local(
@@ -345,11 +356,12 @@
     block, factor = local(unpack_kernel, [((64, WIDTH), bf16), ((64, 3072), bf16)], got)
 
     block, factor = after((block, factor), (up2, down2, seconds))
-    factors = [factor] + [send(factor, SECOND[k]) for k in (1, 2, 3)]
+    factors = spread(factor, SECOND)
     rows1, rows3 = send(block, SECOND[1]), send(block, SECOND[3])
     (factor,) = local(stack_kernel, [((256, 3072 + 256), bf16)], (*factors, seconds))
     factor2 = send(factor, CORE)
-    rows2 = send(after(block, factor), SECOND[2])
+    to1, to3 = local(halves_kernel, [((32, WIDTH), bf16)] * 2, (rows3, rows1))
+    rows2 = (send(to1, SECOND[1]), send(to3, SECOND[3]))
     frozen = (frozen_gate_weight, frozen_up_weight, frozen_down_weight)
     owned = after(frozen, block)
     (touched,) = local(touch_kernel, [((8, 128), f32)], in_vmem(owned))
@@ -364,7 +376,7 @@
         (f32, bf16, bf16),
     )
     back1, back3 = send(part1, SECOND[1]), send(part3, SECOND[3])
-    rows = (after(rows2, part1),)
+    rows = after(rows2, part1)
     acc = project(rows, weights)
     (part2,) = down(
         None, rows, acc, down_weights, (seconds, factor2), (first, second), (bf16,)

time: 134 us -> 125 us (0.933)
  waiting for transfers between devices: 64.5 us -> 53.2 us
  starting transfers between devices: 40.3 us -> 42.2 us
    ppermute x27 -> x28, waiting for transfers between devices: 64.5 us -> 53.2 us  [send(): return lax.ppermute(value, AXES, route)]
    ppermute x27 -> x28, starting transfers between devices: 40.3 us -> 42.2 us  [send(): return lax.ppermute(value, AXES, route)]
    pallas_call x10 -> x11, Pallas kernels: 4.1 us -> 4.2 us  [local(): pl.pallas_call(body, in_specs=[SMEM] * len(lead) + [VMEM] * len(operands)...]
  transfers between devices with their start and end apart: 27 -> 28, of which waited for: 18 -> 19; matrix products, arithmetic and copies ran while one was open for 0% -> 0% of each run, Pallas kernels for 14% -> 15%
where the time goes in v7:
time: 125 us
  waiting for transfers between devices  53.2 us (43%)
  starting transfers between devices  42.2 us (34%)
  Pallas kernels  22 us (18%)
  local copies, waits for them, and re-layouts  6.44 us (5%)
    ppermute x28, waiting for transfers between devices, send(): return lax.ppermute(value, AXES, route)  53.2 us
    ppermute x28, starting transfers between devices, send(): return lax.ppermute(value, AXES, route)  42.2 us
    pallas_call x2, Pallas kernels, down(): pl.pallas_call(body, in_specs=[SMEM] * len(lead) + [VMEM] * len(operands)...  9.62 us
    pallas_call x2, Pallas kernels, project(): pl.pallas_call(lambda *refs: project_kernel(n, *refs[more:]), in_specs=[V...  8.15 us
    unnamed x16, local copies, waits for them, and re-layouts  6.36 us
    pallas_call x11, Pallas kernels, local(): pl.pallas_call(body, in_specs=[SMEM] * len(lead) + [VMEM] * len(operands)...  4.2 us
  transfers between devices with their start and end apart: 28, of which 19 were waited for; matrix products, arithmetic and copies ran while one was open for 0% of the time, Pallas kernels for 15%

profile of v7, /device:TPU:1, one launch (start us, length us, event | category | flops | bytes accessed | tf_op | source)
XLA Modules:
  0.0 124.6 jit_solution(5947360279770736278)
XLA Ops:
  0.1 1.6 %shard_map.100 = (bf16[8,2048]{1,0:T(8,128)(2,1)S(1)}, bf16[8,2048]{1,0:T(8,128)(2,1)S(1)}, bf16[16,1536]{1,0:T(8,128)(2,1)S(1)}) custom-call(s32[5]{0:T(128)S(1)} %stack.23.place.refs_0_, bf16[2,8,2048]{2,1,0:T(8,128)(2,1)} %inputs.1, bf16[64,256]{1,0:T(8,128)(2,1)} %gate.1, bf16[64,256]{1,0:T(8,128)(2,1)} %up.1, bf16[64,256]{1,0:T(8,128)(2,1)} %down.1), custom_call_target="tpu_custom_call" | custom-call | flops 1 | bytes 1 | tf_op jit(solution)/shard_map/pallas_call | solution.py:200
  1.7 1.5 %collective-permute-start = (bf16[8,2048]{1,0:T(8,128)(2,1)S(1)}, bf16[8,2048]{1,0:T(8,128)(2,1)S(1)}, u32[]{:S(2)}, u32[]{:S(2)}) collective-permute-start(bf16[8,2048]{1,0:T(8,128)(2,1)S(1)} %get-tuple-element.42), channel_id=1, source_target_pairs={{0,1},{1,0},{2,3},{3,2},{4,5},{5,4},{6,7},{7,6},{8,9},{9,8},{10,11... | collective-permute-start | bytes 98312 | tf_op jit(solution)/shard_map/ppermute | solution.py:50
  3.2 0.9 collective-permute-done.other
  5.1 3.8 %collective-permute-start.3 = (bf16[16,3584]{1,0:T(8,128)(2,1)S(1)}, bf16[16,3584]{1,0:T(8,128)(2,1)S(1)}, u32[]{:S(2)}, u32[]{:S(2)}) collective-permute-start(bf16[16,3584]{1,0:T(8,128)(2,1)S(1)} %get-tuple-element.45.message), channel_id=1, source_target_pairs={{0,66},{1,67},{2,64},{3,65},{4,70},{5,71},{6,68},{7,69},{8,74},{9,... | collective-permute-start | bytes 344072 | tf_op jit(solution)/shard_map/ppermute | solution.py:50
  8.9 1.2 collective-permute-start.2
  10.1 0.7 collective-permute-start.8
  10.9 1.5 %collective-permute-done.1.z1 = bf16[8,4096]{1,0:T(8,128)(2,1)S(1)} collective-permute-done((bf16[8,4096]{1,0:T(8,128)(2,1)S(1)}, bf16[8,4096]{1,0:T(8,128)(2,1)S(1)}, u32[]{:S(2)}, u32[]{:S(2)}) %collective-permute-start.1) | collective-permute-done | bytes 65568 | tf_op jit(solution)/shard_map/ppermute | solution.py:50
  12.3 1.2 collective-permute-done.2.z2
  14.1 1.7 %collective-permute-start.9 = (bf16[224,8192]{1,0:T(8,128)(2,1)}, bf16[224,8192]{1,0:T(8,128)(2,1)S(1)}, u32[]{:S(2)}, u32[]{:S(2)}) collective-permute-start(bf16[224,8192]{1,0:T(8,128)(2,1)} %refs_3_), channel_id=1, source_target_pairs={{0,1},{1,0},{2,3},{3,2},{4,5},{5,4},{6,7},{7,6},{8,9},{9,8},{10,11... | collective-permute-start | bytes 11010056 | tf_op jit(solution)/shard_map/ppermute | solution.py:50
  15.8 1.3 %collective-permute-start.5 = (bf16[16,11264]{1,0:T(8,128)(2,1)S(1)}, bf16[16,11264]{1,0:T(8,128)(2,1)S(1)}, u32[]{:S(2)}, u32[]{:S(2)}) collective-permute-start(bf16[16,11264]{1,0:T(8,128)(2,1)S(1)} %shard_map.102.refs_0_), channel_id=1, source_target_pairs={{0,4},{1,17},{2,6},{3,19},{4,0},{5,21},{6,2},{7,23},{8,12},{9,25},... | collective-permute-start | bytes 1081352 | tf_op jit(solution)/shard_map/ppermute | solution.py:50
  17.1 2.6 %collective-permute-start.6 = (bf16[16,11264]{1,0:T(8,128)(2,1)S(1)}, bf16[16,11264]{1,0:T(8,128)(2,1)S(1)}, u32[]{:S(2)}, u32[]{:S(2)}) collective-permute-start(bf16[16,11264]{1,0:T(8,128)(2,1)S(1)} %shard_map.102.refs_0_), channel_id=1, source_target_pairs={{0,8},{1,33},{2,10},{3,35},{4,12},{5,37},{6,14},{7,39},{8,0},{9,41... | collective-permute-start | bytes 1081352 | tf_op jit(solution)/shard_map/ppermute | solution.py:50
  19.7 0.8 copy-done.5
  20.5 0.8 copy-done.6
  21.3 0.8 copy-done.7
  22.4 6.4 %collective-permute-done.6.refs_2_ = bf16[16,11264]{1,0:T(8,128)(2,1)S(1)} collective-permute-done((bf16[16,11264]{1,0:T(8,128)(2,1)S(1)}, bf16[16,11264]{1,0:T(8,128)(2,1)S(1)}, u32[]{:S(2)}, u32[]{:S(2)}) %collective-permute-start.6) | collective-permute-done | bytes 360480 | tf_op jit(solution)/shard_map/ppermute | solution.py:50
  28.7 2.6 %collective-permute-done.7.refs_3_ = bf16[16,11264]{1,0:T(8,128)(2,1)S(1)} collective-permute-done((bf16[16,11264]{1,0:T(8,128)(2,1)S(1)}, bf16[16,11264]{1,0:T(8,128)(2,1)S(1)}, u32[]{:S(2)}, u32[]{:S(2)}) %collective-permute-start.7) | collective-permute-done | bytes 360480 | tf_op jit(solution)/shard_map/ppermute | solution.py:50
  31.5 1.0 collective-permute-start.12
  32.5 2.5 %collective-permute-start.13 = (bf16[64,3072]{1,0:T(8,128)(2,1)S(1)}, bf16[64,3072]{1,0:T(8,128)(2,1)S(1)}, u32[]{:S(2)}, u32[]{:S(2)}) collective-permute-start(bf16[64,3072]{1,0:T(8,128)(2,1)S(1)} %get-tuple-element.59.f0), channel_id=1, source_target_pairs={{0,32},{1,9},{2,34},{3,11},{4,36},{5,13},{6,38},{7,15},{8,40},{9,1... | collective-permute-start | bytes 1179656 | tf_op jit(solution)/shard_map/ppermute | solution.py:50
  35.4 2.2 %collective-permute-start.11 = (bf16[64,8192]{1,0:T(8,128)(2,1)S(1)}, bf16[64,8192]{1,0:T(8,128)(2,1)S(1)}, u32[]{:S(2)}, u32[]{:S(2)}) collective-permute-start(bf16[64,8192]{1,0:T(8,128)(2,1)S(1)} %get-tuple-element.55.refs_1_), channel_id=1, source_target_pairs={{0,48},{1,13},{2,50},{3,15},{4,52},{5,9},{6,54},{7,11},{8,56},{9,5... | collective-permute-start | bytes 3145736 | tf_op jit(solution)/shard_map/ppermute | solution.py:50
  37.6 0.9 collective-permute-done.12.f1
  38.5 6.2 %collective-permute-done.13.f2 = bf16[64,3072]{1,0:T(8,128)(2,1)S(1)} collective-permute-done((bf16[64,3072]{1,0:T(8,128)(2,1)S(1)}, bf16[64,3072]{1,0:T(8,128)(2,1)S(1)}, u32[]{:S(2)}, u32[]{:S(2)}) %collective-permute-start.13) | collective-permute-done | bytes 393248 | tf_op jit(solution)/shard_map/ppermute | solution.py:50
  44.7 2.6 %collective-permute-done.14.f3 = bf16[64,3072]{1,0:T(8,128)(2,1)S(1)} collective-permute-done((bf16[64,3072]{1,0:T(8,128)(2,1)S(1)}, bf16[64,3072]{1,0:T(8,128)(2,1)S(1)}, u32[]{:S(2)}, u32[]{:S(2)}) %collective-permute-start.14) | collective-permute-done | bytes 393248 | tf_op jit(solution)/shard_map/ppermute | solution.py:50
  47.4 3.3 %collective-permute-start.15 = (bf16[256,3328]{1,0:T(8,128)(2,1)S(1)}, bf16[256,3328]{1,0:T(8,128)(2,1)S(1)}, u32[]{:S(2)}, u32[]{:S(2)}) collective-permute-start(bf16[256,3328]{1,0:T(8,128)(2,1)S(1)} %shard_map.107.refs_9_), channel_id=1, source_target_pairs={{0,1},{1,0},{2,3},{3,2},{4,5},{5,4},{6,7},{7,6},{8,9},{9,8},{10,11... | collective-permute-start | bytes 5111816 | tf_op jit(solution)/shard_map/ppermute | solution.py:50
  50.7 2.0 %copy-done.1 = bf16[224,8192]{1,0:T(8,128)(2,1)S(1)} copy-done((bf16[224,8192]{1,0:T(8,128)(2,1)S(1)}, bf16[224,8192]{1,0:T(8,128)(2,1)}, u32[]{:S(2)}) %copy-start.1) | copy-done | bytes 3670040
  52.7 2.0 %copy-done.3 = bf16[224,8192]{1,0:T(8,128)(2,1)S(1)} copy-done((bf16[224,8192]{1,0:T(8,128)(2,1)S(1)}, bf16[224,8192]{1,0:T(8,128)(2,1)}, u32[]{:S(2)}) %copy-start.3) | copy-done | bytes 3670040
  54.8 3.7 %collective-permute-done.11.refs_3_.rows3 = bf16[64,8192]{1,0:T(8,128)(2,1)S(1)} collective-permute-done((bf16[64,8192]{1,0:T(8,128)(2,1)S(1)}, bf16[64,8192]{1,0:T(8,128)(2,1)S(1)}, u32[]{:S(2)}, u32[]{:S(2)}) %collective-permute-start.11) | collective-permute-done | bytes 1048608 | tf_op jit(solution)/shard_map/ppermute | solution.py:50
  58.7 0.8 collective-permute-start.19
  59.5 4.1 %shard_map.106.refs_4_ = f32[896,192]{1,0:T(8,128)S(1)} custom-call(f32[8,128]{1,0:T(8,128)S(1)} %shard_map.105.refs_0_, bf16[64,8192]{1,0:T(8,128)(2,1)S(1)} %get-tuple-element.55.refs_1_, bf16[64,8192]{1,0:T(8,128)(2,1)S(1)} %collective-permute-done.10.refs_2_.rows1, bf16[64,8192]{1,0:T(8,128)(2,1)S(1)} %collective-permute-done.11.refs_3_.rows3, ...), custom_call_target="tpu_custom_call" | custom-call | flops 9200000000 | bytes 28800000 | tf_op jit(solution)/shard_map/pallas_call | solution.py:165
  63.5 6.1 %shard_map.108 = (f32[64,8192]{1,0:T(8,128)S(1)}, bf16[64,8192]{1,0:T(8,128)(2,1)S(1)}, bf16[64,8192]{1,0:T(8,128)(2,1)S(1)}, bf16[128,8192]{1,0:T(8,128)(2,1)S(1)}, bf16[64,8192]{1,0:T(8,128)(2,1)S(1)}) custom-call(s32[5]{0:T(128)S(1)} %stack.23.place.refs_0_, bf16[64,8192]{1,0:T(8,128)(2,1)S(1)} %get-tuple-element.55.refs_1_, ...), custom_call_target="tpu_custom_call" | custom-call | flops 1 | bytes 1 | tf_op jit(solution)/shard_map/pallas_call | solution.py:187
  69.6 0.8 collective-permute-start.16
  70.4 2.1 %collective-permute-start.17 = (bf16[64,8192]{1,0:T(8,128)(2,1)S(1)}, bf16[64,8192]{1,0:T(8,128)(2,1)S(1)}, u32[]{:S(2)}, u32[]{:S(2)}) collective-permute-start(bf16[64,8192]{1,0:T(8,128)(2,1)S(1)} %get-tuple-element.62), channel_id=1, source_target_pairs={{0,48},{1,13},{2,50},{3,15},{4,52},{5,9},{6,54},{7,11},{8,56},{9,5... | collective-permute-start | bytes 3145736 | tf_op jit(solution)/shard_map/ppermute | solution.py:50
  72.4 4.1 %shard_map.111.refs_2_ = f32[896,64]{1,0:T(8,128)S(1)} custom-call(bf16[32,8192]{1,0:T(8,128)(2,1)S(1)} %collective-permute-done.18.refs_0_, bf16[32,8192]{1,0:T(8,128)(2,1)S(1)} %collective-permute-done.19.refs_1_, bf16[224,8192]{1,0:T(8,128)(2,1)S(1)} %copy-done.2, bf16[224,8192]{1,0:T(8,128)(2,1)S(1)} %collective-permute-done.4.refs_5_.refs_3_, ...), custom_call_target="tpu_custom_call" | custom-call | flops 9200000000 | bytes 28800000 | tf_op jit(solution)/shard_map/pallas_call | solution.py:165
  76.5 3.6 %shard_map.112 = bf16[64,8192]{1,0:T(8,128)(2,1)S(1)} custom-call(bf16[32,8192]{1,0:T(8,128)(2,1)S(1)} %collective-permute-done.18.refs_0_, bf16[32,8192]{1,0:T(8,128)(2,1)S(1)} %collective-permute-done.19.refs_1_, f32[896,64]{1,0:T(8,128)S(1)} %shard_map.111.refs_2_, bf16[224,8192]{1,0:T(8,128)(2,1)S(1)} %copy-done, ...), custom_call_target="tpu_custom_call" | custom-call | flops 1 | bytes 1 | tf_op jit(solution)/shard_map/pallas_call | solution.py:187
  80.1 0.7 collective-permute-start.20
  80.8 2.9 %collective-permute-done.16.b1 = bf16[64,8192]{1,0:T(8,128)(2,1)S(1)} collective-permute-done((bf16[64,8192]{1,0:T(8,128)(2,1)S(1)}, bf16[64,8192]{1,0:T(8,128)(2,1)S(1)}, u32[]{:S(2)}, u32[]{:S(2)}) %collective-permute-start.16) | collective-permute-done | bytes 1048608 | tf_op jit(solution)/shard_map/ppermute | solution.py:50
  83.6 11.8 %collective-permute-done.17.b3 = bf16[64,8192]{1,0:T(8,128)(2,1)S(1)} collective-permute-done((bf16[64,8192]{1,0:T(8,128)(2,1)S(1)}, bf16[64,8192]{1,0:T(8,128)(2,1)S(1)}, u32[]{:S(2)}, u32[]{:S(2)}) %collective-permute-start.17) | collective-permute-done | bytes 1048608 | tf_op jit(solution)/shard_map/ppermute | solution.py:50
  95.7 1.0 collective-permute-done.20.b
  97.0 1.5 %collective-permute-start.22 = (bf16[16,8192]{1,0:T(8,128)(2,1)S(1)}, bf16[16,8192]{1,0:T(8,128)(2,1)S(1)}, u32[]{:S(2)}, u32[]{:S(2)}) collective-permute-start(bf16[16,8192]{1,0:T(8,128)(2,1)S(1)} %get-tuple-element.71), channel_id=1, source_target_pairs={{0,8},{1,33},{2,10},{3,35},{4,12},{5,37},{6,14},{7,39},{8,0},{9,41... | collective-permute-start | bytes 786440 | tf_op jit(solution)/shard_map/ppermute | solution.py:50
  98.5 2.4 %collective-permute-start.23 = (bf16[16,8192]{1,0:T(8,128)(2,1)S(1)}, bf16[16,8192]{1,0:T(8,128)(2,1)S(1)}, u32[]{:S(2)}, u32[]{:S(2)}) collective-permute-start(bf16[16,8192]{1,0:T(8,128)(2,1)S(1)} %get-tuple-element.72), channel_id=1, source_target_pairs={{0,12},{1,49},{2,14},{3,51},{4,8},{5,53},{6,10},{7,55},{8,4},{9,57... | collective-permute-start | bytes 786440 | tf_op jit(solution)/shard_map/ppermute | solution.py:50
  100.9 1.4 %collective-permute-done.21.b1 = bf16[16,8192]{1,0:T(8,128)(2,1)S(1)} collective-permute-done((bf16[16,8192]{1,0:T(8,128)(2,1)S(1)}, bf16[16,8192]{1,0:T(8,128)(2,1)S(1)}, u32[]{:S(2)}, u32[]{:S(2)}) %collective-permute-start.21) | collective-permute-done | bytes 262176 | tf_op jit(solution)/shard_map/ppermute | solution.py:50
  102.2 4.0 %collective-permute-done.22.b2 = bf16[16,8192]{1,0:T(8,128)(2,1)S(1)} collective-permute-done((bf16[16,8192]{1,0:T(8,128)(2,1)S(1)}, bf16[16,8192]{1,0:T(8,128)(2,1)S(1)}, u32[]{:S(2)}, u32[]{:S(2)}) %collective-permute-start.22) | collective-permute-done | bytes 262176 | tf_op jit(solution)/shard_map/ppermute | solution.py:50
  106.2 1.8 %collective-permute-done.23.b3 = bf16[16,8192]{1,0:T(8,128)(2,1)S(1)} collective-permute-done((bf16[16,8192]{1,0:T(8,128)(2,1)S(1)}, bf16[16,8192]{1,0:T(8,128)(2,1)S(1)}, u32[]{:S(2)}, u32[]{:S(2)}) %collective-permute-start.23) | collective-permute-done | bytes 262176 | tf_op jit(solution)/shard_map/ppermute | solution.py:50
  108.7 2.2 %collective-permute-start.26 = (bf16[8,4096]{1,0:T(8,128)(2,1)S(1)}, bf16[8,4096]{1,0:T(8,128)(2,1)S(1)}, u32[]{:S(2)}, u32[]{:S(2)}) collective-permute-start(bf16[8,4096]{1,0:T(8,128)(2,1)S(1)} %get-tuple-element.76), channel_id=1, source_target_pairs={{0,66},{1,67},{2,64},{3,65},{4,70},{5,71},{6,68},{7,69},{8,74},{9,... | collective-permute-start | bytes 196616 | tf_op jit(solution)/shard_map/ppermute | solution.py:50
  110.9 1.4 %collective-permute-start.25 = (bf16[8,4096]{1,0:T(8,128)(2,1)S(1)}, bf16[8,4096]{1,0:T(8,128)(2,1)S(1)}, u32[]{:S(2)}, u32[]{:S(2)}) collective-permute-start(bf16[8,4096]{1,0:T(8,128)(2,1)S(1)} %get-tuple-element.75), channel_id=1, source_target_pairs={{0,64},{1,65},{2,66},{3,67},{4,68},{5,69},{6,70},{7,71},{8,72},{9,... | collective-permute-start | bytes 196616 | tf_op jit(solution)/shard_map/ppermute | solution.py:50
  112.3 1.1 collective-permute-done.26
  113.4 2.1 %collective-permute-done.25 = bf16[8,4096]{1,0:T(8,128)(2,1)S(1)} collective-permute-done((bf16[8,4096]{1,0:T(8,128)(2,1)S(1)}, bf16[8,4096]{1,0:T(8,128)(2,1)S(1)}, u32[]{:S(2)}, u32[]{:S(2)}) %collective-permute-start.25) | collective-permute-done | bytes 65568 | tf_op jit(solution)/shard_map/ppermute | solution.py:50
  115.5 7.6 %collective-permute-start.27 = (bf16[8,2048]{1,0:T(8,128)(2,1)S(1)}, bf16[8,2048]{1,0:T(8,128)(2,1)S(1)}, u32[]{:S(2)}, u32[]{:S(2)}) collective-permute-start(bf16[8,2048]{1,0:T(8,128)(2,1)S(1)} %get-tuple-element.78), channel_id=1, source_target_pairs={{0,1},{1,0},{2,3},{3,2},{4,5},{5,4},{6,7},{7,6},{8,9},{9,8},{10,11... | collective-permute-start | bytes 98312 | tf_op jit(solution)/shard_map/ppermute | solution.py:50
  123.1 0.9 collective-permute-done.27
  (43 shorter events, 4.8 us)
Async XLA Ops:
  0.1 50.6 %copy-start = (bf16[224,8192]{1,0:T(8,128)(2,1)S(1)}, bf16[224,8192]{1,0:T(8,128)(2,1)}, u32[]{:S(2)}) copy-start(bf16[224,8192]{1,0:T(8,128)(2,1)} %refs_3_) | copy-start | bytes 11010052
  1.7 2.4 %collective-permute-start = (bf16[8,2048]{1,0:T(8,128)(2,1)S(1)}, bf16[8,2048]{1,0:T(8,128)(2,1)S(1)}, u32[]{:S(2)}, u32[]{:S(2)}) collective-permute-start(bf16[8,2048]{1,0:T(8,128)(2,1)S(1)} %get-tuple-element.42), channel_id=1, source_target_pairs={{0,1},{1,0},{2,3},{3,2},{4,5},{5,4},{6,7},{7,6},{8,9},{9,8},{10,11... | collective-permute-start | bytes 98312 | tf_op jit(solution)/shard_map/ppermute | solution.py:50
  4.7 9.5 %collective-permute-start.4 = (bf16[224,8192]{1,0:T(8,128)(2,1)}, bf16[224,8192]{1,0:T(8,128)(2,1)S(1)}, u32[]{:S(2)}, u32[]{:S(2)}) collective-permute-start(bf16[224,8192]{1,0:T(8,128)(2,1)} %refs_2_), channel_id=1, source_target_pairs={{0,1},{1,0},{2,3},{3,2},{4,5},{5,4},{6,7},{7,6},{8,9},{9,8},{10,11... | collective-permute-start | bytes 11010056 | tf_op jit(solution)/shard_map/ppermute | solution.py:50
  5.1 8.5 %collective-permute-start.3 = (bf16[16,3584]{1,0:T(8,128)(2,1)S(1)}, bf16[16,3584]{1,0:T(8,128)(2,1)S(1)}, u32[]{:S(2)}, u32[]{:S(2)}) collective-permute-start(bf16[16,3584]{1,0:T(8,128)(2,1)S(1)} %get-tuple-element.45.message), channel_id=1, source_target_pairs={{0,66},{1,67},{2,64},{3,65},{4,70},{5,71},{6,68},{7,69},{8,74},{9,... | collective-permute-start | bytes 344072 | tf_op jit(solution)/shard_map/ppermute | solution.py:50
  8.9 3.4 %collective-permute-start.1 = (bf16[8,4096]{1,0:T(8,128)(2,1)S(1)}, bf16[8,4096]{1,0:T(8,128)(2,1)S(1)}, u32[]{:S(2)}, u32[]{:S(2)}) collective-permute-start(bf16[8,4096]{1,0:T(8,128)(2,1)S(1)} %get-tuple-element.44.wide), channel_id=1, source_target_pairs={{0,2},{1,3},{2,0},{3,1},{4,6},{5,7},{6,4},{7,5},{8,10},{9,11},{10,... | collective-permute-start | bytes 196616 | tf_op jit(solution)/shard_map/ppermute | solution.py:50
  8.9 4.6 %collective-permute-start.2 = (bf16[8,4096]{1,0:T(8,128)(2,1)S(1)}, bf16[8,4096]{1,0:T(8,128)(2,1)S(1)}, u32[]{:S(2)}, u32[]{:S(2)}) collective-permute-start(bf16[8,4096]{1,0:T(8,128)(2,1)S(1)} %get-tuple-element.44.wide), channel_id=1, source_target_pairs={{0,64},{1,65},{2,66},{3,67},{4,68},{5,69},{6,70},{7,71},{8,72},{9,... | collective-permute-start | bytes 196616 | tf_op jit(solution)/shard_map/ppermute | solution.py:50
  10.1 21.4 %collective-permute-start.8 = (bf16[224,8192]{1,0:T(8,128)(2,1)}, bf16[224,8192]{1,0:T(8,128)(2,1)S(1)}, u32[]{:S(2)}, u32[]{:S(2)}) collective-permute-start(bf16[224,8192]{1,0:T(8,128)(2,1)} %refs_4_.1), channel_id=1, source_target_pairs={{0,1},{1,0},{2,3},{3,2},{4,5},{5,4},{6,7},{7,6},{8,9},{9,8},{10,11... | collective-permute-start | bytes 11010056 | tf_op jit(solution)/shard_map/ppermute | solution.py:50
  14.1 17.3 %collective-permute-start.9 = (bf16[224,8192]{1,0:T(8,128)(2,1)}, bf16[224,8192]{1,0:T(8,128)(2,1)S(1)}, u32[]{:S(2)}, u32[]{:S(2)}) collective-permute-start(bf16[224,8192]{1,0:T(8,128)(2,1)} %refs_3_), channel_id=1, source_target_pairs={{0,1},{1,0},{2,3},{3,2},{4,5},{5,4},{6,7},{7,6},{8,9},{9,8},{10,11... | collective-permute-start | bytes 11010056 | tf_op jit(solution)/shard_map/ppermute | solution.py:50
  15.8 6.6 %collective-permute-start.5 = (bf16[16,11264]{1,0:T(8,128)(2,1)S(1)}, bf16[16,11264]{1,0:T(8,128)(2,1)S(1)}, u32[]{:S(2)}, u32[]{:S(2)}) collective-permute-start(bf16[16,11264]{1,0:T(8,128)(2,1)S(1)} %shard_map.102.refs_0_), channel_id=1, source_target_pairs={{0,4},{1,17},{2,6},{3,19},{4,0},{5,21},{6,2},{7,23},{8,12},{9,25},... | collective-permute-start | bytes 1081352 | tf_op jit(solution)/shard_map/ppermute | solution.py:50
  17.1 11.6 %collective-permute-start.6 = (bf16[16,11264]{1,0:T(8,128)(2,1)S(1)}, bf16[16,11264]{1,0:T(8,128)(2,1)S(1)}, u32[]{:S(2)}, u32[]{:S(2)}) collective-permute-start(bf16[16,11264]{1,0:T(8,128)(2,1)S(1)} %shard_map.102.refs_0_), channel_id=1, source_target_pairs={{0,8},{1,33},{2,10},{3,35},{4,12},{5,37},{6,14},{7,39},{8,0},{9,41... | collective-permute-start | bytes 1081352 | tf_op jit(solution)/shard_map/ppermute | solution.py:50
  19.7 11.6 %collective-permute-start.7 = (bf16[16,11264]{1,0:T(8,128)(2,1)S(1)}, bf16[16,11264]{1,0:T(8,128)(2,1)S(1)}, u32[]{:S(2)}, u32[]{:S(2)}) collective-permute-start(bf16[16,11264]{1,0:T(8,128)(2,1)S(1)} %shard_map.102.refs_0_), channel_id=1, source_target_pairs={{0,12},{1,49},{2,14},{3,51},{4,8},{5,53},{6,10},{7,55},{8,4},{9,57... | collective-permute-start | bytes 1081352 | tf_op jit(solution)/shard_map/ppermute | solution.py:50
  19.7 0.8 copy-start.5
  20.5 0.8 copy-start.6
  21.3 0.8 copy-start.7
  31.5 7.0 %collective-permute-start.12 = (bf16[64,3072]{1,0:T(8,128)(2,1)S(1)}, bf16[64,3072]{1,0:T(8,128)(2,1)S(1)}, u32[]{:S(2)}, u32[]{:S(2)}) collective-permute-start(bf16[64,3072]{1,0:T(8,128)(2,1)S(1)} %get-tuple-element.59.f0), channel_id=1, source_target_pairs={{0,16},{1,5},{2,18},{3,7},{4,20},{5,1},{6,22},{7,3},{8,24},{9,13},... | collective-permute-start | bytes 1179656 | tf_op jit(solution)/shard_map/ppermute | solution.py:50
  32.5 12.2 %collective-permute-start.13 = (bf16[64,3072]{1,0:T(8,128)(2,1)S(1)}, bf16[64,3072]{1,0:T(8,128)(2,1)S(1)}, u32[]{:S(2)}, u32[]{:S(2)}) collective-permute-start(bf16[64,3072]{1,0:T(8,128)(2,1)S(1)} %get-tuple-element.59.f0), channel_id=1, source_target_pairs={{0,32},{1,9},{2,34},{3,11},{4,36},{5,13},{6,38},{7,15},{8,40},{9,1... | collective-permute-start | bytes 1179656 | tf_op jit(solution)/shard_map/ppermute | solution.py:50
  34.9 12.3 %collective-permute-start.14 = (bf16[64,3072]{1,0:T(8,128)(2,1)S(1)}, bf16[64,3072]{1,0:T(8,128)(2,1)S(1)}, u32[]{:S(2)}, u32[]{:S(2)}) collective-permute-start(bf16[64,3072]{1,0:T(8,128)(2,1)S(1)} %get-tuple-element.59.f0), channel_id=1, source_target_pairs={{0,48},{1,13},{2,50},{3,15},{4,52},{5,9},{6,54},{7,11},{8,56},{9,5... | collective-permute-start | bytes 1179656 | tf_op jit(solution)/shard_map/ppermute | solution.py:50
  35.4 19.4 %collective-permute-start.10 = (bf16[64,8192]{1,0:T(8,128)(2,1)S(1)}, bf16[64,8192]{1,0:T(8,128)(2,1)S(1)}, u32[]{:S(2)}, u32[]{:S(2)}) collective-permute-start(bf16[64,8192]{1,0:T(8,128)(2,1)S(1)} %get-tuple-element.55.refs_1_), channel_id=1, source_target_pairs={{0,16},{1,5},{2,18},{3,7},{4,20},{5,1},{6,22},{7,3},{8,24},{9,13},... | collective-permute-start | bytes 3145736 | tf_op jit(solution)/shard_map/ppermute | solution.py:50
  35.4 23.1 %collective-permute-start.11 = (bf16[64,8192]{1,0:T(8,128)(2,1)S(1)}, bf16[64,8192]{1,0:T(8,128)(2,1)S(1)}, u32[]{:S(2)}, u32[]{:S(2)}) collective-permute-start(bf16[64,8192]{1,0:T(8,128)(2,1)S(1)} %get-tuple-element.55.refs_1_), channel_id=1, source_target_pairs={{0,48},{1,13},{2,50},{3,15},{4,52},{5,9},{6,54},{7,11},{8,56},{9,5... | collective-permute-start | bytes 3145736 | tf_op jit(solution)/shard_map/ppermute | solution.py:50
  47.4 16.1 %collective-permute-start.15 = (bf16[256,3328]{1,0:T(8,128)(2,1)S(1)}, bf16[256,3328]{1,0:T(8,128)(2,1)S(1)}, u32[]{:S(2)}, u32[]{:S(2)}) collective-permute-start(bf16[256,3328]{1,0:T(8,128)(2,1)S(1)} %shard_map.107.refs_9_), channel_id=1, source_target_pairs={{0,1},{1,0},{2,3},{3,2},{4,5},{5,4},{6,7},{7,6},{8,9},{9,8},{10,11... | collective-permute-start | bytes 5111816 | tf_op jit(solution)/shard_map/ppermute | solution.py:50
  50.7 2.0 %copy-start.1 = (bf16[224,8192]{1,0:T(8,128)(2,1)S(1)}, bf16[224,8192]{1,0:T(8,128)(2,1)}, u32[]{:S(2)}) copy-start(bf16[224,8192]{1,0:T(8,128)(2,1)} %refs_2_) | copy-start | bytes 11010052
  52.7 2.0 %copy-start.3 = (bf16[224,8192]{1,0:T(8,128)(2,1)S(1)}, bf16[224,8192]{1,0:T(8,128)(2,1)}, u32[]{:S(2)}) copy-start(bf16[224,8192]{1,0:T(8,128)(2,1)} %refs_4_.1) | copy-start | bytes 11010052
  54.8 4.7 %copy-start.2 = (bf16[224,8192]{1,0:T(8,128)(2,1)S(1)}, bf16[224,8192]{1,0:T(8,128)(2,1)}, u32[]{:S(2)}) copy-start(bf16[224,8192]{1,0:T(8,128)(2,1)} %refs_2_) | copy-start | bytes 11010052
  54.8 4.7 %copy-start.4 = (bf16[224,8192]{1,0:T(8,128)(2,1)S(1)}, bf16[224,8192]{1,0:T(8,128)(2,1)}, u32[]{:S(2)}) copy-start(bf16[224,8192]{1,0:T(8,128)(2,1)} %refs_4_.1) | copy-start | bytes 11010052
  58.6 13.8 %collective-permute-start.18 = (bf16[32,8192]{1,0:T(8,128)(2,1)S(1)}, bf16[32,8192]{1,0:T(8,128)(2,1)S(1)}, u32[]{:S(2)}, u32[]{:S(2)}) collective-permute-start(bf16[32,8192]{1,0:T(8,128)(2,1)S(1)} %get-tuple-element.63), channel_id=1, source_target_pairs={{0,16},{1,5},{2,18},{3,7},{4,20},{5,1},{6,22},{7,3},{8,24},{9,13},... | collective-permute-start | bytes 1572872 | tf_op jit(solution)/shard_map/ppermute | solution.py:50
  58.7 13.8 %collective-permute-start.19 = (bf16[32,8192]{1,0:T(8,128)(2,1)S(1)}, bf16[32,8192]{1,0:T(8,128)(2,1)S(1)}, u32[]{:S(2)}, u32[]{:S(2)}) collective-permute-start(bf16[32,8192]{1,0:T(8,128)(2,1)S(1)} %get-tuple-element.64), channel_id=1, source_target_pairs={{0,48},{1,13},{2,50},{3,15},{4,52},{5,9},{6,54},{7,11},{8,56},{9,5... | collective-permute-start | bytes 1572872 | tf_op jit(solution)/shard_map/ppermute | solution.py:50
  69.6 14.0 %collective-permute-start.16 = (bf16[64,8192]{1,0:T(8,128)(2,1)S(1)}, bf16[64,8192]{1,0:T(8,128)(2,1)S(1)}, u32[]{:S(2)}, u32[]{:S(2)}) collective-permute-start(bf16[64,8192]{1,0:T(8,128)(2,1)S(1)} %get-tuple-element.61), channel_id=1, source_target_pairs={{0,16},{1,5},{2,18},{3,7},{4,20},{5,1},{6,22},{7,3},{8,24},{9,13},... | collective-permute-start | bytes 3145736 | tf_op jit(solution)/shard_map/ppermute | solution.py:50
  70.4 25.0 %collective-permute-start.17 = (bf16[64,8192]{1,0:T(8,128)(2,1)S(1)}, bf16[64,8192]{1,0:T(8,128)(2,1)S(1)}, u32[]{:S(2)}, u32[]{:S(2)}) collective-permute-start(bf16[64,8192]{1,0:T(8,128)(2,1)S(1)} %get-tuple-element.62), channel_id=1, source_target_pairs={{0,48},{1,13},{2,50},{3,15},{4,52},{5,9},{6,54},{7,11},{8,56},{9,5... | collective-permute-start | bytes 3145736 | tf_op jit(solution)/shard_map/ppermute | solution.py:50
  80.1 16.7 %collective-permute-start.20 = (bf16[64,8192]{1,0:T(8,128)(2,1)S(1)}, bf16[64,8192]{1,0:T(8,128)(2,1)S(1)}, u32[]{:S(2)}, u32[]{:S(2)}) collective-permute-start(bf16[64,8192]{1,0:T(8,128)(2,1)S(1)} %shard_map.112), channel_id=1, source_target_pairs={{0,32},{1,9},{2,34},{3,11},{4,36},{5,13},{6,38},{7,15},{8,40},{9,1... | collective-permute-start | bytes 3145736 | tf_op jit(solution)/shard_map/ppermute | solution.py:50
  96.9 5.3 %collective-permute-start.21 = (bf16[16,8192]{1,0:T(8,128)(2,1)S(1)}, bf16[16,8192]{1,0:T(8,128)(2,1)S(1)}, u32[]{:S(2)}, u32[]{:S(2)}) collective-permute-start(bf16[16,8192]{1,0:T(8,128)(2,1)S(1)} %get-tuple-element.70), channel_id=1, source_target_pairs={{0,4},{1,17},{2,6},{3,19},{4,0},{5,21},{6,2},{7,23},{8,12},{9,25},... | collective-permute-start | bytes 786440 | tf_op jit(solution)/shard_map/ppermute | solution.py:50
  97.0 9.2 %collective-permute-start.22 = (bf16[16,8192]{1,0:T(8,128)(2,1)S(1)}, bf16[16,8192]{1,0:T(8,128)(2,1)S(1)}, u32[]{:S(2)}, u32[]{:S(2)}) collective-permute-start(bf16[16,8192]{1,0:T(8,128)(2,1)S(1)} %get-tuple-element.71), channel_id=1, source_target_pairs={{0,8},{1,33},{2,10},{3,35},{4,12},{5,37},{6,14},{7,39},{8,0},{9,41... | collective-permute-start | bytes 786440 | tf_op jit(solution)/shard_map/ppermute | solution.py:50
  98.5 9.5 %collective-permute-start.23 = (bf16[16,8192]{1,0:T(8,128)(2,1)S(1)}, bf16[16,8192]{1,0:T(8,128)(2,1)S(1)}, u32[]{:S(2)}, u32[]{:S(2)}) collective-permute-start(bf16[16,8192]{1,0:T(8,128)(2,1)S(1)} %get-tuple-element.72), channel_id=1, source_target_pairs={{0,12},{1,49},{2,14},{3,51},{4,8},{5,53},{6,10},{7,55},{8,4},{9,57... | collective-permute-start | bytes 786440 | tf_op jit(solution)/shard_map/ppermute | solution.py:50
  108.7 4.7 %collective-permute-start.26 = (bf16[8,4096]{1,0:T(8,128)(2,1)S(1)}, bf16[8,4096]{1,0:T(8,128)(2,1)S(1)}, u32[]{:S(2)}, u32[]{:S(2)}) collective-permute-start(bf16[8,4096]{1,0:T(8,128)(2,1)S(1)} %get-tuple-element.76), channel_id=1, source_target_pairs={{0,66},{1,67},{2,64},{3,65},{4,70},{5,71},{6,68},{7,69},{8,74},{9,... | collective-permute-start | bytes 196616 | tf_op jit(solution)/shard_map/ppermute | solution.py:50
  110.9 4.6 %collective-permute-start.25 = (bf16[8,4096]{1,0:T(8,128)(2,1)S(1)}, bf16[8,4096]{1,0:T(8,128)(2,1)S(1)}, u32[]{:S(2)}, u32[]{:S(2)}) collective-permute-start(bf16[8,4096]{1,0:T(8,128)(2,1)S(1)} %get-tuple-element.75), channel_id=1, source_target_pairs={{0,64},{1,65},{2,66},{3,67},{4,68},{5,69},{6,70},{7,71},{8,72},{9,... | collective-permute-start | bytes 196616 | tf_op jit(solution)/shard_map/ppermute | solution.py:50
  112.3 3.2 %collective-permute-start.24 = (bf16[8,4096]{1,0:T(8,128)(2,1)S(1)}, bf16[8,4096]{1,0:T(8,128)(2,1)S(1)}, u32[]{:S(2)}, u32[]{:S(2)}) collective-permute-start(bf16[8,4096]{1,0:T(8,128)(2,1)S(1)} %get-tuple-element.74), channel_id=1, source_target_pairs={{0,2},{1,3},{2,0},{3,1},{4,6},{5,7},{6,4},{7,5},{8,10},{9,11},{10,... | collective-permute-start | bytes 196616 | tf_op jit(solution)/shard_map/ppermute | solution.py:50
  115.5 8.4 %collective-permute-start.27 = (bf16[8,2048]{1,0:T(8,128)(2,1)S(1)}, bf16[8,2048]{1,0:T(8,128)(2,1)S(1)}, u32[]{:S(2)}, u32[]{:S(2)}) collective-permute-start(bf16[8,2048]{1,0:T(8,128)(2,1)S(1)} %get-tuple-element.78), channel_id=1, source_target_pairs={{0,1},{1,0},{2,3},{3,2},{4,5},{5,4},{6,7},{7,6},{8,9},{9,8},{10,11... | collective-permute-start | bytes 98312 | tf_op jit(solution)/shard_map/ppermute | solution.py:50

commit v8 on v7

--- a/solution.py
+++ b/solution.py
@@ -13,6 +13,7 @@
 WIDTH = 8192
 HALF = WIDTH // 2
 QUARTER = WIDTH // 4
+CUT = (WIDTH + 3072) // 2
 UNITS = 224
 TILE = 4096
 STEPS = WIDTH // TILE
@@ -48,11 +49,6 @@
 
 def send(value, route):
     return lax.ppermute(value, AXES, route)
-
-
-def spread(value, routes):
-    got = {k: send(value, routes[k]) for k in (2, 1, 3)}
-    return [value, got[1], got[2], got[3]]
 
 
 def nt(a, b):
@@ -251,16 +247,24 @@
         out[:, at + 256 : at + 512] = far_message[:, col : col + 256]
 
 
-def unpack_kernel(*refs):
-    got, (block, factor) = refs[:4], refs[4:]
-    for k, g in enumerate(got):
+def unpack_kernel(own, got1, left, right, got3, block, factor):
+    for k, g in ((0, own), (1, got1), (3, got3)):
         block[16 * k : 16 * k + 16, :] = g[:, :WIDTH]
         factor[16 * k : 16 * k + 16, :] = g[:, WIDTH:]
-
-
-def halves_kernel(rows3, rows1, to1, to3):
-    to1[...] = rows3[:32, :]
-    to3[...] = rows1[32:, :]
+    block[32:48, :CUT] = left[...]
+    block[32:48, CUT:] = right[:, : WIDTH - CUT]
+    factor[32:48, :] = right[:, WIDTH - CUT :]
+
+
+def halves_kernel(from1, from3, to1, to3):
+    rows, cols = to1.shape
+    to1[...] = from3[:rows, :cols]
+    to3[...] = from1[-rows:, -cols:]
+
+
+def relay(from1, from3, routes, shape):
+    to1, to3 = local(halves_kernel, [(shape, bf16)] * 2, (from1, from3))
+    return send(to1, routes[1]), send(to3, routes[3])
 
 
 def touch_kernel(gate_w, up_w, down_w, out):
@@ -273,9 +277,9 @@
         out[64 * k : 64 * k + 64, :UNITS] = r[...]
 
 
-def stack_kernel(f0, f1, f2, f3, seconds, out):
-    for k, r in enumerate((f0, f1, f2, f3)):
-        out[64 * k : 64 * k + 64, :3072] = r[...]
+def stack_kernel(f0, f1, f2, f2b, f3, seconds, out):
+    for at, r in ((0, f0), (64, f1), (128, f2), (160, f2b), (192, f3)):
+        out[at : at + r.shape[0], :3072] = r[...]
     out[:, 3072:] = seconds[...]
 
 
@@ -347,23 +351,30 @@
     )
 
     packed = after(packed, gate2)
-    got = spread(packed, FIRST)
-    down2 = send(after(frozen_down_weight, packed), CORE)
+    got1, got3 = send(packed, FIRST[1]), send(packed, FIRST[3])
+    got = relay(got1, got3, FIRST, (16, CUT))
     seconds = (adapter_second_gate, adapter_second_up, adapter_first_down)
     (seconds,) = local(
         seconds_kernel, [((256, 256), bf16)], [a.T for a in after(seconds, packed)]
     )
-    block, factor = local(unpack_kernel, [((64, WIDTH), bf16), ((64, 3072), bf16)], got)
-
-    block, factor = after((block, factor), (up2, down2, seconds))
-    factors = spread(factor, SECOND)
+    block, factor = local(
+        unpack_kernel,
+        [((64, WIDTH), bf16), ((64, 3072), bf16)],
+        (packed, got1, *got, got3),
+    )
+
+    block, factor = after((block, factor), (up2, seconds))
+    near1, near3 = send(factor, SECOND[1]), send(factor, SECOND[3])
     rows1, rows3 = send(block, SECOND[1]), send(block, SECOND[3])
-    (factor,) = local(stack_kernel, [((256, 3072 + 256), bf16)], (*factors, seconds))
-    factor2 = send(factor, CORE)
-    to1, to3 = local(halves_kernel, [((32, WIDTH), bf16)] * 2, (rows3, rows1))
-    rows2 = (send(to1, SECOND[1]), send(to3, SECOND[3]))
     frozen = (frozen_gate_weight, frozen_up_weight, frozen_down_weight)
     owned = after(frozen, block)
+    down2 = send(owned[2], CORE)
+    far = relay(near1, near3, SECOND, (32, 3072))
+    (factor,) = local(
+        stack_kernel, [((256, 3072 + 256), bf16)], (factor, near1, *far, near3, seconds)
+    )
+    factor2 = send(factor, CORE)
+    rows2 = relay(rows1, rows3, SECOND, (32, WIDTH))
     (touched,) = local(touch_kernel, [((8, 128), f32)], in_vmem(owned))
 
     weights = (owned[0], gate2, owned[1], up2)

time: 125 us -> 127 us (1.016)
  waiting for transfers between devices: 53.2 us -> 56.5 us
  local copies, waits for them, and re-layouts: 6.44 us -> 4.41 us
    ppermute x28 -> x30, waiting for transfers between devices: 53.2 us -> 56.5 us  [send(): return lax.ppermute(value, AXES, route)]
    unnamed x16 -> x14, local copies, waits for them, and re-layouts: 6.36 us -> 4.32 us
    ppermute x28 -> x30, starting transfers between devices: 42.2 us -> 42.7 us  [send(): return lax.ppermute(value, AXES, route)]
    pallas_call x11 -> x13, Pallas kernels: 4.2 us -> 4 us  [local(): pl.pallas_call(body, in_specs=[SMEM] * len(lead) + [VMEM] * len(operands)...]
  transfers between devices with their start and end apart: 28 -> 30, of which waited for: 19 -> 19; matrix products, arithmetic and copies ran while one was open for 0% -> 0% of each run, Pallas kernels for 15% -> 15%
where the time goes in v8:
time: 127 us; the launch traced here: 126 us
  waiting for transfers between devices  56.5 us (44%)
  starting transfers between devices  42.7 us (34%)
  Pallas kernels  21.7 us (17%)
  local copies, waits for them, and re-layouts  4.41 us (3%)
    ppermute x30, waiting for transfers between devices, send(): return lax.ppermute(value, AXES, route)  56.5 us
    ppermute x30, starting transfers between devices, send(): return lax.ppermute(value, AXES, route)  42.7 us
    pallas_call x2, Pallas kernels, down(): pl.pallas_call(body, in_specs=[SMEM] * len(lead) + [VMEM] * len(operands)...  9.59 us
    pallas_call x2, Pallas kernels, project(): pl.pallas_call(lambda *refs: project_kernel(n, *refs[more:]), in_specs=[V...  8.14 us
    unnamed x14, local copies, waits for them, and re-layouts  4.32 us
    pallas_call x13, Pallas kernels, local(): pl.pallas_call(body, in_specs=[SMEM] * len(lead) + [VMEM] * len(operands)...  4 us
  transfers between devices with their start and end apart: 30, of which 19 were waited for; matrix products, arithmetic and copies ran while one was open for 0% of the time, Pallas kernels for 15%

profile of v8, /device:TPU:1, one launch (start us, length us, event | category | flops | bytes accessed | tf_op | source)
XLA Modules:
  0.0 126.3 jit_solution(3300739189500356798)
XLA Ops:
  0.1 1.4 %shard_map.100 = (bf16[8,2048]{1,0:T(8,128)(2,1)S(1)}, bf16[8,2048]{1,0:T(8,128)(2,1)S(1)}, bf16[16,1536]{1,0:T(8,128)(2,1)S(1)}) custom-call(s32[5]{0:T(128)S(1)} %stack.23.place.refs_0_, bf16[2,8,2048]{2,1,0:T(8,128)(2,1)} %inputs.1, bf16[64,256]{1,0:T(8,128)(2,1)} %gate.1, bf16[64,256]{1,0:T(8,128)(2,1)} %up.1, bf16[64,256]{1,0:T(8,128)(2,1)} %down.1), custom_call_target="tpu_custom_call" | custom-call | flops 1 | bytes 1 | tf_op jit(solution)/shard_map/pallas_call | solution.py:196
  1.5 1.5 %collective-permute-start = (bf16[8,2048]{1,0:T(8,128)(2,1)S(1)}, bf16[8,2048]{1,0:T(8,128)(2,1)S(1)}, u32[]{:S(2)}, u32[]{:S(2)}) collective-permute-start(bf16[8,2048]{1,0:T(8,128)(2,1)S(1)} %get-tuple-element.45), channel_id=1, source_target_pairs={{0,1},{1,0},{2,3},{3,2},{4,5},{5,4},{6,7},{7,6},{8,9},{9,8},{10,11... | collective-permute-start | bytes 98312 | tf_op jit(solution)/shard_map/ppermute | solution.py:51
  3.0 0.9 collective-permute-done.other
  5.0 3.8 %collective-permute-start.3 = (bf16[16,3584]{1,0:T(8,128)(2,1)S(1)}, bf16[16,3584]{1,0:T(8,128)(2,1)S(1)}, u32[]{:S(2)}, u32[]{:S(2)}) collective-permute-start(bf16[16,3584]{1,0:T(8,128)(2,1)S(1)} %get-tuple-element.48.message), channel_id=1, source_target_pairs={{0,66},{1,67},{2,64},{3,65},{4,70},{5,71},{6,68},{7,69},{8,74},{9,... | collective-permute-start | bytes 344072 | tf_op jit(solution)/shard_map/ppermute | solution.py:51
  8.8 1.2 collective-permute-start.2
  10.1 2.2 %collective-permute-done.1.z1 = bf16[8,4096]{1,0:T(8,128)(2,1)S(1)} collective-permute-done((bf16[8,4096]{1,0:T(8,128)(2,1)S(1)}, bf16[8,4096]{1,0:T(8,128)(2,1)S(1)}, u32[]{:S(2)}, u32[]{:S(2)}) %collective-permute-start.1) | collective-permute-done | bytes 65568 | tf_op jit(solution)/shard_map/ppermute | solution.py:51
  12.2 1.2 collective-permute-done.2.z2
  14.0 1.4 %collective-permute-start.5 = (bf16[16,11264]{1,0:T(8,128)(2,1)S(1)}, bf16[16,11264]{1,0:T(8,128)(2,1)S(1)}, u32[]{:S(2)}, u32[]{:S(2)}) collective-permute-start(bf16[16,11264]{1,0:T(8,128)(2,1)S(1)} %shard_map.102.own), channel_id=1, source_target_pairs={{0,4},{1,17},{2,6},{3,19},{4,0},{5,21},{6,2},{7,23},{8,12},{9,25},... | collective-permute-start | bytes 1081352 | tf_op jit(solution)/shard_map/ppermute | solution.py:51
  15.4 1.9 %collective-permute-start.6 = (bf16[16,11264]{1,0:T(8,128)(2,1)S(1)}, bf16[16,11264]{1,0:T(8,128)(2,1)S(1)}, u32[]{:S(2)}, u32[]{:S(2)}) collective-permute-start(bf16[16,11264]{1,0:T(8,128)(2,1)S(1)} %shard_map.102.own), channel_id=1, source_target_pairs={{0,12},{1,49},{2,14},{3,51},{4,8},{5,53},{6,10},{7,55},{8,4},{9,57... | collective-permute-start | bytes 1081352 | tf_op jit(solution)/shard_map/ppermute | solution.py:51
  17.3 3.4 %collective-permute-done.5.from1.got1 = bf16[16,11264]{1,0:T(8,128)(2,1)S(1)} collective-permute-done((bf16[16,11264]{1,0:T(8,128)(2,1)S(1)}, bf16[16,11264]{1,0:T(8,128)(2,1)S(1)}, u32[]{:S(2)}, u32[]{:S(2)}) %collective-permute-start.5) | collective-permute-done | bytes 360480 | tf_op jit(solution)/shard_map/ppermute | solution.py:51
  20.7 2.5 %collective-permute-done.6.from3.got3 = bf16[16,11264]{1,0:T(8,128)(2,1)S(1)} collective-permute-done((bf16[16,11264]{1,0:T(8,128)(2,1)S(1)}, bf16[16,11264]{1,0:T(8,128)(2,1)S(1)}, u32[]{:S(2)}, u32[]{:S(2)}) %collective-permute-start.6) | collective-permute-done | bytes 360480 | tf_op jit(solution)/shard_map/ppermute | solution.py:51
  23.3 2.0 %collective-permute-start.8 = (bf16[16,5632]{1,0:T(8,128)(2,1)S(1)}, bf16[16,5632]{1,0:T(8,128)(2,1)S(1)}, u32[]{:S(2)}, u32[]{:S(2)}) collective-permute-start(bf16[16,5632]{1,0:T(8,128)(2,1)S(1)} %get-tuple-element.52), channel_id=1, source_target_pairs={{0,12},{1,49},{2,14},{3,51},{4,8},{5,53},{6,10},{7,55},{8,4},{9,57... | collective-permute-start | bytes 540680 | tf_op jit(solution)/shard_map/ppermute | solution.py:51
  25.3 0.8 copy-done.4
  26.1 0.8 copy-done.5
  26.8 0.8 copy-done.6
  27.7 1.3 %collective-permute-done.8.right = bf16[16,5632]{1,0:T(8,128)(2,1)S(1)} collective-permute-done((bf16[16,5632]{1,0:T(8,128)(2,1)S(1)}, bf16[16,5632]{1,0:T(8,128)(2,1)S(1)}, u32[]{:S(2)}, u32[]{:S(2)}) %collective-permute-start.8) | collective-permute-done | bytes 180256 | tf_op jit(solution)/shard_map/ppermute | solution.py:51
  29.1 4.1 %collective-permute-start.12 = (bf16[224,8192]{1,0:T(8,128)(2,1)}, bf16[224,8192]{1,0:T(8,128)(2,1)S(1)}, u32[]{:S(2)}, u32[]{:S(2)}) collective-permute-start(bf16[224,8192]{1,0:T(8,128)(2,1)} %refs_3_), channel_id=1, source_target_pairs={{0,1},{1,0},{2,3},{3,2},{4,5},{5,4},{6,7},{7,6},{8,9},{9,8},{10,11... | collective-permute-start | bytes 11010056 | tf_op jit(solution)/shard_map/ppermute | solution.py:51
  33.6 1.8 %collective-permute-start.14 = (bf16[64,3072]{1,0:T(8,128)(2,1)S(1)}, bf16[64,3072]{1,0:T(8,128)(2,1)S(1)}, u32[]{:S(2)}, u32[]{:S(2)}) collective-permute-start(bf16[64,3072]{1,0:T(8,128)(2,1)S(1)} %get-tuple-element.63.f0), channel_id=1, source_target_pairs={{0,48},{1,13},{2,50},{3,15},{4,52},{5,9},{6,54},{7,11},{8,56},{9,5... | collective-permute-start | bytes 1179656 | tf_op jit(solution)/shard_map/ppermute | solution.py:51
  35.8 0.9 collective-permute-start.11
  36.7 3.4 %collective-permute-done.13.from1.f1 = bf16[64,3072]{1,0:T(8,128)(2,1)S(1)} collective-permute-done((bf16[64,3072]{1,0:T(8,128)(2,1)S(1)}, bf16[64,3072]{1,0:T(8,128)(2,1)S(1)}, u32[]{:S(2)}, u32[]{:S(2)}) %collective-permute-start.13) | collective-permute-done | bytes 393248 | tf_op jit(solution)/shard_map/ppermute | solution.py:51
  40.0 1.7 %collective-permute-done.14.from3.f3 = bf16[64,3072]{1,0:T(8,128)(2,1)S(1)} collective-permute-done((bf16[64,3072]{1,0:T(8,128)(2,1)S(1)}, bf16[64,3072]{1,0:T(8,128)(2,1)S(1)}, u32[]{:S(2)}, u32[]{:S(2)}) %collective-permute-start.14) | collective-permute-done | bytes 393248 | tf_op jit(solution)/shard_map/ppermute | solution.py:51
  41.8 1.9 %collective-permute-start.16 = (bf16[32,3072]{1,0:T(8,128)(2,1)S(1)}, bf16[32,3072]{1,0:T(8,128)(2,1)S(1)}, u32[]{:S(2)}, u32[]{:S(2)}) collective-permute-start(bf16[32,3072]{1,0:T(8,128)(2,1)S(1)} %get-tuple-element.65), channel_id=1, source_target_pairs={{0,48},{1,13},{2,50},{3,15},{4,52},{5,9},{6,54},{7,11},{8,56},{9,5... | collective-permute-start | bytes 589832 | tf_op jit(solution)/shard_map/ppermute | solution.py:51
  43.7 9.7 %collective-permute-done.15.f2 = bf16[32,3072]{1,0:T(8,128)(2,1)S(1)} collective-permute-done((bf16[32,3072]{1,0:T(8,128)(2,1)S(1)}, bf16[32,3072]{1,0:T(8,128)(2,1)S(1)}, u32[]{:S(2)}, u32[]{:S(2)}) %collective-permute-start.15) | collective-permute-done | bytes 196640 | tf_op jit(solution)/shard_map/ppermute | solution.py:51
  53.4 1.7 %collective-permute-done.16.f2b = bf16[32,3072]{1,0:T(8,128)(2,1)S(1)} collective-permute-done((bf16[32,3072]{1,0:T(8,128)(2,1)S(1)}, bf16[32,3072]{1,0:T(8,128)(2,1)S(1)}, u32[]{:S(2)}, u32[]{:S(2)}) %collective-permute-start.16) | collective-permute-done | bytes 196640 | tf_op jit(solution)/shard_map/ppermute | solution.py:51
  55.2 2.2 %collective-permute-start.17 = (bf16[256,3328]{1,0:T(8,128)(2,1)S(1)}, bf16[256,3328]{1,0:T(8,128)(2,1)S(1)}, u32[]{:S(2)}, u32[]{:S(2)}) collective-permute-start(bf16[256,3328]{1,0:T(8,128)(2,1)S(1)} %shard_map.109.refs_9_), channel_id=1, source_target_pairs={{0,1},{1,0},{2,3},{3,2},{4,5},{5,4},{6,7},{7,6},{8,9},{9,8},{10,11... | collective-permute-start | bytes 5111816 | tf_op jit(solution)/shard_map/ppermute | solution.py:51
  57.3 2.0 %copy-done.2 = bf16[224,8192]{1,0:T(8,128)(2,1)S(1)} copy-done((bf16[224,8192]{1,0:T(8,128)(2,1)S(1)}, bf16[224,8192]{1,0:T(8,128)(2,1)}, u32[]{:S(2)}) %copy-start.2) | copy-done | bytes 3670040
  60.0 1.8 %collective-permute-start.21 = (bf16[32,8192]{1,0:T(8,128)(2,1)S(1)}, bf16[32,8192]{1,0:T(8,128)(2,1)S(1)}, u32[]{:S(2)}, u32[]{:S(2)}) collective-permute-start(bf16[32,8192]{1,0:T(8,128)(2,1)S(1)} %get-tuple-element.70), channel_id=1, source_target_pairs={{0,48},{1,13},{2,50},{3,15},{4,52},{5,9},{6,54},{7,11},{8,56},{9,5... | collective-permute-start | bytes 1572872 | tf_op jit(solution)/shard_map/ppermute | solution.py:51
  61.8 4.1 %shard_map.107.refs_4_ = f32[896,192]{1,0:T(8,128)S(1)} custom-call(f32[8,128]{1,0:T(8,128)S(1)} %shard_map.106.refs_0_, bf16[64,8192]{1,0:T(8,128)(2,1)S(1)} %get-tuple-element.59.refs_1_, bf16[64,8192]{1,0:T(8,128)(2,1)S(1)} %collective-permute-done.10.refs_2_.from1, bf16[64,8192]{1,0:T(8,128)(2,1)S(1)} %collective-permute-done.11.refs_3_.from3, ...), custom_call_target="tpu_custom_call" | custom-call | flops 9200000000 | bytes 28800000 | tf_op jit(solution)/shard_map/pallas_call | solution.py:161
  65.9 6.0 %shard_map.110 = (f32[64,8192]{1,0:T(8,128)S(1)}, bf16[64,8192]{1,0:T(8,128)(2,1)S(1)}, bf16[64,8192]{1,0:T(8,128)(2,1)S(1)}, bf16[128,8192]{1,0:T(8,128)(2,1)S(1)}, bf16[64,8192]{1,0:T(8,128)(2,1)S(1)}) custom-call(s32[5]{0:T(128)S(1)} %stack.23.place.refs_0_, bf16[64,8192]{1,0:T(8,128)(2,1)S(1)} %get-tuple-element.59.refs_1_, ...), custom_call_target="tpu_custom_call" | custom-call | flops 1 | bytes 1 | tf_op jit(solution)/shard_map/pallas_call | solution.py:183
  72.4 1.4 %collective-permute-start.19 = (bf16[64,8192]{1,0:T(8,128)(2,1)S(1)}, bf16[64,8192]{1,0:T(8,128)(2,1)S(1)}, u32[]{:S(2)}, u32[]{:S(2)}) collective-permute-start(bf16[64,8192]{1,0:T(8,128)(2,1)S(1)} %get-tuple-element.68), channel_id=1, source_target_pairs={{0,48},{1,13},{2,50},{3,15},{4,52},{5,9},{6,54},{7,11},{8,56},{9,5... | collective-permute-start | bytes 3145736 | tf_op jit(solution)/shard_map/ppermute | solution.py:51
  73.9 4.1 %shard_map.113.refs_2_ = f32[896,64]{1,0:T(8,128)S(1)} custom-call(bf16[32,8192]{1,0:T(8,128)(2,1)S(1)} %collective-permute-done.20.refs_0_, bf16[32,8192]{1,0:T(8,128)(2,1)S(1)} %collective-permute-done.21.refs_1_, bf16[224,8192]{1,0:T(8,128)(2,1)S(1)} %copy-done.1, bf16[224,8192]{1,0:T(8,128)(2,1)S(1)} %collective-permute-done.4.refs_5_.refs_3_, ...), custom_call_target="tpu_custom_call" | custom-call | flops 9200000000 | bytes 28800000 | tf_op jit(solution)/shard_map/pallas_call | solution.py:161
  78.0 3.6 %shard_map.114 = bf16[64,8192]{1,0:T(8,128)(2,1)S(1)} custom-call(bf16[32,8192]{1,0:T(8,128)(2,1)S(1)} %collective-permute-done.20.refs_0_, bf16[32,8192]{1,0:T(8,128)(2,1)S(1)} %collective-permute-done.21.refs_1_, f32[896,64]{1,0:T(8,128)S(1)} %shard_map.113.refs_2_, bf16[224,8192]{1,0:T(8,128)(2,1)S(1)} %copy-done, ...), custom_call_target="tpu_custom_call" | custom-call | flops 1 | bytes 1 | tf_op jit(solution)/shard_map/pallas_call | solution.py:183
  81.5 1.4 %collective-permute-start.22 = (bf16[64,8192]{1,0:T(8,128)(2,1)S(1)}, bf16[64,8192]{1,0:T(8,128)(2,1)S(1)}, u32[]{:S(2)}, u32[]{:S(2)}) collective-permute-start(bf16[64,8192]{1,0:T(8,128)(2,1)S(1)} %shard_map.114), channel_id=1, source_target_pairs={{0,32},{1,9},{2,34},{3,11},{4,36},{5,13},{6,38},{7,15},{8,40},{9,1... | collective-permute-start | bytes 3145736 | tf_op jit(solution)/shard_map/ppermute | solution.py:51
  83.0 3.0 %collective-permute-done.18.b1 = bf16[64,8192]{1,0:T(8,128)(2,1)S(1)} collective-permute-done((bf16[64,8192]{1,0:T(8,128)(2,1)S(1)}, bf16[64,8192]{1,0:T(8,128)(2,1)S(1)}, u32[]{:S(2)}, u32[]{:S(2)}) %collective-permute-start.18) | collective-permute-done | bytes 1048608 | tf_op jit(solution)/shard_map/ppermute | solution.py:51
  86.0 12.9 %collective-permute-done.19.b3 = bf16[64,8192]{1,0:T(8,128)(2,1)S(1)} collective-permute-done((bf16[64,8192]{1,0:T(8,128)(2,1)S(1)}, bf16[64,8192]{1,0:T(8,128)(2,1)S(1)}, u32[]{:S(2)}, u32[]{:S(2)}) %collective-permute-start.19) | collective-permute-done | bytes 1048608 | tf_op jit(solution)/shard_map/ppermute | solution.py:51
  99.4 3.1 %collective-permute-start.24 = (bf16[16,8192]{1,0:T(8,128)(2,1)S(1)}, bf16[16,8192]{1,0:T(8,128)(2,1)S(1)}, u32[]{:S(2)}, u32[]{:S(2)}) collective-permute-start(bf16[16,8192]{1,0:T(8,128)(2,1)S(1)} %get-tuple-element.77), channel_id=1, source_target_pairs={{0,8},{1,33},{2,10},{3,35},{4,12},{5,37},{6,14},{7,39},{8,0},{9,41... | collective-permute-start | bytes 786440 | tf_op jit(solution)/shard_map/ppermute | solution.py:51
  102.5 0.8 collective-permute-start.25
  103.3 1.7 %collective-permute-done.23.b1 = bf16[16,8192]{1,0:T(8,128)(2,1)S(1)} collective-permute-done((bf16[16,8192]{1,0:T(8,128)(2,1)S(1)}, bf16[16,8192]{1,0:T(8,128)(2,1)S(1)}, u32[]{:S(2)}, u32[]{:S(2)}) %collective-permute-start.23) | collective-permute-done | bytes 262176 | tf_op jit(solution)/shard_map/ppermute | solution.py:51
  104.9 4.5 %collective-permute-done.24.b2 = bf16[16,8192]{1,0:T(8,128)(2,1)S(1)} collective-permute-done((bf16[16,8192]{1,0:T(8,128)(2,1)S(1)}, bf16[16,8192]{1,0:T(8,128)(2,1)S(1)}, u32[]{:S(2)}, u32[]{:S(2)}) %collective-permute-start.24) | collective-permute-done | bytes 262176 | tf_op jit(solution)/shard_map/ppermute | solution.py:51
  109.4 2.6 %collective-permute-done.25.b3 = bf16[16,8192]{1,0:T(8,128)(2,1)S(1)} collective-permute-done((bf16[16,8192]{1,0:T(8,128)(2,1)S(1)}, bf16[16,8192]{1,0:T(8,128)(2,1)S(1)}, u32[]{:S(2)}, u32[]{:S(2)}) %collective-permute-start.25) | collective-permute-done | bytes 262176 | tf_op jit(solution)/shard_map/ppermute | solution.py:51
  112.0 0.7 shard_map.116
  112.7 1.8 %collective-permute-start.26 = (bf16[8,4096]{1,0:T(8,128)(2,1)S(1)}, bf16[8,4096]{1,0:T(8,128)(2,1)S(1)}, u32[]{:S(2)}, u32[]{:S(2)}) collective-permute-start(bf16[8,4096]{1,0:T(8,128)(2,1)S(1)} %get-tuple-element.80), channel_id=1, source_target_pairs={{0,2},{1,3},{2,0},{3,1},{4,6},{5,7},{6,4},{7,5},{8,10},{9,11},{10,... | collective-permute-start | bytes 196616 | tf_op jit(solution)/shard_map/ppermute | solution.py:51
  114.5 1.3 %collective-permute-start.27 = (bf16[8,4096]{1,0:T(8,128)(2,1)S(1)}, bf16[8,4096]{1,0:T(8,128)(2,1)S(1)}, u32[]{:S(2)}, u32[]{:S(2)}) collective-permute-start(bf16[8,4096]{1,0:T(8,128)(2,1)S(1)} %get-tuple-element.81), channel_id=1, source_target_pairs={{0,64},{1,65},{2,66},{3,67},{4,68},{5,69},{6,70},{7,71},{8,72},{9,... | collective-permute-start | bytes 196616 | tf_op jit(solution)/shard_map/ppermute | solution.py:51
  115.9 1.1 collective-permute-start.28
  117.0 2.1 %collective-permute-done.27 = bf16[8,4096]{1,0:T(8,128)(2,1)S(1)} collective-permute-done((bf16[8,4096]{1,0:T(8,128)(2,1)S(1)}, bf16[8,4096]{1,0:T(8,128)(2,1)S(1)}, u32[]{:S(2)}, u32[]{:S(2)}) %collective-permute-start.27) | collective-permute-done | bytes 65568 | tf_op jit(solution)/shard_map/ppermute | solution.py:51
  119.2 1.0 collective-permute-done.28
  120.3 4.5 %collective-permute-start.29 = (bf16[8,2048]{1,0:T(8,128)(2,1)S(1)}, bf16[8,2048]{1,0:T(8,128)(2,1)S(1)}, u32[]{:S(2)}, u32[]{:S(2)}) collective-permute-start(bf16[8,2048]{1,0:T(8,128)(2,1)S(1)} %get-tuple-element.84), channel_id=1, source_target_pairs={{0,1},{1,0},{2,3},{3,2},{4,5},{5,4},{6,7},{7,6},{8,9},{9,8},{10,11... | collective-permute-start | bytes 98312 | tf_op jit(solution)/shard_map/ppermute | solution.py:51
  124.8 0.9 collective-permute-done.29
  (47 shorter events, 5.6 us)
Async XLA Ops:
  1.5 2.4 %collective-permute-start = (bf16[8,2048]{1,0:T(8,128)(2,1)S(1)}, bf16[8,2048]{1,0:T(8,128)(2,1)S(1)}, u32[]{:S(2)}, u32[]{:S(2)}) collective-permute-start(bf16[8,2048]{1,0:T(8,128)(2,1)S(1)} %get-tuple-element.45), channel_id=1, source_target_pairs={{0,1},{1,0},{2,3},{3,2},{4,5},{5,4},{6,7},{7,6},{8,9},{9,8},{10,11... | collective-permute-start | bytes 98312 | tf_op jit(solution)/shard_map/ppermute | solution.py:51
  4.4 9.6 %collective-permute-start.4 = (bf16[224,8192]{1,0:T(8,128)(2,1)}, bf16[224,8192]{1,0:T(8,128)(2,1)S(1)}, u32[]{:S(2)}, u32[]{:S(2)}) collective-permute-start(bf16[224,8192]{1,0:T(8,128)(2,1)} %refs_2_), channel_id=1, source_target_pairs={{0,1},{1,0},{2,3},{3,2},{4,5},{5,4},{6,7},{7,6},{8,9},{9,8},{10,11... | collective-permute-start | bytes 11010056 | tf_op jit(solution)/shard_map/ppermute | solution.py:51
  4.8 24.2 %collective-permute-start.9 = (bf16[224,8192]{1,0:T(8,128)(2,1)}, bf16[224,8192]{1,0:T(8,128)(2,1)S(1)}, u32[]{:S(2)}, u32[]{:S(2)}) collective-permute-start(bf16[224,8192]{1,0:T(8,128)(2,1)} %refs_4_.1), channel_id=1, source_target_pairs={{0,1},{1,0},{2,3},{3,2},{4,5},{5,4},{6,7},{7,6},{8,9},{9,8},{10,11... | collective-permute-start | bytes 11010056 | tf_op jit(solution)/shard_map/ppermute | solution.py:51
  5.0 52.3 %copy-start = (bf16[224,8192]{1,0:T(8,128)(2,1)S(1)}, bf16[224,8192]{1,0:T(8,128)(2,1)}, u32[]{:S(2)}) copy-start(bf16[224,8192]{1,0:T(8,128)(2,1)} %refs_3_) | copy-start | bytes 11010052
  5.0 52.3 %copy-start.1 = (bf16[224,8192]{1,0:T(8,128)(2,1)S(1)}, bf16[224,8192]{1,0:T(8,128)(2,1)}, u32[]{:S(2)}) copy-start(bf16[224,8192]{1,0:T(8,128)(2,1)} %refs_2_) | copy-start | bytes 11010052
  5.0 8.5 %collective-permute-start.3 = (bf16[16,3584]{1,0:T(8,128)(2,1)S(1)}, bf16[16,3584]{1,0:T(8,128)(2,1)S(1)}, u32[]{:S(2)}, u32[]{:S(2)}) collective-permute-start(bf16[16,3584]{1,0:T(8,128)(2,1)S(1)} %get-tuple-element.48.message), channel_id=1, source_target_pairs={{0,66},{1,67},{2,64},{3,65},{4,70},{5,71},{6,68},{7,69},{8,74},{9,... | collective-permute-start | bytes 344072 | tf_op jit(solution)/shard_map/ppermute | solution.py:51
  8.8 3.4 %collective-permute-start.1 = (bf16[8,4096]{1,0:T(8,128)(2,1)S(1)}, bf16[8,4096]{1,0:T(8,128)(2,1)S(1)}, u32[]{:S(2)}, u32[]{:S(2)}) collective-permute-start(bf16[8,4096]{1,0:T(8,128)(2,1)S(1)} %get-tuple-element.47.wide), channel_id=1, source_target_pairs={{0,2},{1,3},{2,0},{3,1},{4,6},{5,7},{6,4},{7,5},{8,10},{9,11},{10,... | collective-permute-start | bytes 196616 | tf_op jit(solution)/shard_map/ppermute | solution.py:51
  8.8 4.6 %collective-permute-start.2 = (bf16[8,4096]{1,0:T(8,128)(2,1)S(1)}, bf16[8,4096]{1,0:T(8,128)(2,1)S(1)}, u32[]{:S(2)}, u32[]{:S(2)}) collective-permute-start(bf16[8,4096]{1,0:T(8,128)(2,1)S(1)} %get-tuple-element.47.wide), channel_id=1, source_target_pairs={{0,64},{1,65},{2,66},{3,67},{4,68},{5,69},{6,70},{7,71},{8,72},{9,... | collective-permute-start | bytes 196616 | tf_op jit(solution)/shard_map/ppermute | solution.py:51
  14.0 6.7 %collective-permute-start.5 = (bf16[16,11264]{1,0:T(8,128)(2,1)S(1)}, bf16[16,11264]{1,0:T(8,128)(2,1)S(1)}, u32[]{:S(2)}, u32[]{:S(2)}) collective-permute-start(bf16[16,11264]{1,0:T(8,128)(2,1)S(1)} %shard_map.102.own), channel_id=1, source_target_pairs={{0,4},{1,17},{2,6},{3,19},{4,0},{5,21},{6,2},{7,23},{8,12},{9,25},... | collective-permute-start | bytes 1081352 | tf_op jit(solution)/shard_map/ppermute | solution.py:51
  15.4 7.8 %collective-permute-start.6 = (bf16[16,11264]{1,0:T(8,128)(2,1)S(1)}, bf16[16,11264]{1,0:T(8,128)(2,1)S(1)}, u32[]{:S(2)}, u32[]{:S(2)}) collective-permute-start(bf16[16,11264]{1,0:T(8,128)(2,1)S(1)} %shard_map.102.own), channel_id=1, source_target_pairs={{0,12},{1,49},{2,14},{3,51},{4,8},{5,53},{6,10},{7,55},{8,4},{9,57... | collective-permute-start | bytes 1081352 | tf_op jit(solution)/shard_map/ppermute | solution.py:51
  23.2 4.4 %collective-permute-start.7 = (bf16[16,5632]{1,0:T(8,128)(2,1)S(1)}, bf16[16,5632]{1,0:T(8,128)(2,1)S(1)}, u32[]{:S(2)}, u32[]{:S(2)}) collective-permute-start(bf16[16,5632]{1,0:T(8,128)(2,1)S(1)} %get-tuple-element.51), channel_id=1, source_target_pairs={{0,4},{1,17},{2,6},{3,19},{4,0},{5,21},{6,2},{7,23},{8,12},{9,25},... | collective-permute-start | bytes 540680 | tf_op jit(solution)/shard_map/ppermute | solution.py:51
  23.3 5.6 %collective-permute-start.8 = (bf16[16,5632]{1,0:T(8,128)(2,1)S(1)}, bf16[16,5632]{1,0:T(8,128)(2,1)S(1)}, u32[]{:S(2)}, u32[]{:S(2)}) collective-permute-start(bf16[16,5632]{1,0:T(8,128)(2,1)S(1)} %get-tuple-element.52), channel_id=1, source_target_pairs={{0,12},{1,49},{2,14},{3,51},{4,8},{5,53},{6,10},{7,55},{8,4},{9,57... | collective-permute-start | bytes 540680 | tf_op jit(solution)/shard_map/ppermute | solution.py:51
  25.3 0.8 copy-start.4
  26.1 0.8 copy-start.5
  26.8 0.8 copy-start.6
  29.1 36.8 %collective-permute-start.12 = (bf16[224,8192]{1,0:T(8,128)(2,1)}, bf16[224,8192]{1,0:T(8,128)(2,1)S(1)}, u32[]{:S(2)}, u32[]{:S(2)}) collective-permute-start(bf16[224,8192]{1,0:T(8,128)(2,1)} %refs_3_), channel_id=1, source_target_pairs={{0,1},{1,0},{2,3},{3,2},{4,5},{5,4},{6,7},{7,6},{8,9},{9,8},{10,11... | collective-permute-start | bytes 11010056 | tf_op jit(solution)/shard_map/ppermute | solution.py:51
  33.1 6.9 %collective-permute-start.13 = (bf16[64,3072]{1,0:T(8,128)(2,1)S(1)}, bf16[64,3072]{1,0:T(8,128)(2,1)S(1)}, u32[]{:S(2)}, u32[]{:S(2)}) collective-permute-start(bf16[64,3072]{1,0:T(8,128)(2,1)S(1)} %get-tuple-element.63.f0), channel_id=1, source_target_pairs={{0,16},{1,5},{2,18},{3,7},{4,20},{5,1},{6,22},{7,3},{8,24},{9,13},... | collective-permute-start | bytes 1179656 | tf_op jit(solution)/shard_map/ppermute | solution.py:51
  33.6 8.1 %collective-permute-start.14 = (bf16[64,3072]{1,0:T(8,128)(2,1)S(1)}, bf16[64,3072]{1,0:T(8,128)(2,1)S(1)}, u32[]{:S(2)}, u32[]{:S(2)}) collective-permute-start(bf16[64,3072]{1,0:T(8,128)(2,1)S(1)} %get-tuple-element.63.f0), channel_id=1, source_target_pairs={{0,48},{1,13},{2,50},{3,15},{4,52},{5,9},{6,54},{7,11},{8,56},{9,5... | collective-permute-start | bytes 1179656 | tf_op jit(solution)/shard_map/ppermute | solution.py:51
  35.4 24.0 %collective-permute-start.10 = (bf16[64,8192]{1,0:T(8,128)(2,1)S(1)}, bf16[64,8192]{1,0:T(8,128)(2,1)S(1)}, u32[]{:S(2)}, u32[]{:S(2)}) collective-permute-start(bf16[64,8192]{1,0:T(8,128)(2,1)S(1)} %get-tuple-element.59.refs_1_), channel_id=1, source_target_pairs={{0,16},{1,5},{2,18},{3,7},{4,20},{5,1},{6,22},{7,3},{8,24},{9,13},... | collective-permute-start | bytes 3145736 | tf_op jit(solution)/shard_map/ppermute | solution.py:51
  35.8 23.6 %collective-permute-start.11 = (bf16[64,8192]{1,0:T(8,128)(2,1)S(1)}, bf16[64,8192]{1,0:T(8,128)(2,1)S(1)}, u32[]{:S(2)}, u32[]{:S(2)}) collective-permute-start(bf16[64,8192]{1,0:T(8,128)(2,1)S(1)} %get-tuple-element.59.refs_1_), channel_id=1, source_target_pairs={{0,48},{1,13},{2,50},{3,15},{4,52},{5,9},{6,54},{7,11},{8,56},{9,5... | collective-permute-start | bytes 3145736 | tf_op jit(solution)/shard_map/ppermute | solution.py:51
  41.7 11.7 %collective-permute-start.15 = (bf16[32,3072]{1,0:T(8,128)(2,1)S(1)}, bf16[32,3072]{1,0:T(8,128)(2,1)S(1)}, u32[]{:S(2)}, u32[]{:S(2)}) collective-permute-start(bf16[32,3072]{1,0:T(8,128)(2,1)S(1)} %get-tuple-element.64), channel_id=1, source_target_pairs={{0,16},{1,5},{2,18},{3,7},{4,20},{5,1},{6,22},{7,3},{8,24},{9,13},... | collective-permute-start | bytes 589832 | tf_op jit(solution)/shard_map/ppermute | solution.py:51
  41.8 13.2 %collective-permute-start.16 = (bf16[32,3072]{1,0:T(8,128)(2,1)S(1)}, bf16[32,3072]{1,0:T(8,128)(2,1)S(1)}, u32[]{:S(2)}, u32[]{:S(2)}) collective-permute-start(bf16[32,3072]{1,0:T(8,128)(2,1)S(1)} %get-tuple-element.65), channel_id=1, source_target_pairs={{0,48},{1,13},{2,50},{3,15},{4,52},{5,9},{6,54},{7,11},{8,56},{9,5... | collective-permute-start | bytes 589832 | tf_op jit(solution)/shard_map/ppermute | solution.py:51
  55.2 10.7 %collective-permute-start.17 = (bf16[256,3328]{1,0:T(8,128)(2,1)S(1)}, bf16[256,3328]{1,0:T(8,128)(2,1)S(1)}, u32[]{:S(2)}, u32[]{:S(2)}) collective-permute-start(bf16[256,3328]{1,0:T(8,128)(2,1)S(1)} %shard_map.109.refs_9_), channel_id=1, source_target_pairs={{0,1},{1,0},{2,3},{3,2},{4,5},{5,4},{6,7},{7,6},{8,9},{9,8},{10,11... | collective-permute-start | bytes 5111816 | tf_op jit(solution)/shard_map/ppermute | solution.py:51
  57.3 2.0 %copy-start.2 = (bf16[224,8192]{1,0:T(8,128)(2,1)S(1)}, bf16[224,8192]{1,0:T(8,128)(2,1)}, u32[]{:S(2)}) copy-start(bf16[224,8192]{1,0:T(8,128)(2,1)} %refs_4_.1) | copy-start | bytes 11010052
  59.4 2.4 %copy-start.3 = (bf16[224,8192]{1,0:T(8,128)(2,1)S(1)}, bf16[224,8192]{1,0:T(8,128)(2,1)}, u32[]{:S(2)}) copy-start(bf16[224,8192]{1,0:T(8,128)(2,1)} %refs_4_.1) | copy-start | bytes 11010052
  59.5 13.0 %collective-permute-start.20 = (bf16[32,8192]{1,0:T(8,128)(2,1)S(1)}, bf16[32,8192]{1,0:T(8,128)(2,1)S(1)}, u32[]{:S(2)}, u32[]{:S(2)}) collective-permute-start(bf16[32,8192]{1,0:T(8,128)(2,1)S(1)} %get-tuple-element.69), channel_id=1, source_target_pairs={{0,16},{1,5},{2,18},{3,7},{4,20},{5,1},{6,22},{7,3},{8,24},{9,13},... | collective-permute-start | bytes 1572872 | tf_op jit(solution)/shard_map/ppermute | solution.py:51
  60.0 12.5 %collective-permute-start.21 = (bf16[32,8192]{1,0:T(8,128)(2,1)S(1)}, bf16[32,8192]{1,0:T(8,128)(2,1)S(1)}, u32[]{:S(2)}, u32[]{:S(2)}) collective-permute-start(bf16[32,8192]{1,0:T(8,128)(2,1)S(1)} %get-tuple-element.70), channel_id=1, source_target_pairs={{0,48},{1,13},{2,50},{3,15},{4,52},{5,9},{6,54},{7,11},{8,56},{9,5... | collective-permute-start | bytes 1572872 | tf_op jit(solution)/shard_map/ppermute | solution.py:51
  71.9 14.0 %collective-permute-start.18 = (bf16[64,8192]{1,0:T(8,128)(2,1)S(1)}, bf16[64,8192]{1,0:T(8,128)(2,1)S(1)}, u32[]{:S(2)}, u32[]{:S(2)}) collective-permute-start(bf16[64,8192]{1,0:T(8,128)(2,1)S(1)} %get-tuple-element.67), channel_id=1, source_target_pairs={{0,16},{1,5},{2,18},{3,7},{4,20},{5,1},{6,22},{7,3},{8,24},{9,13},... | collective-permute-start | bytes 3145736 | tf_op jit(solution)/shard_map/ppermute | solution.py:51
  72.4 26.4 %collective-permute-start.19 = (bf16[64,8192]{1,0:T(8,128)(2,1)S(1)}, bf16[64,8192]{1,0:T(8,128)(2,1)S(1)}, u32[]{:S(2)}, u32[]{:S(2)}) collective-permute-start(bf16[64,8192]{1,0:T(8,128)(2,1)S(1)} %get-tuple-element.68), channel_id=1, source_target_pairs={{0,48},{1,13},{2,50},{3,15},{4,52},{5,9},{6,54},{7,11},{8,56},{9,5... | collective-permute-start | bytes 3145736 | tf_op jit(solution)/shard_map/ppermute | solution.py:51
  81.5 17.6 %collective-permute-start.22 = (bf16[64,8192]{1,0:T(8,128)(2,1)S(1)}, bf16[64,8192]{1,0:T(8,128)(2,1)S(1)}, u32[]{:S(2)}, u32[]{:S(2)}) collective-permute-start(bf16[64,8192]{1,0:T(8,128)(2,1)S(1)} %shard_map.114), channel_id=1, source_target_pairs={{0,32},{1,9},{2,34},{3,11},{4,36},{5,13},{6,38},{7,15},{8,40},{9,1... | collective-permute-start | bytes 3145736 | tf_op jit(solution)/shard_map/ppermute | solution.py:51
  99.3 5.6 %collective-permute-start.23 = (bf16[16,8192]{1,0:T(8,128)(2,1)S(1)}, bf16[16,8192]{1,0:T(8,128)(2,1)S(1)}, u32[]{:S(2)}, u32[]{:S(2)}) collective-permute-start(bf16[16,8192]{1,0:T(8,128)(2,1)S(1)} %get-tuple-element.76), channel_id=1, source_target_pairs={{0,4},{1,17},{2,6},{3,19},{4,0},{5,21},{6,2},{7,23},{8,12},{9,25},... | collective-permute-start | bytes 786440 | tf_op jit(solution)/shard_map/ppermute | solution.py:51
  99.4 10.0 %collective-permute-start.24 = (bf16[16,8192]{1,0:T(8,128)(2,1)S(1)}, bf16[16,8192]{1,0:T(8,128)(2,1)S(1)}, u32[]{:S(2)}, u32[]{:S(2)}) collective-permute-start(bf16[16,8192]{1,0:T(8,128)(2,1)S(1)} %get-tuple-element.77), channel_id=1, source_target_pairs={{0,8},{1,33},{2,10},{3,35},{4,12},{5,37},{6,14},{7,39},{8,0},{9,41... | collective-permute-start | bytes 786440 | tf_op jit(solution)/shard_map/ppermute | solution.py:51
  102.5 9.5 %collective-permute-start.25 = (bf16[16,8192]{1,0:T(8,128)(2,1)S(1)}, bf16[16,8192]{1,0:T(8,128)(2,1)S(1)}, u32[]{:S(2)}, u32[]{:S(2)}) collective-permute-start(bf16[16,8192]{1,0:T(8,128)(2,1)S(1)} %get-tuple-element.78), channel_id=1, source_target_pairs={{0,12},{1,49},{2,14},{3,51},{4,8},{5,53},{6,10},{7,55},{8,4},{9,57... | collective-permute-start | bytes 786440 | tf_op jit(solution)/shard_map/ppermute | solution.py:51
  112.7 4.3 %collective-permute-start.26 = (bf16[8,4096]{1,0:T(8,128)(2,1)S(1)}, bf16[8,4096]{1,0:T(8,128)(2,1)S(1)}, u32[]{:S(2)}, u32[]{:S(2)}) collective-permute-start(bf16[8,4096]{1,0:T(8,128)(2,1)S(1)} %get-tuple-element.80), channel_id=1, source_target_pairs={{0,2},{1,3},{2,0},{3,1},{4,6},{5,7},{6,4},{7,5},{8,10},{9,11},{10,... | collective-permute-start | bytes 196616 | tf_op jit(solution)/shard_map/ppermute | solution.py:51
  114.5 4.6 %collective-permute-start.27 = (bf16[8,4096]{1,0:T(8,128)(2,1)S(1)}, bf16[8,4096]{1,0:T(8,128)(2,1)S(1)}, u32[]{:S(2)}, u32[]{:S(2)}) collective-permute-start(bf16[8,4096]{1,0:T(8,128)(2,1)S(1)} %get-tuple-element.81), channel_id=1, source_target_pairs={{0,64},{1,65},{2,66},{3,67},{4,68},{5,69},{6,70},{7,71},{8,72},{9,... | collective-permute-start | bytes 196616 | tf_op jit(solution)/shard_map/ppermute | solution.py:51
  115.9 4.3 %collective-permute-start.28 = (bf16[8,4096]{1,0:T(8,128)(2,1)S(1)}, bf16[8,4096]{1,0:T(8,128)(2,1)S(1)}, u32[]{:S(2)}, u32[]{:S(2)}) collective-permute-start(bf16[8,4096]{1,0:T(8,128)(2,1)S(1)} %get-tuple-element.82), channel_id=1, source_target_pairs={{0,66},{1,67},{2,64},{3,65},{4,70},{5,71},{6,68},{7,69},{8,74},{9,... | collective-permute-start | bytes 196616 | tf_op jit(solution)/shard_map/ppermute | solution.py:51
  120.3 5.4 %collective-permute-start.29 = (bf16[8,2048]{1,0:T(8,128)(2,1)S(1)}, bf16[8,2048]{1,0:T(8,128)(2,1)S(1)}, u32[]{:S(2)}, u32[]{:S(2)}) collective-permute-start(bf16[8,2048]{1,0:T(8,128)(2,1)S(1)} %get-tuple-element.84), channel_id=1, source_target_pairs={{0,1},{1,0},{2,3},{3,2},{4,5},{5,4},{6,7},{7,6},{8,9},{9,8},{10,11... | collective-permute-start | bytes 98312 | tf_op jit(solution)/shard_map/ppermute | solution.py:51

commit v9 on v8

--- a/solution.py
+++ b/solution.py
@@ -13,7 +13,6 @@
 WIDTH = 8192
 HALF = WIDTH // 2
 QUARTER = WIDTH // 4
-CUT = (WIDTH + 3072) // 2
 UNITS = 224
 TILE = 4096
 STEPS = WIDTH // TILE
@@ -84,14 +83,18 @@
 
 
 def down_kernel(n, n_out, place, *refs):
-    rows = refs[:n]
-    acc, down_w, down_w2, seconds, theirs = refs[n : n + 5]
+    rows, refs = refs[:n], refs[n:]
     if place is None:
-        first, second = refs[n + 5 : n + 7]
+        weights, refs = refs[:4], refs[4:]
     else:
-        sources = refs[n + 5 : n + 7]
-        first, second = refs[n + 7 + n_out : n + 9 + n_out]
-    outs = refs[n + 7 : n + 7 + n_out]
+        acc, refs = refs[0], refs[1:]
+    down_w, down_w2, seconds, theirs = refs[:4]
+    if place is None:
+        first, second = refs[4:6]
+    else:
+        sources = refs[4:6]
+        first, second = refs[6 + n_out : 8 + n_out]
+    outs = refs[6 : 6 + n_out]
     hidden = refs[-1]
 
     def shards_of(learner, to, groups, base):
@@ -116,8 +119,13 @@
         for j in range(PARTS):
             shards_of(i * PARTS + j, first, 4, 0)
         x = jnp.concatenate([r[:, tile] for r in rows], axis=0)
-        low += nt(first[:, tile], x)
-
+        if place is None:
+            low += nt(jnp.concatenate([r[:, tile] for r in (*weights, first)], axis=0), x)
+        else:
+            low += nt(first[:, tile], x)
+
+    if place is None:
+        acc, low = low[: 4 * UNITS], low[4 * UNITS :]
     u = (adapter_scale * low).astype(bf16)
     hs, back = [], 0.0
     for half, (ref, c) in enumerate(((seconds, 0), (theirs, 3072))):
@@ -168,10 +176,10 @@
     )(*extra, *in_vmem([*rows, *weights]))
 
 
-def down(place, rows, acc, weights, seconds, factors, kinds):
+def down(place, rows, lead_in, weights, seconds, factors, kinds):
     n = len(rows)
     theirs = factors[1] if place is not None else seconds[1]
-    operands = in_vmem([*rows, acc, *weights, seconds[0], theirs, *factors])
+    operands = in_vmem([*rows, *lead_in, *weights, seconds[0], theirs, *factors])
     shapes = [((64, WIDTH), kind) for kind in kinds]
     lead = []
     n_out = len(kinds)
@@ -247,19 +255,21 @@
         out[:, at + 256 : at + 512] = far_message[:, col : col + 256]
 
 
-def unpack_kernel(own, got1, left, right, got3, block, factor):
-    for k, g in ((0, own), (1, got1), (3, got3)):
-        block[16 * k : 16 * k + 16, :] = g[:, :WIDTH]
-        factor[16 * k : 16 * k + 16, :] = g[:, WIDTH:]
-    block[32:48, :CUT] = left[...]
-    block[32:48, CUT:] = right[:, : WIDTH - CUT]
-    factor[32:48, :] = right[:, WIDTH - CUT :]
+def unpack_kernel(own, got2, got1, got3, block, factor, packed):
+    for k, g in enumerate((own, got1, got2, got3)):
+        at = slice(16 * k, 16 * k + 16)
+        block[at, :] = g[:, :WIDTH]
+        factor[at, :] = g[:, WIDTH:]
+        packed[at, :] = g[...]
+
+
+def rows_kernel(rows, out):
+    out[...] = rows[...]
 
 
 def halves_kernel(from1, from3, to1, to3):
-    rows, cols = to1.shape
-    to1[...] = from3[:rows, :cols]
-    to3[...] = from1[-rows:, -cols:]
+    to1[...] = from3[:32, :WIDTH]
+    to3[...] = from1[32:, :WIDTH]
 
 
 def relay(from1, from3, routes, shape):
@@ -277,9 +287,9 @@
         out[64 * k : 64 * k + 64, :UNITS] = r[...]
 
 
-def stack_kernel(f0, f1, f2, f2b, f3, seconds, out):
-    for at, r in ((0, f0), (64, f1), (128, f2), (160, f2b), (192, f3)):
-        out[at : at + r.shape[0], :3072] = r[...]
+def stack_kernel(f0, packed1, f2, packed3, seconds, out):
+    for k, r in enumerate((f0, packed1, f2, packed3)):
+        out[64 * k : 64 * k + 64, :3072] = r[:, -3072:]
     out[:, 3072:] = seconds[...]
 
 
@@ -351,46 +361,44 @@
     )
 
     packed = after(packed, gate2)
-    got1, got3 = send(packed, FIRST[1]), send(packed, FIRST[3])
-    got = relay(got1, got3, FIRST, (16, CUT))
+    got = {k: send(packed, FIRST[k]) for k in (1, 2, 3)}
     seconds = (adapter_second_gate, adapter_second_up, adapter_first_down)
     (seconds,) = local(
         seconds_kernel, [((256, 256), bf16)], [a.T for a in after(seconds, packed)]
     )
-    block, factor = local(
+    block, factor, packed = local(
         unpack_kernel,
-        [((64, WIDTH), bf16), ((64, 3072), bf16)],
-        (packed, got1, *got, got3),
-    )
-
-    block, factor = after((block, factor), (up2, seconds))
-    near1, near3 = send(factor, SECOND[1]), send(factor, SECOND[3])
-    rows1, rows3 = send(block, SECOND[1]), send(block, SECOND[3])
+        [((64, WIDTH), bf16), ((64, 3072), bf16), ((64, WIDTH + 3072), bf16)],
+        (packed, got[2], got[1], got[3]),
+    )
+
+    block, factor, packed = after((block, factor, packed), (up2, seconds))
+    far = send(factor, SECOND[2])
+    packed1, packed3 = send(packed, SECOND[1]), send(packed, SECOND[3])
     frozen = (frozen_gate_weight, frozen_up_weight, frozen_down_weight)
     owned = after(frozen, block)
     down2 = send(owned[2], CORE)
-    far = relay(near1, near3, SECOND, (32, 3072))
+    (far,) = local(rows_kernel, [((64, 3072), bf16)], (far,), price=price_of(11))
     (factor,) = local(
-        stack_kernel, [((256, 3072 + 256), bf16)], (factor, near1, *far, near3, seconds)
+        stack_kernel, [((256, 3072 + 256), bf16)], (factor, packed1, far, packed3, seconds)
     )
     factor2 = send(factor, CORE)
-    rows2 = relay(rows1, rows3, SECOND, (32, WIDTH))
+    rows2 = relay(packed1, packed3, SECOND, (32, WIDTH))
     (touched,) = local(touch_kernel, [((8, 128), f32)], in_vmem(owned))
 
     weights = (owned[0], gate2, owned[1], up2)
     down_weights = (owned[2], down2)
 
-    rows = (block, rows1, rows3)
+    rows = (block, packed1, packed3)
     acc = project(rows, weights, touched)
     total, part1, part3, first, second = down(
-        place, rows, acc, down_weights, (seconds, factor2), (factor, factor2),
+        place, rows, (acc,), down_weights, (seconds, factor2), (factor, factor2),
         (f32, bf16, bf16),
     )
     back1, back3 = send(part1, SECOND[1]), send(part3, SECOND[3])
-    rows = after(rows2, part1)
-    acc = project(rows, weights)
     (part2,) = down(
-        None, rows, acc, down_weights, (seconds, factor2), (first, second), (bf16,)
+        None, after(rows2, part1), weights, down_weights, (seconds, factor2),
+        (first, second), (bf16,),
     )
     back2 = send(part2, SECOND[2])
     (total,) = local(

time: 127 us -> 123 us (0.969)
  starting transfers between devices: 42.7 us -> 37.7 us
  waiting for transfers between devices: 56.5 us -> 58.7 us
  local copies, waits for them, and re-layouts: 4.41 us -> 2.37 us
    ppermute x30 -> x26, starting transfers between devices: 42.7 us -> 37.7 us  [send(): return lax.ppermute(value, AXES, route)]
    pallas_call x2, Pallas kernels: 9.59 us -> 14.5 us  [down(): pl.pallas_call(body, in_specs=[SMEM] * len(lead) + [VMEM] * len(operands)...]
    pallas_call x2 -> x1, Pallas kernels: 8.14 us -> 4.05 us  [project(): pl.pallas_call(lambda *refs: project_kernel(n, *refs[more:]), in_specs=[V...]
    ppermute x30 -> x26, waiting for transfers between devices: 56.5 us -> 58.7 us  [send(): return lax.ppermute(value, AXES, route)]
    unnamed x14 -> x12, local copies, waits for them, and re-layouts: 4.32 us -> 2.29 us
    pallas_call x13 -> x12, Pallas kernels: 4 us -> 4.03 us  [local(): pl.pallas_call(body, in_specs=[SMEM] * len(lead) + [VMEM] * len(operands)...]
  transfers between devices with their start and end apart: 30 -> 26, of which waited for: 19 -> 15; matrix products, arithmetic and copies ran while one was open for 0% -> 0% of each run, Pallas kernels for 15% -> 16%
where the time goes in v9:
time: 123 us; the launch traced here: 122 us
  waiting for transfers between devices  58.7 us (48%)
  starting transfers between devices  37.7 us (31%)
  Pallas kernels  22.6 us (18%)
  local copies, waits for them, and re-layouts  2.37 us (2%)
    ppermute x26, waiting for transfers between devices, send(): return lax.ppermute(value, AXES, route)  58.7 us
    ppermute x26, starting transfers between devices, send(): return lax.ppermute(value, AXES, route)  37.7 us
    pallas_call x2, Pallas kernels, down(): pl.pallas_call(body, in_specs=[SMEM] * len(lead) + [VMEM] * len(operands)...  14.5 us
    pallas_call x1, Pallas kernels, project(): pl.pallas_call(lambda *refs: project_kernel(n, *refs[more:]), in_specs=[V...  4.05 us
    pallas_call x12, Pallas kernels, local(): pl.pallas_call(body, in_specs=[SMEM] * len(lead) + [VMEM] * len(operands)...  4.03 us
  transfers between devices with their start and end apart: 26, of which 15 were waited for; matrix products, arithmetic and copies ran while one was open for 0% of the time, Pallas kernels for 16%

profile of v9, /device:TPU:1, one launch (start us, length us, event | category | flops | bytes accessed | tf_op | source)
XLA Modules:
  0.0 122.3 jit_solution(2501100862759473427)
XLA Ops:
  0.1 1.4 %shard_map.100 = (bf16[8,2048]{1,0:T(8,128)(2,1)S(1)}, bf16[8,2048]{1,0:T(8,128)(2,1)S(1)}, bf16[16,1536]{1,0:T(8,128)(2,1)S(1)}) custom-call(s32[5]{0:T(128)S(1)} %stack.23.place.refs_0_, bf16[2,8,2048]{2,1,0:T(8,128)(2,1)} %inputs.1, bf16[64,256]{1,0:T(8,128)(2,1)} %gate.1, bf16[64,256]{1,0:T(8,128)(2,1)} %up.1, bf16[64,256]{1,0:T(8,128)(2,1)} %down.1), custom_call_target="tpu_custom_call" | custom-call | flops 1 | bytes 1 | tf_op jit(solution)/shard_map/pallas_call | solution.py:204
  1.5 1.5 %collective-permute-start = (bf16[8,2048]{1,0:T(8,128)(2,1)S(1)}, bf16[8,2048]{1,0:T(8,128)(2,1)S(1)}, u32[]{:S(2)}, u32[]{:S(2)}) collective-permute-start(bf16[8,2048]{1,0:T(8,128)(2,1)S(1)} %get-tuple-element.43), channel_id=1, source_target_pairs={{0,1},{1,0},{2,3},{3,2},{4,5},{5,4},{6,7},{7,6},{8,9},{9,8},{10,11... | collective-permute-start | bytes 98312 | tf_op jit(solution)/shard_map/ppermute | solution.py:50
  3.0 0.9 collective-permute-done.other
  3.8 0.6 shard_map.101
  4.4 0.4 collective-permute-start.4
  5.0 3.8 %collective-permute-start.3 = (bf16[16,3584]{1,0:T(8,128)(2,1)S(1)}, bf16[16,3584]{1,0:T(8,128)(2,1)S(1)}, u32[]{:S(2)}, u32[]{:S(2)}) collective-permute-start(bf16[16,3584]{1,0:T(8,128)(2,1)S(1)} %get-tuple-element.46.message), channel_id=1, source_target_pairs={{0,66},{1,67},{2,64},{3,65},{4,70},{5,71},{6,68},{7,69},{8,74},{9,... | collective-permute-start | bytes 344072 | tf_op jit(solution)/shard_map/ppermute | solution.py:50
  8.8 1.2 collective-permute-start.2
  10.0 2.2 %collective-permute-done.1.z1 = bf16[8,4096]{1,0:T(8,128)(2,1)S(1)} collective-permute-done((bf16[8,4096]{1,0:T(8,128)(2,1)S(1)}, bf16[8,4096]{1,0:T(8,128)(2,1)S(1)}, u32[]{:S(2)}, u32[]{:S(2)}) %collective-permute-start.1) | collective-permute-done | bytes 65568 | tf_op jit(solution)/shard_map/ppermute | solution.py:50
  12.2 1.2 collective-permute-done.2.z2
  13.5 0.6 shard_map.102.own
  14.0 3.0 %collective-permute-start.5 = (bf16[16,11264]{1,0:T(8,128)(2,1)S(1)}, bf16[16,11264]{1,0:T(8,128)(2,1)S(1)}, u32[]{:S(2)}, u32[]{:S(2)}) collective-permute-start(bf16[16,11264]{1,0:T(8,128)(2,1)S(1)} %shard_map.102.own), channel_id=1, source_target_pairs={{0,8},{1,33},{2,10},{3,35},{4,12},{5,37},{6,14},{7,39},{8,0},{9,41... | collective-permute-start | bytes 1081352 | tf_op jit(solution)/shard_map/ppermute | solution.py:50
  17.0 0.4 collective-permute-start.6
  17.8 0.8 copy-done.3
  18.6 0.8 copy-done.4
  19.3 0.8 copy-done.5
  20.1 2.1 %collective-permute-done.5.got2 = bf16[16,11264]{1,0:T(8,128)(2,1)S(1)} collective-permute-done((bf16[16,11264]{1,0:T(8,128)(2,1)S(1)}, bf16[16,11264]{1,0:T(8,128)(2,1)S(1)}, u32[]{:S(2)}, u32[]{:S(2)}) %collective-permute-start.5) | collective-permute-done | bytes 360480 | tf_op jit(solution)/shard_map/ppermute | solution.py:50
  22.2 4.2 %collective-permute-done.6.got1 = bf16[16,11264]{1,0:T(8,128)(2,1)S(1)} collective-permute-done((bf16[16,11264]{1,0:T(8,128)(2,1)S(1)}, bf16[16,11264]{1,0:T(8,128)(2,1)S(1)}, u32[]{:S(2)}, u32[]{:S(2)}) %collective-permute-start.6) | collective-permute-done | bytes 360480 | tf_op jit(solution)/shard_map/ppermute | solution.py:50
  26.6 2.5 %collective-permute-start.11 = (bf16[224,8192]{1,0:T(8,128)(2,1)}, bf16[224,8192]{1,0:T(8,128)(2,1)S(1)}, u32[]{:S(2)}, u32[]{:S(2)}) collective-permute-start(bf16[224,8192]{1,0:T(8,128)(2,1)} %refs_6_.1), channel_id=1, source_target_pairs={{0,1},{1,0},{2,3},{3,2},{4,5},{5,4},{6,7},{7,6},{8,9},{9,8},{10,11... | collective-permute-start | bytes 11010056 | tf_op jit(solution)/shard_map/ppermute | solution.py:50
  29.1 2.6 %collective-permute-start.12 = (bf16[64,3072]{1,0:T(8,128)(2,1)S(1)}, bf16[64,3072]{1,0:T(8,128)(2,1)S(1)}, u32[]{:S(2)}, u32[]{:S(2)}) collective-permute-start(bf16[64,3072]{1,0:T(8,128)(2,1)S(1)} %get-tuple-element.61.f0), channel_id=1, source_target_pairs={{0,32},{1,9},{2,34},{3,11},{4,36},{5,13},{6,38},{7,15},{8,40},{9,1... | collective-permute-start | bytes 1179656 | tf_op jit(solution)/shard_map/ppermute | solution.py:50
  31.7 0.9 collective-permute-start.10
  32.7 4.9 %collective-permute-done.12.rows = bf16[64,3072]{1,0:T(8,128)(2,1)S(1)} collective-permute-done((bf16[64,3072]{1,0:T(8,128)(2,1)S(1)}, bf16[64,3072]{1,0:T(8,128)(2,1)S(1)}, u32[]{:S(2)}, u32[]{:S(2)}) %collective-permute-start.12) | collective-permute-done | bytes 393248 | tf_op jit(solution)/shard_map/ppermute | solution.py:50
  37.6 15.4 %collective-permute-done.10.refs_3_.packed3.from3 = bf16[64,11264]{1,0:T(8,128)(2,1)S(1)} collective-permute-done((bf16[64,11264]{1,0:T(8,128)(2,1)S(1)}, bf16[64,11264]{1,0:T(8,128)(2,1)S(1)}, u32[]{:S(2)}, u32[]{:S(2)}) %collective-permute-start.10) | collective-permute-done | bytes 1441824 | tf_op jit(solution)/shard_map/ppermute | solution.py:50
  53.1 1.4 %collective-permute-start.13 = (bf16[256,3328]{1,0:T(8,128)(2,1)S(1)}, bf16[256,3328]{1,0:T(8,128)(2,1)S(1)}, u32[]{:S(2)}, u32[]{:S(2)}) collective-permute-start(bf16[256,3328]{1,0:T(8,128)(2,1)S(1)} %shard_map.108.refs_9_), channel_id=1, source_target_pairs={{0,1},{1,0},{2,3},{3,2},{4,5},{5,4},{6,7},{7,6},{8,9},{9,8},{10,11... | collective-permute-start | bytes 5111816 | tf_op jit(solution)/shard_map/ppermute | solution.py:50
  54.6 1.2 %collective-permute-start.16 = (bf16[32,8192]{1,0:T(8,128)(2,1)S(1)}, bf16[32,8192]{1,0:T(8,128)(2,1)S(1)}, u32[]{:S(2)}, u32[]{:S(2)}) collective-permute-start(bf16[32,8192]{1,0:T(8,128)(2,1)S(1)} %get-tuple-element.65), channel_id=1, source_target_pairs={{0,16},{1,5},{2,18},{3,7},{4,20},{5,1},{6,22},{7,3},{8,24},{9,13},... | collective-permute-start | bytes 1572872 | tf_op jit(solution)/shard_map/ppermute | solution.py:50
  55.8 1.7 %collective-permute-start.17 = (bf16[32,8192]{1,0:T(8,128)(2,1)S(1)}, bf16[32,8192]{1,0:T(8,128)(2,1)S(1)}, u32[]{:S(2)}, u32[]{:S(2)}) collective-permute-start(bf16[32,8192]{1,0:T(8,128)(2,1)S(1)} %get-tuple-element.66), channel_id=1, source_target_pairs={{0,48},{1,13},{2,50},{3,15},{4,52},{5,9},{6,54},{7,11},{8,56},{9,5... | collective-permute-start | bytes 1572872 | tf_op jit(solution)/shard_map/ppermute | solution.py:50
  57.6 4.1 %shard_map.106.refs_4_ = f32[896,192]{1,0:T(8,128)S(1)} custom-call(f32[8,128]{1,0:T(8,128)S(1)} %shard_map.105.refs_0_, bf16[64,8192]{1,0:T(8,128)(2,1)S(1)} %get-tuple-element.56.refs_1_, bf16[64,11264]{1,0:T(8,128)(2,1)S(1)} %collective-permute-done.9.refs_2_.packed1.from1, bf16[64,11264]{1,0:T(8,128)(2,1)S(1)} %collective-permute-done.10.refs_3_.packed3.from3, ...), custom_call_target="tpu_custom_call" | custom-call | flops 9200000000 | bytes 28800000 | tf_op jit(solution)/shard_map/pallas_call | solution.py:169
  61.7 6.0 %shard_map.109 = (f32[64,8192]{1,0:T(8,128)S(1)}, bf16[64,8192]{1,0:T(8,128)(2,1)S(1)}, bf16[64,8192]{1,0:T(8,128)(2,1)S(1)}, bf16[128,8192]{1,0:T(8,128)(2,1)S(1)}, bf16[64,8192]{1,0:T(8,128)(2,1)S(1)}) custom-call(s32[5]{0:T(128)S(1)} %stack.23.place.refs_0_, bf16[64,8192]{1,0:T(8,128)(2,1)S(1)} %get-tuple-element.56.refs_1_, ...), custom_call_target="tpu_custom_call" | custom-call | flops 1 | bytes 1 | tf_op jit(solution)/shard_map/pallas_call | solution.py:191
  67.7 0.4 collective-permute-start.14
  68.1 0.9 collective-permute-start.15
  69.0 8.5 %shard_map.112 = bf16[64,8192]{1,0:T(8,128)(2,1)S(1)} custom-call(bf16[32,8192]{1,0:T(8,128)(2,1)S(1)} %collective-permute-done.16.refs_0_, bf16[32,8192]{1,0:T(8,128)(2,1)S(1)} %collective-permute-done.17.refs_1_, bf16[224,8192]{1,0:T(8,128)(2,1)S(1)} %copy-done.1, bf16[224,8192]{1,0:T(8,128)(2,1)S(1)} %collective-permute-done.4.refs_5_.refs_3_, ...), custom_call_target="tpu_custom_call" | custom-call | flops 1 | bytes 1 | tf_op jit(solution)/shard_map/pallas_call | solution.py:191
  77.5 2.1 %collective-permute-start.18 = (bf16[64,8192]{1,0:T(8,128)(2,1)S(1)}, bf16[64,8192]{1,0:T(8,128)(2,1)S(1)}, u32[]{:S(2)}, u32[]{:S(2)}) collective-permute-start(bf16[64,8192]{1,0:T(8,128)(2,1)S(1)} %shard_map.112), channel_id=1, source_target_pairs={{0,32},{1,9},{2,34},{3,11},{4,36},{5,13},{6,38},{7,15},{8,40},{9,1... | collective-permute-start | bytes 3145736 | tf_op jit(solution)/shard_map/ppermute | solution.py:50
  79.6 2.1 %collective-permute-done.14.b1 = bf16[64,8192]{1,0:T(8,128)(2,1)S(1)} collective-permute-done((bf16[64,8192]{1,0:T(8,128)(2,1)S(1)}, bf16[64,8192]{1,0:T(8,128)(2,1)S(1)}, u32[]{:S(2)}, u32[]{:S(2)}) %collective-permute-start.14) | collective-permute-done | bytes 1048608 | tf_op jit(solution)/shard_map/ppermute | solution.py:50
  81.7 12.8 %collective-permute-done.15.b3 = bf16[64,8192]{1,0:T(8,128)(2,1)S(1)} collective-permute-done((bf16[64,8192]{1,0:T(8,128)(2,1)S(1)}, bf16[64,8192]{1,0:T(8,128)(2,1)S(1)}, u32[]{:S(2)}, u32[]{:S(2)}) %collective-permute-start.15) | collective-permute-done | bytes 1048608 | tf_op jit(solution)/shard_map/ppermute | solution.py:50
  94.9 0.9 collective-permute-start.19
  95.8 2.5 %collective-permute-start.20 = (bf16[16,8192]{1,0:T(8,128)(2,1)S(1)}, bf16[16,8192]{1,0:T(8,128)(2,1)S(1)}, u32[]{:S(2)}, u32[]{:S(2)}) collective-permute-start(bf16[16,8192]{1,0:T(8,128)(2,1)S(1)} %get-tuple-element.73), channel_id=1, source_target_pairs={{0,8},{1,33},{2,10},{3,35},{4,12},{5,37},{6,14},{7,39},{8,0},{9,41... | collective-permute-start | bytes 786440 | tf_op jit(solution)/shard_map/ppermute | solution.py:50
  98.3 0.6 collective-permute-start.21
  98.9 1.7 %collective-permute-done.19.b1 = bf16[16,8192]{1,0:T(8,128)(2,1)S(1)} collective-permute-done((bf16[16,8192]{1,0:T(8,128)(2,1)S(1)}, bf16[16,8192]{1,0:T(8,128)(2,1)S(1)}, u32[]{:S(2)}, u32[]{:S(2)}) %collective-permute-start.19) | collective-permute-done | bytes 262176 | tf_op jit(solution)/shard_map/ppermute | solution.py:50
  100.5 4.6 %collective-permute-done.20.b2 = bf16[16,8192]{1,0:T(8,128)(2,1)S(1)} collective-permute-done((bf16[16,8192]{1,0:T(8,128)(2,1)S(1)}, bf16[16,8192]{1,0:T(8,128)(2,1)S(1)}, u32[]{:S(2)}, u32[]{:S(2)}) %collective-permute-start.20) | collective-permute-done | bytes 262176 | tf_op jit(solution)/shard_map/ppermute | solution.py:50
  105.2 2.6 %collective-permute-done.21.b3 = bf16[16,8192]{1,0:T(8,128)(2,1)S(1)} collective-permute-done((bf16[16,8192]{1,0:T(8,128)(2,1)S(1)}, bf16[16,8192]{1,0:T(8,128)(2,1)S(1)}, u32[]{:S(2)}, u32[]{:S(2)}) %collective-permute-start.21) | collective-permute-done | bytes 262176 | tf_op jit(solution)/shard_map/ppermute | solution.py:50
  107.8 0.7 shard_map.114
  108.5 1.8 %collective-permute-start.22 = (bf16[8,4096]{1,0:T(8,128)(2,1)S(1)}, bf16[8,4096]{1,0:T(8,128)(2,1)S(1)}, u32[]{:S(2)}, u32[]{:S(2)}) collective-permute-start(bf16[8,4096]{1,0:T(8,128)(2,1)S(1)} %get-tuple-element.76), channel_id=1, source_target_pairs={{0,2},{1,3},{2,0},{3,1},{4,6},{5,7},{6,4},{7,5},{8,10},{9,11},{10,... | collective-permute-start | bytes 196616 | tf_op jit(solution)/shard_map/ppermute | solution.py:50
  110.3 1.3 %collective-permute-start.23 = (bf16[8,4096]{1,0:T(8,128)(2,1)S(1)}, bf16[8,4096]{1,0:T(8,128)(2,1)S(1)}, u32[]{:S(2)}, u32[]{:S(2)}) collective-permute-start(bf16[8,4096]{1,0:T(8,128)(2,1)S(1)} %get-tuple-element.77), channel_id=1, source_target_pairs={{0,64},{1,65},{2,66},{3,67},{4,68},{5,69},{6,70},{7,71},{8,72},{9,... | collective-permute-start | bytes 196616 | tf_op jit(solution)/shard_map/ppermute | solution.py:50
  111.6 1.1 collective-permute-start.24
  112.8 2.1 %collective-permute-done.23 = bf16[8,4096]{1,0:T(8,128)(2,1)S(1)} collective-permute-done((bf16[8,4096]{1,0:T(8,128)(2,1)S(1)}, bf16[8,4096]{1,0:T(8,128)(2,1)S(1)}, u32[]{:S(2)}, u32[]{:S(2)}) %collective-permute-start.23) | collective-permute-done | bytes 65568 | tf_op jit(solution)/shard_map/ppermute | solution.py:50
  114.9 1.0 collective-permute-done.24
  116.0 4.8 %collective-permute-start.25 = (bf16[8,2048]{1,0:T(8,128)(2,1)S(1)}, bf16[8,2048]{1,0:T(8,128)(2,1)S(1)}, u32[]{:S(2)}, u32[]{:S(2)}) collective-permute-start(bf16[8,2048]{1,0:T(8,128)(2,1)S(1)} %get-tuple-element.80), channel_id=1, source_target_pairs={{0,1},{1,0},{2,3},{3,2},{4,5},{5,4},{6,7},{7,6},{8,9},{9,8},{10,11... | collective-permute-start | bytes 98312 | tf_op jit(solution)/shard_map/ppermute | solution.py:50
  120.8 0.9 collective-permute-done.25
  121.7 0.6 maximum_select_fusion
  (35 shorter events, 1.6 us)
Async XLA Ops:
  1.5 2.4 %collective-permute-start = (bf16[8,2048]{1,0:T(8,128)(2,1)S(1)}, bf16[8,2048]{1,0:T(8,128)(2,1)S(1)}, u32[]{:S(2)}, u32[]{:S(2)}) collective-permute-start(bf16[8,2048]{1,0:T(8,128)(2,1)S(1)} %get-tuple-element.43), channel_id=1, source_target_pairs={{0,1},{1,0},{2,3},{3,2},{4,5},{5,4},{6,7},{7,6},{8,9},{9,8},{10,11... | collective-permute-start | bytes 98312 | tf_op jit(solution)/shard_map/ppermute | solution.py:50
  4.4 9.6 %collective-permute-start.4 = (bf16[224,8192]{1,0:T(8,128)(2,1)}, bf16[224,8192]{1,0:T(8,128)(2,1)S(1)}, u32[]{:S(2)}, u32[]{:S(2)}) collective-permute-start(bf16[224,8192]{1,0:T(8,128)(2,1)} %refs_2_), channel_id=1, source_target_pairs={{0,1},{1,0},{2,3},{3,2},{4,5},{5,4},{6,7},{7,6},{8,9},{9,8},{10,11... | collective-permute-start | bytes 11010056 | tf_op jit(solution)/shard_map/ppermute | solution.py:50
  4.8 21.8 %collective-permute-start.8 = (bf16[224,8192]{1,0:T(8,128)(2,1)}, bf16[224,8192]{1,0:T(8,128)(2,1)S(1)}, u32[]{:S(2)}, u32[]{:S(2)}) collective-permute-start(bf16[224,8192]{1,0:T(8,128)(2,1)} %refs_4_.1), channel_id=1, source_target_pairs={{0,1},{1,0},{2,3},{3,2},{4,5},{5,4},{6,7},{7,6},{8,9},{9,8},{10,11... | collective-permute-start | bytes 11010056 | tf_op jit(solution)/shard_map/ppermute | solution.py:50
  5.0 8.5 %collective-permute-start.3 = (bf16[16,3584]{1,0:T(8,128)(2,1)S(1)}, bf16[16,3584]{1,0:T(8,128)(2,1)S(1)}, u32[]{:S(2)}, u32[]{:S(2)}) collective-permute-start(bf16[16,3584]{1,0:T(8,128)(2,1)S(1)} %get-tuple-element.46.message), channel_id=1, source_target_pairs={{0,66},{1,67},{2,64},{3,65},{4,70},{5,71},{6,68},{7,69},{8,74},{9,... | collective-permute-start | bytes 344072 | tf_op jit(solution)/shard_map/ppermute | solution.py:50
  8.8 3.4 %collective-permute-start.1 = (bf16[8,4096]{1,0:T(8,128)(2,1)S(1)}, bf16[8,4096]{1,0:T(8,128)(2,1)S(1)}, u32[]{:S(2)}, u32[]{:S(2)}) collective-permute-start(bf16[8,4096]{1,0:T(8,128)(2,1)S(1)} %get-tuple-element.45.wide), channel_id=1, source_target_pairs={{0,2},{1,3},{2,0},{3,1},{4,6},{5,7},{6,4},{7,5},{8,10},{9,11},{10,... | collective-permute-start | bytes 196616 | tf_op jit(solution)/shard_map/ppermute | solution.py:50
  8.8 4.6 %collective-permute-start.2 = (bf16[8,4096]{1,0:T(8,128)(2,1)S(1)}, bf16[8,4096]{1,0:T(8,128)(2,1)S(1)}, u32[]{:S(2)}, u32[]{:S(2)}) collective-permute-start(bf16[8,4096]{1,0:T(8,128)(2,1)S(1)} %get-tuple-element.45.wide), channel_id=1, source_target_pairs={{0,64},{1,65},{2,66},{3,67},{4,68},{5,69},{6,70},{7,71},{8,72},{9,... | collective-permute-start | bytes 196616 | tf_op jit(solution)/shard_map/ppermute | solution.py:50
  14.0 8.2 %collective-permute-start.5 = (bf16[16,11264]{1,0:T(8,128)(2,1)S(1)}, bf16[16,11264]{1,0:T(8,128)(2,1)S(1)}, u32[]{:S(2)}, u32[]{:S(2)}) collective-permute-start(bf16[16,11264]{1,0:T(8,128)(2,1)S(1)} %shard_map.102.own), channel_id=1, source_target_pairs={{0,8},{1,33},{2,10},{3,35},{4,12},{5,37},{6,14},{7,39},{8,0},{9,41... | collective-permute-start | bytes 1081352 | tf_op jit(solution)/shard_map/ppermute | solution.py:50
  17.0 9.4 %collective-permute-start.6 = (bf16[16,11264]{1,0:T(8,128)(2,1)S(1)}, bf16[16,11264]{1,0:T(8,128)(2,1)S(1)}, u32[]{:S(2)}, u32[]{:S(2)}) collective-permute-start(bf16[16,11264]{1,0:T(8,128)(2,1)S(1)} %shard_map.102.own), channel_id=1, source_target_pairs={{0,4},{1,17},{2,6},{3,19},{4,0},{5,21},{6,2},{7,23},{8,12},{9,25},... | collective-permute-start | bytes 1081352 | tf_op jit(solution)/shard_map/ppermute | solution.py:50
  17.4 9.0 %collective-permute-start.7 = (bf16[16,11264]{1,0:T(8,128)(2,1)S(1)}, bf16[16,11264]{1,0:T(8,128)(2,1)S(1)}, u32[]{:S(2)}, u32[]{:S(2)}) collective-permute-start(bf16[16,11264]{1,0:T(8,128)(2,1)S(1)} %shard_map.102.own), channel_id=1, source_target_pairs={{0,12},{1,49},{2,14},{3,51},{4,8},{5,53},{6,10},{7,55},{8,4},{9,57... | collective-permute-start | bytes 1081352 | tf_op jit(solution)/shard_map/ppermute | solution.py:50
  17.8 0.8 copy-start.3
  18.6 0.8 copy-start.4
  19.3 0.8 copy-start.5
  26.6 35.0 %collective-permute-start.11 = (bf16[224,8192]{1,0:T(8,128)(2,1)}, bf16[224,8192]{1,0:T(8,128)(2,1)S(1)}, u32[]{:S(2)}, u32[]{:S(2)}) collective-permute-start(bf16[224,8192]{1,0:T(8,128)(2,1)} %refs_6_.1), channel_id=1, source_target_pairs={{0,1},{1,0},{2,3},{3,2},{4,5},{5,4},{6,7},{7,6},{8,9},{9,8},{10,11... | collective-permute-start | bytes 11010056 | tf_op jit(solution)/shard_map/ppermute | solution.py:50
  29.1 8.5 %collective-permute-start.12 = (bf16[64,3072]{1,0:T(8,128)(2,1)S(1)}, bf16[64,3072]{1,0:T(8,128)(2,1)S(1)}, u32[]{:S(2)}, u32[]{:S(2)}) collective-permute-start(bf16[64,3072]{1,0:T(8,128)(2,1)S(1)} %get-tuple-element.61.f0), channel_id=1, source_target_pairs={{0,32},{1,9},{2,34},{3,11},{4,36},{5,13},{6,38},{7,15},{8,40},{9,1... | collective-permute-start | bytes 1179656 | tf_op jit(solution)/shard_map/ppermute | solution.py:50
  31.7 21.3 %collective-permute-start.10 = (bf16[64,11264]{1,0:T(8,128)(2,1)S(1)}, bf16[64,11264]{1,0:T(8,128)(2,1)S(1)}, u32[]{:S(2)}, u32[]{:S(2)}) collective-permute-start(bf16[64,11264]{1,0:T(8,128)(2,1)S(1)} %get-tuple-element.57), channel_id=1, source_target_pairs={{0,48},{1,13},{2,50},{3,15},{4,52},{5,9},{6,54},{7,11},{8,56},{9,5... | collective-permute-start | bytes 4325384 | tf_op jit(solution)/shard_map/ppermute | solution.py:50
  32.6 20.3 %collective-permute-start.9 = (bf16[64,11264]{1,0:T(8,128)(2,1)S(1)}, bf16[64,11264]{1,0:T(8,128)(2,1)S(1)}, u32[]{:S(2)}, u32[]{:S(2)}) collective-permute-start(bf16[64,11264]{1,0:T(8,128)(2,1)S(1)} %get-tuple-element.57), channel_id=1, source_target_pairs={{0,16},{1,5},{2,18},{3,7},{4,20},{5,1},{6,22},{7,3},{8,24},{9,13},... | collective-permute-start | bytes 4325384 | tf_op jit(solution)/shard_map/ppermute | solution.py:50
  37.6 16.9 %copy-start.1 = (bf16[224,8192]{1,0:T(8,128)(2,1)S(1)}, bf16[224,8192]{1,0:T(8,128)(2,1)}, u32[]{:S(2)}) copy-start(bf16[224,8192]{1,0:T(8,128)(2,1)} %refs_2_) | copy-start | bytes 11010052
  37.6 16.9 %copy-start.2 = (bf16[224,8192]{1,0:T(8,128)(2,1)S(1)}, bf16[224,8192]{1,0:T(8,128)(2,1)}, u32[]{:S(2)}) copy-start(bf16[224,8192]{1,0:T(8,128)(2,1)} %refs_4_.1) | copy-start | bytes 11010052
  37.6 16.9 %copy-start = (bf16[224,8192]{1,0:T(8,128)(2,1)S(1)}, bf16[224,8192]{1,0:T(8,128)(2,1)}, u32[]{:S(2)}) copy-start(bf16[224,8192]{1,0:T(8,128)(2,1)} %refs_6_.1) | copy-start | bytes 11010052
  53.1 8.5 %collective-permute-start.13 = (bf16[256,3328]{1,0:T(8,128)(2,1)S(1)}, bf16[256,3328]{1,0:T(8,128)(2,1)S(1)}, u32[]{:S(2)}, u32[]{:S(2)}) collective-permute-start(bf16[256,3328]{1,0:T(8,128)(2,1)S(1)} %shard_map.108.refs_9_), channel_id=1, source_target_pairs={{0,1},{1,0},{2,3},{3,2},{4,5},{5,4},{6,7},{7,6},{8,9},{9,8},{10,11... | collective-permute-start | bytes 5111816 | tf_op jit(solution)/shard_map/ppermute | solution.py:50
  54.6 14.4 %collective-permute-start.16 = (bf16[32,8192]{1,0:T(8,128)(2,1)S(1)}, bf16[32,8192]{1,0:T(8,128)(2,1)S(1)}, u32[]{:S(2)}, u32[]{:S(2)}) collective-permute-start(bf16[32,8192]{1,0:T(8,128)(2,1)S(1)} %get-tuple-element.65), channel_id=1, source_target_pairs={{0,16},{1,5},{2,18},{3,7},{4,20},{5,1},{6,22},{7,3},{8,24},{9,13},... | collective-permute-start | bytes 1572872 | tf_op jit(solution)/shard_map/ppermute | solution.py:50
  55.8 13.2 %collective-permute-start.17 = (bf16[32,8192]{1,0:T(8,128)(2,1)S(1)}, bf16[32,8192]{1,0:T(8,128)(2,1)S(1)}, u32[]{:S(2)}, u32[]{:S(2)}) collective-permute-start(bf16[32,8192]{1,0:T(8,128)(2,1)S(1)} %get-tuple-element.66), channel_id=1, source_target_pairs={{0,48},{1,13},{2,50},{3,15},{4,52},{5,9},{6,54},{7,11},{8,56},{9,5... | collective-permute-start | bytes 1572872 | tf_op jit(solution)/shard_map/ppermute | solution.py:50
  67.7 14.0 %collective-permute-start.14 = (bf16[64,8192]{1,0:T(8,128)(2,1)S(1)}, bf16[64,8192]{1,0:T(8,128)(2,1)S(1)}, u32[]{:S(2)}, u32[]{:S(2)}) collective-permute-start(bf16[64,8192]{1,0:T(8,128)(2,1)S(1)} %get-tuple-element.63), channel_id=1, source_target_pairs={{0,16},{1,5},{2,18},{3,7},{4,20},{5,1},{6,22},{7,3},{8,24},{9,13},... | collective-permute-start | bytes 3145736 | tf_op jit(solution)/shard_map/ppermute | solution.py:50
  68.1 26.4 %collective-permute-start.15 = (bf16[64,8192]{1,0:T(8,128)(2,1)S(1)}, bf16[64,8192]{1,0:T(8,128)(2,1)S(1)}, u32[]{:S(2)}, u32[]{:S(2)}) collective-permute-start(bf16[64,8192]{1,0:T(8,128)(2,1)S(1)} %get-tuple-element.64), channel_id=1, source_target_pairs={{0,48},{1,13},{2,50},{3,15},{4,52},{5,9},{6,54},{7,11},{8,56},{9,5... | collective-permute-start | bytes 3145736 | tf_op jit(solution)/shard_map/ppermute | solution.py:50
  77.5 17.2 %collective-permute-start.18 = (bf16[64,8192]{1,0:T(8,128)(2,1)S(1)}, bf16[64,8192]{1,0:T(8,128)(2,1)S(1)}, u32[]{:S(2)}, u32[]{:S(2)}) collective-permute-start(bf16[64,8192]{1,0:T(8,128)(2,1)S(1)} %shard_map.112), channel_id=1, source_target_pairs={{0,32},{1,9},{2,34},{3,11},{4,36},{5,13},{6,38},{7,15},{8,40},{9,1... | collective-permute-start | bytes 3145736 | tf_op jit(solution)/shard_map/ppermute | solution.py:50
  94.9 5.6 %collective-permute-start.19 = (bf16[16,8192]{1,0:T(8,128)(2,1)S(1)}, bf16[16,8192]{1,0:T(8,128)(2,1)S(1)}, u32[]{:S(2)}, u32[]{:S(2)}) collective-permute-start(bf16[16,8192]{1,0:T(8,128)(2,1)S(1)} %get-tuple-element.72), channel_id=1, source_target_pairs={{0,4},{1,17},{2,6},{3,19},{4,0},{5,21},{6,2},{7,23},{8,12},{9,25},... | collective-permute-start | bytes 786440 | tf_op jit(solution)/shard_map/ppermute | solution.py:50
  95.8 9.4 %collective-permute-start.20 = (bf16[16,8192]{1,0:T(8,128)(2,1)S(1)}, bf16[16,8192]{1,0:T(8,128)(2,1)S(1)}, u32[]{:S(2)}, u32[]{:S(2)}) collective-permute-start(bf16[16,8192]{1,0:T(8,128)(2,1)S(1)} %get-tuple-element.73), channel_id=1, source_target_pairs={{0,8},{1,33},{2,10},{3,35},{4,12},{5,37},{6,14},{7,39},{8,0},{9,41... | collective-permute-start | bytes 786440 | tf_op jit(solution)/shard_map/ppermute | solution.py:50
  98.3 9.5 %collective-permute-start.21 = (bf16[16,8192]{1,0:T(8,128)(2,1)S(1)}, bf16[16,8192]{1,0:T(8,128)(2,1)S(1)}, u32[]{:S(2)}, u32[]{:S(2)}) collective-permute-start(bf16[16,8192]{1,0:T(8,128)(2,1)S(1)} %get-tuple-element.74), channel_id=1, source_target_pairs={{0,12},{1,49},{2,14},{3,51},{4,8},{5,53},{6,10},{7,55},{8,4},{9,57... | collective-permute-start | bytes 786440 | tf_op jit(solution)/shard_map/ppermute | solution.py:50
  108.5 4.3 %collective-permute-start.22 = (bf16[8,4096]{1,0:T(8,128)(2,1)S(1)}, bf16[8,4096]{1,0:T(8,128)(2,1)S(1)}, u32[]{:S(2)}, u32[]{:S(2)}) collective-permute-start(bf16[8,4096]{1,0:T(8,128)(2,1)S(1)} %get-tuple-element.76), channel_id=1, source_target_pairs={{0,2},{1,3},{2,0},{3,1},{4,6},{5,7},{6,4},{7,5},{8,10},{9,11},{10,... | collective-permute-start | bytes 196616 | tf_op jit(solution)/shard_map/ppermute | solution.py:50
  110.3 4.6 %collective-permute-start.23 = (bf16[8,4096]{1,0:T(8,128)(2,1)S(1)}, bf16[8,4096]{1,0:T(8,128)(2,1)S(1)}, u32[]{:S(2)}, u32[]{:S(2)}) collective-permute-start(bf16[8,4096]{1,0:T(8,128)(2,1)S(1)} %get-tuple-element.77), channel_id=1, source_target_pairs={{0,64},{1,65},{2,66},{3,67},{4,68},{5,69},{6,70},{7,71},{8,72},{9,... | collective-permute-start | bytes 196616 | tf_op jit(solution)/shard_map/ppermute | solution.py:50
  111.6 4.3 %collective-permute-start.24 = (bf16[8,4096]{1,0:T(8,128)(2,1)S(1)}, bf16[8,4096]{1,0:T(8,128)(2,1)S(1)}, u32[]{:S(2)}, u32[]{:S(2)}) collective-permute-start(bf16[8,4096]{1,0:T(8,128)(2,1)S(1)} %get-tuple-element.78), channel_id=1, source_target_pairs={{0,66},{1,67},{2,64},{3,65},{4,70},{5,71},{6,68},{7,69},{8,74},{9,... | collective-permute-start | bytes 196616 | tf_op jit(solution)/shard_map/ppermute | solution.py:50
  116.0 5.7 %collective-permute-start.25 = (bf16[8,2048]{1,0:T(8,128)(2,1)S(1)}, bf16[8,2048]{1,0:T(8,128)(2,1)S(1)}, u32[]{:S(2)}, u32[]{:S(2)}) collective-permute-start(bf16[8,2048]{1,0:T(8,128)(2,1)S(1)} %get-tuple-element.80), channel_id=1, source_target_pairs={{0,1},{1,0},{2,3},{3,2},{4,5},{5,4},{6,7},{7,6},{8,9},{9,8},{10,11... | collective-permute-start | bytes 98312 | tf_op jit(solution)/shard_map/ppermute | solution.py:50

commit v10 on v9

--- a/solution.py
+++ b/solution.py
@@ -82,36 +82,49 @@
             out[...] += nt(w, x)
 
 
+def shard_homes(place):
+    out = []
+    for other in range(2):
+        along_x = (place[3] ^ other) == 0
+        cols = [
+            [pl.ds(pl.multiple_of(g * 512 + (zh ^ place[0]) * 256, 256), 256) for zh in (0, 1)]
+            for g in range(6)
+        ]
+        rows_at = []
+        for y in range(4):
+            for x in range(4):
+                dy, dx = y ^ place[1], x ^ place[2]
+                row = jnp.where(along_x, dy * 64 + dx * 16, dx * 64 + dy * 16)
+                rows_at.append(pl.ds(pl.multiple_of(row, 16), 16))
+        rank = (place[3] ^ other) * 32
+        to_at = [
+            pl.ds(pl.multiple_of(rank + (k // 2) * 64 + (k % 2) * 16, 16), 16)
+            for k in range(4)
+        ]
+        out.append((cols, rows_at, to_at))
+    return out
+
+
 def down_kernel(n, n_out, place, *refs):
-    rows, refs = refs[:n], refs[n:]
+    rows = refs[:n]
+    acc, down_w, down_w2, seconds, theirs = refs[n : n + 5]
     if place is None:
-        weights, refs = refs[:4], refs[4:]
+        first, second = refs[n + 5 : n + 7]
     else:
-        acc, refs = refs[0], refs[1:]
-    down_w, down_w2, seconds, theirs = refs[:4]
-    if place is None:
-        first, second = refs[4:6]
-    else:
-        sources = refs[4:6]
-        first, second = refs[6 + n_out : 8 + n_out]
-    outs = refs[6 : 6 + n_out]
+        sources = refs[n + 5 : n + 7]
+        first, second = refs[n + 7 + n_out : n + 9 + n_out]
+        homes = shard_homes(place)
+    outs = refs[n + 7 : n + 7 + n_out]
     hidden = refs[-1]
 
     def shards_of(learner, to, groups, base):
         if place is None:
             return
-        zh, y, x = learner // 16, (learner // 4) % 4, learner % 4
-        dz, dy, dx = zh ^ place[0], y ^ place[1], x ^ place[2]
         for other, src in enumerate(sources):
-            along_x = (place[3] ^ other) == 0
-            near = jnp.where(along_x, dx, dy)
-            far = jnp.where(along_x, dy, dx)
-            r = pl.ds(pl.multiple_of((far * 4 + near) * 16, 16), 16)
+            cols, rows_at, to_at = homes[other]
             for k in range(groups):
-                at = pl.multiple_of((base + k) * 512 + dz * 256, 256)
-                row = (place[3] ^ other) * 32 + (k // 2) * 64 + (k % 2) * 16
-                row = pl.ds(pl.multiple_of(row, 16), 16)
-                to[row, learner * 256 : learner * 256 + 256] = src[r, pl.ds(at, 256)]
+                piece = src[rows_at[learner % 16], cols[base + k][learner // 16]]
+                to[to_at[k], learner * 256 : learner * 256 + 256] = piece
 
     low = 0.0
     for i in range(STEPS):
@@ -119,13 +132,8 @@
         for j in range(PARTS):
             shards_of(i * PARTS + j, first, 4, 0)
         x = jnp.concatenate([r[:, tile] for r in rows], axis=0)
-        if place is None:
-            low += nt(jnp.concatenate([r[:, tile] for r in (*weights, first)], axis=0), x)
-        else:
-            low += nt(first[:, tile], x)
-
-    if place is None:
-        acc, low = low[: 4 * UNITS], low[4 * UNITS :]
+        low += nt(first[:, tile], x)
+
     u = (adapter_scale * low).astype(bf16)
     hs, back = [], 0.0
     for half, (ref, c) in enumerate(((seconds, 0), (theirs, 3072))):
@@ -176,10 +184,10 @@
     )(*extra, *in_vmem([*rows, *weights]))
 
 
-def down(place, rows, lead_in, weights, seconds, factors, kinds):
+def down(place, rows, acc, weights, seconds, factors, kinds):
     n = len(rows)
     theirs = factors[1] if place is not None else seconds[1]
-    operands = in_vmem([*rows, *lead_in, *weights, seconds[0], theirs, *factors])
+    operands = in_vmem([*rows, acc, *weights, seconds[0], theirs, *factors])
     shapes = [((64, WIDTH), kind) for kind in kinds]
     lead = []
     n_out = len(kinds)
@@ -303,7 +311,7 @@
         out[...] = (own[part, :] + widen(b[part, :])).astype(out.dtype)
 
 
-def split_kernel(place, own, b1, b2, b3, keep, s1, s2, s3):
+def split_kernel(place, own, b2, b1, b3, keep, s1, s2, s3):
     zl = place[4]
     here = pl.ds(pl.multiple_of(zl * HALF, HALF), HALF)
     there = pl.ds(pl.multiple_of((1 - zl) * HALF, HALF), HALF)
@@ -313,6 +321,21 @@
             total += widen(b[:, cols])
         near[...] = total[:8].astype(near.dtype)
         far[...] = total[8:].astype(far.dtype)
+
+
+def last_kernel(place, own, b2, b1, b3, keep, give):
+    c = place[3]
+    for at, out in ((c, keep), (1 - c, give)):
+        cols = pl.ds(pl.multiple_of(at * QUARTER, QUARTER), QUARTER)
+        total = own[:, cols] + widen(b1[:, cols])
+        total += widen(b2[:, cols]) + widen(b3[:, cols])
+        out[...] = total.astype(bf16)
+
+
+def join_kernel(place, keep, got, out):
+    c = place[3]
+    out[c] = keep[...]
+    out[1 - c] = got[...]
 
 
 def shards(
@@ -330,11 +353,6 @@
     zh, y, x, zl, c = (lax.axis_index(a) for a in AXES)
     place = jnp.stack([zh, y, x, c, zl]).astype(jnp.int32)
 
-    def ordered(flag, a, b, axis):
-        return jnp.where(
-            flag == 0, jnp.concatenate([a, b], axis), jnp.concatenate([b, a], axis)
-        )
-
     own, other, factor = local(
         begin_kernel,
         [((8, QUARTER), bf16), ((8, QUARTER), bf16), ((16, 1536), bf16)],
@@ -392,13 +410,14 @@
     rows = (block, packed1, packed3)
     acc = project(rows, weights, touched)
     total, part1, part3, first, second = down(
-        place, rows, (acc,), down_weights, (seconds, factor2), (factor, factor2),
+        place, rows, acc, down_weights, (seconds, factor2), (factor, factor2),
         (f32, bf16, bf16),
     )
     back1, back3 = send(part1, SECOND[1]), send(part3, SECOND[3])
+    rows = after(rows2, part1)
+    acc = project(rows, weights)
     (part2,) = down(
-        None, after(rows2, part1), weights, down_weights, (seconds, factor2),
-        (first, second), (bf16,),
+        None, rows, acc, down_weights, (seconds, factor2), (first, second), (bf16,)
     )
     back2 = send(part2, SECOND[2])
     (total,) = local(
@@ -409,16 +428,16 @@
     )
     small = [((16, WIDTH), f32)] + [((16, WIDTH), bf16)] * 3
     mine, *parts = local(sum_kernel, small, (total, back2))
-    backs = [send(p, FIRST[k]) for k, p in zip((1, 2, 3), parts, strict=True)]
+    b1, b2, b3 = (send(p, FIRST[k]) for k, p in zip((1, 2, 3), parts, strict=True))
     small = [((8, HALF), f32)] + [((8, HALF), bf16)] * 3
-    done, *parts = local(split_kernel, small, (mine, *backs), place)
-    for k, p in zip((1, 2, 3), parts, strict=True):
-        done = done + widen(send(p, ALONG_Z[k]))
-    done = done.astype(bf16)
-    keep = jnp.where(c == 0, done[:, :2048], done[:, 2048:])
-    give = jnp.where(c == 0, done[:, 2048:], done[:, :2048])
-    got = send(give, CORE)
-    return ordered(c, keep[None], got[None], 0)
+    done, *parts = local(split_kernel, small, (mine, b2, b1, b3), place)
+    b1, b2, b3 = (send(p, ALONG_Z[k]) for k, p in zip((1, 2, 3), parts, strict=True))
+    small = [((8, QUARTER), bf16)] * 2
+    keep, give = local(last_kernel, small, (done, b2, b1, b3), place)
+    (out,) = local(
+        join_kernel, [((2, 8, QUARTER), bf16)], (keep, send(give, CORE)), place
+    )
+    return out
 
 
 def solution(mesh):

time: 123 us -> 120 us (0.976)
  waiting for transfers between devices: 58.7 us -> 56.8 us
    pallas_call x2, Pallas kernels: 14.5 us -> 9.41 us  [down(): pl.pallas_call(body, in_specs=[SMEM] * len(lead) + [VMEM] * len(operands)...]
    pallas_call x1 -> x2, Pallas kernels: 4.05 us -> 8.14 us  [project(): pl.pallas_call(lambda *refs: project_kernel(n, *refs[more:]), in_specs=[V...]
    ppermute x26, waiting for transfers between devices: 58.7 us -> 56.8 us  [send(): return lax.ppermute(value, AXES, route)]
    pallas_call x12 -> x14, Pallas kernels: 4.03 us -> 5.78 us  [local(): pl.pallas_call(body, in_specs=[SMEM] * len(lead) + [VMEM] * len(operands)...]
  transfers between devices with their start and end apart: 26 -> 26, of which waited for: 15 -> 16; matrix products, arithmetic and copies ran while one was open for 0% -> 0% of each run, Pallas kernels for 16% -> 16%
where the time goes in v10:
time: 120 us
  waiting for transfers between devices  56.8 us (47%)
  starting transfers between devices  37.2 us (31%)
  Pallas kernels  23.3 us (19%)
  local copies, waits for them, and re-layouts  2.37 us (2%)
    ppermute x26, waiting for transfers between devices, send(): return lax.ppermute(value, AXES, route)  56.8 us
    ppermute x26, starting transfers between devices, send(): return lax.ppermute(value, AXES, route)  37.2 us
    pallas_call x2, Pallas kernels, down(): pl.pallas_call(body, in_specs=[SMEM] * len(lead) + [VMEM] * len(operands)...  9.41 us
    pallas_call x2, Pallas kernels, project(): pl.pallas_call(lambda *refs: project_kernel(n, *refs[more:]), in_specs=[V...  8.14 us
    pallas_call x14, Pallas kernels, local(): pl.pallas_call(body, in_specs=[SMEM] * len(lead) + [VMEM] * len(operands)...  5.78 us
  transfers between devices with their start and end apart: 26, of which 16 were waited for; matrix products, arithmetic and copies ran while one was open for 0% of the time, Pallas kernels for 16%

profile of v10, /device:TPU:1, one launch (start us, length us, event | category | flops | bytes accessed | tf_op | source)
XLA Modules:
  0.0 119.8 jit_solution(11873534354403326761)
XLA Ops:
  0.1 1.4 %shard_map.100 = (bf16[8,2048]{1,0:T(8,128)(2,1)S(1)}, bf16[8,2048]{1,0:T(8,128)(2,1)S(1)}, bf16[16,1536]{1,0:T(8,128)(2,1)S(1)}) custom-call(s32[5]{0:T(128)S(1)} %stack.23.place.refs_0_, bf16[2,8,2048]{2,1,0:T(8,128)(2,1)} %inputs.1, bf16[64,256]{1,0:T(8,128)(2,1)} %gate.1, bf16[64,256]{1,0:T(8,128)(2,1)} %up.1, bf16[64,256]{1,0:T(8,128)(2,1)} %down.1), custom_call_target="tpu_custom_call" | custom-call | flops 1 | bytes 1 | tf_op jit(solution)/shard_map/pallas_call | solution.py:212
  1.5 1.5 %collective-permute-start = (bf16[8,2048]{1,0:T(8,128)(2,1)S(1)}, bf16[8,2048]{1,0:T(8,128)(2,1)S(1)}, u32[]{:S(2)}, u32[]{:S(2)}) collective-permute-start(bf16[8,2048]{1,0:T(8,128)(2,1)S(1)} %get-tuple-element.45), channel_id=1, source_target_pairs={{0,1},{1,0},{2,3},{3,2},{4,5},{5,4},{6,7},{7,6},{8,9},{9,8},{10,11... | collective-permute-start | bytes 98312 | tf_op jit(solution)/shard_map/ppermute | solution.py:50
  3.0 0.9 collective-permute-done.other
  3.8 0.6 shard_map.101
  4.4 0.4 collective-permute-start.4
  5.0 3.8 %collective-permute-start.3 = (bf16[16,3584]{1,0:T(8,128)(2,1)S(1)}, bf16[16,3584]{1,0:T(8,128)(2,1)S(1)}, u32[]{:S(2)}, u32[]{:S(2)}) collective-permute-start(bf16[16,3584]{1,0:T(8,128)(2,1)S(1)} %get-tuple-element.48.message), channel_id=1, source_target_pairs={{0,66},{1,67},{2,64},{3,65},{4,70},{5,71},{6,68},{7,69},{8,74},{9,... | collective-permute-start | bytes 344072 | tf_op jit(solution)/shard_map/ppermute | solution.py:50
  8.8 1.2 collective-permute-start.2
  10.0 2.2 %collective-permute-done.1.z1 = bf16[8,4096]{1,0:T(8,128)(2,1)S(1)} collective-permute-done((bf16[8,4096]{1,0:T(8,128)(2,1)S(1)}, bf16[8,4096]{1,0:T(8,128)(2,1)S(1)}, u32[]{:S(2)}, u32[]{:S(2)}) %collective-permute-start.1) | collective-permute-done | bytes 65568 | tf_op jit(solution)/shard_map/ppermute | solution.py:50
  12.2 1.2 %collective-permute-done.2.z2 = bf16[8,4096]{1,0:T(8,128)(2,1)S(1)} collective-permute-done((bf16[8,4096]{1,0:T(8,128)(2,1)S(1)}, bf16[8,4096]{1,0:T(8,128)(2,1)S(1)}, u32[]{:S(2)}, u32[]{:S(2)}) %collective-permute-start.2) | collective-permute-done | bytes 65568 | tf_op jit(solution)/shard_map/ppermute | solution.py:50
  13.5 0.6 shard_map.102.own
  14.0 3.0 %collective-permute-start.5 = (bf16[16,11264]{1,0:T(8,128)(2,1)S(1)}, bf16[16,11264]{1,0:T(8,128)(2,1)S(1)}, u32[]{:S(2)}, u32[]{:S(2)}) collective-permute-start(bf16[16,11264]{1,0:T(8,128)(2,1)S(1)} %shard_map.102.own), channel_id=1, source_target_pairs={{0,8},{1,33},{2,10},{3,35},{4,12},{5,37},{6,14},{7,39},{8,0},{9,41... | collective-permute-start | bytes 1081352 | tf_op jit(solution)/shard_map/ppermute | solution.py:50
  17.8 0.8 copy-done.3
  18.6 0.8 copy-done.4
  19.3 0.8 copy-done.5
  20.1 2.1 %collective-permute-done.5.got2 = bf16[16,11264]{1,0:T(8,128)(2,1)S(1)} collective-permute-done((bf16[16,11264]{1,0:T(8,128)(2,1)S(1)}, bf16[16,11264]{1,0:T(8,128)(2,1)S(1)}, u32[]{:S(2)}, u32[]{:S(2)}) %collective-permute-start.5) | collective-permute-done | bytes 360480 | tf_op jit(solution)/shard_map/ppermute | solution.py:50
  22.2 4.2 %collective-permute-done.6.got1 = bf16[16,11264]{1,0:T(8,128)(2,1)S(1)} collective-permute-done((bf16[16,11264]{1,0:T(8,128)(2,1)S(1)}, bf16[16,11264]{1,0:T(8,128)(2,1)S(1)}, u32[]{:S(2)}, u32[]{:S(2)}) %collective-permute-start.6) | collective-permute-done | bytes 360480 | tf_op jit(solution)/shard_map/ppermute | solution.py:50
  26.6 2.5 %collective-permute-start.11 = (bf16[224,8192]{1,0:T(8,128)(2,1)}, bf16[224,8192]{1,0:T(8,128)(2,1)S(1)}, u32[]{:S(2)}, u32[]{:S(2)}) collective-permute-start(bf16[224,8192]{1,0:T(8,128)(2,1)} %refs_3_), channel_id=1, source_target_pairs={{0,1},{1,0},{2,3},{3,2},{4,5},{5,4},{6,7},{7,6},{8,9},{9,8},{10,11... | collective-permute-start | bytes 11010056 | tf_op jit(solution)/shard_map/ppermute | solution.py:50
  29.1 2.6 %collective-permute-start.12 = (bf16[64,3072]{1,0:T(8,128)(2,1)S(1)}, bf16[64,3072]{1,0:T(8,128)(2,1)S(1)}, u32[]{:S(2)}, u32[]{:S(2)}) collective-permute-start(bf16[64,3072]{1,0:T(8,128)(2,1)S(1)} %get-tuple-element.63.f0), channel_id=1, source_target_pairs={{0,32},{1,9},{2,34},{3,11},{4,36},{5,13},{6,38},{7,15},{8,40},{9,1... | collective-permute-start | bytes 1179656 | tf_op jit(solution)/shard_map/ppermute | solution.py:50
  31.7 0.9 collective-permute-start.10
  32.7 4.9 %collective-permute-done.12.rows = bf16[64,3072]{1,0:T(8,128)(2,1)S(1)} collective-permute-done((bf16[64,3072]{1,0:T(8,128)(2,1)S(1)}, bf16[64,3072]{1,0:T(8,128)(2,1)S(1)}, u32[]{:S(2)}, u32[]{:S(2)}) %collective-permute-start.12) | collective-permute-done | bytes 393248 | tf_op jit(solution)/shard_map/ppermute | solution.py:50
  37.6 15.4 %collective-permute-done.10.refs_3_.packed3.from3 = bf16[64,11264]{1,0:T(8,128)(2,1)S(1)} collective-permute-done((bf16[64,11264]{1,0:T(8,128)(2,1)S(1)}, bf16[64,11264]{1,0:T(8,128)(2,1)S(1)}, u32[]{:S(2)}, u32[]{:S(2)}) %collective-permute-start.10) | collective-permute-done | bytes 1441824 | tf_op jit(solution)/shard_map/ppermute | solution.py:50
  53.1 1.4 %collective-permute-start.13 = (bf16[256,3328]{1,0:T(8,128)(2,1)S(1)}, bf16[256,3328]{1,0:T(8,128)(2,1)S(1)}, u32[]{:S(2)}, u32[]{:S(2)}) collective-permute-start(bf16[256,3328]{1,0:T(8,128)(2,1)S(1)} %shard_map.108.refs_9_), channel_id=1, source_target_pairs={{0,1},{1,0},{2,3},{3,2},{4,5},{5,4},{6,7},{7,6},{8,9},{9,8},{10,11... | collective-permute-start | bytes 5111816 | tf_op jit(solution)/shard_map/ppermute | solution.py:50
  54.6 1.2 %collective-permute-start.16 = (bf16[32,8192]{1,0:T(8,128)(2,1)S(1)}, bf16[32,8192]{1,0:T(8,128)(2,1)S(1)}, u32[]{:S(2)}, u32[]{:S(2)}) collective-permute-start(bf16[32,8192]{1,0:T(8,128)(2,1)S(1)} %get-tuple-element.67), channel_id=1, source_target_pairs={{0,16},{1,5},{2,18},{3,7},{4,20},{5,1},{6,22},{7,3},{8,24},{9,13},... | collective-permute-start | bytes 1572872 | tf_op jit(solution)/shard_map/ppermute | solution.py:50
  55.8 1.7 %collective-permute-start.17 = (bf16[32,8192]{1,0:T(8,128)(2,1)S(1)}, bf16[32,8192]{1,0:T(8,128)(2,1)S(1)}, u32[]{:S(2)}, u32[]{:S(2)}) collective-permute-start(bf16[32,8192]{1,0:T(8,128)(2,1)S(1)} %get-tuple-element.68), channel_id=1, source_target_pairs={{0,48},{1,13},{2,50},{3,15},{4,52},{5,9},{6,54},{7,11},{8,56},{9,5... | collective-permute-start | bytes 1572872 | tf_op jit(solution)/shard_map/ppermute | solution.py:50
  57.6 4.1 %shard_map.106.refs_4_ = f32[896,192]{1,0:T(8,128)S(1)} custom-call(f32[8,128]{1,0:T(8,128)S(1)} %shard_map.105.refs_0_, bf16[64,8192]{1,0:T(8,128)(2,1)S(1)} %get-tuple-element.58.refs_1_, bf16[64,11264]{1,0:T(8,128)(2,1)S(1)} %collective-permute-done.9.refs_2_.packed1.from1, bf16[64,11264]{1,0:T(8,128)(2,1)S(1)} %collective-permute-done.10.refs_3_.packed3.from3, ...), custom_call_target="tpu_custom_call" | custom-call | flops 9200000000 | bytes 28800000 | tf_op jit(solution)/shard_map/pallas_call | solution.py:177
  61.7 5.8 %shard_map.109 = (f32[64,8192]{1,0:T(8,128)S(1)}, bf16[64,8192]{1,0:T(8,128)(2,1)S(1)}, bf16[64,8192]{1,0:T(8,128)(2,1)S(1)}, bf16[128,8192]{1,0:T(8,128)(2,1)S(1)}, bf16[64,8192]{1,0:T(8,128)(2,1)S(1)}) custom-call(s32[5]{0:T(128)S(1)} %stack.23.place.refs_0_, bf16[64,8192]{1,0:T(8,128)(2,1)S(1)} %get-tuple-element.58.refs_1_, ...), custom_call_target="tpu_custom_call" | custom-call | flops 1 | bytes 1 | tf_op jit(solution)/shard_map/pallas_call | solution.py:199
  67.5 0.6 collective-permute-start.14
  68.1 0.7 collective-permute-start.15
  68.8 4.1 %shard_map.112.refs_2_ = f32[896,64]{1,0:T(8,128)S(1)} custom-call(bf16[32,8192]{1,0:T(8,128)(2,1)S(1)} %collective-permute-done.16.refs_0_, bf16[32,8192]{1,0:T(8,128)(2,1)S(1)} %collective-permute-done.17.refs_1_, bf16[224,8192]{1,0:T(8,128)(2,1)S(1)} %copy-done.1, bf16[224,8192]{1,0:T(8,128)(2,1)S(1)} %collective-permute-done.4.refs_5_.refs_3_, ...), custom_call_target="tpu_custom_call" | custom-call | flops 9200000000 | bytes 28800000 | tf_op jit(solution)/shard_map/pallas_call | solution.py:177
  72.9 3.6 %shard_map.113 = bf16[64,8192]{1,0:T(8,128)(2,1)S(1)} custom-call(bf16[32,8192]{1,0:T(8,128)(2,1)S(1)} %collective-permute-done.16.refs_0_, bf16[32,8192]{1,0:T(8,128)(2,1)S(1)} %collective-permute-done.17.refs_1_, f32[896,64]{1,0:T(8,128)S(1)} %shard_map.112.refs_2_, bf16[224,8192]{1,0:T(8,128)(2,1)S(1)} %copy-done, ...), custom_call_target="tpu_custom_call" | custom-call | flops 1 | bytes 1 | tf_op jit(solution)/shard_map/pallas_call | solution.py:199
  76.5 2.3 %collective-permute-start.18 = (bf16[64,8192]{1,0:T(8,128)(2,1)S(1)}, bf16[64,8192]{1,0:T(8,128)(2,1)S(1)}, u32[]{:S(2)}, u32[]{:S(2)}) collective-permute-start(bf16[64,8192]{1,0:T(8,128)(2,1)S(1)} %shard_map.113), channel_id=1, source_target_pairs={{0,32},{1,9},{2,34},{3,11},{4,36},{5,13},{6,38},{7,15},{8,40},{9,1... | collective-permute-start | bytes 3145736 | tf_op jit(solution)/shard_map/ppermute | solution.py:50
  78.7 3.0 %collective-permute-done.14.b1 = bf16[64,8192]{1,0:T(8,128)(2,1)S(1)} collective-permute-done((bf16[64,8192]{1,0:T(8,128)(2,1)S(1)}, bf16[64,8192]{1,0:T(8,128)(2,1)S(1)}, u32[]{:S(2)}, u32[]{:S(2)}) %collective-permute-start.14) | collective-permute-done | bytes 1048608 | tf_op jit(solution)/shard_map/ppermute | solution.py:50
  81.7 12.8 %collective-permute-done.15.b3 = bf16[64,8192]{1,0:T(8,128)(2,1)S(1)} collective-permute-done((bf16[64,8192]{1,0:T(8,128)(2,1)S(1)}, bf16[64,8192]{1,0:T(8,128)(2,1)S(1)}, u32[]{:S(2)}, u32[]{:S(2)}) %collective-permute-start.15) | collective-permute-done | bytes 1048608 | tf_op jit(solution)/shard_map/ppermute | solution.py:50
  95.0 1.5 %collective-permute-start.19 = (bf16[16,8192]{1,0:T(8,128)(2,1)S(1)}, bf16[16,8192]{1,0:T(8,128)(2,1)S(1)}, u32[]{:S(2)}, u32[]{:S(2)}) collective-permute-start(bf16[16,8192]{1,0:T(8,128)(2,1)S(1)} %get-tuple-element.74), channel_id=1, source_target_pairs={{0,8},{1,33},{2,10},{3,35},{4,12},{5,37},{6,14},{7,39},{8,0},{9,41... | collective-permute-start | bytes 786440 | tf_op jit(solution)/shard_map/ppermute | solution.py:50
  96.5 1.2 collective-permute-start.20
  97.7 0.6 collective-permute-start.21
  98.3 3.8 %collective-permute-done.19.b2 = bf16[16,8192]{1,0:T(8,128)(2,1)S(1)} collective-permute-done((bf16[16,8192]{1,0:T(8,128)(2,1)S(1)}, bf16[16,8192]{1,0:T(8,128)(2,1)S(1)}, u32[]{:S(2)}, u32[]{:S(2)}) %collective-permute-start.19) | collective-permute-done | bytes 262176 | tf_op jit(solution)/shard_map/ppermute | solution.py:50
  102.1 2.5 %collective-permute-done.20.b1 = bf16[16,8192]{1,0:T(8,128)(2,1)S(1)} collective-permute-done((bf16[16,8192]{1,0:T(8,128)(2,1)S(1)}, bf16[16,8192]{1,0:T(8,128)(2,1)S(1)}, u32[]{:S(2)}, u32[]{:S(2)}) %collective-permute-start.20) | collective-permute-done | bytes 262176 | tf_op jit(solution)/shard_map/ppermute | solution.py:50
  104.9 0.7 shard_map.115
  105.5 1.3 %collective-permute-start.22 = (bf16[8,4096]{1,0:T(8,128)(2,1)S(1)}, bf16[8,4096]{1,0:T(8,128)(2,1)S(1)}, u32[]{:S(2)}, u32[]{:S(2)}) collective-permute-start(bf16[8,4096]{1,0:T(8,128)(2,1)S(1)} %get-tuple-element.78), channel_id=1, source_target_pairs={{0,64},{1,65},{2,66},{3,67},{4,68},{5,69},{6,70},{7,71},{8,72},{9,... | collective-permute-start | bytes 196616 | tf_op jit(solution)/shard_map/ppermute | solution.py:50
  106.8 1.3 %collective-permute-start.23 = (bf16[8,4096]{1,0:T(8,128)(2,1)S(1)}, bf16[8,4096]{1,0:T(8,128)(2,1)S(1)}, u32[]{:S(2)}, u32[]{:S(2)}) collective-permute-start(bf16[8,4096]{1,0:T(8,128)(2,1)S(1)} %get-tuple-element.79), channel_id=1, source_target_pairs={{0,2},{1,3},{2,0},{3,1},{4,6},{5,7},{6,4},{7,5},{8,10},{9,11},{10,... | collective-permute-start | bytes 196616 | tf_op jit(solution)/shard_map/ppermute | solution.py:50
  108.1 1.7 %collective-permute-start.24 = (bf16[8,4096]{1,0:T(8,128)(2,1)S(1)}, bf16[8,4096]{1,0:T(8,128)(2,1)S(1)}, u32[]{:S(2)}, u32[]{:S(2)}) collective-permute-start(bf16[8,4096]{1,0:T(8,128)(2,1)S(1)} %get-tuple-element.80), channel_id=1, source_target_pairs={{0,66},{1,67},{2,64},{3,65},{4,70},{5,71},{6,68},{7,69},{8,74},{9,... | collective-permute-start | bytes 196616 | tf_op jit(solution)/shard_map/ppermute | solution.py:50
  109.8 0.5 collective-permute-done.22.b2
  110.4 2.0 %collective-permute-done.24.b3 = bf16[8,4096]{1,0:T(8,128)(2,1)S(1)} collective-permute-done((bf16[8,4096]{1,0:T(8,128)(2,1)S(1)}, bf16[8,4096]{1,0:T(8,128)(2,1)S(1)}, u32[]{:S(2)}, u32[]{:S(2)}) %collective-permute-start.24) | collective-permute-done | bytes 65568 | tf_op jit(solution)/shard_map/ppermute | solution.py:50
  112.4 0.6 shard_map.116
  113.0 4.8 %collective-permute-start.25 = (bf16[8,2048]{1,0:T(8,128)(2,1)S(1)}, bf16[8,2048]{1,0:T(8,128)(2,1)S(1)}, u32[]{:S(2)}, u32[]{:S(2)}) collective-permute-start(bf16[8,2048]{1,0:T(8,128)(2,1)S(1)} %get-tuple-element.82), channel_id=1, source_target_pairs={{0,1},{1,0},{2,3},{3,2},{4,5},{5,4},{6,7},{7,6},{8,9},{9,8},{10,11... | collective-permute-start | bytes 98312 | tf_op jit(solution)/shard_map/ppermute | solution.py:50
  117.8 0.9 collective-permute-done.25.got
  118.6 1.2 shard_map.117
  (35 shorter events, 2.4 us)
Async XLA Ops:
  1.5 2.4 %collective-permute-start = (bf16[8,2048]{1,0:T(8,128)(2,1)S(1)}, bf16[8,2048]{1,0:T(8,128)(2,1)S(1)}, u32[]{:S(2)}, u32[]{:S(2)}) collective-permute-start(bf16[8,2048]{1,0:T(8,128)(2,1)S(1)} %get-tuple-element.45), channel_id=1, source_target_pairs={{0,1},{1,0},{2,3},{3,2},{4,5},{5,4},{6,7},{7,6},{8,9},{9,8},{10,11... | collective-permute-start | bytes 98312 | tf_op jit(solution)/shard_map/ppermute | solution.py:50
  4.4 9.6 %collective-permute-start.4 = (bf16[224,8192]{1,0:T(8,128)(2,1)}, bf16[224,8192]{1,0:T(8,128)(2,1)S(1)}, u32[]{:S(2)}, u32[]{:S(2)}) collective-permute-start(bf16[224,8192]{1,0:T(8,128)(2,1)} %refs_2_), channel_id=1, source_target_pairs={{0,1},{1,0},{2,3},{3,2},{4,5},{5,4},{6,7},{7,6},{8,9},{9,8},{10,11... | collective-permute-start | bytes 11010056 | tf_op jit(solution)/shard_map/ppermute | solution.py:50
  4.8 21.8 %collective-permute-start.8 = (bf16[224,8192]{1,0:T(8,128)(2,1)}, bf16[224,8192]{1,0:T(8,128)(2,1)S(1)}, u32[]{:S(2)}, u32[]{:S(2)}) collective-permute-start(bf16[224,8192]{1,0:T(8,128)(2,1)} %refs_4_.1), channel_id=1, source_target_pairs={{0,1},{1,0},{2,3},{3,2},{4,5},{5,4},{6,7},{7,6},{8,9},{9,8},{10,11... | collective-permute-start | bytes 11010056 | tf_op jit(solution)/shard_map/ppermute | solution.py:50
  5.0 8.5 %collective-permute-start.3 = (bf16[16,3584]{1,0:T(8,128)(2,1)S(1)}, bf16[16,3584]{1,0:T(8,128)(2,1)S(1)}, u32[]{:S(2)}, u32[]{:S(2)}) collective-permute-start(bf16[16,3584]{1,0:T(8,128)(2,1)S(1)} %get-tuple-element.48.message), channel_id=1, source_target_pairs={{0,66},{1,67},{2,64},{3,65},{4,70},{5,71},{6,68},{7,69},{8,74},{9,... | collective-permute-start | bytes 344072 | tf_op jit(solution)/shard_map/ppermute | solution.py:50
  8.8 3.4 %collective-permute-start.1 = (bf16[8,4096]{1,0:T(8,128)(2,1)S(1)}, bf16[8,4096]{1,0:T(8,128)(2,1)S(1)}, u32[]{:S(2)}, u32[]{:S(2)}) collective-permute-start(bf16[8,4096]{1,0:T(8,128)(2,1)S(1)} %get-tuple-element.47.wide), channel_id=1, source_target_pairs={{0,2},{1,3},{2,0},{3,1},{4,6},{5,7},{6,4},{7,5},{8,10},{9,11},{10,... | collective-permute-start | bytes 196616 | tf_op jit(solution)/shard_map/ppermute | solution.py:50
  8.8 4.6 %collective-permute-start.2 = (bf16[8,4096]{1,0:T(8,128)(2,1)S(1)}, bf16[8,4096]{1,0:T(8,128)(2,1)S(1)}, u32[]{:S(2)}, u32[]{:S(2)}) collective-permute-start(bf16[8,4096]{1,0:T(8,128)(2,1)S(1)} %get-tuple-element.47.wide), channel_id=1, source_target_pairs={{0,64},{1,65},{2,66},{3,67},{4,68},{5,69},{6,70},{7,71},{8,72},{9,... | collective-permute-start | bytes 196616 | tf_op jit(solution)/shard_map/ppermute | solution.py:50
  14.0 8.2 %collective-permute-start.5 = (bf16[16,11264]{1,0:T(8,128)(2,1)S(1)}, bf16[16,11264]{1,0:T(8,128)(2,1)S(1)}, u32[]{:S(2)}, u32[]{:S(2)}) collective-permute-start(bf16[16,11264]{1,0:T(8,128)(2,1)S(1)} %shard_map.102.own), channel_id=1, source_target_pairs={{0,8},{1,33},{2,10},{3,35},{4,12},{5,37},{6,14},{7,39},{8,0},{9,41... | collective-permute-start | bytes 1081352 | tf_op jit(solution)/shard_map/ppermute | solution.py:50
  17.0 9.4 %collective-permute-start.6 = (bf16[16,11264]{1,0:T(8,128)(2,1)S(1)}, bf16[16,11264]{1,0:T(8,128)(2,1)S(1)}, u32[]{:S(2)}, u32[]{:S(2)}) collective-permute-start(bf16[16,11264]{1,0:T(8,128)(2,1)S(1)} %shard_map.102.own), channel_id=1, source_target_pairs={{0,4},{1,17},{2,6},{3,19},{4,0},{5,21},{6,2},{7,23},{8,12},{9,25},... | collective-permute-start | bytes 1081352 | tf_op jit(solution)/shard_map/ppermute | solution.py:50
  17.4 9.0 %collective-permute-start.7 = (bf16[16,11264]{1,0:T(8,128)(2,1)S(1)}, bf16[16,11264]{1,0:T(8,128)(2,1)S(1)}, u32[]{:S(2)}, u32[]{:S(2)}) collective-permute-start(bf16[16,11264]{1,0:T(8,128)(2,1)S(1)} %shard_map.102.own), channel_id=1, source_target_pairs={{0,12},{1,49},{2,14},{3,51},{4,8},{5,53},{6,10},{7,55},{8,4},{9,57... | collective-permute-start | bytes 1081352 | tf_op jit(solution)/shard_map/ppermute | solution.py:50
  17.8 0.8 copy-start.3
  18.6 0.8 copy-start.4
  19.3 0.8 copy-start.5
  26.6 35.0 %collective-permute-start.11 = (bf16[224,8192]{1,0:T(8,128)(2,1)}, bf16[224,8192]{1,0:T(8,128)(2,1)S(1)}, u32[]{:S(2)}, u32[]{:S(2)}) collective-permute-start(bf16[224,8192]{1,0:T(8,128)(2,1)} %refs_3_), channel_id=1, source_target_pairs={{0,1},{1,0},{2,3},{3,2},{4,5},{5,4},{6,7},{7,6},{8,9},{9,8},{10,11... | collective-permute-start | bytes 11010056 | tf_op jit(solution)/shard_map/ppermute | solution.py:50
  29.1 8.5 %collective-permute-start.12 = (bf16[64,3072]{1,0:T(8,128)(2,1)S(1)}, bf16[64,3072]{1,0:T(8,128)(2,1)S(1)}, u32[]{:S(2)}, u32[]{:S(2)}) collective-permute-start(bf16[64,3072]{1,0:T(8,128)(2,1)S(1)} %get-tuple-element.63.f0), channel_id=1, source_target_pairs={{0,32},{1,9},{2,34},{3,11},{4,36},{5,13},{6,38},{7,15},{8,40},{9,1... | collective-permute-start | bytes 1179656 | tf_op jit(solution)/shard_map/ppermute | solution.py:50
  31.7 21.3 %collective-permute-start.10 = (bf16[64,11264]{1,0:T(8,128)(2,1)S(1)}, bf16[64,11264]{1,0:T(8,128)(2,1)S(1)}, u32[]{:S(2)}, u32[]{:S(2)}) collective-permute-start(bf16[64,11264]{1,0:T(8,128)(2,1)S(1)} %get-tuple-element.59), channel_id=1, source_target_pairs={{0,48},{1,13},{2,50},{3,15},{4,52},{5,9},{6,54},{7,11},{8,56},{9,5... | collective-permute-start | bytes 4325384 | tf_op jit(solution)/shard_map/ppermute | solution.py:50
  32.6 20.3 %collective-permute-start.9 = (bf16[64,11264]{1,0:T(8,128)(2,1)S(1)}, bf16[64,11264]{1,0:T(8,128)(2,1)S(1)}, u32[]{:S(2)}, u32[]{:S(2)}) collective-permute-start(bf16[64,11264]{1,0:T(8,128)(2,1)S(1)} %get-tuple-element.59), channel_id=1, source_target_pairs={{0,16},{1,5},{2,18},{3,7},{4,20},{5,1},{6,22},{7,3},{8,24},{9,13},... | collective-permute-start | bytes 4325384 | tf_op jit(solution)/shard_map/ppermute | solution.py:50
  37.6 16.9 %copy-start.1 = (bf16[224,8192]{1,0:T(8,128)(2,1)S(1)}, bf16[224,8192]{1,0:T(8,128)(2,1)}, u32[]{:S(2)}) copy-start(bf16[224,8192]{1,0:T(8,128)(2,1)} %refs_2_) | copy-start | bytes 11010052
  37.6 16.9 %copy-start.2 = (bf16[224,8192]{1,0:T(8,128)(2,1)S(1)}, bf16[224,8192]{1,0:T(8,128)(2,1)}, u32[]{:S(2)}) copy-start(bf16[224,8192]{1,0:T(8,128)(2,1)} %refs_4_.1) | copy-start | bytes 11010052
  37.6 16.9 %copy-start = (bf16[224,8192]{1,0:T(8,128)(2,1)S(1)}, bf16[224,8192]{1,0:T(8,128)(2,1)}, u32[]{:S(2)}) copy-start(bf16[224,8192]{1,0:T(8,128)(2,1)} %refs_3_) | copy-start | bytes 11010052
  53.1 8.6 %collective-permute-start.13 = (bf16[256,3328]{1,0:T(8,128)(2,1)S(1)}, bf16[256,3328]{1,0:T(8,128)(2,1)S(1)}, u32[]{:S(2)}, u32[]{:S(2)}) collective-permute-start(bf16[256,3328]{1,0:T(8,128)(2,1)S(1)} %shard_map.108.refs_9_), channel_id=1, source_target_pairs={{0,1},{1,0},{2,3},{3,2},{4,5},{5,4},{6,7},{7,6},{8,9},{9,8},{10,11... | collective-permute-start | bytes 5111816 | tf_op jit(solution)/shard_map/ppermute | solution.py:50
  54.6 13.5 %collective-permute-start.16 = (bf16[32,8192]{1,0:T(8,128)(2,1)S(1)}, bf16[32,8192]{1,0:T(8,128)(2,1)S(1)}, u32[]{:S(2)}, u32[]{:S(2)}) collective-permute-start(bf16[32,8192]{1,0:T(8,128)(2,1)S(1)} %get-tuple-element.67), channel_id=1, source_target_pairs={{0,16},{1,5},{2,18},{3,7},{4,20},{5,1},{6,22},{7,3},{8,24},{9,13},... | collective-permute-start | bytes 1572872 | tf_op jit(solution)/shard_map/ppermute | solution.py:50
  55.8 12.3 %collective-permute-start.17 = (bf16[32,8192]{1,0:T(8,128)(2,1)S(1)}, bf16[32,8192]{1,0:T(8,128)(2,1)S(1)}, u32[]{:S(2)}, u32[]{:S(2)}) collective-permute-start(bf16[32,8192]{1,0:T(8,128)(2,1)S(1)} %get-tuple-element.68), channel_id=1, source_target_pairs={{0,48},{1,13},{2,50},{3,15},{4,52},{5,9},{6,54},{7,11},{8,56},{9,5... | collective-permute-start | bytes 1572872 | tf_op jit(solution)/shard_map/ppermute | solution.py:50
  67.5 14.2 %collective-permute-start.14 = (bf16[64,8192]{1,0:T(8,128)(2,1)S(1)}, bf16[64,8192]{1,0:T(8,128)(2,1)S(1)}, u32[]{:S(2)}, u32[]{:S(2)}) collective-permute-start(bf16[64,8192]{1,0:T(8,128)(2,1)S(1)} %get-tuple-element.65), channel_id=1, source_target_pairs={{0,16},{1,5},{2,18},{3,7},{4,20},{5,1},{6,22},{7,3},{8,24},{9,13},... | collective-permute-start | bytes 3145736 | tf_op jit(solution)/shard_map/ppermute | solution.py:50
  68.1 26.4 %collective-permute-start.15 = (bf16[64,8192]{1,0:T(8,128)(2,1)S(1)}, bf16[64,8192]{1,0:T(8,128)(2,1)S(1)}, u32[]{:S(2)}, u32[]{:S(2)}) collective-permute-start(bf16[64,8192]{1,0:T(8,128)(2,1)S(1)} %get-tuple-element.66), channel_id=1, source_target_pairs={{0,48},{1,13},{2,50},{3,15},{4,52},{5,9},{6,54},{7,11},{8,56},{9,5... | collective-permute-start | bytes 3145736 | tf_op jit(solution)/shard_map/ppermute | solution.py:50
  76.5 18.3 %collective-permute-start.18 = (bf16[64,8192]{1,0:T(8,128)(2,1)S(1)}, bf16[64,8192]{1,0:T(8,128)(2,1)S(1)}, u32[]{:S(2)}, u32[]{:S(2)}) collective-permute-start(bf16[64,8192]{1,0:T(8,128)(2,1)S(1)} %shard_map.113), channel_id=1, source_target_pairs={{0,32},{1,9},{2,34},{3,11},{4,36},{5,13},{6,38},{7,15},{8,40},{9,1... | collective-permute-start | bytes 3145736 | tf_op jit(solution)/shard_map/ppermute | solution.py:50
  95.0 7.1 %collective-permute-start.19 = (bf16[16,8192]{1,0:T(8,128)(2,1)S(1)}, bf16[16,8192]{1,0:T(8,128)(2,1)S(1)}, u32[]{:S(2)}, u32[]{:S(2)}) collective-permute-start(bf16[16,8192]{1,0:T(8,128)(2,1)S(1)} %get-tuple-element.74), channel_id=1, source_target_pairs={{0,8},{1,33},{2,10},{3,35},{4,12},{5,37},{6,14},{7,39},{8,0},{9,41... | collective-permute-start | bytes 786440 | tf_op jit(solution)/shard_map/ppermute | solution.py:50
  96.5 8.1 %collective-permute-start.20 = (bf16[16,8192]{1,0:T(8,128)(2,1)S(1)}, bf16[16,8192]{1,0:T(8,128)(2,1)S(1)}, u32[]{:S(2)}, u32[]{:S(2)}) collective-permute-start(bf16[16,8192]{1,0:T(8,128)(2,1)S(1)} %get-tuple-element.75), channel_id=1, source_target_pairs={{0,4},{1,17},{2,6},{3,19},{4,0},{5,21},{6,2},{7,23},{8,12},{9,25},... | collective-permute-start | bytes 786440 | tf_op jit(solution)/shard_map/ppermute | solution.py:50
  97.7 7.2 %collective-permute-start.21 = (bf16[16,8192]{1,0:T(8,128)(2,1)S(1)}, bf16[16,8192]{1,0:T(8,128)(2,1)S(1)}, u32[]{:S(2)}, u32[]{:S(2)}) collective-permute-start(bf16[16,8192]{1,0:T(8,128)(2,1)S(1)} %get-tuple-element.76), channel_id=1, source_target_pairs={{0,12},{1,49},{2,14},{3,51},{4,8},{5,53},{6,10},{7,55},{8,4},{9,57... | collective-permute-start | bytes 786440 | tf_op jit(solution)/shard_map/ppermute | solution.py:50
  105.5 4.7 %collective-permute-start.22 = (bf16[8,4096]{1,0:T(8,128)(2,1)S(1)}, bf16[8,4096]{1,0:T(8,128)(2,1)S(1)}, u32[]{:S(2)}, u32[]{:S(2)}) collective-permute-start(bf16[8,4096]{1,0:T(8,128)(2,1)S(1)} %get-tuple-element.78), channel_id=1, source_target_pairs={{0,64},{1,65},{2,66},{3,67},{4,68},{5,69},{6,70},{7,71},{8,72},{9,... | collective-permute-start | bytes 196616 | tf_op jit(solution)/shard_map/ppermute | solution.py:50
  106.8 3.6 %collective-permute-start.23 = (bf16[8,4096]{1,0:T(8,128)(2,1)S(1)}, bf16[8,4096]{1,0:T(8,128)(2,1)S(1)}, u32[]{:S(2)}, u32[]{:S(2)}) collective-permute-start(bf16[8,4096]{1,0:T(8,128)(2,1)S(1)} %get-tuple-element.79), channel_id=1, source_target_pairs={{0,2},{1,3},{2,0},{3,1},{4,6},{5,7},{6,4},{7,5},{8,10},{9,11},{10,... | collective-permute-start | bytes 196616 | tf_op jit(solution)/shard_map/ppermute | solution.py:50
  108.1 4.3 %collective-permute-start.24 = (bf16[8,4096]{1,0:T(8,128)(2,1)S(1)}, bf16[8,4096]{1,0:T(8,128)(2,1)S(1)}, u32[]{:S(2)}, u32[]{:S(2)}) collective-permute-start(bf16[8,4096]{1,0:T(8,128)(2,1)S(1)} %get-tuple-element.80), channel_id=1, source_target_pairs={{0,66},{1,67},{2,64},{3,65},{4,70},{5,71},{6,68},{7,69},{8,74},{9,... | collective-permute-start | bytes 196616 | tf_op jit(solution)/shard_map/ppermute | solution.py:50
  113.0 5.6 %collective-permute-start.25 = (bf16[8,2048]{1,0:T(8,128)(2,1)S(1)}, bf16[8,2048]{1,0:T(8,128)(2,1)S(1)}, u32[]{:S(2)}, u32[]{:S(2)}) collective-permute-start(bf16[8,2048]{1,0:T(8,128)(2,1)S(1)} %get-tuple-element.82), channel_id=1, source_target_pairs={{0,1},{1,0},{2,3},{3,2},{4,5},{5,4},{6,7},{7,6},{8,9},{9,8},{10,11... | collective-permute-start | bytes 98312 | tf_op jit(solution)/shard_map/ppermute | solution.py:50

commit v11 on v10

--- a/solution.py
+++ b/solution.py
@@ -71,7 +71,7 @@
 
 
 def project_kernel(n, *refs):
-    rows, weights, out = refs[:n], refs[n : n + 4], refs[n + 4]
+    rows, weights, out = refs[:n], refs[n:-1], refs[-1]
     for i in range(WIDTH // TILE):
         tile = slice(i * TILE, (i + 1) * TILE)
         x = jnp.concatenate([r[:, tile] for r in rows], axis=0)
@@ -105,35 +105,18 @@
     return out
 
 
-def down_kernel(n, n_out, place, *refs):
-    rows = refs[:n]
-    acc, down_w, down_w2, seconds, theirs = refs[n : n + 5]
-    if place is None:
-        first, second = refs[n + 5 : n + 7]
-    else:
-        sources = refs[n + 5 : n + 7]
-        first, second = refs[n + 7 + n_out : n + 9 + n_out]
-        homes = shard_homes(place)
-    outs = refs[n + 7 : n + 7 + n_out]
-    hidden = refs[-1]
-
-    def shards_of(learner, to, groups, base):
-        if place is None:
-            return
-        for other, src in enumerate(sources):
-            cols, rows_at, to_at = homes[other]
-            for k in range(groups):
-                piece = src[rows_at[learner % 16], cols[base + k][learner // 16]]
-                to[to_at[k], learner * 256 : learner * 256 + 256] = piece
-
+def low_rows(rows, first, prepare=None):
     low = 0.0
     for i in range(STEPS):
         tile = slice(i * TILE, (i + 1) * TILE)
-        for j in range(PARTS):
-            shards_of(i * PARTS + j, first, 4, 0)
+        if prepare is not None:
+            prepare(i)
         x = jnp.concatenate([r[:, tile] for r in rows], axis=0)
         low += nt(first[:, tile], x)
-
+    return low
+
+
+def finish(acc, low, seconds, theirs, hidden):
     u = (adapter_scale * low).astype(bf16)
     hs, back = [], 0.0
     for half, (ref, c) in enumerate(((seconds, 0), (theirs, 3072))):
@@ -148,14 +131,43 @@
     h = jnp.concatenate([*hs, adapter_scale * back], axis=0)
     hidden[...] = h.T.astype(bf16)
 
+
+def first_down_kernel(
+    place, rows1, rows3, acc, down_w, down_w2, seconds, theirs, factor,
+    out1, out3, first, second, hidden,
+):
+    homes = shard_homes(place)
+
+    def gather(i, to, groups, base):
+        for learner in range(i * PARTS, (i + 1) * PARTS):
+            for src, (cols, rows_at, to_at) in zip((factor, theirs), homes, strict=True):
+                for k in range(groups):
+                    piece = src[rows_at[learner % 16], cols[base + k][learner // 16]]
+                    to[to_at[k], learner * 256 : learner * 256 + 256] = piece
+
+    low = low_rows((rows1, rows3), first, lambda i: gather(i, first, 4, 0))
+    finish(acc[:, :128], low, seconds, theirs, hidden)
     for i in range(STEPS):
         tile = slice(i * TILE, (i + 1) * TILE)
-        for j in range(PARTS):
-            shards_of(i * PARTS + j, second, 2, 4)
+        gather(i, second, 2, 4)
         w = jnp.concatenate([r[:, tile] for r in (down_w, down_w2, second)], axis=0)
         result = nn(hidden[...], w)
-        for k, out in enumerate(outs):
-            out[:, tile] = result[k * 64 : (k + 1) * 64].astype(out.dtype)
+        out1[:, tile] = result[:64].astype(bf16)
+        out3[:, tile] = result[64:].astype(bf16)
+
+
+def last_down_kernel(
+    own, acc, acc2, down_w, down_w2, seconds, theirs, first, second, total, out2, hidden
+):
+    low = jnp.concatenate([low_rows((own,), first), acc2[4 * UNITS :, :]], axis=1)
+    both = jnp.concatenate([acc[:, 128:], acc2[: 4 * UNITS, :]], axis=1)
+    finish(both, low, seconds, theirs, hidden)
+    for i in range(STEPS):
+        tile = slice(i * TILE, (i + 1) * TILE)
+        w = jnp.concatenate([r[:, tile] for r in (down_w, down_w2, second)], axis=0)
+        result = nn(hidden[...], w)
+        total[:, tile] = result[:64]
+        out2[:, tile] = result[64:].astype(bf16)
 
 
 VMEM = pl.BlockSpec(memory_space=pltpu.VMEM)
@@ -172,39 +184,28 @@
     )
 
 
-def project(rows, weights, *extra):
-    n, more = len(rows), len(extra)
+def project(rows, weights, price, *extra):
+    n, more, heights = len(rows), len(extra), sum(w.shape[0] for w in weights)
     return pl.pallas_call(
         lambda *refs: project_kernel(n, *refs[more:]),
-        in_specs=[VMEM] * (more + n + 4),
+        in_specs=[VMEM] * (more + n + len(weights)),
         out_specs=VMEM,
-        out_shape=jax.ShapeDtypeStruct((4 * UNITS, sum(r.shape[0] for r in rows)), f32),
+        out_shape=jax.ShapeDtypeStruct((heights, sum(r.shape[0] for r in rows)), f32),
         compiler_params=pltpu.CompilerParams(vmem_limit_bytes=10 * 1024 * 1024),
-        cost_estimate=price_of(CK),
+        cost_estimate=price,
     )(*extra, *in_vmem([*rows, *weights]))
 
 
-def down(place, rows, acc, weights, seconds, factors, kinds):
-    n = len(rows)
-    theirs = factors[1] if place is not None else seconds[1]
-    operands = in_vmem([*rows, acc, *weights, seconds[0], theirs, *factors])
-    shapes = [((64, WIDTH), kind) for kind in kinds]
-    lead = []
-    n_out = len(kinds)
-    body = lambda *refs: down_kernel(n, n_out, None, *refs)
-    if place is not None:
-        lead = [place]
-        body = lambda *refs: down_kernel(n, n_out, *refs)
-        shapes += [((128, WIDTH), bf16), ((64, WIDTH), bf16)]
+def down(body, shapes, operands, *lead):
     return pl.pallas_call(
         body,
         in_specs=[SMEM] * len(lead) + [VMEM] * len(operands),
         out_specs=[VMEM] * len(shapes),
         out_shape=[jax.ShapeDtypeStruct(s, kind) for s, kind in shapes],
-        scratch_shapes=[pltpu.VMEM((64 * n_out, 512), bf16)],
+        scratch_shapes=[pltpu.VMEM((128, 512), bf16)],
         compiler_params=pltpu.CompilerParams(vmem_limit_bytes=10 * 1024 * 1024),
         cost_estimate=SMALL,
-    )(*lead, *operands)
+    )(*lead, *in_vmem(operands))
 
 
 def local(body, shapes, operands, place=None, price=SMALL, far=(), scratch=()):
@@ -271,18 +272,8 @@
         packed[at, :] = g[...]
 
 
-def rows_kernel(rows, out):
-    out[...] = rows[...]
-
-
-def halves_kernel(from1, from3, to1, to3):
-    to1[...] = from3[:32, :WIDTH]
-    to3[...] = from1[32:, :WIDTH]
-
-
-def relay(from1, from3, routes, shape):
-    to1, to3 = local(halves_kernel, [(shape, bf16)] * 2, (from1, from3))
-    return send(to1, routes[1]), send(to3, routes[3])
+def part_kernel(rows, out):
+    out[...] = rows[:, : out.shape[1]]
 
 
 def touch_kernel(gate_w, up_w, down_w, out):
@@ -330,12 +321,6 @@
         total = own[:, cols] + widen(b1[:, cols])
         total += widen(b2[:, cols]) + widen(b3[:, cols])
         out[...] = total.astype(bf16)
-
-
-def join_kernel(place, keep, got, out):
-    c = place[3]
-    out[c] = keep[...]
-    out[1 - c] = got[...]
 
 
 def shards(
@@ -396,28 +381,31 @@
     frozen = (frozen_gate_weight, frozen_up_weight, frozen_down_weight)
     owned = after(frozen, block)
     down2 = send(owned[2], CORE)
-    (far,) = local(rows_kernel, [((64, 3072), bf16)], (far,), price=price_of(11))
+    (far,) = local(part_kernel, [((64, 3072), bf16)], (far,), price=price_of(11))
     (factor,) = local(
         stack_kernel, [((256, 3072 + 256), bf16)], (factor, packed1, far, packed3, seconds)
     )
     factor2 = send(factor, CORE)
-    rows2 = relay(packed1, packed3, SECOND, (32, WIDTH))
+    (rows3,) = local(part_kernel, [((64, WIDTH), bf16)], (packed3,))
+    rows2 = send(rows3, SECOND[1])
     (touched,) = local(touch_kernel, [((8, 128), f32)], in_vmem(owned))
 
     weights = (owned[0], gate2, owned[1], up2)
     down_weights = (owned[2], down2)
 
-    rows = (block, packed1, packed3)
-    acc = project(rows, weights, touched)
-    total, part1, part3, first, second = down(
-        place, rows, acc, down_weights, (seconds, factor2), (factor, factor2),
-        (f32, bf16, bf16),
+    acc = project((packed1, packed3, block), weights, price_of(CK), touched)
+    part1, part3, first, second = down(
+        first_down_kernel,
+        [((64, WIDTH), bf16)] * 2 + [((128, WIDTH), bf16), ((64, WIDTH), bf16)],
+        (packed1, packed3, acc, *down_weights, seconds, factor2, factor),
+        place,
     )
     back1, back3 = send(part1, SECOND[1]), send(part3, SECOND[3])
-    rows = after(rows2, part1)
-    acc = project(rows, weights)
-    (part2,) = down(
-        None, rows, acc, down_weights, (seconds, factor2), (first, second), (bf16,)
+    acc2 = project((after(rows2, part1),), (*weights, first), SMALL)
+    total, part2 = down(
+        last_down_kernel,
+        [((64, WIDTH), f32), ((64, WIDTH), bf16)],
+        (block, acc, acc2, *down_weights, seconds, factor2, first, second),
     )
     back2 = send(part2, SECOND[2])
     (total,) = local(
@@ -434,10 +422,8 @@
     b1, b2, b3 = (send(p, ALONG_Z[k]) for k, p in zip((1, 2, 3), parts, strict=True))
     small = [((8, QUARTER), bf16)] * 2
     keep, give = local(last_kernel, small, (done, b2, b1, b3), place)
-    (out,) = local(
-        join_kernel, [((2, 8, QUARTER), bf16)], (keep, send(give, CORE)), place
-    )
-    return out
+    got = send(give, CORE)
+    return jnp.where(c == 0, jnp.stack([keep, got]), jnp.stack([got, keep]))
 
 
 def solution(mesh):

time: 120 us -> 117 us (0.975)
  Pallas kernels: 23.3 us -> 21 us
  starting transfers between devices: 37.2 us -> 35.8 us
    pallas_call x2, Pallas kernels: 9.41 us -> 7.66 us  [down(): pl.pallas_call(body, in_specs=[SMEM] * len(lead) + [VMEM] * len(operands)...]
    ppermute x26 -> x25, starting transfers between devices: 37.2 us -> 35.8 us  [send(): return lax.ppermute(value, AXES, route)]
    pallas_call x14 -> x13, Pallas kernels: 5.78 us -> 4.66 us  [local(): pl.pallas_call(body, in_specs=[SMEM] * len(lead) + [VMEM] * len(operands)...]
    ppermute x26 -> x25, waiting for transfers between devices: 56.8 us -> 56.8 us  [send(): return lax.ppermute(value, AXES, route)]
  transfers between devices with their start and end apart: 26 -> 25, of which waited for: 16 -> 16; matrix products, arithmetic and copies ran while one was open for 0% -> 0% of each run, Pallas kernels for 16% -> 15%
where the time goes in v11:
time: 117 us
  waiting for transfers between devices  56.8 us (49%)
  starting transfers between devices  35.8 us (31%)
  Pallas kernels  21 us (18%)
  local copies, waits for them, and re-layouts  2.37 us (2%)
    ppermute x25, waiting for transfers between devices, send(): return lax.ppermute(value, AXES, route)  56.8 us
    ppermute x25, starting transfers between devices, send(): return lax.ppermute(value, AXES, route)  35.8 us
    pallas_call x2, Pallas kernels, project(): pl.pallas_call(lambda *refs: project_kernel(n, *refs[more:]), in_specs=[V...  8.68 us
    pallas_call x2, Pallas kernels, down(): pl.pallas_call(body, in_specs=[SMEM] * len(lead) + [VMEM] * len(operands)...  7.66 us
    pallas_call x13, Pallas kernels, local(): pl.pallas_call(body, in_specs=[SMEM] * len(lead) + [VMEM] * len(operands)...  4.66 us
  transfers between devices with their start and end apart: 25, of which 16 were waited for; matrix products, arithmetic and copies ran while one was open for 0% of the time, Pallas kernels for 15%

profile of v11, /device:TPU:1, one launch (start us, length us, event | category | flops | bytes accessed | tf_op | source)
XLA Modules:
  0.0 116.8 jit_solution(3081047752480492863)
XLA Ops:
  0.1 1.4 %shard_map.100 = (bf16[8,2048]{1,0:T(8,128)(2,1)S(1)}, bf16[8,2048]{1,0:T(8,128)(2,1)S(1)}, bf16[16,1536]{1,0:T(8,128)(2,1)S(1)}) custom-call(s32[5]{0:T(128)S(1)} %stack.37.place, bf16[2,8,2048]{2,1,0:T(8,128)(2,1)} %inputs.1, bf16[64,256]{1,0:T(8,128)(2,1)} %gate.1, bf16[64,256]{1,0:T(8,128)(2,1)} %up.1, bf16[64,256]{1,0:T(8,128)(2,1)} %down.1), custom_call_target="tpu_custom_call" | custom-call | flops 1 | bytes 1 | tf_op jit(solution)/shard_map/pallas_call | solution.py:213
  1.5 1.5 %collective-permute-start = (bf16[8,2048]{1,0:T(8,128)(2,1)S(1)}, bf16[8,2048]{1,0:T(8,128)(2,1)S(1)}, u32[]{:S(2)}, u32[]{:S(2)}) collective-permute-start(bf16[8,2048]{1,0:T(8,128)(2,1)S(1)} %get-tuple-element.43), channel_id=1, source_target_pairs={{0,1},{1,0},{2,3},{3,2},{4,5},{5,4},{6,7},{7,6},{8,9},{9,8},{10,11... | collective-permute-start | bytes 98312 | tf_op jit(solution)/shard_map/ppermute | solution.py:50
  3.0 0.9 collective-permute-done.other
  3.8 0.6 shard_map.101
  4.4 0.4 collective-permute-start.4
  5.0 3.8 %collective-permute-start.3 = (bf16[16,3584]{1,0:T(8,128)(2,1)S(1)}, bf16[16,3584]{1,0:T(8,128)(2,1)S(1)}, u32[]{:S(2)}, u32[]{:S(2)}) collective-permute-start(bf16[16,3584]{1,0:T(8,128)(2,1)S(1)} %get-tuple-element.46.message), channel_id=1, source_target_pairs={{0,66},{1,67},{2,64},{3,65},{4,70},{5,71},{6,68},{7,69},{8,74},{9,... | collective-permute-start | bytes 344072 | tf_op jit(solution)/shard_map/ppermute | solution.py:50
  8.8 1.2 %collective-permute-start.2 = (bf16[8,4096]{1,0:T(8,128)(2,1)S(1)}, bf16[8,4096]{1,0:T(8,128)(2,1)S(1)}, u32[]{:S(2)}, u32[]{:S(2)}) collective-permute-start(bf16[8,4096]{1,0:T(8,128)(2,1)S(1)} %get-tuple-element.45.wide), channel_id=1, source_target_pairs={{0,64},{1,65},{2,66},{3,67},{4,68},{5,69},{6,70},{7,71},{8,72},{9,... | collective-permute-start | bytes 196616 | tf_op jit(solution)/shard_map/ppermute | solution.py:50
  10.0 2.2 %collective-permute-done.1.z1 = bf16[8,4096]{1,0:T(8,128)(2,1)S(1)} collective-permute-done((bf16[8,4096]{1,0:T(8,128)(2,1)S(1)}, bf16[8,4096]{1,0:T(8,128)(2,1)S(1)}, u32[]{:S(2)}, u32[]{:S(2)}) %collective-permute-start.1) | collective-permute-done | bytes 65568 | tf_op jit(solution)/shard_map/ppermute | solution.py:50
  12.2 1.2 %collective-permute-done.2.z2 = bf16[8,4096]{1,0:T(8,128)(2,1)S(1)} collective-permute-done((bf16[8,4096]{1,0:T(8,128)(2,1)S(1)}, bf16[8,4096]{1,0:T(8,128)(2,1)S(1)}, u32[]{:S(2)}, u32[]{:S(2)}) %collective-permute-start.2) | collective-permute-done | bytes 65568 | tf_op jit(solution)/shard_map/ppermute | solution.py:50
  13.5 0.6 shard_map.102.own
  14.0 3.0 %collective-permute-start.5 = (bf16[16,11264]{1,0:T(8,128)(2,1)S(1)}, bf16[16,11264]{1,0:T(8,128)(2,1)S(1)}, u32[]{:S(2)}, u32[]{:S(2)}) collective-permute-start(bf16[16,11264]{1,0:T(8,128)(2,1)S(1)} %shard_map.102.own), channel_id=1, source_target_pairs={{0,8},{1,33},{2,10},{3,35},{4,12},{5,37},{6,14},{7,39},{8,0},{9,41... | collective-permute-start | bytes 1081352 | tf_op jit(solution)/shard_map/ppermute | solution.py:50
  17.0 0.4 collective-permute-start.6
  17.8 0.8 copy-done.3
  18.6 0.8 copy-done.4
  19.3 0.8 copy-done.5
  20.1 2.1 %collective-permute-done.5.got2 = bf16[16,11264]{1,0:T(8,128)(2,1)S(1)} collective-permute-done((bf16[16,11264]{1,0:T(8,128)(2,1)S(1)}, bf16[16,11264]{1,0:T(8,128)(2,1)S(1)}, u32[]{:S(2)}, u32[]{:S(2)}) %collective-permute-start.5) | collective-permute-done | bytes 360480 | tf_op jit(solution)/shard_map/ppermute | solution.py:50
  22.2 4.2 %collective-permute-done.6.got1 = bf16[16,11264]{1,0:T(8,128)(2,1)S(1)} collective-permute-done((bf16[16,11264]{1,0:T(8,128)(2,1)S(1)}, bf16[16,11264]{1,0:T(8,128)(2,1)S(1)}, u32[]{:S(2)}, u32[]{:S(2)}) %collective-permute-start.6) | collective-permute-done | bytes 360480 | tf_op jit(solution)/shard_map/ppermute | solution.py:50
  26.6 2.5 %collective-permute-start.12 = (bf16[224,8192]{1,0:T(8,128)(2,1)}, bf16[224,8192]{1,0:T(8,128)(2,1)S(1)}, u32[]{:S(2)}, u32[]{:S(2)}) collective-permute-start(bf16[224,8192]{1,0:T(8,128)(2,1)} %down_w.2), channel_id=1, source_target_pairs={{0,1},{1,0},{2,3},{3,2},{4,5},{5,4},{6,7},{7,6},{8,9},{9,8},{10,11... | collective-permute-start | bytes 11010056 | tf_op jit(solution)/shard_map/ppermute | solution.py:50
  29.1 2.6 %collective-permute-start.13 = (bf16[64,3072]{1,0:T(8,128)(2,1)S(1)}, bf16[64,3072]{1,0:T(8,128)(2,1)S(1)}, u32[]{:S(2)}, u32[]{:S(2)}) collective-permute-start(bf16[64,3072]{1,0:T(8,128)(2,1)S(1)} %get-tuple-element.61.f0), channel_id=1, source_target_pairs={{0,32},{1,9},{2,34},{3,11},{4,36},{5,13},{6,38},{7,15},{8,40},{9,1... | collective-permute-start | bytes 1179656 | tf_op jit(solution)/shard_map/ppermute | solution.py:50
  31.7 0.9 collective-permute-start.10
  32.7 4.9 %collective-permute-done.13.rows = bf16[64,3072]{1,0:T(8,128)(2,1)S(1)} collective-permute-done((bf16[64,3072]{1,0:T(8,128)(2,1)S(1)}, bf16[64,3072]{1,0:T(8,128)(2,1)S(1)}, u32[]{:S(2)}, u32[]{:S(2)}) %collective-permute-start.13) | collective-permute-done | bytes 393248 | tf_op jit(solution)/shard_map/ppermute | solution.py:50
  37.6 15.4 %collective-permute-done.10.refs_2_.rows.packed3.rows3 = bf16[64,11264]{1,0:T(8,128)(2,1)S(1)} collective-permute-done((bf16[64,11264]{1,0:T(8,128)(2,1)S(1)}, bf16[64,11264]{1,0:T(8,128)(2,1)S(1)}, u32[]{:S(2)}, u32[]{:S(2)}) %collective-permute-start.10) | collective-permute-done | bytes 1441824 | tf_op jit(solution)/shard_map/ppermute | solution.py:50
  53.1 1.4 %collective-permute-start.14 = (bf16[256,3328]{1,0:T(8,128)(2,1)S(1)}, bf16[256,3328]{1,0:T(8,128)(2,1)S(1)}, u32[]{:S(2)}, u32[]{:S(2)}) collective-permute-start(bf16[256,3328]{1,0:T(8,128)(2,1)S(1)} %shard_map.109.factor), channel_id=1, source_target_pairs={{0,1},{1,0},{2,3},{3,2},{4,5},{5,4},{6,7},{7,6},{8,9},{9,8},{10,11... | collective-permute-start | bytes 5111816 | tf_op jit(solution)/shard_map/ppermute | solution.py:50
  54.6 1.2 %collective-permute-start.11 = (bf16[64,8192]{1,0:T(8,128)(2,1)S(1)}, bf16[64,8192]{1,0:T(8,128)(2,1)S(1)}, u32[]{:S(2)}, u32[]{:S(2)}) collective-permute-start(bf16[64,8192]{1,0:T(8,128)(2,1)S(1)} %shard_map.107), channel_id=1, source_target_pairs={{0,16},{1,5},{2,18},{3,7},{4,20},{5,1},{6,22},{7,3},{8,24},{9,13},... | collective-permute-start | bytes 3145736 | tf_op jit(solution)/shard_map/ppermute | solution.py:50
  55.8 4.0 %shard_map.106.acc = f32[896,192]{1,0:T(8,128)S(1)} custom-call(f32[8,128]{1,0:T(8,128)S(1)} %shard_map.105.refs_0_, bf16[64,11264]{1,0:T(8,128)(2,1)S(1)} %collective-permute-done.9.refs_1_.packed1.rows1, bf16[64,11264]{1,0:T(8,128)(2,1)S(1)} %collective-permute-done.10.refs_2_.rows.packed3.rows3, bf16[64,8192]{1,0:T(8,128)(2,1)S(1)} %get-tuple-element.56.refs_3_.own, ...), custom_call_target="tpu_custom_call" | custom-call | flops 9200000000 | bytes 28800000 | tf_op jit(solution)/shard_map/pallas_call | solution.py:189
  59.9 4.3 %shard_map.110 = (bf16[64,8192]{1,0:T(8,128)(2,1)S(1)}, bf16[64,8192]{1,0:T(8,128)(2,1)S(1)}, bf16[128,8192]{1,0:T(8,128)(2,1)S(1)}, bf16[64,8192]{1,0:T(8,128)(2,1)S(1)}) custom-call(s32[5]{0:T(128)S(1)} %stack.37.place, bf16[64,11264]{1,0:T(8,128)(2,1)S(1)} %collective-permute-done.9.refs_1_.packed1.rows1, ...), custom_call_target="tpu_custom_call" | custom-call | flops 1 | bytes 1 | tf_op jit(solution)/shard_map/pallas_call | solution.py:200
  64.3 0.4 collective-permute-start.15
  64.6 2.3 %collective-permute-start.16 = (bf16[64,8192]{1,0:T(8,128)(2,1)S(1)}, bf16[64,8192]{1,0:T(8,128)(2,1)S(1)}, u32[]{:S(2)}, u32[]{:S(2)}) collective-permute-start(bf16[64,8192]{1,0:T(8,128)(2,1)S(1)} %get-tuple-element.67), channel_id=1, source_target_pairs={{0,48},{1,13},{2,50},{3,15},{4,52},{5,9},{6,54},{7,11},{8,56},{9,5... | collective-permute-start | bytes 3145736 | tf_op jit(solution)/shard_map/ppermute | solution.py:50
  67.0 1.6 %collective-permute-done.11.refs_0_ = bf16[64,8192]{1,0:T(8,128)(2,1)S(1)} collective-permute-done((bf16[64,8192]{1,0:T(8,128)(2,1)S(1)}, bf16[64,8192]{1,0:T(8,128)(2,1)S(1)}, u32[]{:S(2)}, u32[]{:S(2)}) %collective-permute-start.11) | collective-permute-done | bytes 1048608 | tf_op jit(solution)/shard_map/ppermute | solution.py:50
  68.6 4.6 %shard_map.111.acc2 = f32[1024,64]{1,0:T(8,128)S(1)} custom-call(bf16[64,8192]{1,0:T(8,128)(2,1)S(1)} %collective-permute-done.11.refs_0_, bf16[224,8192]{1,0:T(8,128)(2,1)S(1)} %copy-done.1, bf16[224,8192]{1,0:T(8,128)(2,1)S(1)} %collective-permute-done.4.refs_5_.refs_2_, bf16[224,8192]{1,0:T(8,128)(2,1)S(1)} %copy-done.2, ...), custom_call_target="tpu_custom_call" | custom-call | flops 1 | bytes 1 | tf_op jit(solution)/shard_map/pallas_call | solution.py:189
  73.3 3.3 %shard_map.112 = (f32[64,8192]{1,0:T(8,128)S(1)}, bf16[64,8192]{1,0:T(8,128)(2,1)S(1)}) custom-call(bf16[64,8192]{1,0:T(8,128)(2,1)S(1)} %get-tuple-element.56.refs_3_.own, f32[896,192]{1,0:T(8,128)S(1)} %shard_map.106.acc, f32[1024,64]{1,0:T(8,128)S(1)} %shard_map.111.acc2, bf16[224,8192]{1,0:T(8,128)(2,1)S(1)} %copy-done, ...), custom_call_target="tpu_custom_call" | custom-call | flops 1 | bytes 1 | tf_op jit(solution)/shard_map/pallas_call | solution.py:200
  76.6 2.7 %collective-permute-start.17 = (bf16[64,8192]{1,0:T(8,128)(2,1)S(1)}, bf16[64,8192]{1,0:T(8,128)(2,1)S(1)}, u32[]{:S(2)}, u32[]{:S(2)}) collective-permute-start(bf16[64,8192]{1,0:T(8,128)(2,1)S(1)} %get-tuple-element.68), channel_id=1, source_target_pairs={{0,32},{1,9},{2,34},{3,11},{4,36},{5,13},{6,38},{7,15},{8,40},{9,1... | collective-permute-start | bytes 3145736 | tf_op jit(solution)/shard_map/ppermute | solution.py:50
  79.3 0.6 collective-permute-done.15.b1
  80.2 13.0 %collective-permute-done.17.b = bf16[64,8192]{1,0:T(8,128)(2,1)S(1)} collective-permute-done((bf16[64,8192]{1,0:T(8,128)(2,1)S(1)}, bf16[64,8192]{1,0:T(8,128)(2,1)S(1)}, u32[]{:S(2)}, u32[]{:S(2)}) %collective-permute-start.17) | collective-permute-done | bytes 1048608 | tf_op jit(solution)/shard_map/ppermute | solution.py:50
  93.3 1.5 %collective-permute-start.18 = (bf16[16,8192]{1,0:T(8,128)(2,1)S(1)}, bf16[16,8192]{1,0:T(8,128)(2,1)S(1)}, u32[]{:S(2)}, u32[]{:S(2)}) collective-permute-start(bf16[16,8192]{1,0:T(8,128)(2,1)S(1)} %get-tuple-element.70), channel_id=1, source_target_pairs={{0,8},{1,33},{2,10},{3,35},{4,12},{5,37},{6,14},{7,39},{8,0},{9,41... | collective-permute-start | bytes 786440 | tf_op jit(solution)/shard_map/ppermute | solution.py:50
  94.9 1.5 %collective-permute-start.19 = (bf16[16,8192]{1,0:T(8,128)(2,1)S(1)}, bf16[16,8192]{1,0:T(8,128)(2,1)S(1)}, u32[]{:S(2)}, u32[]{:S(2)}) collective-permute-start(bf16[16,8192]{1,0:T(8,128)(2,1)S(1)} %get-tuple-element.71), channel_id=1, source_target_pairs={{0,4},{1,17},{2,6},{3,19},{4,0},{5,21},{6,2},{7,23},{8,12},{9,25},... | collective-permute-start | bytes 786440 | tf_op jit(solution)/shard_map/ppermute | solution.py:50
  96.7 3.8 %collective-permute-done.18.b2 = bf16[16,8192]{1,0:T(8,128)(2,1)S(1)} collective-permute-done((bf16[16,8192]{1,0:T(8,128)(2,1)S(1)}, bf16[16,8192]{1,0:T(8,128)(2,1)S(1)}, u32[]{:S(2)}, u32[]{:S(2)}) %collective-permute-start.18) | collective-permute-done | bytes 262176 | tf_op jit(solution)/shard_map/ppermute | solution.py:50
  100.4 2.8 %collective-permute-done.19.b1 = bf16[16,8192]{1,0:T(8,128)(2,1)S(1)} collective-permute-done((bf16[16,8192]{1,0:T(8,128)(2,1)S(1)}, bf16[16,8192]{1,0:T(8,128)(2,1)S(1)}, u32[]{:S(2)}, u32[]{:S(2)}) %collective-permute-start.19) | collective-permute-done | bytes 262176 | tf_op jit(solution)/shard_map/ppermute | solution.py:50
  103.2 0.7 shard_map.115
  103.9 1.3 %collective-permute-start.21 = (bf16[8,4096]{1,0:T(8,128)(2,1)S(1)}, bf16[8,4096]{1,0:T(8,128)(2,1)S(1)}, u32[]{:S(2)}, u32[]{:S(2)}) collective-permute-start(bf16[8,4096]{1,0:T(8,128)(2,1)S(1)} %get-tuple-element.74), channel_id=1, source_target_pairs={{0,64},{1,65},{2,66},{3,67},{4,68},{5,69},{6,70},{7,71},{8,72},{9,... | collective-permute-start | bytes 196616 | tf_op jit(solution)/shard_map/ppermute | solution.py:50
  105.2 1.3 %collective-permute-start.22 = (bf16[8,4096]{1,0:T(8,128)(2,1)S(1)}, bf16[8,4096]{1,0:T(8,128)(2,1)S(1)}, u32[]{:S(2)}, u32[]{:S(2)}) collective-permute-start(bf16[8,4096]{1,0:T(8,128)(2,1)S(1)} %get-tuple-element.75), channel_id=1, source_target_pairs={{0,2},{1,3},{2,0},{3,1},{4,6},{5,7},{6,4},{7,5},{8,10},{9,11},{10,... | collective-permute-start | bytes 196616 | tf_op jit(solution)/shard_map/ppermute | solution.py:50
  106.5 1.7 %collective-permute-start.23 = (bf16[8,4096]{1,0:T(8,128)(2,1)S(1)}, bf16[8,4096]{1,0:T(8,128)(2,1)S(1)}, u32[]{:S(2)}, u32[]{:S(2)}) collective-permute-start(bf16[8,4096]{1,0:T(8,128)(2,1)S(1)} %get-tuple-element.76), channel_id=1, source_target_pairs={{0,66},{1,67},{2,64},{3,65},{4,70},{5,71},{6,68},{7,69},{8,74},{9,... | collective-permute-start | bytes 196616 | tf_op jit(solution)/shard_map/ppermute | solution.py:50
  108.1 0.5 collective-permute-done.21.b2
  108.8 2.6 %collective-permute-done.23.b3 = bf16[8,4096]{1,0:T(8,128)(2,1)S(1)} collective-permute-done((bf16[8,4096]{1,0:T(8,128)(2,1)S(1)}, bf16[8,4096]{1,0:T(8,128)(2,1)S(1)}, u32[]{:S(2)}, u32[]{:S(2)}) %collective-permute-start.23) | collective-permute-done | bytes 65568 | tf_op jit(solution)/shard_map/ppermute | solution.py:50
  111.4 0.6 shard_map.116
  112.0 3.3 %collective-permute-start.24 = (bf16[8,2048]{1,0:T(8,128)(2,1)S(1)}, bf16[8,2048]{1,0:T(8,128)(2,1)S(1)}, u32[]{:S(2)}, u32[]{:S(2)}) collective-permute-start(bf16[8,2048]{1,0:T(8,128)(2,1)S(1)} %get-tuple-element.78), channel_id=1, source_target_pairs={{0,1},{1,0},{2,3},{3,2},{4,5},{5,4},{6,7},{7,6},{8,9},{9,8},{10,11... | collective-permute-start | bytes 98312 | tf_op jit(solution)/shard_map/ppermute | solution.py:50
  115.3 0.9 collective-permute-done.24
  116.2 0.6 maximum_select_fusion
  (33 shorter events, 2.1 us)
Async XLA Ops:
  1.5 2.4 %collective-permute-start = (bf16[8,2048]{1,0:T(8,128)(2,1)S(1)}, bf16[8,2048]{1,0:T(8,128)(2,1)S(1)}, u32[]{:S(2)}, u32[]{:S(2)}) collective-permute-start(bf16[8,2048]{1,0:T(8,128)(2,1)S(1)} %get-tuple-element.43), channel_id=1, source_target_pairs={{0,1},{1,0},{2,3},{3,2},{4,5},{5,4},{6,7},{7,6},{8,9},{9,8},{10,11... | collective-permute-start | bytes 98312 | tf_op jit(solution)/shard_map/ppermute | solution.py:50
  4.4 9.6 %collective-permute-start.4 = (bf16[224,8192]{1,0:T(8,128)(2,1)}, bf16[224,8192]{1,0:T(8,128)(2,1)S(1)}, u32[]{:S(2)}, u32[]{:S(2)}) collective-permute-start(bf16[224,8192]{1,0:T(8,128)(2,1)} %refs_1_), channel_id=1, source_target_pairs={{0,1},{1,0},{2,3},{3,2},{4,5},{5,4},{6,7},{7,6},{8,9},{9,8},{10,11... | collective-permute-start | bytes 11010056 | tf_op jit(solution)/shard_map/ppermute | solution.py:50
  4.8 21.8 %collective-permute-start.8 = (bf16[224,8192]{1,0:T(8,128)(2,1)}, bf16[224,8192]{1,0:T(8,128)(2,1)S(1)}, u32[]{:S(2)}, u32[]{:S(2)}) collective-permute-start(bf16[224,8192]{1,0:T(8,128)(2,1)} %refs_3_), channel_id=1, source_target_pairs={{0,1},{1,0},{2,3},{3,2},{4,5},{5,4},{6,7},{7,6},{8,9},{9,8},{10,11... | collective-permute-start | bytes 11010056 | tf_op jit(solution)/shard_map/ppermute | solution.py:50
  5.0 8.5 %collective-permute-start.3 = (bf16[16,3584]{1,0:T(8,128)(2,1)S(1)}, bf16[16,3584]{1,0:T(8,128)(2,1)S(1)}, u32[]{:S(2)}, u32[]{:S(2)}) collective-permute-start(bf16[16,3584]{1,0:T(8,128)(2,1)S(1)} %get-tuple-element.46.message), channel_id=1, source_target_pairs={{0,66},{1,67},{2,64},{3,65},{4,70},{5,71},{6,68},{7,69},{8,74},{9,... | collective-permute-start | bytes 344072 | tf_op jit(solution)/shard_map/ppermute | solution.py:50
  8.8 3.4 %collective-permute-start.1 = (bf16[8,4096]{1,0:T(8,128)(2,1)S(1)}, bf16[8,4096]{1,0:T(8,128)(2,1)S(1)}, u32[]{:S(2)}, u32[]{:S(2)}) collective-permute-start(bf16[8,4096]{1,0:T(8,128)(2,1)S(1)} %get-tuple-element.45.wide), channel_id=1, source_target_pairs={{0,2},{1,3},{2,0},{3,1},{4,6},{5,7},{6,4},{7,5},{8,10},{9,11},{10,... | collective-permute-start | bytes 196616 | tf_op jit(solution)/shard_map/ppermute | solution.py:50
  8.8 4.6 %collective-permute-start.2 = (bf16[8,4096]{1,0:T(8,128)(2,1)S(1)}, bf16[8,4096]{1,0:T(8,128)(2,1)S(1)}, u32[]{:S(2)}, u32[]{:S(2)}) collective-permute-start(bf16[8,4096]{1,0:T(8,128)(2,1)S(1)} %get-tuple-element.45.wide), channel_id=1, source_target_pairs={{0,64},{1,65},{2,66},{3,67},{4,68},{5,69},{6,70},{7,71},{8,72},{9,... | collective-permute-start | bytes 196616 | tf_op jit(solution)/shard_map/ppermute | solution.py:50
  14.0 8.2 %collective-permute-start.5 = (bf16[16,11264]{1,0:T(8,128)(2,1)S(1)}, bf16[16,11264]{1,0:T(8,128)(2,1)S(1)}, u32[]{:S(2)}, u32[]{:S(2)}) collective-permute-start(bf16[16,11264]{1,0:T(8,128)(2,1)S(1)} %shard_map.102.own), channel_id=1, source_target_pairs={{0,8},{1,33},{2,10},{3,35},{4,12},{5,37},{6,14},{7,39},{8,0},{9,41... | collective-permute-start | bytes 1081352 | tf_op jit(solution)/shard_map/ppermute | solution.py:50
  17.0 9.4 %collective-permute-start.6 = (bf16[16,11264]{1,0:T(8,128)(2,1)S(1)}, bf16[16,11264]{1,0:T(8,128)(2,1)S(1)}, u32[]{:S(2)}, u32[]{:S(2)}) collective-permute-start(bf16[16,11264]{1,0:T(8,128)(2,1)S(1)} %shard_map.102.own), channel_id=1, source_target_pairs={{0,4},{1,17},{2,6},{3,19},{4,0},{5,21},{6,2},{7,23},{8,12},{9,25},... | collective-permute-start | bytes 1081352 | tf_op jit(solution)/shard_map/ppermute | solution.py:50
  17.4 9.0 %collective-permute-start.7 = (bf16[16,11264]{1,0:T(8,128)(2,1)S(1)}, bf16[16,11264]{1,0:T(8,128)(2,1)S(1)}, u32[]{:S(2)}, u32[]{:S(2)}) collective-permute-start(bf16[16,11264]{1,0:T(8,128)(2,1)S(1)} %shard_map.102.own), channel_id=1, source_target_pairs={{0,12},{1,49},{2,14},{3,51},{4,8},{5,53},{6,10},{7,55},{8,4},{9,57... | collective-permute-start | bytes 1081352 | tf_op jit(solution)/shard_map/ppermute | solution.py:50
  17.8 0.8 copy-start.3
  18.6 0.8 copy-start.4
  19.3 0.8 copy-start.5
  26.6 33.3 %collective-permute-start.12 = (bf16[224,8192]{1,0:T(8,128)(2,1)}, bf16[224,8192]{1,0:T(8,128)(2,1)S(1)}, u32[]{:S(2)}, u32[]{:S(2)}) collective-permute-start(bf16[224,8192]{1,0:T(8,128)(2,1)} %down_w.2), channel_id=1, source_target_pairs={{0,1},{1,0},{2,3},{3,2},{4,5},{5,4},{6,7},{7,6},{8,9},{9,8},{10,11... | collective-permute-start | bytes 11010056 | tf_op jit(solution)/shard_map/ppermute | solution.py:50
  29.1 8.5 %collective-permute-start.13 = (bf16[64,3072]{1,0:T(8,128)(2,1)S(1)}, bf16[64,3072]{1,0:T(8,128)(2,1)S(1)}, u32[]{:S(2)}, u32[]{:S(2)}) collective-permute-start(bf16[64,3072]{1,0:T(8,128)(2,1)S(1)} %get-tuple-element.61.f0), channel_id=1, source_target_pairs={{0,32},{1,9},{2,34},{3,11},{4,36},{5,13},{6,38},{7,15},{8,40},{9,1... | collective-permute-start | bytes 1179656 | tf_op jit(solution)/shard_map/ppermute | solution.py:50
  31.7 21.3 %collective-permute-start.10 = (bf16[64,11264]{1,0:T(8,128)(2,1)S(1)}, bf16[64,11264]{1,0:T(8,128)(2,1)S(1)}, u32[]{:S(2)}, u32[]{:S(2)}) collective-permute-start(bf16[64,11264]{1,0:T(8,128)(2,1)S(1)} %get-tuple-element.60), channel_id=1, source_target_pairs={{0,48},{1,13},{2,50},{3,15},{4,52},{5,9},{6,54},{7,11},{8,56},{9,5... | collective-permute-start | bytes 4325384 | tf_op jit(solution)/shard_map/ppermute | solution.py:50
  32.6 20.3 %collective-permute-start.9 = (bf16[64,11264]{1,0:T(8,128)(2,1)S(1)}, bf16[64,11264]{1,0:T(8,128)(2,1)S(1)}, u32[]{:S(2)}, u32[]{:S(2)}) collective-permute-start(bf16[64,11264]{1,0:T(8,128)(2,1)S(1)} %get-tuple-element.60), channel_id=1, source_target_pairs={{0,16},{1,5},{2,18},{3,7},{4,20},{5,1},{6,22},{7,3},{8,24},{9,13},... | collective-permute-start | bytes 4325384 | tf_op jit(solution)/shard_map/ppermute | solution.py:50
  37.6 16.9 %copy-start.1 = (bf16[224,8192]{1,0:T(8,128)(2,1)S(1)}, bf16[224,8192]{1,0:T(8,128)(2,1)}, u32[]{:S(2)}) copy-start(bf16[224,8192]{1,0:T(8,128)(2,1)} %refs_1_) | copy-start | bytes 11010052
  37.6 16.9 %copy-start.2 = (bf16[224,8192]{1,0:T(8,128)(2,1)S(1)}, bf16[224,8192]{1,0:T(8,128)(2,1)}, u32[]{:S(2)}) copy-start(bf16[224,8192]{1,0:T(8,128)(2,1)} %refs_3_) | copy-start | bytes 11010052
  37.6 16.9 %copy-start = (bf16[224,8192]{1,0:T(8,128)(2,1)S(1)}, bf16[224,8192]{1,0:T(8,128)(2,1)}, u32[]{:S(2)}) copy-start(bf16[224,8192]{1,0:T(8,128)(2,1)} %down_w.2) | copy-start | bytes 11010052
  53.1 6.8 %collective-permute-start.14 = (bf16[256,3328]{1,0:T(8,128)(2,1)S(1)}, bf16[256,3328]{1,0:T(8,128)(2,1)S(1)}, u32[]{:S(2)}, u32[]{:S(2)}) collective-permute-start(bf16[256,3328]{1,0:T(8,128)(2,1)S(1)} %shard_map.109.factor), channel_id=1, source_target_pairs={{0,1},{1,0},{2,3},{3,2},{4,5},{5,4},{6,7},{7,6},{8,9},{9,8},{10,11... | collective-permute-start | bytes 5111816 | tf_op jit(solution)/shard_map/ppermute | solution.py:50
  54.6 14.0 %collective-permute-start.11 = (bf16[64,8192]{1,0:T(8,128)(2,1)S(1)}, bf16[64,8192]{1,0:T(8,128)(2,1)S(1)}, u32[]{:S(2)}, u32[]{:S(2)}) collective-permute-start(bf16[64,8192]{1,0:T(8,128)(2,1)S(1)} %shard_map.107), channel_id=1, source_target_pairs={{0,16},{1,5},{2,18},{3,7},{4,20},{5,1},{6,22},{7,3},{8,24},{9,13},... | collective-permute-start | bytes 3145736 | tf_op jit(solution)/shard_map/ppermute | solution.py:50
  64.3 15.6 %collective-permute-start.15 = (bf16[64,8192]{1,0:T(8,128)(2,1)S(1)}, bf16[64,8192]{1,0:T(8,128)(2,1)S(1)}, u32[]{:S(2)}, u32[]{:S(2)}) collective-permute-start(bf16[64,8192]{1,0:T(8,128)(2,1)S(1)} %get-tuple-element.62), channel_id=1, source_target_pairs={{0,16},{1,5},{2,18},{3,7},{4,20},{5,1},{6,22},{7,3},{8,24},{9,13},... | collective-permute-start | bytes 3145736 | tf_op jit(solution)/shard_map/ppermute | solution.py:50
  64.6 15.2 %collective-permute-start.16 = (bf16[64,8192]{1,0:T(8,128)(2,1)S(1)}, bf16[64,8192]{1,0:T(8,128)(2,1)S(1)}, u32[]{:S(2)}, u32[]{:S(2)}) collective-permute-start(bf16[64,8192]{1,0:T(8,128)(2,1)S(1)} %get-tuple-element.67), channel_id=1, source_target_pairs={{0,48},{1,13},{2,50},{3,15},{4,52},{5,9},{6,54},{7,11},{8,56},{9,5... | collective-permute-start | bytes 3145736 | tf_op jit(solution)/shard_map/ppermute | solution.py:50
  76.6 16.6 %collective-permute-start.17 = (bf16[64,8192]{1,0:T(8,128)(2,1)S(1)}, bf16[64,8192]{1,0:T(8,128)(2,1)S(1)}, u32[]{:S(2)}, u32[]{:S(2)}) collective-permute-start(bf16[64,8192]{1,0:T(8,128)(2,1)S(1)} %get-tuple-element.68), channel_id=1, source_target_pairs={{0,32},{1,9},{2,34},{3,11},{4,36},{5,13},{6,38},{7,15},{8,40},{9,1... | collective-permute-start | bytes 3145736 | tf_op jit(solution)/shard_map/ppermute | solution.py:50
  93.3 7.1 %collective-permute-start.18 = (bf16[16,8192]{1,0:T(8,128)(2,1)S(1)}, bf16[16,8192]{1,0:T(8,128)(2,1)S(1)}, u32[]{:S(2)}, u32[]{:S(2)}) collective-permute-start(bf16[16,8192]{1,0:T(8,128)(2,1)S(1)} %get-tuple-element.70), channel_id=1, source_target_pairs={{0,8},{1,33},{2,10},{3,35},{4,12},{5,37},{6,14},{7,39},{8,0},{9,41... | collective-permute-start | bytes 786440 | tf_op jit(solution)/shard_map/ppermute | solution.py:50
  94.9 8.4 %collective-permute-start.19 = (bf16[16,8192]{1,0:T(8,128)(2,1)S(1)}, bf16[16,8192]{1,0:T(8,128)(2,1)S(1)}, u32[]{:S(2)}, u32[]{:S(2)}) collective-permute-start(bf16[16,8192]{1,0:T(8,128)(2,1)S(1)} %get-tuple-element.71), channel_id=1, source_target_pairs={{0,4},{1,17},{2,6},{3,19},{4,0},{5,21},{6,2},{7,23},{8,12},{9,25},... | collective-permute-start | bytes 786440 | tf_op jit(solution)/shard_map/ppermute | solution.py:50
  96.3 6.9 %collective-permute-start.20 = (bf16[16,8192]{1,0:T(8,128)(2,1)S(1)}, bf16[16,8192]{1,0:T(8,128)(2,1)S(1)}, u32[]{:S(2)}, u32[]{:S(2)}) collective-permute-start(bf16[16,8192]{1,0:T(8,128)(2,1)S(1)} %get-tuple-element.72), channel_id=1, source_target_pairs={{0,12},{1,49},{2,14},{3,51},{4,8},{5,53},{6,10},{7,55},{8,4},{9,57... | collective-permute-start | bytes 786440 | tf_op jit(solution)/shard_map/ppermute | solution.py:50
  103.9 4.7 %collective-permute-start.21 = (bf16[8,4096]{1,0:T(8,128)(2,1)S(1)}, bf16[8,4096]{1,0:T(8,128)(2,1)S(1)}, u32[]{:S(2)}, u32[]{:S(2)}) collective-permute-start(bf16[8,4096]{1,0:T(8,128)(2,1)S(1)} %get-tuple-element.74), channel_id=1, source_target_pairs={{0,64},{1,65},{2,66},{3,67},{4,68},{5,69},{6,70},{7,71},{8,72},{9,... | collective-permute-start | bytes 196616 | tf_op jit(solution)/shard_map/ppermute | solution.py:50
  105.2 3.6 %collective-permute-start.22 = (bf16[8,4096]{1,0:T(8,128)(2,1)S(1)}, bf16[8,4096]{1,0:T(8,128)(2,1)S(1)}, u32[]{:S(2)}, u32[]{:S(2)}) collective-permute-start(bf16[8,4096]{1,0:T(8,128)(2,1)S(1)} %get-tuple-element.75), channel_id=1, source_target_pairs={{0,2},{1,3},{2,0},{3,1},{4,6},{5,7},{6,4},{7,5},{8,10},{9,11},{10,... | collective-permute-start | bytes 196616 | tf_op jit(solution)/shard_map/ppermute | solution.py:50
  106.5 4.9 %collective-permute-start.23 = (bf16[8,4096]{1,0:T(8,128)(2,1)S(1)}, bf16[8,4096]{1,0:T(8,128)(2,1)S(1)}, u32[]{:S(2)}, u32[]{:S(2)}) collective-permute-start(bf16[8,4096]{1,0:T(8,128)(2,1)S(1)} %get-tuple-element.76), channel_id=1, source_target_pairs={{0,66},{1,67},{2,64},{3,65},{4,70},{5,71},{6,68},{7,69},{8,74},{9,... | collective-permute-start | bytes 196616 | tf_op jit(solution)/shard_map/ppermute | solution.py:50
  112.0 4.2 %collective-permute-start.24 = (bf16[8,2048]{1,0:T(8,128)(2,1)S(1)}, bf16[8,2048]{1,0:T(8,128)(2,1)S(1)}, u32[]{:S(2)}, u32[]{:S(2)}) collective-permute-start(bf16[8,2048]{1,0:T(8,128)(2,1)S(1)} %get-tuple-element.78), channel_id=1, source_target_pairs={{0,1},{1,0},{2,3},{3,2},{4,5},{5,4},{6,7},{7,6},{8,9},{9,8},{10,11... | collective-permute-start | bytes 98312 | tf_op jit(solution)/shard_map/ppermute | solution.py:50

commit v12 on v11

--- a/solution.py
+++ b/solution.py
@@ -18,7 +18,7 @@
 STEPS = WIDTH // TILE
 PARTS = TILE // 256
 f32, bf16 = jnp.float32, jnp.bfloat16
-CK = 8
+CK, CU = 8, 2
 SMALL = pl.CostEstimate(flops=1, bytes_accessed=1, transcendentals=0)
 
 
@@ -133,8 +133,8 @@
 
 
 def first_down_kernel(
-    place, rows1, rows3, acc, down_w, down_w2, seconds, theirs, factor,
-    out1, out3, first, second, hidden,
+    place, own1, rest1, own3, rest3, own, got1, got2, got3, acc, down_w, down_w2, seconds,
+    theirs, factor, out1, out3, total, first, second, hidden,
 ):
     homes = shard_homes(place)
 
@@ -145,29 +145,25 @@
                     piece = src[rows_at[learner % 16], cols[base + k][learner // 16]]
                     to[to_at[k], learner * 256 : learner * 256 + 256] = piece
 
-    low = low_rows((rows1, rows3), first, lambda i: gather(i, first, 4, 0))
-    finish(acc[:, :128], low, seconds, theirs, hidden)
+    rows = (own1, rest1, own3, rest3, own, got1, got2, got3)
+    low = low_rows(rows, first, lambda i: gather(i, first, 4, 0))
+    finish(acc, low, seconds, theirs, hidden)
     for i in range(STEPS):
         tile = slice(i * TILE, (i + 1) * TILE)
         gather(i, second, 2, 4)
         w = jnp.concatenate([r[:, tile] for r in (down_w, down_w2, second)], axis=0)
         result = nn(hidden[...], w)
         out1[:, tile] = result[:64].astype(bf16)
-        out3[:, tile] = result[64:].astype(bf16)
-
-
-def last_down_kernel(
-    own, acc, acc2, down_w, down_w2, seconds, theirs, first, second, total, out2, hidden
-):
-    low = jnp.concatenate([low_rows((own,), first), acc2[4 * UNITS :, :]], axis=1)
-    both = jnp.concatenate([acc[:, 128:], acc2[: 4 * UNITS, :]], axis=1)
-    finish(both, low, seconds, theirs, hidden)
+        out3[:, tile] = result[64:128].astype(bf16)
+        total[:, tile] = result[128:]
+
+
+def last_down_kernel(acc, down_w, down_w2, seconds, theirs, second, out2, hidden):
+    finish(acc[: 4 * UNITS, :], acc[4 * UNITS :, :], seconds, theirs, hidden)
     for i in range(STEPS):
         tile = slice(i * TILE, (i + 1) * TILE)
         w = jnp.concatenate([r[:, tile] for r in (down_w, down_w2, second)], axis=0)
-        result = nn(hidden[...], w)
-        total[:, tile] = result[:64]
-        out2[:, tile] = result[64:].astype(bf16)
+        out2[:, tile] = nn(hidden[...], w).astype(bf16)
 
 
 VMEM = pl.BlockSpec(memory_space=pltpu.VMEM)
@@ -196,13 +192,13 @@
     )(*extra, *in_vmem([*rows, *weights]))
 
 
-def down(body, shapes, operands, *lead):
+def down(body, m, shapes, operands, *lead):
     return pl.pallas_call(
         body,
         in_specs=[SMEM] * len(lead) + [VMEM] * len(operands),
         out_specs=[VMEM] * len(shapes),
         out_shape=[jax.ShapeDtypeStruct(s, kind) for s, kind in shapes],
-        scratch_shapes=[pltpu.VMEM((128, 512), bf16)],
+        scratch_shapes=[pltpu.VMEM((m, 512), bf16)],
         compiler_params=pltpu.CompilerParams(vmem_limit_bytes=10 * 1024 * 1024),
         cost_estimate=SMALL,
     )(*lead, *in_vmem(operands))
@@ -264,16 +260,18 @@
         out[:, at + 256 : at + 512] = far_message[:, col : col + 256]
 
 
-def unpack_kernel(own, got2, got1, got3, block, factor, packed):
+def unpack_kernel(own, got2, got1, got3, factor, packed):
     for k, g in enumerate((own, got1, got2, got3)):
-        at = slice(16 * k, 16 * k + 16)
-        block[at, :] = g[:, :WIDTH]
-        factor[at, :] = g[:, WIDTH:]
-        packed[at, :] = g[...]
-
-
-def part_kernel(rows, out):
-    out[...] = rows[:, : out.shape[1]]
+        factor[16 * k : 16 * k + 16, :] = g[:, WIDTH:]
+        if k:
+            packed[16 * k - 16 : 16 * k, :] = g[...]
+
+
+def part_kernel(*refs):
+    at, out = 0, refs[-1]
+    for r in refs[:-1]:
+        out[at : at + r.shape[0], :] = r[:, : out.shape[1]]
+        at += r.shape[0]
 
 
 def touch_kernel(gate_w, up_w, down_w, out):
@@ -286,9 +284,11 @@
         out[64 * k : 64 * k + 64, :UNITS] = r[...]
 
 
-def stack_kernel(f0, packed1, f2, packed3, seconds, out):
-    for k, r in enumerate((f0, packed1, f2, packed3)):
-        out[64 * k : 64 * k + 64, :3072] = r[:, -3072:]
+def stack_kernel(f0, own1, rest1, f2, own3, rest3, seconds, out):
+    at = 0
+    for r in (f0, own1, rest1, f2, own3, rest3):
+        out[at : at + r.shape[0], :3072] = r[:, -3072:]
+        at += r.shape[0]
     out[:, 3072:] = seconds[...]
 
 
@@ -358,54 +358,62 @@
         send(v, ALONG_Z[k]) for k, v in ((1, wide), (2, wide), (3, message))
     )
     gate2 = send(after(frozen_gate_weight, wide), CORE)
-    up2 = send(after(frozen_up_weight, wide), CORE)
     (packed,) = local(
         pack_kernel, [((16, WIDTH + 3072), bf16)], (wide, z1, z2, message, z3), place
     )
 
     packed = after(packed, gate2)
+    own = packed
     got = {k: send(packed, FIRST[k]) for k in (1, 2, 3)}
     seconds = (adapter_second_gate, adapter_second_up, adapter_first_down)
     (seconds,) = local(
         seconds_kernel, [((256, 256), bf16)], [a.T for a in after(seconds, packed)]
     )
-    block, factor, packed = local(
+    factor, packed = local(
         unpack_kernel,
-        [((64, WIDTH), bf16), ((64, 3072), bf16), ((64, WIDTH + 3072), bf16)],
-        (packed, got[2], got[1], got[3]),
-    )
-
-    block, factor, packed = after((block, factor, packed), (up2, seconds))
+        [((64, 3072), bf16), ((48, WIDTH + 3072), bf16)],
+        (own, got[2], got[1], got[3]),
+        price=price_of(CU),
+    )
+
+    own1, own3 = send(own, SECOND[1]), send(own, SECOND[3])
+    factor, packed = after((factor, packed), (own1, own3, seconds))
     far = send(factor, SECOND[2])
-    packed1, packed3 = send(packed, SECOND[1]), send(packed, SECOND[3])
+    rest1, rest3 = send(packed, SECOND[1]), send(packed, SECOND[3])
     frozen = (frozen_gate_weight, frozen_up_weight, frozen_down_weight)
-    owned = after(frozen, block)
-    down2 = send(owned[2], CORE)
+    owned = after(frozen, packed)
+    up2, down2 = send(owned[1], CORE), send(owned[2], CORE)
     (far,) = local(part_kernel, [((64, 3072), bf16)], (far,), price=price_of(11))
     (factor,) = local(
-        stack_kernel, [((256, 3072 + 256), bf16)], (factor, packed1, far, packed3, seconds)
+        stack_kernel,
+        [((256, 3072 + 256), bf16)],
+        (factor, own1, rest1, far, own3, rest3, seconds),
     )
     factor2 = send(factor, CORE)
-    (rows3,) = local(part_kernel, [((64, WIDTH), bf16)], (packed3,))
+    (rows3,) = local(part_kernel, [((64, WIDTH), bf16)], (own3, rest3))
     rows2 = send(rows3, SECOND[1])
     (touched,) = local(touch_kernel, [((8, 128), f32)], in_vmem(owned))
 
     weights = (owned[0], gate2, owned[1], up2)
     down_weights = (owned[2], down2)
 
-    acc = project((packed1, packed3, block), weights, price_of(CK), touched)
-    part1, part3, first, second = down(
+    rows = (own1, rest1, own3, rest3, own, got[1], got[2], got[3])
+    acc = project(rows, weights, price_of(CK), touched)
+    part1, part3, total, first, second = down(
         first_down_kernel,
-        [((64, WIDTH), bf16)] * 2 + [((128, WIDTH), bf16), ((64, WIDTH), bf16)],
-        (packed1, packed3, acc, *down_weights, seconds, factor2, factor),
+        192,
+        [((64, WIDTH), bf16)] * 2
+        + [((64, WIDTH), f32), ((128, WIDTH), bf16), ((64, WIDTH), bf16)],
+        (*rows, acc, *down_weights, seconds, factor2, factor),
         place,
     )
     back1, back3 = send(part1, SECOND[1]), send(part3, SECOND[3])
-    acc2 = project((after(rows2, part1),), (*weights, first), SMALL)
-    total, part2 = down(
+    acc = project((after(rows2, part1),), (*weights, first), SMALL)
+    (part2,) = down(
         last_down_kernel,
-        [((64, WIDTH), f32), ((64, WIDTH), bf16)],
-        (block, acc, acc2, *down_weights, seconds, factor2, first, second),
+        64,
+        [((64, WIDTH), bf16)],
+        (acc, *down_weights, seconds, factor2, second),
     )
     back2 = send(part2, SECOND[2])
     (total,) = local(

time: 117 us -> 118 us (level)
  starting transfers between devices: 35.8 us -> 38 us
  waiting for transfers between devices: 56.8 us -> 55.2 us
    ppermute x25 -> x27, starting transfers between devices: 35.8 us -> 38 us  [send(): return lax.ppermute(value, AXES, route)]
    ppermute x25 -> x27, waiting for transfers between devices: 56.8 us -> 55.2 us  [send(): return lax.ppermute(value, AXES, route)]
  transfers between devices with their start and end apart: 25 -> 27, of which waited for: 16 -> 17; matrix products, arithmetic and copies ran while one was open for 0% -> 0% of each run, Pallas kernels for 15% -> 15%
where the time goes in v12:
time: 118 us; the launch traced here: 117 us
  waiting for transfers between devices  55.2 us (47%)
  starting transfers between devices  38 us (32%)
  Pallas kernels  21.1 us (18%)
  local copies, waits for them, and re-layouts  2.37 us (2%)
    ppermute x27, waiting for transfers between devices, send(): return lax.ppermute(value, AXES, route)  55.2 us
    ppermute x27, starting transfers between devices, send(): return lax.ppermute(value, AXES, route)  38 us
    pallas_call x2, Pallas kernels, project(): pl.pallas_call(lambda *refs: project_kernel(n, *refs[more:]), in_specs=[V...  8.7 us
    pallas_call x2, Pallas kernels, down(): pl.pallas_call(body, in_specs=[SMEM] * len(lead) + [VMEM] * len(operands)...  7.84 us
    pallas_call x13, Pallas kernels, local(): pl.pallas_call(body, in_specs=[SMEM] * len(lead) + [VMEM] * len(operands)...  4.55 us
  transfers between devices with their start and end apart: 27, of which 17 were waited for; matrix products, arithmetic and copies ran while one was open for 0% of the time, Pallas kernels for 15%

profile of v12, /device:TPU:1, one launch (start us, length us, event | category | flops | bytes accessed | tf_op | source)
XLA Modules:
  0.0 117.5 jit_solution(5788373696244301798)
XLA Ops:
  0.1 1.4 %shard_map.100 = (bf16[8,2048]{1,0:T(8,128)(2,1)S(1)}, bf16[8,2048]{1,0:T(8,128)(2,1)S(1)}, bf16[16,1536]{1,0:T(8,128)(2,1)S(1)}) custom-call(s32[5]{0:T(128)S(1)} %stack.37.place, bf16[2,8,2048]{2,1,0:T(8,128)(2,1)} %inputs.1, bf16[64,256]{1,0:T(8,128)(2,1)} %gate.1, bf16[64,256]{1,0:T(8,128)(2,1)} %up.1, bf16[64,256]{1,0:T(8,128)(2,1)} %down.1), custom_call_target="tpu_custom_call" | custom-call | flops 1 | bytes 1 | tf_op jit(solution)/shard_map/pallas_call | solution.py:209
  1.5 1.5 %collective-permute-start = (bf16[8,2048]{1,0:T(8,128)(2,1)S(1)}, bf16[8,2048]{1,0:T(8,128)(2,1)S(1)}, u32[]{:S(2)}, u32[]{:S(2)}) collective-permute-start(bf16[8,2048]{1,0:T(8,128)(2,1)S(1)} %get-tuple-element.39), channel_id=1, source_target_pairs={{0,1},{1,0},{2,3},{3,2},{4,5},{5,4},{6,7},{7,6},{8,9},{9,8},{10,11... | collective-permute-start | bytes 98312 | tf_op jit(solution)/shard_map/ppermute | solution.py:50
  3.0 0.9 collective-permute-done.other
  3.8 0.6 shard_map.101
  4.4 0.4 collective-permute-start.4
  4.8 3.8 %collective-permute-start.3 = (bf16[16,3584]{1,0:T(8,128)(2,1)S(1)}, bf16[16,3584]{1,0:T(8,128)(2,1)S(1)}, u32[]{:S(2)}, u32[]{:S(2)}) collective-permute-start(bf16[16,3584]{1,0:T(8,128)(2,1)S(1)} %get-tuple-element.42.message), channel_id=1, source_target_pairs={{0,66},{1,67},{2,64},{3,65},{4,70},{5,71},{6,68},{7,69},{8,74},{9,... | collective-permute-start | bytes 344072 | tf_op jit(solution)/shard_map/ppermute | solution.py:50
  8.7 1.2 %collective-permute-start.2 = (bf16[8,4096]{1,0:T(8,128)(2,1)S(1)}, bf16[8,4096]{1,0:T(8,128)(2,1)S(1)}, u32[]{:S(2)}, u32[]{:S(2)}) collective-permute-start(bf16[8,4096]{1,0:T(8,128)(2,1)S(1)} %get-tuple-element.41.wide), channel_id=1, source_target_pairs={{0,64},{1,65},{2,66},{3,67},{4,68},{5,69},{6,70},{7,71},{8,72},{9,... | collective-permute-start | bytes 196616 | tf_op jit(solution)/shard_map/ppermute | solution.py:50
  9.8 2.2 %collective-permute-done.1.z1 = bf16[8,4096]{1,0:T(8,128)(2,1)S(1)} collective-permute-done((bf16[8,4096]{1,0:T(8,128)(2,1)S(1)}, bf16[8,4096]{1,0:T(8,128)(2,1)S(1)}, u32[]{:S(2)}, u32[]{:S(2)}) %collective-permute-start.1) | collective-permute-done | bytes 65568 | tf_op jit(solution)/shard_map/ppermute | solution.py:50
  12.1 1.2 %collective-permute-done.2.z2 = bf16[8,4096]{1,0:T(8,128)(2,1)S(1)} collective-permute-done((bf16[8,4096]{1,0:T(8,128)(2,1)S(1)}, bf16[8,4096]{1,0:T(8,128)(2,1)S(1)}, u32[]{:S(2)}, u32[]{:S(2)}) %collective-permute-start.2) | collective-permute-done | bytes 65568 | tf_op jit(solution)/shard_map/ppermute | solution.py:50
  13.3 0.6 shard_map.102.own.refs_5_
  13.9 3.0 %collective-permute-start.6 = (bf16[16,11264]{1,0:T(8,128)(2,1)S(1)}, bf16[16,11264]{1,0:T(8,128)(2,1)S(1)}, u32[]{:S(2)}, u32[]{:S(2)}) collective-permute-start(bf16[16,11264]{1,0:T(8,128)(2,1)S(1)} %shard_map.102.own.refs_5_), channel_id=1, source_target_pairs={{0,8},{1,33},{2,10},{3,35},{4,12},{5,37},{6,14},{7,39},{8,0},{9,41... | collective-permute-start | bytes 1081352 | tf_op jit(solution)/shard_map/ppermute | solution.py:50
  17.6 1.2 %collective-permute-start.5 = (bf16[16,11264]{1,0:T(8,128)(2,1)S(1)}, bf16[16,11264]{1,0:T(8,128)(2,1)S(1)}, u32[]{:S(2)}, u32[]{:S(2)}) collective-permute-start(bf16[16,11264]{1,0:T(8,128)(2,1)S(1)} %shard_map.102.own.refs_5_), channel_id=1, source_target_pairs={{0,16},{1,5},{2,18},{3,7},{4,20},{5,1},{6,22},{7,3},{8,24},{9,13},... | collective-permute-start | bytes 1081352 | tf_op jit(solution)/shard_map/ppermute | solution.py:50
  18.9 1.8 %collective-permute-start.9 = (bf16[16,11264]{1,0:T(8,128)(2,1)S(1)}, bf16[16,11264]{1,0:T(8,128)(2,1)S(1)}, u32[]{:S(2)}, u32[]{:S(2)}) collective-permute-start(bf16[16,11264]{1,0:T(8,128)(2,1)S(1)} %shard_map.102.own.refs_5_), channel_id=1, source_target_pairs={{0,48},{1,13},{2,50},{3,15},{4,52},{5,9},{6,54},{7,11},{8,56},{9,5... | collective-permute-start | bytes 1081352 | tf_op jit(solution)/shard_map/ppermute | solution.py:50
  20.7 0.8 copy-done.3
  21.4 0.8 copy-done.4
  22.2 0.8 copy-done.5
  23.0 6.6 %collective-permute-done.7.got1.refs_6_ = bf16[16,11264]{1,0:T(8,128)(2,1)S(1)} collective-permute-done((bf16[16,11264]{1,0:T(8,128)(2,1)S(1)}, bf16[16,11264]{1,0:T(8,128)(2,1)S(1)}, u32[]{:S(2)}, u32[]{:S(2)}) %collective-permute-start.7) | collective-permute-done | bytes 360480 | tf_op jit(solution)/shard_map/ppermute | solution.py:50
  29.7 1.8 %collective-permute-done.9.refs_3_.own3.refs_0_ = bf16[16,11264]{1,0:T(8,128)(2,1)S(1)} collective-permute-done((bf16[16,11264]{1,0:T(8,128)(2,1)S(1)}, bf16[16,11264]{1,0:T(8,128)(2,1)S(1)}, u32[]{:S(2)}, u32[]{:S(2)}) %collective-permute-start.9) | collective-permute-done | bytes 360480 | tf_op jit(solution)/shard_map/ppermute | solution.py:50
  31.5 1.0 collective-permute-start.12
  32.6 3.1 %collective-permute-start.14 = (bf16[64,3072]{1,0:T(8,128)(2,1)S(1)}, bf16[64,3072]{1,0:T(8,128)(2,1)S(1)}, u32[]{:S(2)}, u32[]{:S(2)}) collective-permute-start(bf16[64,3072]{1,0:T(8,128)(2,1)S(1)} %get-tuple-element.54.f0), channel_id=1, source_target_pairs={{0,32},{1,9},{2,34},{3,11},{4,36},{5,13},{6,38},{7,15},{8,40},{9,1... | collective-permute-start | bytes 1179656 | tf_op jit(solution)/shard_map/ppermute | solution.py:50
  35.7 0.4 collective-permute-start.11
  36.2 5.0 %collective-permute-done.14.refs_0_ = bf16[64,3072]{1,0:T(8,128)(2,1)S(1)} collective-permute-done((bf16[64,3072]{1,0:T(8,128)(2,1)S(1)}, bf16[64,3072]{1,0:T(8,128)(2,1)S(1)}, u32[]{:S(2)}, u32[]{:S(2)}) %collective-permute-start.14) | collective-permute-done | bytes 393248 | tf_op jit(solution)/shard_map/ppermute | solution.py:50
  41.2 11.6 %collective-permute-done.10.refs_2_.rest1 = bf16[48,11264]{1,0:T(8,128)(2,1)S(1)} collective-permute-done((bf16[48,11264]{1,0:T(8,128)(2,1)S(1)}, bf16[48,11264]{1,0:T(8,128)(2,1)S(1)}, u32[]{:S(2)}, u32[]{:S(2)}) %collective-permute-start.10) | collective-permute-done | bytes 1081376 | tf_op jit(solution)/shard_map/ppermute | solution.py:50
  53.0 1.5 %collective-permute-start.15 = (bf16[256,3328]{1,0:T(8,128)(2,1)S(1)}, bf16[256,3328]{1,0:T(8,128)(2,1)S(1)}, u32[]{:S(2)}, u32[]{:S(2)}) collective-permute-start(bf16[256,3328]{1,0:T(8,128)(2,1)S(1)} %shard_map.108.factor), channel_id=1, source_target_pairs={{0,1},{1,0},{2,3},{3,2},{4,5},{5,4},{6,7},{7,6},{8,9},{9,8},{10,11... | collective-permute-start | bytes 5111816 | tf_op jit(solution)/shard_map/ppermute | solution.py:50
  54.5 1.4 %collective-permute-start.18 = (bf16[64,8192]{1,0:T(8,128)(2,1)S(1)}, bf16[64,8192]{1,0:T(8,128)(2,1)S(1)}, u32[]{:S(2)}, u32[]{:S(2)}) collective-permute-start(bf16[64,8192]{1,0:T(8,128)(2,1)S(1)} %shard_map.111), channel_id=1, source_target_pairs={{0,16},{1,5},{2,18},{3,7},{4,20},{5,1},{6,22},{7,3},{8,24},{9,13},... | collective-permute-start | bytes 3145736 | tf_op jit(solution)/shard_map/ppermute | solution.py:50
  55.9 4.0 %shard_map.106.acc = f32[896,192]{1,0:T(8,128)S(1)} custom-call(f32[8,128]{1,0:T(8,128)S(1)} %shard_map.105.refs_0_, bf16[16,11264]{1,0:T(8,128)(2,1)S(1)} %collective-permute-done.5.refs_1_.own1, bf16[48,11264]{1,0:T(8,128)(2,1)S(1)} %collective-permute-done.10.refs_2_.rest1, bf16[16,11264]{1,0:T(8,128)(2,1)S(1)} %collective-permute-done.9.refs_3_.own3.refs_0_, ...), custom_call_target="tpu_custom_call" | custom-call | flops 9200000000 | bytes 28800000 | tf_op jit(solution)/shard_map/pallas_call | solution.py:185
  60.0 5.8 %shard_map.109 = (bf16[64,8192]{1,0:T(8,128)(2,1)S(1)}, bf16[64,8192]{1,0:T(8,128)(2,1)S(1)}, f32[64,8192]{1,0:T(8,128)S(1)}, bf16[128,8192]{1,0:T(8,128)(2,1)S(1)}, bf16[64,8192]{1,0:T(8,128)(2,1)S(1)}) custom-call(s32[5]{0:T(128)S(1)} %stack.37.place, bf16[16,11264]{1,0:T(8,128)(2,1)S(1)} %collective-permute-done.5.refs_1_.own1, ...), custom_call_target="tpu_custom_call" | custom-call | flops 1 | bytes 1 | tf_op jit(solution)/shard_map/pallas_call | solution.py:196
  65.9 0.4 collective-permute-start.16
  66.3 2.7 %collective-permute-start.17 = (bf16[64,8192]{1,0:T(8,128)(2,1)S(1)}, bf16[64,8192]{1,0:T(8,128)(2,1)S(1)}, u32[]{:S(2)}, u32[]{:S(2)}) collective-permute-start(bf16[64,8192]{1,0:T(8,128)(2,1)S(1)} %get-tuple-element.57), channel_id=1, source_target_pairs={{0,48},{1,13},{2,50},{3,15},{4,52},{5,9},{6,54},{7,11},{8,56},{9,5... | collective-permute-start | bytes 3145736 | tf_op jit(solution)/shard_map/ppermute | solution.py:50
  69.0 4.6 %shard_map.112.acc = f32[1024,64]{1,0:T(8,128)S(1)} custom-call(bf16[64,8192]{1,0:T(8,128)(2,1)S(1)} %collective-permute-done.18.refs_0_, bf16[224,8192]{1,0:T(8,128)(2,1)S(1)} %copy-done.1, bf16[224,8192]{1,0:T(8,128)(2,1)S(1)} %collective-permute-done.4.refs_10_.refs_2_, bf16[224,8192]{1,0:T(8,128)(2,1)S(1)} %copy-done.2, ...), custom_call_target="tpu_custom_call" | custom-call | flops 1 | bytes 1 | tf_op jit(solution)/shard_map/pallas_call | solution.py:185
  73.7 2.0 %shard_map.113 = bf16[64,8192]{1,0:T(8,128)(2,1)S(1)} custom-call(f32[1024,64]{1,0:T(8,128)S(1)} %shard_map.112.acc, bf16[224,8192]{1,0:T(8,128)(2,1)S(1)} %copy-done, bf16[224,8192]{1,0:T(8,128)(2,1)S(1)} %collective-permute-done.13.down_w2, bf16[256,256]{1,0:T(8,128)(2,1)S(1)} %shard_map.104.seconds, bf16[256,3328]{1,0:T(8,128)(2,1)S(1)} %collective-permute-done.15.theirs, ...), custom_call_target="tpu_custom_call" | custom-call | flops 1 | bytes 1 | tf_op jit(solution)/shard_map/pallas_call | solution.py:196
  75.7 2.8 %collective-permute-start.19 = (bf16[64,8192]{1,0:T(8,128)(2,1)S(1)}, bf16[64,8192]{1,0:T(8,128)(2,1)S(1)}, u32[]{:S(2)}, u32[]{:S(2)}) collective-permute-start(bf16[64,8192]{1,0:T(8,128)(2,1)S(1)} %shard_map.113), channel_id=1, source_target_pairs={{0,32},{1,9},{2,34},{3,11},{4,36},{5,13},{6,38},{7,15},{8,40},{9,1... | collective-permute-start | bytes 3145736 | tf_op jit(solution)/shard_map/ppermute | solution.py:50
  78.4 1.5 %collective-permute-done.16.b1 = bf16[64,8192]{1,0:T(8,128)(2,1)S(1)} collective-permute-done((bf16[64,8192]{1,0:T(8,128)(2,1)S(1)}, bf16[64,8192]{1,0:T(8,128)(2,1)S(1)}, u32[]{:S(2)}, u32[]{:S(2)}) %collective-permute-start.16) | collective-permute-done | bytes 1048608 | tf_op jit(solution)/shard_map/ppermute | solution.py:50
  80.0 12.0 %collective-permute-done.17.b3 = bf16[64,8192]{1,0:T(8,128)(2,1)S(1)} collective-permute-done((bf16[64,8192]{1,0:T(8,128)(2,1)S(1)}, bf16[64,8192]{1,0:T(8,128)(2,1)S(1)}, u32[]{:S(2)}, u32[]{:S(2)}) %collective-permute-start.17) | collective-permute-done | bytes 1048608 | tf_op jit(solution)/shard_map/ppermute | solution.py:50
  92.3 1.4 %collective-permute-done.19.b = bf16[64,8192]{1,0:T(8,128)(2,1)S(1)} collective-permute-done((bf16[64,8192]{1,0:T(8,128)(2,1)S(1)}, bf16[64,8192]{1,0:T(8,128)(2,1)S(1)}, u32[]{:S(2)}, u32[]{:S(2)}) %collective-permute-start.19) | collective-permute-done | bytes 1048608 | tf_op jit(solution)/shard_map/ppermute | solution.py:50
  93.8 2.3 %collective-permute-start.20 = (bf16[16,8192]{1,0:T(8,128)(2,1)S(1)}, bf16[16,8192]{1,0:T(8,128)(2,1)S(1)}, u32[]{:S(2)}, u32[]{:S(2)}) collective-permute-start(bf16[16,8192]{1,0:T(8,128)(2,1)S(1)} %get-tuple-element.62), channel_id=1, source_target_pairs={{0,8},{1,33},{2,10},{3,35},{4,12},{5,37},{6,14},{7,39},{8,0},{9,41... | collective-permute-start | bytes 786440 | tf_op jit(solution)/shard_map/ppermute | solution.py:50
  96.5 0.6 collective-permute-start.22
  97.2 3.8 %collective-permute-done.20.b2 = bf16[16,8192]{1,0:T(8,128)(2,1)S(1)} collective-permute-done((bf16[16,8192]{1,0:T(8,128)(2,1)S(1)}, bf16[16,8192]{1,0:T(8,128)(2,1)S(1)}, u32[]{:S(2)}, u32[]{:S(2)}) %collective-permute-start.20) | collective-permute-done | bytes 262176 | tf_op jit(solution)/shard_map/ppermute | solution.py:50
  100.9 2.5 %collective-permute-done.21.b1 = bf16[16,8192]{1,0:T(8,128)(2,1)S(1)} collective-permute-done((bf16[16,8192]{1,0:T(8,128)(2,1)S(1)}, bf16[16,8192]{1,0:T(8,128)(2,1)S(1)}, u32[]{:S(2)}, u32[]{:S(2)}) %collective-permute-start.21) | collective-permute-done | bytes 262176 | tf_op jit(solution)/shard_map/ppermute | solution.py:50
  103.7 0.7 shard_map.115
  104.4 1.2 %collective-permute-start.23 = (bf16[8,4096]{1,0:T(8,128)(2,1)S(1)}, bf16[8,4096]{1,0:T(8,128)(2,1)S(1)}, u32[]{:S(2)}, u32[]{:S(2)}) collective-permute-start(bf16[8,4096]{1,0:T(8,128)(2,1)S(1)} %get-tuple-element.66), channel_id=1, source_target_pairs={{0,64},{1,65},{2,66},{3,67},{4,68},{5,69},{6,70},{7,71},{8,72},{9,... | collective-permute-start | bytes 196616 | tf_op jit(solution)/shard_map/ppermute | solution.py:50
  105.6 1.5 %collective-permute-start.24 = (bf16[8,4096]{1,0:T(8,128)(2,1)S(1)}, bf16[8,4096]{1,0:T(8,128)(2,1)S(1)}, u32[]{:S(2)}, u32[]{:S(2)}) collective-permute-start(bf16[8,4096]{1,0:T(8,128)(2,1)S(1)} %get-tuple-element.67), channel_id=1, source_target_pairs={{0,2},{1,3},{2,0},{3,1},{4,6},{5,7},{6,4},{7,5},{8,10},{9,11},{10,... | collective-permute-start | bytes 196616 | tf_op jit(solution)/shard_map/ppermute | solution.py:50
  107.2 1.6 %collective-permute-start.25 = (bf16[8,4096]{1,0:T(8,128)(2,1)S(1)}, bf16[8,4096]{1,0:T(8,128)(2,1)S(1)}, u32[]{:S(2)}, u32[]{:S(2)}) collective-permute-start(bf16[8,4096]{1,0:T(8,128)(2,1)S(1)} %get-tuple-element.68), channel_id=1, source_target_pairs={{0,66},{1,67},{2,64},{3,65},{4,70},{5,71},{6,68},{7,69},{8,74},{9,... | collective-permute-start | bytes 196616 | tf_op jit(solution)/shard_map/ppermute | solution.py:50
  109.5 2.7 %collective-permute-done.25.b3 = bf16[8,4096]{1,0:T(8,128)(2,1)S(1)} collective-permute-done((bf16[8,4096]{1,0:T(8,128)(2,1)S(1)}, bf16[8,4096]{1,0:T(8,128)(2,1)S(1)}, u32[]{:S(2)}, u32[]{:S(2)}) %collective-permute-start.25) | collective-permute-done | bytes 65568 | tf_op jit(solution)/shard_map/ppermute | solution.py:50
  112.3 0.6 shard_map.116
  112.8 3.1 %collective-permute-start.26 = (bf16[8,2048]{1,0:T(8,128)(2,1)S(1)}, bf16[8,2048]{1,0:T(8,128)(2,1)S(1)}, u32[]{:S(2)}, u32[]{:S(2)}) collective-permute-start(bf16[8,2048]{1,0:T(8,128)(2,1)S(1)} %get-tuple-element.70), channel_id=1, source_target_pairs={{0,1},{1,0},{2,3},{3,2},{4,5},{5,4},{6,7},{7,6},{8,9},{9,8},{10,11... | collective-permute-start | bytes 98312 | tf_op jit(solution)/shard_map/ppermute | solution.py:50
  116.0 0.9 collective-permute-done.26
  116.8 0.6 maximum_select_fusion
  (37 shorter events, 3.3 us)
Async XLA Ops:
  1.5 2.4 %collective-permute-start = (bf16[8,2048]{1,0:T(8,128)(2,1)S(1)}, bf16[8,2048]{1,0:T(8,128)(2,1)S(1)}, u32[]{:S(2)}, u32[]{:S(2)}) collective-permute-start(bf16[8,2048]{1,0:T(8,128)(2,1)S(1)} %get-tuple-element.39), channel_id=1, source_target_pairs={{0,1},{1,0},{2,3},{3,2},{4,5},{5,4},{6,7},{7,6},{8,9},{9,8},{10,11... | collective-permute-start | bytes 98312 | tf_op jit(solution)/shard_map/ppermute | solution.py:50
  4.4 9.5 %collective-permute-start.4 = (bf16[224,8192]{1,0:T(8,128)(2,1)}, bf16[224,8192]{1,0:T(8,128)(2,1)S(1)}, u32[]{:S(2)}, u32[]{:S(2)}) collective-permute-start(bf16[224,8192]{1,0:T(8,128)(2,1)} %refs_1_), channel_id=1, source_target_pairs={{0,1},{1,0},{2,3},{3,2},{4,5},{5,4},{6,7},{7,6},{8,9},{9,8},{10,11... | collective-permute-start | bytes 11010056 | tf_op jit(solution)/shard_map/ppermute | solution.py:50
  4.8 8.5 %collective-permute-start.3 = (bf16[16,3584]{1,0:T(8,128)(2,1)S(1)}, bf16[16,3584]{1,0:T(8,128)(2,1)S(1)}, u32[]{:S(2)}, u32[]{:S(2)}) collective-permute-start(bf16[16,3584]{1,0:T(8,128)(2,1)S(1)} %get-tuple-element.42.message), channel_id=1, source_target_pairs={{0,66},{1,67},{2,64},{3,65},{4,70},{5,71},{6,68},{7,69},{8,74},{9,... | collective-permute-start | bytes 344072 | tf_op jit(solution)/shard_map/ppermute | solution.py:50
  8.7 3.4 %collective-permute-start.1 = (bf16[8,4096]{1,0:T(8,128)(2,1)S(1)}, bf16[8,4096]{1,0:T(8,128)(2,1)S(1)}, u32[]{:S(2)}, u32[]{:S(2)}) collective-permute-start(bf16[8,4096]{1,0:T(8,128)(2,1)S(1)} %get-tuple-element.41.wide), channel_id=1, source_target_pairs={{0,2},{1,3},{2,0},{3,1},{4,6},{5,7},{6,4},{7,5},{8,10},{9,11},{10,... | collective-permute-start | bytes 196616 | tf_op jit(solution)/shard_map/ppermute | solution.py:50
  8.7 4.6 %collective-permute-start.2 = (bf16[8,4096]{1,0:T(8,128)(2,1)S(1)}, bf16[8,4096]{1,0:T(8,128)(2,1)S(1)}, u32[]{:S(2)}, u32[]{:S(2)}) collective-permute-start(bf16[8,4096]{1,0:T(8,128)(2,1)S(1)} %get-tuple-element.41.wide), channel_id=1, source_target_pairs={{0,64},{1,65},{2,66},{3,67},{4,68},{5,69},{6,70},{7,71},{8,72},{9,... | collective-permute-start | bytes 196616 | tf_op jit(solution)/shard_map/ppermute | solution.py:50
  13.9 9.1 %collective-permute-start.6 = (bf16[16,11264]{1,0:T(8,128)(2,1)S(1)}, bf16[16,11264]{1,0:T(8,128)(2,1)S(1)}, u32[]{:S(2)}, u32[]{:S(2)}) collective-permute-start(bf16[16,11264]{1,0:T(8,128)(2,1)S(1)} %shard_map.102.own.refs_5_), channel_id=1, source_target_pairs={{0,8},{1,33},{2,10},{3,35},{4,12},{5,37},{6,14},{7,39},{8,0},{9,41... | collective-permute-start | bytes 1081352 | tf_op jit(solution)/shard_map/ppermute | solution.py:50
  16.9 12.7 %collective-permute-start.7 = (bf16[16,11264]{1,0:T(8,128)(2,1)S(1)}, bf16[16,11264]{1,0:T(8,128)(2,1)S(1)}, u32[]{:S(2)}, u32[]{:S(2)}) collective-permute-start(bf16[16,11264]{1,0:T(8,128)(2,1)S(1)} %shard_map.102.own.refs_5_), channel_id=1, source_target_pairs={{0,4},{1,17},{2,6},{3,19},{4,0},{5,21},{6,2},{7,23},{8,12},{9,25},... | collective-permute-start | bytes 1081352 | tf_op jit(solution)/shard_map/ppermute | solution.py:50
  17.3 12.3 %collective-permute-start.8 = (bf16[16,11264]{1,0:T(8,128)(2,1)S(1)}, bf16[16,11264]{1,0:T(8,128)(2,1)S(1)}, u32[]{:S(2)}, u32[]{:S(2)}) collective-permute-start(bf16[16,11264]{1,0:T(8,128)(2,1)S(1)} %shard_map.102.own.refs_5_), channel_id=1, source_target_pairs={{0,12},{1,49},{2,14},{3,51},{4,8},{5,53},{6,10},{7,55},{8,4},{9,57... | collective-permute-start | bytes 1081352 | tf_op jit(solution)/shard_map/ppermute | solution.py:50
  17.6 12.1 %collective-permute-start.5 = (bf16[16,11264]{1,0:T(8,128)(2,1)S(1)}, bf16[16,11264]{1,0:T(8,128)(2,1)S(1)}, u32[]{:S(2)}, u32[]{:S(2)}) collective-permute-start(bf16[16,11264]{1,0:T(8,128)(2,1)S(1)} %shard_map.102.own.refs_5_), channel_id=1, source_target_pairs={{0,16},{1,5},{2,18},{3,7},{4,20},{5,1},{6,22},{7,3},{8,24},{9,13},... | collective-permute-start | bytes 1081352 | tf_op jit(solution)/shard_map/ppermute | solution.py:50
  18.9 12.7 %collective-permute-start.9 = (bf16[16,11264]{1,0:T(8,128)(2,1)S(1)}, bf16[16,11264]{1,0:T(8,128)(2,1)S(1)}, u32[]{:S(2)}, u32[]{:S(2)}) collective-permute-start(bf16[16,11264]{1,0:T(8,128)(2,1)S(1)} %shard_map.102.own.refs_5_), channel_id=1, source_target_pairs={{0,48},{1,13},{2,50},{3,15},{4,52},{5,9},{6,54},{7,11},{8,56},{9,5... | collective-permute-start | bytes 1081352 | tf_op jit(solution)/shard_map/ppermute | solution.py:50
  20.7 0.8 copy-start.3
  21.4 0.8 copy-start.4
  22.2 0.8 copy-start.5
  23.0 8.6 %copy-start.2 = (bf16[224,8192]{1,0:T(8,128)(2,1)S(1)}, bf16[224,8192]{1,0:T(8,128)(2,1)}, u32[]{:S(2)}) copy-start(bf16[224,8192]{1,0:T(8,128)(2,1)} %refs_3_) | copy-start | bytes 11010052
  23.0 9.5 %copy-start = (bf16[224,8192]{1,0:T(8,128)(2,1)S(1)}, bf16[224,8192]{1,0:T(8,128)(2,1)}, u32[]{:S(2)}) copy-start(bf16[224,8192]{1,0:T(8,128)(2,1)} %down_w.2) | copy-start | bytes 11010052
  31.5 24.4 %collective-permute-start.12 = (bf16[224,8192]{1,0:T(8,128)(2,1)S(1)}, bf16[224,8192]{1,0:T(8,128)(2,1)S(1)}, u32[]{:S(2)}, u32[]{:S(2)}) collective-permute-start(bf16[224,8192]{1,0:T(8,128)(2,1)S(1)} %copy-done.2), channel_id=1, source_target_pairs={{0,1},{1,0},{2,3},{3,2},{4,5},{5,4},{6,7},{7,6},{8,9},{9,8},{10,11... | collective-permute-start | bytes 11010056 | tf_op jit(solution)/shard_map/ppermute | solution.py:50
  32.5 27.5 %collective-permute-start.13 = (bf16[224,8192]{1,0:T(8,128)(2,1)S(1)}, bf16[224,8192]{1,0:T(8,128)(2,1)S(1)}, u32[]{:S(2)}, u32[]{:S(2)}) collective-permute-start(bf16[224,8192]{1,0:T(8,128)(2,1)S(1)} %copy-done), channel_id=1, source_target_pairs={{0,1},{1,0},{2,3},{3,2},{4,5},{5,4},{6,7},{7,6},{8,9},{9,8},{10,11... | collective-permute-start | bytes 11010056 | tf_op jit(solution)/shard_map/ppermute | solution.py:50
  32.6 8.6 %collective-permute-start.14 = (bf16[64,3072]{1,0:T(8,128)(2,1)S(1)}, bf16[64,3072]{1,0:T(8,128)(2,1)S(1)}, u32[]{:S(2)}, u32[]{:S(2)}) collective-permute-start(bf16[64,3072]{1,0:T(8,128)(2,1)S(1)} %get-tuple-element.54.f0), channel_id=1, source_target_pairs={{0,32},{1,9},{2,34},{3,11},{4,36},{5,13},{6,38},{7,15},{8,40},{9,1... | collective-permute-start | bytes 1179656 | tf_op jit(solution)/shard_map/ppermute | solution.py:50
  35.7 17.1 %collective-permute-start.10 = (bf16[48,11264]{1,0:T(8,128)(2,1)S(1)}, bf16[48,11264]{1,0:T(8,128)(2,1)S(1)}, u32[]{:S(2)}, u32[]{:S(2)}) collective-permute-start(bf16[48,11264]{1,0:T(8,128)(2,1)S(1)} %get-tuple-element.50), channel_id=1, source_target_pairs={{0,16},{1,5},{2,18},{3,7},{4,20},{5,1},{6,22},{7,3},{8,24},{9,13},... | collective-permute-start | bytes 3244040 | tf_op jit(solution)/shard_map/ppermute | solution.py:50
  35.7 17.1 %collective-permute-start.11 = (bf16[48,11264]{1,0:T(8,128)(2,1)S(1)}, bf16[48,11264]{1,0:T(8,128)(2,1)S(1)}, u32[]{:S(2)}, u32[]{:S(2)}) collective-permute-start(bf16[48,11264]{1,0:T(8,128)(2,1)S(1)} %get-tuple-element.50), channel_id=1, source_target_pairs={{0,48},{1,13},{2,50},{3,15},{4,52},{5,9},{6,54},{7,11},{8,56},{9,5... | collective-permute-start | bytes 3244040 | tf_op jit(solution)/shard_map/ppermute | solution.py:50
  41.2 13.2 %copy-start.1 = (bf16[224,8192]{1,0:T(8,128)(2,1)S(1)}, bf16[224,8192]{1,0:T(8,128)(2,1)}, u32[]{:S(2)}) copy-start(bf16[224,8192]{1,0:T(8,128)(2,1)} %refs_1_) | copy-start | bytes 11010052
  53.0 7.0 %collective-permute-start.15 = (bf16[256,3328]{1,0:T(8,128)(2,1)S(1)}, bf16[256,3328]{1,0:T(8,128)(2,1)S(1)}, u32[]{:S(2)}, u32[]{:S(2)}) collective-permute-start(bf16[256,3328]{1,0:T(8,128)(2,1)S(1)} %shard_map.108.factor), channel_id=1, source_target_pairs={{0,1},{1,0},{2,3},{3,2},{4,5},{5,4},{6,7},{7,6},{8,9},{9,8},{10,11... | collective-permute-start | bytes 5111816 | tf_op jit(solution)/shard_map/ppermute | solution.py:50
  54.5 14.5 %collective-permute-start.18 = (bf16[64,8192]{1,0:T(8,128)(2,1)S(1)}, bf16[64,8192]{1,0:T(8,128)(2,1)S(1)}, u32[]{:S(2)}, u32[]{:S(2)}) collective-permute-start(bf16[64,8192]{1,0:T(8,128)(2,1)S(1)} %shard_map.111), channel_id=1, source_target_pairs={{0,16},{1,5},{2,18},{3,7},{4,20},{5,1},{6,22},{7,3},{8,24},{9,13},... | collective-permute-start | bytes 3145736 | tf_op jit(solution)/shard_map/ppermute | solution.py:50
  65.9 14.1 %collective-permute-start.16 = (bf16[64,8192]{1,0:T(8,128)(2,1)S(1)}, bf16[64,8192]{1,0:T(8,128)(2,1)S(1)}, u32[]{:S(2)}, u32[]{:S(2)}) collective-permute-start(bf16[64,8192]{1,0:T(8,128)(2,1)S(1)} %get-tuple-element.56), channel_id=1, source_target_pairs={{0,16},{1,5},{2,18},{3,7},{4,20},{5,1},{6,22},{7,3},{8,24},{9,13},... | collective-permute-start | bytes 3145736 | tf_op jit(solution)/shard_map/ppermute | solution.py:50
  66.3 25.7 %collective-permute-start.17 = (bf16[64,8192]{1,0:T(8,128)(2,1)S(1)}, bf16[64,8192]{1,0:T(8,128)(2,1)S(1)}, u32[]{:S(2)}, u32[]{:S(2)}) collective-permute-start(bf16[64,8192]{1,0:T(8,128)(2,1)S(1)} %get-tuple-element.57), channel_id=1, source_target_pairs={{0,48},{1,13},{2,50},{3,15},{4,52},{5,9},{6,54},{7,11},{8,56},{9,5... | collective-permute-start | bytes 3145736 | tf_op jit(solution)/shard_map/ppermute | solution.py:50
  75.7 18.0 %collective-permute-start.19 = (bf16[64,8192]{1,0:T(8,128)(2,1)S(1)}, bf16[64,8192]{1,0:T(8,128)(2,1)S(1)}, u32[]{:S(2)}, u32[]{:S(2)}) collective-permute-start(bf16[64,8192]{1,0:T(8,128)(2,1)S(1)} %shard_map.113), channel_id=1, source_target_pairs={{0,32},{1,9},{2,34},{3,11},{4,36},{5,13},{6,38},{7,15},{8,40},{9,1... | collective-permute-start | bytes 3145736 | tf_op jit(solution)/shard_map/ppermute | solution.py:50
  93.8 7.1 %collective-permute-start.20 = (bf16[16,8192]{1,0:T(8,128)(2,1)S(1)}, bf16[16,8192]{1,0:T(8,128)(2,1)S(1)}, u32[]{:S(2)}, u32[]{:S(2)}) collective-permute-start(bf16[16,8192]{1,0:T(8,128)(2,1)S(1)} %get-tuple-element.62), channel_id=1, source_target_pairs={{0,8},{1,33},{2,10},{3,35},{4,12},{5,37},{6,14},{7,39},{8,0},{9,41... | collective-permute-start | bytes 786440 | tf_op jit(solution)/shard_map/ppermute | solution.py:50
  96.1 7.3 %collective-permute-start.21 = (bf16[16,8192]{1,0:T(8,128)(2,1)S(1)}, bf16[16,8192]{1,0:T(8,128)(2,1)S(1)}, u32[]{:S(2)}, u32[]{:S(2)}) collective-permute-start(bf16[16,8192]{1,0:T(8,128)(2,1)S(1)} %get-tuple-element.63), channel_id=1, source_target_pairs={{0,4},{1,17},{2,6},{3,19},{4,0},{5,21},{6,2},{7,23},{8,12},{9,25},... | collective-permute-start | bytes 786440 | tf_op jit(solution)/shard_map/ppermute | solution.py:50
  96.5 7.2 %collective-permute-start.22 = (bf16[16,8192]{1,0:T(8,128)(2,1)S(1)}, bf16[16,8192]{1,0:T(8,128)(2,1)S(1)}, u32[]{:S(2)}, u32[]{:S(2)}) collective-permute-start(bf16[16,8192]{1,0:T(8,128)(2,1)S(1)} %get-tuple-element.64), channel_id=1, source_target_pairs={{0,12},{1,49},{2,14},{3,51},{4,8},{5,53},{6,10},{7,55},{8,4},{9,57... | collective-permute-start | bytes 786440 | tf_op jit(solution)/shard_map/ppermute | solution.py:50
  104.4 4.7 %collective-permute-start.23 = (bf16[8,4096]{1,0:T(8,128)(2,1)S(1)}, bf16[8,4096]{1,0:T(8,128)(2,1)S(1)}, u32[]{:S(2)}, u32[]{:S(2)}) collective-permute-start(bf16[8,4096]{1,0:T(8,128)(2,1)S(1)} %get-tuple-element.66), channel_id=1, source_target_pairs={{0,64},{1,65},{2,66},{3,67},{4,68},{5,69},{6,70},{7,71},{8,72},{9,... | collective-permute-start | bytes 196616 | tf_op jit(solution)/shard_map/ppermute | solution.py:50
  105.6 3.9 %collective-permute-start.24 = (bf16[8,4096]{1,0:T(8,128)(2,1)S(1)}, bf16[8,4096]{1,0:T(8,128)(2,1)S(1)}, u32[]{:S(2)}, u32[]{:S(2)}) collective-permute-start(bf16[8,4096]{1,0:T(8,128)(2,1)S(1)} %get-tuple-element.67), channel_id=1, source_target_pairs={{0,2},{1,3},{2,0},{3,1},{4,6},{5,7},{6,4},{7,5},{8,10},{9,11},{10,... | collective-permute-start | bytes 196616 | tf_op jit(solution)/shard_map/ppermute | solution.py:50
  107.2 5.1 %collective-permute-start.25 = (bf16[8,4096]{1,0:T(8,128)(2,1)S(1)}, bf16[8,4096]{1,0:T(8,128)(2,1)S(1)}, u32[]{:S(2)}, u32[]{:S(2)}) collective-permute-start(bf16[8,4096]{1,0:T(8,128)(2,1)S(1)} %get-tuple-element.68), channel_id=1, source_target_pairs={{0,66},{1,67},{2,64},{3,65},{4,70},{5,71},{6,68},{7,69},{8,74},{9,... | collective-permute-start | bytes 196616 | tf_op jit(solution)/shard_map/ppermute | solution.py:50
  112.8 4.0 %collective-permute-start.26 = (bf16[8,2048]{1,0:T(8,128)(2,1)S(1)}, bf16[8,2048]{1,0:T(8,128)(2,1)S(1)}, u32[]{:S(2)}, u32[]{:S(2)}) collective-permute-start(bf16[8,2048]{1,0:T(8,128)(2,1)S(1)} %get-tuple-element.70), channel_id=1, source_target_pairs={{0,1},{1,0},{2,3},{3,2},{4,5},{5,4},{6,7},{7,6},{8,9},{9,8},{10,11... | collective-permute-start | bytes 98312 | tf_op jit(solution)/shard_map/ppermute | solution.py:50

commit v13 on v12

--- a/solution.py
+++ b/solution.py
@@ -18,7 +18,7 @@
 STEPS = WIDTH // TILE
 PARTS = TILE // 256
 f32, bf16 = jnp.float32, jnp.bfloat16
-CK, CU = 8, 2
+CK = 8
 SMALL = pl.CostEstimate(flops=1, bytes_accessed=1, transcendentals=0)
 
 
@@ -133,8 +133,8 @@
 
 
 def first_down_kernel(
-    place, own1, rest1, own3, rest3, own, got1, got2, got3, acc, down_w, down_w2, seconds,
-    theirs, factor, out1, out3, total, first, second, hidden,
+    place, rows1, rows3, own, acc, down_w, down_w2, seconds, theirs, factor,
+    out1, out3, total, first, second, hidden,
 ):
     homes = shard_homes(place)
 
@@ -145,8 +145,7 @@
                     piece = src[rows_at[learner % 16], cols[base + k][learner // 16]]
                     to[to_at[k], learner * 256 : learner * 256 + 256] = piece
 
-    rows = (own1, rest1, own3, rest3, own, got1, got2, got3)
-    low = low_rows(rows, first, lambda i: gather(i, first, 4, 0))
+    low = low_rows((rows1, rows3, own), first, lambda i: gather(i, first, 4, 0))
     finish(acc, low, seconds, theirs, hidden)
     for i in range(STEPS):
         tile = slice(i * TILE, (i + 1) * TILE)
@@ -263,8 +262,7 @@
 def unpack_kernel(own, got2, got1, got3, factor, packed):
     for k, g in enumerate((own, got1, got2, got3)):
         factor[16 * k : 16 * k + 16, :] = g[:, WIDTH:]
-        if k:
-            packed[16 * k - 16 : 16 * k, :] = g[...]
+        packed[16 * k : 16 * k + 16, :] = g[...]
 
 
 def part_kernel(*refs):
@@ -284,9 +282,9 @@
         out[64 * k : 64 * k + 64, :UNITS] = r[...]
 
 
-def stack_kernel(f0, own1, rest1, f2, own3, rest3, seconds, out):
+def stack_kernel(f0, packed1, f2, packed3, seconds, out):
     at = 0
-    for r in (f0, own1, rest1, f2, own3, rest3):
+    for r in (f0, packed1, f2, packed3):
         out[at : at + r.shape[0], :3072] = r[:, -3072:]
         at += r.shape[0]
     out[:, 3072:] = seconds[...]
@@ -363,7 +361,6 @@
     )
 
     packed = after(packed, gate2)
-    own = packed
     got = {k: send(packed, FIRST[k]) for k in (1, 2, 3)}
     seconds = (adapter_second_gate, adapter_second_up, adapter_first_down)
     (seconds,) = local(
@@ -371,15 +368,13 @@
     )
     factor, packed = local(
         unpack_kernel,
-        [((64, 3072), bf16), ((48, WIDTH + 3072), bf16)],
-        (own, got[2], got[1], got[3]),
-        price=price_of(CU),
-    )
-
-    own1, own3 = send(own, SECOND[1]), send(own, SECOND[3])
-    factor, packed = after((factor, packed), (own1, own3, seconds))
+        [((64, 3072), bf16), ((64, WIDTH + 3072), bf16)],
+        (packed, got[2], got[1], got[3]),
+    )
+
+    factor, packed = after((factor, packed), seconds)
     far = send(factor, SECOND[2])
-    rest1, rest3 = send(packed, SECOND[1]), send(packed, SECOND[3])
+    packed1, packed3 = send(packed, SECOND[1]), send(packed, SECOND[3])
     frozen = (frozen_gate_weight, frozen_up_weight, frozen_down_weight)
     owned = after(frozen, packed)
     up2, down2 = send(owned[1], CORE), send(owned[2], CORE)
@@ -387,17 +382,17 @@
     (factor,) = local(
         stack_kernel,
         [((256, 3072 + 256), bf16)],
-        (factor, own1, rest1, far, own3, rest3, seconds),
+        (factor, packed1, far, packed3, seconds),
     )
     factor2 = send(factor, CORE)
-    (rows3,) = local(part_kernel, [((64, WIDTH), bf16)], (own3, rest3))
+    (rows3,) = local(part_kernel, [((64, WIDTH), bf16)], (packed3,))
     rows2 = send(rows3, SECOND[1])
     (touched,) = local(touch_kernel, [((8, 128), f32)], in_vmem(owned))
 
     weights = (owned[0], gate2, owned[1], up2)
     down_weights = (owned[2], down2)
 
-    rows = (own1, rest1, own3, rest3, own, got[1], got[2], got[3])
+    rows = (packed1, packed3, packed)
     acc = project(rows, weights, price_of(CK), touched)
     part1, part3, total, first, second = down(
         first_down_kernel,
@@ -419,7 +414,7 @@
     (total,) = local(
         add_kernel,
         [((64, WIDTH), f32)],
-        (total, back1, back3),
+        (total, back3, back1),
         price=price_of(4.5),
     )
     small = [((16, WIDTH), f32)] + [((16, WIDTH), bf16)] * 3

time: 118 us -> 118 us (level)
  waiting for transfers between devices: 55.2 us -> 57.4 us
  starting transfers between devices: 38 us -> 36.1 us
    ppermute x27 -> x25, waiting for transfers between devices: 55.2 us -> 57.4 us  [send(): return lax.ppermute(value, AXES, route)]
    ppermute x27 -> x25, starting transfers between devices: 38 us -> 36.1 us  [send(): return lax.ppermute(value, AXES, route)]
  transfers between devices with their start and end apart: 27 -> 25, of which waited for: 17 -> 17; matrix products, arithmetic and copies ran while one was open for 0% -> 0% of each run, Pallas kernels for 15% -> 15%
where the time goes in v13:
time: 118 us
  waiting for transfers between devices  57.4 us (49%)
  starting transfers between devices  36.1 us (31%)
  Pallas kernels  21.1 us (18%)
  local copies, waits for them, and re-layouts  2.37 us (2%)
    ppermute x25, waiting for transfers between devices, send(): return lax.ppermute(value, AXES, route)  57.4 us
    ppermute x25, starting transfers between devices, send(): return lax.ppermute(value, AXES, route)  36.1 us
    pallas_call x2, Pallas kernels, project(): pl.pallas_call(lambda *refs: project_kernel(n, *refs[more:]), in_specs=[V...  8.7 us
    pallas_call x2, Pallas kernels, down(): pl.pallas_call(body, in_specs=[SMEM] * len(lead) + [VMEM] * len(operands)...  7.84 us
    pallas_call x13, Pallas kernels, local(): pl.pallas_call(body, in_specs=[SMEM] * len(lead) + [VMEM] * len(operands)...  4.53 us
  transfers between devices with their start and end apart: 25, of which 17 were waited for; matrix products, arithmetic and copies ran while one was open for 0% of the time, Pallas kernels for 15%

profile of v13, /device:TPU:1, one launch (start us, length us, event | category | flops | bytes accessed | tf_op | source)
XLA Modules:
  0.0 117.7 jit_solution(535210608336533758)
XLA Ops:
  0.1 1.4 %shard_map.100 = (bf16[8,2048]{1,0:T(8,128)(2,1)S(1)}, bf16[8,2048]{1,0:T(8,128)(2,1)S(1)}, bf16[16,1536]{1,0:T(8,128)(2,1)S(1)}) custom-call(s32[5]{0:T(128)S(1)} %stack.37.place, bf16[2,8,2048]{2,1,0:T(8,128)(2,1)} %inputs.1, bf16[64,256]{1,0:T(8,128)(2,1)} %gate.1, bf16[64,256]{1,0:T(8,128)(2,1)} %up.1, bf16[64,256]{1,0:T(8,128)(2,1)} %down.1), custom_call_target="tpu_custom_call" | custom-call | flops 1 | bytes 1 | tf_op jit(solution)/shard_map/pallas_call | solution.py:208
  1.5 1.5 %collective-permute-start = (bf16[8,2048]{1,0:T(8,128)(2,1)S(1)}, bf16[8,2048]{1,0:T(8,128)(2,1)S(1)}, u32[]{:S(2)}, u32[]{:S(2)}) collective-permute-start(bf16[8,2048]{1,0:T(8,128)(2,1)S(1)} %get-tuple-element.39), channel_id=1, source_target_pairs={{0,1},{1,0},{2,3},{3,2},{4,5},{5,4},{6,7},{7,6},{8,9},{9,8},{10,11... | collective-permute-start | bytes 98312 | tf_op jit(solution)/shard_map/ppermute | solution.py:50
  3.0 0.9 collective-permute-done.other
  3.8 0.6 shard_map.101
  4.4 0.4 collective-permute-start.4
  4.8 3.8 %collective-permute-start.3 = (bf16[16,3584]{1,0:T(8,128)(2,1)S(1)}, bf16[16,3584]{1,0:T(8,128)(2,1)S(1)}, u32[]{:S(2)}, u32[]{:S(2)}) collective-permute-start(bf16[16,3584]{1,0:T(8,128)(2,1)S(1)} %get-tuple-element.42.message), channel_id=1, source_target_pairs={{0,66},{1,67},{2,64},{3,65},{4,70},{5,71},{6,68},{7,69},{8,74},{9,... | collective-permute-start | bytes 344072 | tf_op jit(solution)/shard_map/ppermute | solution.py:50
  8.7 1.2 %collective-permute-start.2 = (bf16[8,4096]{1,0:T(8,128)(2,1)S(1)}, bf16[8,4096]{1,0:T(8,128)(2,1)S(1)}, u32[]{:S(2)}, u32[]{:S(2)}) collective-permute-start(bf16[8,4096]{1,0:T(8,128)(2,1)S(1)} %get-tuple-element.41.wide), channel_id=1, source_target_pairs={{0,64},{1,65},{2,66},{3,67},{4,68},{5,69},{6,70},{7,71},{8,72},{9,... | collective-permute-start | bytes 196616 | tf_op jit(solution)/shard_map/ppermute | solution.py:50
  9.8 2.2 %collective-permute-done.1.z1 = bf16[8,4096]{1,0:T(8,128)(2,1)S(1)} collective-permute-done((bf16[8,4096]{1,0:T(8,128)(2,1)S(1)}, bf16[8,4096]{1,0:T(8,128)(2,1)S(1)}, u32[]{:S(2)}, u32[]{:S(2)}) %collective-permute-start.1) | collective-permute-done | bytes 65568 | tf_op jit(solution)/shard_map/ppermute | solution.py:50
  12.1 1.2 %collective-permute-done.2.z2 = bf16[8,4096]{1,0:T(8,128)(2,1)S(1)} collective-permute-done((bf16[8,4096]{1,0:T(8,128)(2,1)S(1)}, bf16[8,4096]{1,0:T(8,128)(2,1)S(1)}, u32[]{:S(2)}, u32[]{:S(2)}) %collective-permute-start.2) | collective-permute-done | bytes 65568 | tf_op jit(solution)/shard_map/ppermute | solution.py:50
  13.3 0.6 shard_map.102.own
  13.9 3.0 %collective-permute-start.5 = (bf16[16,11264]{1,0:T(8,128)(2,1)S(1)}, bf16[16,11264]{1,0:T(8,128)(2,1)S(1)}, u32[]{:S(2)}, u32[]{:S(2)}) collective-permute-start(bf16[16,11264]{1,0:T(8,128)(2,1)S(1)} %shard_map.102.own), channel_id=1, source_target_pairs={{0,8},{1,33},{2,10},{3,35},{4,12},{5,37},{6,14},{7,39},{8,0},{9,41... | collective-permute-start | bytes 1081352 | tf_op jit(solution)/shard_map/ppermute | solution.py:50
  17.7 0.8 copy-done.3
  18.4 0.8 copy-done.4
  19.2 0.8 copy-done.5
  19.9 2.1 %collective-permute-done.5.got2 = bf16[16,11264]{1,0:T(8,128)(2,1)S(1)} collective-permute-done((bf16[16,11264]{1,0:T(8,128)(2,1)S(1)}, bf16[16,11264]{1,0:T(8,128)(2,1)S(1)}, u32[]{:S(2)}, u32[]{:S(2)}) %collective-permute-start.5) | collective-permute-done | bytes 360480 | tf_op jit(solution)/shard_map/ppermute | solution.py:50
  22.0 4.2 %collective-permute-done.6.got1 = bf16[16,11264]{1,0:T(8,128)(2,1)S(1)} collective-permute-done((bf16[16,11264]{1,0:T(8,128)(2,1)S(1)}, bf16[16,11264]{1,0:T(8,128)(2,1)S(1)}, u32[]{:S(2)}, u32[]{:S(2)}) %collective-permute-start.6) | collective-permute-done | bytes 360480 | tf_op jit(solution)/shard_map/ppermute | solution.py:50
  26.4 2.3 %collective-permute-start.10 = (bf16[224,8192]{1,0:T(8,128)(2,1)}, bf16[224,8192]{1,0:T(8,128)(2,1)S(1)}, u32[]{:S(2)}, u32[]{:S(2)}) collective-permute-start(bf16[224,8192]{1,0:T(8,128)(2,1)} %refs_3_), channel_id=1, source_target_pairs={{0,1},{1,0},{2,3},{3,2},{4,5},{5,4},{6,7},{7,6},{8,9},{9,8},{10,11... | collective-permute-start | bytes 11010056 | tf_op jit(solution)/shard_map/ppermute | solution.py:50
  28.8 2.6 %collective-permute-start.12 = (bf16[64,3072]{1,0:T(8,128)(2,1)S(1)}, bf16[64,3072]{1,0:T(8,128)(2,1)S(1)}, u32[]{:S(2)}, u32[]{:S(2)}) collective-permute-start(bf16[64,3072]{1,0:T(8,128)(2,1)S(1)} %get-tuple-element.54.f0), channel_id=1, source_target_pairs={{0,32},{1,9},{2,34},{3,11},{4,36},{5,13},{6,38},{7,15},{8,40},{9,1... | collective-permute-start | bytes 1179656 | tf_op jit(solution)/shard_map/ppermute | solution.py:50
  31.7 0.6 collective-permute-start.9
  32.3 4.9 %collective-permute-done.12.refs_0_ = bf16[64,3072]{1,0:T(8,128)(2,1)S(1)} collective-permute-done((bf16[64,3072]{1,0:T(8,128)(2,1)S(1)}, bf16[64,3072]{1,0:T(8,128)(2,1)S(1)}, u32[]{:S(2)}, u32[]{:S(2)}) %collective-permute-start.12) | collective-permute-done | bytes 393248 | tf_op jit(solution)/shard_map/ppermute | solution.py:50
  37.3 15.4 %collective-permute-done.8.refs_1_.packed1.rows1 = bf16[64,11264]{1,0:T(8,128)(2,1)S(1)} collective-permute-done((bf16[64,11264]{1,0:T(8,128)(2,1)S(1)}, bf16[64,11264]{1,0:T(8,128)(2,1)S(1)}, u32[]{:S(2)}, u32[]{:S(2)}) %collective-permute-start.8) | collective-permute-done | bytes 1441824 | tf_op jit(solution)/shard_map/ppermute | solution.py:50
  52.8 1.7 %collective-permute-start.13 = (bf16[256,3328]{1,0:T(8,128)(2,1)S(1)}, bf16[256,3328]{1,0:T(8,128)(2,1)S(1)}, u32[]{:S(2)}, u32[]{:S(2)}) collective-permute-start(bf16[256,3328]{1,0:T(8,128)(2,1)S(1)} %shard_map.108.factor), channel_id=1, source_target_pairs={{0,1},{1,0},{2,3},{3,2},{4,5},{5,4},{6,7},{7,6},{8,9},{9,8},{10,11... | collective-permute-start | bytes 5111816 | tf_op jit(solution)/shard_map/ppermute | solution.py:50
  54.6 1.2 %collective-permute-start.16 = (bf16[64,8192]{1,0:T(8,128)(2,1)S(1)}, bf16[64,8192]{1,0:T(8,128)(2,1)S(1)}, u32[]{:S(2)}, u32[]{:S(2)}) collective-permute-start(bf16[64,8192]{1,0:T(8,128)(2,1)S(1)} %shard_map.111), channel_id=1, source_target_pairs={{0,16},{1,5},{2,18},{3,7},{4,20},{5,1},{6,22},{7,3},{8,24},{9,13},... | collective-permute-start | bytes 3145736 | tf_op jit(solution)/shard_map/ppermute | solution.py:50
  55.8 4.1 %shard_map.106.acc = f32[896,192]{1,0:T(8,128)S(1)} custom-call(f32[8,128]{1,0:T(8,128)S(1)} %shard_map.105.refs_0_, bf16[64,11264]{1,0:T(8,128)(2,1)S(1)} %collective-permute-done.8.refs_1_.packed1.rows1, bf16[64,11264]{1,0:T(8,128)(2,1)S(1)} %collective-permute-done.9.refs_2_.packed3.rows3.refs_0_, bf16[64,11264]{1,0:T(8,128)(2,1)S(1)} %get-tuple-element.50.refs_3_.own, ...), custom_call_target="tpu_custom_call" | custom-call | flops 9200000000 | bytes 28800000 | tf_op jit(solution)/shard_map/pallas_call | solution.py:184
  59.9 5.8 %shard_map.109 = (bf16[64,8192]{1,0:T(8,128)(2,1)S(1)}, bf16[64,8192]{1,0:T(8,128)(2,1)S(1)}, f32[64,8192]{1,0:T(8,128)S(1)}, bf16[128,8192]{1,0:T(8,128)(2,1)S(1)}, bf16[64,8192]{1,0:T(8,128)(2,1)S(1)}) custom-call(s32[5]{0:T(128)S(1)} %stack.37.place, bf16[64,11264]{1,0:T(8,128)(2,1)S(1)} %collective-permute-done.8.refs_1_.packed1.rows1, ...), custom_call_target="tpu_custom_call" | custom-call | flops 1 | bytes 1 | tf_op jit(solution)/shard_map/pallas_call | solution.py:195
  65.8 1.8 %collective-permute-start.14 = (bf16[64,8192]{1,0:T(8,128)(2,1)S(1)}, bf16[64,8192]{1,0:T(8,128)(2,1)S(1)}, u32[]{:S(2)}, u32[]{:S(2)}) collective-permute-start(bf16[64,8192]{1,0:T(8,128)(2,1)S(1)} %get-tuple-element.56), channel_id=1, source_target_pairs={{0,48},{1,13},{2,50},{3,15},{4,52},{5,9},{6,54},{7,11},{8,56},{9,5... | collective-permute-start | bytes 3145736 | tf_op jit(solution)/shard_map/ppermute | solution.py:50
  67.9 0.7 collective-permute-done.16.refs_0_
  68.6 4.6 %shard_map.112.acc = f32[1024,64]{1,0:T(8,128)S(1)} custom-call(bf16[64,8192]{1,0:T(8,128)(2,1)S(1)} %collective-permute-done.16.refs_0_, bf16[224,8192]{1,0:T(8,128)(2,1)S(1)} %copy-done.1, bf16[224,8192]{1,0:T(8,128)(2,1)S(1)} %collective-permute-done.4.refs_5_.refs_2_, bf16[224,8192]{1,0:T(8,128)(2,1)S(1)} %copy-done.2, ...), custom_call_target="tpu_custom_call" | custom-call | flops 1 | bytes 1 | tf_op jit(solution)/shard_map/pallas_call | solution.py:184
  73.3 2.0 %shard_map.113 = bf16[64,8192]{1,0:T(8,128)(2,1)S(1)} custom-call(f32[1024,64]{1,0:T(8,128)S(1)} %shard_map.112.acc, bf16[224,8192]{1,0:T(8,128)(2,1)S(1)} %copy-done, bf16[224,8192]{1,0:T(8,128)(2,1)S(1)} %collective-permute-done.11.down_w2, bf16[256,256]{1,0:T(8,128)(2,1)S(1)} %shard_map.104.seconds, bf16[256,3328]{1,0:T(8,128)(2,1)S(1)} %collective-permute-done.13.theirs, ...), custom_call_target="tpu_custom_call" | custom-call | flops 1 | bytes 1 | tf_op jit(solution)/shard_map/pallas_call | solution.py:195
  75.3 2.7 %collective-permute-start.17 = (bf16[64,8192]{1,0:T(8,128)(2,1)S(1)}, bf16[64,8192]{1,0:T(8,128)(2,1)S(1)}, u32[]{:S(2)}, u32[]{:S(2)}) collective-permute-start(bf16[64,8192]{1,0:T(8,128)(2,1)S(1)} %shard_map.113), channel_id=1, source_target_pairs={{0,32},{1,9},{2,34},{3,11},{4,36},{5,13},{6,38},{7,15},{8,40},{9,1... | collective-permute-start | bytes 3145736 | tf_op jit(solution)/shard_map/ppermute | solution.py:50
  78.0 3.0 %collective-permute-done.14.b1 = bf16[64,8192]{1,0:T(8,128)(2,1)S(1)} collective-permute-done((bf16[64,8192]{1,0:T(8,128)(2,1)S(1)}, bf16[64,8192]{1,0:T(8,128)(2,1)S(1)}, u32[]{:S(2)}, u32[]{:S(2)}) %collective-permute-start.14) | collective-permute-done | bytes 1048608 | tf_op jit(solution)/shard_map/ppermute | solution.py:50
  81.0 0.5 collective-permute-done.15.b3
  81.8 11.6 %collective-permute-done.17.b = bf16[64,8192]{1,0:T(8,128)(2,1)S(1)} collective-permute-done((bf16[64,8192]{1,0:T(8,128)(2,1)S(1)}, bf16[64,8192]{1,0:T(8,128)(2,1)S(1)}, u32[]{:S(2)}, u32[]{:S(2)}) %collective-permute-start.17) | collective-permute-done | bytes 1048608 | tf_op jit(solution)/shard_map/ppermute | solution.py:50
  93.6 2.3 %collective-permute-start.18 = (bf16[16,8192]{1,0:T(8,128)(2,1)S(1)}, bf16[16,8192]{1,0:T(8,128)(2,1)S(1)}, u32[]{:S(2)}, u32[]{:S(2)}) collective-permute-start(bf16[16,8192]{1,0:T(8,128)(2,1)S(1)} %get-tuple-element.62), channel_id=1, source_target_pairs={{0,8},{1,33},{2,10},{3,35},{4,12},{5,37},{6,14},{7,39},{8,0},{9,41... | collective-permute-start | bytes 786440 | tf_op jit(solution)/shard_map/ppermute | solution.py:50
  95.9 0.7 collective-permute-start.19
  96.9 3.8 %collective-permute-done.18.b2 = bf16[16,8192]{1,0:T(8,128)(2,1)S(1)} collective-permute-done((bf16[16,8192]{1,0:T(8,128)(2,1)S(1)}, bf16[16,8192]{1,0:T(8,128)(2,1)S(1)}, u32[]{:S(2)}, u32[]{:S(2)}) %collective-permute-start.18) | collective-permute-done | bytes 262176 | tf_op jit(solution)/shard_map/ppermute | solution.py:50
  100.7 2.8 %collective-permute-done.19.b1 = bf16[16,8192]{1,0:T(8,128)(2,1)S(1)} collective-permute-done((bf16[16,8192]{1,0:T(8,128)(2,1)S(1)}, bf16[16,8192]{1,0:T(8,128)(2,1)S(1)}, u32[]{:S(2)}, u32[]{:S(2)}) %collective-permute-start.19) | collective-permute-done | bytes 262176 | tf_op jit(solution)/shard_map/ppermute | solution.py:50
  103.5 0.7 shard_map.115
  104.2 1.3 %collective-permute-start.21 = (bf16[8,4096]{1,0:T(8,128)(2,1)S(1)}, bf16[8,4096]{1,0:T(8,128)(2,1)S(1)}, u32[]{:S(2)}, u32[]{:S(2)}) collective-permute-start(bf16[8,4096]{1,0:T(8,128)(2,1)S(1)} %get-tuple-element.66), channel_id=1, source_target_pairs={{0,64},{1,65},{2,66},{3,67},{4,68},{5,69},{6,70},{7,71},{8,72},{9,... | collective-permute-start | bytes 196616 | tf_op jit(solution)/shard_map/ppermute | solution.py:50
  105.5 1.5 %collective-permute-start.22 = (bf16[8,4096]{1,0:T(8,128)(2,1)S(1)}, bf16[8,4096]{1,0:T(8,128)(2,1)S(1)}, u32[]{:S(2)}, u32[]{:S(2)}) collective-permute-start(bf16[8,4096]{1,0:T(8,128)(2,1)S(1)} %get-tuple-element.67), channel_id=1, source_target_pairs={{0,2},{1,3},{2,0},{3,1},{4,6},{5,7},{6,4},{7,5},{8,10},{9,11},{10,... | collective-permute-start | bytes 196616 | tf_op jit(solution)/shard_map/ppermute | solution.py:50
  106.9 1.5 %collective-permute-start.23 = (bf16[8,4096]{1,0:T(8,128)(2,1)S(1)}, bf16[8,4096]{1,0:T(8,128)(2,1)S(1)}, u32[]{:S(2)}, u32[]{:S(2)}) collective-permute-start(bf16[8,4096]{1,0:T(8,128)(2,1)S(1)} %get-tuple-element.68), channel_id=1, source_target_pairs={{0,66},{1,67},{2,64},{3,65},{4,70},{5,71},{6,68},{7,69},{8,74},{9,... | collective-permute-start | bytes 196616 | tf_op jit(solution)/shard_map/ppermute | solution.py:50
  108.4 0.5 collective-permute-done.21.b2
  108.9 0.4 collective-permute-done.22.b1
  109.3 2.3 %collective-permute-done.23.b3 = bf16[8,4096]{1,0:T(8,128)(2,1)S(1)} collective-permute-done((bf16[8,4096]{1,0:T(8,128)(2,1)S(1)}, bf16[8,4096]{1,0:T(8,128)(2,1)S(1)}, u32[]{:S(2)}, u32[]{:S(2)}) %collective-permute-start.23) | collective-permute-done | bytes 65568 | tf_op jit(solution)/shard_map/ppermute | solution.py:50
  111.5 0.6 shard_map.116
  112.1 4.1 %collective-permute-start.24 = (bf16[8,2048]{1,0:T(8,128)(2,1)S(1)}, bf16[8,2048]{1,0:T(8,128)(2,1)S(1)}, u32[]{:S(2)}, u32[]{:S(2)}) collective-permute-start(bf16[8,2048]{1,0:T(8,128)(2,1)S(1)} %get-tuple-element.70), channel_id=1, source_target_pairs={{0,1},{1,0},{2,3},{3,2},{4,5},{5,4},{6,7},{7,6},{8,9},{9,8},{10,11... | collective-permute-start | bytes 98312 | tf_op jit(solution)/shard_map/ppermute | solution.py:50
  116.2 0.9 collective-permute-done.24
  117.1 0.6 maximum_select_fusion
  (33 shorter events, 2.7 us)
Async XLA Ops:
  1.5 2.4 %collective-permute-start = (bf16[8,2048]{1,0:T(8,128)(2,1)S(1)}, bf16[8,2048]{1,0:T(8,128)(2,1)S(1)}, u32[]{:S(2)}, u32[]{:S(2)}) collective-permute-start(bf16[8,2048]{1,0:T(8,128)(2,1)S(1)} %get-tuple-element.39), channel_id=1, source_target_pairs={{0,1},{1,0},{2,3},{3,2},{4,5},{5,4},{6,7},{7,6},{8,9},{9,8},{10,11... | collective-permute-start | bytes 98312 | tf_op jit(solution)/shard_map/ppermute | solution.py:50
  4.4 9.5 %collective-permute-start.4 = (bf16[224,8192]{1,0:T(8,128)(2,1)}, bf16[224,8192]{1,0:T(8,128)(2,1)S(1)}, u32[]{:S(2)}, u32[]{:S(2)}) collective-permute-start(bf16[224,8192]{1,0:T(8,128)(2,1)} %refs_1_), channel_id=1, source_target_pairs={{0,1},{1,0},{2,3},{3,2},{4,5},{5,4},{6,7},{7,6},{8,9},{9,8},{10,11... | collective-permute-start | bytes 11010056 | tf_op jit(solution)/shard_map/ppermute | solution.py:50
  4.8 8.5 %collective-permute-start.3 = (bf16[16,3584]{1,0:T(8,128)(2,1)S(1)}, bf16[16,3584]{1,0:T(8,128)(2,1)S(1)}, u32[]{:S(2)}, u32[]{:S(2)}) collective-permute-start(bf16[16,3584]{1,0:T(8,128)(2,1)S(1)} %get-tuple-element.42.message), channel_id=1, source_target_pairs={{0,66},{1,67},{2,64},{3,65},{4,70},{5,71},{6,68},{7,69},{8,74},{9,... | collective-permute-start | bytes 344072 | tf_op jit(solution)/shard_map/ppermute | solution.py:50
  8.7 3.4 %collective-permute-start.1 = (bf16[8,4096]{1,0:T(8,128)(2,1)S(1)}, bf16[8,4096]{1,0:T(8,128)(2,1)S(1)}, u32[]{:S(2)}, u32[]{:S(2)}) collective-permute-start(bf16[8,4096]{1,0:T(8,128)(2,1)S(1)} %get-tuple-element.41.wide), channel_id=1, source_target_pairs={{0,2},{1,3},{2,0},{3,1},{4,6},{5,7},{6,4},{7,5},{8,10},{9,11},{10,... | collective-permute-start | bytes 196616 | tf_op jit(solution)/shard_map/ppermute | solution.py:50
  8.7 4.6 %collective-permute-start.2 = (bf16[8,4096]{1,0:T(8,128)(2,1)S(1)}, bf16[8,4096]{1,0:T(8,128)(2,1)S(1)}, u32[]{:S(2)}, u32[]{:S(2)}) collective-permute-start(bf16[8,4096]{1,0:T(8,128)(2,1)S(1)} %get-tuple-element.41.wide), channel_id=1, source_target_pairs={{0,64},{1,65},{2,66},{3,67},{4,68},{5,69},{6,70},{7,71},{8,72},{9,... | collective-permute-start | bytes 196616 | tf_op jit(solution)/shard_map/ppermute | solution.py:50
  13.9 8.2 %collective-permute-start.5 = (bf16[16,11264]{1,0:T(8,128)(2,1)S(1)}, bf16[16,11264]{1,0:T(8,128)(2,1)S(1)}, u32[]{:S(2)}, u32[]{:S(2)}) collective-permute-start(bf16[16,11264]{1,0:T(8,128)(2,1)S(1)} %shard_map.102.own), channel_id=1, source_target_pairs={{0,8},{1,33},{2,10},{3,35},{4,12},{5,37},{6,14},{7,39},{8,0},{9,41... | collective-permute-start | bytes 1081352 | tf_op jit(solution)/shard_map/ppermute | solution.py:50
  16.9 9.4 %collective-permute-start.6 = (bf16[16,11264]{1,0:T(8,128)(2,1)S(1)}, bf16[16,11264]{1,0:T(8,128)(2,1)S(1)}, u32[]{:S(2)}, u32[]{:S(2)}) collective-permute-start(bf16[16,11264]{1,0:T(8,128)(2,1)S(1)} %shard_map.102.own), channel_id=1, source_target_pairs={{0,4},{1,17},{2,6},{3,19},{4,0},{5,21},{6,2},{7,23},{8,12},{9,25},... | collective-permute-start | bytes 1081352 | tf_op jit(solution)/shard_map/ppermute | solution.py:50
  17.3 9.0 %collective-permute-start.7 = (bf16[16,11264]{1,0:T(8,128)(2,1)S(1)}, bf16[16,11264]{1,0:T(8,128)(2,1)S(1)}, u32[]{:S(2)}, u32[]{:S(2)}) collective-permute-start(bf16[16,11264]{1,0:T(8,128)(2,1)S(1)} %shard_map.102.own), channel_id=1, source_target_pairs={{0,12},{1,49},{2,14},{3,51},{4,8},{5,53},{6,10},{7,55},{8,4},{9,57... | collective-permute-start | bytes 1081352 | tf_op jit(solution)/shard_map/ppermute | solution.py:50
  17.6 0.8 copy-start.3
  18.4 0.8 copy-start.4
  19.2 0.8 copy-start.5
  26.4 29.4 %collective-permute-start.10 = (bf16[224,8192]{1,0:T(8,128)(2,1)}, bf16[224,8192]{1,0:T(8,128)(2,1)S(1)}, u32[]{:S(2)}, u32[]{:S(2)}) collective-permute-start(bf16[224,8192]{1,0:T(8,128)(2,1)} %refs_3_), channel_id=1, source_target_pairs={{0,1},{1,0},{2,3},{3,2},{4,5},{5,4},{6,7},{7,6},{8,9},{9,8},{10,11... | collective-permute-start | bytes 11010056 | tf_op jit(solution)/shard_map/ppermute | solution.py:50
  28.7 31.2 %collective-permute-start.11 = (bf16[224,8192]{1,0:T(8,128)(2,1)}, bf16[224,8192]{1,0:T(8,128)(2,1)S(1)}, u32[]{:S(2)}, u32[]{:S(2)}) collective-permute-start(bf16[224,8192]{1,0:T(8,128)(2,1)} %down_w.2), channel_id=1, source_target_pairs={{0,1},{1,0},{2,3},{3,2},{4,5},{5,4},{6,7},{7,6},{8,9},{9,8},{10,11... | collective-permute-start | bytes 11010056 | tf_op jit(solution)/shard_map/ppermute | solution.py:50
  28.8 8.4 %collective-permute-start.12 = (bf16[64,3072]{1,0:T(8,128)(2,1)S(1)}, bf16[64,3072]{1,0:T(8,128)(2,1)S(1)}, u32[]{:S(2)}, u32[]{:S(2)}) collective-permute-start(bf16[64,3072]{1,0:T(8,128)(2,1)S(1)} %get-tuple-element.54.f0), channel_id=1, source_target_pairs={{0,32},{1,9},{2,34},{3,11},{4,36},{5,13},{6,38},{7,15},{8,40},{9,1... | collective-permute-start | bytes 1179656 | tf_op jit(solution)/shard_map/ppermute | solution.py:50
  31.4 21.3 %collective-permute-start.8 = (bf16[64,11264]{1,0:T(8,128)(2,1)S(1)}, bf16[64,11264]{1,0:T(8,128)(2,1)S(1)}, u32[]{:S(2)}, u32[]{:S(2)}) collective-permute-start(bf16[64,11264]{1,0:T(8,128)(2,1)S(1)} %get-tuple-element.50.refs_3_.own), channel_id=1, source_target_pairs={{0,16},{1,5},{2,18},{3,7},{4,20},{5,1},{6,22},{7,3},{8,24},{9,13},... | collective-permute-start | bytes 4325384 | tf_op jit(solution)/shard_map/ppermute | solution.py:50
  31.7 21.0 %collective-permute-start.9 = (bf16[64,11264]{1,0:T(8,128)(2,1)S(1)}, bf16[64,11264]{1,0:T(8,128)(2,1)S(1)}, u32[]{:S(2)}, u32[]{:S(2)}) collective-permute-start(bf16[64,11264]{1,0:T(8,128)(2,1)S(1)} %get-tuple-element.50.refs_3_.own), channel_id=1, source_target_pairs={{0,48},{1,13},{2,50},{3,15},{4,52},{5,9},{6,54},{7,11},{8,56},{9,5... | collective-permute-start | bytes 4325384 | tf_op jit(solution)/shard_map/ppermute | solution.py:50
  37.2 17.3 %copy-start.1 = (bf16[224,8192]{1,0:T(8,128)(2,1)S(1)}, bf16[224,8192]{1,0:T(8,128)(2,1)}, u32[]{:S(2)}) copy-start(bf16[224,8192]{1,0:T(8,128)(2,1)} %refs_1_) | copy-start | bytes 11010052
  37.2 17.3 %copy-start.2 = (bf16[224,8192]{1,0:T(8,128)(2,1)S(1)}, bf16[224,8192]{1,0:T(8,128)(2,1)}, u32[]{:S(2)}) copy-start(bf16[224,8192]{1,0:T(8,128)(2,1)} %refs_3_) | copy-start | bytes 11010052
  37.2 17.3 %copy-start = (bf16[224,8192]{1,0:T(8,128)(2,1)S(1)}, bf16[224,8192]{1,0:T(8,128)(2,1)}, u32[]{:S(2)}) copy-start(bf16[224,8192]{1,0:T(8,128)(2,1)} %down_w.2) | copy-start | bytes 11010052
  52.8 7.1 %collective-permute-start.13 = (bf16[256,3328]{1,0:T(8,128)(2,1)S(1)}, bf16[256,3328]{1,0:T(8,128)(2,1)S(1)}, u32[]{:S(2)}, u32[]{:S(2)}) collective-permute-start(bf16[256,3328]{1,0:T(8,128)(2,1)S(1)} %shard_map.108.factor), channel_id=1, source_target_pairs={{0,1},{1,0},{2,3},{3,2},{4,5},{5,4},{6,7},{7,6},{8,9},{9,8},{10,11... | collective-permute-start | bytes 5111816 | tf_op jit(solution)/shard_map/ppermute | solution.py:50
  54.6 14.0 %collective-permute-start.16 = (bf16[64,8192]{1,0:T(8,128)(2,1)S(1)}, bf16[64,8192]{1,0:T(8,128)(2,1)S(1)}, u32[]{:S(2)}, u32[]{:S(2)}) collective-permute-start(bf16[64,8192]{1,0:T(8,128)(2,1)S(1)} %shard_map.111), channel_id=1, source_target_pairs={{0,16},{1,5},{2,18},{3,7},{4,20},{5,1},{6,22},{7,3},{8,24},{9,13},... | collective-permute-start | bytes 3145736 | tf_op jit(solution)/shard_map/ppermute | solution.py:50
  65.8 15.2 %collective-permute-start.14 = (bf16[64,8192]{1,0:T(8,128)(2,1)S(1)}, bf16[64,8192]{1,0:T(8,128)(2,1)S(1)}, u32[]{:S(2)}, u32[]{:S(2)}) collective-permute-start(bf16[64,8192]{1,0:T(8,128)(2,1)S(1)} %get-tuple-element.56), channel_id=1, source_target_pairs={{0,48},{1,13},{2,50},{3,15},{4,52},{5,9},{6,54},{7,11},{8,56},{9,5... | collective-permute-start | bytes 3145736 | tf_op jit(solution)/shard_map/ppermute | solution.py:50
  67.6 13.9 %collective-permute-start.15 = (bf16[64,8192]{1,0:T(8,128)(2,1)S(1)}, bf16[64,8192]{1,0:T(8,128)(2,1)S(1)}, u32[]{:S(2)}, u32[]{:S(2)}) collective-permute-start(bf16[64,8192]{1,0:T(8,128)(2,1)S(1)} %get-tuple-element.57), channel_id=1, source_target_pairs={{0,16},{1,5},{2,18},{3,7},{4,20},{5,1},{6,22},{7,3},{8,24},{9,13},... | collective-permute-start | bytes 3145736 | tf_op jit(solution)/shard_map/ppermute | solution.py:50
  75.3 18.1 %collective-permute-start.17 = (bf16[64,8192]{1,0:T(8,128)(2,1)S(1)}, bf16[64,8192]{1,0:T(8,128)(2,1)S(1)}, u32[]{:S(2)}, u32[]{:S(2)}) collective-permute-start(bf16[64,8192]{1,0:T(8,128)(2,1)S(1)} %shard_map.113), channel_id=1, source_target_pairs={{0,32},{1,9},{2,34},{3,11},{4,36},{5,13},{6,38},{7,15},{8,40},{9,1... | collective-permute-start | bytes 3145736 | tf_op jit(solution)/shard_map/ppermute | solution.py:50
  93.6 7.1 %collective-permute-start.18 = (bf16[16,8192]{1,0:T(8,128)(2,1)S(1)}, bf16[16,8192]{1,0:T(8,128)(2,1)S(1)}, u32[]{:S(2)}, u32[]{:S(2)}) collective-permute-start(bf16[16,8192]{1,0:T(8,128)(2,1)S(1)} %get-tuple-element.62), channel_id=1, source_target_pairs={{0,8},{1,33},{2,10},{3,35},{4,12},{5,37},{6,14},{7,39},{8,0},{9,41... | collective-permute-start | bytes 786440 | tf_op jit(solution)/shard_map/ppermute | solution.py:50
  95.9 7.6 %collective-permute-start.19 = (bf16[16,8192]{1,0:T(8,128)(2,1)S(1)}, bf16[16,8192]{1,0:T(8,128)(2,1)S(1)}, u32[]{:S(2)}, u32[]{:S(2)}) collective-permute-start(bf16[16,8192]{1,0:T(8,128)(2,1)S(1)} %get-tuple-element.63), channel_id=1, source_target_pairs={{0,4},{1,17},{2,6},{3,19},{4,0},{5,21},{6,2},{7,23},{8,12},{9,25},... | collective-permute-start | bytes 786440 | tf_op jit(solution)/shard_map/ppermute | solution.py:50
  96.6 6.9 %collective-permute-start.20 = (bf16[16,8192]{1,0:T(8,128)(2,1)S(1)}, bf16[16,8192]{1,0:T(8,128)(2,1)S(1)}, u32[]{:S(2)}, u32[]{:S(2)}) collective-permute-start(bf16[16,8192]{1,0:T(8,128)(2,1)S(1)} %get-tuple-element.64), channel_id=1, source_target_pairs={{0,12},{1,49},{2,14},{3,51},{4,8},{5,53},{6,10},{7,55},{8,4},{9,57... | collective-permute-start | bytes 786440 | tf_op jit(solution)/shard_map/ppermute | solution.py:50
  104.2 4.7 %collective-permute-start.21 = (bf16[8,4096]{1,0:T(8,128)(2,1)S(1)}, bf16[8,4096]{1,0:T(8,128)(2,1)S(1)}, u32[]{:S(2)}, u32[]{:S(2)}) collective-permute-start(bf16[8,4096]{1,0:T(8,128)(2,1)S(1)} %get-tuple-element.66), channel_id=1, source_target_pairs={{0,64},{1,65},{2,66},{3,67},{4,68},{5,69},{6,70},{7,71},{8,72},{9,... | collective-permute-start | bytes 196616 | tf_op jit(solution)/shard_map/ppermute | solution.py:50
  105.5 3.8 %collective-permute-start.22 = (bf16[8,4096]{1,0:T(8,128)(2,1)S(1)}, bf16[8,4096]{1,0:T(8,128)(2,1)S(1)}, u32[]{:S(2)}, u32[]{:S(2)}) collective-permute-start(bf16[8,4096]{1,0:T(8,128)(2,1)S(1)} %get-tuple-element.67), channel_id=1, source_target_pairs={{0,2},{1,3},{2,0},{3,1},{4,6},{5,7},{6,4},{7,5},{8,10},{9,11},{10,... | collective-permute-start | bytes 196616 | tf_op jit(solution)/shard_map/ppermute | solution.py:50
  106.9 4.6 %collective-permute-start.23 = (bf16[8,4096]{1,0:T(8,128)(2,1)S(1)}, bf16[8,4096]{1,0:T(8,128)(2,1)S(1)}, u32[]{:S(2)}, u32[]{:S(2)}) collective-permute-start(bf16[8,4096]{1,0:T(8,128)(2,1)S(1)} %get-tuple-element.68), channel_id=1, source_target_pairs={{0,66},{1,67},{2,64},{3,65},{4,70},{5,71},{6,68},{7,69},{8,74},{9,... | collective-permute-start | bytes 196616 | tf_op jit(solution)/shard_map/ppermute | solution.py:50
  112.1 4.9 %collective-permute-start.24 = (bf16[8,2048]{1,0:T(8,128)(2,1)S(1)}, bf16[8,2048]{1,0:T(8,128)(2,1)S(1)}, u32[]{:S(2)}, u32[]{:S(2)}) collective-permute-start(bf16[8,2048]{1,0:T(8,128)(2,1)S(1)} %get-tuple-element.70), channel_id=1, source_target_pairs={{0,1},{1,0},{2,3},{3,2},{4,5},{5,4},{6,7},{7,6},{8,9},{9,8},{10,11... | collective-permute-start | bytes 98312 | tf_op jit(solution)/shard_map/ppermute | solution.py:50

commit v14 on v13

--- a/solution.py
+++ b/solution.py
@@ -133,8 +133,8 @@
 
 
 def first_down_kernel(
-    place, rows1, rows3, own, acc, down_w, down_w2, seconds, theirs, factor,
-    out1, out3, total, first, second, hidden,
+    place, rows1, rows3, acc, down_w, down_w2, seconds, theirs, factor,
+    out1, out3, first, second, hidden,
 ):
     homes = shard_homes(place)
 
@@ -145,16 +145,25 @@
                     piece = src[rows_at[learner % 16], cols[base + k][learner // 16]]
                     to[to_at[k], learner * 256 : learner * 256 + 256] = piece
 
-    low = low_rows((rows1, rows3, own), first, lambda i: gather(i, first, 4, 0))
-    finish(acc, low, seconds, theirs, hidden)
+    low = low_rows((rows1, rows3), first, lambda i: gather(i, first, 4, 0))
+    finish(acc[:, :128], low, seconds, theirs, hidden)
     for i in range(STEPS):
         tile = slice(i * TILE, (i + 1) * TILE)
         gather(i, second, 2, 4)
         w = jnp.concatenate([r[:, tile] for r in (down_w, down_w2, second)], axis=0)
         result = nn(hidden[...], w)
         out1[:, tile] = result[:64].astype(bf16)
-        out3[:, tile] = result[64:128].astype(bf16)
-        total[:, tile] = result[128:]
+        out3[:, tile] = result[64:].astype(bf16)
+
+
+def own_down_kernel(
+    own, acc, down_w, down_w2, seconds, theirs, first, second, total, hidden
+):
+    finish(acc[:, 128:], low_rows((own,), first), seconds, theirs, hidden)
+    for i in range(STEPS):
+        tile = slice(i * TILE, (i + 1) * TILE)
+        w = jnp.concatenate([r[:, tile] for r in (down_w, down_w2, second)], axis=0)
+        total[:, tile] = nn(hidden[...], w)
 
 
 def last_down_kernel(acc, down_w, down_w2, seconds, theirs, second, out2, hidden):
@@ -218,13 +227,12 @@
     )(*lead, *operands, *(pltpu.with_memory_space_constraint(a, pltpu.HBM) for a in far))
 
 
-def begin_kernel(place, inputs, gate, up, down, own, other, factor, ranks, sems):
-    c = place[3]
-    half = pl.ds(pl.multiple_of(c * 32, 32), 32)
-    copies = [pltpu.make_async_copy(inputs.at[c], own, sems.at[0])]
-    copies += [pltpu.make_async_copy(inputs.at[1 - c], other, sems.at[1])]
-    for k, r in enumerate((gate, up, down)):
-        copies += [pltpu.make_async_copy(r.at[half, :], ranks.at[k], sems.at[2 + k])]
+def half_kernel(place, gate, up, down, factor, ranks, sems):
+    half = pl.ds(pl.multiple_of(place[3] * 32, 32), 32)
+    copies = [
+        pltpu.make_async_copy(r.at[half, :], ranks.at[k], sems.at[k])
+        for k, r in enumerate((gate, up, down))
+    ]
     for copy in copies:
         copy.start()
     for copy in copies:
@@ -336,15 +344,16 @@
     zh, y, x, zl, c = (lax.axis_index(a) for a in AXES)
     place = jnp.stack([zh, y, x, c, zl]).astype(jnp.int32)
 
-    own, other, factor = local(
-        begin_kernel,
-        [((8, QUARTER), bf16), ((8, QUARTER), bf16), ((16, 1536), bf16)],
+    own = jnp.where(c == 0, inputs[0], inputs[1])
+    other = send(jnp.where(c == 0, inputs[1], inputs[0]), CORE)
+    (factor,) = local(
+        half_kernel,
+        [((16, 1536), bf16)],
         (),
         place,
-        far=(inputs, adapter_first_gate, adapter_first_up, adapter_second_down),
-        scratch=[pltpu.VMEM((3, 32, 256), bf16), pltpu.SemaphoreType.DMA((5,))],
-    )
-    other = send(other, CORE)
+        far=(adapter_first_gate, adapter_first_up, adapter_second_down),
+        scratch=[pltpu.VMEM((3, 32, 256), bf16), pltpu.SemaphoreType.DMA((3,))],
+    )
     wide, message = local(
         shape_kernel,
         [((8, HALF), bf16), ((16, QUARTER + 1536), bf16)],
@@ -392,29 +401,33 @@
     weights = (owned[0], gate2, owned[1], up2)
     down_weights = (owned[2], down2)
 
-    rows = (packed1, packed3, packed)
-    acc = project(rows, weights, price_of(CK), touched)
-    part1, part3, total, first, second = down(
+    acc = project((packed1, packed3, packed), weights, price_of(CK), touched)
+    part1, part3, first, second = down(
         first_down_kernel,
-        192,
-        [((64, WIDTH), bf16)] * 2
-        + [((64, WIDTH), f32), ((128, WIDTH), bf16), ((64, WIDTH), bf16)],
-        (*rows, acc, *down_weights, seconds, factor2, factor),
+        128,
+        [((64, WIDTH), bf16)] * 2 + [((128, WIDTH), bf16), ((64, WIDTH), bf16)],
+        (packed1, packed3, acc, *down_weights, seconds, factor2, factor),
         place,
     )
     back1, back3 = send(part1, SECOND[1]), send(part3, SECOND[3])
-    acc = project((after(rows2, part1),), (*weights, first), SMALL)
+    acc2 = project((after(rows2, part1),), (*weights, first), SMALL)
     (part2,) = down(
         last_down_kernel,
         64,
         [((64, WIDTH), bf16)],
-        (acc, *down_weights, seconds, factor2, second),
+        (acc2, *down_weights, seconds, factor2, second),
     )
     back2 = send(part2, SECOND[2])
+    (total,) = down(
+        own_down_kernel,
+        64,
+        [((64, WIDTH), f32)],
+        (packed, after(acc, part2), *down_weights, seconds, factor2, first, second),
+    )
     (total,) = local(
         add_kernel,
         [((64, WIDTH), f32)],
-        (total, back3, back1),
+        (total, back1, back3),
         price=price_of(4.5),
     )
     small = [((16, WIDTH), f32)] + [((16, WIDTH), bf16)] * 3

time: 118 us -> 117 us (level)
  waiting for transfers between devices: 57.4 us -> 53.5 us
  Pallas kernels: 21.1 us -> 23.1 us
    ppermute x25, waiting for transfers between devices: 57.4 us -> 53.5 us  [send(): return lax.ppermute(value, AXES, route)]
    pallas_call x2 -> x3, Pallas kernels: 7.84 us -> 9.9 us  [down(): pl.pallas_call(body, in_specs=[SMEM] * len(lead) + [VMEM] * len(operands)...]
  transfers between devices with their start and end apart: 25 -> 25, of which waited for: 17 -> 15; matrix products, arithmetic and copies ran while one was open for 0% -> 0% of each run, Pallas kernels for 15% -> 18%
where the time goes in v14:
time: 117 us
  waiting for transfers between devices  53.5 us (46%)
  starting transfers between devices  36.1 us (31%)
  Pallas kernels  23.1 us (20%)
  local copies, waits for them, and re-layouts  2.37 us (2%)
  other arithmetic  1.42 us (1%)
    ppermute x25, waiting for transfers between devices, send(): return lax.ppermute(value, AXES, route)  53.5 us
    ppermute x25, starting transfers between devices, send(): return lax.ppermute(value, AXES, route)  36.1 us
    pallas_call x3, Pallas kernels, down(): pl.pallas_call(body, in_specs=[SMEM] * len(lead) + [VMEM] * len(operands)...  9.9 us
    pallas_call x2, Pallas kernels, project(): pl.pallas_call(lambda *refs: project_kernel(n, *refs[more:]), in_specs=[V...  8.69 us
    pallas_call x13, Pallas kernels, local(): pl.pallas_call(body, in_specs=[SMEM] * len(lead) + [VMEM] * len(operands)...  4.52 us
  transfers between devices with their start and end apart: 25, of which 15 were waited for; matrix products, arithmetic and copies ran while one was open for 0% of the time, Pallas kernels for 18%

profile of v14, /device:TPU:1, one launch (start us, length us, event | category | flops | bytes accessed | tf_op | source)
XLA Modules:
  0.0 116.6 jit_solution(592259265421537166)
XLA Ops:
  0.0 0.8 select_bitcast_fusion
  0.8 1.5 %collective-permute-start = (bf16[8,2048]{1,0:T(8,128)(2,1)S(1)}, bf16[8,2048]{1,0:T(8,128)(2,1)S(1)}, u32[]{:S(2)}, u32[]{:S(2)}) collective-permute-start(bf16[8,2048]{1,0:T(8,128)(2,1)S(1)} %get-tuple-element.65), channel_id=1, source_target_pairs={{0,1},{1,0},{2,3},{3,2},{4,5},{5,4},{6,7},{7,6},{8,9},{9,8},{10,11... | collective-permute-start | bytes 98312 | tf_op jit(solution)/shard_map/ppermute | solution.py:50
  2.4 1.3 %shard_map.100.factor = bf16[16,1536]{1,0:T(8,128)(2,1)S(1)} custom-call(s32[5]{0:T(128)S(1)} %stack.37.place, bf16[64,256]{1,0:T(8,128)(2,1)} %gate.1, bf16[64,256]{1,0:T(8,128)(2,1)} %up.1, bf16[64,256]{1,0:T(8,128)(2,1)} %down.1), custom_call_target="tpu_custom_call" | custom-call | flops 1 | bytes 1 | tf_op jit(solution)/shard_map/pallas_call | solution.py:217
  3.7 0.6 shard_map.101
  4.4 3.9 %collective-permute-start.3 = (bf16[16,3584]{1,0:T(8,128)(2,1)S(1)}, bf16[16,3584]{1,0:T(8,128)(2,1)S(1)}, u32[]{:S(2)}, u32[]{:S(2)}) collective-permute-start(bf16[16,3584]{1,0:T(8,128)(2,1)S(1)} %get-tuple-element.36.message), channel_id=1, source_target_pairs={{0,66},{1,67},{2,64},{3,65},{4,70},{5,71},{6,68},{7,69},{8,74},{9,... | collective-permute-start | bytes 344072 | tf_op jit(solution)/shard_map/ppermute | solution.py:50
  8.3 1.3 %collective-permute-start.2 = (bf16[8,4096]{1,0:T(8,128)(2,1)S(1)}, bf16[8,4096]{1,0:T(8,128)(2,1)S(1)}, u32[]{:S(2)}, u32[]{:S(2)}) collective-permute-start(bf16[8,4096]{1,0:T(8,128)(2,1)S(1)} %get-tuple-element.35.wide), channel_id=1, source_target_pairs={{0,64},{1,65},{2,66},{3,67},{4,68},{5,69},{6,70},{7,71},{8,72},{9,... | collective-permute-start | bytes 196616 | tf_op jit(solution)/shard_map/ppermute | solution.py:50
  9.6 2.1 %collective-permute-done.1.z1 = bf16[8,4096]{1,0:T(8,128)(2,1)S(1)} collective-permute-done((bf16[8,4096]{1,0:T(8,128)(2,1)S(1)}, bf16[8,4096]{1,0:T(8,128)(2,1)S(1)}, u32[]{:S(2)}, u32[]{:S(2)}) %collective-permute-start.1) | collective-permute-done | bytes 65568 | tf_op jit(solution)/shard_map/ppermute | solution.py:50
  11.7 1.2 %collective-permute-done.2.z2 = bf16[8,4096]{1,0:T(8,128)(2,1)S(1)} collective-permute-done((bf16[8,4096]{1,0:T(8,128)(2,1)S(1)}, bf16[8,4096]{1,0:T(8,128)(2,1)S(1)}, u32[]{:S(2)}, u32[]{:S(2)}) %collective-permute-start.2) | collective-permute-done | bytes 65568 | tf_op jit(solution)/shard_map/ppermute | solution.py:50
  12.9 0.6 shard_map.102.own
  13.5 3.0 %collective-permute-start.5 = (bf16[16,11264]{1,0:T(8,128)(2,1)S(1)}, bf16[16,11264]{1,0:T(8,128)(2,1)S(1)}, u32[]{:S(2)}, u32[]{:S(2)}) collective-permute-start(bf16[16,11264]{1,0:T(8,128)(2,1)S(1)} %shard_map.102.own), channel_id=1, source_target_pairs={{0,8},{1,33},{2,10},{3,35},{4,12},{5,37},{6,14},{7,39},{8,0},{9,41... | collective-permute-start | bytes 1081352 | tf_op jit(solution)/shard_map/ppermute | solution.py:50
  16.5 0.4 collective-permute-start.6
  16.9 0.4 collective-permute-start.7
  17.3 0.8 copy-done.3
  18.0 0.8 copy-done.4
  18.8 0.8 copy-done.5
  19.6 2.1 %collective-permute-done.5.got2 = bf16[16,11264]{1,0:T(8,128)(2,1)S(1)} collective-permute-done((bf16[16,11264]{1,0:T(8,128)(2,1)S(1)}, bf16[16,11264]{1,0:T(8,128)(2,1)S(1)}, u32[]{:S(2)}, u32[]{:S(2)}) %collective-permute-start.5) | collective-permute-done | bytes 360480 | tf_op jit(solution)/shard_map/ppermute | solution.py:50
  21.7 4.2 %collective-permute-done.6.got1 = bf16[16,11264]{1,0:T(8,128)(2,1)S(1)} collective-permute-done((bf16[16,11264]{1,0:T(8,128)(2,1)S(1)}, bf16[16,11264]{1,0:T(8,128)(2,1)S(1)}, u32[]{:S(2)}, u32[]{:S(2)}) %collective-permute-start.6) | collective-permute-done | bytes 360480 | tf_op jit(solution)/shard_map/ppermute | solution.py:50
  26.0 2.5 %collective-permute-start.10 = (bf16[224,8192]{1,0:T(8,128)(2,1)}, bf16[224,8192]{1,0:T(8,128)(2,1)S(1)}, u32[]{:S(2)}, u32[]{:S(2)}) collective-permute-start(bf16[224,8192]{1,0:T(8,128)(2,1)} %refs_3_), channel_id=1, source_target_pairs={{0,1},{1,0},{2,3},{3,2},{4,5},{5,4},{6,7},{7,6},{8,9},{9,8},{10,11... | collective-permute-start | bytes 11010056 | tf_op jit(solution)/shard_map/ppermute | solution.py:50
  28.6 2.6 %collective-permute-start.13 = (bf16[64,3072]{1,0:T(8,128)(2,1)S(1)}, bf16[64,3072]{1,0:T(8,128)(2,1)S(1)}, u32[]{:S(2)}, u32[]{:S(2)}) collective-permute-start(bf16[64,3072]{1,0:T(8,128)(2,1)S(1)} %get-tuple-element.48.f0), channel_id=1, source_target_pairs={{0,32},{1,9},{2,34},{3,11},{4,36},{5,13},{6,38},{7,15},{8,40},{9,1... | collective-permute-start | bytes 1179656 | tf_op jit(solution)/shard_map/ppermute | solution.py:50
  31.6 0.6 collective-permute-start.9
  32.2 4.9 %collective-permute-done.13.refs_0_ = bf16[64,3072]{1,0:T(8,128)(2,1)S(1)} collective-permute-done((bf16[64,3072]{1,0:T(8,128)(2,1)S(1)}, bf16[64,3072]{1,0:T(8,128)(2,1)S(1)}, u32[]{:S(2)}, u32[]{:S(2)}) %collective-permute-start.13) | collective-permute-done | bytes 393248 | tf_op jit(solution)/shard_map/ppermute | solution.py:50
  37.1 15.4 %collective-permute-done.8.refs_1_.packed1.rows1 = bf16[64,11264]{1,0:T(8,128)(2,1)S(1)} collective-permute-done((bf16[64,11264]{1,0:T(8,128)(2,1)S(1)}, bf16[64,11264]{1,0:T(8,128)(2,1)S(1)}, u32[]{:S(2)}, u32[]{:S(2)}) %collective-permute-start.8) | collective-permute-done | bytes 1441824 | tf_op jit(solution)/shard_map/ppermute | solution.py:50
  52.6 1.7 %collective-permute-start.14 = (bf16[256,3328]{1,0:T(8,128)(2,1)S(1)}, bf16[256,3328]{1,0:T(8,128)(2,1)S(1)}, u32[]{:S(2)}, u32[]{:S(2)}) collective-permute-start(bf16[256,3328]{1,0:T(8,128)(2,1)S(1)} %shard_map.109.factor), channel_id=1, source_target_pairs={{0,1},{1,0},{2,3},{3,2},{4,5},{5,4},{6,7},{7,6},{8,9},{9,8},{10,11... | collective-permute-start | bytes 5111816 | tf_op jit(solution)/shard_map/ppermute | solution.py:50
  54.5 1.2 %collective-permute-start.11 = (bf16[64,8192]{1,0:T(8,128)(2,1)S(1)}, bf16[64,8192]{1,0:T(8,128)(2,1)S(1)}, u32[]{:S(2)}, u32[]{:S(2)}) collective-permute-start(bf16[64,8192]{1,0:T(8,128)(2,1)S(1)} %shard_map.107), channel_id=1, source_target_pairs={{0,16},{1,5},{2,18},{3,7},{4,20},{5,1},{6,22},{7,3},{8,24},{9,13},... | collective-permute-start | bytes 3145736 | tf_op jit(solution)/shard_map/ppermute | solution.py:50
  55.7 4.1 %shard_map.106.acc = f32[896,192]{1,0:T(8,128)S(1)} custom-call(f32[8,128]{1,0:T(8,128)S(1)} %shard_map.105.refs_0_, bf16[64,11264]{1,0:T(8,128)(2,1)S(1)} %collective-permute-done.8.refs_1_.packed1.rows1, bf16[64,11264]{1,0:T(8,128)(2,1)S(1)} %collective-permute-done.9.refs_2_.refs_0_.packed3.rows3, bf16[64,11264]{1,0:T(8,128)(2,1)S(1)} %get-tuple-element.44.refs_3_.own, ...), custom_call_target="tpu_custom_call" | custom-call | flops 9200000000 | bytes 28800000 | tf_op jit(solution)/shard_map/pallas_call | solution.py:193
  59.8 4.3 %shard_map.110 = (bf16[64,8192]{1,0:T(8,128)(2,1)S(1)}, bf16[64,8192]{1,0:T(8,128)(2,1)S(1)}, bf16[128,8192]{1,0:T(8,128)(2,1)S(1)}, bf16[64,8192]{1,0:T(8,128)(2,1)S(1)}) custom-call(s32[5]{0:T(128)S(1)} %stack.37.place, bf16[64,11264]{1,0:T(8,128)(2,1)S(1)} %collective-permute-done.8.refs_1_.packed1.rows1, ...), custom_call_target="tpu_custom_call" | custom-call | flops 1 | bytes 1 | tf_op jit(solution)/shard_map/pallas_call | solution.py:204
  64.5 2.4 %collective-permute-start.16 = (bf16[64,8192]{1,0:T(8,128)(2,1)S(1)}, bf16[64,8192]{1,0:T(8,128)(2,1)S(1)}, u32[]{:S(2)}, u32[]{:S(2)}) collective-permute-start(bf16[64,8192]{1,0:T(8,128)(2,1)S(1)} %get-tuple-element.54), channel_id=1, source_target_pairs={{0,48},{1,13},{2,50},{3,15},{4,52},{5,9},{6,54},{7,11},{8,56},{9,5... | collective-permute-start | bytes 3145736 | tf_op jit(solution)/shard_map/ppermute | solution.py:50
  66.9 1.6 %collective-permute-done.11.refs_0_ = bf16[64,8192]{1,0:T(8,128)(2,1)S(1)} collective-permute-done((bf16[64,8192]{1,0:T(8,128)(2,1)S(1)}, bf16[64,8192]{1,0:T(8,128)(2,1)S(1)}, u32[]{:S(2)}, u32[]{:S(2)}) %collective-permute-start.11) | collective-permute-done | bytes 1048608 | tf_op jit(solution)/shard_map/ppermute | solution.py:50
  68.5 4.6 %shard_map.111.acc = f32[1024,64]{1,0:T(8,128)S(1)} custom-call(bf16[64,8192]{1,0:T(8,128)(2,1)S(1)} %collective-permute-done.11.refs_0_, bf16[224,8192]{1,0:T(8,128)(2,1)S(1)} %copy-done.1, bf16[224,8192]{1,0:T(8,128)(2,1)S(1)} %collective-permute-done.4.refs_5_.refs_2_, bf16[224,8192]{1,0:T(8,128)(2,1)S(1)} %copy-done.2, ...), custom_call_target="tpu_custom_call" | custom-call | flops 1 | bytes 1 | tf_op jit(solution)/shard_map/pallas_call | solution.py:193
  73.1 2.0 %shard_map.112 = bf16[64,8192]{1,0:T(8,128)(2,1)S(1)} custom-call(f32[1024,64]{1,0:T(8,128)S(1)} %shard_map.111.acc, bf16[224,8192]{1,0:T(8,128)(2,1)S(1)} %copy-done, bf16[224,8192]{1,0:T(8,128)(2,1)S(1)} %collective-permute-done.12.down_w2, bf16[256,256]{1,0:T(8,128)(2,1)S(1)} %shard_map.104.seconds, bf16[256,3328]{1,0:T(8,128)(2,1)S(1)} %collective-permute-done.14.theirs, ...), custom_call_target="tpu_custom_call" | custom-call | flops 1 | bytes 1 | tf_op jit(solution)/shard_map/pallas_call | solution.py:204
  75.1 2.7 %collective-permute-start.17 = (bf16[64,8192]{1,0:T(8,128)(2,1)S(1)}, bf16[64,8192]{1,0:T(8,128)(2,1)S(1)}, u32[]{:S(2)}, u32[]{:S(2)}) collective-permute-start(bf16[64,8192]{1,0:T(8,128)(2,1)S(1)} %shard_map.112), channel_id=1, source_target_pairs={{0,32},{1,9},{2,34},{3,11},{4,36},{5,13},{6,38},{7,15},{8,40},{9,1... | collective-permute-start | bytes 3145736 | tf_op jit(solution)/shard_map/ppermute | solution.py:50
  77.8 3.6 %shard_map.113.own = f32[64,8192]{1,0:T(8,128)S(1)} custom-call(bf16[64,11264]{1,0:T(8,128)(2,1)S(1)} %get-tuple-element.44.refs_3_.own, f32[896,192]{1,0:T(8,128)S(1)} %shard_map.106.acc, bf16[224,8192]{1,0:T(8,128)(2,1)S(1)} %copy-done, bf16[224,8192]{1,0:T(8,128)(2,1)S(1)} %collective-permute-done.12.down_w2, bf16[256,256]{1,0:T(8,128)(2,1)S(1)} %shard_map.104.seconds, ...), custom_call_target="tpu_custom_call" | custom-call | flops 1 | bytes 1 | tf_op jit(solution)/shard_map/pallas_call | solution.py:204
  81.7 11.3 %collective-permute-done.17.b = bf16[64,8192]{1,0:T(8,128)(2,1)S(1)} collective-permute-done((bf16[64,8192]{1,0:T(8,128)(2,1)S(1)}, bf16[64,8192]{1,0:T(8,128)(2,1)S(1)}, u32[]{:S(2)}, u32[]{:S(2)}) %collective-permute-start.17) | collective-permute-done | bytes 1048608 | tf_op jit(solution)/shard_map/ppermute | solution.py:50
  93.2 2.3 %collective-permute-start.18 = (bf16[16,8192]{1,0:T(8,128)(2,1)S(1)}, bf16[16,8192]{1,0:T(8,128)(2,1)S(1)}, u32[]{:S(2)}, u32[]{:S(2)}) collective-permute-start(bf16[16,8192]{1,0:T(8,128)(2,1)S(1)} %get-tuple-element.56), channel_id=1, source_target_pairs={{0,8},{1,33},{2,10},{3,35},{4,12},{5,37},{6,14},{7,39},{8,0},{9,41... | collective-permute-start | bytes 786440 | tf_op jit(solution)/shard_map/ppermute | solution.py:50
  95.5 0.4 collective-permute-start.19
  95.9 0.6 collective-permute-start.20
  96.5 3.8 %collective-permute-done.18.b2 = bf16[16,8192]{1,0:T(8,128)(2,1)S(1)} collective-permute-done((bf16[16,8192]{1,0:T(8,128)(2,1)S(1)}, bf16[16,8192]{1,0:T(8,128)(2,1)S(1)}, u32[]{:S(2)}, u32[]{:S(2)}) %collective-permute-start.18) | collective-permute-done | bytes 262176 | tf_op jit(solution)/shard_map/ppermute | solution.py:50
  100.3 2.5 %collective-permute-done.19.b1 = bf16[16,8192]{1,0:T(8,128)(2,1)S(1)} collective-permute-done((bf16[16,8192]{1,0:T(8,128)(2,1)S(1)}, bf16[16,8192]{1,0:T(8,128)(2,1)S(1)}, u32[]{:S(2)}, u32[]{:S(2)}) %collective-permute-start.19) | collective-permute-done | bytes 262176 | tf_op jit(solution)/shard_map/ppermute | solution.py:50
  103.1 0.7 shard_map.116
  103.8 1.3 %collective-permute-start.21 = (bf16[8,4096]{1,0:T(8,128)(2,1)S(1)}, bf16[8,4096]{1,0:T(8,128)(2,1)S(1)}, u32[]{:S(2)}, u32[]{:S(2)}) collective-permute-start(bf16[8,4096]{1,0:T(8,128)(2,1)S(1)} %get-tuple-element.60), channel_id=1, source_target_pairs={{0,64},{1,65},{2,66},{3,67},{4,68},{5,69},{6,70},{7,71},{8,72},{9,... | collective-permute-start | bytes 196616 | tf_op jit(solution)/shard_map/ppermute | solution.py:50
  105.0 1.2 %collective-permute-start.22 = (bf16[8,4096]{1,0:T(8,128)(2,1)S(1)}, bf16[8,4096]{1,0:T(8,128)(2,1)S(1)}, u32[]{:S(2)}, u32[]{:S(2)}) collective-permute-start(bf16[8,4096]{1,0:T(8,128)(2,1)S(1)} %get-tuple-element.61), channel_id=1, source_target_pairs={{0,2},{1,3},{2,0},{3,1},{4,6},{5,7},{6,4},{7,5},{8,10},{9,11},{10,... | collective-permute-start | bytes 196616 | tf_op jit(solution)/shard_map/ppermute | solution.py:50
  106.3 1.7 %collective-permute-start.23 = (bf16[8,4096]{1,0:T(8,128)(2,1)S(1)}, bf16[8,4096]{1,0:T(8,128)(2,1)S(1)}, u32[]{:S(2)}, u32[]{:S(2)}) collective-permute-start(bf16[8,4096]{1,0:T(8,128)(2,1)S(1)} %get-tuple-element.62), channel_id=1, source_target_pairs={{0,66},{1,67},{2,64},{3,65},{4,70},{5,71},{6,68},{7,69},{8,74},{9,... | collective-permute-start | bytes 196616 | tf_op jit(solution)/shard_map/ppermute | solution.py:50
  108.0 0.5 collective-permute-done.21.b2
  108.6 2.5 %collective-permute-done.23.b3 = bf16[8,4096]{1,0:T(8,128)(2,1)S(1)} collective-permute-done((bf16[8,4096]{1,0:T(8,128)(2,1)S(1)}, bf16[8,4096]{1,0:T(8,128)(2,1)S(1)}, u32[]{:S(2)}, u32[]{:S(2)}) %collective-permute-start.23) | collective-permute-done | bytes 65568 | tf_op jit(solution)/shard_map/ppermute | solution.py:50
  111.1 0.6 shard_map.117
  111.7 3.4 %collective-permute-start.24 = (bf16[8,2048]{1,0:T(8,128)(2,1)S(1)}, bf16[8,2048]{1,0:T(8,128)(2,1)S(1)}, u32[]{:S(2)}, u32[]{:S(2)}) collective-permute-start(bf16[8,2048]{1,0:T(8,128)(2,1)S(1)} %get-tuple-element.64), channel_id=1, source_target_pairs={{0,1},{1,0},{2,3},{3,2},{4,5},{5,4},{6,7},{7,6},{8,9},{9,8},{10,11... | collective-permute-start | bytes 98312 | tf_op jit(solution)/shard_map/ppermute | solution.py:50
  115.1 0.9 collective-permute-done.24
  116.0 0.6 maximum_select_fusion
  (35 shorter events, 2.3 us)
Async XLA Ops:
  0.8 2.9 %collective-permute-start = (bf16[8,2048]{1,0:T(8,128)(2,1)S(1)}, bf16[8,2048]{1,0:T(8,128)(2,1)S(1)}, u32[]{:S(2)}, u32[]{:S(2)}) collective-permute-start(bf16[8,2048]{1,0:T(8,128)(2,1)S(1)} %get-tuple-element.65), channel_id=1, source_target_pairs={{0,1},{1,0},{2,3},{3,2},{4,5},{5,4},{6,7},{7,6},{8,9},{9,8},{10,11... | collective-permute-start | bytes 98312 | tf_op jit(solution)/shard_map/ppermute | solution.py:50
  4.3 9.2 %collective-permute-start.4 = (bf16[224,8192]{1,0:T(8,128)(2,1)}, bf16[224,8192]{1,0:T(8,128)(2,1)S(1)}, u32[]{:S(2)}, u32[]{:S(2)}) collective-permute-start(bf16[224,8192]{1,0:T(8,128)(2,1)} %refs_1_), channel_id=1, source_target_pairs={{0,1},{1,0},{2,3},{3,2},{4,5},{5,4},{6,7},{7,6},{8,9},{9,8},{10,11... | collective-permute-start | bytes 11010056 | tf_op jit(solution)/shard_map/ppermute | solution.py:50
  4.4 8.5 %collective-permute-start.3 = (bf16[16,3584]{1,0:T(8,128)(2,1)S(1)}, bf16[16,3584]{1,0:T(8,128)(2,1)S(1)}, u32[]{:S(2)}, u32[]{:S(2)}) collective-permute-start(bf16[16,3584]{1,0:T(8,128)(2,1)S(1)} %get-tuple-element.36.message), channel_id=1, source_target_pairs={{0,66},{1,67},{2,64},{3,65},{4,70},{5,71},{6,68},{7,69},{8,74},{9,... | collective-permute-start | bytes 344072 | tf_op jit(solution)/shard_map/ppermute | solution.py:50
  8.3 3.4 %collective-permute-start.1 = (bf16[8,4096]{1,0:T(8,128)(2,1)S(1)}, bf16[8,4096]{1,0:T(8,128)(2,1)S(1)}, u32[]{:S(2)}, u32[]{:S(2)}) collective-permute-start(bf16[8,4096]{1,0:T(8,128)(2,1)S(1)} %get-tuple-element.35.wide), channel_id=1, source_target_pairs={{0,2},{1,3},{2,0},{3,1},{4,6},{5,7},{6,4},{7,5},{8,10},{9,11},{10,... | collective-permute-start | bytes 196616 | tf_op jit(solution)/shard_map/ppermute | solution.py:50
  8.3 4.6 %collective-permute-start.2 = (bf16[8,4096]{1,0:T(8,128)(2,1)S(1)}, bf16[8,4096]{1,0:T(8,128)(2,1)S(1)}, u32[]{:S(2)}, u32[]{:S(2)}) collective-permute-start(bf16[8,4096]{1,0:T(8,128)(2,1)S(1)} %get-tuple-element.35.wide), channel_id=1, source_target_pairs={{0,64},{1,65},{2,66},{3,67},{4,68},{5,69},{6,70},{7,71},{8,72},{9,... | collective-permute-start | bytes 196616 | tf_op jit(solution)/shard_map/ppermute | solution.py:50
  13.5 8.2 %collective-permute-start.5 = (bf16[16,11264]{1,0:T(8,128)(2,1)S(1)}, bf16[16,11264]{1,0:T(8,128)(2,1)S(1)}, u32[]{:S(2)}, u32[]{:S(2)}) collective-permute-start(bf16[16,11264]{1,0:T(8,128)(2,1)S(1)} %shard_map.102.own), channel_id=1, source_target_pairs={{0,8},{1,33},{2,10},{3,35},{4,12},{5,37},{6,14},{7,39},{8,0},{9,41... | collective-permute-start | bytes 1081352 | tf_op jit(solution)/shard_map/ppermute | solution.py:50
  16.5 9.4 %collective-permute-start.6 = (bf16[16,11264]{1,0:T(8,128)(2,1)S(1)}, bf16[16,11264]{1,0:T(8,128)(2,1)S(1)}, u32[]{:S(2)}, u32[]{:S(2)}) collective-permute-start(bf16[16,11264]{1,0:T(8,128)(2,1)S(1)} %shard_map.102.own), channel_id=1, source_target_pairs={{0,4},{1,17},{2,6},{3,19},{4,0},{5,21},{6,2},{7,23},{8,12},{9,25},... | collective-permute-start | bytes 1081352 | tf_op jit(solution)/shard_map/ppermute | solution.py:50
  16.9 9.0 %collective-permute-start.7 = (bf16[16,11264]{1,0:T(8,128)(2,1)S(1)}, bf16[16,11264]{1,0:T(8,128)(2,1)S(1)}, u32[]{:S(2)}, u32[]{:S(2)}) collective-permute-start(bf16[16,11264]{1,0:T(8,128)(2,1)S(1)} %shard_map.102.own), channel_id=1, source_target_pairs={{0,12},{1,49},{2,14},{3,51},{4,8},{5,53},{6,10},{7,55},{8,4},{9,57... | collective-permute-start | bytes 1081352 | tf_op jit(solution)/shard_map/ppermute | solution.py:50
  17.3 0.8 copy-start.3
  18.0 0.8 copy-start.4
  18.8 0.8 copy-start.5
  26.0 29.7 %collective-permute-start.10 = (bf16[224,8192]{1,0:T(8,128)(2,1)}, bf16[224,8192]{1,0:T(8,128)(2,1)S(1)}, u32[]{:S(2)}, u32[]{:S(2)}) collective-permute-start(bf16[224,8192]{1,0:T(8,128)(2,1)} %refs_3_), channel_id=1, source_target_pairs={{0,1},{1,0},{2,3},{3,2},{4,5},{5,4},{6,7},{7,6},{8,9},{9,8},{10,11... | collective-permute-start | bytes 11010056 | tf_op jit(solution)/shard_map/ppermute | solution.py:50
  28.6 31.2 %collective-permute-start.12 = (bf16[224,8192]{1,0:T(8,128)(2,1)}, bf16[224,8192]{1,0:T(8,128)(2,1)S(1)}, u32[]{:S(2)}, u32[]{:S(2)}) collective-permute-start(bf16[224,8192]{1,0:T(8,128)(2,1)} %down_w.3), channel_id=1, source_target_pairs={{0,1},{1,0},{2,3},{3,2},{4,5},{5,4},{6,7},{7,6},{8,9},{9,8},{10,11... | collective-permute-start | bytes 11010056 | tf_op jit(solution)/shard_map/ppermute | solution.py:50
  28.6 8.4 %collective-permute-start.13 = (bf16[64,3072]{1,0:T(8,128)(2,1)S(1)}, bf16[64,3072]{1,0:T(8,128)(2,1)S(1)}, u32[]{:S(2)}, u32[]{:S(2)}) collective-permute-start(bf16[64,3072]{1,0:T(8,128)(2,1)S(1)} %get-tuple-element.48.f0), channel_id=1, source_target_pairs={{0,32},{1,9},{2,34},{3,11},{4,36},{5,13},{6,38},{7,15},{8,40},{9,1... | collective-permute-start | bytes 1179656 | tf_op jit(solution)/shard_map/ppermute | solution.py:50
  31.3 21.3 %collective-permute-start.8 = (bf16[64,11264]{1,0:T(8,128)(2,1)S(1)}, bf16[64,11264]{1,0:T(8,128)(2,1)S(1)}, u32[]{:S(2)}, u32[]{:S(2)}) collective-permute-start(bf16[64,11264]{1,0:T(8,128)(2,1)S(1)} %get-tuple-element.44.refs_3_.own), channel_id=1, source_target_pairs={{0,16},{1,5},{2,18},{3,7},{4,20},{5,1},{6,22},{7,3},{8,24},{9,13},... | collective-permute-start | bytes 4325384 | tf_op jit(solution)/shard_map/ppermute | solution.py:50
  31.6 21.0 %collective-permute-start.9 = (bf16[64,11264]{1,0:T(8,128)(2,1)S(1)}, bf16[64,11264]{1,0:T(8,128)(2,1)S(1)}, u32[]{:S(2)}, u32[]{:S(2)}) collective-permute-start(bf16[64,11264]{1,0:T(8,128)(2,1)S(1)} %get-tuple-element.44.refs_3_.own), channel_id=1, source_target_pairs={{0,48},{1,13},{2,50},{3,15},{4,52},{5,9},{6,54},{7,11},{8,56},{9,5... | collective-permute-start | bytes 4325384 | tf_op jit(solution)/shard_map/ppermute | solution.py:50
  37.1 17.3 %copy-start.1 = (bf16[224,8192]{1,0:T(8,128)(2,1)S(1)}, bf16[224,8192]{1,0:T(8,128)(2,1)}, u32[]{:S(2)}) copy-start(bf16[224,8192]{1,0:T(8,128)(2,1)} %refs_1_) | copy-start | bytes 11010052
  37.1 17.3 %copy-start.2 = (bf16[224,8192]{1,0:T(8,128)(2,1)S(1)}, bf16[224,8192]{1,0:T(8,128)(2,1)}, u32[]{:S(2)}) copy-start(bf16[224,8192]{1,0:T(8,128)(2,1)} %refs_3_) | copy-start | bytes 11010052
  37.1 17.3 %copy-start = (bf16[224,8192]{1,0:T(8,128)(2,1)S(1)}, bf16[224,8192]{1,0:T(8,128)(2,1)}, u32[]{:S(2)}) copy-start(bf16[224,8192]{1,0:T(8,128)(2,1)} %down_w.3) | copy-start | bytes 11010052
  52.6 7.1 %collective-permute-start.14 = (bf16[256,3328]{1,0:T(8,128)(2,1)S(1)}, bf16[256,3328]{1,0:T(8,128)(2,1)S(1)}, u32[]{:S(2)}, u32[]{:S(2)}) collective-permute-start(bf16[256,3328]{1,0:T(8,128)(2,1)S(1)} %shard_map.109.factor), channel_id=1, source_target_pairs={{0,1},{1,0},{2,3},{3,2},{4,5},{5,4},{6,7},{7,6},{8,9},{9,8},{10,11... | collective-permute-start | bytes 5111816 | tf_op jit(solution)/shard_map/ppermute | solution.py:50
  54.5 14.0 %collective-permute-start.11 = (bf16[64,8192]{1,0:T(8,128)(2,1)S(1)}, bf16[64,8192]{1,0:T(8,128)(2,1)S(1)}, u32[]{:S(2)}, u32[]{:S(2)}) collective-permute-start(bf16[64,8192]{1,0:T(8,128)(2,1)S(1)} %shard_map.107), channel_id=1, source_target_pairs={{0,16},{1,5},{2,18},{3,7},{4,20},{5,1},{6,22},{7,3},{8,24},{9,13},... | collective-permute-start | bytes 3145736 | tf_op jit(solution)/shard_map/ppermute | solution.py:50
  64.1 17.2 %collective-permute-start.15 = (bf16[64,8192]{1,0:T(8,128)(2,1)S(1)}, bf16[64,8192]{1,0:T(8,128)(2,1)S(1)}, u32[]{:S(2)}, u32[]{:S(2)}) collective-permute-start(bf16[64,8192]{1,0:T(8,128)(2,1)S(1)} %get-tuple-element.49), channel_id=1, source_target_pairs={{0,16},{1,5},{2,18},{3,7},{4,20},{5,1},{6,22},{7,3},{8,24},{9,13},... | collective-permute-start | bytes 3145736 | tf_op jit(solution)/shard_map/ppermute | solution.py:50
  64.5 16.9 %collective-permute-start.16 = (bf16[64,8192]{1,0:T(8,128)(2,1)S(1)}, bf16[64,8192]{1,0:T(8,128)(2,1)S(1)}, u32[]{:S(2)}, u32[]{:S(2)}) collective-permute-start(bf16[64,8192]{1,0:T(8,128)(2,1)S(1)} %get-tuple-element.54), channel_id=1, source_target_pairs={{0,48},{1,13},{2,50},{3,15},{4,52},{5,9},{6,54},{7,11},{8,56},{9,5... | collective-permute-start | bytes 3145736 | tf_op jit(solution)/shard_map/ppermute | solution.py:50
  75.1 17.9 %collective-permute-start.17 = (bf16[64,8192]{1,0:T(8,128)(2,1)S(1)}, bf16[64,8192]{1,0:T(8,128)(2,1)S(1)}, u32[]{:S(2)}, u32[]{:S(2)}) collective-permute-start(bf16[64,8192]{1,0:T(8,128)(2,1)S(1)} %shard_map.112), channel_id=1, source_target_pairs={{0,32},{1,9},{2,34},{3,11},{4,36},{5,13},{6,38},{7,15},{8,40},{9,1... | collective-permute-start | bytes 3145736 | tf_op jit(solution)/shard_map/ppermute | solution.py:50
  93.2 7.1 %collective-permute-start.18 = (bf16[16,8192]{1,0:T(8,128)(2,1)S(1)}, bf16[16,8192]{1,0:T(8,128)(2,1)S(1)}, u32[]{:S(2)}, u32[]{:S(2)}) collective-permute-start(bf16[16,8192]{1,0:T(8,128)(2,1)S(1)} %get-tuple-element.56), channel_id=1, source_target_pairs={{0,8},{1,33},{2,10},{3,35},{4,12},{5,37},{6,14},{7,39},{8,0},{9,41... | collective-permute-start | bytes 786440 | tf_op jit(solution)/shard_map/ppermute | solution.py:50
  95.5 7.3 %collective-permute-start.19 = (bf16[16,8192]{1,0:T(8,128)(2,1)S(1)}, bf16[16,8192]{1,0:T(8,128)(2,1)S(1)}, u32[]{:S(2)}, u32[]{:S(2)}) collective-permute-start(bf16[16,8192]{1,0:T(8,128)(2,1)S(1)} %get-tuple-element.57), channel_id=1, source_target_pairs={{0,4},{1,17},{2,6},{3,19},{4,0},{5,21},{6,2},{7,23},{8,12},{9,25},... | collective-permute-start | bytes 786440 | tf_op jit(solution)/shard_map/ppermute | solution.py:50
  95.9 7.2 %collective-permute-start.20 = (bf16[16,8192]{1,0:T(8,128)(2,1)S(1)}, bf16[16,8192]{1,0:T(8,128)(2,1)S(1)}, u32[]{:S(2)}, u32[]{:S(2)}) collective-permute-start(bf16[16,8192]{1,0:T(8,128)(2,1)S(1)} %get-tuple-element.58), channel_id=1, source_target_pairs={{0,12},{1,49},{2,14},{3,51},{4,8},{5,53},{6,10},{7,55},{8,4},{9,57... | collective-permute-start | bytes 786440 | tf_op jit(solution)/shard_map/ppermute | solution.py:50
  103.8 4.7 %collective-permute-start.21 = (bf16[8,4096]{1,0:T(8,128)(2,1)S(1)}, bf16[8,4096]{1,0:T(8,128)(2,1)S(1)}, u32[]{:S(2)}, u32[]{:S(2)}) collective-permute-start(bf16[8,4096]{1,0:T(8,128)(2,1)S(1)} %get-tuple-element.60), channel_id=1, source_target_pairs={{0,64},{1,65},{2,66},{3,67},{4,68},{5,69},{6,70},{7,71},{8,72},{9,... | collective-permute-start | bytes 196616 | tf_op jit(solution)/shard_map/ppermute | solution.py:50
  105.0 3.6 %collective-permute-start.22 = (bf16[8,4096]{1,0:T(8,128)(2,1)S(1)}, bf16[8,4096]{1,0:T(8,128)(2,1)S(1)}, u32[]{:S(2)}, u32[]{:S(2)}) collective-permute-start(bf16[8,4096]{1,0:T(8,128)(2,1)S(1)} %get-tuple-element.61), channel_id=1, source_target_pairs={{0,2},{1,3},{2,0},{3,1},{4,6},{5,7},{6,4},{7,5},{8,10},{9,11},{10,... | collective-permute-start | bytes 196616 | tf_op jit(solution)/shard_map/ppermute | solution.py:50
  106.3 4.8 %collective-permute-start.23 = (bf16[8,4096]{1,0:T(8,128)(2,1)S(1)}, bf16[8,4096]{1,0:T(8,128)(2,1)S(1)}, u32[]{:S(2)}, u32[]{:S(2)}) collective-permute-start(bf16[8,4096]{1,0:T(8,128)(2,1)S(1)} %get-tuple-element.62), channel_id=1, source_target_pairs={{0,66},{1,67},{2,64},{3,65},{4,70},{5,71},{6,68},{7,69},{8,74},{9,... | collective-permute-start | bytes 196616 | tf_op jit(solution)/shard_map/ppermute | solution.py:50
  111.7 4.3 %collective-permute-start.24 = (bf16[8,2048]{1,0:T(8,128)(2,1)S(1)}, bf16[8,2048]{1,0:T(8,128)(2,1)S(1)}, u32[]{:S(2)}, u32[]{:S(2)}) collective-permute-start(bf16[8,2048]{1,0:T(8,128)(2,1)S(1)} %get-tuple-element.64), channel_id=1, source_target_pairs={{0,1},{1,0},{2,3},{3,2},{4,5},{5,4},{6,7},{7,6},{8,9},{9,8},{10,11... | collective-permute-start | bytes 98312 | tf_op jit(solution)/shard_map/ppermute | solution.py:50

commit v15 on v14

--- a/solution.py
+++ b/solution.py
@@ -18,7 +18,7 @@
 STEPS = WIDTH // TILE
 PARTS = TILE // 256
 f32, bf16 = jnp.float32, jnp.bfloat16
-CK = 8
+CK = 1
 SMALL = pl.CostEstimate(flops=1, bytes_accessed=1, transcendentals=0)
 
 
@@ -273,11 +273,9 @@
         packed[16 * k : 16 * k + 16, :] = g[...]
 
 
-def part_kernel(*refs):
-    at, out = 0, refs[-1]
-    for r in refs[:-1]:
-        out[at : at + r.shape[0], :] = r[:, : out.shape[1]]
-        at += r.shape[0]
+def halves_kernel(from3, from1, to1, to3):
+    to1[...] = from3[:32, :WIDTH]
+    to3[...] = from1[32:, :WIDTH]
 
 
 def touch_kernel(gate_w, up_w, down_w, out):
@@ -387,21 +385,19 @@
     frozen = (frozen_gate_weight, frozen_up_weight, frozen_down_weight)
     owned = after(frozen, packed)
     up2, down2 = send(owned[1], CORE), send(owned[2], CORE)
-    (far,) = local(part_kernel, [((64, 3072), bf16)], (far,), price=price_of(11))
+    to1, to3 = local(halves_kernel, [((32, WIDTH), bf16)] * 2, (packed3, packed1))
+    rows2 = (send(to1, SECOND[1]), send(to3, SECOND[3]))
+    (touched,) = local(touch_kernel, [((8, 128), f32)], in_vmem(owned))
+    weights = (owned[0], gate2, owned[1], up2)
+    down_weights = (owned[2], down2)
+
+    acc = project((packed1, packed3, packed), weights, price_of(CK), touched)
     (factor,) = local(
         stack_kernel,
         [((256, 3072 + 256), bf16)],
-        (factor, packed1, far, packed3, seconds),
+        (factor, packed1, after(far, acc), packed3, seconds),
     )
     factor2 = send(factor, CORE)
-    (rows3,) = local(part_kernel, [((64, WIDTH), bf16)], (packed3,))
-    rows2 = send(rows3, SECOND[1])
-    (touched,) = local(touch_kernel, [((8, 128), f32)], in_vmem(owned))
-
-    weights = (owned[0], gate2, owned[1], up2)
-    down_weights = (owned[2], down2)
-
-    acc = project((packed1, packed3, packed), weights, price_of(CK), touched)
     part1, part3, first, second = down(
         first_down_kernel,
         128,
@@ -410,7 +406,7 @@
         place,
     )
     back1, back3 = send(part1, SECOND[1]), send(part3, SECOND[3])
-    acc2 = project((after(rows2, part1),), (*weights, first), SMALL)
+    acc2 = project(after(rows2, part1), (*weights, first), SMALL)
     (part2,) = down(
         last_down_kernel,
         64,

time: 117 us -> 118 us (level)
  local copies, waits for them, and re-layouts: 2.37 us -> 8.48 us
  waiting for transfers between devices: 53.5 us -> 48.4 us
    unnamed x12 -> x18, local copies, waits for them, and re-layouts: 2.29 us -> 8.4 us
    ppermute x25 -> x26, waiting for transfers between devices: 53.5 us -> 48.4 us  [send(): return lax.ppermute(value, AXES, route)]
    ppermute x25 -> x26, starting transfers between devices: 36.1 us -> 36.3 us  [send(): return lax.ppermute(value, AXES, route)]
    pallas_call x13 -> x12, Pallas kernels: 4.52 us -> 4.55 us  [local(): pl.pallas_call(body, in_specs=[SMEM] * len(lead) + [VMEM] * len(operands)...]
  transfers between devices with their start and end apart: 25 -> 26, of which waited for: 15 -> 15; matrix products, arithmetic and copies ran while one was open for 0% -> 0% of each run, Pallas kernels for 18% -> 18%
where the time goes in v15:
time: 118 us
  waiting for transfers between devices  48.4 us (41%)
  starting transfers between devices  36.3 us (31%)
  Pallas kernels  23.1 us (20%)
  local copies, waits for them, and re-layouts  8.48 us (7%)
  other arithmetic  1.42 us (1%)
    ppermute x26, waiting for transfers between devices, send(): return lax.ppermute(value, AXES, route)  48.4 us
    ppermute x26, starting transfers between devices, send(): return lax.ppermute(value, AXES, route)  36.3 us
    pallas_call x3, Pallas kernels, down(): pl.pallas_call(body, in_specs=[SMEM] * len(lead) + [VMEM] * len(operands)...  9.88 us
    pallas_call x2, Pallas kernels, project(): pl.pallas_call(lambda *refs: project_kernel(n, *refs[more:]), in_specs=[V...  8.66 us
    unnamed x18, local copies, waits for them, and re-layouts  8.4 us
    pallas_call x12, Pallas kernels, local(): pl.pallas_call(body, in_specs=[SMEM] * len(lead) + [VMEM] * len(operands)...  4.55 us
  transfers between devices with their start and end apart: 26, of which 15 were waited for; matrix products, arithmetic and copies ran while one was open for 0% of the time, Pallas kernels for 18%

profile of v15, /device:TPU:1, one launch (start us, length us, event | category | flops | bytes accessed | tf_op | source)
XLA Modules:
  0.0 117.8 jit_solution(719935113288613816)
XLA Ops:
  0.0 0.8 select_bitcast_fusion
  0.8 1.5 %collective-permute-start = (bf16[8,2048]{1,0:T(8,128)(2,1)S(1)}, bf16[8,2048]{1,0:T(8,128)(2,1)S(1)}, u32[]{:S(2)}, u32[]{:S(2)}) collective-permute-start(bf16[8,2048]{1,0:T(8,128)(2,1)S(1)} %get-tuple-element.73), channel_id=1, source_target_pairs={{0,1},{1,0},{2,3},{3,2},{4,5},{5,4},{6,7},{7,6},{8,9},{9,8},{10,11... | collective-permute-start | bytes 98312 | tf_op jit(solution)/shard_map/ppermute | solution.py:50
  2.4 1.3 %shard_map.100.factor = bf16[16,1536]{1,0:T(8,128)(2,1)S(1)} custom-call(s32[5]{0:T(128)S(1)} %stack.37.place, bf16[64,256]{1,0:T(8,128)(2,1)} %gate.1, bf16[64,256]{1,0:T(8,128)(2,1)} %up.1, bf16[64,256]{1,0:T(8,128)(2,1)} %down.1), custom_call_target="tpu_custom_call" | custom-call | flops 1 | bytes 1 | tf_op jit(solution)/shard_map/pallas_call | solution.py:217
  4.4 3.9 %collective-permute-start.3 = (bf16[16,3584]{1,0:T(8,128)(2,1)S(1)}, bf16[16,3584]{1,0:T(8,128)(2,1)S(1)}, u32[]{:S(2)}, u32[]{:S(2)}) collective-permute-start(bf16[16,3584]{1,0:T(8,128)(2,1)S(1)} %get-tuple-element.40.message), channel_id=1, source_target_pairs={{0,66},{1,67},{2,64},{3,65},{4,70},{5,71},{6,68},{7,69},{8,74},{9,... | collective-permute-start | bytes 344072 | tf_op jit(solution)/shard_map/ppermute | solution.py:50
  8.3 1.3 %collective-permute-start.2 = (bf16[8,4096]{1,0:T(8,128)(2,1)S(1)}, bf16[8,4096]{1,0:T(8,128)(2,1)S(1)}, u32[]{:S(2)}, u32[]{:S(2)}) collective-permute-start(bf16[8,4096]{1,0:T(8,128)(2,1)S(1)} %get-tuple-element.39.wide), channel_id=1, source_target_pairs={{0,64},{1,65},{2,66},{3,67},{4,68},{5,69},{6,70},{7,71},{8,72},{9,... | collective-permute-start | bytes 196616 | tf_op jit(solution)/shard_map/ppermute | solution.py:50
  9.6 2.1 %collective-permute-done.1.z1 = bf16[8,4096]{1,0:T(8,128)(2,1)S(1)} collective-permute-done((bf16[8,4096]{1,0:T(8,128)(2,1)S(1)}, bf16[8,4096]{1,0:T(8,128)(2,1)S(1)}, u32[]{:S(2)}, u32[]{:S(2)}) %collective-permute-start.1) | collective-permute-done | bytes 65568 | tf_op jit(solution)/shard_map/ppermute | solution.py:50
  11.7 1.2 %collective-permute-done.2.z2 = bf16[8,4096]{1,0:T(8,128)(2,1)S(1)} collective-permute-done((bf16[8,4096]{1,0:T(8,128)(2,1)S(1)}, bf16[8,4096]{1,0:T(8,128)(2,1)S(1)}, u32[]{:S(2)}, u32[]{:S(2)}) %collective-permute-start.2) | collective-permute-done | bytes 65568 | tf_op jit(solution)/shard_map/ppermute | solution.py:50
  13.5 3.0 %collective-permute-start.5 = (bf16[16,11264]{1,0:T(8,128)(2,1)S(1)}, bf16[16,11264]{1,0:T(8,128)(2,1)S(1)}, u32[]{:S(2)}, u32[]{:S(2)}) collective-permute-start(bf16[16,11264]{1,0:T(8,128)(2,1)S(1)} %shard_map.102.own), channel_id=1, source_target_pairs={{0,8},{1,33},{2,10},{3,35},{4,12},{5,37},{6,14},{7,39},{8,0},{9,41... | collective-permute-start | bytes 1081352 | tf_op jit(solution)/shard_map/ppermute | solution.py:50
  17.3 0.8 copy-done.6
  18.0 0.8 copy-done.7
  18.8 0.8 copy-done.8
  19.6 2.1 %collective-permute-done.5.got2 = bf16[16,11264]{1,0:T(8,128)(2,1)S(1)} collective-permute-done((bf16[16,11264]{1,0:T(8,128)(2,1)S(1)}, bf16[16,11264]{1,0:T(8,128)(2,1)S(1)}, u32[]{:S(2)}, u32[]{:S(2)}) %collective-permute-start.5) | collective-permute-done | bytes 360480 | tf_op jit(solution)/shard_map/ppermute | solution.py:50
  21.7 4.2 %collective-permute-done.6.got1 = bf16[16,11264]{1,0:T(8,128)(2,1)S(1)} collective-permute-done((bf16[16,11264]{1,0:T(8,128)(2,1)S(1)}, bf16[16,11264]{1,0:T(8,128)(2,1)S(1)}, u32[]{:S(2)}, u32[]{:S(2)}) %collective-permute-start.6) | collective-permute-done | bytes 360480 | tf_op jit(solution)/shard_map/ppermute | solution.py:50
  26.0 2.5 %collective-permute-start.10 = (bf16[224,8192]{1,0:T(8,128)(2,1)}, bf16[224,8192]{1,0:T(8,128)(2,1)S(1)}, u32[]{:S(2)}, u32[]{:S(2)}) collective-permute-start(bf16[224,8192]{1,0:T(8,128)(2,1)} %refs_4_.1), channel_id=1, source_target_pairs={{0,1},{1,0},{2,3},{3,2},{4,5},{5,4},{6,7},{7,6},{8,9},{9,8},{10,11... | collective-permute-start | bytes 11010056 | tf_op jit(solution)/shard_map/ppermute | solution.py:50
  28.6 1.2 collective-permute-start.8
  29.8 1.7 %collective-permute-start.9 = (bf16[64,11264]{1,0:T(8,128)(2,1)S(1)}, bf16[64,11264]{1,0:T(8,128)(2,1)S(1)}, u32[]{:S(2)}, u32[]{:S(2)}) collective-permute-start(bf16[64,11264]{1,0:T(8,128)(2,1)S(1)} %get-tuple-element.48.refs_3_.own), channel_id=1, source_target_pairs={{0,48},{1,13},{2,50},{3,15},{4,52},{5,9},{6,54},{7,11},{8,56},{9,5... | collective-permute-start | bytes 4325384 | tf_op jit(solution)/shard_map/ppermute | solution.py:50
  31.5 0.6 collective-permute-start.14
  32.2 2.0 %copy-done = bf16[224,8192]{1,0:T(8,128)(2,1)S(1)} copy-done((bf16[224,8192]{1,0:T(8,128)(2,1)S(1)}, bf16[224,8192]{1,0:T(8,128)(2,1)}, u32[]{:S(2)}) %copy-start) | copy-done | bytes 3670040
  34.2 2.0 %copy-done.2 = bf16[224,8192]{1,0:T(8,128)(2,1)S(1)} copy-done((bf16[224,8192]{1,0:T(8,128)(2,1)S(1)}, bf16[224,8192]{1,0:T(8,128)(2,1)}, u32[]{:S(2)}) %copy-start.2) | copy-done | bytes 3670040
  36.3 2.0 %copy-done.4 = bf16[224,8192]{1,0:T(8,128)(2,1)S(1)} copy-done((bf16[224,8192]{1,0:T(8,128)(2,1)S(1)}, bf16[224,8192]{1,0:T(8,128)(2,1)}, u32[]{:S(2)}) %copy-start.4) | copy-done | bytes 3670040
  38.3 8.5 %collective-permute-done.8.refs_1_.from1.packed1.rows1 = bf16[64,11264]{1,0:T(8,128)(2,1)S(1)} collective-permute-done((bf16[64,11264]{1,0:T(8,128)(2,1)S(1)}, bf16[64,11264]{1,0:T(8,128)(2,1)S(1)}, u32[]{:S(2)}, u32[]{:S(2)}) %collective-permute-start.8) | collective-permute-done | bytes 1441824 | tf_op jit(solution)/shard_map/ppermute | solution.py:50
  46.8 6.6 %collective-permute-done.9.refs_2_.from3.packed3.rows3 = bf16[64,11264]{1,0:T(8,128)(2,1)S(1)} collective-permute-done((bf16[64,11264]{1,0:T(8,128)(2,1)S(1)}, bf16[64,11264]{1,0:T(8,128)(2,1)S(1)}, u32[]{:S(2)}, u32[]{:S(2)}) %collective-permute-start.9) | collective-permute-done | bytes 1441824 | tf_op jit(solution)/shard_map/ppermute | solution.py:50
  53.4 4.0 %shard_map.106.acc = f32[896,192]{1,0:T(8,128)S(1)} custom-call(f32[8,128]{1,0:T(8,128)S(1)} %shard_map.105.refs_0_, bf16[64,11264]{1,0:T(8,128)(2,1)S(1)} %collective-permute-done.8.refs_1_.from1.packed1.rows1, bf16[64,11264]{1,0:T(8,128)(2,1)S(1)} %collective-permute-done.9.refs_2_.from3.packed3.rows3, ...), custom_call_target="tpu_custom_call" | custom-call | flops 1150000000 | bytes 3600000 | tf_op jit(solution)/shard_map/pallas_call | solution.py:193
  57.6 1.8 %collective-permute-start.15 = (bf16[256,3328]{1,0:T(8,128)(2,1)S(1)}, bf16[256,3328]{1,0:T(8,128)(2,1)S(1)}, u32[]{:S(2)}, u32[]{:S(2)}) collective-permute-start(bf16[256,3328]{1,0:T(8,128)(2,1)S(1)} %shard_map.108.factor), channel_id=1, source_target_pairs={{0,1},{1,0},{2,3},{3,2},{4,5},{5,4},{6,7},{7,6},{8,9},{9,8},{10,11... | collective-permute-start | bytes 5111816 | tf_op jit(solution)/shard_map/ppermute | solution.py:50
  59.4 1.2 %collective-permute-start.11 = (bf16[32,8192]{1,0:T(8,128)(2,1)S(1)}, bf16[32,8192]{1,0:T(8,128)(2,1)S(1)}, u32[]{:S(2)}, u32[]{:S(2)}) collective-permute-start(bf16[32,8192]{1,0:T(8,128)(2,1)S(1)} %get-tuple-element.52), channel_id=1, source_target_pairs={{0,16},{1,5},{2,18},{3,7},{4,20},{5,1},{6,22},{7,3},{8,24},{9,13},... | collective-permute-start | bytes 1572872 | tf_op jit(solution)/shard_map/ppermute | solution.py:50
  60.7 1.7 %collective-permute-start.12 = (bf16[32,8192]{1,0:T(8,128)(2,1)S(1)}, bf16[32,8192]{1,0:T(8,128)(2,1)S(1)}, u32[]{:S(2)}, u32[]{:S(2)}) collective-permute-start(bf16[32,8192]{1,0:T(8,128)(2,1)S(1)} %get-tuple-element.53), channel_id=1, source_target_pairs={{0,48},{1,13},{2,50},{3,15},{4,52},{5,9},{6,54},{7,11},{8,56},{9,5... | collective-permute-start | bytes 1572872 | tf_op jit(solution)/shard_map/ppermute | solution.py:50
  62.6 4.3 %shard_map.109 = (bf16[64,8192]{1,0:T(8,128)(2,1)S(1)}, bf16[64,8192]{1,0:T(8,128)(2,1)S(1)}, bf16[128,8192]{1,0:T(8,128)(2,1)S(1)}, bf16[64,8192]{1,0:T(8,128)(2,1)S(1)}) custom-call(s32[5]{0:T(128)S(1)} %stack.37.place, bf16[64,11264]{1,0:T(8,128)(2,1)S(1)} %collective-permute-done.8.refs_1_.from1.packed1.rows1, ...), custom_call_target="tpu_custom_call" | custom-call | flops 1 | bytes 1 | tf_op jit(solution)/shard_map/pallas_call | solution.py:204
  66.9 1.2 %collective-permute-start.16 = (bf16[64,8192]{1,0:T(8,128)(2,1)S(1)}, bf16[64,8192]{1,0:T(8,128)(2,1)S(1)}, u32[]{:S(2)}, u32[]{:S(2)}) collective-permute-start(bf16[64,8192]{1,0:T(8,128)(2,1)S(1)} %get-tuple-element.56), channel_id=1, source_target_pairs={{0,16},{1,5},{2,18},{3,7},{4,20},{5,1},{6,22},{7,3},{8,24},{9,13},... | collective-permute-start | bytes 3145736 | tf_op jit(solution)/shard_map/ppermute | solution.py:50
  68.2 1.7 %collective-permute-start.17 = (bf16[64,8192]{1,0:T(8,128)(2,1)S(1)}, bf16[64,8192]{1,0:T(8,128)(2,1)S(1)}, u32[]{:S(2)}, u32[]{:S(2)}) collective-permute-start(bf16[64,8192]{1,0:T(8,128)(2,1)S(1)} %get-tuple-element.62), channel_id=1, source_target_pairs={{0,48},{1,13},{2,50},{3,15},{4,52},{5,9},{6,54},{7,11},{8,56},{9,5... | collective-permute-start | bytes 3145736 | tf_op jit(solution)/shard_map/ppermute | solution.py:50
  69.9 4.6 %shard_map.110.acc = f32[1024,64]{1,0:T(8,128)S(1)} custom-call(bf16[32,8192]{1,0:T(8,128)(2,1)S(1)} %collective-permute-done.11.refs_0_, bf16[32,8192]{1,0:T(8,128)(2,1)S(1)} %collective-permute-done.12.refs_1_, bf16[224,8192]{1,0:T(8,128)(2,1)S(1)} %copy-done.3, bf16[224,8192]{1,0:T(8,128)(2,1)S(1)} %collective-permute-done.4.refs_5_.refs_3_, ...), custom_call_target="tpu_custom_call" | custom-call | flops 1 | bytes 1 | tf_op jit(solution)/shard_map/pallas_call | solution.py:193
  74.5 2.0 %shard_map.111 = bf16[64,8192]{1,0:T(8,128)(2,1)S(1)} custom-call(f32[1024,64]{1,0:T(8,128)S(1)} %shard_map.110.acc, bf16[224,8192]{1,0:T(8,128)(2,1)S(1)} %copy-done.1, bf16[224,8192]{1,0:T(8,128)(2,1)S(1)} %collective-permute-done.13.down_w2, bf16[256,256]{1,0:T(8,128)(2,1)S(1)} %shard_map.104.seconds, ...), custom_call_target="tpu_custom_call" | custom-call | flops 1 | bytes 1 | tf_op jit(solution)/shard_map/pallas_call | solution.py:204
  76.5 1.5 %collective-permute-start.18 = (bf16[64,8192]{1,0:T(8,128)(2,1)S(1)}, bf16[64,8192]{1,0:T(8,128)(2,1)S(1)}, u32[]{:S(2)}, u32[]{:S(2)}) collective-permute-start(bf16[64,8192]{1,0:T(8,128)(2,1)S(1)} %shard_map.111), channel_id=1, source_target_pairs={{0,32},{1,9},{2,34},{3,11},{4,36},{5,13},{6,38},{7,15},{8,40},{9,1... | collective-permute-start | bytes 3145736 | tf_op jit(solution)/shard_map/ppermute | solution.py:50
  78.1 3.6 %shard_map.112.own = f32[64,8192]{1,0:T(8,128)S(1)} custom-call(bf16[64,11264]{1,0:T(8,128)(2,1)S(1)} %get-tuple-element.48.refs_3_.own, f32[896,192]{1,0:T(8,128)S(1)} %shard_map.106.acc, bf16[224,8192]{1,0:T(8,128)(2,1)S(1)} %copy-done.1, bf16[224,8192]{1,0:T(8,128)(2,1)S(1)} %collective-permute-done.13.down_w2, bf16[256,256]{1,0:T(8,128)(2,1)S(1)} %shard_map.104.seconds, ...), custom_call_target="tpu_custom_call" | custom-call | flops 1 | bytes 1 | tf_op jit(solution)/shard_map/pallas_call | solution.py:204
  81.6 12.9 %collective-permute-done.17.b3 = bf16[64,8192]{1,0:T(8,128)(2,1)S(1)} collective-permute-done((bf16[64,8192]{1,0:T(8,128)(2,1)S(1)}, bf16[64,8192]{1,0:T(8,128)(2,1)S(1)}, u32[]{:S(2)}, u32[]{:S(2)}) %collective-permute-start.17) | collective-permute-done | bytes 1048608 | tf_op jit(solution)/shard_map/ppermute | solution.py:50
  95.1 1.2 %collective-permute-start.19 = (bf16[16,8192]{1,0:T(8,128)(2,1)S(1)}, bf16[16,8192]{1,0:T(8,128)(2,1)S(1)}, u32[]{:S(2)}, u32[]{:S(2)}) collective-permute-start(bf16[16,8192]{1,0:T(8,128)(2,1)S(1)} %get-tuple-element.64), channel_id=1, source_target_pairs={{0,8},{1,33},{2,10},{3,35},{4,12},{5,37},{6,14},{7,39},{8,0},{9,41... | collective-permute-start | bytes 786440 | tf_op jit(solution)/shard_map/ppermute | solution.py:50
  96.3 1.3 %collective-permute-start.20 = (bf16[16,8192]{1,0:T(8,128)(2,1)S(1)}, bf16[16,8192]{1,0:T(8,128)(2,1)S(1)}, u32[]{:S(2)}, u32[]{:S(2)}) collective-permute-start(bf16[16,8192]{1,0:T(8,128)(2,1)S(1)} %get-tuple-element.65), channel_id=1, source_target_pairs={{0,4},{1,17},{2,6},{3,19},{4,0},{5,21},{6,2},{7,23},{8,12},{9,25},... | collective-permute-start | bytes 786440 | tf_op jit(solution)/shard_map/ppermute | solution.py:50
  97.6 0.8 collective-permute-start.21
  98.4 3.8 %collective-permute-done.19.b2 = bf16[16,8192]{1,0:T(8,128)(2,1)S(1)} collective-permute-done((bf16[16,8192]{1,0:T(8,128)(2,1)S(1)}, bf16[16,8192]{1,0:T(8,128)(2,1)S(1)}, u32[]{:S(2)}, u32[]{:S(2)}) %collective-permute-start.19) | collective-permute-done | bytes 262176 | tf_op jit(solution)/shard_map/ppermute | solution.py:50
  102.2 2.3 %collective-permute-done.20.b1 = bf16[16,8192]{1,0:T(8,128)(2,1)S(1)} collective-permute-done((bf16[16,8192]{1,0:T(8,128)(2,1)S(1)}, bf16[16,8192]{1,0:T(8,128)(2,1)S(1)}, u32[]{:S(2)}, u32[]{:S(2)}) %collective-permute-start.20) | collective-permute-done | bytes 262176 | tf_op jit(solution)/shard_map/ppermute | solution.py:50
  105.0 0.7 shard_map.115
  105.7 1.3 %collective-permute-start.22 = (bf16[8,4096]{1,0:T(8,128)(2,1)S(1)}, bf16[8,4096]{1,0:T(8,128)(2,1)S(1)}, u32[]{:S(2)}, u32[]{:S(2)}) collective-permute-start(bf16[8,4096]{1,0:T(8,128)(2,1)S(1)} %get-tuple-element.68), channel_id=1, source_target_pairs={{0,64},{1,65},{2,66},{3,67},{4,68},{5,69},{6,70},{7,71},{8,72},{9,... | collective-permute-start | bytes 196616 | tf_op jit(solution)/shard_map/ppermute | solution.py:50
  106.9 1.2 %collective-permute-start.23 = (bf16[8,4096]{1,0:T(8,128)(2,1)S(1)}, bf16[8,4096]{1,0:T(8,128)(2,1)S(1)}, u32[]{:S(2)}, u32[]{:S(2)}) collective-permute-start(bf16[8,4096]{1,0:T(8,128)(2,1)S(1)} %get-tuple-element.69), channel_id=1, source_target_pairs={{0,2},{1,3},{2,0},{3,1},{4,6},{5,7},{6,4},{7,5},{8,10},{9,11},{10,... | collective-permute-start | bytes 196616 | tf_op jit(solution)/shard_map/ppermute | solution.py:50
  108.2 1.7 %collective-permute-start.24 = (bf16[8,4096]{1,0:T(8,128)(2,1)S(1)}, bf16[8,4096]{1,0:T(8,128)(2,1)S(1)}, u32[]{:S(2)}, u32[]{:S(2)}) collective-permute-start(bf16[8,4096]{1,0:T(8,128)(2,1)S(1)} %get-tuple-element.70), channel_id=1, source_target_pairs={{0,66},{1,67},{2,64},{3,65},{4,70},{5,71},{6,68},{7,69},{8,74},{9,... | collective-permute-start | bytes 196616 | tf_op jit(solution)/shard_map/ppermute | solution.py:50
  110.5 2.4 %collective-permute-done.24.b3 = bf16[8,4096]{1,0:T(8,128)(2,1)S(1)} collective-permute-done((bf16[8,4096]{1,0:T(8,128)(2,1)S(1)}, bf16[8,4096]{1,0:T(8,128)(2,1)S(1)}, u32[]{:S(2)}, u32[]{:S(2)}) %collective-permute-start.24) | collective-permute-done | bytes 65568 | tf_op jit(solution)/shard_map/ppermute | solution.py:50
  113.0 0.6 shard_map.116
  113.5 2.8 %collective-permute-start.25 = (bf16[8,2048]{1,0:T(8,128)(2,1)S(1)}, bf16[8,2048]{1,0:T(8,128)(2,1)S(1)}, u32[]{:S(2)}, u32[]{:S(2)}) collective-permute-start(bf16[8,2048]{1,0:T(8,128)(2,1)S(1)} %get-tuple-element.72), channel_id=1, source_target_pairs={{0,1},{1,0},{2,3},{3,2},{4,5},{5,4},{6,7},{7,6},{8,9},{9,8},{10,11... | collective-permute-start | bytes 98312 | tf_op jit(solution)/shard_map/ppermute | solution.py:50
  116.3 0.9 collective-permute-done.25
  117.2 0.6 maximum_select_fusion
  (42 shorter events, 4.4 us)
Async XLA Ops:
  0.8 2.9 %collective-permute-start = (bf16[8,2048]{1,0:T(8,128)(2,1)S(1)}, bf16[8,2048]{1,0:T(8,128)(2,1)S(1)}, u32[]{:S(2)}, u32[]{:S(2)}) collective-permute-start(bf16[8,2048]{1,0:T(8,128)(2,1)S(1)} %get-tuple-element.73), channel_id=1, source_target_pairs={{0,1},{1,0},{2,3},{3,2},{4,5},{5,4},{6,7},{7,6},{8,9},{9,8},{10,11... | collective-permute-start | bytes 98312 | tf_op jit(solution)/shard_map/ppermute | solution.py:50
  4.3 9.2 %collective-permute-start.4 = (bf16[224,8192]{1,0:T(8,128)(2,1)}, bf16[224,8192]{1,0:T(8,128)(2,1)S(1)}, u32[]{:S(2)}, u32[]{:S(2)}) collective-permute-start(bf16[224,8192]{1,0:T(8,128)(2,1)} %refs_2_), channel_id=1, source_target_pairs={{0,1},{1,0},{2,3},{3,2},{4,5},{5,4},{6,7},{7,6},{8,9},{9,8},{10,11... | collective-permute-start | bytes 11010056 | tf_op jit(solution)/shard_map/ppermute | solution.py:50
  4.4 8.5 %collective-permute-start.3 = (bf16[16,3584]{1,0:T(8,128)(2,1)S(1)}, bf16[16,3584]{1,0:T(8,128)(2,1)S(1)}, u32[]{:S(2)}, u32[]{:S(2)}) collective-permute-start(bf16[16,3584]{1,0:T(8,128)(2,1)S(1)} %get-tuple-element.40.message), channel_id=1, source_target_pairs={{0,66},{1,67},{2,64},{3,65},{4,70},{5,71},{6,68},{7,69},{8,74},{9,... | collective-permute-start | bytes 344072 | tf_op jit(solution)/shard_map/ppermute | solution.py:50
  8.3 3.4 %collective-permute-start.1 = (bf16[8,4096]{1,0:T(8,128)(2,1)S(1)}, bf16[8,4096]{1,0:T(8,128)(2,1)S(1)}, u32[]{:S(2)}, u32[]{:S(2)}) collective-permute-start(bf16[8,4096]{1,0:T(8,128)(2,1)S(1)} %get-tuple-element.39.wide), channel_id=1, source_target_pairs={{0,2},{1,3},{2,0},{3,1},{4,6},{5,7},{6,4},{7,5},{8,10},{9,11},{10,... | collective-permute-start | bytes 196616 | tf_op jit(solution)/shard_map/ppermute | solution.py:50
  8.3 4.6 %collective-permute-start.2 = (bf16[8,4096]{1,0:T(8,128)(2,1)S(1)}, bf16[8,4096]{1,0:T(8,128)(2,1)S(1)}, u32[]{:S(2)}, u32[]{:S(2)}) collective-permute-start(bf16[8,4096]{1,0:T(8,128)(2,1)S(1)} %get-tuple-element.39.wide), channel_id=1, source_target_pairs={{0,64},{1,65},{2,66},{3,67},{4,68},{5,69},{6,70},{7,71},{8,72},{9,... | collective-permute-start | bytes 196616 | tf_op jit(solution)/shard_map/ppermute | solution.py:50
  13.5 8.2 %collective-permute-start.5 = (bf16[16,11264]{1,0:T(8,128)(2,1)S(1)}, bf16[16,11264]{1,0:T(8,128)(2,1)S(1)}, u32[]{:S(2)}, u32[]{:S(2)}) collective-permute-start(bf16[16,11264]{1,0:T(8,128)(2,1)S(1)} %shard_map.102.own), channel_id=1, source_target_pairs={{0,8},{1,33},{2,10},{3,35},{4,12},{5,37},{6,14},{7,39},{8,0},{9,41... | collective-permute-start | bytes 1081352 | tf_op jit(solution)/shard_map/ppermute | solution.py:50
  16.5 9.4 %collective-permute-start.6 = (bf16[16,11264]{1,0:T(8,128)(2,1)S(1)}, bf16[16,11264]{1,0:T(8,128)(2,1)S(1)}, u32[]{:S(2)}, u32[]{:S(2)}) collective-permute-start(bf16[16,11264]{1,0:T(8,128)(2,1)S(1)} %shard_map.102.own), channel_id=1, source_target_pairs={{0,4},{1,17},{2,6},{3,19},{4,0},{5,21},{6,2},{7,23},{8,12},{9,25},... | collective-permute-start | bytes 1081352 | tf_op jit(solution)/shard_map/ppermute | solution.py:50
  16.9 9.0 %collective-permute-start.7 = (bf16[16,11264]{1,0:T(8,128)(2,1)S(1)}, bf16[16,11264]{1,0:T(8,128)(2,1)S(1)}, u32[]{:S(2)}, u32[]{:S(2)}) collective-permute-start(bf16[16,11264]{1,0:T(8,128)(2,1)S(1)} %shard_map.102.own), channel_id=1, source_target_pairs={{0,12},{1,49},{2,14},{3,51},{4,8},{5,53},{6,10},{7,55},{8,4},{9,57... | collective-permute-start | bytes 1081352 | tf_op jit(solution)/shard_map/ppermute | solution.py:50
  17.3 0.8 copy-start.6
  18.0 0.8 copy-start.7
  18.8 0.8 copy-start.8
  26.0 27.4 %collective-permute-start.10 = (bf16[224,8192]{1,0:T(8,128)(2,1)}, bf16[224,8192]{1,0:T(8,128)(2,1)S(1)}, u32[]{:S(2)}, u32[]{:S(2)}) collective-permute-start(bf16[224,8192]{1,0:T(8,128)(2,1)} %refs_4_.1), channel_id=1, source_target_pairs={{0,1},{1,0},{2,3},{3,2},{4,5},{5,4},{6,7},{7,6},{8,9},{9,8},{10,11... | collective-permute-start | bytes 11010056 | tf_op jit(solution)/shard_map/ppermute | solution.py:50
  28.6 33.9 %collective-permute-start.13 = (bf16[224,8192]{1,0:T(8,128)(2,1)}, bf16[224,8192]{1,0:T(8,128)(2,1)S(1)}, u32[]{:S(2)}, u32[]{:S(2)}) collective-permute-start(bf16[224,8192]{1,0:T(8,128)(2,1)} %down_w.3), channel_id=1, source_target_pairs={{0,1},{1,0},{2,3},{3,2},{4,5},{5,4},{6,7},{7,6},{8,9},{9,8},{10,11... | collective-permute-start | bytes 11010056 | tf_op jit(solution)/shard_map/ppermute | solution.py:50
  28.6 18.2 %collective-permute-start.8 = (bf16[64,11264]{1,0:T(8,128)(2,1)S(1)}, bf16[64,11264]{1,0:T(8,128)(2,1)S(1)}, u32[]{:S(2)}, u32[]{:S(2)}) collective-permute-start(bf16[64,11264]{1,0:T(8,128)(2,1)S(1)} %get-tuple-element.48.refs_3_.own), channel_id=1, source_target_pairs={{0,16},{1,5},{2,18},{3,7},{4,20},{5,1},{6,22},{7,3},{8,24},{9,13},... | collective-permute-start | bytes 4325384 | tf_op jit(solution)/shard_map/ppermute | solution.py:50
  29.8 23.6 %collective-permute-start.9 = (bf16[64,11264]{1,0:T(8,128)(2,1)S(1)}, bf16[64,11264]{1,0:T(8,128)(2,1)S(1)}, u32[]{:S(2)}, u32[]{:S(2)}) collective-permute-start(bf16[64,11264]{1,0:T(8,128)(2,1)S(1)} %get-tuple-element.48.refs_3_.own), channel_id=1, source_target_pairs={{0,48},{1,13},{2,50},{3,15},{4,52},{5,9},{6,54},{7,11},{8,56},{9,5... | collective-permute-start | bytes 4325384 | tf_op jit(solution)/shard_map/ppermute | solution.py:50
  31.5 25.9 %collective-permute-start.14 = (bf16[64,3072]{1,0:T(8,128)(2,1)S(1)}, bf16[64,3072]{1,0:T(8,128)(2,1)S(1)}, u32[]{:S(2)}, u32[]{:S(2)}) collective-permute-start(bf16[64,3072]{1,0:T(8,128)(2,1)S(1)} %get-tuple-element.54.f0), channel_id=1, source_target_pairs={{0,32},{1,9},{2,34},{3,11},{4,36},{5,13},{6,38},{7,15},{8,40},{9,1... | collective-permute-start | bytes 1179656 | tf_op jit(solution)/shard_map/ppermute | solution.py:50
  32.2 2.0 %copy-start = (bf16[224,8192]{1,0:T(8,128)(2,1)S(1)}, bf16[224,8192]{1,0:T(8,128)(2,1)}, u32[]{:S(2)}) copy-start(bf16[224,8192]{1,0:T(8,128)(2,1)} %down_w.3) | copy-start | bytes 11010052
  34.2 2.0 %copy-start.2 = (bf16[224,8192]{1,0:T(8,128)(2,1)S(1)}, bf16[224,8192]{1,0:T(8,128)(2,1)}, u32[]{:S(2)}) copy-start(bf16[224,8192]{1,0:T(8,128)(2,1)} %refs_2_) | copy-start | bytes 11010052
  36.3 2.0 %copy-start.4 = (bf16[224,8192]{1,0:T(8,128)(2,1)S(1)}, bf16[224,8192]{1,0:T(8,128)(2,1)}, u32[]{:S(2)}) copy-start(bf16[224,8192]{1,0:T(8,128)(2,1)} %refs_4_.1) | copy-start | bytes 11010052
  38.3 15.1 %copy-start.3 = (bf16[224,8192]{1,0:T(8,128)(2,1)S(1)}, bf16[224,8192]{1,0:T(8,128)(2,1)}, u32[]{:S(2)}) copy-start(bf16[224,8192]{1,0:T(8,128)(2,1)} %refs_2_) | copy-start | bytes 11010052
  38.3 15.1 %copy-start.5 = (bf16[224,8192]{1,0:T(8,128)(2,1)S(1)}, bf16[224,8192]{1,0:T(8,128)(2,1)}, u32[]{:S(2)}) copy-start(bf16[224,8192]{1,0:T(8,128)(2,1)} %refs_4_.1) | copy-start | bytes 11010052
  57.5 5.1 %copy-start.1 = (bf16[224,8192]{1,0:T(8,128)(2,1)S(1)}, bf16[224,8192]{1,0:T(8,128)(2,1)}, u32[]{:S(2)}) copy-start(bf16[224,8192]{1,0:T(8,128)(2,1)} %down_w.3) | copy-start | bytes 11010052
  57.6 5.0 %collective-permute-start.15 = (bf16[256,3328]{1,0:T(8,128)(2,1)S(1)}, bf16[256,3328]{1,0:T(8,128)(2,1)S(1)}, u32[]{:S(2)}, u32[]{:S(2)}) collective-permute-start(bf16[256,3328]{1,0:T(8,128)(2,1)S(1)} %shard_map.108.factor), channel_id=1, source_target_pairs={{0,1},{1,0},{2,3},{3,2},{4,5},{5,4},{6,7},{7,6},{8,9},{9,8},{10,11... | collective-permute-start | bytes 5111816 | tf_op jit(solution)/shard_map/ppermute | solution.py:50
  59.4 10.5 %collective-permute-start.11 = (bf16[32,8192]{1,0:T(8,128)(2,1)S(1)}, bf16[32,8192]{1,0:T(8,128)(2,1)S(1)}, u32[]{:S(2)}, u32[]{:S(2)}) collective-permute-start(bf16[32,8192]{1,0:T(8,128)(2,1)S(1)} %get-tuple-element.52), channel_id=1, source_target_pairs={{0,16},{1,5},{2,18},{3,7},{4,20},{5,1},{6,22},{7,3},{8,24},{9,13},... | collective-permute-start | bytes 1572872 | tf_op jit(solution)/shard_map/ppermute | solution.py:50
  60.7 9.2 %collective-permute-start.12 = (bf16[32,8192]{1,0:T(8,128)(2,1)S(1)}, bf16[32,8192]{1,0:T(8,128)(2,1)S(1)}, u32[]{:S(2)}, u32[]{:S(2)}) collective-permute-start(bf16[32,8192]{1,0:T(8,128)(2,1)S(1)} %get-tuple-element.53), channel_id=1, source_target_pairs={{0,48},{1,13},{2,50},{3,15},{4,52},{5,9},{6,54},{7,11},{8,56},{9,5... | collective-permute-start | bytes 1572872 | tf_op jit(solution)/shard_map/ppermute | solution.py:50
  66.9 14.7 %collective-permute-start.16 = (bf16[64,8192]{1,0:T(8,128)(2,1)S(1)}, bf16[64,8192]{1,0:T(8,128)(2,1)S(1)}, u32[]{:S(2)}, u32[]{:S(2)}) collective-permute-start(bf16[64,8192]{1,0:T(8,128)(2,1)S(1)} %get-tuple-element.56), channel_id=1, source_target_pairs={{0,16},{1,5},{2,18},{3,7},{4,20},{5,1},{6,22},{7,3},{8,24},{9,13},... | collective-permute-start | bytes 3145736 | tf_op jit(solution)/shard_map/ppermute | solution.py:50
  68.2 26.4 %collective-permute-start.17 = (bf16[64,8192]{1,0:T(8,128)(2,1)S(1)}, bf16[64,8192]{1,0:T(8,128)(2,1)S(1)}, u32[]{:S(2)}, u32[]{:S(2)}) collective-permute-start(bf16[64,8192]{1,0:T(8,128)(2,1)S(1)} %get-tuple-element.62), channel_id=1, source_target_pairs={{0,48},{1,13},{2,50},{3,15},{4,52},{5,9},{6,54},{7,11},{8,56},{9,5... | collective-permute-start | bytes 3145736 | tf_op jit(solution)/shard_map/ppermute | solution.py:50
  76.5 18.3 %collective-permute-start.18 = (bf16[64,8192]{1,0:T(8,128)(2,1)S(1)}, bf16[64,8192]{1,0:T(8,128)(2,1)S(1)}, u32[]{:S(2)}, u32[]{:S(2)}) collective-permute-start(bf16[64,8192]{1,0:T(8,128)(2,1)S(1)} %shard_map.111), channel_id=1, source_target_pairs={{0,32},{1,9},{2,34},{3,11},{4,36},{5,13},{6,38},{7,15},{8,40},{9,1... | collective-permute-start | bytes 3145736 | tf_op jit(solution)/shard_map/ppermute | solution.py:50
  95.1 7.1 %collective-permute-start.19 = (bf16[16,8192]{1,0:T(8,128)(2,1)S(1)}, bf16[16,8192]{1,0:T(8,128)(2,1)S(1)}, u32[]{:S(2)}, u32[]{:S(2)}) collective-permute-start(bf16[16,8192]{1,0:T(8,128)(2,1)S(1)} %get-tuple-element.64), channel_id=1, source_target_pairs={{0,8},{1,33},{2,10},{3,35},{4,12},{5,37},{6,14},{7,39},{8,0},{9,41... | collective-permute-start | bytes 786440 | tf_op jit(solution)/shard_map/ppermute | solution.py:50
  96.3 8.2 %collective-permute-start.20 = (bf16[16,8192]{1,0:T(8,128)(2,1)S(1)}, bf16[16,8192]{1,0:T(8,128)(2,1)S(1)}, u32[]{:S(2)}, u32[]{:S(2)}) collective-permute-start(bf16[16,8192]{1,0:T(8,128)(2,1)S(1)} %get-tuple-element.65), channel_id=1, source_target_pairs={{0,4},{1,17},{2,6},{3,19},{4,0},{5,21},{6,2},{7,23},{8,12},{9,25},... | collective-permute-start | bytes 786440 | tf_op jit(solution)/shard_map/ppermute | solution.py:50
  97.6 7.4 %collective-permute-start.21 = (bf16[16,8192]{1,0:T(8,128)(2,1)S(1)}, bf16[16,8192]{1,0:T(8,128)(2,1)S(1)}, u32[]{:S(2)}, u32[]{:S(2)}) collective-permute-start(bf16[16,8192]{1,0:T(8,128)(2,1)S(1)} %get-tuple-element.66), channel_id=1, source_target_pairs={{0,12},{1,49},{2,14},{3,51},{4,8},{5,53},{6,10},{7,55},{8,4},{9,57... | collective-permute-start | bytes 786440 | tf_op jit(solution)/shard_map/ppermute | solution.py:50
  105.7 4.7 %collective-permute-start.22 = (bf16[8,4096]{1,0:T(8,128)(2,1)S(1)}, bf16[8,4096]{1,0:T(8,128)(2,1)S(1)}, u32[]{:S(2)}, u32[]{:S(2)}) collective-permute-start(bf16[8,4096]{1,0:T(8,128)(2,1)S(1)} %get-tuple-element.68), channel_id=1, source_target_pairs={{0,64},{1,65},{2,66},{3,67},{4,68},{5,69},{6,70},{7,71},{8,72},{9,... | collective-permute-start | bytes 196616 | tf_op jit(solution)/shard_map/ppermute | solution.py:50
  106.9 3.6 %collective-permute-start.23 = (bf16[8,4096]{1,0:T(8,128)(2,1)S(1)}, bf16[8,4096]{1,0:T(8,128)(2,1)S(1)}, u32[]{:S(2)}, u32[]{:S(2)}) collective-permute-start(bf16[8,4096]{1,0:T(8,128)(2,1)S(1)} %get-tuple-element.69), channel_id=1, source_target_pairs={{0,2},{1,3},{2,0},{3,1},{4,6},{5,7},{6,4},{7,5},{8,10},{9,11},{10,... | collective-permute-start | bytes 196616 | tf_op jit(solution)/shard_map/ppermute | solution.py:50
  108.2 4.8 %collective-permute-start.24 = (bf16[8,4096]{1,0:T(8,128)(2,1)S(1)}, bf16[8,4096]{1,0:T(8,128)(2,1)S(1)}, u32[]{:S(2)}, u32[]{:S(2)}) collective-permute-start(bf16[8,4096]{1,0:T(8,128)(2,1)S(1)} %get-tuple-element.70), channel_id=1, source_target_pairs={{0,66},{1,67},{2,64},{3,65},{4,70},{5,71},{6,68},{7,69},{8,74},{9,... | collective-permute-start | bytes 196616 | tf_op jit(solution)/shard_map/ppermute | solution.py:50
  113.5 3.6 %collective-permute-start.25 = (bf16[8,2048]{1,0:T(8,128)(2,1)S(1)}, bf16[8,2048]{1,0:T(8,128)(2,1)S(1)}, u32[]{:S(2)}, u32[]{:S(2)}) collective-permute-start(bf16[8,2048]{1,0:T(8,128)(2,1)S(1)} %get-tuple-element.72), channel_id=1, source_target_pairs={{0,1},{1,0},{2,3},{3,2},{4,5},{5,4},{6,7},{7,6},{8,9},{9,8},{10,11... | collective-permute-start | bytes 98312 | tf_op jit(solution)/shard_map/ppermute | solution.py:50

commit v16 on v14

--- a/solution.py
+++ b/solution.py
@@ -133,8 +133,8 @@
 
 
 def first_down_kernel(
-    place, rows1, rows3, acc, down_w, down_w2, seconds, theirs, factor,
-    out1, out3, first, second, hidden,
+    place, rows3, rows1, acc, down_w, down_w2, seconds, theirs, factor,
+    out3, out1, first, second, hidden,
 ):
     homes = shard_homes(place)
 
@@ -145,15 +145,15 @@
                     piece = src[rows_at[learner % 16], cols[base + k][learner // 16]]
                     to[to_at[k], learner * 256 : learner * 256 + 256] = piece
 
-    low = low_rows((rows1, rows3), first, lambda i: gather(i, first, 4, 0))
+    low = low_rows((rows3, rows1), first, lambda i: gather(i, first, 4, 0))
     finish(acc[:, :128], low, seconds, theirs, hidden)
     for i in range(STEPS):
         tile = slice(i * TILE, (i + 1) * TILE)
         gather(i, second, 2, 4)
         w = jnp.concatenate([r[:, tile] for r in (down_w, down_w2, second)], axis=0)
         result = nn(hidden[...], w)
-        out1[:, tile] = result[:64].astype(bf16)
-        out3[:, tile] = result[64:].astype(bf16)
+        out3[:, tile] = result[:64].astype(bf16)
+        out1[:, tile] = result[64:].astype(bf16)
 
 
 def own_down_kernel(
@@ -290,7 +290,7 @@
         out[64 * k : 64 * k + 64, :UNITS] = r[...]
 
 
-def stack_kernel(f0, packed1, f2, packed3, seconds, out):
+def stack_kernel(f0, packed3, packed1, f2, seconds, out):
     at = 0
     for r in (f0, packed1, f2, packed3):
         out[at : at + r.shape[0], :3072] = r[:, -3072:]
@@ -391,7 +391,7 @@
     (factor,) = local(
         stack_kernel,
         [((256, 3072 + 256), bf16)],
-        (factor, packed1, far, packed3, seconds),
+        (factor, packed3, packed1, far, seconds),
     )
     factor2 = send(factor, CORE)
     (rows3,) = local(part_kernel, [((64, WIDTH), bf16)], (packed3,))
@@ -401,12 +401,12 @@
     weights = (owned[0], gate2, owned[1], up2)
     down_weights = (owned[2], down2)
 
-    acc = project((packed1, packed3, packed), weights, price_of(CK), touched)
-    part1, part3, first, second = down(
+    acc = project((packed3, packed1, packed), weights, price_of(CK), touched)
+    part3, part1, first, second = down(
         first_down_kernel,
         128,
         [((64, WIDTH), bf16)] * 2 + [((128, WIDTH), bf16), ((64, WIDTH), bf16)],
-        (packed1, packed3, acc, *down_weights, seconds, factor2, factor),
+        (packed3, packed1, acc, *down_weights, seconds, factor2, factor),
         place,
     )
     back1, back3 = send(part1, SECOND[1]), send(part3, SECOND[3])

time: 117 us -> 117 us (level)
  no operation moved by 1% of the time
where the time goes in v16:
time: 117 us
  waiting for transfers between devices  53.5 us (46%)
  starting transfers between devices  36.1 us (31%)
  Pallas kernels  23.1 us (20%)
  local copies, waits for them, and re-layouts  2.37 us (2%)
  other arithmetic  1.42 us (1%)
    ppermute x25, waiting for transfers between devices, send(): return lax.ppermute(value, AXES, route)  53.5 us
    ppermute x25, starting transfers between devices, send(): return lax.ppermute(value, AXES, route)  36.1 us
    pallas_call x3, Pallas kernels, down(): pl.pallas_call(body, in_specs=[SMEM] * len(lead) + [VMEM] * len(operands)...  9.88 us
    pallas_call x2, Pallas kernels, project(): pl.pallas_call(lambda *refs: project_kernel(n, *refs[more:]), in_specs=[V...  8.72 us
    pallas_call x13, Pallas kernels, local(): pl.pallas_call(body, in_specs=[SMEM] * len(lead) + [VMEM] * len(operands)...  4.52 us
  transfers between devices with their start and end apart: 25, of which 15 were waited for; matrix products, arithmetic and copies ran while one was open for 0% of the time, Pallas kernels for 18%

profile of v16, /device:TPU:1, one launch (start us, length us, event | category | flops | bytes accessed | tf_op | source)
XLA Modules:
  0.0 116.6 jit_solution(1790216707773675822)
XLA Ops:
  0.0 0.8 select_bitcast_fusion
  0.8 1.5 %collective-permute-start = (bf16[8,2048]{1,0:T(8,128)(2,1)S(1)}, bf16[8,2048]{1,0:T(8,128)(2,1)S(1)}, u32[]{:S(2)}, u32[]{:S(2)}) collective-permute-start(bf16[8,2048]{1,0:T(8,128)(2,1)S(1)} %get-tuple-element.65), channel_id=1, source_target_pairs={{0,1},{1,0},{2,3},{3,2},{4,5},{5,4},{6,7},{7,6},{8,9},{9,8},{10,11... | collective-permute-start | bytes 98312 | tf_op jit(solution)/shard_map/ppermute | solution.py:50
  2.4 1.3 %shard_map.100.factor = bf16[16,1536]{1,0:T(8,128)(2,1)S(1)} custom-call(s32[5]{0:T(128)S(1)} %stack.37.place, bf16[64,256]{1,0:T(8,128)(2,1)} %gate.1, bf16[64,256]{1,0:T(8,128)(2,1)} %up.1, bf16[64,256]{1,0:T(8,128)(2,1)} %down.1), custom_call_target="tpu_custom_call" | custom-call | flops 1 | bytes 1 | tf_op jit(solution)/shard_map/pallas_call | solution.py:217
  3.7 0.6 shard_map.101
  4.4 3.9 %collective-permute-start.3 = (bf16[16,3584]{1,0:T(8,128)(2,1)S(1)}, bf16[16,3584]{1,0:T(8,128)(2,1)S(1)}, u32[]{:S(2)}, u32[]{:S(2)}) collective-permute-start(bf16[16,3584]{1,0:T(8,128)(2,1)S(1)} %get-tuple-element.36.message), channel_id=1, source_target_pairs={{0,66},{1,67},{2,64},{3,65},{4,70},{5,71},{6,68},{7,69},{8,74},{9,... | collective-permute-start | bytes 344072 | tf_op jit(solution)/shard_map/ppermute | solution.py:50
  8.3 1.3 %collective-permute-start.2 = (bf16[8,4096]{1,0:T(8,128)(2,1)S(1)}, bf16[8,4096]{1,0:T(8,128)(2,1)S(1)}, u32[]{:S(2)}, u32[]{:S(2)}) collective-permute-start(bf16[8,4096]{1,0:T(8,128)(2,1)S(1)} %get-tuple-element.35.wide), channel_id=1, source_target_pairs={{0,64},{1,65},{2,66},{3,67},{4,68},{5,69},{6,70},{7,71},{8,72},{9,... | collective-permute-start | bytes 196616 | tf_op jit(solution)/shard_map/ppermute | solution.py:50
  9.6 2.1 %collective-permute-done.1.z1 = bf16[8,4096]{1,0:T(8,128)(2,1)S(1)} collective-permute-done((bf16[8,4096]{1,0:T(8,128)(2,1)S(1)}, bf16[8,4096]{1,0:T(8,128)(2,1)S(1)}, u32[]{:S(2)}, u32[]{:S(2)}) %collective-permute-start.1) | collective-permute-done | bytes 65568 | tf_op jit(solution)/shard_map/ppermute | solution.py:50
  11.7 1.2 %collective-permute-done.2.z2 = bf16[8,4096]{1,0:T(8,128)(2,1)S(1)} collective-permute-done((bf16[8,4096]{1,0:T(8,128)(2,1)S(1)}, bf16[8,4096]{1,0:T(8,128)(2,1)S(1)}, u32[]{:S(2)}, u32[]{:S(2)}) %collective-permute-start.2) | collective-permute-done | bytes 65568 | tf_op jit(solution)/shard_map/ppermute | solution.py:50
  12.9 0.6 shard_map.102.own
  13.5 3.0 %collective-permute-start.5 = (bf16[16,11264]{1,0:T(8,128)(2,1)S(1)}, bf16[16,11264]{1,0:T(8,128)(2,1)S(1)}, u32[]{:S(2)}, u32[]{:S(2)}) collective-permute-start(bf16[16,11264]{1,0:T(8,128)(2,1)S(1)} %shard_map.102.own), channel_id=1, source_target_pairs={{0,8},{1,33},{2,10},{3,35},{4,12},{5,37},{6,14},{7,39},{8,0},{9,41... | collective-permute-start | bytes 1081352 | tf_op jit(solution)/shard_map/ppermute | solution.py:50
  16.5 0.4 collective-permute-start.6
  17.3 0.8 copy-done.3
  18.0 0.8 copy-done.4
  18.8 0.8 copy-done.5
  19.6 2.1 %collective-permute-done.5.got2 = bf16[16,11264]{1,0:T(8,128)(2,1)S(1)} collective-permute-done((bf16[16,11264]{1,0:T(8,128)(2,1)S(1)}, bf16[16,11264]{1,0:T(8,128)(2,1)S(1)}, u32[]{:S(2)}, u32[]{:S(2)}) %collective-permute-start.5) | collective-permute-done | bytes 360480 | tf_op jit(solution)/shard_map/ppermute | solution.py:50
  21.7 4.2 %collective-permute-done.6.got1 = bf16[16,11264]{1,0:T(8,128)(2,1)S(1)} collective-permute-done((bf16[16,11264]{1,0:T(8,128)(2,1)S(1)}, bf16[16,11264]{1,0:T(8,128)(2,1)S(1)}, u32[]{:S(2)}, u32[]{:S(2)}) %collective-permute-start.6) | collective-permute-done | bytes 360480 | tf_op jit(solution)/shard_map/ppermute | solution.py:50
  26.0 2.5 %collective-permute-start.10 = (bf16[224,8192]{1,0:T(8,128)(2,1)}, bf16[224,8192]{1,0:T(8,128)(2,1)S(1)}, u32[]{:S(2)}, u32[]{:S(2)}) collective-permute-start(bf16[224,8192]{1,0:T(8,128)(2,1)} %refs_3_), channel_id=1, source_target_pairs={{0,1},{1,0},{2,3},{3,2},{4,5},{5,4},{6,7},{7,6},{8,9},{9,8},{10,11... | collective-permute-start | bytes 11010056 | tf_op jit(solution)/shard_map/ppermute | solution.py:50
  28.6 2.6 %collective-permute-start.13 = (bf16[64,3072]{1,0:T(8,128)(2,1)S(1)}, bf16[64,3072]{1,0:T(8,128)(2,1)S(1)}, u32[]{:S(2)}, u32[]{:S(2)}) collective-permute-start(bf16[64,3072]{1,0:T(8,128)(2,1)S(1)} %get-tuple-element.48.f0), channel_id=1, source_target_pairs={{0,32},{1,9},{2,34},{3,11},{4,36},{5,13},{6,38},{7,15},{8,40},{9,1... | collective-permute-start | bytes 1179656 | tf_op jit(solution)/shard_map/ppermute | solution.py:50
  31.3 0.9 collective-permute-start.8
  32.2 4.9 %collective-permute-done.13.refs_0_ = bf16[64,3072]{1,0:T(8,128)(2,1)S(1)} collective-permute-done((bf16[64,3072]{1,0:T(8,128)(2,1)S(1)}, bf16[64,3072]{1,0:T(8,128)(2,1)S(1)}, u32[]{:S(2)}, u32[]{:S(2)}) %collective-permute-start.13) | collective-permute-done | bytes 393248 | tf_op jit(solution)/shard_map/ppermute | solution.py:50
  37.2 15.4 %collective-permute-done.8.refs_1_.refs_0_.packed3.rows3 = bf16[64,11264]{1,0:T(8,128)(2,1)S(1)} collective-permute-done((bf16[64,11264]{1,0:T(8,128)(2,1)S(1)}, bf16[64,11264]{1,0:T(8,128)(2,1)S(1)}, u32[]{:S(2)}, u32[]{:S(2)}) %collective-permute-start.8) | collective-permute-done | bytes 1441824 | tf_op jit(solution)/shard_map/ppermute | solution.py:50
  52.6 1.7 %collective-permute-start.14 = (bf16[256,3328]{1,0:T(8,128)(2,1)S(1)}, bf16[256,3328]{1,0:T(8,128)(2,1)S(1)}, u32[]{:S(2)}, u32[]{:S(2)}) collective-permute-start(bf16[256,3328]{1,0:T(8,128)(2,1)S(1)} %shard_map.109.factor), channel_id=1, source_target_pairs={{0,1},{1,0},{2,3},{3,2},{4,5},{5,4},{6,7},{7,6},{8,9},{9,8},{10,11... | collective-permute-start | bytes 5111816 | tf_op jit(solution)/shard_map/ppermute | solution.py:50
  54.5 1.2 %collective-permute-start.11 = (bf16[64,8192]{1,0:T(8,128)(2,1)S(1)}, bf16[64,8192]{1,0:T(8,128)(2,1)S(1)}, u32[]{:S(2)}, u32[]{:S(2)}) collective-permute-start(bf16[64,8192]{1,0:T(8,128)(2,1)S(1)} %shard_map.107), channel_id=1, source_target_pairs={{0,16},{1,5},{2,18},{3,7},{4,20},{5,1},{6,22},{7,3},{8,24},{9,13},... | collective-permute-start | bytes 3145736 | tf_op jit(solution)/shard_map/ppermute | solution.py:50
  55.7 4.1 %shard_map.106.acc = f32[896,192]{1,0:T(8,128)S(1)} custom-call(f32[8,128]{1,0:T(8,128)S(1)} %shard_map.105.refs_0_, bf16[64,11264]{1,0:T(8,128)(2,1)S(1)} %collective-permute-done.8.refs_1_.refs_0_.packed3.rows3, bf16[64,11264]{1,0:T(8,128)(2,1)S(1)} %collective-permute-done.9.refs_2_.packed1.rows1, bf16[64,11264]{1,0:T(8,128)(2,1)S(1)} %get-tuple-element.44.refs_3_.own, ...), custom_call_target="tpu_custom_call" | custom-call | flops 9200000000 | bytes 28800000 | tf_op jit(solution)/shard_map/pallas_call | solution.py:193
  59.8 4.3 %shard_map.110 = (bf16[64,8192]{1,0:T(8,128)(2,1)S(1)}, bf16[64,8192]{1,0:T(8,128)(2,1)S(1)}, bf16[128,8192]{1,0:T(8,128)(2,1)S(1)}, bf16[64,8192]{1,0:T(8,128)(2,1)S(1)}) custom-call(s32[5]{0:T(128)S(1)} %stack.37.place, bf16[64,11264]{1,0:T(8,128)(2,1)S(1)} %collective-permute-done.8.refs_1_.refs_0_.packed3.rows3, ...), custom_call_target="tpu_custom_call" | custom-call | flops 1 | bytes 1 | tf_op jit(solution)/shard_map/pallas_call | solution.py:204
  64.2 0.4 collective-permute-start.15
  64.5 2.4 %collective-permute-start.16 = (bf16[64,8192]{1,0:T(8,128)(2,1)S(1)}, bf16[64,8192]{1,0:T(8,128)(2,1)S(1)}, u32[]{:S(2)}, u32[]{:S(2)}) collective-permute-start(bf16[64,8192]{1,0:T(8,128)(2,1)S(1)} %get-tuple-element.54), channel_id=1, source_target_pairs={{0,48},{1,13},{2,50},{3,15},{4,52},{5,9},{6,54},{7,11},{8,56},{9,5... | collective-permute-start | bytes 3145736 | tf_op jit(solution)/shard_map/ppermute | solution.py:50
  66.9 1.6 %collective-permute-done.11.refs_0_ = bf16[64,8192]{1,0:T(8,128)(2,1)S(1)} collective-permute-done((bf16[64,8192]{1,0:T(8,128)(2,1)S(1)}, bf16[64,8192]{1,0:T(8,128)(2,1)S(1)}, u32[]{:S(2)}, u32[]{:S(2)}) %collective-permute-start.11) | collective-permute-done | bytes 1048608 | tf_op jit(solution)/shard_map/ppermute | solution.py:50
  68.5 4.6 %shard_map.111.acc = f32[1024,64]{1,0:T(8,128)S(1)} custom-call(bf16[64,8192]{1,0:T(8,128)(2,1)S(1)} %collective-permute-done.11.refs_0_, bf16[224,8192]{1,0:T(8,128)(2,1)S(1)} %copy-done.1, bf16[224,8192]{1,0:T(8,128)(2,1)S(1)} %collective-permute-done.4.refs_5_.refs_2_, bf16[224,8192]{1,0:T(8,128)(2,1)S(1)} %copy-done.2, ...), custom_call_target="tpu_custom_call" | custom-call | flops 1 | bytes 1 | tf_op jit(solution)/shard_map/pallas_call | solution.py:193
  73.1 2.0 %shard_map.112 = bf16[64,8192]{1,0:T(8,128)(2,1)S(1)} custom-call(f32[1024,64]{1,0:T(8,128)S(1)} %shard_map.111.acc, bf16[224,8192]{1,0:T(8,128)(2,1)S(1)} %copy-done, bf16[224,8192]{1,0:T(8,128)(2,1)S(1)} %collective-permute-done.12.down_w2, bf16[256,256]{1,0:T(8,128)(2,1)S(1)} %shard_map.104.seconds, bf16[256,3328]{1,0:T(8,128)(2,1)S(1)} %collective-permute-done.14.theirs, ...), custom_call_target="tpu_custom_call" | custom-call | flops 1 | bytes 1 | tf_op jit(solution)/shard_map/pallas_call | solution.py:204
  75.1 2.7 %collective-permute-start.17 = (bf16[64,8192]{1,0:T(8,128)(2,1)S(1)}, bf16[64,8192]{1,0:T(8,128)(2,1)S(1)}, u32[]{:S(2)}, u32[]{:S(2)}) collective-permute-start(bf16[64,8192]{1,0:T(8,128)(2,1)S(1)} %shard_map.112), channel_id=1, source_target_pairs={{0,32},{1,9},{2,34},{3,11},{4,36},{5,13},{6,38},{7,15},{8,40},{9,1... | collective-permute-start | bytes 3145736 | tf_op jit(solution)/shard_map/ppermute | solution.py:50
  77.8 3.5 %shard_map.113.own = f32[64,8192]{1,0:T(8,128)S(1)} custom-call(bf16[64,11264]{1,0:T(8,128)(2,1)S(1)} %get-tuple-element.44.refs_3_.own, f32[896,192]{1,0:T(8,128)S(1)} %shard_map.106.acc, bf16[224,8192]{1,0:T(8,128)(2,1)S(1)} %copy-done, bf16[224,8192]{1,0:T(8,128)(2,1)S(1)} %collective-permute-done.12.down_w2, bf16[256,256]{1,0:T(8,128)(2,1)S(1)} %shard_map.104.seconds, ...), custom_call_target="tpu_custom_call" | custom-call | flops 1 | bytes 1 | tf_op jit(solution)/shard_map/pallas_call | solution.py:204
  81.7 11.3 %collective-permute-done.17.b = bf16[64,8192]{1,0:T(8,128)(2,1)S(1)} collective-permute-done((bf16[64,8192]{1,0:T(8,128)(2,1)S(1)}, bf16[64,8192]{1,0:T(8,128)(2,1)S(1)}, u32[]{:S(2)}, u32[]{:S(2)}) %collective-permute-start.17) | collective-permute-done | bytes 1048608 | tf_op jit(solution)/shard_map/ppermute | solution.py:50
  93.2 1.5 %collective-permute-start.18 = (bf16[16,8192]{1,0:T(8,128)(2,1)S(1)}, bf16[16,8192]{1,0:T(8,128)(2,1)S(1)}, u32[]{:S(2)}, u32[]{:S(2)}) collective-permute-start(bf16[16,8192]{1,0:T(8,128)(2,1)S(1)} %get-tuple-element.56), channel_id=1, source_target_pairs={{0,8},{1,33},{2,10},{3,35},{4,12},{5,37},{6,14},{7,39},{8,0},{9,41... | collective-permute-start | bytes 786440 | tf_op jit(solution)/shard_map/ppermute | solution.py:50
  94.7 1.2 %collective-permute-start.19 = (bf16[16,8192]{1,0:T(8,128)(2,1)S(1)}, bf16[16,8192]{1,0:T(8,128)(2,1)S(1)}, u32[]{:S(2)}, u32[]{:S(2)}) collective-permute-start(bf16[16,8192]{1,0:T(8,128)(2,1)S(1)} %get-tuple-element.57), channel_id=1, source_target_pairs={{0,4},{1,17},{2,6},{3,19},{4,0},{5,21},{6,2},{7,23},{8,12},{9,25},... | collective-permute-start | bytes 786440 | tf_op jit(solution)/shard_map/ppermute | solution.py:50
  95.9 0.6 collective-permute-start.20
  96.5 3.8 %collective-permute-done.18.b2 = bf16[16,8192]{1,0:T(8,128)(2,1)S(1)} collective-permute-done((bf16[16,8192]{1,0:T(8,128)(2,1)S(1)}, bf16[16,8192]{1,0:T(8,128)(2,1)S(1)}, u32[]{:S(2)}, u32[]{:S(2)}) %collective-permute-start.18) | collective-permute-done | bytes 262176 | tf_op jit(solution)/shard_map/ppermute | solution.py:50
  100.3 2.5 %collective-permute-done.19.b1 = bf16[16,8192]{1,0:T(8,128)(2,1)S(1)} collective-permute-done((bf16[16,8192]{1,0:T(8,128)(2,1)S(1)}, bf16[16,8192]{1,0:T(8,128)(2,1)S(1)}, u32[]{:S(2)}, u32[]{:S(2)}) %collective-permute-start.19) | collective-permute-done | bytes 262176 | tf_op jit(solution)/shard_map/ppermute | solution.py:50
  103.1 0.7 shard_map.116
  103.8 1.3 %collective-permute-start.21 = (bf16[8,4096]{1,0:T(8,128)(2,1)S(1)}, bf16[8,4096]{1,0:T(8,128)(2,1)S(1)}, u32[]{:S(2)}, u32[]{:S(2)}) collective-permute-start(bf16[8,4096]{1,0:T(8,128)(2,1)S(1)} %get-tuple-element.60), channel_id=1, source_target_pairs={{0,64},{1,65},{2,66},{3,67},{4,68},{5,69},{6,70},{7,71},{8,72},{9,... | collective-permute-start | bytes 196616 | tf_op jit(solution)/shard_map/ppermute | solution.py:50
  105.0 1.2 %collective-permute-start.22 = (bf16[8,4096]{1,0:T(8,128)(2,1)S(1)}, bf16[8,4096]{1,0:T(8,128)(2,1)S(1)}, u32[]{:S(2)}, u32[]{:S(2)}) collective-permute-start(bf16[8,4096]{1,0:T(8,128)(2,1)S(1)} %get-tuple-element.61), channel_id=1, source_target_pairs={{0,2},{1,3},{2,0},{3,1},{4,6},{5,7},{6,4},{7,5},{8,10},{9,11},{10,... | collective-permute-start | bytes 196616 | tf_op jit(solution)/shard_map/ppermute | solution.py:50
  106.3 1.7 %collective-permute-start.23 = (bf16[8,4096]{1,0:T(8,128)(2,1)S(1)}, bf16[8,4096]{1,0:T(8,128)(2,1)S(1)}, u32[]{:S(2)}, u32[]{:S(2)}) collective-permute-start(bf16[8,4096]{1,0:T(8,128)(2,1)S(1)} %get-tuple-element.62), channel_id=1, source_target_pairs={{0,66},{1,67},{2,64},{3,65},{4,70},{5,71},{6,68},{7,69},{8,74},{9,... | collective-permute-start | bytes 196616 | tf_op jit(solution)/shard_map/ppermute | solution.py:50
  108.0 0.5 collective-permute-done.21.b2
  108.6 2.5 %collective-permute-done.23.b3 = bf16[8,4096]{1,0:T(8,128)(2,1)S(1)} collective-permute-done((bf16[8,4096]{1,0:T(8,128)(2,1)S(1)}, bf16[8,4096]{1,0:T(8,128)(2,1)S(1)}, u32[]{:S(2)}, u32[]{:S(2)}) %collective-permute-start.23) | collective-permute-done | bytes 65568 | tf_op jit(solution)/shard_map/ppermute | solution.py:50
  111.1 0.6 shard_map.117
  111.7 3.4 %collective-permute-start.24 = (bf16[8,2048]{1,0:T(8,128)(2,1)S(1)}, bf16[8,2048]{1,0:T(8,128)(2,1)S(1)}, u32[]{:S(2)}, u32[]{:S(2)}) collective-permute-start(bf16[8,2048]{1,0:T(8,128)(2,1)S(1)} %get-tuple-element.64), channel_id=1, source_target_pairs={{0,1},{1,0},{2,3},{3,2},{4,5},{5,4},{6,7},{7,6},{8,9},{9,8},{10,11... | collective-permute-start | bytes 98312 | tf_op jit(solution)/shard_map/ppermute | solution.py:50
  115.1 0.9 collective-permute-done.24
  116.0 0.6 maximum_select_fusion
  (35 shorter events, 2.0 us)
Async XLA Ops:
  0.8 2.9 %collective-permute-start = (bf16[8,2048]{1,0:T(8,128)(2,1)S(1)}, bf16[8,2048]{1,0:T(8,128)(2,1)S(1)}, u32[]{:S(2)}, u32[]{:S(2)}) collective-permute-start(bf16[8,2048]{1,0:T(8,128)(2,1)S(1)} %get-tuple-element.65), channel_id=1, source_target_pairs={{0,1},{1,0},{2,3},{3,2},{4,5},{5,4},{6,7},{7,6},{8,9},{9,8},{10,11... | collective-permute-start | bytes 98312 | tf_op jit(solution)/shard_map/ppermute | solution.py:50
  4.3 9.2 %collective-permute-start.4 = (bf16[224,8192]{1,0:T(8,128)(2,1)}, bf16[224,8192]{1,0:T(8,128)(2,1)S(1)}, u32[]{:S(2)}, u32[]{:S(2)}) collective-permute-start(bf16[224,8192]{1,0:T(8,128)(2,1)} %refs_1_), channel_id=1, source_target_pairs={{0,1},{1,0},{2,3},{3,2},{4,5},{5,4},{6,7},{7,6},{8,9},{9,8},{10,11... | collective-permute-start | bytes 11010056 | tf_op jit(solution)/shard_map/ppermute | solution.py:50
  4.4 8.5 %collective-permute-start.3 = (bf16[16,3584]{1,0:T(8,128)(2,1)S(1)}, bf16[16,3584]{1,0:T(8,128)(2,1)S(1)}, u32[]{:S(2)}, u32[]{:S(2)}) collective-permute-start(bf16[16,3584]{1,0:T(8,128)(2,1)S(1)} %get-tuple-element.36.message), channel_id=1, source_target_pairs={{0,66},{1,67},{2,64},{3,65},{4,70},{5,71},{6,68},{7,69},{8,74},{9,... | collective-permute-start | bytes 344072 | tf_op jit(solution)/shard_map/ppermute | solution.py:50
  8.3 3.4 %collective-permute-start.1 = (bf16[8,4096]{1,0:T(8,128)(2,1)S(1)}, bf16[8,4096]{1,0:T(8,128)(2,1)S(1)}, u32[]{:S(2)}, u32[]{:S(2)}) collective-permute-start(bf16[8,4096]{1,0:T(8,128)(2,1)S(1)} %get-tuple-element.35.wide), channel_id=1, source_target_pairs={{0,2},{1,3},{2,0},{3,1},{4,6},{5,7},{6,4},{7,5},{8,10},{9,11},{10,... | collective-permute-start | bytes 196616 | tf_op jit(solution)/shard_map/ppermute | solution.py:50
  8.3 4.6 %collective-permute-start.2 = (bf16[8,4096]{1,0:T(8,128)(2,1)S(1)}, bf16[8,4096]{1,0:T(8,128)(2,1)S(1)}, u32[]{:S(2)}, u32[]{:S(2)}) collective-permute-start(bf16[8,4096]{1,0:T(8,128)(2,1)S(1)} %get-tuple-element.35.wide), channel_id=1, source_target_pairs={{0,64},{1,65},{2,66},{3,67},{4,68},{5,69},{6,70},{7,71},{8,72},{9,... | collective-permute-start | bytes 196616 | tf_op jit(solution)/shard_map/ppermute | solution.py:50
  13.5 8.2 %collective-permute-start.5 = (bf16[16,11264]{1,0:T(8,128)(2,1)S(1)}, bf16[16,11264]{1,0:T(8,128)(2,1)S(1)}, u32[]{:S(2)}, u32[]{:S(2)}) collective-permute-start(bf16[16,11264]{1,0:T(8,128)(2,1)S(1)} %shard_map.102.own), channel_id=1, source_target_pairs={{0,8},{1,33},{2,10},{3,35},{4,12},{5,37},{6,14},{7,39},{8,0},{9,41... | collective-permute-start | bytes 1081352 | tf_op jit(solution)/shard_map/ppermute | solution.py:50
  16.5 9.4 %collective-permute-start.6 = (bf16[16,11264]{1,0:T(8,128)(2,1)S(1)}, bf16[16,11264]{1,0:T(8,128)(2,1)S(1)}, u32[]{:S(2)}, u32[]{:S(2)}) collective-permute-start(bf16[16,11264]{1,0:T(8,128)(2,1)S(1)} %shard_map.102.own), channel_id=1, source_target_pairs={{0,4},{1,17},{2,6},{3,19},{4,0},{5,21},{6,2},{7,23},{8,12},{9,25},... | collective-permute-start | bytes 1081352 | tf_op jit(solution)/shard_map/ppermute | solution.py:50
  16.9 9.0 %collective-permute-start.7 = (bf16[16,11264]{1,0:T(8,128)(2,1)S(1)}, bf16[16,11264]{1,0:T(8,128)(2,1)S(1)}, u32[]{:S(2)}, u32[]{:S(2)}) collective-permute-start(bf16[16,11264]{1,0:T(8,128)(2,1)S(1)} %shard_map.102.own), channel_id=1, source_target_pairs={{0,12},{1,49},{2,14},{3,51},{4,8},{5,53},{6,10},{7,55},{8,4},{9,57... | collective-permute-start | bytes 1081352 | tf_op jit(solution)/shard_map/ppermute | solution.py:50
  17.3 0.8 copy-start.3
  18.0 0.8 copy-start.4
  18.8 0.8 copy-start.5
  26.0 29.7 %collective-permute-start.10 = (bf16[224,8192]{1,0:T(8,128)(2,1)}, bf16[224,8192]{1,0:T(8,128)(2,1)S(1)}, u32[]{:S(2)}, u32[]{:S(2)}) collective-permute-start(bf16[224,8192]{1,0:T(8,128)(2,1)} %refs_3_), channel_id=1, source_target_pairs={{0,1},{1,0},{2,3},{3,2},{4,5},{5,4},{6,7},{7,6},{8,9},{9,8},{10,11... | collective-permute-start | bytes 11010056 | tf_op jit(solution)/shard_map/ppermute | solution.py:50
  28.6 31.2 %collective-permute-start.12 = (bf16[224,8192]{1,0:T(8,128)(2,1)}, bf16[224,8192]{1,0:T(8,128)(2,1)S(1)}, u32[]{:S(2)}, u32[]{:S(2)}) collective-permute-start(bf16[224,8192]{1,0:T(8,128)(2,1)} %down_w.3), channel_id=1, source_target_pairs={{0,1},{1,0},{2,3},{3,2},{4,5},{5,4},{6,7},{7,6},{8,9},{9,8},{10,11... | collective-permute-start | bytes 11010056 | tf_op jit(solution)/shard_map/ppermute | solution.py:50
  28.6 8.5 %collective-permute-start.13 = (bf16[64,3072]{1,0:T(8,128)(2,1)S(1)}, bf16[64,3072]{1,0:T(8,128)(2,1)S(1)}, u32[]{:S(2)}, u32[]{:S(2)}) collective-permute-start(bf16[64,3072]{1,0:T(8,128)(2,1)S(1)} %get-tuple-element.48.f0), channel_id=1, source_target_pairs={{0,32},{1,9},{2,34},{3,11},{4,36},{5,13},{6,38},{7,15},{8,40},{9,1... | collective-permute-start | bytes 1179656 | tf_op jit(solution)/shard_map/ppermute | solution.py:50
  31.3 21.3 %collective-permute-start.8 = (bf16[64,11264]{1,0:T(8,128)(2,1)S(1)}, bf16[64,11264]{1,0:T(8,128)(2,1)S(1)}, u32[]{:S(2)}, u32[]{:S(2)}) collective-permute-start(bf16[64,11264]{1,0:T(8,128)(2,1)S(1)} %get-tuple-element.44.refs_3_.own), channel_id=1, source_target_pairs={{0,48},{1,13},{2,50},{3,15},{4,52},{5,9},{6,54},{7,11},{8,56},{9,5... | collective-permute-start | bytes 4325384 | tf_op jit(solution)/shard_map/ppermute | solution.py:50
  32.2 20.3 %collective-permute-start.9 = (bf16[64,11264]{1,0:T(8,128)(2,1)S(1)}, bf16[64,11264]{1,0:T(8,128)(2,1)S(1)}, u32[]{:S(2)}, u32[]{:S(2)}) collective-permute-start(bf16[64,11264]{1,0:T(8,128)(2,1)S(1)} %get-tuple-element.44.refs_3_.own), channel_id=1, source_target_pairs={{0,16},{1,5},{2,18},{3,7},{4,20},{5,1},{6,22},{7,3},{8,24},{9,13},... | collective-permute-start | bytes 4325384 | tf_op jit(solution)/shard_map/ppermute | solution.py:50
  37.1 17.3 %copy-start.1 = (bf16[224,8192]{1,0:T(8,128)(2,1)S(1)}, bf16[224,8192]{1,0:T(8,128)(2,1)}, u32[]{:S(2)}) copy-start(bf16[224,8192]{1,0:T(8,128)(2,1)} %refs_1_) | copy-start | bytes 11010052
  37.1 17.3 %copy-start.2 = (bf16[224,8192]{1,0:T(8,128)(2,1)S(1)}, bf16[224,8192]{1,0:T(8,128)(2,1)}, u32[]{:S(2)}) copy-start(bf16[224,8192]{1,0:T(8,128)(2,1)} %refs_3_) | copy-start | bytes 11010052
  37.2 17.2 %copy-start = (bf16[224,8192]{1,0:T(8,128)(2,1)S(1)}, bf16[224,8192]{1,0:T(8,128)(2,1)}, u32[]{:S(2)}) copy-start(bf16[224,8192]{1,0:T(8,128)(2,1)} %down_w.3) | copy-start | bytes 11010052
  52.6 7.1 %collective-permute-start.14 = (bf16[256,3328]{1,0:T(8,128)(2,1)S(1)}, bf16[256,3328]{1,0:T(8,128)(2,1)S(1)}, u32[]{:S(2)}, u32[]{:S(2)}) collective-permute-start(bf16[256,3328]{1,0:T(8,128)(2,1)S(1)} %shard_map.109.factor), channel_id=1, source_target_pairs={{0,1},{1,0},{2,3},{3,2},{4,5},{5,4},{6,7},{7,6},{8,9},{9,8},{10,11... | collective-permute-start | bytes 5111816 | tf_op jit(solution)/shard_map/ppermute | solution.py:50
  54.5 14.0 %collective-permute-start.11 = (bf16[64,8192]{1,0:T(8,128)(2,1)S(1)}, bf16[64,8192]{1,0:T(8,128)(2,1)S(1)}, u32[]{:S(2)}, u32[]{:S(2)}) collective-permute-start(bf16[64,8192]{1,0:T(8,128)(2,1)S(1)} %shard_map.107), channel_id=1, source_target_pairs={{0,16},{1,5},{2,18},{3,7},{4,20},{5,1},{6,22},{7,3},{8,24},{9,13},... | collective-permute-start | bytes 3145736 | tf_op jit(solution)/shard_map/ppermute | solution.py:50
  64.2 17.2 %collective-permute-start.15 = (bf16[64,8192]{1,0:T(8,128)(2,1)S(1)}, bf16[64,8192]{1,0:T(8,128)(2,1)S(1)}, u32[]{:S(2)}, u32[]{:S(2)}) collective-permute-start(bf16[64,8192]{1,0:T(8,128)(2,1)S(1)} %get-tuple-element.49), channel_id=1, source_target_pairs={{0,16},{1,5},{2,18},{3,7},{4,20},{5,1},{6,22},{7,3},{8,24},{9,13},... | collective-permute-start | bytes 3145736 | tf_op jit(solution)/shard_map/ppermute | solution.py:50
  64.5 16.8 %collective-permute-start.16 = (bf16[64,8192]{1,0:T(8,128)(2,1)S(1)}, bf16[64,8192]{1,0:T(8,128)(2,1)S(1)}, u32[]{:S(2)}, u32[]{:S(2)}) collective-permute-start(bf16[64,8192]{1,0:T(8,128)(2,1)S(1)} %get-tuple-element.54), channel_id=1, source_target_pairs={{0,48},{1,13},{2,50},{3,15},{4,52},{5,9},{6,54},{7,11},{8,56},{9,5... | collective-permute-start | bytes 3145736 | tf_op jit(solution)/shard_map/ppermute | solution.py:50
  75.1 17.9 %collective-permute-start.17 = (bf16[64,8192]{1,0:T(8,128)(2,1)S(1)}, bf16[64,8192]{1,0:T(8,128)(2,1)S(1)}, u32[]{:S(2)}, u32[]{:S(2)}) collective-permute-start(bf16[64,8192]{1,0:T(8,128)(2,1)S(1)} %shard_map.112), channel_id=1, source_target_pairs={{0,32},{1,9},{2,34},{3,11},{4,36},{5,13},{6,38},{7,15},{8,40},{9,1... | collective-permute-start | bytes 3145736 | tf_op jit(solution)/shard_map/ppermute | solution.py:50
  93.2 7.1 %collective-permute-start.18 = (bf16[16,8192]{1,0:T(8,128)(2,1)S(1)}, bf16[16,8192]{1,0:T(8,128)(2,1)S(1)}, u32[]{:S(2)}, u32[]{:S(2)}) collective-permute-start(bf16[16,8192]{1,0:T(8,128)(2,1)S(1)} %get-tuple-element.56), channel_id=1, source_target_pairs={{0,8},{1,33},{2,10},{3,35},{4,12},{5,37},{6,14},{7,39},{8,0},{9,41... | collective-permute-start | bytes 786440 | tf_op jit(solution)/shard_map/ppermute | solution.py:50
  94.7 8.1 %collective-permute-start.19 = (bf16[16,8192]{1,0:T(8,128)(2,1)S(1)}, bf16[16,8192]{1,0:T(8,128)(2,1)S(1)}, u32[]{:S(2)}, u32[]{:S(2)}) collective-permute-start(bf16[16,8192]{1,0:T(8,128)(2,1)S(1)} %get-tuple-element.57), channel_id=1, source_target_pairs={{0,4},{1,17},{2,6},{3,19},{4,0},{5,21},{6,2},{7,23},{8,12},{9,25},... | collective-permute-start | bytes 786440 | tf_op jit(solution)/shard_map/ppermute | solution.py:50
  95.9 7.2 %collective-permute-start.20 = (bf16[16,8192]{1,0:T(8,128)(2,1)S(1)}, bf16[16,8192]{1,0:T(8,128)(2,1)S(1)}, u32[]{:S(2)}, u32[]{:S(2)}) collective-permute-start(bf16[16,8192]{1,0:T(8,128)(2,1)S(1)} %get-tuple-element.58), channel_id=1, source_target_pairs={{0,12},{1,49},{2,14},{3,51},{4,8},{5,53},{6,10},{7,55},{8,4},{9,57... | collective-permute-start | bytes 786440 | tf_op jit(solution)/shard_map/ppermute | solution.py:50
  103.8 4.7 %collective-permute-start.21 = (bf16[8,4096]{1,0:T(8,128)(2,1)S(1)}, bf16[8,4096]{1,0:T(8,128)(2,1)S(1)}, u32[]{:S(2)}, u32[]{:S(2)}) collective-permute-start(bf16[8,4096]{1,0:T(8,128)(2,1)S(1)} %get-tuple-element.60), channel_id=1, source_target_pairs={{0,64},{1,65},{2,66},{3,67},{4,68},{5,69},{6,70},{7,71},{8,72},{9,... | collective-permute-start | bytes 196616 | tf_op jit(solution)/shard_map/ppermute | solution.py:50
  105.0 3.6 %collective-permute-start.22 = (bf16[8,4096]{1,0:T(8,128)(2,1)S(1)}, bf16[8,4096]{1,0:T(8,128)(2,1)S(1)}, u32[]{:S(2)}, u32[]{:S(2)}) collective-permute-start(bf16[8,4096]{1,0:T(8,128)(2,1)S(1)} %get-tuple-element.61), channel_id=1, source_target_pairs={{0,2},{1,3},{2,0},{3,1},{4,6},{5,7},{6,4},{7,5},{8,10},{9,11},{10,... | collective-permute-start | bytes 196616 | tf_op jit(solution)/shard_map/ppermute | solution.py:50
  106.3 4.8 %collective-permute-start.23 = (bf16[8,4096]{1,0:T(8,128)(2,1)S(1)}, bf16[8,4096]{1,0:T(8,128)(2,1)S(1)}, u32[]{:S(2)}, u32[]{:S(2)}) collective-permute-start(bf16[8,4096]{1,0:T(8,128)(2,1)S(1)} %get-tuple-element.62), channel_id=1, source_target_pairs={{0,66},{1,67},{2,64},{3,65},{4,70},{5,71},{6,68},{7,69},{8,74},{9,... | collective-permute-start | bytes 196616 | tf_op jit(solution)/shard_map/ppermute | solution.py:50
  111.7 4.3 %collective-permute-start.24 = (bf16[8,2048]{1,0:T(8,128)(2,1)S(1)}, bf16[8,2048]{1,0:T(8,128)(2,1)S(1)}, u32[]{:S(2)}, u32[]{:S(2)}) collective-permute-start(bf16[8,2048]{1,0:T(8,128)(2,1)S(1)} %get-tuple-element.64), channel_id=1, source_target_pairs={{0,1},{1,0},{2,3},{3,2},{4,5},{5,4},{6,7},{7,6},{8,9},{9,8},{10,11... | collective-permute-start | bytes 98312 | tf_op jit(solution)/shard_map/ppermute | solution.py:50

commit v17 on v16

--- a/solution.py
+++ b/solution.py
@@ -394,8 +394,8 @@
         (factor, packed3, packed1, far, seconds),
     )
     factor2 = send(factor, CORE)
-    (rows3,) = local(part_kernel, [((64, WIDTH), bf16)], (packed3,))
-    rows2 = send(rows3, SECOND[1])
+    (rows1,) = local(part_kernel, [((64, WIDTH), bf16)], (packed1,))
+    rows2 = send(rows1, SECOND[3])
     (touched,) = local(touch_kernel, [((8, 128), f32)], in_vmem(owned))
 
     weights = (owned[0], gate2, owned[1], up2)

time: 117 us -> 117 us (level)
  starting transfers between devices: 36.1 us -> 34.7 us
    ppermute x25, starting transfers between devices: 36.1 us -> 34.7 us  [send(): return lax.ppermute(value, AXES, route)]
  transfers between devices with their start and end apart: 25 -> 25, of which waited for: 15 -> 14; matrix products, arithmetic and copies ran while one was open for 0% -> 0% of each run, Pallas kernels for 18% -> 18%
where the time goes in v17:
time: 117 us; the launch traced here: 116 us
  waiting for transfers between devices  54.5 us (47%)
  starting transfers between devices  34.7 us (30%)
  Pallas kernels  23.1 us (20%)
  local copies, waits for them, and re-layouts  2.37 us (2%)
  other arithmetic  1.42 us (1%)
    ppermute x25, waiting for transfers between devices, send(): return lax.ppermute(value, AXES, route)  54.5 us
    ppermute x25, starting transfers between devices, send(): return lax.ppermute(value, AXES, route)  34.7 us
    pallas_call x3, Pallas kernels, down(): pl.pallas_call(body, in_specs=[SMEM] * len(lead) + [VMEM] * len(operands)...  9.9 us
    pallas_call x2, Pallas kernels, project(): pl.pallas_call(lambda *refs: project_kernel(n, *refs[more:]), in_specs=[V...  8.69 us
    pallas_call x13, Pallas kernels, local(): pl.pallas_call(body, in_specs=[SMEM] * len(lead) + [VMEM] * len(operands)...  4.52 us
  transfers between devices with their start and end apart: 25, of which 14 were waited for; matrix products, arithmetic and copies ran while one was open for 0% of the time, Pallas kernels for 18%

profile of v17, /device:TPU:1, one launch (start us, length us, event | category | flops | bytes accessed | tf_op | source)
XLA Modules:
  0.0 116.3 jit_solution(7893458338192679498)
XLA Ops:
  0.0 0.8 select_bitcast_fusion
  0.8 1.5 %collective-permute-start = (bf16[8,2048]{1,0:T(8,128)(2,1)S(1)}, bf16[8,2048]{1,0:T(8,128)(2,1)S(1)}, u32[]{:S(2)}, u32[]{:S(2)}) collective-permute-start(bf16[8,2048]{1,0:T(8,128)(2,1)S(1)} %get-tuple-element.65), channel_id=1, source_target_pairs={{0,1},{1,0},{2,3},{3,2},{4,5},{5,4},{6,7},{7,6},{8,9},{9,8},{10,11... | collective-permute-start | bytes 98312 | tf_op jit(solution)/shard_map/ppermute | solution.py:50
  2.4 1.3 %shard_map.100.factor = bf16[16,1536]{1,0:T(8,128)(2,1)S(1)} custom-call(s32[5]{0:T(128)S(1)} %stack.37.place, bf16[64,256]{1,0:T(8,128)(2,1)} %gate.1, bf16[64,256]{1,0:T(8,128)(2,1)} %up.1, bf16[64,256]{1,0:T(8,128)(2,1)} %down.1), custom_call_target="tpu_custom_call" | custom-call | flops 1 | bytes 1 | tf_op jit(solution)/shard_map/pallas_call | solution.py:217
  3.7 0.6 shard_map.101
  4.4 3.9 %collective-permute-start.3 = (bf16[16,3584]{1,0:T(8,128)(2,1)S(1)}, bf16[16,3584]{1,0:T(8,128)(2,1)S(1)}, u32[]{:S(2)}, u32[]{:S(2)}) collective-permute-start(bf16[16,3584]{1,0:T(8,128)(2,1)S(1)} %get-tuple-element.36.message), channel_id=1, source_target_pairs={{0,66},{1,67},{2,64},{3,65},{4,70},{5,71},{6,68},{7,69},{8,74},{9,... | collective-permute-start | bytes 344072 | tf_op jit(solution)/shard_map/ppermute | solution.py:50
  8.3 1.3 %collective-permute-start.2 = (bf16[8,4096]{1,0:T(8,128)(2,1)S(1)}, bf16[8,4096]{1,0:T(8,128)(2,1)S(1)}, u32[]{:S(2)}, u32[]{:S(2)}) collective-permute-start(bf16[8,4096]{1,0:T(8,128)(2,1)S(1)} %get-tuple-element.35.wide), channel_id=1, source_target_pairs={{0,64},{1,65},{2,66},{3,67},{4,68},{5,69},{6,70},{7,71},{8,72},{9,... | collective-permute-start | bytes 196616 | tf_op jit(solution)/shard_map/ppermute | solution.py:50
  9.6 2.1 %collective-permute-done.1.z1 = bf16[8,4096]{1,0:T(8,128)(2,1)S(1)} collective-permute-done((bf16[8,4096]{1,0:T(8,128)(2,1)S(1)}, bf16[8,4096]{1,0:T(8,128)(2,1)S(1)}, u32[]{:S(2)}, u32[]{:S(2)}) %collective-permute-start.1) | collective-permute-done | bytes 65568 | tf_op jit(solution)/shard_map/ppermute | solution.py:50
  11.7 1.2 %collective-permute-done.2.z2 = bf16[8,4096]{1,0:T(8,128)(2,1)S(1)} collective-permute-done((bf16[8,4096]{1,0:T(8,128)(2,1)S(1)}, bf16[8,4096]{1,0:T(8,128)(2,1)S(1)}, u32[]{:S(2)}, u32[]{:S(2)}) %collective-permute-start.2) | collective-permute-done | bytes 65568 | tf_op jit(solution)/shard_map/ppermute | solution.py:50
  12.9 0.6 shard_map.102.own
  13.5 3.0 %collective-permute-start.5 = (bf16[16,11264]{1,0:T(8,128)(2,1)S(1)}, bf16[16,11264]{1,0:T(8,128)(2,1)S(1)}, u32[]{:S(2)}, u32[]{:S(2)}) collective-permute-start(bf16[16,11264]{1,0:T(8,128)(2,1)S(1)} %shard_map.102.own), channel_id=1, source_target_pairs={{0,8},{1,33},{2,10},{3,35},{4,12},{5,37},{6,14},{7,39},{8,0},{9,41... | collective-permute-start | bytes 1081352 | tf_op jit(solution)/shard_map/ppermute | solution.py:50
  16.5 0.4 collective-permute-start.6
  16.9 0.4 collective-permute-start.7
  17.3 0.8 copy-done.3
  18.0 0.8 copy-done.4
  18.8 0.8 copy-done.5
  19.6 2.1 %collective-permute-done.5.got2 = bf16[16,11264]{1,0:T(8,128)(2,1)S(1)} collective-permute-done((bf16[16,11264]{1,0:T(8,128)(2,1)S(1)}, bf16[16,11264]{1,0:T(8,128)(2,1)S(1)}, u32[]{:S(2)}, u32[]{:S(2)}) %collective-permute-start.5) | collective-permute-done | bytes 360480 | tf_op jit(solution)/shard_map/ppermute | solution.py:50
  21.7 4.2 %collective-permute-done.6.got1 = bf16[16,11264]{1,0:T(8,128)(2,1)S(1)} collective-permute-done((bf16[16,11264]{1,0:T(8,128)(2,1)S(1)}, bf16[16,11264]{1,0:T(8,128)(2,1)S(1)}, u32[]{:S(2)}, u32[]{:S(2)}) %collective-permute-start.6) | collective-permute-done | bytes 360480 | tf_op jit(solution)/shard_map/ppermute | solution.py:50
  26.0 2.5 %collective-permute-start.10 = (bf16[224,8192]{1,0:T(8,128)(2,1)}, bf16[224,8192]{1,0:T(8,128)(2,1)S(1)}, u32[]{:S(2)}, u32[]{:S(2)}) collective-permute-start(bf16[224,8192]{1,0:T(8,128)(2,1)} %refs_3_), channel_id=1, source_target_pairs={{0,1},{1,0},{2,3},{3,2},{4,5},{5,4},{6,7},{7,6},{8,9},{9,8},{10,11... | collective-permute-start | bytes 11010056 | tf_op jit(solution)/shard_map/ppermute | solution.py:50
  28.6 2.6 %collective-permute-start.13 = (bf16[64,3072]{1,0:T(8,128)(2,1)S(1)}, bf16[64,3072]{1,0:T(8,128)(2,1)S(1)}, u32[]{:S(2)}, u32[]{:S(2)}) collective-permute-start(bf16[64,3072]{1,0:T(8,128)(2,1)S(1)} %get-tuple-element.48.f0), channel_id=1, source_target_pairs={{0,32},{1,9},{2,34},{3,11},{4,36},{5,13},{6,38},{7,15},{8,40},{9,1... | collective-permute-start | bytes 1179656 | tf_op jit(solution)/shard_map/ppermute | solution.py:50
  31.3 0.9 collective-permute-start.8
  32.2 4.9 %collective-permute-done.13.refs_0_ = bf16[64,3072]{1,0:T(8,128)(2,1)S(1)} collective-permute-done((bf16[64,3072]{1,0:T(8,128)(2,1)S(1)}, bf16[64,3072]{1,0:T(8,128)(2,1)S(1)}, u32[]{:S(2)}, u32[]{:S(2)}) %collective-permute-start.13) | collective-permute-done | bytes 393248 | tf_op jit(solution)/shard_map/ppermute | solution.py:50
  37.2 15.4 %collective-permute-done.8.refs_1_.packed3.rows3 = bf16[64,11264]{1,0:T(8,128)(2,1)S(1)} collective-permute-done((bf16[64,11264]{1,0:T(8,128)(2,1)S(1)}, bf16[64,11264]{1,0:T(8,128)(2,1)S(1)}, u32[]{:S(2)}, u32[]{:S(2)}) %collective-permute-start.8) | collective-permute-done | bytes 1441824 | tf_op jit(solution)/shard_map/ppermute | solution.py:50
  52.6 1.7 %collective-permute-start.14 = (bf16[256,3328]{1,0:T(8,128)(2,1)S(1)}, bf16[256,3328]{1,0:T(8,128)(2,1)S(1)}, u32[]{:S(2)}, u32[]{:S(2)}) collective-permute-start(bf16[256,3328]{1,0:T(8,128)(2,1)S(1)} %shard_map.109.factor), channel_id=1, source_target_pairs={{0,1},{1,0},{2,3},{3,2},{4,5},{5,4},{6,7},{7,6},{8,9},{9,8},{10,11... | collective-permute-start | bytes 5111816 | tf_op jit(solution)/shard_map/ppermute | solution.py:50
  54.5 2.4 %collective-permute-start.11 = (bf16[64,8192]{1,0:T(8,128)(2,1)S(1)}, bf16[64,8192]{1,0:T(8,128)(2,1)S(1)}, u32[]{:S(2)}, u32[]{:S(2)}) collective-permute-start(bf16[64,8192]{1,0:T(8,128)(2,1)S(1)} %shard_map.107), channel_id=1, source_target_pairs={{0,48},{1,13},{2,50},{3,15},{4,52},{5,9},{6,54},{7,11},{8,56},{9,5... | collective-permute-start | bytes 3145736 | tf_op jit(solution)/shard_map/ppermute | solution.py:50
  56.9 4.1 %shard_map.106.acc = f32[896,192]{1,0:T(8,128)S(1)} custom-call(f32[8,128]{1,0:T(8,128)S(1)} %shard_map.105.refs_0_, bf16[64,11264]{1,0:T(8,128)(2,1)S(1)} %collective-permute-done.8.refs_1_.packed3.rows3, bf16[64,11264]{1,0:T(8,128)(2,1)S(1)} %collective-permute-done.9.refs_2_.refs_0_.packed1.rows1, bf16[64,11264]{1,0:T(8,128)(2,1)S(1)} %get-tuple-element.44.refs_3_.own, ...), custom_call_target="tpu_custom_call" | custom-call | flops 9200000000 | bytes 28800000 | tf_op jit(solution)/shard_map/pallas_call | solution.py:193
  61.0 4.3 %shard_map.110 = (bf16[64,8192]{1,0:T(8,128)(2,1)S(1)}, bf16[64,8192]{1,0:T(8,128)(2,1)S(1)}, bf16[128,8192]{1,0:T(8,128)(2,1)S(1)}, bf16[64,8192]{1,0:T(8,128)(2,1)S(1)}) custom-call(s32[5]{0:T(128)S(1)} %stack.37.place, bf16[64,11264]{1,0:T(8,128)(2,1)S(1)} %collective-permute-done.8.refs_1_.packed3.rows3, ...), custom_call_target="tpu_custom_call" | custom-call | flops 1 | bytes 1 | tf_op jit(solution)/shard_map/pallas_call | solution.py:204
  65.4 0.9 collective-permute-start.16
  66.3 3.4 %collective-permute-done.11.refs_0_ = bf16[64,8192]{1,0:T(8,128)(2,1)S(1)} collective-permute-done((bf16[64,8192]{1,0:T(8,128)(2,1)S(1)}, bf16[64,8192]{1,0:T(8,128)(2,1)S(1)}, u32[]{:S(2)}, u32[]{:S(2)}) %collective-permute-start.11) | collective-permute-done | bytes 1048608 | tf_op jit(solution)/shard_map/ppermute | solution.py:50
  69.7 4.6 %shard_map.111.acc = f32[1024,64]{1,0:T(8,128)S(1)} custom-call(bf16[64,8192]{1,0:T(8,128)(2,1)S(1)} %collective-permute-done.11.refs_0_, bf16[224,8192]{1,0:T(8,128)(2,1)S(1)} %copy-done.1, bf16[224,8192]{1,0:T(8,128)(2,1)S(1)} %collective-permute-done.4.refs_5_.refs_2_, bf16[224,8192]{1,0:T(8,128)(2,1)S(1)} %copy-done.2, ...), custom_call_target="tpu_custom_call" | custom-call | flops 1 | bytes 1 | tf_op jit(solution)/shard_map/pallas_call | solution.py:193
  74.3 2.0 %shard_map.112 = bf16[64,8192]{1,0:T(8,128)(2,1)S(1)} custom-call(f32[1024,64]{1,0:T(8,128)S(1)} %shard_map.111.acc, bf16[224,8192]{1,0:T(8,128)(2,1)S(1)} %copy-done, bf16[224,8192]{1,0:T(8,128)(2,1)S(1)} %collective-permute-done.12.down_w2, bf16[256,256]{1,0:T(8,128)(2,1)S(1)} %shard_map.104.seconds, bf16[256,3328]{1,0:T(8,128)(2,1)S(1)} %collective-permute-done.14.theirs, ...), custom_call_target="tpu_custom_call" | custom-call | flops 1 | bytes 1 | tf_op jit(solution)/shard_map/pallas_call | solution.py:204
  76.3 1.5 %collective-permute-start.17 = (bf16[64,8192]{1,0:T(8,128)(2,1)S(1)}, bf16[64,8192]{1,0:T(8,128)(2,1)S(1)}, u32[]{:S(2)}, u32[]{:S(2)}) collective-permute-start(bf16[64,8192]{1,0:T(8,128)(2,1)S(1)} %shard_map.112), channel_id=1, source_target_pairs={{0,32},{1,9},{2,34},{3,11},{4,36},{5,13},{6,38},{7,15},{8,40},{9,1... | collective-permute-start | bytes 3145736 | tf_op jit(solution)/shard_map/ppermute | solution.py:50
  77.8 3.6 %shard_map.113.own = f32[64,8192]{1,0:T(8,128)S(1)} custom-call(bf16[64,11264]{1,0:T(8,128)(2,1)S(1)} %get-tuple-element.44.refs_3_.own, f32[896,192]{1,0:T(8,128)S(1)} %shard_map.106.acc, bf16[224,8192]{1,0:T(8,128)(2,1)S(1)} %copy-done, bf16[224,8192]{1,0:T(8,128)(2,1)S(1)} %collective-permute-done.12.down_w2, bf16[256,256]{1,0:T(8,128)(2,1)S(1)} %shard_map.104.seconds, ...), custom_call_target="tpu_custom_call" | custom-call | flops 1 | bytes 1 | tf_op jit(solution)/shard_map/pallas_call | solution.py:204
  81.4 10.8 %collective-permute-done.16.b3 = bf16[64,8192]{1,0:T(8,128)(2,1)S(1)} collective-permute-done((bf16[64,8192]{1,0:T(8,128)(2,1)S(1)}, bf16[64,8192]{1,0:T(8,128)(2,1)S(1)}, u32[]{:S(2)}, u32[]{:S(2)}) %collective-permute-start.16) | collective-permute-done | bytes 1048608 | tf_op jit(solution)/shard_map/ppermute | solution.py:50
  92.7 1.7 %collective-permute-start.18 = (bf16[16,8192]{1,0:T(8,128)(2,1)S(1)}, bf16[16,8192]{1,0:T(8,128)(2,1)S(1)}, u32[]{:S(2)}, u32[]{:S(2)}) collective-permute-start(bf16[16,8192]{1,0:T(8,128)(2,1)S(1)} %get-tuple-element.56), channel_id=1, source_target_pairs={{0,8},{1,33},{2,10},{3,35},{4,12},{5,37},{6,14},{7,39},{8,0},{9,41... | collective-permute-start | bytes 786440 | tf_op jit(solution)/shard_map/ppermute | solution.py:50
  94.3 1.3 %collective-permute-start.19 = (bf16[16,8192]{1,0:T(8,128)(2,1)S(1)}, bf16[16,8192]{1,0:T(8,128)(2,1)S(1)}, u32[]{:S(2)}, u32[]{:S(2)}) collective-permute-start(bf16[16,8192]{1,0:T(8,128)(2,1)S(1)} %get-tuple-element.57), channel_id=1, source_target_pairs={{0,4},{1,17},{2,6},{3,19},{4,0},{5,21},{6,2},{7,23},{8,12},{9,25},... | collective-permute-start | bytes 786440 | tf_op jit(solution)/shard_map/ppermute | solution.py:50
  95.7 0.4 collective-permute-start.20
  96.1 3.7 %collective-permute-done.18.b2 = bf16[16,8192]{1,0:T(8,128)(2,1)S(1)} collective-permute-done((bf16[16,8192]{1,0:T(8,128)(2,1)S(1)}, bf16[16,8192]{1,0:T(8,128)(2,1)S(1)}, u32[]{:S(2)}, u32[]{:S(2)}) %collective-permute-start.18) | collective-permute-done | bytes 262176 | tf_op jit(solution)/shard_map/ppermute | solution.py:50
  99.8 2.8 %collective-permute-done.19.b1 = bf16[16,8192]{1,0:T(8,128)(2,1)S(1)} collective-permute-done((bf16[16,8192]{1,0:T(8,128)(2,1)S(1)}, bf16[16,8192]{1,0:T(8,128)(2,1)S(1)}, u32[]{:S(2)}, u32[]{:S(2)}) %collective-permute-start.19) | collective-permute-done | bytes 262176 | tf_op jit(solution)/shard_map/ppermute | solution.py:50
  102.6 0.7 shard_map.116
  103.3 1.3 %collective-permute-start.21 = (bf16[8,4096]{1,0:T(8,128)(2,1)S(1)}, bf16[8,4096]{1,0:T(8,128)(2,1)S(1)}, u32[]{:S(2)}, u32[]{:S(2)}) collective-permute-start(bf16[8,4096]{1,0:T(8,128)(2,1)S(1)} %get-tuple-element.60), channel_id=1, source_target_pairs={{0,64},{1,65},{2,66},{3,67},{4,68},{5,69},{6,70},{7,71},{8,72},{9,... | collective-permute-start | bytes 196616 | tf_op jit(solution)/shard_map/ppermute | solution.py:50
  104.5 1.2 %collective-permute-start.22 = (bf16[8,4096]{1,0:T(8,128)(2,1)S(1)}, bf16[8,4096]{1,0:T(8,128)(2,1)S(1)}, u32[]{:S(2)}, u32[]{:S(2)}) collective-permute-start(bf16[8,4096]{1,0:T(8,128)(2,1)S(1)} %get-tuple-element.61), channel_id=1, source_target_pairs={{0,2},{1,3},{2,0},{3,1},{4,6},{5,7},{6,4},{7,5},{8,10},{9,11},{10,... | collective-permute-start | bytes 196616 | tf_op jit(solution)/shard_map/ppermute | solution.py:50
  105.8 1.7 %collective-permute-start.23 = (bf16[8,4096]{1,0:T(8,128)(2,1)S(1)}, bf16[8,4096]{1,0:T(8,128)(2,1)S(1)}, u32[]{:S(2)}, u32[]{:S(2)}) collective-permute-start(bf16[8,4096]{1,0:T(8,128)(2,1)S(1)} %get-tuple-element.62), channel_id=1, source_target_pairs={{0,66},{1,67},{2,64},{3,65},{4,70},{5,71},{6,68},{7,69},{8,74},{9,... | collective-permute-start | bytes 196616 | tf_op jit(solution)/shard_map/ppermute | solution.py:50
  107.5 0.5 collective-permute-done.21.b2
  108.1 2.3 %collective-permute-done.23.b3 = bf16[8,4096]{1,0:T(8,128)(2,1)S(1)} collective-permute-done((bf16[8,4096]{1,0:T(8,128)(2,1)S(1)}, bf16[8,4096]{1,0:T(8,128)(2,1)S(1)}, u32[]{:S(2)}, u32[]{:S(2)}) %collective-permute-start.23) | collective-permute-done | bytes 65568 | tf_op jit(solution)/shard_map/ppermute | solution.py:50
  110.4 0.6 shard_map.117
  111.0 3.8 %collective-permute-start.24 = (bf16[8,2048]{1,0:T(8,128)(2,1)S(1)}, bf16[8,2048]{1,0:T(8,128)(2,1)S(1)}, u32[]{:S(2)}, u32[]{:S(2)}) collective-permute-start(bf16[8,2048]{1,0:T(8,128)(2,1)S(1)} %get-tuple-element.64), channel_id=1, source_target_pairs={{0,1},{1,0},{2,3},{3,2},{4,5},{5,4},{6,7},{7,6},{8,9},{9,8},{10,11... | collective-permute-start | bytes 98312 | tf_op jit(solution)/shard_map/ppermute | solution.py:50
  114.8 0.9 collective-permute-done.24
  115.7 0.6 maximum_select_fusion
  (35 shorter events, 1.4 us)
Async XLA Ops:
  0.8 2.9 %collective-permute-start = (bf16[8,2048]{1,0:T(8,128)(2,1)S(1)}, bf16[8,2048]{1,0:T(8,128)(2,1)S(1)}, u32[]{:S(2)}, u32[]{:S(2)}) collective-permute-start(bf16[8,2048]{1,0:T(8,128)(2,1)S(1)} %get-tuple-element.65), channel_id=1, source_target_pairs={{0,1},{1,0},{2,3},{3,2},{4,5},{5,4},{6,7},{7,6},{8,9},{9,8},{10,11... | collective-permute-start | bytes 98312 | tf_op jit(solution)/shard_map/ppermute | solution.py:50
  4.3 9.2 %collective-permute-start.4 = (bf16[224,8192]{1,0:T(8,128)(2,1)}, bf16[224,8192]{1,0:T(8,128)(2,1)S(1)}, u32[]{:S(2)}, u32[]{:S(2)}) collective-permute-start(bf16[224,8192]{1,0:T(8,128)(2,1)} %refs_1_), channel_id=1, source_target_pairs={{0,1},{1,0},{2,3},{3,2},{4,5},{5,4},{6,7},{7,6},{8,9},{9,8},{10,11... | collective-permute-start | bytes 11010056 | tf_op jit(solution)/shard_map/ppermute | solution.py:50
  4.4 8.5 %collective-permute-start.3 = (bf16[16,3584]{1,0:T(8,128)(2,1)S(1)}, bf16[16,3584]{1,0:T(8,128)(2,1)S(1)}, u32[]{:S(2)}, u32[]{:S(2)}) collective-permute-start(bf16[16,3584]{1,0:T(8,128)(2,1)S(1)} %get-tuple-element.36.message), channel_id=1, source_target_pairs={{0,66},{1,67},{2,64},{3,65},{4,70},{5,71},{6,68},{7,69},{8,74},{9,... | collective-permute-start | bytes 344072 | tf_op jit(solution)/shard_map/ppermute | solution.py:50
  8.3 3.4 %collective-permute-start.1 = (bf16[8,4096]{1,0:T(8,128)(2,1)S(1)}, bf16[8,4096]{1,0:T(8,128)(2,1)S(1)}, u32[]{:S(2)}, u32[]{:S(2)}) collective-permute-start(bf16[8,4096]{1,0:T(8,128)(2,1)S(1)} %get-tuple-element.35.wide), channel_id=1, source_target_pairs={{0,2},{1,3},{2,0},{3,1},{4,6},{5,7},{6,4},{7,5},{8,10},{9,11},{10,... | collective-permute-start | bytes 196616 | tf_op jit(solution)/shard_map/ppermute | solution.py:50
  8.3 4.6 %collective-permute-start.2 = (bf16[8,4096]{1,0:T(8,128)(2,1)S(1)}, bf16[8,4096]{1,0:T(8,128)(2,1)S(1)}, u32[]{:S(2)}, u32[]{:S(2)}) collective-permute-start(bf16[8,4096]{1,0:T(8,128)(2,1)S(1)} %get-tuple-element.35.wide), channel_id=1, source_target_pairs={{0,64},{1,65},{2,66},{3,67},{4,68},{5,69},{6,70},{7,71},{8,72},{9,... | collective-permute-start | bytes 196616 | tf_op jit(solution)/shard_map/ppermute | solution.py:50
  13.5 8.2 %collective-permute-start.5 = (bf16[16,11264]{1,0:T(8,128)(2,1)S(1)}, bf16[16,11264]{1,0:T(8,128)(2,1)S(1)}, u32[]{:S(2)}, u32[]{:S(2)}) collective-permute-start(bf16[16,11264]{1,0:T(8,128)(2,1)S(1)} %shard_map.102.own), channel_id=1, source_target_pairs={{0,8},{1,33},{2,10},{3,35},{4,12},{5,37},{6,14},{7,39},{8,0},{9,41... | collective-permute-start | bytes 1081352 | tf_op jit(solution)/shard_map/ppermute | solution.py:50
  16.5 9.4 %collective-permute-start.6 = (bf16[16,11264]{1,0:T(8,128)(2,1)S(1)}, bf16[16,11264]{1,0:T(8,128)(2,1)S(1)}, u32[]{:S(2)}, u32[]{:S(2)}) collective-permute-start(bf16[16,11264]{1,0:T(8,128)(2,1)S(1)} %shard_map.102.own), channel_id=1, source_target_pairs={{0,4},{1,17},{2,6},{3,19},{4,0},{5,21},{6,2},{7,23},{8,12},{9,25},... | collective-permute-start | bytes 1081352 | tf_op jit(solution)/shard_map/ppermute | solution.py:50
  16.9 9.0 %collective-permute-start.7 = (bf16[16,11264]{1,0:T(8,128)(2,1)S(1)}, bf16[16,11264]{1,0:T(8,128)(2,1)S(1)}, u32[]{:S(2)}, u32[]{:S(2)}) collective-permute-start(bf16[16,11264]{1,0:T(8,128)(2,1)S(1)} %shard_map.102.own), channel_id=1, source_target_pairs={{0,12},{1,49},{2,14},{3,51},{4,8},{5,53},{6,10},{7,55},{8,4},{9,57... | collective-permute-start | bytes 1081352 | tf_op jit(solution)/shard_map/ppermute | solution.py:50
  17.3 0.8 copy-start.3
  18.0 0.8 copy-start.4
  18.8 0.8 copy-start.5
  26.0 30.9 %collective-permute-start.10 = (bf16[224,8192]{1,0:T(8,128)(2,1)}, bf16[224,8192]{1,0:T(8,128)(2,1)S(1)}, u32[]{:S(2)}, u32[]{:S(2)}) collective-permute-start(bf16[224,8192]{1,0:T(8,128)(2,1)} %refs_3_), channel_id=1, source_target_pairs={{0,1},{1,0},{2,3},{3,2},{4,5},{5,4},{6,7},{7,6},{8,9},{9,8},{10,11... | collective-permute-start | bytes 11010056 | tf_op jit(solution)/shard_map/ppermute | solution.py:50
  28.6 32.4 %collective-permute-start.12 = (bf16[224,8192]{1,0:T(8,128)(2,1)}, bf16[224,8192]{1,0:T(8,128)(2,1)S(1)}, u32[]{:S(2)}, u32[]{:S(2)}) collective-permute-start(bf16[224,8192]{1,0:T(8,128)(2,1)} %down_w.3), channel_id=1, source_target_pairs={{0,1},{1,0},{2,3},{3,2},{4,5},{5,4},{6,7},{7,6},{8,9},{9,8},{10,11... | collective-permute-start | bytes 11010056 | tf_op jit(solution)/shard_map/ppermute | solution.py:50
  28.6 8.5 %collective-permute-start.13 = (bf16[64,3072]{1,0:T(8,128)(2,1)S(1)}, bf16[64,3072]{1,0:T(8,128)(2,1)S(1)}, u32[]{:S(2)}, u32[]{:S(2)}) collective-permute-start(bf16[64,3072]{1,0:T(8,128)(2,1)S(1)} %get-tuple-element.48.f0), channel_id=1, source_target_pairs={{0,32},{1,9},{2,34},{3,11},{4,36},{5,13},{6,38},{7,15},{8,40},{9,1... | collective-permute-start | bytes 1179656 | tf_op jit(solution)/shard_map/ppermute | solution.py:50
  31.3 21.3 %collective-permute-start.8 = (bf16[64,11264]{1,0:T(8,128)(2,1)S(1)}, bf16[64,11264]{1,0:T(8,128)(2,1)S(1)}, u32[]{:S(2)}, u32[]{:S(2)}) collective-permute-start(bf16[64,11264]{1,0:T(8,128)(2,1)S(1)} %get-tuple-element.44.refs_3_.own), channel_id=1, source_target_pairs={{0,48},{1,13},{2,50},{3,15},{4,52},{5,9},{6,54},{7,11},{8,56},{9,5... | collective-permute-start | bytes 4325384 | tf_op jit(solution)/shard_map/ppermute | solution.py:50
  32.2 20.3 %collective-permute-start.9 = (bf16[64,11264]{1,0:T(8,128)(2,1)S(1)}, bf16[64,11264]{1,0:T(8,128)(2,1)S(1)}, u32[]{:S(2)}, u32[]{:S(2)}) collective-permute-start(bf16[64,11264]{1,0:T(8,128)(2,1)S(1)} %get-tuple-element.44.refs_3_.own), channel_id=1, source_target_pairs={{0,16},{1,5},{2,18},{3,7},{4,20},{5,1},{6,22},{7,3},{8,24},{9,13},... | collective-permute-start | bytes 4325384 | tf_op jit(solution)/shard_map/ppermute | solution.py:50
  37.1 17.3 %copy-start.1 = (bf16[224,8192]{1,0:T(8,128)(2,1)S(1)}, bf16[224,8192]{1,0:T(8,128)(2,1)}, u32[]{:S(2)}) copy-start(bf16[224,8192]{1,0:T(8,128)(2,1)} %refs_1_) | copy-start | bytes 11010052
  37.1 17.3 %copy-start.2 = (bf16[224,8192]{1,0:T(8,128)(2,1)S(1)}, bf16[224,8192]{1,0:T(8,128)(2,1)}, u32[]{:S(2)}) copy-start(bf16[224,8192]{1,0:T(8,128)(2,1)} %refs_3_) | copy-start | bytes 11010052
  37.2 17.2 %copy-start = (bf16[224,8192]{1,0:T(8,128)(2,1)S(1)}, bf16[224,8192]{1,0:T(8,128)(2,1)}, u32[]{:S(2)}) copy-start(bf16[224,8192]{1,0:T(8,128)(2,1)} %down_w.3) | copy-start | bytes 11010052
  52.6 8.3 %collective-permute-start.14 = (bf16[256,3328]{1,0:T(8,128)(2,1)S(1)}, bf16[256,3328]{1,0:T(8,128)(2,1)S(1)}, u32[]{:S(2)}, u32[]{:S(2)}) collective-permute-start(bf16[256,3328]{1,0:T(8,128)(2,1)S(1)} %shard_map.109.factor), channel_id=1, source_target_pairs={{0,1},{1,0},{2,3},{3,2},{4,5},{5,4},{6,7},{7,6},{8,9},{9,8},{10,11... | collective-permute-start | bytes 5111816 | tf_op jit(solution)/shard_map/ppermute | solution.py:50
  54.5 15.2 %collective-permute-start.11 = (bf16[64,8192]{1,0:T(8,128)(2,1)S(1)}, bf16[64,8192]{1,0:T(8,128)(2,1)S(1)}, u32[]{:S(2)}, u32[]{:S(2)}) collective-permute-start(bf16[64,8192]{1,0:T(8,128)(2,1)S(1)} %shard_map.107), channel_id=1, source_target_pairs={{0,48},{1,13},{2,50},{3,15},{4,52},{5,9},{6,54},{7,11},{8,56},{9,5... | collective-permute-start | bytes 3145736 | tf_op jit(solution)/shard_map/ppermute | solution.py:50
  65.3 16.0 %collective-permute-start.15 = (bf16[64,8192]{1,0:T(8,128)(2,1)S(1)}, bf16[64,8192]{1,0:T(8,128)(2,1)S(1)}, u32[]{:S(2)}, u32[]{:S(2)}) collective-permute-start(bf16[64,8192]{1,0:T(8,128)(2,1)S(1)} %get-tuple-element.49), channel_id=1, source_target_pairs={{0,16},{1,5},{2,18},{3,7},{4,20},{5,1},{6,22},{7,3},{8,24},{9,13},... | collective-permute-start | bytes 3145736 | tf_op jit(solution)/shard_map/ppermute | solution.py:50
  65.4 26.7 %collective-permute-start.16 = (bf16[64,8192]{1,0:T(8,128)(2,1)S(1)}, bf16[64,8192]{1,0:T(8,128)(2,1)S(1)}, u32[]{:S(2)}, u32[]{:S(2)}) collective-permute-start(bf16[64,8192]{1,0:T(8,128)(2,1)S(1)} %get-tuple-element.54), channel_id=1, source_target_pairs={{0,48},{1,13},{2,50},{3,15},{4,52},{5,9},{6,54},{7,11},{8,56},{9,5... | collective-permute-start | bytes 3145736 | tf_op jit(solution)/shard_map/ppermute | solution.py:50
  76.3 16.2 %collective-permute-start.17 = (bf16[64,8192]{1,0:T(8,128)(2,1)S(1)}, bf16[64,8192]{1,0:T(8,128)(2,1)S(1)}, u32[]{:S(2)}, u32[]{:S(2)}) collective-permute-start(bf16[64,8192]{1,0:T(8,128)(2,1)S(1)} %shard_map.112), channel_id=1, source_target_pairs={{0,32},{1,9},{2,34},{3,11},{4,36},{5,13},{6,38},{7,15},{8,40},{9,1... | collective-permute-start | bytes 3145736 | tf_op jit(solution)/shard_map/ppermute | solution.py:50
  92.7 7.1 %collective-permute-start.18 = (bf16[16,8192]{1,0:T(8,128)(2,1)S(1)}, bf16[16,8192]{1,0:T(8,128)(2,1)S(1)}, u32[]{:S(2)}, u32[]{:S(2)}) collective-permute-start(bf16[16,8192]{1,0:T(8,128)(2,1)S(1)} %get-tuple-element.56), channel_id=1, source_target_pairs={{0,8},{1,33},{2,10},{3,35},{4,12},{5,37},{6,14},{7,39},{8,0},{9,41... | collective-permute-start | bytes 786440 | tf_op jit(solution)/shard_map/ppermute | solution.py:50
  94.3 8.2 %collective-permute-start.19 = (bf16[16,8192]{1,0:T(8,128)(2,1)S(1)}, bf16[16,8192]{1,0:T(8,128)(2,1)S(1)}, u32[]{:S(2)}, u32[]{:S(2)}) collective-permute-start(bf16[16,8192]{1,0:T(8,128)(2,1)S(1)} %get-tuple-element.57), channel_id=1, source_target_pairs={{0,4},{1,17},{2,6},{3,19},{4,0},{5,21},{6,2},{7,23},{8,12},{9,25},... | collective-permute-start | bytes 786440 | tf_op jit(solution)/shard_map/ppermute | solution.py:50
  95.7 6.9 %collective-permute-start.20 = (bf16[16,8192]{1,0:T(8,128)(2,1)S(1)}, bf16[16,8192]{1,0:T(8,128)(2,1)S(1)}, u32[]{:S(2)}, u32[]{:S(2)}) collective-permute-start(bf16[16,8192]{1,0:T(8,128)(2,1)S(1)} %get-tuple-element.58), channel_id=1, source_target_pairs={{0,12},{1,49},{2,14},{3,51},{4,8},{5,53},{6,10},{7,55},{8,4},{9,57... | collective-permute-start | bytes 786440 | tf_op jit(solution)/shard_map/ppermute | solution.py:50
  103.3 4.7 %collective-permute-start.21 = (bf16[8,4096]{1,0:T(8,128)(2,1)S(1)}, bf16[8,4096]{1,0:T(8,128)(2,1)S(1)}, u32[]{:S(2)}, u32[]{:S(2)}) collective-permute-start(bf16[8,4096]{1,0:T(8,128)(2,1)S(1)} %get-tuple-element.60), channel_id=1, source_target_pairs={{0,64},{1,65},{2,66},{3,67},{4,68},{5,69},{6,70},{7,71},{8,72},{9,... | collective-permute-start | bytes 196616 | tf_op jit(solution)/shard_map/ppermute | solution.py:50
  104.5 3.6 %collective-permute-start.22 = (bf16[8,4096]{1,0:T(8,128)(2,1)S(1)}, bf16[8,4096]{1,0:T(8,128)(2,1)S(1)}, u32[]{:S(2)}, u32[]{:S(2)}) collective-permute-start(bf16[8,4096]{1,0:T(8,128)(2,1)S(1)} %get-tuple-element.61), channel_id=1, source_target_pairs={{0,2},{1,3},{2,0},{3,1},{4,6},{5,7},{6,4},{7,5},{8,10},{9,11},{10,... | collective-permute-start | bytes 196616 | tf_op jit(solution)/shard_map/ppermute | solution.py:50
  105.8 4.6 %collective-permute-start.23 = (bf16[8,4096]{1,0:T(8,128)(2,1)S(1)}, bf16[8,4096]{1,0:T(8,128)(2,1)S(1)}, u32[]{:S(2)}, u32[]{:S(2)}) collective-permute-start(bf16[8,4096]{1,0:T(8,128)(2,1)S(1)} %get-tuple-element.62), channel_id=1, source_target_pairs={{0,66},{1,67},{2,64},{3,65},{4,70},{5,71},{6,68},{7,69},{8,74},{9,... | collective-permute-start | bytes 196616 | tf_op jit(solution)/shard_map/ppermute | solution.py:50
  111.0 4.7 %collective-permute-start.24 = (bf16[8,2048]{1,0:T(8,128)(2,1)S(1)}, bf16[8,2048]{1,0:T(8,128)(2,1)S(1)}, u32[]{:S(2)}, u32[]{:S(2)}) collective-permute-start(bf16[8,2048]{1,0:T(8,128)(2,1)S(1)} %get-tuple-element.64), channel_id=1, source_target_pairs={{0,1},{1,0},{2,3},{3,2},{4,5},{5,4},{6,7},{7,6},{8,9},{9,8},{10,11... | collective-permute-start | bytes 98312 | tf_op jit(solution)/shard_map/ppermute | solution.py:50
